TPU v7x, 32 devices: a whole 2x2x4 slice. The times are simulated.
32 devices in a mesh: fsdp: 32 (over z, y, x, core).
Axes of the slice: x: 2, y: 2, z: 4, core: 2. Of those that a mesh axis runs over, the one named last changes fastest.
Arguments:
- tokens: bfloat16 [32768, 256], P('fsdp'), may hold values from -6 to 6
- params: bfloat16 [6176, 128], P('fsdp'), as said below
- segment_ids: int32 [32768], P('fsdp'), may hold values from 0 to 15, as said below
- cotangent: bfloat16 [32768, 256], P('fsdp'), may hold values from -6 to 6
Outputs:
- outputs: bfloat16 [32768, 256], P('fsdp')
- input_grad: float32 [32768, 256], P('fsdp')
- param_grad: float32 [6176, 128], P('fsdp')
Inputs may be any that keep to these rules, and one draw needn't show every extreme that they name: `segment_ids`: within each sequence of 128 positions the ids start at 0 and never fall; a new document may begin only at positions that are multiples of 8. `params`: entries after the first 789504 are padding and are not used.
All inputs are finite; a program needn't handle non-finite values.
Results may differ from a plain program's by a relative error of at most 0.0081.
Values may be sent and summed in bfloat16 or wider, within the bound.
No kernel may reach another device: no remote copies, remote signals or barrier semaphores. Data moves between devices by JAX's collectives and lax.ppermute only.
A program may use at most 64 MiB of HBM per device.

v0:
```python
import math

import jax
import jax.numpy as jnp
from jax import lax
from jax.sharding import PartitionSpec as P

D = 256
HEADS = 4
HEAD_DIM = 64
FF = 1024
SEQ = 128


EPSILON = 1e-05


def layer_norm(values, gain, shift):
    center = values - jnp.mean(values, axis=-1, keepdims=True)
    spread = jnp.mean(center * center, axis=-1, keepdims=True)
    return center * lax.rsqrt(spread + EPSILON) * gain + shift


def piece_shapes():
    return [
        (D, 3 * D),
        (D, D),
        (D, FF),
        (FF, D),
        (D,),
        (D,),
        (D,),
        (D,),
        (D,),
        (D,),
        (D,),
        (FF,),
        (D,),
    ]


def split_params(flat):
    pieces = []
    offset = 0
    for piece_shape in piece_shapes():
        length = math.prod(piece_shape)
        pieces.append(flat[offset : offset + length].reshape(piece_shape))
        offset += length
    return pieces


def times_transpose(left, right):
    return lax.dot_general(
        left, right, (((1,), (1,)), ((), ())), preferred_element_type=jnp.float32
    )


def transpose_times(left, right):
    return lax.dot_general(
        left, right, (((0,), (0,)), ((), ())), preferred_element_type=jnp.float32
    )


def attention_scores(query_rows, key_rows, allowed):
    scores = jnp.einsum(
        "gqhd,gkhd->ghqk", query_rows, key_rows, preferred_element_type=jnp.float32
    ) * HEAD_DIM ** (-0.5)
    return jnp.where(allowed[:, None], scores, -1e30)


def gelu_tanh(values):
    return jax.nn.gelu(values, approximate=True)


def local(tokens, params, segment_ids, cotangent):
    count = tokens.shape[0] // SEQ
    rows_local = tokens.shape[0]
    gathered = lax.all_gather(params, "fsdp", axis=0, tiled=True)
    unpacked = split_params(gathered.reshape(-1))
    w_qkv, w_out, w_up, w_down = unpacked[:4]
    small = [piece.astype(jnp.float32) for piece in unpacked[4:]]
    (
        gain_one,
        shift_one,
        bias_query,
        bias_value,
        bias_out,
        gain_two,
        shift_two,
        bias_up,
        bias_down,
    ) = small
    inputs = tokens.astype(jnp.float32)
    normed, norm_back = jax.vjp(layer_norm, inputs, gain_one, shift_one)
    normed_low = normed.astype(jnp.bfloat16)
    bias_all = jnp.concatenate([bias_query, jnp.zeros_like(bias_query), bias_value])
    project = (jnp.dot(normed_low, w_qkv, preferred_element_type=jnp.float32) + bias_all).astype(
        jnp.bfloat16
    )
    project = project.reshape(count, SEQ, 3, HEADS, HEAD_DIM)
    query_rows = project[:, :, 0]
    key_rows = project[:, :, 1]
    value_rows = project[:, :, 2]
    positions = jnp.arange(SEQ)
    causal = positions[None, :] <= positions[:, None]
    segments = segment_ids.reshape(count, SEQ)
    allowed = causal[None] & (segments[:, :, None] == segments[:, None, :])
    scores = attention_scores(query_rows, key_rows, allowed)
    highest = jnp.max(scores, axis=-1, keepdims=True)
    log_total = highest + jnp.log(jnp.sum(jnp.exp(scores - highest), axis=-1, keepdims=True))
    weights = jnp.exp(scores - log_total)
    attended = jnp.einsum(
        "ghqk,gkhd->gqhd",
        weights.astype(jnp.bfloat16),
        value_rows,
        preferred_element_type=jnp.float32,
    )
    attended_low = attended.reshape(rows_local, D).astype(jnp.bfloat16)
    middle = inputs + jnp.dot(attended_low, w_out, preferred_element_type=jnp.float32) + bias_out
    normed_two, norm_two_back = jax.vjp(layer_norm, middle, gain_two, shift_two)
    normed_two_low = normed_two.astype(jnp.bfloat16)
    hidden_pre = jnp.dot(normed_two_low, w_up, preferred_element_type=jnp.float32) + bias_up
    activated, gelu_back = jax.vjp(gelu_tanh, hidden_pre)
    activated_low = activated.astype(jnp.bfloat16)
    result = middle + jnp.dot(activated_low, w_down, preferred_element_type=jnp.float32) + bias_down
    outputs = result.astype(jnp.bfloat16)
    again = lax.all_gather(params, "fsdp", axis=0, tiled=True)
    w_qkv, w_out, w_up, w_down = split_params(again.reshape(-1))[:4]
    grad_result = cotangent.astype(jnp.float32)
    grad_down = transpose_times(activated_low, cotangent)
    grad_bias_down = jnp.sum(cotangent.astype(jnp.float32), axis=0)
    grad_activated = times_transpose(cotangent, w_down)
    (grad_hidden,) = gelu_back(grad_activated)
    grad_hidden_low = grad_hidden.astype(jnp.bfloat16)
    grad_up = transpose_times(normed_two_low, grad_hidden_low)
    grad_bias_up = jnp.sum(grad_hidden_low.astype(jnp.float32), axis=0)
    grad_normed_two = times_transpose(grad_hidden_low, w_up)
    grad_mid_part, grad_gain_two, grad_shift_two = norm_two_back(grad_normed_two)
    grad_middle = grad_result + grad_mid_part
    grad_middle_low = grad_middle.astype(jnp.bfloat16)
    grad_out_weight = transpose_times(attended_low, grad_middle_low)
    grad_bias_out = jnp.sum(grad_middle_low.astype(jnp.float32), axis=0)
    grad_attended = (
        times_transpose(grad_middle_low, w_out)
        .astype(jnp.bfloat16)
        .reshape(count, SEQ, HEADS, HEAD_DIM)
    )
    scores_again = attention_scores(query_rows, key_rows, allowed)
    weights_again = jnp.exp(scores_again - log_total)
    grad_value = jnp.einsum(
        "ghqk,gqhd->gkhd",
        weights_again.astype(jnp.bfloat16),
        grad_attended,
        preferred_element_type=jnp.float32,
    )
    grad_weights = jnp.einsum(
        "gqhd,gkhd->ghqk", grad_attended, value_rows, preferred_element_type=jnp.float32
    )
    grad_scores = weights_again * (
        grad_weights - jnp.sum(weights_again * grad_weights, axis=-1, keepdims=True)
    )
    grad_scores_low = grad_scores.astype(jnp.bfloat16)
    grad_query = jnp.einsum(
        "ghqk,gkhd->gqhd", grad_scores_low, key_rows, preferred_element_type=jnp.float32
    ) * HEAD_DIM ** (-0.5)
    grad_key = jnp.einsum(
        "ghqk,gqhd->gkhd", grad_scores_low, query_rows, preferred_element_type=jnp.float32
    ) * HEAD_DIM ** (-0.5)
    grad_project = (
        jnp.stack([grad_query, grad_key, grad_value], axis=2)
        .reshape(rows_local, 3 * D)
        .astype(jnp.bfloat16)
    )
    grad_project_wide = grad_project.astype(jnp.float32)
    grad_bias_query = jnp.sum(grad_project_wide[:, :D], axis=0)
    grad_bias_value = jnp.sum(grad_project_wide[:, 2 * D :], axis=0)
    grad_qkv = transpose_times(normed_low, grad_project)
    grad_normed = times_transpose(grad_project, w_qkv)
    grad_in_part, grad_gain_one, grad_shift_one = norm_back(grad_normed)
    input_grad = grad_middle + grad_in_part
    flat_grad = jnp.concatenate(
        [
            piece.reshape(-1)
            for piece in (
                grad_qkv,
                grad_out_weight,
                grad_up,
                grad_down,
                grad_gain_one,
                grad_shift_one,
                grad_bias_query,
                grad_bias_value,
                grad_bias_out,
                grad_gain_two,
                grad_shift_two,
                grad_bias_up,
                grad_bias_down,
            )
        ]
    )
    padding = jnp.zeros((gathered.size - flat_grad.shape[0],), jnp.float32)
    full_grad = jnp.concatenate([flat_grad, padding]).reshape(gathered.shape)
    param_grad = lax.psum_scatter(full_grad, "fsdp", scatter_dimension=0, tiled=True)
    return (outputs, input_grad, param_grad)


def solution(mesh):
    in_specs = (P("fsdp", None), P("fsdp", None), P("fsdp"), P("fsdp", None))
    out_specs = (P("fsdp", None), P("fsdp", None), P("fsdp", None))
    return jax.shard_map(local, mesh=mesh, in_specs=in_specs, out_specs=out_specs, check_vma=False)
```

profile of v0, /device:TPU:0, one launch (start us, length us, event | category | flops | bytes accessed | tf_op | source)
XLA Modules:
  0.0 260.9 jit_solution(7293904280929041019)
XLA Ops:
  7.9 1.2 copy.47
  9.2 2.1 copy.55
  11.7 57.0 %all-gather.3.cloned.1.call-done = bf16[32,193,128]{2,1,0:T(8,128)(2,1)} async-done(((bf16[1,193,128]{2,1,0:T(8,128)(2,1)}), bf16[32,193,128]{2,1,0:T(8,128)(2,1)}) %all-gather.3.cloned.1.call-update) | async-done | bytes 1581072 | tf_op jit(solution)/shard_map/all_gather | solution.py:78
  68.8 1.6 reshape.235
  70.5 1.2 fusion.64
  72.1 1.9 add_convert_fusion
  74.0 5.7 %reshape.236 = bf16[8,128,3,4,64]{4,3,2,1,0:T(4,128)(2,1)} reshape(bf16[1024,768]{1,0:T(8,128)(2,1)} %add_convert_fusion) | data formatting | bytes 3145728 | tf_op jit(solution)/shard_map/reshape | solution.py:100
  79.7 4.3 %fusion.63 = (bf16[8,128,1,4,64]{4,3,2,1,0:T(4,128)(2,1)}, bf16[8,128,1,4,64]{4,3,2,1,0:T(4,128)(2,1)S(1)}, bf16[8,128,1,4,64]{4,3,2,1,0:T(4,128)(2,1)S(1)}) fusion(bf16[8,128,3,4,64]{4,3,2,1,0:T(4,128)(2,1)} %reshape.236), kind=kLoop, calls=%fused_computation.129 | loop fusion | bytes 3145728 | tf_op jit(solution)/shard_map/slice | solution.py:101
  84.0 1.5 copy.79
  85.5 1.2 copy.80
  86.7 1.2 copy.78
  87.9 1.7 fusion.65
  90.4 1.2 copy.53
  91.6 1.4 fusion.66
  94.2 2.1 reshape.217
  96.3 2.0 reshape.218
  98.3 4.6 %multiply_convert_fusion = (bf16[1024,1024]{1,0:T(8,128)(2,1)}, f32[1024,1024]{1,0:T(8,128)S(1)}) fusion(f32[1024]{0:T(1024)S(1)} %fusion.49, bf16[256,1024]{1,0:T(8,128)(2,1)} %reshape.217, f32[1024,256]{0,1:T(8,128)} %copy-done, f32[256]{0:T(256)S(1)} %get-tuple-element.26, f32[256]{0:T(256)S(1)} %get-tuple-element.27, f32[1024]{0:T(1024)S(1)} %fusion.48, ...), kind=kOutput, calls=%fused_computation.10 | convolution fusion | flops 548667392 | bytes 7878656 | tf_op jit(solution)/shard_map/dot_general | solution.py:122
  102.9 3.7 %convert_reduce_fusion = (f32[1024]{0:T(1024)S(1)}, bf16[1024,1024]{1,0:T(8,128)(2,1)S(1)}) fusion(f32[1024,1024]{1,0:T(8,128)S(1)} %get-tuple-element.42, f32[1024]{0:T(1024)S(1)} %fusion.49, bf16[1024,256]{1,0:T(8,128)(2,1)S(1)} %copy-done.17, bf16[1024,256]{1,0:T(8,128)(2,1)S(1)} %copy-done.18), kind=kOutput, calls=%fused_computation.9 | convolution fusion | flops 560987136 | bytes 7348224 | tf_op jit(solution)/shard_map/dot_general | solution.py:53
  106.6 1.8 convolution_bitcast_fusion.1
  108.3 1.8 fusion.68
  110.1 2.5 copy.56
  112.7 1.9 multiply_reduce_fusion.1
  114.6 1.8 fusion.62
  119.7 2.8 %reshape.237 = bf16[8,128,4,64]{3,2,1,0:T(4,128)(2,1)} reshape(bf16[1024,256]{1,0:T(8,128)(2,1)} %convolution_convert_fusion) | data formatting | bytes 1048576 | tf_op jit(solution)/shard_map/reshape | solution.py:146
  122.5 2.2 copy.58
  124.6 1.9 multiply_reduce_fusion
  130.2 1.2 copy.63
  132.8 2.1 bitcast_convert_fusion
  135.0 1.2 copy.84
  137.3 2.4 convolution_bitcast_fusion
  139.7 1.5 copy.85
  142.2 1.8 slice_reduce_fusion
  147.6 1.3 constant_dynamic-update-slice_fusion.9
  148.9 1.3 constant_dynamic-update-slice_fusion.8
  150.2 1.3 constant_dynamic-update-slice_fusion.7
  151.5 1.3 constant_dynamic-update-slice_fusion.6
  152.8 1.3 constant_dynamic-update-slice_fusion.5
  154.1 1.3 constant_dynamic-update-slice_fusion.4
  155.4 1.3 constant_dynamic-update-slice_fusion.3
  156.7 1.3 constant_dynamic-update-slice_fusion.2
  158.0 1.3 constant_dynamic-update-slice_fusion.1
  159.9 82.2 %fusion = f32[208,128]{1,0:T(8,128)S(1)} fusion(f32[6176,128]{1,0:T(8,128)} %bitcast.21), kind=kCustom, calls=%all-reduce-scatter | all-reduce-scatter fusion | flops 851969 | bytes 3268608
  242.1 1.3 collective-permute-start
  243.4 1.3 collective-permute-start.1
  244.7 1.3 collective-permute-start.2
  246.0 3.1 %fusion.21 = bf16[1024,256]{0,1:T(8,128)(2,1)} fusion(f32[1024,256]{0,1:T(8,128)S(1)} %copy-done.2, bf16[1024,1024]{1,0:T(8,128)(2,1)} %get-tuple-element.41, bf16[1024,256]{1,0:T(8,128)(2,1)S(1)} %copy-done.19, f32[256]{0:T(256)S(1)} %get-tuple-element.25), kind=kOutput, calls=%fused_computation.45 | convolution fusion | flops 537657344 | bytes 4195328 | tf_op jit(solution)/shard_map/dot_general | solution.py:125
  249.2 1.3 copy.68
  250.5 2.0 copy.67
  (102 shorter events, 19.7 us)
Async XLA Ops:
  7.2 4.4 %copy-start.23 = (s32[1024]{0:T(1024)S(1)}, s32[1024]{0:T(1024)}, u32[]{:S(2)}) copy-start(s32[1024]{0:T(1024)} %param.6) | copy-start | bytes 12292
  7.2 61.6 %all-gather.3.cloned.1.call-start = ((), (), s32[]{:S(2)}) async-start(), calls=%async_computation | async-start | bytes 1689600 | tf_op jit(solution)/shard_map/all_gather | solution.py:78
  70.4 3.6 %copy-start.5 = (bf16[6176,128]{1,0:T(8,128)(2,1)}, bf16[6176,128]{1,0:T(8,128)(2,1)S(1)}, u32[]{:S(2)}) copy-start(bf16[6176,128]{1,0:T(8,128)(2,1)S(1)} %reshape.235) | copy-start | bytes 4743172
  72.0 7.7 %copy-start.21 = (bf16[256,768]{1,0:T(8,128)(2,1)}, bf16[256,768]{1,0:T(8,128)(2,1)S(1)}, u32[]{:S(2)}) copy-start(bf16[256,768]{1,0:T(8,128)(2,1)S(1)} %reshape.214) | copy-start | bytes 1179652
  87.9 2.1 copy-start.7
  89.6 2.0 slice-start
  93.1 1.0 copy-start
  98.3 4.6 %copy-start.17 = (bf16[1024,256]{1,0:T(8,128)(2,1)S(1)}, bf16[1024,256]{1,0:T(8,128)(2,1)}, u32[]{:S(2)}) copy-start(bf16[1024,256]{1,0:T(8,128)(2,1)} %param.7) | copy-start | bytes 1572868
  98.3 4.6 %copy-start.18 = (bf16[1024,256]{1,0:T(8,128)(2,1)S(1)}, bf16[1024,256]{1,0:T(8,128)(2,1)}, u32[]{:S(2)}) copy-start(bf16[1024,256]{1,0:T(8,128)(2,1)} %reshape.218) | copy-start | bytes 1572868
  102.9 3.7 %copy-start.1 = (f32[1024,256]{0,1:T(8,128)S(1)}, f32[1024,256]{0,1:T(8,128)}, u32[]{:S(2)}) copy-start(f32[1024,256]{0,1:T(8,128)} %copy-done) | copy-start | bytes 3145732
  106.5 1.8 copy-start.20
  112.7 4.8 %copy-start.9 = (bf16[1024,256]{0,1:T(8,128)(2,1)S(1)}, bf16[1024,256]{0,1:T(8,128)(2,1)}, u32[]{:S(2)}) copy-start(bf16[1024,256]{0,1:T(8,128)(2,1)} %copy.55) | copy-start | bytes 1572868
  116.4 1.1 copy-start.3
  117.7 0.8 copy-start.12
  126.5 1.0 copy-start.6
  127.6 1.2 copy-start.8
  127.6 2.1 copy-start.11
  127.6 2.1 copy-start.13
  130.2 1.9 copy-start.22
  132.8 2.2 copy-start.16
  141.5 2.5 copy-start.4
  141.5 2.5 copy-start.10
  142.2 3.3 %copy-start.14 = (f32[32,8,8,128]{3,1,2,0:T(8,128)S(1)}, f32[32,8,8,128]{3,1,2,0:T(8,128)}, u32[]{:S(2)}) copy-start(f32[32,8,8,128]{3,1,2,0:T(8,128)} %copy.84) | copy-start | bytes 3145732
  144.0 2.5 copy-start.15
  146.6 99.4 %copy-start.2 = (f32[1024,256]{0,1:T(8,128)S(1)}, f32[1024,256]{0,1:T(8,128)}, u32[]{:S(2)}) copy-start(f32[1024,256]{0,1:T(8,128)} %copy-done) | copy-start | bytes 3145732
  146.6 99.5 %copy-start.19 = (bf16[1024,256]{1,0:T(8,128)(2,1)S(1)}, bf16[1024,256]{1,0:T(8,128)(2,1)}, u32[]{:S(2)}) copy-start(bf16[1024,256]{1,0:T(8,128)(2,1)} %reshape.218) | copy-start | bytes 1572868
  242.1 10.4 %collective-permute-start = (f32[208,128]{1,0:T(8,128)S(1)}, f32[208,128]{1,0:T(8,128)S(1)}, u32[]{:S(2)}, u32[]{:S(2)}) collective-permute-start(f32[208,128]{1,0:T(8,128)S(1)} %fusion), channel_id=1, source_target_pairs={{0,1},{1,2},{2,3},{3,4},{4,5},{5,6},{6,7},{7,8},{8,9},{9,10},{10,1... | collective-permute-start | bytes 319496
  243.4 9.1 %collective-permute-start.1 = (f32[208,128]{1,0:T(8,128)S(1)}, f32[208,128]{1,0:T(8,128)S(1)}, u32[]{:S(2)}, u32[]{:S(2)}) collective-permute-start(f32[208,128]{1,0:T(8,128)S(1)} %fusion), channel_id=1, source_target_pairs={{0,2},{1,3},{2,4},{3,5},{4,6},{5,7},{6,8},{7,9},{8,10},{9,11},{10,... | collective-permute-start | bytes 319496
  244.7 7.8 %collective-permute-start.2 = (f32[49,128]{1,0:T(8,128)S(1)}, f32[49,128]{1,0:T(8,128)S(1)}, u32[]{:S(2)}, u32[]{:S(2)}) collective-permute-start(f32[49,128]{1,0:T(8,128)S(1)} %slice.107), channel_id=1, source_target_pairs={{0,3},{1,4},{2,5},{3,6},{4,7},{5,8},{6,9},{7,10},{8,11},{9,12},{10... | collective-permute-start | bytes 75272
Sparse Core Ops, SparseCore 0:
  10.9 57.8 all-gather.2
where the time goes:
time: 262 us; the launch traced here: 261 us
  blocking collectives  82.2 us (31%)
  local copies, waits for them, and re-layouts  61.9 us (24%)
  waiting for transfers between devices  57.7 us (22%)
  matrix products  29.6 us (11%)
  between operations  14.5 us (6%)
  other arithmetic  11.1 us (4%)
  starting transfers between devices  3.92 us (1%)
    unnamed x1, blocking collectives  82.2 us
    all_gather x1, waiting for transfers between devices, local(): gathered = lax.all_gather(params, 'fsdp', axis=0, tiled=True)  57 us
    unnamed x75, local copies, waits for them, and re-layouts  35.4 us
    dot_general x4, matrix products, times_transpose(): lax.dot_general(left, right, (((1,), (1,)), ((), ())), preferred_element_...  7.25 us
    reshape x1, local copies, waits for them, and re-layouts, local(): project = project.reshape(count, SEQ, 3, HEADS, HEAD_DIM)  5.72 us
  transfers between devices with their start and end apart: 4, of which 1 were waited for; matrix products, arithmetic and copies ran while one was open for 4% of the time, Pallas kernels for 0%

commit v1 on v0

v1 whole, which is shorter than its diff:
```python
import functools

import jax
import jax.numpy as jnp
from jax import lax
from jax.experimental import pallas as pl
from jax.experimental.pallas import tpu as pltpu
from jax.sharding import PartitionSpec as P

D = 256
HEADS = 4
HEAD_DIM = 64
FF = 1024
SEQ = 128
LANES = 128
BLOCK = 2 * SEQ
EPSILON = 1e-05
SCALE = HEAD_DIM ** (-0.5)
VMEM_BYTES = 48 * 1024 * 1024

ROW_QKV = 0
ROW_OUT = 1536
ROW_UP = 2048
ROW_DOWN = 4096
ROW_SMALL = 6144
ROW_END = 6168
GAIN_ONE, SHIFT_ONE, BIAS_QUERY, BIAS_VALUE, BIAS_OUT = 0, 2, 4, 6, 8
GAIN_TWO, SHIFT_TWO, BIAS_UP, BIAS_DOWN = 10, 12, 14, 22
SMALL_ROWS = 24

F32 = jnp.float32
BF16 = jnp.bfloat16


def dot(left, right):
    return jnp.dot(left, right, preferred_element_type=F32)


def dot_nt(left, right):
    return lax.dot_general(left, right, (((1,), (1,)), ((), ())), preferred_element_type=F32)


def dot_tn(left, right):
    return lax.dot_general(left, right, (((0,), (0,)), ((), ())), preferred_element_type=F32)


def small_vector(small, row, count):
    return jnp.concatenate([small[row + i : row + i + 1, :] for i in range(count)], axis=1)


def fold_rows(values):
    rows, columns = values.shape
    return jnp.sum(values.reshape(rows // 8, 8, columns), axis=0)


def normalize(values):
    center = values - jnp.mean(values, axis=-1, keepdims=True)
    rate = lax.rsqrt(jnp.mean(center * center, axis=-1, keepdims=True) + EPSILON)
    return center * rate, rate


def normalize_back(grad, gain, normed, rate):
    scaled = grad * gain
    return rate * (
        scaled
        - jnp.mean(scaled, axis=-1, keepdims=True)
        - normed * jnp.mean(scaled * normed, axis=-1, keepdims=True)
    )


def head_masks():
    lane = lax.broadcasted_iota(jnp.int32, (1, D), 1)
    return [(lane // HEAD_DIM == h).astype(F32).astype(BF16) for h in range(HEADS)]


def spread_heads(rows):
    return jnp.concatenate([rows * mask for mask in head_masks()], axis=0)


def matrix_from_flat(flat, start, rows, columns, out):
    per_row = columns // LANES
    for j in range(per_row):
        out[:, j * LANES : (j + 1) * LANES] = flat[
            pl.ds(start + j, rows, stride=per_row), :
        ].astype(BF16)


def matrix_to_flat(matrix, rows, columns, flat, start):
    per_row = columns // LANES
    for j in range(per_row):
        flat[pl.ds(start + j, rows, stride=per_row), :] = matrix[:, j * LANES : (j + 1) * LANES]


def attend_kernel(n_bufs, ids, seg, tok, *refs):
    bufs = refs[:n_bufs]
    (project_out, weights_out, attended_out, w_qkv, w_out, w_up, w_down, small, flat) = refs[n_bufs:]

    @pl.when(pl.program_id(0) == 0)
    def _():
        slot = 0
        for buf in bufs:
            count, rows, _ = buf.shape

            def place(i, carry, buf=buf, slot=slot, rows=rows):
                flat[pl.ds(ids[slot + i] * rows, rows), :] = buf[i].astype(F32)
                return carry

            lax.fori_loop(0, count, place, 0)
            slot += count
        matrix_from_flat(flat, ROW_QKV, D, 3 * D, w_qkv)
        matrix_from_flat(flat, ROW_OUT, D, D, w_out)
        matrix_from_flat(flat, ROW_UP, D, FF, w_up)
        matrix_from_flat(flat, ROW_DOWN, FF, D, w_down)
        small[...] = flat[ROW_SMALL:ROW_END, :]

    normed, _ = normalize(tok[...].astype(F32))
    normed_low = (
        normed * small_vector(small, GAIN_ONE, 2) + small_vector(small, SHIFT_ONE, 2)
    ).astype(BF16)
    bias = jnp.concatenate(
        [
            small_vector(small, BIAS_QUERY, 2),
            jnp.zeros((1, D), F32),
            small_vector(small, BIAS_VALUE, 2),
        ],
        axis=1,
    )
    project = (dot(normed_low, w_qkv[...]) + bias).astype(BF16)
    project_out[...] = project
    causal = lax.broadcasted_iota(jnp.int32, (SEQ, SEQ), 1) <= lax.broadcasted_iota(
        jnp.int32, (SEQ, SEQ), 0
    )
    for s in range(BLOCK // SEQ):
        rows = slice(s * SEQ, (s + 1) * SEQ)
        across = jnp.broadcast_to(seg[s].astype(F32), (SEQ, SEQ))
        allowed = causal & (across == across.T)
        query = project[rows, :D]
        key = spread_heads(project[rows, D : 2 * D])
        value = spread_heads(project[rows, 2 * D :])
        scores = dot_nt(query, key) * SCALE
        low = []
        for h in range(HEADS):
            columns = slice(h * SEQ, (h + 1) * SEQ)
            mine = jnp.where(allowed, scores[:, columns], -1e30)
            grown = jnp.exp(mine - jnp.max(mine, axis=-1, keepdims=True))
            weights = grown * (1.0 / jnp.sum(grown, axis=-1, keepdims=True))
            weights_out[rows, columns] = weights
            low.append(weights.astype(BF16))
        attended_out[rows, :] = dot(jnp.concatenate(low, axis=1), value).astype(BF16)


def feed_kernel(
    tok, attended, cot, w_out, w_up, w_down, small,
    result_out, grad_middle_out, grad_attended_out, flat_out, small_out,
    acc_out, acc_up, acc_down, acc_small,
):
    step = pl.program_id(0)

    @pl.when(step == 0)
    def _():
        acc_out[...] = jnp.zeros_like(acc_out)
        acc_up[...] = jnp.zeros_like(acc_up)
        acc_down[...] = jnp.zeros_like(acc_down)
        acc_small[...] = jnp.zeros_like(acc_small)

    gain = small_vector(small, GAIN_TWO, 2)
    middle = tok[...].astype(F32) + dot(attended[...], w_out[...]) + small_vector(small, BIAS_OUT, 2)
    normed, rate = normalize(middle)
    normed_low = (normed * gain + small_vector(small, SHIFT_TWO, 2)).astype(BF16)
    hidden = dot(normed_low, w_up[...]) + small_vector(small, BIAS_UP, 8)
    square = hidden * hidden
    slope = 0.7978845608028654
    bent = jnp.tanh(hidden * (slope + (slope * 0.044715) * square))
    half = 0.5 + 0.5 * bent
    activated = (hidden * half).astype(BF16)
    derivative = half + hidden * (0.5 - 0.5 * bent * bent) * (
        slope + (3 * slope * 0.044715) * square
    )
    result = middle + dot(activated, w_down[...]) + small_vector(small, BIAS_DOWN, 2)
    result_out[...] = result.astype(BF16)
    cotangent = cot[...]
    grad_result = cotangent.astype(F32)
    acc_down[...] += dot_tn(activated, cotangent)
    grad_hidden = (dot_nt(cotangent, w_down[...]) * derivative).astype(BF16)
    acc_up[...] += dot_tn(normed_low, grad_hidden)
    grad_normed = dot_nt(grad_hidden, w_up[...])
    grad_middle = grad_result + normalize_back(grad_normed, gain, normed, rate)
    grad_middle_out[...] = grad_middle
    grad_middle_low = grad_middle.astype(BF16)
    acc_out[...] += dot_tn(attended[...], grad_middle_low)
    grad_attended_out[...] = dot_nt(grad_middle_low, w_out[...]).astype(BF16)
    acc_small[:, 0:D] += fold_rows(grad_middle_low.astype(F32))
    acc_small[:, D : 2 * D] += fold_rows(grad_normed * normed)
    acc_small[:, 2 * D : 3 * D] += fold_rows(grad_normed)
    acc_small[:, 3 * D : 3 * D + FF] += fold_rows(grad_hidden.astype(F32))
    acc_small[:, 3 * D + FF :] += fold_rows(grad_result)

    @pl.when(step == pl.num_programs(0) - 1)
    def _():
        matrix_to_flat(acc_out, D, D, flat_out, ROW_OUT - ROW_OUT)
        matrix_to_flat(acc_up, D, FF, flat_out, ROW_UP - ROW_OUT)
        matrix_to_flat(acc_down, FF, D, flat_out, ROW_DOWN - ROW_OUT)
        sums = jnp.sum(acc_small[...], axis=0, keepdims=True)
        for i in range(SMALL_ROWS - BIAS_OUT):
            small_out[i : i + 1, :] = sums[:, i * LANES : (i + 1) * LANES]


def attend_back_kernel(
    n_bufs, ids, tok, project, weights, grad_attended, grad_middle, w_qkv, small, flat_in, small_in,
    input_grad_out, *refs,
):
    bufs = refs[:n_bufs]
    acc_qkv, acc_small, flat, grad_project = refs[n_bufs:]
    step = pl.program_id(0)

    @pl.when(step == 0)
    def _():
        acc_qkv[...] = jnp.zeros_like(acc_qkv)
        acc_small[...] = jnp.zeros_like(acc_small)

    masks = head_masks()
    for s in range(BLOCK // SEQ):
        rows = slice(s * SEQ, (s + 1) * SEQ)
        query = spread_heads(project[rows, :D])
        key = spread_heads(project[rows, D : 2 * D])
        value = spread_heads(project[rows, 2 * D :])
        grad_rows = grad_attended[rows, :]
        grad_weights = dot_nt(grad_rows, value)
        scores_low, scores_turned, weights_turned = [], [], []
        for h in range(HEADS):
            columns = slice(h * SEQ, (h + 1) * SEQ)
            mine = weights[rows, columns]
            product = mine * grad_weights[:, columns]
            grad_scores = product - mine * jnp.sum(product, axis=-1, keepdims=True)
            scores_low.append(grad_scores.astype(BF16))
            scores_turned.append(grad_scores.T.astype(BF16))
            weights_turned.append(mine.T.astype(BF16))
        grad_query = dot(jnp.concatenate(scores_low, axis=1), key) * SCALE
        grad_key = dot(jnp.concatenate(scores_turned, axis=1), query) * SCALE
        grad_value = dot(jnp.concatenate(weights_turned, axis=1), spread_heads(grad_rows))
        grad_project[rows, :D] = grad_query.astype(BF16)
        grad_project[rows, D : 2 * D] = grad_key.astype(BF16)
        grad_project[rows, 2 * D :] = grad_value.astype(BF16)

    gain = small_vector(small, GAIN_ONE, 2)
    normed, rate = normalize(tok[...].astype(F32))
    normed_low = (normed * gain + small_vector(small, SHIFT_ONE, 2)).astype(BF16)
    acc_qkv[...] += dot_tn(normed_low, grad_project[...])
    grad_normed = dot_nt(grad_project[...], w_qkv[...])
    input_grad_out[...] = grad_middle[...] + normalize_back(grad_normed, gain, normed, rate)
    acc_small[:, 0:D] += fold_rows(grad_normed * normed)
    acc_small[:, D : 2 * D] += fold_rows(grad_normed)
    acc_small[:, 2 * D : 3 * D] += fold_rows(grad_project[:, :D].astype(F32))
    acc_small[:, 3 * D :] += fold_rows(grad_project[:, 2 * D :].astype(F32))

    @pl.when(step == pl.num_programs(0) - 1)
    def _():
        matrix_to_flat(acc_qkv, D, 3 * D, flat, ROW_QKV)
        flat[ROW_OUT:ROW_SMALL, :] = flat_in[...]
        sums = jnp.sum(acc_small[...], axis=0, keepdims=True)
        for i in range(BIAS_OUT):
            flat[ROW_SMALL + i : ROW_SMALL + i + 1, :] = sums[:, i * LANES : (i + 1) * LANES]
        flat[ROW_SMALL + BIAS_OUT : ROW_END, :] = small_in[...]
        if flat.shape[0] > ROW_END:
            flat[ROW_END:, :] = jnp.zeros((flat.shape[0] - ROW_END, LANES), F32)
        slot = 0
        for buf in bufs:
            count, rows, _ = buf.shape

            def place(i, carry, buf=buf, slot=slot, rows=rows):
                buf[i] = flat[pl.ds(ids[slot + i] * rows, rows), :].astype(buf.dtype)
                return carry

            lax.fori_loop(0, count, place, 0)
            slot += count


def rows_spec(columns):
    return pl.BlockSpec((BLOCK, columns), lambda i: (i, 0))


def whole_spec(shape):
    return pl.BlockSpec(shape, lambda i: (0,) * len(shape))


SMEM_SPEC = pl.BlockSpec(memory_space=pltpu.SMEM)
PARAMS = pltpu.CompilerParams(
    dimension_semantics=("arbitrary",), vmem_limit_bytes=VMEM_BYTES
)


def attend(ids, segments, tokens, bufs):
    rows = tokens.shape[0]
    total = sum(buf.shape[0] * buf.shape[1] for buf in bufs)
    fixed = [(D, 3 * D), (D, D), (D, FF), (FF, D)]
    outs = [((rows, 3 * D), BF16), ((rows, HEADS * SEQ), F32), ((rows, D), BF16)]
    return pl.pallas_call(
        functools.partial(attend_kernel, len(bufs)),
        grid=(rows // BLOCK,),
        in_specs=[
            SMEM_SPEC,
            pl.BlockSpec((BLOCK // SEQ, 1, SEQ), lambda i: (i, 0, 0)),
            rows_spec(D),
        ]
        + [whole_spec(buf.shape) for buf in bufs],
        out_specs=[rows_spec(shape[1]) for shape, _ in outs]
        + [whole_spec(shape) for shape in fixed]
        + [whole_spec((SMALL_ROWS, LANES))],
        out_shape=[jax.ShapeDtypeStruct(shape, kind) for shape, kind in outs]
        + [jax.ShapeDtypeStruct(shape, BF16) for shape in fixed]
        + [jax.ShapeDtypeStruct((SMALL_ROWS, LANES), F32)],
        scratch_shapes=[pltpu.VMEM((total, LANES), F32)],
        compiler_params=PARAMS,
        name="attend",
    )(ids, segments, tokens, *bufs)


def feed(tokens, attended, cotangent, w_out, w_up, w_down, small):
    rows = tokens.shape[0]
    flat_rows = ROW_SMALL - ROW_OUT
    small_rows = SMALL_ROWS - BIAS_OUT
    return pl.pallas_call(
        feed_kernel,
        grid=(rows // BLOCK,),
        in_specs=[rows_spec(D)] * 3
        + [whole_spec(item.shape) for item in (w_out, w_up, w_down, small)],
        out_specs=[rows_spec(D)] * 3
        + [whole_spec((flat_rows, LANES)), whole_spec((small_rows, LANES))],
        out_shape=[
            jax.ShapeDtypeStruct((rows, D), BF16),
            jax.ShapeDtypeStruct((rows, D), F32),
            jax.ShapeDtypeStruct((rows, D), BF16),
            jax.ShapeDtypeStruct((flat_rows, LANES), F32),
            jax.ShapeDtypeStruct((small_rows, LANES), F32),
        ],
        scratch_shapes=[
            pltpu.VMEM((D, D), F32),
            pltpu.VMEM((D, FF), F32),
            pltpu.VMEM((FF, D), F32),
            pltpu.VMEM((8, small_rows * LANES), F32),
        ],
        compiler_params=PARAMS,
        name="feed",
    )(tokens, attended, cotangent, w_out, w_up, w_down, small)


def attend_back(ids, tokens, project, weights, grad_attended, grad_middle, w_qkv, small, flat, few, bufs):
    rows = tokens.shape[0]
    total = sum(shape[0] * shape[1] for shape, _ in bufs)
    return pl.pallas_call(
        functools.partial(attend_back_kernel, len(bufs)),
        grid=(rows // BLOCK,),
        in_specs=[SMEM_SPEC]
        + [rows_spec(item.shape[1]) for item in (tokens, project, weights, grad_attended, grad_middle)]
        + [whole_spec(item.shape) for item in (w_qkv, small, flat, few)],
        out_specs=[rows_spec(D)] + [whole_spec(shape) for shape, _ in bufs],
        out_shape=[jax.ShapeDtypeStruct((rows, D), F32)]
        + [jax.ShapeDtypeStruct(shape, kind) for shape, kind in bufs],
        scratch_shapes=[
            pltpu.VMEM((D, 3 * D), F32),
            pltpu.VMEM((8, BIAS_OUT * LANES), F32),
            pltpu.VMEM((total, LANES), F32),
            pltpu.VMEM((BLOCK, 3 * D), BF16),
        ],
        compiler_params=PARAMS,
        name="attend_back",
    )(ids, tokens, project, weights, grad_attended, grad_middle, w_qkv, small, flat, few)


def block(tokens, segment_ids, cotangent, share_ids, shares, grad_ids, grad_bufs):
    segments = segment_ids.reshape(-1, 1, SEQ)
    project, weights, attended, w_qkv, w_out, w_up, w_down, small = attend(
        share_ids, segments, tokens, shares
    )
    outputs, grad_middle, grad_attended, flat, few = feed(
        tokens, attended, cotangent, w_out, w_up, w_down, small
    )
    input_grad, *grads = attend_back(
        grad_ids, tokens, project, weights, grad_attended, grad_middle, w_qkv, small, flat, few, grad_bufs
    )
    return outputs, input_grad, grads


def local_any(n, tokens, params, segment_ids, cotangent):
    rows = params.shape[0]
    gathered = lax.all_gather(params, "fsdp", axis=0)
    ids = jnp.arange(n, dtype=jnp.int32)
    outputs, input_grad, (grads,) = block(
        tokens, segment_ids, cotangent, ids, [gathered], ids, [((n, rows, LANES), F32)]
    )
    param_grad = lax.psum_scatter(
        grads.reshape(n * rows, LANES), "fsdp", scatter_dimension=0, tiled=True
    )
    return outputs, input_grad, param_grad


Z, PLANE = 4, 4


def index_of(z, plane, core):
    return (z * PLANE + plane) * 2 + core


def move(values, step_z, step_plane, step_core):
    pairs = [
        (index_of(z, p, c), index_of((z + step_z) % Z, p ^ step_plane, c ^ step_core))
        for z in range(Z)
        for p in range(PLANE)
        for c in range(2)
    ]
    return lax.ppermute(values, "fsdp", pairs)


def local_slice(tokens, params, segment_ids, cotangent):
    me = lax.axis_index("fsdp").astype(jnp.int32)
    z, plane, core = me // (2 * PLANE), (me // 2) % PLANE, me % 2

    column = jnp.stack([params] + [move(params, d, 0, 0) for d in range(1, Z)])
    same = [column] + [move(column, 0, d, 0) for d in range(1, PLANE)]
    shares = same + [move(item, 0, 0, 1) for item in same]
    share_ids = jnp.stack(
        [
            index_of((z - dz) % Z, plane ^ dp, core ^ dc)
            for dc in range(2)
            for dp in range(PLANE)
            for dz in range(Z)
        ]
    )
    grad_ids = jnp.stack(
        [
            index_of((z + dz) % Z, plane ^ dp, core ^ dc)
            for dc in range(2)
            for dp in range(PLANE)
            for dz in range(Z)
        ]
    )
    shape = (PLANE * Z,) + params.shape
    outputs, input_grad, (kept, sent) = block(
        tokens, segment_ids, cotangent, share_ids, shares, grad_ids, [(shape, F32), (shape, BF16)]
    )

    totals = kept + move(sent, 0, 0, 1).astype(F32)
    totals = totals.reshape((PLANE, Z) + params.shape)
    column = totals[0]
    for d in range(1, PLANE):
        column = column + move(totals[d].astype(BF16), 0, d, 0).astype(F32)
    param_grad = column[0]
    for d in range(1, Z):
        param_grad = param_grad + move(column[d].astype(BF16), d, 0, 0).astype(F32)
    return outputs, input_grad, param_grad


def solution(mesh):
    n = mesh.shape["fsdp"]
    local = local_slice if n == 2 * PLANE * Z else functools.partial(local_any, n)
    in_specs = (P("fsdp", None), P("fsdp", None), P("fsdp"), P("fsdp", None))
    out_specs = (P("fsdp", None), P("fsdp", None), P("fsdp", None))
    return jax.shard_map(local, mesh=mesh, in_specs=in_specs, out_specs=out_specs, check_vma=False)
```

time: 262 us -> 82.9 us (0.32)
  blocking collectives: 82.2 us -> 0 us
  local copies, waits for them, and re-layouts: 61.9 us -> 2.13 us
  matrix products: 29.6 us -> 0 us
  Pallas kernels: 0 us -> 29.1 us
  waiting for transfers between devices: 57.7 us -> 28.8 us
  starting transfers between devices: 3.92 us -> 18.5 us
  between operations: 14.5 us -> 0.71 us
  other arithmetic: 11.1 us -> 3.3 us
    unnamed x1 -> x0, blocking collectives: 82.2 us -> none
    all_gather x1 -> x0, waiting for transfers between devices: 57 us -> none  [local(): gathered = lax.all_gather(params, 'fsdp', axis=0, tiled=True)]
    unnamed x75 -> x8, local copies, waits for them, and re-layouts: 35.4 us -> 1.74 us
    dot_general x18 -> x0, matrix products: 29.6 us -> none  [the longest x4 7.25 us: times_transpose(): lax.dot_general(left, right, (((1,), (1,)), ((), ())), preferred_element_...]
    pallas_call x0 -> x3, Pallas kernels: none -> 29.1 us  [the longest x1 10.7 us: feed(): pl.pallas_call(feed_kernel, grid=(rows // BLOCK,), in_specs=[rows_spec(D)...]
    ppermute x0 -> x17, waiting for transfers between devices: none -> 28.8 us  [move(): return lax.ppermute(values, 'fsdp', pairs)]
    ppermute x0 -> x17, starting transfers between devices: none -> 18.5 us  [move(): return lax.ppermute(values, 'fsdp', pairs)]
    reshape x8 -> x0, local copies, waits for them, and re-layouts: 15.2 us -> none  [the longest x1 5.72 us: local(): project = project.reshape(count, SEQ, 3, HEADS, HEAD_DIM)]
  transfers between devices with their start and end apart: 4 -> 17, of which waited for: 1 -> 12; matrix products, arithmetic and copies ran while one was open for 4% -> 0% of each run, Pallas kernels for 0% -> 0%
where the time goes in v1:
time: 82.9 us; the launch traced here: 82.6 us
  Pallas kernels  29.1 us (35%)
  waiting for transfers between devices  28.8 us (35%)
  starting transfers between devices  18.5 us (22%)
  other arithmetic  3.3 us (4%)
  local copies, waits for them, and re-layouts  2.13 us (3%)
    ppermute x17, waiting for transfers between devices, move(): return lax.ppermute(values, 'fsdp', pairs)  28.8 us
    ppermute x17, starting transfers between devices, move(): return lax.ppermute(values, 'fsdp', pairs)  18.5 us
    pallas_call x1, Pallas kernels, feed(): pl.pallas_call(feed_kernel, grid=(rows // BLOCK,), in_specs=[rows_spec(D)...  10.7 us
    pallas_call x1, Pallas kernels, attend_back(): pl.pallas_call(functools.partial(attend_back_kernel, len(bufs)), grid=(ro...  10.7 us
    pallas_call x1, Pallas kernels, attend(): pl.pallas_call(functools.partial(attend_kernel, len(bufs)), grid=(rows //...  7.71 us
    another operation x2, other arithmetic  1.8 us
    unnamed x8, local copies, waits for them, and re-layouts  1.74 us
  transfers between devices with their start and end apart: 17, of which 12 were waited for; matrix products, arithmetic and copies ran while one was open for 0% of the time, Pallas kernels for 0%

profile of v1, /device:TPU:0, one launch (start us, length us, event | category | flops | bytes accessed | tf_op | source)
XLA Modules:
  0.0 82.6 jit_solution(3539241515292767405)
XLA Ops:
  0.6 0.0 copy-start.1
  0.6 5.1 %collective-permute-start.2 = (bf16[193,128]{1,0:T(8,128)(2,1)}, bf16[193,128]{1,0:T(8,128)(2,1)S(1)}, u32[]{:S(2)}, u32[]{:S(2)}) collective-permute-start(bf16[193,128]{1,0:T(8,128)(2,1)} %param.5), channel_id=1, source_target_pairs={{0,24},{1,25},{2,26},{3,27},{4,28},{5,29},{6,30},{7,31},{8,0},{9,1... | collective-permute-start | bytes 148232 | tf_op jit(solution)/shard_map/ppermute | solution.py:411
  5.7 0.0 collective-permute-start.1
  5.7 1.0 %collective-permute-start = (bf16[193,128]{1,0:T(8,128)(2,1)}, bf16[193,128]{1,0:T(8,128)(2,1)S(1)}, u32[]{:S(2)}, u32[]{:S(2)}) collective-permute-start(bf16[193,128]{1,0:T(8,128)(2,1)} %param.5), channel_id=1, source_target_pairs={{0,8},{1,9},{2,10},{3,11},{4,12},{5,13},{6,14},{7,15},{8,16},{9,17... | collective-permute-start | bytes 148232 | tf_op jit(solution)/shard_map/ppermute | solution.py:411
  6.8 1.4 %collective-permute-done.2 = bf16[193,128]{1,0:T(8,128)(2,1)S(1)} collective-permute-done((bf16[193,128]{1,0:T(8,128)(2,1)}, bf16[193,128]{1,0:T(8,128)(2,1)S(1)}, u32[]{:S(2)}, u32[]{:S(2)}) %collective-permute-start.2) | collective-permute-done | bytes 49440 | tf_op jit(solution)/shard_map/ppermute | solution.py:411
  8.2 2.8 %collective-permute-done.1 = bf16[193,128]{1,0:T(8,128)(2,1)S(1)} collective-permute-done((bf16[193,128]{1,0:T(8,128)(2,1)}, bf16[193,128]{1,0:T(8,128)(2,1)S(1)}, u32[]{:S(2)}, u32[]{:S(2)}) %collective-permute-start.1) | collective-permute-done | bytes 49440 | tf_op jit(solution)/shard_map/ppermute | solution.py:411
  11.0 0.9 %collective-permute-done = bf16[193,128]{1,0:T(8,128)(2,1)S(1)} collective-permute-done((bf16[193,128]{1,0:T(8,128)(2,1)}, bf16[193,128]{1,0:T(8,128)(2,1)S(1)}, u32[]{:S(2)}, u32[]{:S(2)}) %collective-permute-start) | collective-permute-done | bytes 49440 | tf_op jit(solution)/shard_map/ppermute | solution.py:411
  11.9 0.8 %pad_maximum_fusion.refs_0_ = bf16[4,193,128]{2,1,0:T(8,128)(2,1)S(1)} fusion(bf16[1,193,128]{2,1,0:T(8,128)(2,1)S(1)} %bitcast.77, bf16[1,193,128]{2,1,0:T(8,128)(2,1)S(1)} %bitcast.78, bf16[1,193,128]{2,1,0:T(8,128)(2,1)S(1)} %bitcast.79, bf16[1,193,128]{2,1,0:T(8,128)(2,1)} %bitcast.76), kind=kLoop, calls=%fused_computation.4 | loop fusion | flops 296448 | bytes 395264 | tf_op jit(solution)/shard_map/stack | solution.py:418
  12.7 1.6 %collective-permute-start.3 = (bf16[4,193,128]{2,1,0:T(8,128)(2,1)S(1)}, bf16[4,193,128]{2,1,0:T(8,128)(2,1)S(1)}, u32[]{:S(2)}, u32[]{:S(2)}) collective-permute-start(bf16[4,193,128]{2,1,0:T(8,128)(2,1)S(1)} %pad_maximum_fusion.refs_0_), channel_id=1, source_target_pairs={{0,2},{1,3},{2,0},{3,1},{4,6},{5,7},{6,4},{7,5},{8,10},{9,11},{10,... | collective-permute-start | bytes 592904 | tf_op jit(solution)/shard_map/ppermute | solution.py:411
  14.3 1.5 %collective-permute-start.4 = (bf16[4,193,128]{2,1,0:T(8,128)(2,1)S(1)}, bf16[4,193,128]{2,1,0:T(8,128)(2,1)S(1)}, u32[]{:S(2)}, u32[]{:S(2)}) collective-permute-start(bf16[4,193,128]{2,1,0:T(8,128)(2,1)S(1)} %pad_maximum_fusion.refs_0_), channel_id=1, source_target_pairs={{0,4},{1,5},{2,6},{3,7},{4,0},{5,1},{6,2},{7,3},{8,12},{9,13},{10,... | collective-permute-start | bytes 592904 | tf_op jit(solution)/shard_map/ppermute | solution.py:411
  15.8 0.5 collective-permute-start.5
  16.3 0.0 collective-permute-start.6
  16.3 4.3 %collective-permute-done.3.refs_1_ = bf16[4,193,128]{2,1,0:T(8,128)(2,1)S(1)} collective-permute-done((bf16[4,193,128]{2,1,0:T(8,128)(2,1)S(1)}, bf16[4,193,128]{2,1,0:T(8,128)(2,1)S(1)}, u32[]{:S(2)}, u32[]{:S(2)}) %collective-permute-start.3) | collective-permute-done | bytes 197664 | tf_op jit(solution)/shard_map/ppermute | solution.py:411
  20.6 0.0 collective-permute-start.7
  20.6 3.4 %collective-permute-done.4.refs_2_ = bf16[4,193,128]{2,1,0:T(8,128)(2,1)S(1)} collective-permute-done((bf16[4,193,128]{2,1,0:T(8,128)(2,1)S(1)}, bf16[4,193,128]{2,1,0:T(8,128)(2,1)S(1)}, u32[]{:S(2)}, u32[]{:S(2)}) %collective-permute-start.4) | collective-permute-done | bytes 197664 | tf_op jit(solution)/shard_map/ppermute | solution.py:411
  24.0 0.0 collective-permute-start.8
  24.0 0.0 collective-permute-done.5.refs_3_
  24.0 0.5 collective-permute-start.9
  24.5 0.1 stack.229.ids
  24.6 0.1 stack.259.ids
  24.7 0.0 collective-permute-done.6.refs_4_
  24.7 0.0 collective-permute-done.7.refs_5_
  24.7 0.7 collective-permute-done.8.refs_6_
  25.4 0.3 collective-permute-done.9.refs_7_
  25.7 1.0 %copy-done = bf16[1024,256]{1,0:T(8,128)(2,1)S(1)} copy-done((bf16[1024,256]{1,0:T(8,128)(2,1)S(1)}, bf16[1024,256]{1,0:T(8,128)(2,1)}, u32[]{:S(2)}) %copy-start) | copy-done | bytes 524312
  26.8 0.7 copy-done.3
  27.4 7.7 %attend.1 = (bf16[1024,768]{1,0:T(8,128)(2,1)S(1)}, f32[1024,512]{1,0:T(8,128)}, bf16[1024,256]{1,0:T(8,128)(2,1)S(1)}, bf16[256,768]{1,0:T(8,128)(2,1)S(1)}, bf...) custom-call(s32[32]{0:T(128)S(1)} %stack.229.ids, ...), custom_call_target="tpu_custom_call" | custom-call | tf_op jit(solution)/shard_map/attend/pallas_call | solution.py:297
  35.2 0.0 copy-done.2
  35.2 10.7 %feed.1 = (bf16[1024,256]{1,0:T(8,128)(2,1)}, f32[1024,256]{1,0:T(8,128)S(1)}, bf16[1024,256]{1,0:T(8,128)(2,1)S(1)}, f32[4608,128]{1,0:T(8,128)}, f32[16,128]{1,0:T(8,128)S(1)}) custom-call(bf16[1024,256]{1,0:T(8,128)(2,1)S(1)} %copy-done.1, bf16[1024,256]{1,0:T(8,128)(2,1)S(1)} %get-tuple-element.19.attended, bf16[1024,256]{1,0:T(8,128)(2,1)S(1)} %copy-done.2, ...), custom_call_target="tpu_custom_call" | custom-call | tf_op jit(solution)/shard_map/feed/pallas_call | solution.py:322
  45.9 10.7 %attend_back.1 = (f32[1024,256]{1,0:T(8,128)}, f32[16,193,128]{2,1,0:T(8,128)}, bf16[16,193,128]{2,1,0:T(8,128)(2,1)S(1)}) custom-call(s32[32]{0:T(128)S(1)} %stack.259.ids, bf16[1024,256]{1,0:T(8,128)(2,1)S(1)} %copy-done.1, bf16[1024,768]{1,0:T(8,128)(2,1)S(1)} %get-tuple-element.25.project, f32[1024,512]{1,0:T(8,128)} %get-tuple-element.26.weights, ...), custom_call_target="tpu_custom_call" | custom-call | tf_op jit(solution)/shard_map/attend_back/pallas_call | solution.py:350
  56.6 0.1 copy.7
  56.7 0.3 collective-permute-start.10
  57.0 2.1 %collective-permute-done.10 = bf16[16,193,128]{2,0,1:T(8,128)(2,1)S(1)} collective-permute-done((bf16[16,193,128]{2,0,1:T(8,128)(2,1)S(1)}, bf16[16,193,128]{2,0,1:T(8,128)(2,1)S(1)}, u32[]{:S(2)}, u32[]{:S(2)}) %collective-permute-start.10) | collective-permute-done | bytes 790560 | tf_op jit(solution)/shard_map/ppermute | solution.py:411
  59.0 1.7 %fusion.7 = (bf16[16,193,128]{2,1,0:T(8,128)(2,1)S(1)}, f32[16,193,128]{2,1,0:T(8,128)S(1)}) fusion(f32[16,193,128]{2,1,0:T(8,128)} %get-tuple-element.33, bf16[16,193,128]{2,0,1:T(8,128)(2,1)S(1)} %collective-permute-done.10), kind=kLoop, calls=%fused_computation.13 | loop fusion | flops 1185792 | bytes 4743168 | tf_op jit(solution)/shard_map/convert.5
  60.8 1.3 %collective-permute-start.13 = (bf16[4,193,128]{2,1,0:T(8,128)(2,1)S(1)}, bf16[4,193,128]{2,1,0:T(8,128)(2,1)S(1)}, u32[]{:S(2)}, u32[]{:S(2)}) collective-permute-start(bf16[4,193,128]{2,1,0:T(8,128)(2,1)S(1)} %get-tuple-element.40), channel_id=1, source_target_pairs={{0,6},{1,7},{2,4},{3,5},{4,2},{5,3},{6,0},{7,1},{8,14},{9,15},{10,... | collective-permute-start | bytes 592904 | tf_op jit(solution)/shard_map/ppermute | solution.py:411
  62.1 0.9 %collective-permute-start.12 = (bf16[4,193,128]{2,1,0:T(8,128)(2,1)S(1)}, bf16[4,193,128]{2,1,0:T(8,128)(2,1)S(1)}, u32[]{:S(2)}, u32[]{:S(2)}) collective-permute-start(bf16[4,193,128]{2,1,0:T(8,128)(2,1)S(1)} %get-tuple-element.41), channel_id=1, source_target_pairs={{0,4},{1,5},{2,6},{3,7},{4,0},{5,1},{6,2},{7,3},{8,12},{9,13},{10,... | collective-permute-start | bytes 592904 | tf_op jit(solution)/shard_map/ppermute | solution.py:411
  63.1 1.3 %collective-permute-start.11 = (bf16[4,193,128]{2,1,0:T(8,128)(2,1)S(1)}, bf16[4,193,128]{2,1,0:T(8,128)(2,1)S(1)}, u32[]{:S(2)}, u32[]{:S(2)}) collective-permute-start(bf16[4,193,128]{2,1,0:T(8,128)(2,1)S(1)} %get-tuple-element.39), channel_id=1, source_target_pairs={{0,2},{1,3},{2,0},{3,1},{4,6},{5,7},{6,4},{7,5},{8,10},{9,11},{10,... | collective-permute-start | bytes 592904 | tf_op jit(solution)/shard_map/ppermute | solution.py:411
  64.4 5.4 %collective-permute-done.13 = bf16[4,193,128]{2,1,0:T(8,128)(2,1)S(1)} collective-permute-done((bf16[4,193,128]{2,1,0:T(8,128)(2,1)S(1)}, bf16[4,193,128]{2,1,0:T(8,128)(2,1)S(1)}, u32[]{:S(2)}, u32[]{:S(2)}) %collective-permute-start.13) | collective-permute-done | bytes 197664 | tf_op jit(solution)/shard_map/ppermute | solution.py:411
  69.7 3.6 %collective-permute-done.12 = bf16[4,193,128]{2,1,0:T(8,128)(2,1)S(1)} collective-permute-done((bf16[4,193,128]{2,1,0:T(8,128)(2,1)S(1)}, bf16[4,193,128]{2,1,0:T(8,128)(2,1)S(1)}, u32[]{:S(2)}, u32[]{:S(2)}) %collective-permute-start.12) | collective-permute-done | bytes 197664 | tf_op jit(solution)/shard_map/ppermute | solution.py:411
  73.4 0.0 collective-permute-done.11
  73.4 0.1 fusion.5
  73.5 1.3 %collective-permute-start.16 = (bf16[193,128]{1,0:T(8,128)(2,1)S(1)}, bf16[193,128]{1,0:T(8,128)(2,1)S(1)}, u32[]{:S(2)}, u32[]{:S(2)}) collective-permute-start(bf16[193,128]{1,0:T(8,128)(2,1)S(1)} %get-tuple-element.43), channel_id=1, source_target_pairs={{0,24},{1,25},{2,26},{3,27},{4,28},{5,29},{6,30},{7,31},{8,0},{9,1... | collective-permute-start | bytes 148232 | tf_op jit(solution)/shard_map/ppermute | solution.py:411
  74.7 1.2 %collective-permute-start.15 = (bf16[193,128]{1,0:T(8,128)(2,1)S(1)}, bf16[193,128]{1,0:T(8,128)(2,1)S(1)}, u32[]{:S(2)}, u32[]{:S(2)}) collective-permute-start(bf16[193,128]{1,0:T(8,128)(2,1)S(1)} %get-tuple-element.44), channel_id=1, source_target_pairs={{0,16},{1,17},{2,18},{3,19},{4,20},{5,21},{6,22},{7,23},{8,24},{9,... | collective-permute-start | bytes 148232 | tf_op jit(solution)/shard_map/ppermute | solution.py:411
  76.0 1.9 %collective-permute-start.14 = (bf16[193,128]{1,0:T(8,128)(2,1)S(1)}, bf16[193,128]{1,0:T(8,128)(2,1)S(1)}, u32[]{:S(2)}, u32[]{:S(2)}) collective-permute-start(bf16[193,128]{1,0:T(8,128)(2,1)S(1)} %get-tuple-element.42), channel_id=1, source_target_pairs={{0,8},{1,9},{2,10},{3,11},{4,12},{5,13},{6,14},{7,15},{8,16},{9,17... | collective-permute-start | bytes 148232 | tf_op jit(solution)/shard_map/ppermute | solution.py:411
  77.9 0.0 collective-permute-done.16
  77.9 2.9 %collective-permute-done.15 = bf16[193,128]{1,0:T(8,128)(2,1)S(1)} collective-permute-done((bf16[193,128]{1,0:T(8,128)(2,1)S(1)}, bf16[193,128]{1,0:T(8,128)(2,1)S(1)}, u32[]{:S(2)}, u32[]{:S(2)}) %collective-permute-start.15) | collective-permute-done | bytes 49440 | tf_op jit(solution)/shard_map/ppermute | solution.py:411
  80.9 1.0 %collective-permute-done.14 = bf16[193,128]{1,0:T(8,128)(2,1)S(1)} collective-permute-done((bf16[193,128]{1,0:T(8,128)(2,1)S(1)}, bf16[193,128]{1,0:T(8,128)(2,1)S(1)}, u32[]{:S(2)}, u32[]{:S(2)}) %collective-permute-start.14) | collective-permute-done | bytes 49440 | tf_op jit(solution)/shard_map/ppermute | solution.py:411
  81.9 0.7 fusion.4
  (6 shorter events, 0.1 us)
Async XLA Ops:
  0.6 34.5 %copy-start.1 = (bf16[1024,256]{1,0:T(8,128)(2,1)S(1)}, bf16[1024,256]{1,0:T(8,128)(2,1)}, u32[]{:S(2)}) copy-start(bf16[1024,256]{1,0:T(8,128)(2,1)} %tok.5) | copy-start | bytes 1572868
  0.6 7.6 %collective-permute-start.2 = (bf16[193,128]{1,0:T(8,128)(2,1)}, bf16[193,128]{1,0:T(8,128)(2,1)S(1)}, u32[]{:S(2)}, u32[]{:S(2)}) collective-permute-start(bf16[193,128]{1,0:T(8,128)(2,1)} %param.5), channel_id=1, source_target_pairs={{0,24},{1,25},{2,26},{3,27},{4,28},{5,29},{6,30},{7,31},{8,0},{9,1... | collective-permute-start | bytes 148232 | tf_op jit(solution)/shard_map/ppermute | solution.py:411
  5.7 5.3 %collective-permute-start.1 = (bf16[193,128]{1,0:T(8,128)(2,1)}, bf16[193,128]{1,0:T(8,128)(2,1)S(1)}, u32[]{:S(2)}, u32[]{:S(2)}) collective-permute-start(bf16[193,128]{1,0:T(8,128)(2,1)} %param.5), channel_id=1, source_target_pairs={{0,16},{1,17},{2,18},{3,19},{4,20},{5,21},{6,22},{7,23},{8,24},{9,... | collective-permute-start | bytes 148232 | tf_op jit(solution)/shard_map/ppermute | solution.py:411
  5.7 6.1 %collective-permute-start = (bf16[193,128]{1,0:T(8,128)(2,1)}, bf16[193,128]{1,0:T(8,128)(2,1)S(1)}, u32[]{:S(2)}, u32[]{:S(2)}) collective-permute-start(bf16[193,128]{1,0:T(8,128)(2,1)} %param.5), channel_id=1, source_target_pairs={{0,8},{1,9},{2,10},{3,11},{4,12},{5,13},{6,14},{7,15},{8,16},{9,17... | collective-permute-start | bytes 148232 | tf_op jit(solution)/shard_map/ppermute | solution.py:411
  12.7 7.8 %collective-permute-start.3 = (bf16[4,193,128]{2,1,0:T(8,128)(2,1)S(1)}, bf16[4,193,128]{2,1,0:T(8,128)(2,1)S(1)}, u32[]{:S(2)}, u32[]{:S(2)}) collective-permute-start(bf16[4,193,128]{2,1,0:T(8,128)(2,1)S(1)} %pad_maximum_fusion.refs_0_), channel_id=1, source_target_pairs={{0,2},{1,3},{2,0},{3,1},{4,6},{5,7},{6,4},{7,5},{8,10},{9,11},{10,... | collective-permute-start | bytes 592904 | tf_op jit(solution)/shard_map/ppermute | solution.py:411
  14.3 9.7 %collective-permute-start.4 = (bf16[4,193,128]{2,1,0:T(8,128)(2,1)S(1)}, bf16[4,193,128]{2,1,0:T(8,128)(2,1)S(1)}, u32[]{:S(2)}, u32[]{:S(2)}) collective-permute-start(bf16[4,193,128]{2,1,0:T(8,128)(2,1)S(1)} %pad_maximum_fusion.refs_0_), channel_id=1, source_target_pairs={{0,4},{1,5},{2,6},{3,7},{4,0},{5,1},{6,2},{7,3},{8,12},{9,13},{10,... | collective-permute-start | bytes 592904 | tf_op jit(solution)/shard_map/ppermute | solution.py:411
  15.8 8.2 %collective-permute-start.5 = (bf16[4,193,128]{2,1,0:T(8,128)(2,1)S(1)}, bf16[4,193,128]{2,1,0:T(8,128)(2,1)S(1)}, u32[]{:S(2)}, u32[]{:S(2)}) collective-permute-start(bf16[4,193,128]{2,1,0:T(8,128)(2,1)S(1)} %pad_maximum_fusion.refs_0_), channel_id=1, source_target_pairs={{0,6},{1,7},{2,4},{3,5},{4,2},{5,3},{6,0},{7,1},{8,14},{9,15},{10,... | collective-permute-start | bytes 592904 | tf_op jit(solution)/shard_map/ppermute | solution.py:411
  16.3 8.5 %collective-permute-start.6 = (bf16[4,193,128]{2,1,0:T(8,128)(2,1)S(1)}, bf16[4,193,128]{2,1,0:T(8,128)(2,1)S(1)}, u32[]{:S(2)}, u32[]{:S(2)}) collective-permute-start(bf16[4,193,128]{2,1,0:T(8,128)(2,1)S(1)} %pad_maximum_fusion.refs_0_), channel_id=1, source_target_pairs={{0,1},{1,0},{2,3},{3,2},{4,5},{5,4},{6,7},{7,6},{8,9},{9,8},{10,11... | collective-permute-start | bytes 592904 | tf_op jit(solution)/shard_map/ppermute | solution.py:411
  20.6 4.2 %collective-permute-start.7 = (bf16[4,193,128]{2,1,0:T(8,128)(2,1)S(1)}, bf16[4,193,128]{2,1,0:T(8,128)(2,1)S(1)}, u32[]{:S(2)}, u32[]{:S(2)}) collective-permute-start(bf16[4,193,128]{2,1,0:T(8,128)(2,1)S(1)} %collective-permute-done.3.refs_1_), channel_id=1, source_target_pairs={{0,1},{1,0},{2,3},{3,2},{4,5},{5,4},{6,7},{7,6},{8,9},{9,8},{10,11... | collective-permute-start | bytes 592904 | tf_op jit(solution)/shard_map/ppermute | solution.py:411
  24.0 1.5 %collective-permute-start.8 = (bf16[4,193,128]{2,1,0:T(8,128)(2,1)S(1)}, bf16[4,193,128]{2,1,0:T(8,128)(2,1)S(1)}, u32[]{:S(2)}, u32[]{:S(2)}) collective-permute-start(bf16[4,193,128]{2,1,0:T(8,128)(2,1)S(1)} %collective-permute-done.4.refs_2_), channel_id=1, source_target_pairs={{0,1},{1,0},{2,3},{3,2},{4,5},{5,4},{6,7},{7,6},{8,9},{9,8},{10,11... | collective-permute-start | bytes 592904 | tf_op jit(solution)/shard_map/ppermute | solution.py:411
  24.0 1.7 %collective-permute-start.9 = (bf16[4,193,128]{2,1,0:T(8,128)(2,1)S(1)}, bf16[4,193,128]{2,1,0:T(8,128)(2,1)S(1)}, u32[]{:S(2)}, u32[]{:S(2)}) collective-permute-start(bf16[4,193,128]{2,1,0:T(8,128)(2,1)S(1)} %collective-permute-done.5.refs_3_), channel_id=1, source_target_pairs={{0,1},{1,0},{2,3},{3,2},{4,5},{5,4},{6,7},{7,6},{8,9},{9,8},{10,11... | collective-permute-start | bytes 592904 | tf_op jit(solution)/shard_map/ppermute | solution.py:411
  25.7 1.0 %copy-start = (bf16[1024,256]{1,0:T(8,128)(2,1)S(1)}, bf16[1024,256]{1,0:T(8,128)(2,1)}, u32[]{:S(2)}) copy-start(bf16[1024,256]{1,0:T(8,128)(2,1)} %tok.5) | copy-start | bytes 1572868
  26.8 0.7 copy-start.3
  27.4 7.7 %copy-start.2 = (bf16[1024,256]{1,0:T(8,128)(2,1)S(1)}, bf16[1024,256]{1,0:T(8,128)(2,1)}, u32[]{:S(2)}) copy-start(bf16[1024,256]{1,0:T(8,128)(2,1)} %cot.1) | copy-start | bytes 1572868
  56.7 2.4 %collective-permute-start.10 = (bf16[16,193,128]{2,0,1:T(8,128)(2,1)S(1)}, bf16[16,193,128]{2,0,1:T(8,128)(2,1)S(1)}, u32[]{:S(2)}, u32[]{:S(2)}) collective-permute-start(bf16[16,193,128]{2,0,1:T(8,128)(2,1)S(1)} %copy.7), channel_id=1, source_target_pairs={{0,1},{1,0},{2,3},{3,2},{4,5},{5,4},{6,7},{7,6},{8,9},{9,8},{10,11... | collective-permute-start | bytes 2371592 | tf_op jit(solution)/shard_map/ppermute | solution.py:411
  60.8 8.9 %collective-permute-start.13 = (bf16[4,193,128]{2,1,0:T(8,128)(2,1)S(1)}, bf16[4,193,128]{2,1,0:T(8,128)(2,1)S(1)}, u32[]{:S(2)}, u32[]{:S(2)}) collective-permute-start(bf16[4,193,128]{2,1,0:T(8,128)(2,1)S(1)} %get-tuple-element.40), channel_id=1, source_target_pairs={{0,6},{1,7},{2,4},{3,5},{4,2},{5,3},{6,0},{7,1},{8,14},{9,15},{10,... | collective-permute-start | bytes 592904 | tf_op jit(solution)/shard_map/ppermute | solution.py:411
  62.1 11.2 %collective-permute-start.12 = (bf16[4,193,128]{2,1,0:T(8,128)(2,1)S(1)}, bf16[4,193,128]{2,1,0:T(8,128)(2,1)S(1)}, u32[]{:S(2)}, u32[]{:S(2)}) collective-permute-start(bf16[4,193,128]{2,1,0:T(8,128)(2,1)S(1)} %get-tuple-element.41), channel_id=1, source_target_pairs={{0,4},{1,5},{2,6},{3,7},{4,0},{5,1},{6,2},{7,3},{8,12},{9,13},{10,... | collective-permute-start | bytes 592904 | tf_op jit(solution)/shard_map/ppermute | solution.py:411
  63.1 10.3 %collective-permute-start.11 = (bf16[4,193,128]{2,1,0:T(8,128)(2,1)S(1)}, bf16[4,193,128]{2,1,0:T(8,128)(2,1)S(1)}, u32[]{:S(2)}, u32[]{:S(2)}) collective-permute-start(bf16[4,193,128]{2,1,0:T(8,128)(2,1)S(1)} %get-tuple-element.39), channel_id=1, source_target_pairs={{0,2},{1,3},{2,0},{3,1},{4,6},{5,7},{6,4},{7,5},{8,10},{9,11},{10,... | collective-permute-start | bytes 592904 | tf_op jit(solution)/shard_map/ppermute | solution.py:411
  73.5 4.4 %collective-permute-start.16 = (bf16[193,128]{1,0:T(8,128)(2,1)S(1)}, bf16[193,128]{1,0:T(8,128)(2,1)S(1)}, u32[]{:S(2)}, u32[]{:S(2)}) collective-permute-start(bf16[193,128]{1,0:T(8,128)(2,1)S(1)} %get-tuple-element.43), channel_id=1, source_target_pairs={{0,24},{1,25},{2,26},{3,27},{4,28},{5,29},{6,30},{7,31},{8,0},{9,1... | collective-permute-start | bytes 148232 | tf_op jit(solution)/shard_map/ppermute | solution.py:411
  74.7 6.1 %collective-permute-start.15 = (bf16[193,128]{1,0:T(8,128)(2,1)S(1)}, bf16[193,128]{1,0:T(8,128)(2,1)S(1)}, u32[]{:S(2)}, u32[]{:S(2)}) collective-permute-start(bf16[193,128]{1,0:T(8,128)(2,1)S(1)} %get-tuple-element.44), channel_id=1, source_target_pairs={{0,16},{1,17},{2,18},{3,19},{4,20},{5,21},{6,22},{7,23},{8,24},{9,... | collective-permute-start | bytes 148232 | tf_op jit(solution)/shard_map/ppermute | solution.py:411
  76.0 5.9 %collective-permute-start.14 = (bf16[193,128]{1,0:T(8,128)(2,1)S(1)}, bf16[193,128]{1,0:T(8,128)(2,1)S(1)}, u32[]{:S(2)}, u32[]{:S(2)}) collective-permute-start(bf16[193,128]{1,0:T(8,128)(2,1)S(1)} %get-tuple-element.42), channel_id=1, source_target_pairs={{0,8},{1,9},{2,10},{3,11},{4,12},{5,13},{6,14},{7,15},{8,16},{9,17... | collective-permute-start | bytes 148232 | tf_op jit(solution)/shard_map/ppermute | solution.py:411

commit v2 on v1

v2 whole, which is shorter than its diff:
```python
import functools

import jax
import jax.numpy as jnp
from jax import lax
from jax.experimental import pallas as pl
from jax.experimental.pallas import tpu as pltpu
from jax.sharding import PartitionSpec as P

D = 256
HEADS = 4
HEAD_DIM = 64
FF = 1024
SEQ = 128
LANES = 128
BLOCK = 2 * SEQ
EPSILON = 1e-05
SCALE = HEAD_DIM ** (-0.5)
VMEM_BYTES = 48 * 1024 * 1024

ROW_QKV = 0
ROW_OUT = 1536
ROW_UP = 2048
ROW_DOWN = 4096
ROW_SMALL = 6144
ROW_END = 6168
ROW_TOTAL = 6176
GAIN_ONE, SHIFT_ONE, BIAS_QUERY, BIAS_VALUE, BIAS_OUT = 0, 2, 4, 6, 8
GAIN_TWO, SHIFT_TWO, BIAS_UP, BIAS_DOWN = 10, 12, 14, 22
SMALL_ROWS = 32
LATE_SMALL = 8

SHARE = 193
Z, PLANE = 4, 4
FIRST_ROWS = 2 * PLANE * SHARE
HEAD_ROWS = FIRST_ROWS - ROW_OUT
SMALL_IN_SHARE = ROW_SMALL - (2 * PLANE * Z - 1) * SHARE
SIDE = 208

F32 = jnp.float32
BF16 = jnp.bfloat16


def dot(left, right):
    return jnp.dot(left, right, preferred_element_type=F32)


def dot_nt(left, right):
    return lax.dot_general(left, right, (((1,), (1,)), ((), ())), preferred_element_type=F32)


def dot_tn(left, right):
    return lax.dot_general(left, right, (((0,), (0,)), ((), ())), preferred_element_type=F32)


def small_vector(small, row, count):
    return jnp.concatenate([small[row + i : row + i + 1, :] for i in range(count)], axis=1)


def fold_rows(values):
    rows, columns = values.shape
    return jnp.sum(values.reshape(rows // 8, 8, columns), axis=0)


def normalize(values):
    center = values - jnp.mean(values, axis=-1, keepdims=True)
    rate = lax.rsqrt(jnp.mean(center * center, axis=-1, keepdims=True) + EPSILON)
    return center * rate, rate


def normalize_back(grad, gain, normed, rate):
    scaled = grad * gain
    return rate * (
        scaled
        - jnp.mean(scaled, axis=-1, keepdims=True)
        - normed * jnp.mean(scaled * normed, axis=-1, keepdims=True)
    )


def head_masks():
    lane = lax.broadcasted_iota(jnp.int32, (1, D), 1)
    return [(lane // HEAD_DIM == h).astype(F32).astype(BF16) for h in range(HEADS)]


def spread_heads(rows):
    return jnp.concatenate([rows * mask for mask in head_masks()], axis=0)


def matrix_from_flat(flat, start, rows, columns, out):
    per_row = columns // LANES
    for j in range(per_row):
        out[:, j * LANES : (j + 1) * LANES] = flat[
            pl.ds(start + j, rows, stride=per_row), :
        ].astype(BF16)


def matrix_to_flat(matrix, rows, columns, flat, start):
    per_row = columns // LANES
    for j in range(per_row):
        flat[pl.ds(start + j, rows, stride=per_row), :] = matrix[:, j * LANES : (j + 1) * LANES]


def place_shares(bufs, ids, flat, base):
    for slot, buf in enumerate(bufs):
        for z in range(Z - 1):
            share = ids[slot] + (z + 1) * 2 * PLANE
            flat[pl.ds(share * SHARE - base, SHARE), :] = buf[z].astype(F32)


def sort_kernel(ids, *refs):
    received, (first, rest, stage, wide) = refs[:Z], refs[Z:]
    for d in range(Z):
        stage[lax.rem(ids[0] + Z - d, Z)] = received[d][...]
    rest[...] = stage[1:]
    wide[:SHARE, :] = stage[0].astype(F32)
    wide[SHARE:SIDE, :] = jnp.zeros((SIDE - SHARE, LANES), F32)
    last = stage[Z - 1].astype(F32)
    wide[SIDE:, :] = last[SMALL_IN_SHARE:, :]
    first[...] = wide[...].astype(BF16)


def attend_kernel(
    ids, seg, tok, *refs,
):
    bufs = refs[: 2 * PLANE]
    project_out, weights_out, attended_out, w_qkv, small, first_out, flat = refs[2 * PLANE :]

    @pl.when(pl.program_id(0) == 0)
    def _():
        for slot, buf in enumerate(bufs):
            wide = buf[...].astype(F32)
            flat[pl.ds(ids[slot] * SHARE, SHARE), :] = wide[:SHARE, :]

            @pl.when(ids[slot] == 2 * PLANE - 1)
            def _():
                small[...] = wide[SIDE:, :]

        matrix_from_flat(flat, ROW_QKV, D, 3 * D, w_qkv)
        first_out[...] = flat[ROW_OUT:FIRST_ROWS, :]

    normed, _ = normalize(tok[...].astype(F32))
    normed_low = (
        normed * small_vector(small, GAIN_ONE, 2) + small_vector(small, SHIFT_ONE, 2)
    ).astype(BF16)
    bias = jnp.concatenate(
        [
            small_vector(small, BIAS_QUERY, 2),
            jnp.zeros((1, D), F32),
            small_vector(small, BIAS_VALUE, 2),
        ],
        axis=1,
    )
    project = (dot(normed_low, w_qkv[...]) + bias).astype(BF16)
    project_out[...] = project
    causal = lax.broadcasted_iota(jnp.int32, (SEQ, SEQ), 1) <= lax.broadcasted_iota(
        jnp.int32, (SEQ, SEQ), 0
    )
    for s in range(BLOCK // SEQ):
        rows = slice(s * SEQ, (s + 1) * SEQ)
        across = jnp.broadcast_to(seg[s].astype(F32), (SEQ, SEQ))
        allowed = causal & (across == across.T)
        query = project[rows, :D]
        key = spread_heads(project[rows, D : 2 * D])
        value = spread_heads(project[rows, 2 * D :])
        scores = dot_nt(query, key) * SCALE
        low = []
        for h in range(HEADS):
            columns = slice(h * SEQ, (h + 1) * SEQ)
            mine = jnp.where(allowed, scores[:, columns], -1e30)
            grown = jnp.exp(mine - jnp.max(mine, axis=-1, keepdims=True))
            weights = grown * (1.0 / jnp.sum(grown, axis=-1, keepdims=True))
            weights_out[rows, columns] = weights
            low.append(weights.astype(BF16))
        attended_out[rows, :] = dot(jnp.concatenate(low, axis=1), value).astype(BF16)


def feed_kernel(
    ids, tok, attended, cot, small, first_in, *refs,
):
    bufs = refs[: 2 * PLANE]
    (
        result_out, grad_middle_out, grad_attended_out, keep_out, send_out, first_out,
        w_out, w_up, w_down, acc_out, acc_up, acc_down, acc_small, flat,
    ) = refs[2 * PLANE :]
    step = pl.program_id(0)

    @pl.when(step == 0)
    def _():
        flat[:HEAD_ROWS, :] = first_in[...]
        place_shares(bufs, ids, flat, ROW_OUT)
        matrix_from_flat(flat, 0, D, D, w_out)
        matrix_from_flat(flat, ROW_UP - ROW_OUT, D, FF, w_up)
        matrix_from_flat(flat, ROW_DOWN - ROW_OUT, FF, D, w_down)
        acc_out[...] = jnp.zeros_like(acc_out)
        acc_up[...] = jnp.zeros_like(acc_up)
        acc_down[...] = jnp.zeros_like(acc_down)
        acc_small[...] = jnp.zeros_like(acc_small)

    gain = small_vector(small, GAIN_TWO, 2)
    middle = tok[...].astype(F32) + dot(attended[...], w_out[...]) + small_vector(small, BIAS_OUT, 2)
    normed, rate = normalize(middle)
    normed_low = (normed * gain + small_vector(small, SHIFT_TWO, 2)).astype(BF16)
    hidden = dot(normed_low, w_up[...]) + small_vector(small, BIAS_UP, 8)
    square = hidden * hidden
    slope = 0.7978845608028654
    bent = jnp.tanh(hidden * (slope + (slope * 0.044715) * square))
    half = 0.5 + 0.5 * bent
    activated = (hidden * half).astype(BF16)
    derivative = half + hidden * (0.5 - 0.5 * bent * bent) * (
        slope + (3 * slope * 0.044715) * square
    )
    result = middle + dot(activated, w_down[...]) + small_vector(small, BIAS_DOWN, 2)
    result_out[...] = result.astype(BF16)
    cotangent = cot[...]
    grad_result = cotangent.astype(F32)
    acc_down[...] += dot_tn(activated, cotangent)
    grad_hidden = (dot_nt(cotangent, w_down[...]) * derivative).astype(BF16)
    acc_up[...] += dot_tn(normed_low, grad_hidden)
    grad_normed = dot_nt(grad_hidden, w_up[...])
    grad_middle = grad_result + normalize_back(grad_normed, gain, normed, rate)
    grad_middle_out[...] = grad_middle
    grad_middle_low = grad_middle.astype(BF16)
    acc_out[...] += dot_tn(attended[...], grad_middle_low)
    grad_attended_out[...] = dot_nt(grad_middle_low, w_out[...]).astype(BF16)
    acc_small[:, 0:D] += fold_rows(grad_middle_low.astype(F32))
    acc_small[:, D : 2 * D] += fold_rows(grad_normed * normed)
    acc_small[:, 2 * D : 3 * D] += fold_rows(grad_normed)
    acc_small[:, 3 * D : 3 * D + FF] += fold_rows(grad_hidden.astype(F32))
    acc_small[:, 3 * D + FF :] += fold_rows(grad_result)

    @pl.when(step == pl.num_programs(0) - 1)
    def _():
        matrix_to_flat(acc_out, D, D, flat, 0)
        matrix_to_flat(acc_up, D, FF, flat, ROW_UP - ROW_OUT)
        matrix_to_flat(acc_down, FF, D, flat, ROW_DOWN - ROW_OUT)
        sums = jnp.sum(acc_small[...], axis=0, keepdims=True)
        base = ROW_SMALL - ROW_OUT
        flat[base : base + LATE_SMALL, :] = jnp.zeros((LATE_SMALL, LANES), F32)
        for i in range(sums.shape[1] // LANES):
            row = base + LATE_SMALL + i
            flat[row : row + 1, :] = sums[:, i * LANES : (i + 1) * LANES]
        flat[ROW_END - ROW_OUT :, :] = jnp.zeros((ROW_TOTAL - ROW_END, LANES), F32)
        first_out[...] = flat[:HEAD_ROWS, :]
        for target, out in enumerate((keep_out, send_out)):
            for p in range(PLANE):
                for z in range(Z - 1):
                    share = ids[target * PLANE + p] + (z + 1) * 2 * PLANE
                    rows = flat[pl.ds(share * SHARE - ROW_OUT, SHARE), :]
                    out[p, z] = rows.astype(out.dtype)


def attend_back_kernel(project, weights, grad_attended, grad_project):
    for s in range(BLOCK // SEQ):
        rows = slice(s * SEQ, (s + 1) * SEQ)
        query = spread_heads(project[rows, :D])
        key = spread_heads(project[rows, D : 2 * D])
        value = spread_heads(project[rows, 2 * D :])
        grad_rows = grad_attended[rows, :]
        grad_weights = dot_nt(grad_rows, value)
        scores_low, scores_turned, weights_turned = [], [], []
        for h in range(HEADS):
            columns = slice(h * SEQ, (h + 1) * SEQ)
            mine = weights[rows, columns]
            product = mine * grad_weights[:, columns]
            grad_scores = product - mine * jnp.sum(product, axis=-1, keepdims=True)
            scores_low.append(grad_scores.astype(BF16))
            scores_turned.append(grad_scores.T.astype(BF16))
            weights_turned.append(mine.T.astype(BF16))
        grad_query = dot(jnp.concatenate(scores_low, axis=1), key) * SCALE
        grad_key = dot(jnp.concatenate(scores_turned, axis=1), query) * SCALE
        grad_value = dot(jnp.concatenate(weights_turned, axis=1), spread_heads(grad_rows))
        grad_project[rows, :D] = grad_query.astype(BF16)
        grad_project[rows, D : 2 * D] = grad_key.astype(BF16)
        grad_project[rows, 2 * D :] = grad_value.astype(BF16)

def project_back_kernel(
    ids, tok, grad_project, grad_middle, w_qkv, small, first_in,
    input_grad_out, keep_out, send_out, acc_qkv, acc_small, flat,
):
    step = pl.program_id(0)

    @pl.when(step == 0)
    def _():
        acc_qkv[...] = jnp.zeros_like(acc_qkv)
        acc_small[...] = jnp.zeros_like(acc_small)

    gain = small_vector(small, GAIN_ONE, 2)
    normed, rate = normalize(tok[...].astype(F32))
    normed_low = (normed * gain + small_vector(small, SHIFT_ONE, 2)).astype(BF16)
    acc_qkv[...] += dot_tn(normed_low, grad_project[...])
    grad_normed = dot_nt(grad_project[...], w_qkv[...])
    input_grad_out[...] = grad_middle[...] + normalize_back(grad_normed, gain, normed, rate)
    acc_small[:, 0:D] += fold_rows(grad_normed * normed)
    acc_small[:, D : 2 * D] += fold_rows(grad_normed)
    acc_small[:, 2 * D : 3 * D] += fold_rows(grad_project[:, :D].astype(F32))
    acc_small[:, 3 * D :] += fold_rows(grad_project[:, 2 * D :].astype(F32))

    @pl.when(step == pl.num_programs(0) - 1)
    def _():
        matrix_to_flat(acc_qkv, D, 3 * D, flat, ROW_QKV)
        flat[ROW_OUT:, :] = first_in[...]
        sums = jnp.sum(acc_small[...], axis=0, keepdims=True)
        side = jnp.concatenate(
            [sums[:, i * LANES : (i + 1) * LANES] for i in range(LATE_SMALL)]
            + [jnp.zeros((16 - LATE_SMALL, LANES), F32)],
            axis=0,
        )
        for target, out in enumerate((keep_out, send_out)):
            for p in range(PLANE):
                share = ids[target * PLANE + p]
                rows = flat[pl.ds(share * SHARE, SHARE), :]
                padded = jnp.concatenate([rows, jnp.zeros((SIDE - SHARE, LANES), F32)], axis=0)
                mine = jnp.where(share == 2 * PLANE - 1, side, 0.0)
                out[p] = jnp.concatenate([padded, mine], axis=0).astype(out.dtype)


def add_core_kernel(kept, received, keep_out, *sends):
    keep_out[...] = kept[0] + received[0].astype(F32)
    for p, out in enumerate(sends):
        out[...] = (kept[p + 1] + received[p + 1].astype(F32)).astype(BF16)


def add_plane_kernel(ids, first_kept, rest_kept, *refs):
    firsts, rests = refs[: PLANE - 1], refs[PLANE - 1 : 2 * (PLANE - 1)]
    keep_out, *sends, first, column = refs[2 * (PLANE - 1) :]
    first[...] = first_kept[...] + sum(item[...].astype(F32) for item in firsts)
    column[0] = first[:SHARE, :]
    column[1:] = rest_kept[...] + sum(item[...].astype(F32) for item in rests)
    end = SMALL_IN_SHARE + LATE_SMALL
    column[Z - 1, SMALL_IN_SHARE:end, :] += first[SIDE : SIDE + LATE_SMALL, :]
    keep_out[...] = column[ids[0]]
    for d, out in enumerate(sends):
        out[...] = column[lax.rem(ids[0] + d + 1, Z)].astype(BF16)


def rows_spec(columns):
    return pl.BlockSpec((BLOCK, columns), lambda i: (i, 0))


def whole_spec(item):
    return pl.BlockSpec(item.shape, lambda i: (0,) * len(item.shape))


def like(*shape, kind=F32):
    return jax.ShapeDtypeStruct(shape, kind)


SMEM_SPEC = pl.BlockSpec(memory_space=pltpu.SMEM)
PARAMS = pltpu.CompilerParams(
    dimension_semantics=("arbitrary",), vmem_limit_bytes=VMEM_BYTES
)


def cost(us):
    return pl.CostEstimate(flops=int(us * 1e9), bytes_accessed=1 << 20, transcendentals=0)


def small_call(kernel, name, ids, inputs, outs, scratch=()):
    with_ids = ids is not None
    return pl.pallas_call(
        kernel,
        in_specs=[SMEM_SPEC] * with_ids + [pl.BlockSpec(memory_space=pltpu.VMEM)] * len(inputs),
        out_specs=[pl.BlockSpec(memory_space=pltpu.VMEM)] * len(outs),
        out_shape=list(outs),
        scratch_shapes=list(scratch),
        compiler_params=pltpu.CompilerParams(vmem_limit_bytes=VMEM_BYTES),
        cost_estimate=cost(1),
        name=name,
    )(*([ids] if with_ids else []), *inputs)


def attend(ids, segments, tokens, bufs):
    rows = tokens.shape[0]
    blocked = [like(rows, 3 * D, kind=BF16), like(rows, HEADS * SEQ), like(rows, D, kind=BF16)]
    fixed = [like(D, 3 * D, kind=BF16), like(SMALL_ROWS, LANES), like(HEAD_ROWS, LANES)]
    return pl.pallas_call(
        attend_kernel,
        grid=(rows // BLOCK,),
        in_specs=[
            SMEM_SPEC,
            pl.BlockSpec((BLOCK // SEQ, 1, SEQ), lambda i: (i, 0, 0)),
            rows_spec(D),
        ]
        + [whole_spec(buf) for buf in bufs],
        out_specs=[rows_spec(item.shape[1]) for item in blocked] + [whole_spec(item) for item in fixed],
        out_shape=blocked + fixed,
        scratch_shapes=[pltpu.VMEM((FIRST_ROWS, LANES), F32)],
        compiler_params=PARAMS,
        cost_estimate=cost(7),
        name="attend",
    )(ids, segments, tokens, *bufs)


def feed(ids, tokens, attended, cotangent, small, first, bufs, send_kind):
    rows = tokens.shape[0]
    small_rows = ROW_END - ROW_SMALL - LATE_SMALL
    blocked = [like(rows, D, kind=BF16), like(rows, D), like(rows, D, kind=BF16)]
    fixed = [
        like(PLANE, Z - 1, SHARE, LANES),
        like(PLANE, Z - 1, SHARE, LANES, kind=send_kind),
        like(HEAD_ROWS, LANES),
    ]
    return pl.pallas_call(
        feed_kernel,
        grid=(rows // BLOCK,),
        in_specs=[SMEM_SPEC] + [rows_spec(D)] * 3 + [whole_spec(item) for item in (small, first, *bufs)],
        out_specs=[rows_spec(D)] * 3 + [whole_spec(item) for item in fixed],
        out_shape=blocked + fixed,
        scratch_shapes=[
            pltpu.VMEM((D, D), BF16),
            pltpu.VMEM((D, FF), BF16),
            pltpu.VMEM((FF, D), BF16),
            pltpu.VMEM((D, D), F32),
            pltpu.VMEM((D, FF), F32),
            pltpu.VMEM((FF, D), F32),
            pltpu.VMEM((8, small_rows * LANES), F32),
            pltpu.VMEM((ROW_TOTAL - ROW_OUT, LANES), F32),
        ],
        compiler_params=PARAMS,
        cost_estimate=cost(10),
        name="feed",
    )(ids, tokens, attended, cotangent, small, first, *bufs)


def attend_back(project, weights, grad_attended):
    return pl.pallas_call(
        attend_back_kernel,
        grid=(project.shape[0] // BLOCK,),
        in_specs=[rows_spec(item.shape[1]) for item in (project, weights, grad_attended)],
        out_specs=rows_spec(3 * D),
        out_shape=like(*project.shape, kind=BF16),
        compiler_params=PARAMS,
        cost_estimate=cost(6),
        name="attend_back",
    )(project, weights, grad_attended)


def project_back(ids, tokens, grad_project, grad_middle, w_qkv, small, first, send_kind):
    rows = tokens.shape[0]
    fixed = [
        like(PLANE, SIDE + 16, LANES),
        like(PLANE, SIDE + 16, LANES, kind=send_kind),
    ]
    return pl.pallas_call(
        project_back_kernel,
        grid=(rows // BLOCK,),
        in_specs=[SMEM_SPEC]
        + [rows_spec(item.shape[1]) for item in (tokens, grad_project, grad_middle)]
        + [whole_spec(item) for item in (w_qkv, small, first)],
        out_specs=[rows_spec(D)] + [whole_spec(item) for item in fixed],
        out_shape=[like(rows, D)] + fixed,
        scratch_shapes=[
            pltpu.VMEM((D, 3 * D), F32),
            pltpu.VMEM((8, LATE_SMALL * LANES), F32),
            pltpu.VMEM((FIRST_ROWS, LANES), F32),
        ],
        compiler_params=PARAMS,
        cost_estimate=cost(6),
        name="project_back",
    )(ids, tokens, grad_project, grad_middle, w_qkv, small, first)


def local_any(n, tokens, params, segment_ids, cotangent):
    total = n * params.shape[0]
    gathered = lax.all_gather(params, "fsdp", axis=0).reshape(total, LANES)
    shares = gathered[:ROW_TOTAL].reshape(Z, 2 * PLANE, SHARE, LANES)
    order = [p * 2 + c for c in range(2) for p in range(PLANE)]
    side = jnp.concatenate(
        [jnp.zeros((SIDE - SHARE, LANES), BF16), gathered[ROW_SMALL:ROW_TOTAL]], axis=0
    )
    firsts = [jnp.concatenate([shares[0, k], side], axis=0) for k in order]
    rests = [shares[1:, k] for k in order]
    ids = jnp.array(order, jnp.int32)
    segments = segment_ids.reshape(-1, 1, SEQ)
    project, weights, attended, w_qkv, small, first = attend(ids, segments, tokens, firsts)
    outputs, grad_middle, grad_attended, rest_keep, rest_send, first_grad = feed(
        ids, tokens, attended, cotangent, small, first, rests, F32
    )
    grad_project = attend_back(project, weights, grad_attended)
    input_grad, keep, send = project_back(
        ids, tokens, grad_project, grad_middle, w_qkv, small, first_grad, F32
    )
    first = jnp.stack([keep, send], axis=1)
    rest = jnp.stack([rest_keep, rest_send], axis=1).transpose(2, 0, 1, 3, 4)
    flat = jnp.concatenate(
        [
            first[:, :, :SHARE].reshape(-1, LANES),
            rest.reshape(-1, LANES),
            jnp.zeros((total - ROW_TOTAL, LANES), F32),
        ],
        axis=0,
    )
    flat = flat.at[ROW_SMALL : ROW_SMALL + LATE_SMALL].add(
        first[PLANE - 1, 1, SIDE : SIDE + LATE_SMALL]
    )
    param_grad = lax.psum_scatter(flat, "fsdp", scatter_dimension=0, tiled=True)
    return outputs, input_grad, param_grad


def index_of(z, plane, core):
    return (z * PLANE + plane) * 2 + core


def move(values, step_z, step_plane, step_core):
    pairs = [
        (index_of(z, p, c), index_of((z + step_z) % Z, p ^ step_plane, c ^ step_core))
        for z in range(Z)
        for p in range(PLANE)
        for c in range(2)
    ]
    return lax.ppermute(values, "fsdp", pairs)


def spread(values):
    same = [values] + [move(values, 0, d, 0) for d in range(1, PLANE)]
    return same + [move(item, 0, 0, 1) for item in same]


def add_core(keep, send):
    item = keep.shape[1:]
    return small_call(
        add_core_kernel, "add_core", None, [keep, move(send, 0, 0, 1)],
        [like(*item)] + [like(*item, kind=BF16)] * (PLANE - 1),
    )


def add_plane(where, first, rest):
    arrived = [move(item, 0, d + 1, 0) for items in (first, rest) for d, item in enumerate(items[1:])]
    return small_call(
        add_plane_kernel, "add_plane", where, [first[0], rest[0]] + arrived,
        [like(SHARE, LANES)] + [like(SHARE, LANES, kind=BF16)] * (Z - 1),
        [pltpu.VMEM((SIDE + 16, LANES), F32), pltpu.VMEM((Z, SHARE, LANES), F32)],
    )


def local_slice(tokens, params, segment_ids, cotangent):
    me = lax.axis_index("fsdp").astype(jnp.int32)
    z, plane, core = me // (2 * PLANE), (me // 2) % PLANE, me % 2
    where = z.reshape(1)
    ids = jnp.stack([(plane ^ dp) * 2 + (core ^ dc) for dc in range(2) for dp in range(PLANE)])
    segments = segment_ids.reshape(-1, 1, SEQ)

    column = [params] + [move(params, d, 0, 0) for d in range(1, Z)]
    first, rest = small_call(
        sort_kernel, "sort_shares", where, column,
        [like(SIDE + SMALL_ROWS, LANES, kind=BF16), like(Z - 1, SHARE, LANES, kind=BF16)],
        [pltpu.VMEM((Z, SHARE, LANES), BF16), pltpu.VMEM((SIDE + SMALL_ROWS, LANES), F32)],
    )
    project, weights, attended, w_qkv, small, first = attend(ids, segments, tokens, spread(first))
    outputs, grad_middle, grad_attended, rest_keep, rest_send, first_grad = feed(
        ids, tokens, attended, cotangent, small, first, spread(rest), BF16
    )

    rest_sums = add_core(rest_keep, rest_send)
    grad_project = attend_back(project, weights, grad_attended)
    input_grad, keep, send = project_back(
        ids, tokens, grad_project, grad_middle, w_qkv, small, first_grad, BF16
    )
    first_sums = add_core(keep, send)
    param_grad, *sends = add_plane(where, first_sums, rest_sums)
    for d, item in enumerate(sends):
        param_grad = param_grad + move(item, d + 1, 0, 0).astype(F32)
    return outputs, input_grad, param_grad


def solution(mesh):
    n = mesh.shape["fsdp"]
    local = local_slice if n == 2 * PLANE * Z else functools.partial(local_any, n)
    in_specs = (P("fsdp", None), P("fsdp", None), P("fsdp"), P("fsdp", None))
    out_specs = (P("fsdp", None), P("fsdp", None), P("fsdp", None))
    return jax.shard_map(local, mesh=mesh, in_specs=in_specs, out_specs=out_specs, check_vma=False)
```

time: 82.9 us -> 81.2 us (0.979)
  starting transfers between devices: 18.5 us -> 26.3 us
  waiting for transfers between devices: 28.8 us -> 25.4 us
  other arithmetic: 3.3 us -> 0.67 us
  Pallas kernels: 29.1 us -> 26.7 us
  local copies, waits for them, and re-layouts: 2.13 us -> 1.22 us
    ppermute x17 -> x28, starting transfers between devices: 18.5 us -> 26.3 us  [move(): return lax.ppermute(values, 'fsdp', pairs)]
    ppermute x17 -> x28, waiting for transfers between devices: 28.8 us -> 25.4 us  [move(): return lax.ppermute(values, 'fsdp', pairs)]
    another operation x3 -> x0, other arithmetic: 2.63 us -> none
    pallas_call x3 -> x8, Pallas kernels: 29.1 us -> 26.7 us  [the longest x1 11.3 us: feed(): pl.pallas_call(feed_kernel, grid=(rows // BLOCK,), in_specs=[SMEM_SPEC] +...]
    unnamed x8 -> x10, local copies, waits for them, and re-layouts: 1.74 us -> 0.82 us
  transfers between devices with their start and end apart: 17 -> 28, of which waited for: 12 -> 10; matrix products, arithmetic and copies ran while one was open for 0% -> 0% of each run, Pallas kernels for 0% -> 19%
where the time goes in v2:
time: 81.2 us; the launch traced here: 81.1 us
  Pallas kernels  26.7 us (33%)
  starting transfers between devices  26.3 us (32%)
  waiting for transfers between devices  25.4 us (31%)
  local copies, waits for them, and re-layouts  1.22 us (2%)
    ppermute x28, starting transfers between devices, move(): return lax.ppermute(values, 'fsdp', pairs)  26.3 us
    ppermute x28, waiting for transfers between devices, move(): return lax.ppermute(values, 'fsdp', pairs)  25.4 us
    pallas_call x1, Pallas kernels, feed(): pl.pallas_call(feed_kernel, grid=(rows // BLOCK,), in_specs=[SMEM_SPEC] +...  11.3 us
    pallas_call x1, Pallas kernels, attend(): pl.pallas_call(attend_kernel, grid=(rows // BLOCK,), in_specs=[SMEM_SPEC,...  6.4 us
    pallas_call x1, Pallas kernels, project_back(): pl.pallas_call(project_back_kernel, grid=(rows // BLOCK,), in_specs=[SMEM...  4.33 us
    pallas_call x1, Pallas kernels, attend_back(): pl.pallas_call(attend_back_kernel, grid=(project.shape[0] // BLOCK,), in_...  4.26 us
  transfers between devices with their start and end apart: 28, of which 10 were waited for; matrix products, arithmetic and copies ran while one was open for 0% of the time, Pallas kernels for 19%

profile of v2, /device:TPU:0, one launch (start us, length us, event | category | flops | bytes accessed | tf_op | source)
XLA Modules:
  0.0 81.1 jit_solution(15148891419684850039)
XLA Ops:
  0.6 4.1 %collective-permute-start.1 = (bf16[193,128]{1,0:T(8,128)(2,1)}, bf16[193,128]{1,0:T(8,128)(2,1)S(1)}, u32[]{:S(2)}, u32[]{:S(2)}) collective-permute-start(bf16[193,128]{1,0:T(8,128)(2,1)} %refs_0_.1), channel_id=1, source_target_pairs={{0,16},{1,17},{2,18},{3,19},{4,20},{5,21},{6,22},{7,23},{8,24},{9,... | collective-permute-start | bytes 148232 | tf_op jit(solution)/shard_map/ppermute | solution.py:511
  4.7 1.6 %collective-permute-start = (bf16[193,128]{1,0:T(8,128)(2,1)}, bf16[193,128]{1,0:T(8,128)(2,1)S(1)}, u32[]{:S(2)}, u32[]{:S(2)}) collective-permute-start(bf16[193,128]{1,0:T(8,128)(2,1)} %refs_0_.1), channel_id=1, source_target_pairs={{0,8},{1,9},{2,10},{3,11},{4,12},{5,13},{6,14},{7,15},{8,16},{9,17... | collective-permute-start | bytes 148232 | tf_op jit(solution)/shard_map/ppermute | solution.py:511
  6.3 2.2 %collective-permute-start.2 = (bf16[193,128]{1,0:T(8,128)(2,1)}, bf16[193,128]{1,0:T(8,128)(2,1)S(1)}, u32[]{:S(2)}, u32[]{:S(2)}) collective-permute-start(bf16[193,128]{1,0:T(8,128)(2,1)} %refs_0_.1), channel_id=1, source_target_pairs={{0,24},{1,25},{2,26},{3,27},{4,28},{5,29},{6,30},{7,31},{8,0},{9,1... | collective-permute-start | bytes 148232 | tf_op jit(solution)/shard_map/ppermute | solution.py:511
  8.6 2.4 %collective-permute-done.refs_1_ = bf16[193,128]{1,0:T(8,128)(2,1)S(1)} collective-permute-done((bf16[193,128]{1,0:T(8,128)(2,1)}, bf16[193,128]{1,0:T(8,128)(2,1)S(1)}, u32[]{:S(2)}, u32[]{:S(2)}) %collective-permute-start) | collective-permute-done | bytes 49440 | tf_op jit(solution)/shard_map/ppermute | solution.py:511
  11.0 0.2 collective-permute-done.2.refs_3_
  11.2 0.8 copy-done.2
  12.0 0.1 collective-permute-start.6
  12.1 2.5 %collective-permute-start.5 = (bf16[240,128]{1,0:T(8,128)(2,1)S(1)}, bf16[240,128]{1,0:T(8,128)(2,1)S(1)}, u32[]{:S(2)}, u32[]{:S(2)}) collective-permute-start(bf16[240,128]{1,0:T(8,128)(2,1)S(1)} %get-tuple-element.32.refs_0_), channel_id=1, source_target_pairs={{0,6},{1,7},{2,4},{3,5},{4,2},{5,3},{6,0},{7,1},{8,14},{9,15},{10,... | collective-permute-start | bytes 184328 | tf_op jit(solution)/shard_map/ppermute | solution.py:511
  14.6 0.5 collective-permute-start.4
  15.1 1.5 %collective-permute-start.12 = (bf16[3,193,128]{2,1,0:T(8,128)(2,1)S(1)}, bf16[3,193,128]{2,1,0:T(8,128)(2,1)S(1)}, u32[]{:S(2)}, u32[]{:S(2)}) collective-permute-start(bf16[3,193,128]{2,1,0:T(8,128)(2,1)S(1)} %get-tuple-element.36.refs_0_), channel_id=1, source_target_pairs={{0,6},{1,7},{2,4},{3,5},{4,2},{5,3},{6,0},{7,1},{8,14},{9,15},{10,... | collective-permute-start | bytes 444680 | tf_op jit(solution)/shard_map/ppermute | solution.py:511
  16.6 0.5 collective-permute-start.11
  17.1 1.5 %collective-permute-start.10 = (bf16[3,193,128]{2,1,0:T(8,128)(2,1)S(1)}, bf16[3,193,128]{2,1,0:T(8,128)(2,1)S(1)}, u32[]{:S(2)}, u32[]{:S(2)}) collective-permute-start(bf16[3,193,128]{2,1,0:T(8,128)(2,1)S(1)} %get-tuple-element.36.refs_0_), channel_id=1, source_target_pairs={{0,2},{1,3},{2,0},{3,1},{4,6},{5,7},{6,4},{7,5},{8,10},{9,11},{10,... | collective-permute-start | bytes 444680 | tf_op jit(solution)/shard_map/ppermute | solution.py:511
  18.6 0.5 collective-permute-start.3
  19.2 2.8 %collective-permute-done.4.refs_2_ = bf16[240,128]{1,0:T(8,128)(2,1)S(1)} collective-permute-done((bf16[240,128]{1,0:T(8,128)(2,1)S(1)}, bf16[240,128]{1,0:T(8,128)(2,1)S(1)}, u32[]{:S(2)}, u32[]{:S(2)}) %collective-permute-start.4) | collective-permute-done | bytes 61472 | tf_op jit(solution)/shard_map/ppermute | solution.py:511
  22.0 4.6 %collective-permute-done.3.refs_1_ = bf16[240,128]{1,0:T(8,128)(2,1)S(1)} collective-permute-done((bf16[240,128]{1,0:T(8,128)(2,1)S(1)}, bf16[240,128]{1,0:T(8,128)(2,1)S(1)}, u32[]{:S(2)}, u32[]{:S(2)}) %collective-permute-start.3) | collective-permute-done | bytes 61472 | tf_op jit(solution)/shard_map/ppermute | solution.py:511
  26.5 0.5 collective-permute-start.7
  27.0 0.1 stack.35.ids
  27.1 0.6 collective-permute-done.8.refs_6_
  27.8 0.2 collective-permute-start.13
  27.9 0.4 collective-permute-start.16
  28.3 0.2 collective-permute-start.15
  28.4 0.4 collective-permute-start.14
  28.8 0.0 copy-start
  28.8 6.4 %attend.1 = (bf16[1024,768]{1,0:T(8,128)(2,1)S(1)}, f32[1024,512]{1,0:T(8,128)S(1)}, bf16[1024,256]{1,0:T(8,128)(2,1)S(1)}, bf16[256,768]{1,0:T(8,128)(2,1)S(1)}...) custom-call(s32[8]{0:T(128)S(1)} %stack.35.ids, s32[8,1,128]{2,1,0:T(1,128)S(1)} %bitcast.10, ...), custom_call_target="tpu_custom_call" | custom-call | flops 7000000000 | bytes 1048576 | tf_op jit(solution)/shard_map/attend/pallas_call | solution.py:376
  35.3 11.3 %feed.1 = (bf16[1024,256]{1,0:T(8,128)(2,1)}, f32[1024,256]{1,0:T(8,128)S(1)}, bf16[1024,256]{1,0:T(8,128)(2,1)S(1)}, f32[4,3,193,128]{3,2,1,0:T(8,128)}, bf16[4...) custom-call(s32[8]{0:T(128)S(1)} %stack.35.ids, bf16[1024,256]{1,0:T(8,128)(2,1)S(1)} %copy-done.1, ...), custom_call_target="tpu_custom_call" | custom-call | flops 10000000000 | bytes 1048576 | tf_op jit(solution)/shard_map/feed/pallas_call | solution.py:403
  46.6 0.2 copy.7
  46.8 0.2 collective-permute-start.18
  47.0 4.3 %attend_back.1.grad_project = bf16[1024,768]{1,0:T(8,128)(2,1)S(1)} custom-call(bf16[1024,768]{1,0:T(8,128)(2,1)S(1)} %get-tuple-element.38.project, f32[1024,512]{1,0:T(8,128)S(1)} %get-tuple-element.39.weights, bf16[1024,256]{1,0:T(8,128)(2,1)S(1)} %get-tuple-element.40.grad_attended), custom_call_target="tpu_custom_call" | custom-call | flops 6000000000 | bytes 1048576 | tf_op jit(solution)/shard_map/attend_back/pallas_call | solution.py:426
  51.3 4.3 %project_back.1 = (f32[1024,256]{1,0:T(8,128)}, f32[4,224,128]{2,1,0:T(8,128)S(1)}, bf16[4,224,128]{2,1,0:T(8,128)(2,1)S(1)}) custom-call(s32[8]{0:T(128)S(1)} %stack.35.ids, bf16[1024,256]{1,0:T(8,128)(2,1)S(1)} %copy-done.1, bf16[1024,768]{1,0:T(8,128)(2,1)S(1)} %attend_back.1.grad_project, f32[1024,256]{1,0:T(8,128)S(1)} %get-tuple-element.41.grad_middle, ...), custom_call_target="tpu_custom_call" | custom-call | flops 6000000000 | bytes 1048576 | tf_op jit(solution)/shard_map/project_back/pallas_call | solution.py:444
  55.6 0.4 collective-permute-start.17
  56.0 0.1 copy.8.received
  56.1 0.1 add_core.3
  56.2 0.5 collective-permute-start.22
  56.8 0.5 collective-permute-start.23
  57.3 2.5 %collective-permute-start.24 = (bf16[3,193,128]{2,1,0:T(8,128)(2,1)S(1)}, bf16[3,193,128]{2,1,0:T(8,128)(2,1)S(1)}, u32[]{:S(2)}, u32[]{:S(2)}) collective-permute-start(bf16[3,193,128]{2,1,0:T(8,128)(2,1)S(1)} %get-tuple-element.56), channel_id=1, source_target_pairs={{0,6},{1,7},{2,4},{3,5},{4,2},{5,3},{6,0},{7,1},{8,14},{9,15},{10,... | collective-permute-start | bytes 444680 | tf_op jit(solution)/shard_map/ppermute | solution.py:511
  59.8 0.1 add_core.2
  59.9 0.5 collective-permute-start.19
  60.4 0.5 collective-permute-start.20
  60.9 6.0 %collective-permute-done.19.refs_0_ = bf16[224,128]{1,0:T(8,128)(2,1)S(1)} collective-permute-done((bf16[224,128]{1,0:T(8,128)(2,1)S(1)}, bf16[224,128]{1,0:T(8,128)(2,1)S(1)}, u32[]{:S(2)}, u32[]{:S(2)}) %collective-permute-start.19) | collective-permute-done | bytes 57376 | tf_op jit(solution)/shard_map/ppermute | solution.py:511
  66.9 0.4 collective-permute-start.21
  67.4 4.6 %collective-permute-done.21.refs_2_ = bf16[224,128]{1,0:T(8,128)(2,1)S(1)} collective-permute-done((bf16[224,128]{1,0:T(8,128)(2,1)S(1)}, bf16[224,128]{1,0:T(8,128)(2,1)S(1)}, u32[]{:S(2)}, u32[]{:S(2)}) %collective-permute-start.21) | collective-permute-done | bytes 57376 | tf_op jit(solution)/shard_map/ppermute | solution.py:511
  72.0 0.2 add_plane.1
  72.2 0.1 collective-permute-start.25
  72.2 4.0 %collective-permute-start.26 = (bf16[193,128]{1,0:T(8,128)(2,1)S(1)}, bf16[193,128]{1,0:T(8,128)(2,1)S(1)}, u32[]{:S(2)}, u32[]{:S(2)}) collective-permute-start(bf16[193,128]{1,0:T(8,128)(2,1)S(1)} %get-tuple-element.59), channel_id=1, source_target_pairs={{0,16},{1,17},{2,18},{3,19},{4,20},{5,21},{6,22},{7,23},{8,24},{9,... | collective-permute-start | bytes 148232 | tf_op jit(solution)/shard_map/ppermute | solution.py:511
  76.3 1.9 %collective-permute-done.25 = bf16[193,128]{1,0:T(8,128)(2,1)S(1)} collective-permute-done((bf16[193,128]{1,0:T(8,128)(2,1)S(1)}, bf16[193,128]{1,0:T(8,128)(2,1)S(1)}, u32[]{:S(2)}, u32[]{:S(2)}) %collective-permute-start.25) | collective-permute-done | bytes 49440 | tf_op jit(solution)/shard_map/ppermute | solution.py:511
  78.2 1.1 %collective-permute-done.26 = bf16[193,128]{1,0:T(8,128)(2,1)S(1)} collective-permute-done((bf16[193,128]{1,0:T(8,128)(2,1)S(1)}, bf16[193,128]{1,0:T(8,128)(2,1)S(1)}, u32[]{:S(2)}, u32[]{:S(2)}) %collective-permute-start.26) | collective-permute-done | bytes 49440 | tf_op jit(solution)/shard_map/ppermute | solution.py:511
  79.2 1.2 %collective-permute-done.27 = bf16[193,128]{1,0:T(8,128)(2,1)S(1)} collective-permute-done((bf16[193,128]{1,0:T(8,128)(2,1)S(1)}, bf16[193,128]{1,0:T(8,128)(2,1)S(1)}, u32[]{:S(2)}, u32[]{:S(2)}) %collective-permute-start.27) | collective-permute-done | bytes 49440 | tf_op jit(solution)/shard_map/ppermute | solution.py:511
  80.4 0.7 convert_add_fusion
  (30 shorter events, 0.1 us)
Async XLA Ops:
  0.6 7.9 %collective-permute-start.1 = (bf16[193,128]{1,0:T(8,128)(2,1)}, bf16[193,128]{1,0:T(8,128)(2,1)S(1)}, u32[]{:S(2)}, u32[]{:S(2)}) collective-permute-start(bf16[193,128]{1,0:T(8,128)(2,1)} %refs_0_.1), channel_id=1, source_target_pairs={{0,16},{1,17},{2,18},{3,19},{4,20},{5,21},{6,22},{7,23},{8,24},{9,... | collective-permute-start | bytes 148232 | tf_op jit(solution)/shard_map/ppermute | solution.py:511
  4.7 6.2 %collective-permute-start = (bf16[193,128]{1,0:T(8,128)(2,1)}, bf16[193,128]{1,0:T(8,128)(2,1)S(1)}, u32[]{:S(2)}, u32[]{:S(2)}) collective-permute-start(bf16[193,128]{1,0:T(8,128)(2,1)} %refs_0_.1), channel_id=1, source_target_pairs={{0,8},{1,9},{2,10},{3,11},{4,12},{5,13},{6,14},{7,15},{8,16},{9,17... | collective-permute-start | bytes 148232 | tf_op jit(solution)/shard_map/ppermute | solution.py:511
  6.3 4.9 %collective-permute-start.2 = (bf16[193,128]{1,0:T(8,128)(2,1)}, bf16[193,128]{1,0:T(8,128)(2,1)S(1)}, u32[]{:S(2)}, u32[]{:S(2)}) collective-permute-start(bf16[193,128]{1,0:T(8,128)(2,1)} %refs_0_.1), channel_id=1, source_target_pairs={{0,24},{1,25},{2,26},{3,27},{4,28},{5,29},{6,30},{7,31},{8,0},{9,1... | collective-permute-start | bytes 148232 | tf_op jit(solution)/shard_map/ppermute | solution.py:511
  11.2 0.8 copy-start.2
  12.0 16.8 %copy-start.1 = (bf16[1024,256]{1,0:T(8,128)(2,1)S(1)}, bf16[1024,256]{1,0:T(8,128)(2,1)}, u32[]{:S(2)}) copy-start(bf16[1024,256]{1,0:T(8,128)(2,1)} %tok.5) | copy-start | bytes 1572868
  12.0 16.8 %copy-start.3 = (s32[1024]{0:T(1024)S(1)}, s32[1024]{0:T(1024)}, u32[]{:S(2)}) copy-start(s32[1024]{0:T(1024)} %param.6) | copy-start | bytes 12292
  12.0 5.1 %collective-permute-start.6 = (bf16[240,128]{1,0:T(8,128)(2,1)S(1)}, bf16[240,128]{1,0:T(8,128)(2,1)S(1)}, u32[]{:S(2)}, u32[]{:S(2)}) collective-permute-start(bf16[240,128]{1,0:T(8,128)(2,1)S(1)} %get-tuple-element.32.refs_0_), channel_id=1, source_target_pairs={{0,1},{1,0},{2,3},{3,2},{4,5},{5,4},{6,7},{7,6},{8,9},{9,8},{10,11... | collective-permute-start | bytes 184328 | tf_op jit(solution)/shard_map/ppermute | solution.py:511
  12.1 6.5 %collective-permute-start.5 = (bf16[240,128]{1,0:T(8,128)(2,1)S(1)}, bf16[240,128]{1,0:T(8,128)(2,1)S(1)}, u32[]{:S(2)}, u32[]{:S(2)}) collective-permute-start(bf16[240,128]{1,0:T(8,128)(2,1)S(1)} %get-tuple-element.32.refs_0_), channel_id=1, source_target_pairs={{0,6},{1,7},{2,4},{3,5},{4,2},{5,3},{6,0},{7,1},{8,14},{9,15},{10,... | collective-permute-start | bytes 184328 | tf_op jit(solution)/shard_map/ppermute | solution.py:511
  14.6 7.3 %collective-permute-start.4 = (bf16[240,128]{1,0:T(8,128)(2,1)S(1)}, bf16[240,128]{1,0:T(8,128)(2,1)S(1)}, u32[]{:S(2)}, u32[]{:S(2)}) collective-permute-start(bf16[240,128]{1,0:T(8,128)(2,1)S(1)} %get-tuple-element.32.refs_0_), channel_id=1, source_target_pairs={{0,4},{1,5},{2,6},{3,7},{4,0},{5,1},{6,2},{7,3},{8,12},{9,13},{10,... | collective-permute-start | bytes 184328 | tf_op jit(solution)/shard_map/ppermute | solution.py:511
  15.1 12.8 %collective-permute-start.12 = (bf16[3,193,128]{2,1,0:T(8,128)(2,1)S(1)}, bf16[3,193,128]{2,1,0:T(8,128)(2,1)S(1)}, u32[]{:S(2)}, u32[]{:S(2)}) collective-permute-start(bf16[3,193,128]{2,1,0:T(8,128)(2,1)S(1)} %get-tuple-element.36.refs_0_), channel_id=1, source_target_pairs={{0,6},{1,7},{2,4},{3,5},{4,2},{5,3},{6,0},{7,1},{8,14},{9,15},{10,... | collective-permute-start | bytes 444680 | tf_op jit(solution)/shard_map/ppermute | solution.py:511
  16.6 11.7 %collective-permute-start.11 = (bf16[3,193,128]{2,1,0:T(8,128)(2,1)S(1)}, bf16[3,193,128]{2,1,0:T(8,128)(2,1)S(1)}, u32[]{:S(2)}, u32[]{:S(2)}) collective-permute-start(bf16[3,193,128]{2,1,0:T(8,128)(2,1)S(1)} %get-tuple-element.36.refs_0_), channel_id=1, source_target_pairs={{0,4},{1,5},{2,6},{3,7},{4,0},{5,1},{6,2},{7,3},{8,12},{9,13},{10,... | collective-permute-start | bytes 444680 | tf_op jit(solution)/shard_map/ppermute | solution.py:511
  17.1 11.3 %collective-permute-start.10 = (bf16[3,193,128]{2,1,0:T(8,128)(2,1)S(1)}, bf16[3,193,128]{2,1,0:T(8,128)(2,1)S(1)}, u32[]{:S(2)}, u32[]{:S(2)}) collective-permute-start(bf16[3,193,128]{2,1,0:T(8,128)(2,1)S(1)} %get-tuple-element.36.refs_0_), channel_id=1, source_target_pairs={{0,2},{1,3},{2,0},{3,1},{4,6},{5,7},{6,4},{7,5},{8,10},{9,11},{10,... | collective-permute-start | bytes 444680 | tf_op jit(solution)/shard_map/ppermute | solution.py:511
  18.6 7.9 %collective-permute-start.3 = (bf16[240,128]{1,0:T(8,128)(2,1)S(1)}, bf16[240,128]{1,0:T(8,128)(2,1)S(1)}, u32[]{:S(2)}, u32[]{:S(2)}) collective-permute-start(bf16[240,128]{1,0:T(8,128)(2,1)S(1)} %get-tuple-element.32.refs_0_), channel_id=1, source_target_pairs={{0,2},{1,3},{2,0},{3,1},{4,6},{5,7},{6,4},{7,5},{8,10},{9,11},{10,... | collective-permute-start | bytes 184328 | tf_op jit(solution)/shard_map/ppermute | solution.py:511
  22.0 4.6 %collective-permute-start.9 = (bf16[240,128]{1,0:T(8,128)(2,1)S(1)}, bf16[240,128]{1,0:T(8,128)(2,1)S(1)}, u32[]{:S(2)}, u32[]{:S(2)}) collective-permute-start(bf16[240,128]{1,0:T(8,128)(2,1)S(1)} %collective-permute-done.5.refs_3_), channel_id=1, source_target_pairs={{0,1},{1,0},{2,3},{3,2},{4,5},{5,4},{6,7},{7,6},{8,9},{9,8},{10,11... | collective-permute-start | bytes 184328 | tf_op jit(solution)/shard_map/ppermute | solution.py:511
  26.5 1.2 %collective-permute-start.8 = (bf16[240,128]{1,0:T(8,128)(2,1)S(1)}, bf16[240,128]{1,0:T(8,128)(2,1)S(1)}, u32[]{:S(2)}, u32[]{:S(2)}) collective-permute-start(bf16[240,128]{1,0:T(8,128)(2,1)S(1)} %collective-permute-done.4.refs_2_), channel_id=1, source_target_pairs={{0,1},{1,0},{2,3},{3,2},{4,5},{5,4},{6,7},{7,6},{8,9},{9,8},{10,11... | collective-permute-start | bytes 184328 | tf_op jit(solution)/shard_map/ppermute | solution.py:511
  26.5 2.3 %collective-permute-start.7 = (bf16[240,128]{1,0:T(8,128)(2,1)S(1)}, bf16[240,128]{1,0:T(8,128)(2,1)S(1)}, u32[]{:S(2)}, u32[]{:S(2)}) collective-permute-start(bf16[240,128]{1,0:T(8,128)(2,1)S(1)} %collective-permute-done.3.refs_1_), channel_id=1, source_target_pairs={{0,1},{1,0},{2,3},{3,2},{4,5},{5,4},{6,7},{7,6},{8,9},{9,8},{10,11... | collective-permute-start | bytes 184328 | tf_op jit(solution)/shard_map/ppermute | solution.py:511
  27.8 7.5 %collective-permute-start.13 = (bf16[3,193,128]{2,1,0:T(8,128)(2,1)S(1)}, bf16[3,193,128]{2,1,0:T(8,128)(2,1)S(1)}, u32[]{:S(2)}, u32[]{:S(2)}) collective-permute-start(bf16[3,193,128]{2,1,0:T(8,128)(2,1)S(1)} %get-tuple-element.36.refs_0_), channel_id=1, source_target_pairs={{0,1},{1,0},{2,3},{3,2},{4,5},{5,4},{6,7},{7,6},{8,9},{9,8},{10,11... | collective-permute-start | bytes 444680 | tf_op jit(solution)/shard_map/ppermute | solution.py:511
  27.9 7.3 %collective-permute-start.16 = (bf16[3,193,128]{2,1,0:T(8,128)(2,1)S(1)}, bf16[3,193,128]{2,1,0:T(8,128)(2,1)S(1)}, u32[]{:S(2)}, u32[]{:S(2)}) collective-permute-start(bf16[3,193,128]{2,1,0:T(8,128)(2,1)S(1)} %collective-permute-done.12.refs_3_), channel_id=1, source_target_pairs={{0,1},{1,0},{2,3},{3,2},{4,5},{5,4},{6,7},{7,6},{8,9},{9,8},{10,11... | collective-permute-start | bytes 444680 | tf_op jit(solution)/shard_map/ppermute | solution.py:511
  28.3 7.0 %collective-permute-start.15 = (bf16[3,193,128]{2,1,0:T(8,128)(2,1)S(1)}, bf16[3,193,128]{2,1,0:T(8,128)(2,1)S(1)}, u32[]{:S(2)}, u32[]{:S(2)}) collective-permute-start(bf16[3,193,128]{2,1,0:T(8,128)(2,1)S(1)} %collective-permute-done.11.refs_2_), channel_id=1, source_target_pairs={{0,1},{1,0},{2,3},{3,2},{4,5},{5,4},{6,7},{7,6},{8,9},{9,8},{10,11... | collective-permute-start | bytes 444680 | tf_op jit(solution)/shard_map/ppermute | solution.py:511
  28.4 6.8 %collective-permute-start.14 = (bf16[3,193,128]{2,1,0:T(8,128)(2,1)S(1)}, bf16[3,193,128]{2,1,0:T(8,128)(2,1)S(1)}, u32[]{:S(2)}, u32[]{:S(2)}) collective-permute-start(bf16[3,193,128]{2,1,0:T(8,128)(2,1)S(1)} %collective-permute-done.10.refs_1_), channel_id=1, source_target_pairs={{0,1},{1,0},{2,3},{3,2},{4,5},{5,4},{6,7},{7,6},{8,9},{9,8},{10,11... | collective-permute-start | bytes 444680 | tf_op jit(solution)/shard_map/ppermute | solution.py:511
  28.8 6.5 %copy-start = (bf16[1024,256]{1,0:T(8,128)(2,1)S(1)}, bf16[1024,256]{1,0:T(8,128)(2,1)}, u32[]{:S(2)}) copy-start(bf16[1024,256]{1,0:T(8,128)(2,1)} %cot.1) | copy-start | bytes 1572868
  46.8 9.2 %collective-permute-start.18 = (bf16[4,3,193,128]{3,0,2,1:T(4,128)(2,1)S(1)}, bf16[4,3,193,128]{3,0,2,1:T(4,128)(2,1)S(1)}, u32[]{:S(2)}, u32[]{:S(2)}) collective-permute-start(bf16[4,3,193,128]{3,0,2,1:T(4,128)(2,1)S(1)} %copy.7), channel_id=1, source_target_pairs={{0,1},{1,0},{2,3},{3,2},{4,5},{5,4},{6,7},{7,6},{8,9},{9,8},{10,11... | collective-permute-start | bytes 1778696 | tf_op jit(solution)/shard_map/ppermute | solution.py:511
  51.3 4.8 %copy-start.4 = (f32[4,3,193,128]{3,2,1,0:T(8,128)S(1)}, f32[4,3,193,128]{3,2,1,0:T(8,128)}, u32[]{:S(2)}) copy-start(f32[4,3,193,128]{3,2,1,0:T(8,128)} %get-tuple-element.48.kept) | copy-start | bytes 3557380
  55.6 4.2 %collective-permute-start.17 = (bf16[4,224,128]{2,1,0:T(8,128)(2,1)S(1)}, bf16[4,224,128]{2,1,0:T(8,128)(2,1)S(1)}, u32[]{:S(2)}, u32[]{:S(2)}) collective-permute-start(bf16[4,224,128]{2,1,0:T(8,128)(2,1)S(1)} %get-tuple-element.46), channel_id=1, source_target_pairs={{0,1},{1,0},{2,3},{3,2},{4,5},{5,4},{6,7},{7,6},{8,9},{9,8},{10,11... | collective-permute-start | bytes 688136 | tf_op jit(solution)/shard_map/ppermute | solution.py:511
  56.2 15.7 %collective-permute-start.22 = (bf16[3,193,128]{2,1,0:T(8,128)(2,1)S(1)}, bf16[3,193,128]{2,1,0:T(8,128)(2,1)S(1)}, u32[]{:S(2)}, u32[]{:S(2)}) collective-permute-start(bf16[3,193,128]{2,1,0:T(8,128)(2,1)S(1)} %get-tuple-element.54), channel_id=1, source_target_pairs={{0,2},{1,3},{2,0},{3,1},{4,6},{5,7},{6,4},{7,5},{8,10},{9,11},{10,... | collective-permute-start | bytes 444680 | tf_op jit(solution)/shard_map/ppermute | solution.py:511
  56.8 15.2 %collective-permute-start.23 = (bf16[3,193,128]{2,1,0:T(8,128)(2,1)S(1)}, bf16[3,193,128]{2,1,0:T(8,128)(2,1)S(1)}, u32[]{:S(2)}, u32[]{:S(2)}) collective-permute-start(bf16[3,193,128]{2,1,0:T(8,128)(2,1)S(1)} %get-tuple-element.55), channel_id=1, source_target_pairs={{0,4},{1,5},{2,6},{3,7},{4,0},{5,1},{6,2},{7,3},{8,12},{9,13},{10,... | collective-permute-start | bytes 444680 | tf_op jit(solution)/shard_map/ppermute | solution.py:511
  57.3 14.7 %collective-permute-start.24 = (bf16[3,193,128]{2,1,0:T(8,128)(2,1)S(1)}, bf16[3,193,128]{2,1,0:T(8,128)(2,1)S(1)}, u32[]{:S(2)}, u32[]{:S(2)}) collective-permute-start(bf16[3,193,128]{2,1,0:T(8,128)(2,1)S(1)} %get-tuple-element.56), channel_id=1, source_target_pairs={{0,6},{1,7},{2,4},{3,5},{4,2},{5,3},{6,0},{7,1},{8,14},{9,15},{10,... | collective-permute-start | bytes 444680 | tf_op jit(solution)/shard_map/ppermute | solution.py:511
  59.9 7.0 %collective-permute-start.19 = (bf16[224,128]{1,0:T(8,128)(2,1)S(1)}, bf16[224,128]{1,0:T(8,128)(2,1)S(1)}, u32[]{:S(2)}, u32[]{:S(2)}) collective-permute-start(bf16[224,128]{1,0:T(8,128)(2,1)S(1)} %get-tuple-element.51), channel_id=1, source_target_pairs={{0,2},{1,3},{2,0},{3,1},{4,6},{5,7},{6,4},{7,5},{8,10},{9,11},{10,... | collective-permute-start | bytes 172040 | tf_op jit(solution)/shard_map/ppermute | solution.py:511
  60.4 6.9 %collective-permute-start.20 = (bf16[224,128]{1,0:T(8,128)(2,1)S(1)}, bf16[224,128]{1,0:T(8,128)(2,1)S(1)}, u32[]{:S(2)}, u32[]{:S(2)}) collective-permute-start(bf16[224,128]{1,0:T(8,128)(2,1)S(1)} %get-tuple-element.52), channel_id=1, source_target_pairs={{0,4},{1,5},{2,6},{3,7},{4,0},{5,1},{6,2},{7,3},{8,12},{9,13},{10,... | collective-permute-start | bytes 172040 | tf_op jit(solution)/shard_map/ppermute | solution.py:511
  66.9 5.1 %collective-permute-start.21 = (bf16[224,128]{1,0:T(8,128)(2,1)S(1)}, bf16[224,128]{1,0:T(8,128)(2,1)S(1)}, u32[]{:S(2)}, u32[]{:S(2)}) collective-permute-start(bf16[224,128]{1,0:T(8,128)(2,1)S(1)} %get-tuple-element.53), channel_id=1, source_target_pairs={{0,6},{1,7},{2,4},{3,5},{4,2},{5,3},{6,0},{7,1},{8,14},{9,15},{10,... | collective-permute-start | bytes 172040 | tf_op jit(solution)/shard_map/ppermute | solution.py:511
  72.2 6.0 %collective-permute-start.25 = (bf16[193,128]{1,0:T(8,128)(2,1)S(1)}, bf16[193,128]{1,0:T(8,128)(2,1)S(1)}, u32[]{:S(2)}, u32[]{:S(2)}) collective-permute-start(bf16[193,128]{1,0:T(8,128)(2,1)S(1)} %get-tuple-element.58), channel_id=1, source_target_pairs={{0,8},{1,9},{2,10},{3,11},{4,12},{5,13},{6,14},{7,15},{8,16},{9,17... | collective-permute-start | bytes 148232 | tf_op jit(solution)/shard_map/ppermute | solution.py:511
  72.2 7.0 %collective-permute-start.26 = (bf16[193,128]{1,0:T(8,128)(2,1)S(1)}, bf16[193,128]{1,0:T(8,128)(2,1)S(1)}, u32[]{:S(2)}, u32[]{:S(2)}) collective-permute-start(bf16[193,128]{1,0:T(8,128)(2,1)S(1)} %get-tuple-element.59), channel_id=1, source_target_pairs={{0,16},{1,17},{2,18},{3,19},{4,20},{5,21},{6,22},{7,23},{8,24},{9,... | collective-permute-start | bytes 148232 | tf_op jit(solution)/shard_map/ppermute | solution.py:511
  76.3 4.1 %collective-permute-start.27 = (bf16[193,128]{1,0:T(8,128)(2,1)S(1)}, bf16[193,128]{1,0:T(8,128)(2,1)S(1)}, u32[]{:S(2)}, u32[]{:S(2)}) collective-permute-start(bf16[193,128]{1,0:T(8,128)(2,1)S(1)} %get-tuple-element.60), channel_id=1, source_target_pairs={{0,24},{1,25},{2,26},{3,27},{4,28},{5,29},{6,30},{7,31},{8,0},{9,1... | collective-permute-start | bytes 148232 | tf_op jit(solution)/shard_map/ppermute | solution.py:511

commit v3 on v2

--- a/solution.py
+++ b/solution.py
@@ -107,23 +107,21 @@
             flat[pl.ds(share * SHARE - base, SHARE), :] = buf[z].astype(F32)
 
 
-def sort_kernel(ids, *refs):
-    received, (first, rest, stage, wide) = refs[:Z], refs[Z:]
-    for d in range(Z):
-        stage[lax.rem(ids[0] + Z - d, Z)] = received[d][...]
-    rest[...] = stage[1:]
-    wide[:SHARE, :] = stage[0].astype(F32)
+def sort_kernel(column, first, rest, wide):
+    wide[:SHARE, :] = column[0].astype(F32)
     wide[SHARE:SIDE, :] = jnp.zeros((SIDE - SHARE, LANES), F32)
-    last = stage[Z - 1].astype(F32)
+    last = column[Z - 1].astype(F32)
     wide[SIDE:, :] = last[SMALL_IN_SHARE:, :]
-    first[...] = wide[...].astype(BF16)
+    for p in range(PLANE):
+        first[p] = wide[...].astype(BF16)
+        rest[p * (Z - 1) : (p + 1) * (Z - 1)] = column[1:]
 
 
 def attend_kernel(
     ids, seg, tok, *refs,
 ):
-    bufs = refs[: 2 * PLANE]
-    project_out, weights_out, attended_out, w_qkv, small, first_out, flat = refs[2 * PLANE :]
+    bufs = [ref.at[p] for ref in refs[:2] for p in range(PLANE)]
+    project_out, weights_out, attended_out, w_qkv, small, first_out, flat = refs[2:]
 
     @pl.when(pl.program_id(0) == 0)
     def _():
@@ -177,11 +175,11 @@
 def feed_kernel(
     ids, tok, attended, cot, small, first_in, *refs,
 ):
-    bufs = refs[: 2 * PLANE]
+    bufs = [ref.at[pl.ds(p * (Z - 1), Z - 1)] for ref in refs[:2] for p in range(PLANE)]
     (
         result_out, grad_middle_out, grad_attended_out, keep_out, send_out, first_out,
         w_out, w_up, w_down, acc_out, acc_up, acc_down, acc_small, flat,
-    ) = refs[2 * PLANE :]
+    ) = refs[2:]
     step = pl.program_id(0)
 
     @pl.when(step == 0)
@@ -246,7 +244,7 @@
                 for z in range(Z - 1):
                     share = ids[target * PLANE + p] + (z + 1) * 2 * PLANE
                     rows = flat[pl.ds(share * SHARE - ROW_OUT, SHARE), :]
-                    out[p, z] = rows.astype(out.dtype)
+                    out[p * (Z - 1) + z] = rows.astype(out.dtype)
 
 
 def attend_back_kernel(project, weights, grad_attended, grad_project):
@@ -314,23 +312,23 @@
                 out[p] = jnp.concatenate([padded, mine], axis=0).astype(out.dtype)
 
 
-def add_core_kernel(kept, received, keep_out, *sends):
-    keep_out[...] = kept[0] + received[0].astype(F32)
-    for p, out in enumerate(sends):
-        out[...] = (kept[p + 1] + received[p + 1].astype(F32)).astype(BF16)
-
-
-def add_plane_kernel(ids, first_kept, rest_kept, *refs):
-    firsts, rests = refs[: PLANE - 1], refs[PLANE - 1 : 2 * (PLANE - 1)]
-    keep_out, *sends, first, column = refs[2 * (PLANE - 1) :]
-    first[...] = first_kept[...] + sum(item[...].astype(F32) for item in firsts)
+def add_core_kernel(kept, received, out):
+    out[...] = (kept[...] + received[...].astype(F32)).astype(BF16)
+
+
+def add_plane_kernel(first_in, rest_in, out, first, column):
+    first[...] = sum(first_in[p].astype(F32) for p in range(PLANE))
     column[0] = first[:SHARE, :]
-    column[1:] = rest_kept[...] + sum(item[...].astype(F32) for item in rests)
+    column[1:] = sum(
+        rest_in[p * (Z - 1) : (p + 1) * (Z - 1)].astype(F32) for p in range(PLANE)
+    )
     end = SMALL_IN_SHARE + LATE_SMALL
     column[Z - 1, SMALL_IN_SHARE:end, :] += first[SIDE : SIDE + LATE_SMALL, :]
-    keep_out[...] = column[ids[0]]
-    for d, out in enumerate(sends):
-        out[...] = column[lax.rem(ids[0] + d + 1, Z)].astype(BF16)
+    out[...] = column[...].astype(BF16)
+
+
+def add_column_kernel(received, out):
+    out[...] = sum(received[z].astype(F32) for z in range(Z))
 
 
 def rows_spec(columns):
@@ -357,7 +355,7 @@
 
 def small_call(kernel, name, ids, inputs, outs, scratch=()):
     with_ids = ids is not None
-    return pl.pallas_call(
+    results = pl.pallas_call(
         kernel,
         in_specs=[SMEM_SPEC] * with_ids + [pl.BlockSpec(memory_space=pltpu.VMEM)] * len(inputs),
         out_specs=[pl.BlockSpec(memory_space=pltpu.VMEM)] * len(outs),
@@ -367,6 +365,7 @@
         cost_estimate=cost(1),
         name=name,
     )(*([ids] if with_ids else []), *inputs)
+    return results if len(outs) > 1 else results[0]
 
 
 def attend(ids, segments, tokens, bufs):
@@ -396,8 +395,8 @@
     small_rows = ROW_END - ROW_SMALL - LATE_SMALL
     blocked = [like(rows, D, kind=BF16), like(rows, D), like(rows, D, kind=BF16)]
     fixed = [
-        like(PLANE, Z - 1, SHARE, LANES),
-        like(PLANE, Z - 1, SHARE, LANES, kind=send_kind),
+        like(PLANE * (Z - 1), SHARE, LANES),
+        like(PLANE * (Z - 1), SHARE, LANES, kind=send_kind),
         like(HEAD_ROWS, LANES),
     ]
     return pl.pallas_call(
@@ -468,8 +467,11 @@
     side = jnp.concatenate(
         [jnp.zeros((SIDE - SHARE, LANES), BF16), gathered[ROW_SMALL:ROW_TOTAL]], axis=0
     )
-    firsts = [jnp.concatenate([shares[0, k], side], axis=0) for k in order]
-    rests = [shares[1:, k] for k in order]
+    firsts = [
+        jnp.stack([jnp.concatenate([shares[0, p * 2 + c], side], axis=0) for p in range(PLANE)])
+        for c in range(2)
+    ]
+    rests = [jnp.concatenate([shares[1:, p * 2 + c] for p in range(PLANE)]) for c in range(2)]
     ids = jnp.array(order, jnp.int32)
     segments = segment_ids.reshape(-1, 1, SEQ)
     project, weights, attended, w_qkv, small, first = attend(ids, segments, tokens, firsts)
@@ -481,7 +483,7 @@
         ids, tokens, grad_project, grad_middle, w_qkv, small, first_grad, F32
     )
     first = jnp.stack([keep, send], axis=1)
-    rest = jnp.stack([rest_keep, rest_send], axis=1).transpose(2, 0, 1, 3, 4)
+    rest = jnp.stack([rest_keep, rest_send]).reshape(2, PLANE, Z - 1, SHARE, LANES).transpose(2, 1, 0, 3, 4)
     flat = jnp.concatenate(
         [
             first[:, :, :SHARE].reshape(-1, LANES),
@@ -501,65 +503,61 @@
     return (z * PLANE + plane) * 2 + core
 
 
-def move(values, step_z, step_plane, step_core):
-    pairs = [
-        (index_of(z, p, c), index_of((z + step_z) % Z, p ^ step_plane, c ^ step_core))
-        for z in range(Z)
-        for p in range(PLANE)
-        for c in range(2)
-    ]
-    return lax.ppermute(values, "fsdp", pairs)
-
-
-def spread(values):
-    same = [values] + [move(values, 0, d, 0) for d in range(1, PLANE)]
-    return same + [move(item, 0, 0, 1) for item in same]
+COLUMNS = [[index_of(z, p, c) for z in range(Z)] for p in range(PLANE) for c in range(2)]
+PLANES = [[index_of(z, p, c) for p in range(PLANE)] for z in range(Z) for c in range(2)]
+CORES = [(index_of(z, p, c), index_of(z, p, 1 - c)) for z in range(Z) for p in range(PLANE) for c in range(2)]
+
+
+def exchange(values, groups):
+    return lax.all_to_all(values, "fsdp", 0, 0, axis_index_groups=groups, tiled=True)
+
+
+def other_core(values):
+    return lax.ppermute(values, "fsdp", CORES)
 
 
 def add_core(keep, send):
-    item = keep.shape[1:]
     return small_call(
-        add_core_kernel, "add_core", None, [keep, move(send, 0, 0, 1)],
-        [like(*item)] + [like(*item, kind=BF16)] * (PLANE - 1),
-    )
-
-
-def add_plane(where, first, rest):
-    arrived = [move(item, 0, d + 1, 0) for items in (first, rest) for d, item in enumerate(items[1:])]
-    return small_call(
-        add_plane_kernel, "add_plane", where, [first[0], rest[0]] + arrived,
-        [like(SHARE, LANES)] + [like(SHARE, LANES, kind=BF16)] * (Z - 1),
-        [pltpu.VMEM((SIDE + 16, LANES), F32), pltpu.VMEM((Z, SHARE, LANES), F32)],
+        add_core_kernel, "add_core", None, [keep, other_core(send)], [like(*keep.shape, kind=BF16)]
     )
 
 
 def local_slice(tokens, params, segment_ids, cotangent):
     me = lax.axis_index("fsdp").astype(jnp.int32)
-    z, plane, core = me // (2 * PLANE), (me // 2) % PLANE, me % 2
-    where = z.reshape(1)
-    ids = jnp.stack([(plane ^ dp) * 2 + (core ^ dc) for dc in range(2) for dp in range(PLANE)])
+    core = me % 2
+    ids = jnp.stack([p * 2 + (core ^ dc) for dc in range(2) for p in range(PLANE)])
     segments = segment_ids.reshape(-1, 1, SEQ)
 
-    column = [params] + [move(params, d, 0, 0) for d in range(1, Z)]
+    column = exchange(jnp.broadcast_to(params, (Z,) + params.shape), COLUMNS)
     first, rest = small_call(
-        sort_kernel, "sort_shares", where, column,
-        [like(SIDE + SMALL_ROWS, LANES, kind=BF16), like(Z - 1, SHARE, LANES, kind=BF16)],
-        [pltpu.VMEM((Z, SHARE, LANES), BF16), pltpu.VMEM((SIDE + SMALL_ROWS, LANES), F32)],
-    )
-    project, weights, attended, w_qkv, small, first = attend(ids, segments, tokens, spread(first))
-    outputs, grad_middle, grad_attended, rest_keep, rest_send, first_grad = feed(
-        ids, tokens, attended, cotangent, small, first, spread(rest), BF16
-    )
-
-    rest_sums = add_core(rest_keep, rest_send)
+        sort_kernel, "sort_shares", None, [column],
+        [like(PLANE, SIDE + SMALL_ROWS, LANES, kind=BF16), like(PLANE * (Z - 1), SHARE, LANES, kind=BF16)],
+        [pltpu.VMEM((SIDE + SMALL_ROWS, LANES), F32)],
+    )
+    first = exchange(first, PLANES)
+    rest = exchange(rest, PLANES)
+    project, weights, attended, w_qkv, small, first = attend(
+        ids, segments, tokens, [first, other_core(first)]
+    )
+    outputs, grad_middle, grad_attended, keep, send, first_grad = feed(
+        ids, tokens, attended, cotangent, small, first, [rest, other_core(rest)], BF16
+    )
+
     grad_project = attend_back(project, weights, grad_attended)
+    rest_sums, grad_project = lax.optimization_barrier((add_core(keep, send), grad_project))
+    rest_sums = exchange(rest_sums, PLANES)
     input_grad, keep, send = project_back(
         ids, tokens, grad_project, grad_middle, w_qkv, small, first_grad, BF16
     )
-    first_sums = add_core(keep, send)
-    param_grad, *sends = add_plane(where, first_sums, rest_sums)
-    for d, item in enumerate(sends):
-        param_grad = param_grad + move(item, d + 1, 0, 0).astype(F32)
+    first_sums = exchange(add_core(keep, send), PLANES)
+    column = small_call(
+        add_plane_kernel, "add_plane", None, [first_sums, rest_sums],
+        [like(Z, SHARE, LANES, kind=BF16)],
+        [pltpu.VMEM((SIDE + 16, LANES), F32), pltpu.VMEM((Z, SHARE, LANES), F32)],
+    )
+    param_grad = small_call(
+        add_column_kernel, "add_column", None, [exchange(column, COLUMNS)], [like(SHARE, LANES)]
+    )
     return outputs, input_grad, param_grad
 
 

time: 81.2 us -> 95.1 us (1.17)
  blocking collectives: 0 us -> 52.4 us
  starting transfers between devices: 26.3 us -> 4.07 us
  waiting for transfers between devices: 25.4 us -> 8.37 us
  Pallas kernels: 26.7 us -> 28.2 us
    all_to_all x0 -> x5, blocking collectives: none -> 52.4 us  [exchange(): lax.all_to_all(values, 'fsdp', 0, 0, axis_index_groups=groups, tiled=True)]
    ppermute x28 -> x4, starting transfers between devices: 26.3 us -> 0.59 us  [other_core(): return lax.ppermute(values, 'fsdp', CORES)]
    ppermute x28 -> x4, waiting for transfers between devices: 25.4 us -> 1.47 us  [other_core(): return lax.ppermute(values, 'fsdp', CORES)]
    all_to_all x0 -> x1, waiting for transfers between devices: none -> 6.89 us  [exchange(): lax.all_to_all(values, 'fsdp', 0, 0, axis_index_groups=groups, tiled=True)]
    all_to_all x0 -> x1, starting transfers between devices: none -> 3.48 us  [exchange(): lax.all_to_all(values, 'fsdp', 0, 0, axis_index_groups=groups, tiled=True)]
    pallas_call x4 -> x5, Pallas kernels: 0.42 us -> 1.93 us  [small_call(): pl.pallas_call(kernel, in_specs=[SMEM_SPEC] * with_ids + [pl.BlockSpec(me...]
  transfers between devices with their start and end apart: 28 -> 5, of which waited for: 10 -> 2; matrix products, arithmetic and copies ran while one was open for 0% -> 0% of each run, Pallas kernels for 19% -> 11%
where the time goes in v3:
time: 95.1 us; the launch traced here: 94.7 us
  blocking collectives  52.4 us (55%)
  Pallas kernels  28.2 us (30%)
  waiting for transfers between devices  8.37 us (9%)
  starting transfers between devices  4.07 us (4%)
    all_to_all x5, blocking collectives, exchange(): lax.all_to_all(values, 'fsdp', 0, 0, axis_index_groups=groups, tiled=True)  52.4 us
    pallas_call x1, Pallas kernels, feed(): pl.pallas_call(feed_kernel, grid=(rows // BLOCK,), in_specs=[SMEM_SPEC] +...  11.2 us
    all_to_all x1, waiting for transfers between devices, exchange(): lax.all_to_all(values, 'fsdp', 0, 0, axis_index_groups=groups, tiled=True)  6.89 us
    pallas_call x1, Pallas kernels, attend(): pl.pallas_call(attend_kernel, grid=(rows // BLOCK,), in_specs=[SMEM_SPEC,...  6.38 us
    pallas_call x1, Pallas kernels, project_back(): pl.pallas_call(project_back_kernel, grid=(rows // BLOCK,), in_specs=[SMEM...  4.36 us
    pallas_call x1, Pallas kernels, attend_back(): pl.pallas_call(attend_back_kernel, grid=(project.shape[0] // BLOCK,), in_...  4.28 us
    all_to_all x1, starting transfers between devices, exchange(): lax.all_to_all(values, 'fsdp', 0, 0, axis_index_groups=groups, tiled=True)  3.48 us
    pallas_call x5, Pallas kernels, small_call(): pl.pallas_call(kernel, in_specs=[SMEM_SPEC] * with_ids + [pl.BlockSpec(me...  1.93 us
  transfers between devices with their start and end apart: 5, of which 2 were waited for; matrix products, arithmetic and copies ran while one was open for 0% of the time, Pallas kernels for 11%

profile of v3, /device:TPU:0, one launch (start us, length us, event | category | flops | bytes accessed | tf_op | source)
XLA Modules:
  0.0 94.7 jit_solution(10811782005257305033)
XLA Ops:
  0.6 0.8 broadcast_in_dim.3
  1.5 13.8 %all_to_all.30.column = bf16[4,193,128]{2,1,0:T(8,128)(2,1)S(1)} all-to-all(bf16[4,193,128]{2,1,0:T(8,128)(2,1)S(1)} %broadcast_in_dim.3), channel_id=1, replica_groups={{0,8,16,24},{1,9,17,25},{2,10,18,26},{3,11,19,27},{4,12,20,28},{5,13,21..., dimensions={0} | all-to-all | bytes 395264 | tf_op jit(solution)/shard_map/all_to_all | solution.py:512
  15.2 0.9 sort_shares.1
  16.1 0.0 copy-start.1
  16.1 0.0 copy-start.2
  16.2 9.3 %all_to_all.31.refs_0_ = bf16[4,240,128]{2,1,0:T(8,128)(2,1)S(1)} all-to-all(bf16[4,240,128]{2,1,0:T(8,128)(2,1)S(1)} %get-tuple-element.22), channel_id=1, replica_groups={{0,2,4,6},{1,3,5,7},{8,10,12,14},{9,11,13,15},{16,18,20,22},{17,19,21,2..., dimensions={0} | all-to-all | bytes 491520 | tf_op jit(solution)/shard_map/all_to_all | solution.py:512
  25.5 3.5 %all-to-all-start.2 = ((bf16[12,193,128]{2,1,0:T(8,128)(2,1)}), bf16[12,193,128]{2,1,0:T(8,128)(2,1)S(1)}, u32[]{:S(2)}, u32[]{:S(2)}) async-start(bf16[12,193,128]{2,1,0:T(8,128)(2,1)} %get-tuple-element.26), calls=%async_computation.2 | async-start | bytes 1228800 | tf_op jit(solution)/shard_map/all_to_all | solution.py:512
  29.0 0.1 collective-permute-start
  29.0 0.1 stack.35.ids
  29.1 6.9 %all-to-all-done.2.refs_0_ = bf16[12,193,128]{2,1,0:T(8,128)(2,1)S(1)} async-done(((bf16[12,193,128]{2,1,0:T(8,128)(2,1)}), bf16[12,193,128]{2,1,0:T(8,128)(2,1)S(1)}, u32[]{:S(2)}, u32[]{:S(2)}) %all-to-all-start.2) | async-done | bytes 592928 | tf_op jit(solution)/shard_map/all_to_all | solution.py:512
  36.0 0.0 collective-permute-start.1
  36.0 0.0 collective-permute-done.refs_1_
  36.0 0.0 copy-done.1
  36.0 0.0 copy-done.2
  36.0 0.0 copy-start
  36.1 6.4 %attend.1 = (bf16[1024,768]{1,0:T(8,128)(2,1)S(1)}, f32[1024,512]{1,0:T(8,128)S(1)}, bf16[1024,256]{1,0:T(8,128)(2,1)S(1)}, bf16[256,768]{1,0:T(8,128)(2,1)S(1)}...) custom-call(s32[8]{0:T(128)S(1)} %stack.35.ids, s32[8,1,128]{2,1,0:T(1,128)S(1)} %bitcast.9, ...), custom_call_target="tpu_custom_call" | custom-call | flops 7000000000 | bytes 1048576 | tf_op jit(solution)/shard_map/attend/pallas_call | solution.py:375
  42.4 0.0 collective-permute-done.1.refs_1_
  42.5 0.0 copy-done
  42.5 11.2 %feed.1 = (bf16[1024,256]{1,0:T(8,128)(2,1)}, f32[1024,256]{1,0:T(8,128)S(1)}, bf16[1024,256]{1,0:T(8,128)(2,1)S(1)}, f32[12,193,128]{2,1,0:T(8,128)}, bf16[12,1...) custom-call(s32[8]{0:T(128)S(1)} %stack.35.ids, bf16[1024,256]{1,0:T(8,128)(2,1)S(1)} %copy-done.1, ...), custom_call_target="tpu_custom_call" | custom-call | flops 10000000000 | bytes 1048576 | tf_op jit(solution)/shard_map/feed/pallas_call | solution.py:402
  53.7 0.5 collective-permute-start.2
  54.2 0.0 copy-start.3
  54.2 4.3 %attend_back.1.grad_project = bf16[1024,768]{1,0:T(8,128)(2,1)S(1)} custom-call(bf16[1024,768]{1,0:T(8,128)(2,1)S(1)} %get-tuple-element.30.project, f32[1024,512]{1,0:T(8,128)S(1)} %get-tuple-element.31.weights, bf16[1024,256]{1,0:T(8,128)(2,1)S(1)} %get-tuple-element.32.grad_attended), custom_call_target="tpu_custom_call" | custom-call | flops 6000000000 | bytes 1048576 | tf_op jit(solution)/shard_map/attend_back/pallas_call | solution.py:425
  58.5 0.0 collective-permute-done.2.received
  58.5 0.0 copy-done.3
  58.5 0.1 add_core.2
  58.7 4.4 %project_back.1 = (f32[1024,256]{1,0:T(8,128)}, f32[4,224,128]{2,1,0:T(8,128)S(1)}, bf16[4,224,128]{2,1,0:T(8,128)(2,1)S(1)}) custom-call(s32[8]{0:T(128)S(1)} %stack.35.ids, bf16[1024,256]{1,0:T(8,128)(2,1)S(1)} %copy-done.1, bf16[1024,768]{1,0:T(8,128)(2,1)S(1)} %attend_back.1.grad_project, f32[1024,256]{1,0:T(8,128)S(1)} %get-tuple-element.34.grad_middle, ...), custom_call_target="tpu_custom_call" | custom-call | flops 6000000000 | bytes 1048576 | tf_op jit(solution)/shard_map/project_back/pallas_call | solution.py:443
  63.0 0.0 collective-permute-start.3
  63.0 1.5 %collective-permute-done.3.received = bf16[4,224,128]{2,1,0:T(8,128)(2,1)S(1)} collective-permute-done((bf16[4,224,128]{2,1,0:T(8,128)(2,1)S(1)}, bf16[4,224,128]{2,1,0:T(8,128)(2,1)S(1)}, u32[]{:S(2)}, u32[]{:S(2)}) %collective-permute-start.3) | collective-permute-done | bytes 229408 | tf_op jit(solution)/shard_map/ppermute | solution.py:516
  64.5 0.1 add_core.3
  64.6 8.4 %all_to_all.32.first_in = bf16[4,224,128]{2,1,0:T(8,128)(2,1)S(1)} all-to-all(bf16[4,224,128]{2,1,0:T(8,128)(2,1)S(1)} %add_core.3), channel_id=1, replica_groups={{0,2,4,6},{1,3,5,7},{8,10,12,14},{9,11,13,15},{16,18,20,22},{17,19,21,2..., dimensions={0} | all-to-all | bytes 458752 | tf_op jit(solution)/shard_map/all_to_all | solution.py:512
  73.0 11.0 %all_to_all.33.rest_in = bf16[12,193,128]{2,1,0:T(8,128)(2,1)S(1)} all-to-all(bf16[12,193,128]{2,1,0:T(8,128)(2,1)S(1)} %add_core.2), channel_id=1, replica_groups={{0,2,4,6},{1,3,5,7},{8,10,12,14},{9,11,13,15},{16,18,20,22},{17,19,21,2..., dimensions={0} | all-to-all | bytes 1185792 | tf_op jit(solution)/shard_map/all_to_all | solution.py:512
  84.0 0.1 add_plane.1
  84.2 9.8 %all_to_all.34.received = bf16[4,193,128]{2,1,0:T(8,128)(2,1)S(1)} all-to-all(bf16[4,193,128]{2,1,0:T(8,128)(2,1)S(1)} %add_plane.1), channel_id=1, replica_groups={{0,8,16,24},{1,9,17,25},{2,10,18,26},{3,11,19,27},{4,12,20,28},{5,13,21..., dimensions={0} | all-to-all | bytes 395264 | tf_op jit(solution)/shard_map/all_to_all | solution.py:512
  94.0 0.7 add_column.1
Async XLA Ops:
  16.1 19.9 %copy-start.1 = (bf16[1024,256]{1,0:T(8,128)(2,1)S(1)}, bf16[1024,256]{1,0:T(8,128)(2,1)}, u32[]{:S(2)}) copy-start(bf16[1024,256]{1,0:T(8,128)(2,1)} %tok.5) | copy-start | bytes 1572868
  16.1 19.9 %copy-start.2 = (s32[1024]{0:T(1024)S(1)}, s32[1024]{0:T(1024)}, u32[]{:S(2)}) copy-start(s32[1024]{0:T(1024)} %param.6) | copy-start | bytes 12292
  25.5 10.6 %all-to-all-start.2 = ((bf16[12,193,128]{2,1,0:T(8,128)(2,1)}), bf16[12,193,128]{2,1,0:T(8,128)(2,1)S(1)}, u32[]{:S(2)}, u32[]{:S(2)}) async-start(bf16[12,193,128]{2,1,0:T(8,128)(2,1)} %get-tuple-element.26), calls=%async_computation.2 | async-start | bytes 1228800 | tf_op jit(solution)/shard_map/all_to_all | solution.py:512
  29.0 7.1 %collective-permute-start = (bf16[4,240,128]{2,1,0:T(8,128)(2,1)S(1)}, bf16[4,240,128]{2,1,0:T(8,128)(2,1)S(1)}, u32[]{:S(2)}, u32[]{:S(2)}) collective-permute-start(bf16[4,240,128]{2,1,0:T(8,128)(2,1)S(1)} %all_to_all.31.refs_0_), channel_id=1, source_target_pairs={{0,1},{1,0},{2,3},{3,2},{4,5},{5,4},{6,7},{7,6},{8,9},{9,8},{10,11... | collective-permute-start | bytes 737288 | tf_op jit(solution)/shard_map/ppermute | solution.py:516
  36.0 6.4 %collective-permute-start.1 = (bf16[12,193,128]{2,1,0:T(8,128)(2,1)S(1)}, bf16[12,193,128]{2,1,0:T(8,128)(2,1)S(1)}, u32[]{:S(2)}, u32[]{:S(2)}) collective-permute-start(bf16[12,193,128]{2,1,0:T(8,128)(2,1)S(1)} %all-to-all-done.2.refs_0_), channel_id=1, source_target_pairs={{0,1},{1,0},{2,3},{3,2},{4,5},{5,4},{6,7},{7,6},{8,9},{9,8},{10,11... | collective-permute-start | bytes 1778696 | tf_op jit(solution)/shard_map/ppermute | solution.py:516
  36.0 6.4 %copy-start = (bf16[1024,256]{1,0:T(8,128)(2,1)S(1)}, bf16[1024,256]{1,0:T(8,128)(2,1)}, u32[]{:S(2)}) copy-start(bf16[1024,256]{1,0:T(8,128)(2,1)} %cot.1) | copy-start | bytes 1572868
  53.7 4.8 %collective-permute-start.2 = (bf16[12,193,128]{2,1,0:T(8,128)(2,1)S(1)}, bf16[12,193,128]{2,1,0:T(8,128)(2,1)S(1)}, u32[]{:S(2)}, u32[]{:S(2)}) collective-permute-start(bf16[12,193,128]{2,1,0:T(8,128)(2,1)S(1)} %get-tuple-element.29), channel_id=1, source_target_pairs={{0,1},{1,0},{2,3},{3,2},{4,5},{5,4},{6,7},{7,6},{8,9},{9,8},{10,11... | collective-permute-start | bytes 1778696 | tf_op jit(solution)/shard_map/ppermute | solution.py:516
  54.2 4.3 %copy-start.3 = (f32[12,193,128]{2,1,0:T(8,128)S(1)}, f32[12,193,128]{2,1,0:T(8,128)}, u32[]{:S(2)}) copy-start(f32[12,193,128]{2,1,0:T(8,128)} %get-tuple-element.28.kept) | copy-start | bytes 3557380
  63.0 1.5 %collective-permute-start.3 = (bf16[4,224,128]{2,1,0:T(8,128)(2,1)S(1)}, bf16[4,224,128]{2,1,0:T(8,128)(2,1)S(1)}, u32[]{:S(2)}, u32[]{:S(2)}) collective-permute-start(bf16[4,224,128]{2,1,0:T(8,128)(2,1)S(1)} %get-tuple-element.39), channel_id=1, source_target_pairs={{0,1},{1,0},{2,3},{3,2},{4,5},{5,4},{6,7},{7,6},{8,9},{9,8},{10,11... | collective-permute-start | bytes 688136 | tf_op jit(solution)/shard_map/ppermute | solution.py:516

commit v4 on v2

--- a/solution.py
+++ b/solution.py
@@ -177,11 +177,11 @@
 def feed_kernel(
     ids, tok, attended, cot, small, first_in, *refs,
 ):
-    bufs = refs[: 2 * PLANE]
+    bufs = [ref.at[pl.ds(p * (Z - 1), Z - 1)] for ref in refs[:2] for p in range(PLANE)]
     (
         result_out, grad_middle_out, grad_attended_out, keep_out, send_out, first_out,
         w_out, w_up, w_down, acc_out, acc_up, acc_down, acc_small, flat,
-    ) = refs[2 * PLANE :]
+    ) = refs[2:]
     step = pl.program_id(0)
 
     @pl.when(step == 0)
@@ -246,7 +246,7 @@
                 for z in range(Z - 1):
                     share = ids[target * PLANE + p] + (z + 1) * 2 * PLANE
                     rows = flat[pl.ds(share * SHARE - ROW_OUT, SHARE), :]
-                    out[p, z] = rows.astype(out.dtype)
+                    out[p * (Z - 1) + z] = rows.astype(out.dtype)
 
 
 def attend_back_kernel(project, weights, grad_attended, grad_project):
@@ -314,18 +314,22 @@
                 out[p] = jnp.concatenate([padded, mine], axis=0).astype(out.dtype)
 
 
-def add_core_kernel(kept, received, keep_out, *sends):
+def add_first_kernel(kept, received, keep_out, *sends):
     keep_out[...] = kept[0] + received[0].astype(F32)
     for p, out in enumerate(sends):
         out[...] = (kept[p + 1] + received[p + 1].astype(F32)).astype(BF16)
 
 
-def add_plane_kernel(ids, first_kept, rest_kept, *refs):
-    firsts, rests = refs[: PLANE - 1], refs[PLANE - 1 : 2 * (PLANE - 1)]
-    keep_out, *sends, first, column = refs[2 * (PLANE - 1) :]
+def add_rest_kernel(kept, received, out):
+    out[...] = (kept[...] + received[...].astype(F32)).astype(out.dtype)
+
+
+def add_plane_kernel(ids, rest, first_kept, *refs):
+    firsts = refs[: PLANE - 1]
+    keep_out, *sends, first, column = refs[PLANE - 1 :]
     first[...] = first_kept[...] + sum(item[...].astype(F32) for item in firsts)
     column[0] = first[:SHARE, :]
-    column[1:] = rest_kept[...] + sum(item[...].astype(F32) for item in rests)
+    column[1:] = rest[...].astype(F32)
     end = SMALL_IN_SHARE + LATE_SMALL
     column[Z - 1, SMALL_IN_SHARE:end, :] += first[SIDE : SIDE + LATE_SMALL, :]
     keep_out[...] = column[ids[0]]
@@ -357,7 +361,7 @@
 
 def small_call(kernel, name, ids, inputs, outs, scratch=()):
     with_ids = ids is not None
-    return pl.pallas_call(
+    results = pl.pallas_call(
         kernel,
         in_specs=[SMEM_SPEC] * with_ids + [pl.BlockSpec(memory_space=pltpu.VMEM)] * len(inputs),
         out_specs=[pl.BlockSpec(memory_space=pltpu.VMEM)] * len(outs),
@@ -367,6 +371,7 @@
         cost_estimate=cost(1),
         name=name,
     )(*([ids] if with_ids else []), *inputs)
+    return results if len(outs) > 1 else results[0]
 
 
 def attend(ids, segments, tokens, bufs):
@@ -396,8 +401,8 @@
     small_rows = ROW_END - ROW_SMALL - LATE_SMALL
     blocked = [like(rows, D, kind=BF16), like(rows, D), like(rows, D, kind=BF16)]
     fixed = [
-        like(PLANE, Z - 1, SHARE, LANES),
-        like(PLANE, Z - 1, SHARE, LANES, kind=send_kind),
+        like(PLANE * (Z - 1), SHARE, LANES),
+        like(PLANE * (Z - 1), SHARE, LANES, kind=send_kind),
         like(HEAD_ROWS, LANES),
     ]
     return pl.pallas_call(
@@ -469,7 +474,7 @@
         [jnp.zeros((SIDE - SHARE, LANES), BF16), gathered[ROW_SMALL:ROW_TOTAL]], axis=0
     )
     firsts = [jnp.concatenate([shares[0, k], side], axis=0) for k in order]
-    rests = [shares[1:, k] for k in order]
+    rests = [jnp.concatenate([shares[1:, p * 2 + c] for p in range(PLANE)]) for c in range(2)]
     ids = jnp.array(order, jnp.int32)
     segments = segment_ids.reshape(-1, 1, SEQ)
     project, weights, attended, w_qkv, small, first = attend(ids, segments, tokens, firsts)
@@ -481,7 +486,7 @@
         ids, tokens, grad_project, grad_middle, w_qkv, small, first_grad, F32
     )
     first = jnp.stack([keep, send], axis=1)
-    rest = jnp.stack([rest_keep, rest_send], axis=1).transpose(2, 0, 1, 3, 4)
+    rest = jnp.stack([rest_keep, rest_send]).reshape(2, PLANE, Z - 1, SHARE, LANES).transpose(2, 1, 0, 3, 4)
     flat = jnp.concatenate(
         [
             first[:, :, :SHARE].reshape(-1, LANES),
@@ -499,6 +504,9 @@
 
 def index_of(z, plane, core):
     return (z * PLANE + plane) * 2 + core
+
+
+PLANES = [[index_of(z, p, c) for p in range(PLANE)] for z in range(Z) for c in range(2)]
 
 
 def move(values, step_z, step_plane, step_core):
@@ -511,33 +519,12 @@
     return lax.ppermute(values, "fsdp", pairs)
 
 
-def spread(values):
-    same = [values] + [move(values, 0, d, 0) for d in range(1, PLANE)]
-    return same + [move(item, 0, 0, 1) for item in same]
-
-
-def add_core(keep, send):
-    item = keep.shape[1:]
-    return small_call(
-        add_core_kernel, "add_core", None, [keep, move(send, 0, 0, 1)],
-        [like(*item)] + [like(*item, kind=BF16)] * (PLANE - 1),
-    )
-
-
-def add_plane(where, first, rest):
-    arrived = [move(item, 0, d + 1, 0) for items in (first, rest) for d, item in enumerate(items[1:])]
-    return small_call(
-        add_plane_kernel, "add_plane", where, [first[0], rest[0]] + arrived,
-        [like(SHARE, LANES)] + [like(SHARE, LANES, kind=BF16)] * (Z - 1),
-        [pltpu.VMEM((SIDE + 16, LANES), F32), pltpu.VMEM((Z, SHARE, LANES), F32)],
-    )
-
-
 def local_slice(tokens, params, segment_ids, cotangent):
     me = lax.axis_index("fsdp").astype(jnp.int32)
     z, plane, core = me // (2 * PLANE), (me // 2) % PLANE, me % 2
     where = z.reshape(1)
     ids = jnp.stack([(plane ^ dp) * 2 + (core ^ dc) for dc in range(2) for dp in range(PLANE)])
+    plain_ids = jnp.stack([p * 2 + (core ^ dc) for dc in range(2) for p in range(PLANE)])
     segments = segment_ids.reshape(-1, 1, SEQ)
 
     column = [params] + [move(params, d, 0, 0) for d in range(1, Z)]
@@ -546,18 +533,36 @@
         [like(SIDE + SMALL_ROWS, LANES, kind=BF16), like(Z - 1, SHARE, LANES, kind=BF16)],
         [pltpu.VMEM((Z, SHARE, LANES), BF16), pltpu.VMEM((SIDE + SMALL_ROWS, LANES), F32)],
     )
-    project, weights, attended, w_qkv, small, first = attend(ids, segments, tokens, spread(first))
-    outputs, grad_middle, grad_attended, rest_keep, rest_send, first_grad = feed(
-        ids, tokens, attended, cotangent, small, first, spread(rest), BF16
-    )
-
-    rest_sums = add_core(rest_keep, rest_send)
+    rest = lax.all_gather(rest, "fsdp", axis=0, axis_index_groups=PLANES, tiled=True)
+    same = [first] + [move(first, 0, d, 0) for d in range(1, PLANE)]
+    firsts = same + [move(item, 0, 0, 1) for item in same]
+    project, weights, attended, w_qkv, small, first = attend(ids, segments, tokens, firsts)
+    rest, attended = lax.optimization_barrier((rest, attended))
+    outputs, grad_middle, grad_attended, keep, send, first_grad = feed(
+        plain_ids, tokens, attended, cotangent, small, first, [rest, move(rest, 0, 0, 1)], BF16
+    )
+
     grad_project = attend_back(project, weights, grad_attended)
+    rest_sums = small_call(
+        add_rest_kernel, "add_rest", None, [keep, move(send, 0, 0, 1)], [like(*keep.shape)]
+    )
+    rest_sums, grad_project = lax.optimization_barrier((rest_sums, grad_project))
+    rest_sums = lax.psum_scatter(
+        rest_sums, "fsdp", scatter_dimension=0, axis_index_groups=PLANES, tiled=True
+    )
     input_grad, keep, send = project_back(
         ids, tokens, grad_project, grad_middle, w_qkv, small, first_grad, BF16
     )
-    first_sums = add_core(keep, send)
-    param_grad, *sends = add_plane(where, first_sums, rest_sums)
+    kept, *sends = small_call(
+        add_first_kernel, "add_first", None, [keep, move(send, 0, 0, 1)],
+        [like(SIDE + 16, LANES)] + [like(SIDE + 16, LANES, kind=BF16)] * (PLANE - 1),
+    )
+    arrived = [move(item, 0, d + 1, 0) for d, item in enumerate(sends)]
+    param_grad, *sends = small_call(
+        add_plane_kernel, "add_plane", where, [rest_sums, kept] + arrived,
+        [like(SHARE, LANES)] + [like(SHARE, LANES, kind=BF16)] * (Z - 1),
+        [pltpu.VMEM((SIDE + 16, LANES), F32), pltpu.VMEM((Z, SHARE, LANES), F32)],
+    )
     for d, item in enumerate(sends):
         param_grad = param_grad + move(item, d + 1, 0, 0).astype(F32)
     return outputs, input_grad, param_grad

time: 81.2 us -> 118 us (1.45)
  between operations: 0.78 us -> 14.2 us
  blocking collectives: 0 us -> 11.5 us
  local copies, waits for them, and re-layouts: 1.22 us -> 9.62 us
  waiting for transfers between devices: 25.4 us -> 33.1 us
  starting transfers between devices: 26.3 us -> 21 us
    unnamed x0 -> x2, waiting for transfers between devices: none -> 15.8 us
    all_gather x0 -> x1, blocking collectives: none -> 11.5 us  [local_slice(): lax.all_gather(rest, 'fsdp', axis=0, axis_index_groups=PLANES, tiled=True)]
    unnamed x10 -> x32, local copies, waits for them, and re-layouts: 0.82 us -> 9.45 us
    ppermute x28 -> x19, waiting for transfers between devices: 25.4 us -> 17.3 us  [move(): return lax.ppermute(values, 'fsdp', pairs)]
    ppermute x28 -> x19, starting transfers between devices: 26.3 us -> 21 us  [move(): return lax.ppermute(values, 'fsdp', pairs)]
  transfers between devices with their start and end apart: 28 -> 20, of which waited for: 10 -> 14; matrix products, arithmetic and copies ran while one was open for 0% -> 0% of each run, Pallas kernels for 19% -> 7%
where the time goes in v4:
time: 118 us
  waiting for transfers between devices  33.1 us (28%)
  Pallas kernels  27.5 us (23%)
  starting transfers between devices  21 us (18%)
  between operations  14.2 us (12%)
  blocking collectives  11.5 us (10%)
  local copies, waits for them, and re-layouts  9.62 us (8%)
    ppermute x19, starting transfers between devices, move(): return lax.ppermute(values, 'fsdp', pairs)  21 us
    ppermute x19, waiting for transfers between devices, move(): return lax.ppermute(values, 'fsdp', pairs)  17.3 us
    unnamed x2, waiting for transfers between devices  15.8 us
    all_gather x1, blocking collectives, local_slice(): lax.all_gather(rest, 'fsdp', axis=0, axis_index_groups=PLANES, tiled=True)  11.5 us
    pallas_call x1, Pallas kernels, feed(): pl.pallas_call(feed_kernel, grid=(rows // BLOCK,), in_specs=[SMEM_SPEC] +...  11.2 us
    unnamed x32, local copies, waits for them, and re-layouts  9.45 us
    pallas_call x1, Pallas kernels, attend(): pl.pallas_call(attend_kernel, grid=(rows // BLOCK,), in_specs=[SMEM_SPEC,...  6.41 us
    pallas_call x1, Pallas kernels, project_back(): pl.pallas_call(project_back_kernel, grid=(rows // BLOCK,), in_specs=[SMEM...  4.33 us
  transfers between devices with their start and end apart: 20, of which 14 were waited for; matrix products, arithmetic and copies ran while one was open for 0% of the time, Pallas kernels for 7%

profile of v4, /device:TPU:0, one launch (start us, length us, event | category | flops | bytes accessed | tf_op | source)
XLA Modules:
  0.0 117.6 jit_solution(16444775633399406411)
XLA Ops:
  7.2 4.1 %collective-permute-start.1 = (bf16[193,128]{1,0:T(8,128)(2,1)}, bf16[193,128]{1,0:T(8,128)(2,1)S(1)}, u32[]{:S(2)}, u32[]{:S(2)}) collective-permute-start(bf16[193,128]{1,0:T(8,128)(2,1)} %refs_0_.1), channel_id=1, source_target_pairs={{0,16},{1,17},{2,18},{3,19},{4,20},{5,21},{6,22},{7,23},{8,24},{9,... | collective-permute-start | bytes 148232 | tf_op jit(solution)/shard_map/ppermute | solution.py:519
  11.3 1.6 %collective-permute-start = (bf16[193,128]{1,0:T(8,128)(2,1)}, bf16[193,128]{1,0:T(8,128)(2,1)S(1)}, u32[]{:S(2)}, u32[]{:S(2)}) collective-permute-start(bf16[193,128]{1,0:T(8,128)(2,1)} %refs_0_.1), channel_id=1, source_target_pairs={{0,8},{1,9},{2,10},{3,11},{4,12},{5,13},{6,14},{7,15},{8,16},{9,17... | collective-permute-start | bytes 148232 | tf_op jit(solution)/shard_map/ppermute | solution.py:519
  12.9 2.2 %collective-permute-start.2 = (bf16[193,128]{1,0:T(8,128)(2,1)}, bf16[193,128]{1,0:T(8,128)(2,1)S(1)}, u32[]{:S(2)}, u32[]{:S(2)}) collective-permute-start(bf16[193,128]{1,0:T(8,128)(2,1)} %refs_0_.1), channel_id=1, source_target_pairs={{0,24},{1,25},{2,26},{3,27},{4,28},{5,29},{6,30},{7,31},{8,0},{9,1... | collective-permute-start | bytes 148232 | tf_op jit(solution)/shard_map/ppermute | solution.py:519
  15.1 2.4 %collective-permute-done.refs_1_ = bf16[193,128]{1,0:T(8,128)(2,1)S(1)} collective-permute-done((bf16[193,128]{1,0:T(8,128)(2,1)}, bf16[193,128]{1,0:T(8,128)(2,1)S(1)}, u32[]{:S(2)}, u32[]{:S(2)}) %collective-permute-start) | collective-permute-done | bytes 49440 | tf_op jit(solution)/shard_map/ppermute | solution.py:519
  17.5 0.2 collective-permute-done.2.refs_3_
  17.8 0.8 copy-done.3
  18.6 2.5 %collective-permute-start.5 = (bf16[240,128]{1,0:T(8,128)(2,1)S(1)}, bf16[240,128]{1,0:T(8,128)(2,1)S(1)}, u32[]{:S(2)}, u32[]{:S(2)}) collective-permute-start(bf16[240,128]{1,0:T(8,128)(2,1)S(1)} %get-tuple-element.33.refs_0_), channel_id=1, source_target_pairs={{0,6},{1,7},{2,4},{3,5},{4,2},{5,3},{6,0},{7,1},{8,14},{9,15},{10,... | collective-permute-start | bytes 184328 | tf_op jit(solution)/shard_map/ppermute | solution.py:519
  21.1 0.5 collective-permute-start.4
  21.6 0.5 collective-permute-start.3
  22.2 0.1 stack.71.ids
  22.3 1.8 %collective-permute-done.5.refs_3_ = bf16[240,128]{1,0:T(8,128)(2,1)S(1)} collective-permute-done((bf16[240,128]{1,0:T(8,128)(2,1)S(1)}, bf16[240,128]{1,0:T(8,128)(2,1)S(1)}, u32[]{:S(2)}, u32[]{:S(2)}) %collective-permute-start.5) | collective-permute-done | bytes 61472 | tf_op jit(solution)/shard_map/ppermute | solution.py:519
  24.1 1.3 %collective-permute-done.4.refs_2_ = bf16[240,128]{1,0:T(8,128)(2,1)S(1)} collective-permute-done((bf16[240,128]{1,0:T(8,128)(2,1)S(1)}, bf16[240,128]{1,0:T(8,128)(2,1)S(1)}, u32[]{:S(2)}, u32[]{:S(2)}) %collective-permute-start.4) | collective-permute-done | bytes 61472 | tf_op jit(solution)/shard_map/ppermute | solution.py:519
  25.4 0.5 collective-permute-done.3.refs_1_
  25.9 11.5 %all_gather.3.refs_0_ = bf16[12,193,128]{2,1,0:T(8,128)(2,1)S(1)} all-gather(bf16[3,193,128]{2,1,0:T(8,128)(2,1)S(1)} %get-tuple-element.32), channel_id=1, replica_groups={{0,2,4,6},{1,3,5,7},{8,10,12,14},{9,11,13,15},{16,18,20,22},{17,19,21,2..., dimensions={0}, use_global_device_ids=true | all-gather | bytes 741120 | tf_op jit(solution)/shard_map/all_gather | solution.py:536
  37.4 6.4 %attend.1 = (bf16[1024,768]{1,0:T(8,128)(2,1)S(1)}, f32[1024,512]{1,0:T(8,128)S(1)}, bf16[1024,256]{1,0:T(8,128)(2,1)S(1)}, bf16[256,768]{1,0:T(8,128)(2,1)S(1)}...) custom-call(s32[8]{0:T(128)S(1)} %stack.71.ids, s32[8,1,128]{2,1,0:T(1,128)S(1)} %bitcast.19, ...), custom_call_target="tpu_custom_call" | custom-call | flops 7000000000 | bytes 1048576 | tf_op jit(solution)/shard_map/attend/pallas_call | solution.py:381
  43.9 1.3 %copy-done.6 = f32[1024,512]{1,0:T(8,128)} copy-done((f32[1024,512]{1,0:T(8,128)}, f32[1024,512]{1,0:T(8,128)S(1)}, u32[]{:S(2)}) %copy-start.6) | copy-done | bytes 2097176
  45.2 1.2 copy-done.8
  46.4 0.7 copy-done.12
  47.1 0.8 copy-done.14
  47.9 0.1 stack.62.ids
  48.0 2.0 %collective-permute-done.10.refs_1_ = bf16[12,193,128]{2,1,0:T(8,128)(2,1)S(1)} collective-permute-done((bf16[12,193,128]{2,1,0:T(8,128)(2,1)S(1)}, bf16[12,193,128]{2,1,0:T(8,128)(2,1)S(1)}, u32[]{:S(2)}, u32[]{:S(2)}) %collective-permute-start.10) | collective-permute-done | bytes 592928 | tf_op jit(solution)/shard_map/ppermute | solution.py:519
  49.9 1.0 copy-done.15
  51.0 11.2 %feed.1 = (bf16[1024,256]{1,0:T(8,128)(2,1)}, f32[1024,256]{1,0:T(8,128)S(1)}, bf16[1024,256]{1,0:T(8,128)(2,1)S(1)}, f32[12,193,128]{2,1,0:T(8,128)}, bf16[12,1...) custom-call(s32[8]{0:T(128)S(1)} %stack.62.ids, bf16[1024,256]{1,0:T(8,128)(2,1)S(1)} %copy-done.1, ...), custom_call_target="tpu_custom_call" | custom-call | flops 10000000000 | bytes 1048576 | tf_op jit(solution)/shard_map/feed/pallas_call | solution.py:408
  62.2 0.1 collective-permute-start.11
  62.3 4.3 %attend_back.1.grad_project = bf16[1024,768]{1,0:T(8,128)(2,1)S(1)} custom-call(bf16[1024,768]{1,0:T(8,128)(2,1)S(1)} %copy-done.9, f32[1024,512]{1,0:T(8,128)S(1)} %copy-done.7, bf16[1024,256]{1,0:T(8,128)(2,1)S(1)} %get-tuple-element.44.grad_attended), custom_call_target="tpu_custom_call" | custom-call | flops 6000000000 | bytes 1048576 | tf_op jit(solution)/shard_map/attend_back/pallas_call | solution.py:431
  66.6 1.2 copy-done.10
  67.8 1.2 %add_rest.1 = f32[12,193,128]{2,1,0:T(8,128)} custom-call(f32[12,193,128]{2,1,0:T(8,128)S(1)} %copy-done.5, bf16[12,193,128]{2,1,0:T(8,128)(2,1)S(1)} %collective-permute-done.11.received), custom_call_target="tpu_custom_call" | custom-call | flops 1000000000 | bytes 1048576 | tf_op jit(solution)/shard_map/add_rest/pallas_call | solution.py:364
  69.0 1.4 %copy-done.11 = bf16[1024,768]{1,0:T(8,128)(2,1)S(1)} copy-done((bf16[1024,768]{1,0:T(8,128)(2,1)S(1)}, bf16[1024,768]{1,0:T(8,128)(2,1)}, u32[]{:S(2)}) %copy-start.11) | copy-done | bytes 1572888
  70.4 4.3 %project_back.1 = (f32[1024,256]{1,0:T(8,128)}, f32[4,224,128]{2,1,0:T(8,128)S(1)}, bf16[4,224,128]{2,1,0:T(8,128)(2,1)S(1)}) custom-call(s32[8]{0:T(128)S(1)} %stack.71.ids, bf16[1024,256]{1,0:T(8,128)(2,1)S(1)} %copy-done.1, bf16[1024,768]{1,0:T(8,128)(2,1)S(1)} %copy-done.11, f32[1024,256]{1,0:T(8,128)S(1)} %get-tuple-element.46.grad_middle, ...), custom_call_target="tpu_custom_call" | custom-call | flops 6000000000 | bytes 1048576 | tf_op jit(solution)/shard_map/project_back/pallas_call | solution.py:449
  74.7 0.4 collective-permute-start.12
  75.1 1.1 collective-permute-done.12.received
  76.2 0.1 add_first.1
  76.3 0.6 collective-permute-start.13
  76.9 1.5 %collective-permute-start.14 = (bf16[224,128]{1,0:T(8,128)(2,1)S(1)}, bf16[224,128]{1,0:T(8,128)(2,1)S(1)}, u32[]{:S(2)}, u32[]{:S(2)}) collective-permute-start(bf16[224,128]{1,0:T(8,128)(2,1)S(1)} %get-tuple-element.55), channel_id=1, source_target_pairs={{0,4},{1,5},{2,6},{3,7},{4,0},{5,1},{6,2},{7,3},{8,12},{9,13},{10,... | collective-permute-start | bytes 172040 | tf_op jit(solution)/shard_map/ppermute | solution.py:519
  78.4 1.5 %collective-permute-start.15 = (bf16[224,128]{1,0:T(8,128)(2,1)S(1)}, bf16[224,128]{1,0:T(8,128)(2,1)S(1)}, u32[]{:S(2)}, u32[]{:S(2)}) collective-permute-start(bf16[224,128]{1,0:T(8,128)(2,1)S(1)} %get-tuple-element.56), channel_id=1, source_target_pairs={{0,6},{1,7},{2,4},{3,5},{4,2},{5,3},{6,0},{7,1},{8,14},{9,15},{10,... | collective-permute-start | bytes 172040 | tf_op jit(solution)/shard_map/ppermute | solution.py:519
  79.9 2.5 %collective-permute-done.13.refs_0_ = bf16[224,128]{1,0:T(8,128)(2,1)S(1)} collective-permute-done((bf16[224,128]{1,0:T(8,128)(2,1)S(1)}, bf16[224,128]{1,0:T(8,128)(2,1)S(1)}, u32[]{:S(2)}, u32[]{:S(2)}) %collective-permute-start.13) | collective-permute-done | bytes 57376 | tf_op jit(solution)/shard_map/ppermute | solution.py:519
  82.3 0.7 collective-permute-done.14.refs_1_
  83.0 1.9 %collective-permute-done.15.refs_2_ = bf16[224,128]{1,0:T(8,128)(2,1)S(1)} collective-permute-done((bf16[224,128]{1,0:T(8,128)(2,1)S(1)}, bf16[224,128]{1,0:T(8,128)(2,1)S(1)}, u32[]{:S(2)}, u32[]{:S(2)}) %collective-permute-start.15) | collective-permute-done | bytes 57376 | tf_op jit(solution)/shard_map/ppermute | solution.py:519
  84.9 15.8 %reduce-scatter.4.cloned.1.call-done.rest = f32[3,193,128]{2,1,0:T(8,128)} async-done(((f32[12,193,128]{2,1,0:T(8,128)}), f32[3,193,128]{2,1,0:T(8,128)}) %reduce-scatter.4.cloned.1.call-update) | async-done | bytes 296464
  100.7 1.0 copy-done.2
  101.7 0.1 add_plane.1
  101.8 1.5 %collective-permute-start.16 = (bf16[193,128]{1,0:T(8,128)(2,1)S(1)}, bf16[193,128]{1,0:T(8,128)(2,1)S(1)}, u32[]{:S(2)}, u32[]{:S(2)}) collective-permute-start(bf16[193,128]{1,0:T(8,128)(2,1)S(1)} %get-tuple-element.58), channel_id=1, source_target_pairs={{0,8},{1,9},{2,10},{3,11},{4,12},{5,13},{6,14},{7,15},{8,16},{9,17... | collective-permute-start | bytes 148232 | tf_op jit(solution)/shard_map/ppermute | solution.py:519
  103.3 2.4 %collective-permute-start.17 = (bf16[193,128]{1,0:T(8,128)(2,1)S(1)}, bf16[193,128]{1,0:T(8,128)(2,1)S(1)}, u32[]{:S(2)}, u32[]{:S(2)}) collective-permute-start(bf16[193,128]{1,0:T(8,128)(2,1)S(1)} %get-tuple-element.59), channel_id=1, source_target_pairs={{0,16},{1,17},{2,18},{3,19},{4,20},{5,21},{6,22},{7,23},{8,24},{9,... | collective-permute-start | bytes 148232 | tf_op jit(solution)/shard_map/ppermute | solution.py:519
  105.7 1.4 %collective-permute-start.18 = (bf16[193,128]{1,0:T(8,128)(2,1)S(1)}, bf16[193,128]{1,0:T(8,128)(2,1)S(1)}, u32[]{:S(2)}, u32[]{:S(2)}) collective-permute-start(bf16[193,128]{1,0:T(8,128)(2,1)S(1)} %get-tuple-element.60), channel_id=1, source_target_pairs={{0,24},{1,25},{2,26},{3,27},{4,28},{5,29},{6,30},{7,31},{8,0},{9,1... | collective-permute-start | bytes 148232 | tf_op jit(solution)/shard_map/ppermute | solution.py:519
  107.1 1.1 collective-permute-done.16
  108.3 1.7 %collective-permute-done.17 = bf16[193,128]{1,0:T(8,128)(2,1)S(1)} collective-permute-done((bf16[193,128]{1,0:T(8,128)(2,1)S(1)}, bf16[193,128]{1,0:T(8,128)(2,1)S(1)}, u32[]{:S(2)}, u32[]{:S(2)}) %collective-permute-start.17) | collective-permute-done | bytes 49440 | tf_op jit(solution)/shard_map/ppermute | solution.py:519
  110.0 0.1 collective-permute-done.18
  110.1 0.7 convert_add_fusion
  (37 shorter events, 0.2 us)
Async XLA Ops:
  7.2 93.5 %reduce-scatter.4.cloned.1.call-start = ((), (), s32[]{:S(2)}) async-start(), calls=%async_computation.1 | async-start | bytes 1536000
  7.2 7.9 %collective-permute-start.1 = (bf16[193,128]{1,0:T(8,128)(2,1)}, bf16[193,128]{1,0:T(8,128)(2,1)S(1)}, u32[]{:S(2)}, u32[]{:S(2)}) collective-permute-start(bf16[193,128]{1,0:T(8,128)(2,1)} %refs_0_.1), channel_id=1, source_target_pairs={{0,16},{1,17},{2,18},{3,19},{4,20},{5,21},{6,22},{7,23},{8,24},{9,... | collective-permute-start | bytes 148232 | tf_op jit(solution)/shard_map/ppermute | solution.py:519
  11.3 6.2 %collective-permute-start = (bf16[193,128]{1,0:T(8,128)(2,1)}, bf16[193,128]{1,0:T(8,128)(2,1)S(1)}, u32[]{:S(2)}, u32[]{:S(2)}) collective-permute-start(bf16[193,128]{1,0:T(8,128)(2,1)} %refs_0_.1), channel_id=1, source_target_pairs={{0,8},{1,9},{2,10},{3,11},{4,12},{5,13},{6,14},{7,15},{8,16},{9,17... | collective-permute-start | bytes 148232 | tf_op jit(solution)/shard_map/ppermute | solution.py:519
  12.9 4.9 %collective-permute-start.2 = (bf16[193,128]{1,0:T(8,128)(2,1)}, bf16[193,128]{1,0:T(8,128)(2,1)S(1)}, u32[]{:S(2)}, u32[]{:S(2)}) collective-permute-start(bf16[193,128]{1,0:T(8,128)(2,1)} %refs_0_.1), channel_id=1, source_target_pairs={{0,24},{1,25},{2,26},{3,27},{4,28},{5,29},{6,30},{7,31},{8,0},{9,1... | collective-permute-start | bytes 148232 | tf_op jit(solution)/shard_map/ppermute | solution.py:519
  17.8 0.8 copy-start.3
  18.6 18.8 %copy-start.1 = (bf16[1024,256]{1,0:T(8,128)(2,1)S(1)}, bf16[1024,256]{1,0:T(8,128)(2,1)}, u32[]{:S(2)}) copy-start(bf16[1024,256]{1,0:T(8,128)(2,1)} %tok.5) | copy-start | bytes 1572868
  18.6 18.8 %copy-start.4 = (s32[1024]{0:T(1024)S(1)}, s32[1024]{0:T(1024)}, u32[]{:S(2)}) copy-start(s32[1024]{0:T(1024)} %param.6) | copy-start | bytes 12292
  18.6 5.5 %collective-permute-start.5 = (bf16[240,128]{1,0:T(8,128)(2,1)S(1)}, bf16[240,128]{1,0:T(8,128)(2,1)S(1)}, u32[]{:S(2)}, u32[]{:S(2)}) collective-permute-start(bf16[240,128]{1,0:T(8,128)(2,1)S(1)} %get-tuple-element.33.refs_0_), channel_id=1, source_target_pairs={{0,6},{1,7},{2,4},{3,5},{4,2},{5,3},{6,0},{7,1},{8,14},{9,15},{10,... | collective-permute-start | bytes 184328 | tf_op jit(solution)/shard_map/ppermute | solution.py:519
  21.1 4.2 %collective-permute-start.4 = (bf16[240,128]{1,0:T(8,128)(2,1)S(1)}, bf16[240,128]{1,0:T(8,128)(2,1)S(1)}, u32[]{:S(2)}, u32[]{:S(2)}) collective-permute-start(bf16[240,128]{1,0:T(8,128)(2,1)S(1)} %get-tuple-element.33.refs_0_), channel_id=1, source_target_pairs={{0,4},{1,5},{2,6},{3,7},{4,0},{5,1},{6,2},{7,3},{8,12},{9,13},{10,... | collective-permute-start | bytes 184328 | tf_op jit(solution)/shard_map/ppermute | solution.py:519
  21.6 4.2 %collective-permute-start.3 = (bf16[240,128]{1,0:T(8,128)(2,1)S(1)}, bf16[240,128]{1,0:T(8,128)(2,1)S(1)}, u32[]{:S(2)}, u32[]{:S(2)}) collective-permute-start(bf16[240,128]{1,0:T(8,128)(2,1)S(1)} %get-tuple-element.33.refs_0_), channel_id=1, source_target_pairs={{0,2},{1,3},{2,0},{3,1},{4,6},{5,7},{6,4},{7,5},{8,10},{9,11},{10,... | collective-permute-start | bytes 184328 | tf_op jit(solution)/shard_map/ppermute | solution.py:519
  22.3 15.1 %collective-permute-start.6 = (bf16[240,128]{1,0:T(8,128)(2,1)S(1)}, bf16[240,128]{1,0:T(8,128)(2,1)S(1)}, u32[]{:S(2)}, u32[]{:S(2)}) collective-permute-start(bf16[240,128]{1,0:T(8,128)(2,1)S(1)} %get-tuple-element.33.refs_0_), channel_id=1, source_target_pairs={{0,1},{1,0},{2,3},{3,2},{4,5},{5,4},{6,7},{7,6},{8,9},{9,8},{10,11... | collective-permute-start | bytes 184328 | tf_op jit(solution)/shard_map/ppermute | solution.py:519
  24.1 13.3 %collective-permute-start.9 = (bf16[240,128]{1,0:T(8,128)(2,1)S(1)}, bf16[240,128]{1,0:T(8,128)(2,1)S(1)}, u32[]{:S(2)}, u32[]{:S(2)}) collective-permute-start(bf16[240,128]{1,0:T(8,128)(2,1)S(1)} %collective-permute-done.5.refs_3_), channel_id=1, source_target_pairs={{0,1},{1,0},{2,3},{3,2},{4,5},{5,4},{6,7},{7,6},{8,9},{9,8},{10,11... | collective-permute-start | bytes 184328 | tf_op jit(solution)/shard_map/ppermute | solution.py:519
  25.4 12.0 %collective-permute-start.8 = (bf16[240,128]{1,0:T(8,128)(2,1)S(1)}, bf16[240,128]{1,0:T(8,128)(2,1)S(1)}, u32[]{:S(2)}, u32[]{:S(2)}) collective-permute-start(bf16[240,128]{1,0:T(8,128)(2,1)S(1)} %collective-permute-done.4.refs_2_), channel_id=1, source_target_pairs={{0,1},{1,0},{2,3},{3,2},{4,5},{5,4},{6,7},{7,6},{8,9},{9,8},{10,11... | collective-permute-start | bytes 184328 | tf_op jit(solution)/shard_map/ppermute | solution.py:519
  25.9 11.5 %collective-permute-start.7 = (bf16[240,128]{1,0:T(8,128)(2,1)S(1)}, bf16[240,128]{1,0:T(8,128)(2,1)S(1)}, u32[]{:S(2)}, u32[]{:S(2)}) collective-permute-start(bf16[240,128]{1,0:T(8,128)(2,1)S(1)} %collective-permute-done.3.refs_1_), channel_id=1, source_target_pairs={{0,1},{1,0},{2,3},{3,2},{4,5},{5,4},{6,7},{7,6},{8,9},{9,8},{10,11... | collective-permute-start | bytes 184328 | tf_op jit(solution)/shard_map/ppermute | solution.py:519
  37.4 12.5 %copy-start = (bf16[1024,256]{1,0:T(8,128)(2,1)S(1)}, bf16[1024,256]{1,0:T(8,128)(2,1)}, u32[]{:S(2)}) copy-start(bf16[1024,256]{1,0:T(8,128)(2,1)} %cot.1) | copy-start | bytes 1572868
  43.8 1.4 %copy-start.6 = (f32[1024,512]{1,0:T(8,128)}, f32[1024,512]{1,0:T(8,128)S(1)}, u32[]{:S(2)}) copy-start(f32[1024,512]{1,0:T(8,128)S(1)} %get-tuple-element.43.weights) | copy-start | bytes 6291460
  45.2 1.2 copy-start.8
  46.4 0.7 copy-start.12
  47.1 0.8 copy-start.14
  47.9 2.0 %collective-permute-start.10 = (bf16[12,193,128]{2,1,0:T(8,128)(2,1)S(1)}, bf16[12,193,128]{2,1,0:T(8,128)(2,1)S(1)}, u32[]{:S(2)}, u32[]{:S(2)}) collective-permute-start(bf16[12,193,128]{2,1,0:T(8,128)(2,1)S(1)} %all_gather.3.refs_0_), channel_id=1, source_target_pairs={{0,1},{1,0},{2,3},{3,2},{4,5},{5,4},{6,7},{7,6},{8,9},{9,8},{10,11... | collective-permute-start | bytes 1778696 | tf_op jit(solution)/shard_map/ppermute | solution.py:519
  49.9 1.0 copy-start.15
  51.0 11.3 %copy-start.7 = (f32[1024,512]{1,0:T(8,128)S(1)}, f32[1024,512]{1,0:T(8,128)}, u32[]{:S(2)}) copy-start(f32[1024,512]{1,0:T(8,128)} %copy-done.6) | copy-start | bytes 6291460
  51.0 11.3 %copy-start.9 = (bf16[1024,768]{1,0:T(8,128)(2,1)S(1)}, bf16[1024,768]{1,0:T(8,128)(2,1)}, u32[]{:S(2)}) copy-start(bf16[1024,768]{1,0:T(8,128)(2,1)} %copy-done.8) | copy-start | bytes 4718596
  62.2 5.6 %collective-permute-start.11 = (bf16[12,193,128]{2,1,0:T(8,128)(2,1)S(1)}, bf16[12,193,128]{2,1,0:T(8,128)(2,1)S(1)}, u32[]{:S(2)}, u32[]{:S(2)}) collective-permute-start(bf16[12,193,128]{2,1,0:T(8,128)(2,1)S(1)} %get-tuple-element.41), channel_id=1, source_target_pairs={{0,1},{1,0},{2,3},{3,2},{4,5},{5,4},{6,7},{7,6},{8,9},{9,8},{10,11... | collective-permute-start | bytes 1778696 | tf_op jit(solution)/shard_map/ppermute | solution.py:519
  62.3 5.5 %copy-start.5 = (f32[12,193,128]{2,1,0:T(8,128)S(1)}, f32[12,193,128]{2,1,0:T(8,128)}, u32[]{:S(2)}) copy-start(f32[12,193,128]{2,1,0:T(8,128)} %get-tuple-element.40.kept) | copy-start | bytes 3557380
  66.6 1.2 %copy-start.10 = (bf16[1024,768]{1,0:T(8,128)(2,1)}, bf16[1024,768]{1,0:T(8,128)(2,1)S(1)}, u32[]{:S(2)}) copy-start(bf16[1024,768]{1,0:T(8,128)(2,1)S(1)} %attend_back.1.grad_project) | copy-start | bytes 4718596
  67.8 1.2 %copy-start.13 = (bf16[256,768]{1,0:T(8,128)(2,1)S(1)}, bf16[256,768]{1,0:T(8,128)(2,1)}, u32[]{:S(2)}) copy-start(bf16[256,768]{1,0:T(8,128)(2,1)} %copy-done.12) | copy-start | bytes 1179652
  69.0 1.4 %copy-start.11 = (bf16[1024,768]{1,0:T(8,128)(2,1)S(1)}, bf16[1024,768]{1,0:T(8,128)(2,1)}, u32[]{:S(2)}) copy-start(bf16[1024,768]{1,0:T(8,128)(2,1)} %copy-done.10) | copy-start | bytes 4718596
  74.7 1.5 %collective-permute-start.12 = (bf16[4,224,128]{2,1,0:T(8,128)(2,1)S(1)}, bf16[4,224,128]{2,1,0:T(8,128)(2,1)S(1)}, u32[]{:S(2)}, u32[]{:S(2)}) collective-permute-start(bf16[4,224,128]{2,1,0:T(8,128)(2,1)S(1)} %get-tuple-element.52), channel_id=1, source_target_pairs={{0,1},{1,0},{2,3},{3,2},{4,5},{5,4},{6,7},{7,6},{8,9},{9,8},{10,11... | collective-permute-start | bytes 688136 | tf_op jit(solution)/shard_map/ppermute | solution.py:519
  76.3 6.1 %collective-permute-start.13 = (bf16[224,128]{1,0:T(8,128)(2,1)S(1)}, bf16[224,128]{1,0:T(8,128)(2,1)S(1)}, u32[]{:S(2)}, u32[]{:S(2)}) collective-permute-start(bf16[224,128]{1,0:T(8,128)(2,1)S(1)} %get-tuple-element.54), channel_id=1, source_target_pairs={{0,2},{1,3},{2,0},{3,1},{4,6},{5,7},{6,4},{7,5},{8,10},{9,11},{10,... | collective-permute-start | bytes 172040 | tf_op jit(solution)/shard_map/ppermute | solution.py:519
  76.9 6.1 %collective-permute-start.14 = (bf16[224,128]{1,0:T(8,128)(2,1)S(1)}, bf16[224,128]{1,0:T(8,128)(2,1)S(1)}, u32[]{:S(2)}, u32[]{:S(2)}) collective-permute-start(bf16[224,128]{1,0:T(8,128)(2,1)S(1)} %get-tuple-element.55), channel_id=1, source_target_pairs={{0,4},{1,5},{2,6},{3,7},{4,0},{5,1},{6,2},{7,3},{8,12},{9,13},{10,... | collective-permute-start | bytes 172040 | tf_op jit(solution)/shard_map/ppermute | solution.py:519
  78.4 6.5 %collective-permute-start.15 = (bf16[224,128]{1,0:T(8,128)(2,1)S(1)}, bf16[224,128]{1,0:T(8,128)(2,1)S(1)}, u32[]{:S(2)}, u32[]{:S(2)}) collective-permute-start(bf16[224,128]{1,0:T(8,128)(2,1)S(1)} %get-tuple-element.56), channel_id=1, source_target_pairs={{0,6},{1,7},{2,4},{3,5},{4,2},{5,3},{6,0},{7,1},{8,14},{9,15},{10,... | collective-permute-start | bytes 172040 | tf_op jit(solution)/shard_map/ppermute | solution.py:519
  100.7 1.0 copy-start.2
  101.8 6.5 %collective-permute-start.16 = (bf16[193,128]{1,0:T(8,128)(2,1)S(1)}, bf16[193,128]{1,0:T(8,128)(2,1)S(1)}, u32[]{:S(2)}, u32[]{:S(2)}) collective-permute-start(bf16[193,128]{1,0:T(8,128)(2,1)S(1)} %get-tuple-element.58), channel_id=1, source_target_pairs={{0,8},{1,9},{2,10},{3,11},{4,12},{5,13},{6,14},{7,15},{8,16},{9,17... | collective-permute-start | bytes 148232 | tf_op jit(solution)/shard_map/ppermute | solution.py:519
  103.3 6.7 %collective-permute-start.17 = (bf16[193,128]{1,0:T(8,128)(2,1)S(1)}, bf16[193,128]{1,0:T(8,128)(2,1)S(1)}, u32[]{:S(2)}, u32[]{:S(2)}) collective-permute-start(bf16[193,128]{1,0:T(8,128)(2,1)S(1)} %get-tuple-element.59), channel_id=1, source_target_pairs={{0,16},{1,17},{2,18},{3,19},{4,20},{5,21},{6,22},{7,23},{8,24},{9,... | collective-permute-start | bytes 148232 | tf_op jit(solution)/shard_map/ppermute | solution.py:519
  105.7 4.4 %collective-permute-start.18 = (bf16[193,128]{1,0:T(8,128)(2,1)S(1)}, bf16[193,128]{1,0:T(8,128)(2,1)S(1)}, u32[]{:S(2)}, u32[]{:S(2)}) collective-permute-start(bf16[193,128]{1,0:T(8,128)(2,1)S(1)} %get-tuple-element.60), channel_id=1, source_target_pairs={{0,24},{1,25},{2,26},{3,27},{4,28},{5,29},{6,30},{7,31},{8,0},{9,1... | collective-permute-start | bytes 148232 | tf_op jit(solution)/shard_map/ppermute | solution.py:519
Sparse Core Ops, SparseCore 0:
  69.1 31.5 reduce-scatter.3

commit v5 on v1

v5 whole, which is shorter than its diff:
```python
import functools

import jax
import jax.numpy as jnp
from jax import lax
from jax.experimental import pallas as pl
from jax.experimental.pallas import tpu as pltpu
from jax.sharding import PartitionSpec as P

D = 256
HEADS = 4
HEAD_DIM = 64
FF = 1024
SEQ = 128
LANES = 128
BLOCK = 2 * SEQ
WIDE = 4 * SEQ
CHUNK = 256
STRIP = 64
EPSILON = 1e-05
SCALE = HEAD_DIM ** (-0.5)
VMEM_BYTES = 32 * 1024 * 1024

ROW_QKV = 0
ROW_OUT = 1536
ROW_UP = 2048
ROW_DOWN = 4096
ROW_SMALL = 6144
ROW_END = 6168
ROW_TOTAL = 6176
GAIN_ONE, SHIFT_ONE, BIAS_QUERY, BIAS_VALUE, BIAS_OUT = 0, 2, 4, 6, 8
GAIN_TWO, SHIFT_TWO, BIAS_UP, BIAS_DOWN = 10, 12, 14, 22
SMALL_ROWS = 24
LATE_SMALL = 8

SHARE = 193
Z, PLANE = 4, 4
FIRST_ROWS = 2 * PLANE * SHARE
HEAD_ROWS = FIRST_ROWS - ROW_OUT
SIDE, SIDE_ROWS = 208, 16
SMALL_IN_SHARE = ROW_SMALL - (2 * PLANE * Z - 1) * SHARE

F32 = jnp.float32
BF16 = jnp.bfloat16


def dot(left, right):
    return jnp.dot(left, right, preferred_element_type=F32)


def dot_nt(left, right):
    return lax.dot_general(left, right, (((1,), (1,)), ((), ())), preferred_element_type=F32)


def dot_tn(left, right):
    return lax.dot_general(left, right, (((0,), (0,)), ((), ())), preferred_element_type=F32)


def small_vector(small, row, count):
    return jnp.concatenate([small[row + i : row + i + 1, :] for i in range(count)], axis=1)


def fold_rows(values):
    rows, columns = values.shape
    return jnp.sum(values.reshape(rows // 8, 8, columns), axis=0)


def normalize(values):
    center = values - jnp.mean(values, axis=-1, keepdims=True)
    rate = lax.rsqrt(jnp.mean(center * center, axis=-1, keepdims=True) + EPSILON)
    return center * rate, rate


def normalize_back(grad, gain, normed, rate):
    scaled = grad * gain
    return rate * (
        scaled
        - jnp.mean(scaled, axis=-1, keepdims=True)
        - normed * jnp.mean(scaled * normed, axis=-1, keepdims=True)
    )


def head_masks():
    lane = lax.broadcasted_iota(jnp.int32, (1, D), 1)
    return [(lane // HEAD_DIM == h).astype(F32).astype(BF16) for h in range(HEADS)]


def spread_heads(rows):
    return jnp.concatenate([rows * mask for mask in head_masks()], axis=0)


def matrix_from_flat(flat, start, rows, columns, out):
    per_row = columns // LANES
    for j in range(per_row):
        out[:, j * LANES : (j + 1) * LANES] = flat[
            pl.ds(start + j, rows, stride=per_row), :
        ].astype(BF16)


def turned_to_flat(turned, rows, columns, flat, start):
    per_row = columns // LANES
    for j in range(per_row):
        flat[pl.ds(start + j, rows, stride=per_row), :] = turned[j * LANES : (j + 1) * LANES, :].T


def matrix_to_flat(matrix, rows, columns, flat, start):
    per_row = columns // LANES
    for j in range(per_row):
        flat[pl.ds(start + j, rows, stride=per_row), :] = matrix[:, j * LANES : (j + 1) * LANES]


def attend_kernel(n_bufs, ids, seg, tok, *refs):
    bufs = refs[:n_bufs]
    (
        project_out, weights_out, attended_out, normed_out, w_qkv, w_out, w_up, w_down, small, flat,
    ) = refs[n_bufs:]

    @pl.when(pl.program_id(0) == 0)
    def _():
        slot = 0
        for buf in bufs:
            count, rows, _ = buf.shape

            def place(i, carry, buf=buf, slot=slot, rows=rows):
                flat[pl.ds(ids[slot + i] * rows, rows), :] = buf[i].astype(F32)
                return carry

            lax.fori_loop(0, count, place, 0)
            slot += count
        matrix_from_flat(flat, ROW_QKV, D, 3 * D, w_qkv)
        matrix_from_flat(flat, ROW_OUT, D, D, w_out)
        matrix_from_flat(flat, ROW_UP, D, FF, w_up)
        matrix_from_flat(flat, ROW_DOWN, FF, D, w_down)
        small[...] = flat[ROW_SMALL:ROW_END, :]

    normed, _ = normalize(tok[...].astype(F32))
    normed_out[...] = normed.astype(BF16)
    normed_low = (
        normed * small_vector(small, GAIN_ONE, 2) + small_vector(small, SHIFT_ONE, 2)
    ).astype(BF16)
    bias = jnp.concatenate(
        [
            small_vector(small, BIAS_QUERY, 2),
            jnp.zeros((1, D), F32),
            small_vector(small, BIAS_VALUE, 2),
        ],
        axis=1,
    )
    project = (dot(normed_low, w_qkv[...]) + bias).astype(BF16)
    project_out[...] = project
    causal = lax.broadcasted_iota(jnp.int32, (SEQ, SEQ), 1) <= lax.broadcasted_iota(
        jnp.int32, (SEQ, SEQ), 0
    )
    for s in range(BLOCK // SEQ):
        rows = slice(s * SEQ, (s + 1) * SEQ)
        across = jnp.broadcast_to(seg[s].astype(F32), (SEQ, SEQ))
        allowed = causal & (across == across.T)
        query = project[rows, :D]
        key = spread_heads(project[rows, D : 2 * D])
        value = spread_heads(project[rows, 2 * D :])
        scores = dot_nt(query, key) * SCALE
        low = []
        for h in range(HEADS):
            columns = slice(h * SEQ, (h + 1) * SEQ)
            mine = jnp.where(allowed, scores[:, columns], -1e30)
            grown = jnp.exp(mine - jnp.max(mine, axis=-1, keepdims=True))
            weights = grown * (1.0 / jnp.sum(grown, axis=-1, keepdims=True))
            weights_out[rows, columns] = weights
            low.append(weights.astype(BF16))
        attended_out[rows, :] = dot(jnp.concatenate(low, axis=1), value).astype(BF16)


def feed_kernel(
    ids, tok, attended, cot, w_out, w_up, w_down, small,
    middle_out, activated_out, grad_middle_out, grad_attended_out, keep_out, send_out, first_out,
    grad_hidden, acc_out, acc_up, acc_down, acc_small, flat,
):
    step = pl.program_id(0)

    @pl.when(step == 0)
    def _():
        acc_out[...] = jnp.zeros_like(acc_out)
        acc_up[...] = jnp.zeros_like(acc_up)
        acc_down[...] = jnp.zeros_like(acc_down)
        acc_small[...] = jnp.zeros_like(acc_small)

    gain = small_vector(small, GAIN_TWO, 2)
    middle = tok[...].astype(F32) + dot(attended[...], w_out[...]) + small_vector(small, BIAS_OUT, 2)
    middle_out[...] = middle
    normed, rate = normalize(middle)
    normed_low = (normed * gain + small_vector(small, SHIFT_TWO, 2)).astype(BF16)
    cotangent = cot[...]
    slope = 0.7978845608028654
    cubic = slope * 0.044715
    for c in range(0, FF, CHUNK):
        columns = slice(c, c + CHUNK)
        bias = small_vector(small, BIAS_UP + c // LANES, CHUNK // LANES)
        hidden_all = dot(normed_low, w_up[:, columns])
        grad_all = dot_nt(cotangent, w_down[columns, :])
        total = jnp.zeros((8, CHUNK), F32)
        for r in range(0, WIDE, STRIP):
            rows = slice(r, r + STRIP)
            hidden = hidden_all[rows] + bias
            square = hidden * hidden
            half = 0.5 + 0.5 * jnp.tanh(hidden * (slope + cubic * square))
            activated = hidden * half
            derivative = half + activated * (1.0 - half) * (2 * slope + (6 * cubic) * square)
            low = (grad_all[rows] * derivative).astype(BF16)
            activated_out[rows, columns] = activated.astype(BF16)
            grad_hidden[rows, columns] = low
            total += fold_rows(low.astype(F32))
        acc_small[:, 3 * D + c : 3 * D + c + CHUNK] += total
    grad_result = cotangent.astype(F32)
    acc_down[...] += dot_tn(cotangent, activated_out[...])
    acc_up[...] += dot_tn(normed_low, grad_hidden[...])
    grad_normed = dot_nt(grad_hidden[...], w_up[...])
    grad_middle = grad_result + normalize_back(grad_normed, gain, normed, rate)
    grad_middle_out[...] = grad_middle
    grad_middle_low = grad_middle.astype(BF16)
    acc_out[...] += dot_tn(attended[...], grad_middle_low)
    grad_attended_out[...] = dot_nt(grad_middle_low, w_out[...]).astype(BF16)
    acc_small[:, 0:D] += fold_rows(grad_middle_low.astype(F32))
    acc_small[:, D : 2 * D] += fold_rows(grad_normed * normed)
    acc_small[:, 2 * D : 3 * D] += fold_rows(grad_normed)
    acc_small[:, 3 * D + FF :] += fold_rows(grad_result)

    @pl.when(step == pl.num_programs(0) - 1)
    def _():
        matrix_to_flat(acc_out, D, D, flat, 0)
        matrix_to_flat(acc_up, D, FF, flat, ROW_UP - ROW_OUT)
        turned_to_flat(acc_down, FF, D, flat, ROW_DOWN - ROW_OUT)
        sums = jnp.sum(acc_small[...], axis=0, keepdims=True)
        base = ROW_SMALL - ROW_OUT
        flat[base : base + LATE_SMALL, :] = jnp.zeros((LATE_SMALL, LANES), F32)
        for i in range(sums.shape[1] // LANES):
            row = base + LATE_SMALL + i
            flat[row : row + 1, :] = sums[:, i * LANES : (i + 1) * LANES]
        flat[ROW_END - ROW_OUT :, :] = jnp.zeros((ROW_TOTAL - ROW_END, LANES), F32)
        first_out[...] = flat[:HEAD_ROWS, :]
        for target, out in enumerate((keep_out, send_out)):
            for p in range(PLANE):
                for z in range(1, Z):
                    share = ids[target * PLANE + p] + z * 2 * PLANE
                    rows = flat[pl.ds(share * SHARE - ROW_OUT, SHARE), :]
                    out[p * (Z - 1) + z - 1] = rows.astype(out.dtype)


def result_kernel(middle, activated, w_down, small, result_out):
    result = middle[...] + dot(activated[...], w_down[...]) + small_vector(small, BIAS_DOWN, 2)
    result_out[...] = result.astype(BF16)


def attend_back_kernel(
    ids, project, weights, grad_attended, normed_low, w_qkv, small, first_in,
    grad_project, keep_out, send_out, acc_qkv, acc_sum, flat, wide,
):
    step = pl.program_id(0)

    @pl.when(step == 0)
    def _():
        acc_qkv[...] = jnp.zeros_like(acc_qkv)
        acc_sum[...] = jnp.zeros_like(acc_sum)

    for s in range(BLOCK // SEQ):
        rows = slice(s * SEQ, (s + 1) * SEQ)
        query = spread_heads(project[rows, :D])
        key = spread_heads(project[rows, D : 2 * D])
        value = spread_heads(project[rows, 2 * D :])
        grad_rows = grad_attended[rows, :]
        grad_weights = dot_nt(grad_rows, value)
        scores_low, scores_turned, weights_turned = [], [], []
        for h in range(HEADS):
            columns = slice(h * SEQ, (h + 1) * SEQ)
            mine = weights[rows, columns]
            product = mine * grad_weights[:, columns]
            grad_scores = product - mine * jnp.sum(product, axis=-1, keepdims=True)
            scores_low.append(grad_scores.astype(BF16))
            scores_turned.append(grad_scores.T.astype(BF16))
            weights_turned.append(mine.T.astype(BF16))
        grad_query = dot(jnp.concatenate(scores_low, axis=1), key) * SCALE
        grad_key = dot(jnp.concatenate(scores_turned, axis=1), query) * SCALE
        grad_value = dot(jnp.concatenate(weights_turned, axis=1), spread_heads(grad_rows))
        grad_project[rows, :D] = grad_query.astype(BF16)
        grad_project[rows, D : 2 * D] = grad_key.astype(BF16)
        grad_project[rows, 2 * D :] = grad_value.astype(BF16)

    acc_qkv[...] += dot_tn(normed_low[...], grad_project[...])
    acc_sum[...] += fold_rows(grad_project[...].astype(F32))

    @pl.when(step == pl.num_programs(0) - 1)
    def _():
        gain = jnp.broadcast_to(small_vector(small, GAIN_ONE, 2), (LANES, D)).T
        shift = jnp.broadcast_to(small_vector(small, SHIFT_ONE, 2), (LANES, D)).T
        sums = jnp.sum(acc_sum[...], axis=0, keepdims=True)
        grad_gain = jnp.zeros((D, LANES), F32)
        grad_shift = jnp.zeros((D, LANES), F32)
        per_row = 3 * D // LANES
        for j in range(per_row):
            columns = slice(j * LANES, (j + 1) * LANES)
            weight = w_qkv[:, columns].astype(F32)
            grad_gain += acc_qkv[:, columns] * weight
            grad_shift += sums[:, columns] * weight
            flat[pl.ds(j, D, stride=per_row), :] = (
                acc_qkv[:, columns] * gain + sums[:, columns] * shift
            )
        flat[ROW_OUT:, :] = first_in[...]
        grad_gain = jnp.sum(grad_gain.T, axis=0, keepdims=True)
        grad_shift = jnp.sum(grad_shift.T, axis=0, keepdims=True)
        late = jnp.concatenate([grad_gain, grad_shift, sums[:, :D], sums[:, 2 * D :]], axis=1)
        side = jnp.concatenate(
            [late[:, i * LANES : (i + 1) * LANES] for i in range(LATE_SMALL)]
            + [jnp.zeros((SIDE_ROWS - LATE_SMALL, LANES), F32)],
            axis=0,
        )
        wide[SHARE:SIDE, :] = jnp.zeros((SIDE - SHARE, LANES), F32)
        for target, out in enumerate((keep_out, send_out)):
            for p in range(PLANE):
                share = ids[target * PLANE + p]
                wide[:SHARE, :] = flat[pl.ds(share * SHARE, SHARE), :]
                wide[SIDE:, :] = jnp.where(share == 2 * PLANE - 1, side, 0.0)
                out[p] = wide[...].astype(out.dtype)


def input_grad_kernel(tok, grad_project, grad_middle, w_qkv, small, input_grad_out):
    normed, rate = normalize(tok[...].astype(F32))
    grad_normed = dot_nt(grad_project[...], w_qkv[...])
    gain = small_vector(small, GAIN_ONE, 2)
    input_grad_out[...] = grad_middle[...] + normalize_back(grad_normed, gain, normed, rate)


def stack_kernel(*refs):
    for d, ref in enumerate(refs[:-1]):
        refs[-1][d] = ref[...]


def add_core_kernel(first, first_in, rest, rest_in, keep_out, *refs):
    sends, column = refs[:-1], refs[-1]
    end = SMALL_IN_SHARE + LATE_SMALL
    for p, out in enumerate((keep_out, *sends)):
        item = first[p] + first_in[p].astype(F32)
        span = slice(p * (Z - 1), (p + 1) * (Z - 1))
        column[0] = item[:SHARE, :]
        column[1:] = rest[span] + rest_in[span].astype(F32)
        column[Z - 1, SMALL_IN_SHARE:end, :] += item[SIDE : SIDE + LATE_SMALL, :]
        out[...] = column[...].astype(out.dtype)


def add_plane_kernel(ids, kept, *refs):
    arrived = refs[: PLANE - 1]
    keep_out, *sends, column = refs[PLANE - 1 :]
    column[...] = kept[...] + sum(item[...].astype(F32) for item in arrived)
    keep_out[...] = column[ids[0]]
    for d, out in enumerate(sends):
        out[...] = column[lax.rem(ids[0] + d + 1, Z)].astype(BF16)


def add_column_kernel(kept, *refs):
    refs[-1][...] = kept[...] + sum(item[...].astype(F32) for item in refs[:-1])


def rows_spec(columns, rows=BLOCK):
    return pl.BlockSpec((rows, columns), lambda i: (i, 0))


def whole_spec(item):
    return pl.BlockSpec(item.shape, lambda i: (0,) * len(item.shape))


def like(*shape, kind=F32):
    return jax.ShapeDtypeStruct(shape, kind)


SMEM_SPEC = pl.BlockSpec(memory_space=pltpu.SMEM)
PARAMS = pltpu.CompilerParams(
    dimension_semantics=("arbitrary",), vmem_limit_bytes=VMEM_BYTES
)


def cost(us):
    return pl.CostEstimate(flops=int(us * 1e9), bytes_accessed=1 << 20, transcendentals=0)


def small_call(kernel, name, ids, inputs, outs, scratch=()):
    with_ids = ids is not None
    results = pl.pallas_call(
        kernel,
        in_specs=[SMEM_SPEC] * with_ids + [pl.BlockSpec(memory_space=pltpu.VMEM)] * len(inputs),
        out_specs=[pl.BlockSpec(memory_space=pltpu.VMEM)] * len(outs),
        out_shape=list(outs),
        scratch_shapes=list(scratch),
        compiler_params=pltpu.CompilerParams(vmem_limit_bytes=VMEM_BYTES),
        cost_estimate=cost(1),
        name=name,
    )(*([ids] if with_ids else []), *inputs)
    return results if len(outs) > 1 else results[0]


def attend(ids, segments, tokens, bufs):
    rows = tokens.shape[0]
    total = sum(buf.shape[0] * buf.shape[1] for buf in bufs)
    blocked = [
        like(rows, 3 * D, kind=BF16), like(rows, HEADS * SEQ), like(rows, D, kind=BF16),
        like(rows, D, kind=BF16),
    ]
    fixed = [
        like(D, 3 * D, kind=BF16), like(D, D, kind=BF16), like(D, FF, kind=BF16),
        like(FF, D, kind=BF16), like(SMALL_ROWS, LANES),
    ]
    return pl.pallas_call(
        functools.partial(attend_kernel, len(bufs)),
        grid=(rows // BLOCK,),
        in_specs=[
            SMEM_SPEC,
            pl.BlockSpec((BLOCK // SEQ, 1, SEQ), lambda i: (i, 0, 0)),
            rows_spec(D),
        ]
        + [whole_spec(buf) for buf in bufs],
        out_specs=[rows_spec(item.shape[1]) for item in blocked] + [whole_spec(item) for item in fixed],
        out_shape=blocked + fixed,
        scratch_shapes=[pltpu.VMEM((total, LANES), F32)],
        compiler_params=PARAMS,
        cost_estimate=cost(7),
        name="attend",
    )(ids, segments, tokens, *bufs)


def feed(ids, tokens, attended, cotangent, w_out, w_up, w_down, small, send_kind):
    rows = tokens.shape[0]
    small_rows = SMALL_ROWS - LATE_SMALL
    blocked = [
        like(rows, D), like(rows, FF, kind=BF16), like(rows, D), like(rows, D, kind=BF16),
    ]
    fixed = [
        like(PLANE * (Z - 1), SHARE, LANES),
        like(PLANE * (Z - 1), SHARE, LANES, kind=send_kind),
        like(HEAD_ROWS, LANES),
    ]
    return pl.pallas_call(
        feed_kernel,
        grid=(rows // WIDE,),
        in_specs=[SMEM_SPEC]
        + [rows_spec(D, WIDE)] * 3
        + [whole_spec(item) for item in (w_out, w_up, w_down, small)],
        out_specs=[rows_spec(item.shape[1], WIDE) for item in blocked]
        + [whole_spec(item) for item in fixed],
        out_shape=blocked + fixed,
        scratch_shapes=[
            pltpu.VMEM((WIDE, FF), BF16),
            pltpu.VMEM((D, D), F32),
            pltpu.VMEM((D, FF), F32),
            pltpu.VMEM((D, FF), F32),
            pltpu.VMEM((8, small_rows * LANES), F32),
            pltpu.VMEM((ROW_TOTAL - ROW_OUT, LANES), F32),
        ],
        compiler_params=PARAMS,
        cost_estimate=cost(10),
        name="feed",
    )(ids, tokens, attended, cotangent, w_out, w_up, w_down, small)


def result(middle, activated, w_down, small):
    rows = middle.shape[0]
    return pl.pallas_call(
        result_kernel,
        grid=(rows // BLOCK,),
        in_specs=[rows_spec(D), rows_spec(FF), whole_spec(w_down), whole_spec(small)],
        out_specs=rows_spec(D),
        out_shape=like(rows, D, kind=BF16),
        compiler_params=PARAMS,
        cost_estimate=cost(2),
        name="result",
    )(middle, activated, w_down, small)


def attend_back(ids, project, weights, grad_attended, normed_low, w_qkv, small, first, send_kind):
    rows = project.shape[0]
    fixed = [
        like(PLANE, SIDE + SIDE_ROWS, LANES),
        like(PLANE, SIDE + SIDE_ROWS, LANES, kind=send_kind),
    ]
    blocked = (project, weights, grad_attended, normed_low)
    return pl.pallas_call(
        attend_back_kernel,
        grid=(rows // BLOCK,),
        in_specs=[SMEM_SPEC]
        + [rows_spec(item.shape[1]) for item in blocked]
        + [whole_spec(item) for item in (w_qkv, small, first)],
        out_specs=[rows_spec(3 * D)] + [whole_spec(item) for item in fixed],
        out_shape=[like(rows, 3 * D, kind=BF16)] + fixed,
        scratch_shapes=[
            pltpu.VMEM((D, 3 * D), F32),
            pltpu.VMEM((8, 3 * D), F32),
            pltpu.VMEM((FIRST_ROWS, LANES), F32),
            pltpu.VMEM((SIDE + SIDE_ROWS, LANES), F32),
        ],
        compiler_params=PARAMS,
        cost_estimate=cost(6),
        name="attend_back",
    )(ids, *blocked, w_qkv, small, first)


def input_gradient(tokens, grad_project, grad_middle, w_qkv, small):
    rows = tokens.shape[0]
    blocked = (tokens, grad_project, grad_middle)
    return pl.pallas_call(
        input_grad_kernel,
        grid=(rows // BLOCK,),
        in_specs=[rows_spec(item.shape[1]) for item in blocked] + [whole_spec(w_qkv), whole_spec(small)],
        out_specs=rows_spec(D),
        out_shape=like(rows, D),
        compiler_params=PARAMS,
        cost_estimate=cost(3),
        name="input_grad",
    )(*blocked, w_qkv, small)


def block(tokens, segment_ids, cotangent, share_ids, shares, grad_ids, send_kind, core_exchange):
    segments = segment_ids.reshape(-1, 1, SEQ)
    project, weights, attended, normed_low, w_qkv, w_out, w_up, w_down, small = attend(
        share_ids, segments, tokens, shares
    )
    middle, activated, grad_middle, grad_attended, rest, rest_send, first_grad = feed(
        grad_ids, tokens, attended, cotangent, w_out, w_up, w_down, small, send_kind
    )
    rest_in = core_exchange(rest_send)
    grad_project, first, first_send = attend_back(
        grad_ids, project, weights, grad_attended, normed_low, w_qkv, small, first_grad, send_kind
    )
    first_in = core_exchange(first_send)
    outputs = result(middle, activated, w_down, small)
    input_grad = input_gradient(tokens, grad_project, grad_middle, w_qkv, small)
    return outputs, input_grad, first, first_in, rest, rest_in


def local_any(n, tokens, params, segment_ids, cotangent):
    gathered = lax.all_gather(params, "fsdp", axis=0)
    ids = jnp.arange(n, dtype=jnp.int32)
    order = jnp.array([p * 2 + c for c in range(2) for p in range(PLANE)], jnp.int32)
    outputs, input_grad, first, first_send, rest, rest_send = block(
        tokens, segment_ids, cotangent, ids, [gathered], order, F32, lambda values: values
    )
    first = jnp.stack([first, first_send], axis=1)
    rest = jnp.stack([rest, rest_send]).reshape(2, PLANE, Z - 1, SHARE, LANES).transpose(2, 1, 0, 3, 4)
    flat = jnp.concatenate(
        [
            first[:, :, :SHARE].reshape(-1, LANES),
            rest.reshape(-1, LANES),
            jnp.zeros((n * params.shape[0] - ROW_TOTAL, LANES), F32),
        ],
        axis=0,
    )
    flat = flat.at[ROW_SMALL : ROW_SMALL + LATE_SMALL].add(
        first[PLANE - 1, 1, SIDE : SIDE + LATE_SMALL]
    )
    param_grad = lax.psum_scatter(flat, "fsdp", scatter_dimension=0, tiled=True)
    return outputs, input_grad, param_grad


def index_of(z, plane, core):
    return (z * PLANE + plane) * 2 + core


def move(values, step_z, step_plane, step_core):
    pairs = [
        (index_of(z, p, c), index_of((z + step_z) % Z, p ^ step_plane, c ^ step_core))
        for z in range(Z)
        for p in range(PLANE)
        for c in range(2)
    ]
    return lax.ppermute(values, "fsdp", pairs)


def local_slice(tokens, params, segment_ids, cotangent):
    me = lax.axis_index("fsdp").astype(jnp.int32)
    z, plane, core = me // (2 * PLANE), (me // 2) % PLANE, me % 2
    planes = [(dc, dp) for dc in range(2) for dp in range(PLANE)]
    share_ids = jnp.stack(
        [index_of((z - dz) % Z, plane ^ dp, core ^ dc) for dc, dp in planes for dz in range(Z)]
    )
    grad_ids = jnp.stack([(plane ^ dp) * 2 + (core ^ dc) for dc, dp in planes])

    column = small_call(
        stack_kernel, "stack", None, [params] + [move(params, d, 0, 0) for d in range(1, Z)],
        [like(Z, SHARE, LANES, kind=BF16)],
    )
    same = [column] + [move(column, 0, d, 0) for d in range(1, PLANE)]
    shares = same + [move(item, 0, 0, 1) for item in same]
    outputs, input_grad, first, first_in, rest, rest_in = block(
        tokens, segment_ids, cotangent, share_ids, shares, grad_ids, BF16,
        lambda values: move(values, 0, 0, 1),
    )

    part = (Z, SHARE, LANES)
    kept, *sends = small_call(
        add_core_kernel, "add_core", None, [first, first_in, rest, rest_in],
        [like(*part)] + [like(*part, kind=BF16)] * (PLANE - 1), [pltpu.VMEM(part, F32)],
    )
    arrived = [move(item, 0, d + 1, 0) for d, item in enumerate(sends)]
    kept, *sends = small_call(
        add_plane_kernel, "add_plane", z.reshape(1), [kept] + arrived,
        [like(SHARE, LANES)] + [like(SHARE, LANES, kind=BF16)] * (Z - 1), [pltpu.VMEM(part, F32)],
    )
    arrived = [move(item, d + 1, 0, 0) for d, item in enumerate(sends)]
    param_grad = small_call(
        add_column_kernel, "add_column", None, [kept] + arrived, [like(SHARE, LANES)]
    )
    return outputs, input_grad, param_grad


def solution(mesh):
    n = mesh.shape["fsdp"]
    local = local_slice if n == 2 * PLANE * Z else functools.partial(local_any, n)
    in_specs = (P("fsdp", None), P("fsdp", None), P("fsdp"), P("fsdp", None))
    out_specs = (P("fsdp", None), P("fsdp", None), P("fsdp", None))
    return jax.shard_map(local, mesh=mesh, in_specs=in_specs, out_specs=out_specs, check_vma=False)
```

time: 82.9 us -> 69.3 us (0.84)
  waiting for transfers between devices: 28.8 us -> 21.2 us
  other arithmetic: 3.3 us -> 0 us
  Pallas kernels: 29.1 us -> 26.9 us
  local copies, waits for them, and re-layouts: 2.13 us -> 1.02 us
    ppermute x17 -> x18, waiting for transfers between devices: 28.8 us -> 21.2 us  [move(): return lax.ppermute(values, 'fsdp', pairs)]
    another operation x3 -> x0, other arithmetic: 2.63 us -> none
    pallas_call x2 -> x8, Pallas kernels: 21.4 us -> 19.9 us  [the longest x1 8.16 us: feed(): pl.pallas_call(feed_kernel, grid=(rows // WIDE,), in_specs=[SMEM_SPEC] +...]
    unnamed x8, local copies, waits for them, and re-layouts: 1.74 us -> 0.82 us
    ppermute x17 -> x18, starting transfers between devices: 18.5 us -> 19.3 us  [move(): return lax.ppermute(values, 'fsdp', pairs)]
  transfers between devices with their start and end apart: 17 -> 18, of which waited for: 12 -> 14; matrix products, arithmetic and copies ran while one was open for 0% -> 0% of each run, Pallas kernels for 0% -> 15%
where the time goes in v5:
time: 69.3 us; the launch traced here: 69.2 us
  Pallas kernels  26.9 us (39%)
  waiting for transfers between devices  21.2 us (31%)
  starting transfers between devices  19.3 us (28%)
  local copies, waits for them, and re-layouts  1.02 us (1%)
  between operations  0.72 us (1%)
    ppermute x18, waiting for transfers between devices, move(): return lax.ppermute(values, 'fsdp', pairs)  21.2 us
    ppermute x18, starting transfers between devices, move(): return lax.ppermute(values, 'fsdp', pairs)  19.3 us
    pallas_call x1, Pallas kernels, feed(): pl.pallas_call(feed_kernel, grid=(rows // WIDE,), in_specs=[SMEM_SPEC] +...  8.16 us
    pallas_call x1, Pallas kernels, attend(): pl.pallas_call(functools.partial(attend_kernel, len(bufs)), grid=(rows //...  7.04 us
    pallas_call x1, Pallas kernels, attend_back(): pl.pallas_call(attend_back_kernel, grid=(rows // BLOCK,), in_specs=[SMEM_...  5.71 us
    pallas_call x1, Pallas kernels, input_gradient(): pl.pallas_call(input_grad_kernel, grid=(rows // BLOCK,), in_specs=[rows_s...  2.7 us
    pallas_call x1, Pallas kernels, result(): pl.pallas_call(result_kernel, grid=(rows // BLOCK,), in_specs=[rows_spec(...  2.24 us
  transfers between devices with their start and end apart: 18, of which 14 were waited for; matrix products, arithmetic and copies ran while one was open for 0% of the time, Pallas kernels for 15%

profile of v5, /device:TPU:0, one launch (start us, length us, event | category | flops | bytes accessed | tf_op | source)
XLA Modules:
  0.0 69.2 jit_solution(15619261294071237108)
XLA Ops:
  0.6 3.1 %collective-permute-start = (bf16[193,128]{1,0:T(8,128)(2,1)}, bf16[193,128]{1,0:T(8,128)(2,1)S(1)}, u32[]{:S(2)}, u32[]{:S(2)}) collective-permute-start(bf16[193,128]{1,0:T(8,128)(2,1)} %refs_0_.1), channel_id=1, source_target_pairs={{0,8},{1,9},{2,10},{3,11},{4,12},{5,13},{6,14},{7,15},{8,16},{9,17... | collective-permute-start | bytes 148232 | tf_op jit(solution)/shard_map/ppermute | solution.py:570
  3.7 2.6 %collective-permute-start.1 = (bf16[193,128]{1,0:T(8,128)(2,1)}, bf16[193,128]{1,0:T(8,128)(2,1)S(1)}, u32[]{:S(2)}, u32[]{:S(2)}) collective-permute-start(bf16[193,128]{1,0:T(8,128)(2,1)} %refs_0_.1), channel_id=1, source_target_pairs={{0,16},{1,17},{2,18},{3,19},{4,20},{5,21},{6,22},{7,23},{8,24},{9,... | collective-permute-start | bytes 148232 | tf_op jit(solution)/shard_map/ppermute | solution.py:570
  6.3 1.3 %collective-permute-start.2 = (bf16[193,128]{1,0:T(8,128)(2,1)}, bf16[193,128]{1,0:T(8,128)(2,1)S(1)}, u32[]{:S(2)}, u32[]{:S(2)}) collective-permute-start(bf16[193,128]{1,0:T(8,128)(2,1)} %refs_0_.1), channel_id=1, source_target_pairs={{0,24},{1,25},{2,26},{3,27},{4,28},{5,29},{6,30},{7,31},{8,0},{9,1... | collective-permute-start | bytes 148232 | tf_op jit(solution)/shard_map/ppermute | solution.py:570
  7.7 0.5 collective-permute-done.refs_1_
  8.2 2.1 %collective-permute-done.1.refs_2_ = bf16[193,128]{1,0:T(8,128)(2,1)S(1)} collective-permute-done((bf16[193,128]{1,0:T(8,128)(2,1)}, bf16[193,128]{1,0:T(8,128)(2,1)S(1)}, u32[]{:S(2)}, u32[]{:S(2)}) %collective-permute-start.1) | collective-permute-done | bytes 49440 | tf_op jit(solution)/shard_map/ppermute | solution.py:570
  10.2 0.5 collective-permute-done.2.refs_3_
  10.7 0.8 %copy-done.2 = bf16[193,128]{1,0:T(8,128)(2,1)S(1)} copy-done((bf16[193,128]{1,0:T(8,128)(2,1)S(1)}, bf16[193,128]{1,0:T(8,128)(2,1)}, u32[]{:S(2)}) %copy-start.2) | copy-done | bytes 49432
  11.5 1.7 %collective-permute-start.3 = (bf16[4,193,128]{2,1,0:T(8,128)(2,1)S(1)}, bf16[4,193,128]{2,1,0:T(8,128)(2,1)S(1)}, u32[]{:S(2)}, u32[]{:S(2)}) collective-permute-start(bf16[4,193,128]{2,1,0:T(8,128)(2,1)S(1)} %stack.169.refs_0_), channel_id=1, source_target_pairs={{0,2},{1,3},{2,0},{3,1},{4,6},{5,7},{6,4},{7,5},{8,10},{9,11},{10,... | collective-permute-start | bytes 592904 | tf_op jit(solution)/shard_map/ppermute | solution.py:570
  13.2 1.5 %collective-permute-start.4 = (bf16[4,193,128]{2,1,0:T(8,128)(2,1)S(1)}, bf16[4,193,128]{2,1,0:T(8,128)(2,1)S(1)}, u32[]{:S(2)}, u32[]{:S(2)}) collective-permute-start(bf16[4,193,128]{2,1,0:T(8,128)(2,1)S(1)} %stack.169.refs_0_), channel_id=1, source_target_pairs={{0,4},{1,5},{2,6},{3,7},{4,0},{5,1},{6,2},{7,3},{8,12},{9,13},{10,... | collective-permute-start | bytes 592904 | tf_op jit(solution)/shard_map/ppermute | solution.py:570
  14.7 0.3 collective-permute-start.5
  15.1 0.0 collective-permute-start.6
  15.1 4.5 %collective-permute-done.3.refs_1_ = bf16[4,193,128]{2,1,0:T(8,128)(2,1)S(1)} collective-permute-done((bf16[4,193,128]{2,1,0:T(8,128)(2,1)S(1)}, bf16[4,193,128]{2,1,0:T(8,128)(2,1)S(1)}, u32[]{:S(2)}, u32[]{:S(2)}) %collective-permute-start.3) | collective-permute-done | bytes 197664 | tf_op jit(solution)/shard_map/ppermute | solution.py:570
  19.6 0.0 collective-permute-start.7
  19.6 3.4 %collective-permute-done.4.refs_2_ = bf16[4,193,128]{2,1,0:T(8,128)(2,1)S(1)} collective-permute-done((bf16[4,193,128]{2,1,0:T(8,128)(2,1)S(1)}, bf16[4,193,128]{2,1,0:T(8,128)(2,1)S(1)}, u32[]{:S(2)}, u32[]{:S(2)}) %collective-permute-start.4) | collective-permute-done | bytes 197664 | tf_op jit(solution)/shard_map/ppermute | solution.py:570
  23.0 0.0 collective-permute-start.8
  23.0 0.0 collective-permute-done.5.refs_3_
  23.0 0.5 collective-permute-start.9
  23.5 0.1 stack.135.ids
  23.6 0.1 stack.168.ids
  23.7 0.0 collective-permute-done.6.refs_4_
  23.7 0.0 collective-permute-done.7.refs_5_
  23.7 0.7 %collective-permute-done.8.refs_6_ = bf16[4,193,128]{2,1,0:T(8,128)(2,1)S(1)} collective-permute-done((bf16[4,193,128]{2,1,0:T(8,128)(2,1)S(1)}, bf16[4,193,128]{2,1,0:T(8,128)(2,1)S(1)}, u32[]{:S(2)}, u32[]{:S(2)}) %collective-permute-start.8) | collective-permute-done | bytes 197664 | tf_op jit(solution)/shard_map/ppermute | solution.py:570
  24.5 0.3 collective-permute-done.9.refs_7_
  24.8 0.0 copy-done.1
  24.8 7.0 %attend.1 = (bf16[1024,768]{1,0:T(8,128)(2,1)S(1)}, f32[1024,512]{1,0:T(8,128)S(1)}, bf16[1024,256]{1,0:T(8,128)(2,1)S(1)}, bf16[1024,256]{1,0:T(8,128)(2,1)S(1)...) custom-call(s32[32]{0:T(128)S(1)} %stack.168.ids, ...), custom_call_target="tpu_custom_call" | custom-call | flops 7000000000 | bytes 1048576 | tf_op jit(solution)/shard_map/attend/pallas_call | solution.py:409
  31.8 8.2 %feed.1 = (f32[1024,256]{1,0:T(8,128)S(1)}, bf16[1024,1024]{1,0:T(8,128)(2,1)S(1)}, f32[1024,256]{1,0:T(8,128)S(1)}, bf16[1024,256]{1,0:T(8,128)(2,1)S(1)}, f32[...) custom-call(s32[8]{0:T(128)S(1)} %stack.135.ids, ...), custom_call_target="tpu_custom_call" | custom-call | flops 10000000000 | bytes 1048576 | tf_op jit(solution)/shard_map/feed/pallas_call | solution.py:438
  40.0 0.3 collective-permute-start.11
  40.3 5.7 %attend_back.1 = (bf16[1024,768]{1,0:T(8,128)(2,1)S(1)}, f32[4,224,128]{2,1,0:T(8,128)S(1)}, bf16[4,224,128]{2,1,0:T(8,128)(2,1)S(1)}) custom-call(s32[8]{0:T(128)S(1)} %stack.135.ids, bf16[1024,768]{1,0:T(8,128)(2,1)S(1)} %get-tuple-element.37.project, f32[1024,512]{1,0:T(8,128)S(1)} %get-tuple-element.38.weights, ...), custom_call_target="tpu_custom_call" | custom-call | flops 6000000000 | bytes 1048576 | tf_op jit(solution)/shard_map/attend_back/pallas_call | solution.py:482
  46.0 0.4 collective-permute-start.10
  46.3 1.2 %collective-permute-done.10.first_in = bf16[4,224,128]{2,1,0:T(8,128)(2,1)S(1)} collective-permute-done((bf16[4,224,128]{2,1,0:T(8,128)(2,1)S(1)}, bf16[4,224,128]{2,1,0:T(8,128)(2,1)S(1)}, u32[]{:S(2)}, u32[]{:S(2)}) %collective-permute-start.10) | collective-permute-done | bytes 229408 | tf_op jit(solution)/shard_map/ppermute | solution.py:570
  47.5 0.0 collective-permute-done.11.rest_in
  47.5 0.2 add_core.1
  47.8 0.7 %collective-permute-start.12 = (bf16[4,193,128]{2,1,0:T(8,128)(2,1)S(1)}, bf16[4,193,128]{2,1,0:T(8,128)(2,1)S(1)}, u32[]{:S(2)}, u32[]{:S(2)}) collective-permute-start(bf16[4,193,128]{2,1,0:T(8,128)(2,1)S(1)} %get-tuple-element.50), channel_id=1, source_target_pairs={{0,2},{1,3},{2,0},{3,1},{4,6},{5,7},{6,4},{7,5},{8,10},{9,11},{10,... | collective-permute-start | bytes 592904 | tf_op jit(solution)/shard_map/ppermute | solution.py:570
  48.5 1.2 %collective-permute-start.13 = (bf16[4,193,128]{2,1,0:T(8,128)(2,1)S(1)}, bf16[4,193,128]{2,1,0:T(8,128)(2,1)S(1)}, u32[]{:S(2)}, u32[]{:S(2)}) collective-permute-start(bf16[4,193,128]{2,1,0:T(8,128)(2,1)S(1)} %get-tuple-element.51), channel_id=1, source_target_pairs={{0,4},{1,5},{2,6},{3,7},{4,0},{5,1},{6,2},{7,3},{8,12},{9,13},{10,... | collective-permute-start | bytes 592904 | tf_op jit(solution)/shard_map/ppermute | solution.py:570
  49.7 1.6 %collective-permute-start.14 = (bf16[4,193,128]{2,1,0:T(8,128)(2,1)S(1)}, bf16[4,193,128]{2,1,0:T(8,128)(2,1)S(1)}, u32[]{:S(2)}, u32[]{:S(2)}) collective-permute-start(bf16[4,193,128]{2,1,0:T(8,128)(2,1)S(1)} %get-tuple-element.52), channel_id=1, source_target_pairs={{0,6},{1,7},{2,4},{3,5},{4,2},{5,3},{6,0},{7,1},{8,14},{9,15},{10,... | collective-permute-start | bytes 592904 | tf_op jit(solution)/shard_map/ppermute | solution.py:570
  51.3 2.7 %input_grad.1 = f32[1024,256]{1,0:T(8,128)} custom-call(bf16[1024,256]{1,0:T(8,128)(2,1)S(1)} %copy-done.1, bf16[1024,768]{1,0:T(8,128)(2,1)S(1)} %get-tuple-element.43.grad_project, f32[1024,256]{1,0:T(8,128)S(1)} %get-tuple-element.44.grad_middle, bf16[256,768]{1,0:T(8,128)(2,1)S(1)} %get-tuple-element.41.w_qkv, f32[24,128]{1,0:T(8,128)S(1)} %get-tuple-element.34.small), custom_call_target="tpu_custom_call" | custom-call | flops 3000000000 | bytes 1048576 | tf_op jit(solution)/shard_map/input_grad/pallas_call | solution.py:505
  54.0 1.7 %collective-permute-done.12.refs_0_ = bf16[4,193,128]{2,1,0:T(8,128)(2,1)S(1)} collective-permute-done((bf16[4,193,128]{2,1,0:T(8,128)(2,1)S(1)}, bf16[4,193,128]{2,1,0:T(8,128)(2,1)S(1)}, u32[]{:S(2)}, u32[]{:S(2)}) %collective-permute-start.12) | collective-permute-done | bytes 197664 | tf_op jit(solution)/shard_map/ppermute | solution.py:570
  55.7 0.2 collective-permute-done.13.refs_1_
  55.9 4.3 %collective-permute-done.14.refs_2_ = bf16[4,193,128]{2,1,0:T(8,128)(2,1)S(1)} collective-permute-done((bf16[4,193,128]{2,1,0:T(8,128)(2,1)S(1)}, bf16[4,193,128]{2,1,0:T(8,128)(2,1)S(1)}, u32[]{:S(2)}, u32[]{:S(2)}) %collective-permute-start.14) | collective-permute-done | bytes 197664 | tf_op jit(solution)/shard_map/ppermute | solution.py:570
  60.2 0.2 add_plane.1
  60.4 1.6 %collective-permute-start.15 = (bf16[193,128]{1,0:T(8,128)(2,1)S(1)}, bf16[193,128]{1,0:T(8,128)(2,1)S(1)}, u32[]{:S(2)}, u32[]{:S(2)}) collective-permute-start(bf16[193,128]{1,0:T(8,128)(2,1)S(1)} %get-tuple-element.54), channel_id=1, source_target_pairs={{0,8},{1,9},{2,10},{3,11},{4,12},{5,13},{6,14},{7,15},{8,16},{9,17... | collective-permute-start | bytes 148232 | tf_op jit(solution)/shard_map/ppermute | solution.py:570
  62.0 1.9 %collective-permute-start.16 = (bf16[193,128]{1,0:T(8,128)(2,1)S(1)}, bf16[193,128]{1,0:T(8,128)(2,1)S(1)}, u32[]{:S(2)}, u32[]{:S(2)}) collective-permute-start(bf16[193,128]{1,0:T(8,128)(2,1)S(1)} %get-tuple-element.55), channel_id=1, source_target_pairs={{0,16},{1,17},{2,18},{3,19},{4,20},{5,21},{6,22},{7,23},{8,24},{9,... | collective-permute-start | bytes 148232 | tf_op jit(solution)/shard_map/ppermute | solution.py:570
  63.9 0.5 collective-permute-start.17
  64.4 2.2 %result.1 = bf16[1024,256]{1,0:T(8,128)(2,1)} custom-call(f32[1024,256]{1,0:T(8,128)S(1)} %get-tuple-element.35.middle, bf16[1024,1024]{1,0:T(8,128)(2,1)S(1)} %get-tuple-element.36.activated, bf16[1024,256]{1,0:T(8,128)(2,1)S(1)} %get-tuple-element.33.w_down, f32[24,128]{1,0:T(8,128)S(1)} %get-tuple-element.34.small), custom_call_target="tpu_custom_call" | custom-call | flops 2000000000 | bytes 1048576 | tf_op jit(solution)/shard_map/result/pallas_call | solution.py:463
  66.7 0.2 collective-permute-done.15.refs_0_
  66.9 1.4 %collective-permute-done.16.refs_1_ = bf16[193,128]{1,0:T(8,128)(2,1)S(1)} collective-permute-done((bf16[193,128]{1,0:T(8,128)(2,1)S(1)}, bf16[193,128]{1,0:T(8,128)(2,1)S(1)}, u32[]{:S(2)}, u32[]{:S(2)}) %collective-permute-start.16) | collective-permute-done | bytes 49440 | tf_op jit(solution)/shard_map/ppermute | solution.py:570
  68.3 0.2 collective-permute-done.17.refs_2_
  68.5 0.7 add_column.1
  (7 shorter events, 0.0 us)
Async XLA Ops:
  0.6 24.1 %copy-start.1 = (bf16[1024,256]{1,0:T(8,128)(2,1)S(1)}, bf16[1024,256]{1,0:T(8,128)(2,1)}, u32[]{:S(2)}) copy-start(bf16[1024,256]{1,0:T(8,128)(2,1)} %tok.5) | copy-start | bytes 1572868
  0.6 7.5 %collective-permute-start = (bf16[193,128]{1,0:T(8,128)(2,1)}, bf16[193,128]{1,0:T(8,128)(2,1)S(1)}, u32[]{:S(2)}, u32[]{:S(2)}) collective-permute-start(bf16[193,128]{1,0:T(8,128)(2,1)} %refs_0_.1), channel_id=1, source_target_pairs={{0,8},{1,9},{2,10},{3,11},{4,12},{5,13},{6,14},{7,15},{8,16},{9,17... | collective-permute-start | bytes 148232 | tf_op jit(solution)/shard_map/ppermute | solution.py:570
  3.7 6.5 %collective-permute-start.1 = (bf16[193,128]{1,0:T(8,128)(2,1)}, bf16[193,128]{1,0:T(8,128)(2,1)S(1)}, u32[]{:S(2)}, u32[]{:S(2)}) collective-permute-start(bf16[193,128]{1,0:T(8,128)(2,1)} %refs_0_.1), channel_id=1, source_target_pairs={{0,16},{1,17},{2,18},{3,19},{4,20},{5,21},{6,22},{7,23},{8,24},{9,... | collective-permute-start | bytes 148232 | tf_op jit(solution)/shard_map/ppermute | solution.py:570
  6.3 4.4 %collective-permute-start.2 = (bf16[193,128]{1,0:T(8,128)(2,1)}, bf16[193,128]{1,0:T(8,128)(2,1)S(1)}, u32[]{:S(2)}, u32[]{:S(2)}) collective-permute-start(bf16[193,128]{1,0:T(8,128)(2,1)} %refs_0_.1), channel_id=1, source_target_pairs={{0,24},{1,25},{2,26},{3,27},{4,28},{5,29},{6,30},{7,31},{8,0},{9,1... | collective-permute-start | bytes 148232 | tf_op jit(solution)/shard_map/ppermute | solution.py:570
  10.7 0.8 %copy-start.2 = (bf16[193,128]{1,0:T(8,128)(2,1)S(1)}, bf16[193,128]{1,0:T(8,128)(2,1)}, u32[]{:S(2)}) copy-start(bf16[193,128]{1,0:T(8,128)(2,1)} %refs_0_.1) | copy-start | bytes 148228
  11.5 13.2 %copy-start.3 = (s32[1024]{0:T(1024)S(1)}, s32[1024]{0:T(1024)}, u32[]{:S(2)}) copy-start(s32[1024]{0:T(1024)} %param.6) | copy-start | bytes 12292
  11.5 8.1 %collective-permute-start.3 = (bf16[4,193,128]{2,1,0:T(8,128)(2,1)S(1)}, bf16[4,193,128]{2,1,0:T(8,128)(2,1)S(1)}, u32[]{:S(2)}, u32[]{:S(2)}) collective-permute-start(bf16[4,193,128]{2,1,0:T(8,128)(2,1)S(1)} %stack.169.refs_0_), channel_id=1, source_target_pairs={{0,2},{1,3},{2,0},{3,1},{4,6},{5,7},{6,4},{7,5},{8,10},{9,11},{10,... | collective-permute-start | bytes 592904 | tf_op jit(solution)/shard_map/ppermute | solution.py:570
  13.2 9.8 %collective-permute-start.4 = (bf16[4,193,128]{2,1,0:T(8,128)(2,1)S(1)}, bf16[4,193,128]{2,1,0:T(8,128)(2,1)S(1)}, u32[]{:S(2)}, u32[]{:S(2)}) collective-permute-start(bf16[4,193,128]{2,1,0:T(8,128)(2,1)S(1)} %stack.169.refs_0_), channel_id=1, source_target_pairs={{0,4},{1,5},{2,6},{3,7},{4,0},{5,1},{6,2},{7,3},{8,12},{9,13},{10,... | collective-permute-start | bytes 592904 | tf_op jit(solution)/shard_map/ppermute | solution.py:570
  14.7 8.3 %collective-permute-start.5 = (bf16[4,193,128]{2,1,0:T(8,128)(2,1)S(1)}, bf16[4,193,128]{2,1,0:T(8,128)(2,1)S(1)}, u32[]{:S(2)}, u32[]{:S(2)}) collective-permute-start(bf16[4,193,128]{2,1,0:T(8,128)(2,1)S(1)} %stack.169.refs_0_), channel_id=1, source_target_pairs={{0,6},{1,7},{2,4},{3,5},{4,2},{5,3},{6,0},{7,1},{8,14},{9,15},{10,... | collective-permute-start | bytes 592904 | tf_op jit(solution)/shard_map/ppermute | solution.py:570
  15.1 8.6 %collective-permute-start.6 = (bf16[4,193,128]{2,1,0:T(8,128)(2,1)S(1)}, bf16[4,193,128]{2,1,0:T(8,128)(2,1)S(1)}, u32[]{:S(2)}, u32[]{:S(2)}) collective-permute-start(bf16[4,193,128]{2,1,0:T(8,128)(2,1)S(1)} %stack.169.refs_0_), channel_id=1, source_target_pairs={{0,1},{1,0},{2,3},{3,2},{4,5},{5,4},{6,7},{7,6},{8,9},{9,8},{10,11... | collective-permute-start | bytes 592904 | tf_op jit(solution)/shard_map/ppermute | solution.py:570
  19.6 4.1 %collective-permute-start.7 = (bf16[4,193,128]{2,1,0:T(8,128)(2,1)S(1)}, bf16[4,193,128]{2,1,0:T(8,128)(2,1)S(1)}, u32[]{:S(2)}, u32[]{:S(2)}) collective-permute-start(bf16[4,193,128]{2,1,0:T(8,128)(2,1)S(1)} %collective-permute-done.3.refs_1_), channel_id=1, source_target_pairs={{0,1},{1,0},{2,3},{3,2},{4,5},{5,4},{6,7},{7,6},{8,9},{9,8},{10,11... | collective-permute-start | bytes 592904 | tf_op jit(solution)/shard_map/ppermute | solution.py:570
  23.0 1.5 %collective-permute-start.8 = (bf16[4,193,128]{2,1,0:T(8,128)(2,1)S(1)}, bf16[4,193,128]{2,1,0:T(8,128)(2,1)S(1)}, u32[]{:S(2)}, u32[]{:S(2)}) collective-permute-start(bf16[4,193,128]{2,1,0:T(8,128)(2,1)S(1)} %collective-permute-done.4.refs_2_), channel_id=1, source_target_pairs={{0,1},{1,0},{2,3},{3,2},{4,5},{5,4},{6,7},{7,6},{8,9},{9,8},{10,11... | collective-permute-start | bytes 592904 | tf_op jit(solution)/shard_map/ppermute | solution.py:570
  23.0 1.7 %collective-permute-start.9 = (bf16[4,193,128]{2,1,0:T(8,128)(2,1)S(1)}, bf16[4,193,128]{2,1,0:T(8,128)(2,1)S(1)}, u32[]{:S(2)}, u32[]{:S(2)}) collective-permute-start(bf16[4,193,128]{2,1,0:T(8,128)(2,1)S(1)} %collective-permute-done.5.refs_3_), channel_id=1, source_target_pairs={{0,1},{1,0},{2,3},{3,2},{4,5},{5,4},{6,7},{7,6},{8,9},{9,8},{10,11... | collective-permute-start | bytes 592904 | tf_op jit(solution)/shard_map/ppermute | solution.py:570
  24.8 7.0 %copy-start = (bf16[1024,256]{1,0:T(8,128)(2,1)S(1)}, bf16[1024,256]{1,0:T(8,128)(2,1)}, u32[]{:S(2)}) copy-start(bf16[1024,256]{1,0:T(8,128)(2,1)} %cot.1) | copy-start | bytes 1572868
  40.0 7.6 %collective-permute-start.11 = (bf16[12,193,128]{2,1,0:T(8,128)(2,1)S(1)}, bf16[12,193,128]{2,1,0:T(8,128)(2,1)S(1)}, u32[]{:S(2)}, u32[]{:S(2)}) collective-permute-start(bf16[12,193,128]{2,1,0:T(8,128)(2,1)S(1)} %get-tuple-element.48), channel_id=1, source_target_pairs={{0,1},{1,0},{2,3},{3,2},{4,5},{5,4},{6,7},{7,6},{8,9},{9,8},{10,11... | collective-permute-start | bytes 1778696 | tf_op jit(solution)/shard_map/ppermute | solution.py:570
  46.0 1.6 %collective-permute-start.10 = (bf16[4,224,128]{2,1,0:T(8,128)(2,1)S(1)}, bf16[4,224,128]{2,1,0:T(8,128)(2,1)S(1)}, u32[]{:S(2)}, u32[]{:S(2)}) collective-permute-start(bf16[4,224,128]{2,1,0:T(8,128)(2,1)S(1)} %get-tuple-element.46), channel_id=1, source_target_pairs={{0,1},{1,0},{2,3},{3,2},{4,5},{5,4},{6,7},{7,6},{8,9},{9,8},{10,11... | collective-permute-start | bytes 688136 | tf_op jit(solution)/shard_map/ppermute | solution.py:570
  47.8 8.0 %collective-permute-start.12 = (bf16[4,193,128]{2,1,0:T(8,128)(2,1)S(1)}, bf16[4,193,128]{2,1,0:T(8,128)(2,1)S(1)}, u32[]{:S(2)}, u32[]{:S(2)}) collective-permute-start(bf16[4,193,128]{2,1,0:T(8,128)(2,1)S(1)} %get-tuple-element.50), channel_id=1, source_target_pairs={{0,2},{1,3},{2,0},{3,1},{4,6},{5,7},{6,4},{7,5},{8,10},{9,11},{10,... | collective-permute-start | bytes 592904 | tf_op jit(solution)/shard_map/ppermute | solution.py:570
  48.5 7.4 %collective-permute-start.13 = (bf16[4,193,128]{2,1,0:T(8,128)(2,1)S(1)}, bf16[4,193,128]{2,1,0:T(8,128)(2,1)S(1)}, u32[]{:S(2)}, u32[]{:S(2)}) collective-permute-start(bf16[4,193,128]{2,1,0:T(8,128)(2,1)S(1)} %get-tuple-element.51), channel_id=1, source_target_pairs={{0,4},{1,5},{2,6},{3,7},{4,0},{5,1},{6,2},{7,3},{8,12},{9,13},{10,... | collective-permute-start | bytes 592904 | tf_op jit(solution)/shard_map/ppermute | solution.py:570
  49.7 10.6 %collective-permute-start.14 = (bf16[4,193,128]{2,1,0:T(8,128)(2,1)S(1)}, bf16[4,193,128]{2,1,0:T(8,128)(2,1)S(1)}, u32[]{:S(2)}, u32[]{:S(2)}) collective-permute-start(bf16[4,193,128]{2,1,0:T(8,128)(2,1)S(1)} %get-tuple-element.52), channel_id=1, source_target_pairs={{0,6},{1,7},{2,4},{3,5},{4,2},{5,3},{6,0},{7,1},{8,14},{9,15},{10,... | collective-permute-start | bytes 592904 | tf_op jit(solution)/shard_map/ppermute | solution.py:570
  60.4 6.5 %collective-permute-start.15 = (bf16[193,128]{1,0:T(8,128)(2,1)S(1)}, bf16[193,128]{1,0:T(8,128)(2,1)S(1)}, u32[]{:S(2)}, u32[]{:S(2)}) collective-permute-start(bf16[193,128]{1,0:T(8,128)(2,1)S(1)} %get-tuple-element.54), channel_id=1, source_target_pairs={{0,8},{1,9},{2,10},{3,11},{4,12},{5,13},{6,14},{7,15},{8,16},{9,17... | collective-permute-start | bytes 148232 | tf_op jit(solution)/shard_map/ppermute | solution.py:570
  62.0 6.3 %collective-permute-start.16 = (bf16[193,128]{1,0:T(8,128)(2,1)S(1)}, bf16[193,128]{1,0:T(8,128)(2,1)S(1)}, u32[]{:S(2)}, u32[]{:S(2)}) collective-permute-start(bf16[193,128]{1,0:T(8,128)(2,1)S(1)} %get-tuple-element.55), channel_id=1, source_target_pairs={{0,16},{1,17},{2,18},{3,19},{4,20},{5,21},{6,22},{7,23},{8,24},{9,... | collective-permute-start | bytes 148232 | tf_op jit(solution)/shard_map/ppermute | solution.py:570
  63.9 4.6 %collective-permute-start.17 = (bf16[193,128]{1,0:T(8,128)(2,1)S(1)}, bf16[193,128]{1,0:T(8,128)(2,1)S(1)}, u32[]{:S(2)}, u32[]{:S(2)}) collective-permute-start(bf16[193,128]{1,0:T(8,128)(2,1)S(1)} %get-tuple-element.56), channel_id=1, source_target_pairs={{0,24},{1,25},{2,26},{3,27},{4,28},{5,29},{6,30},{7,31},{8,0},{9,1... | collective-permute-start | bytes 148232 | tf_op jit(solution)/shard_map/ppermute | solution.py:570

commit v6 on v5

v6 whole, which is shorter than its diff:
```python
import functools

import jax
import jax.numpy as jnp
from jax import lax
from jax.experimental import pallas as pl
from jax.experimental.pallas import tpu as pltpu
from jax.sharding import PartitionSpec as P

D = 256
HEADS = 4
HEAD_DIM = 64
FF = 1024
SEQ = 128
LANES = 128
GROUP = 4
WIDE = GROUP * SEQ
CHUNK = 256
STRIP = 64
EPSILON = 1e-05
SCALE = HEAD_DIM ** (-0.5)
VMEM_BYTES = 24 * 1024 * 1024

ROW_QKV = 0
ROW_OUT = 1536
ROW_UP = 2048
ROW_DOWN = 4096
ROW_SMALL = 6144
ROW_END = 6168
ROW_TOTAL = 6176
GAIN_ONE, SHIFT_ONE, BIAS_QUERY, BIAS_VALUE, BIAS_OUT = 0, 2, 4, 6, 8
GAIN_TWO, SHIFT_TWO, BIAS_UP, BIAS_DOWN = 10, 12, 14, 22
SMALL_ROWS = 24
LATE_SMALL = 8

SHARE = 193
Z, PLANE = 4, 4
FIRST_ROWS = 2 * PLANE * SHARE
HEAD_ROWS = FIRST_ROWS - ROW_OUT
SIDE, SIDE_ROWS = 208, 16
SMALL_IN_SHARE = ROW_SMALL - (2 * PLANE * Z - 1) * SHARE

F32 = jnp.float32
BF16 = jnp.bfloat16


def dot(left, right):
    return jnp.dot(left, right, preferred_element_type=F32)


def dot_nt(left, right):
    return lax.dot_general(left, right, (((1,), (1,)), ((), ())), preferred_element_type=F32)


def dot_tn(left, right):
    return lax.dot_general(left, right, (((0,), (0,)), ((), ())), preferred_element_type=F32)


def small_vector(small, row, count):
    return jnp.concatenate([small[row + i : row + i + 1, :] for i in range(count)], axis=1)


def fold_rows(values):
    rows, columns = values.shape
    return jnp.sum(values.reshape(rows // 8, 8, columns), axis=0)


def normalize(values):
    center = values - jnp.mean(values, axis=-1, keepdims=True)
    rate = lax.rsqrt(jnp.mean(center * center, axis=-1, keepdims=True) + EPSILON)
    return center * rate, rate


def normalize_back(grad, gain, normed, rate):
    scaled = grad * gain
    return rate * (
        scaled
        - jnp.mean(scaled, axis=-1, keepdims=True)
        - normed * jnp.mean(scaled * normed, axis=-1, keepdims=True)
    )


def head_masks():
    lane = lax.broadcasted_iota(jnp.int32, (1, D), 1)
    return [(lane // HEAD_DIM == h).astype(F32).astype(BF16) for h in range(HEADS)]


def spread_heads(rows):
    return jnp.concatenate([rows * mask for mask in head_masks()], axis=0)


def matrix_from_flat(flat, start, rows, columns, out):
    per_row = columns // LANES
    for j in range(per_row):
        out[:, j * LANES : (j + 1) * LANES] = flat[
            pl.ds(start + j, rows, stride=per_row), :
        ].astype(BF16)


def turned_to_flat(turned, rows, columns, flat, start):
    per_row = columns // LANES
    for j in range(per_row):
        flat[pl.ds(start + j, rows, stride=per_row), :] = turned[j * LANES : (j + 1) * LANES, :].T


def matrix_to_flat(matrix, rows, columns, flat, start):
    per_row = columns // LANES
    for j in range(per_row):
        flat[pl.ds(start + j, rows, stride=per_row), :] = matrix[:, j * LANES : (j + 1) * LANES]


def prepare_kernel(tok, cot, params, normed_out, normed_turned, cot_turned, own):
    normed, _ = normalize(tok[...].astype(F32))
    normed_out[...] = normed
    normed_turned[...] = normed.astype(BF16).T
    cot_turned[...] = cot[...].T
    own[...] = params[...]


def unpack(ids, bufs, flat):
    slot = 0
    for buf in bufs:
        count, rows, _ = buf.shape

        def place(i, carry, buf=buf, slot=slot, rows=rows):
            flat[pl.ds(ids[slot + i] * rows, rows), :] = buf[i].astype(F32)
            return carry

        lax.fori_loop(0, count, place, 0)
        slot += count


def attend_kernel(n_bufs, ids, seg, normed, *refs):
    bufs = refs[:n_bufs]
    (
        project_out, weights_out, attended_out, w_qkv, w_out, w_up, w_down, small, flat,
    ) = refs[n_bufs:]
    unpack(ids, bufs, flat)
    matrix_from_flat(flat, ROW_QKV, D, 3 * D, w_qkv)
    matrix_from_flat(flat, ROW_OUT, D, D, w_out)
    matrix_from_flat(flat, ROW_UP, D, FF, w_up)
    matrix_from_flat(flat, ROW_DOWN, FF, D, w_down)
    small[...] = flat[ROW_SMALL:ROW_END, :]

    gain = small_vector(small, GAIN_ONE, 2)
    shift = small_vector(small, SHIFT_ONE, 2)
    bias = jnp.concatenate(
        [
            small_vector(small, BIAS_QUERY, 2),
            jnp.zeros((1, D), F32),
            small_vector(small, BIAS_VALUE, 2),
        ],
        axis=1,
    )
    causal = lax.broadcasted_iota(jnp.int32, (SEQ, SEQ), 1) <= lax.broadcasted_iota(
        jnp.int32, (SEQ, SEQ), 0
    )

    def some(g, carry):
        span = pl.ds(pl.multiple_of(g * WIDE, WIDE), WIDE)
        normed_low = (normed[span, :] * gain + shift).astype(BF16)
        project = (dot(normed_low, w_qkv[...]) + bias).astype(BF16)
        project_out[span, :] = project
        scores, values, allowed = [], [], []
        for s in range(GROUP):
            rows = slice(s * SEQ, (s + 1) * SEQ)
            across = jnp.broadcast_to(seg[pl.ds(g * GROUP + s, 1), :].astype(F32), (SEQ, SEQ))
            allowed.append(causal & (across == across.T))
            scores.append(
                dot_nt(project[rows, :D] * SCALE, spread_heads(project[rows, D : 2 * D]))
            )
            values.append(spread_heads(project[rows, 2 * D :]))
        weights = []
        for s in range(GROUP):
            low = []
            for h in range(HEADS):
                mine = jnp.where(allowed[s], scores[s][:, h * SEQ : (h + 1) * SEQ], -1e30)
                grown = jnp.exp(mine - jnp.max(mine, axis=-1, keepdims=True))
                low.append(
                    (grown * (1.0 / jnp.sum(grown, axis=-1, keepdims=True))).astype(BF16)
                )
            weights.append(jnp.concatenate(low, axis=1))
        weights_out[span, :] = jnp.concatenate(weights, axis=0)
        attended_out[span, :] = jnp.concatenate(
            [dot(weights[s], values[s]).astype(BF16) for s in range(GROUP)], axis=0
        )
        return carry

    lax.fori_loop(0, normed.shape[0] // WIDE, some, 0)


def feed_kernel(
    ids, tok, attended, cot, cot_turned, w_out, w_up, w_down, small,
    middle_out, activated_out, grad_middle_out, grad_attended_out, keep_out, send_out, first_out,
    normed_low_all, grad_hidden, grad_middle_low_all, acc_small, flat,
):
    acc_small[...] = jnp.zeros_like(acc_small)
    gain = small_vector(small, GAIN_TWO, 2)
    shift = small_vector(small, SHIFT_TWO, 2)
    bias_out = small_vector(small, BIAS_OUT, 2)
    slope = 0.7978845608028654
    cubic = slope * 0.044715

    def some(g, carry):
        base = pl.multiple_of(g * WIDE, WIDE)
        span = pl.ds(base, WIDE)
        middle = tok[span, :].astype(F32) + dot(attended[span, :], w_out[...]) + bias_out
        middle_out[span, :] = middle
        normed, rate = normalize(middle)
        normed_low = (normed * gain + shift).astype(BF16)
        normed_low_all[span, :] = normed_low
        cotangent = cot[span, :]
        for c in range(0, FF, CHUNK):
            columns = slice(c, c + CHUNK)
            bias = small_vector(small, BIAS_UP + c // LANES, CHUNK // LANES)
            hidden_all = dot(normed_low, w_up[:, columns])
            grad_all = dot_nt(cotangent, w_down[columns, :])
            total = jnp.zeros((8, CHUNK), F32)
            for r in range(0, WIDE, STRIP):
                rows = slice(r, r + STRIP)
                strip = pl.ds(pl.multiple_of(base + r, STRIP), STRIP)
                hidden = hidden_all[rows] + bias
                square = hidden * hidden
                half = 0.5 + 0.5 * jnp.tanh(hidden * (slope + cubic * square))
                activated = hidden * half
                derivative = half + activated * (1.0 - half) * (2 * slope + (6 * cubic) * square)
                low = (grad_all[rows] * derivative).astype(BF16)
                activated_out[strip, columns] = activated.astype(BF16)
                grad_hidden[strip, columns] = low
                total += fold_rows(low.astype(F32))
            acc_small[:, 3 * D + c : 3 * D + c + CHUNK] += total
        grad_result = cotangent.astype(F32)
        grad_normed = dot_nt(grad_hidden[span, :], w_up[...])
        grad_middle = grad_result + normalize_back(grad_normed, gain, normed, rate)
        grad_middle_out[span, :] = grad_middle
        grad_middle_low = grad_middle.astype(BF16)
        grad_middle_low_all[span, :] = grad_middle_low
        grad_attended_out[span, :] = dot_nt(grad_middle_low, w_out[...]).astype(BF16)
        acc_small[:, 0:D] += fold_rows(grad_middle_low.astype(F32))
        acc_small[:, D : 2 * D] += fold_rows(grad_normed * normed)
        acc_small[:, 2 * D : 3 * D] += fold_rows(grad_normed)
        acc_small[:, 3 * D + FF :] += fold_rows(grad_result)
        return carry

    lax.fori_loop(0, tok.shape[0] // WIDE, some, 0)
    turned_to_flat(dot(cot_turned[...], activated_out[...]), FF, D, flat, ROW_DOWN - ROW_OUT)
    matrix_to_flat(dot_tn(normed_low_all[...], grad_hidden[...]), D, FF, flat, ROW_UP - ROW_OUT)
    matrix_to_flat(dot_tn(attended[...], grad_middle_low_all[...]), D, D, flat, 0)
    sums = jnp.sum(acc_small[...], axis=0, keepdims=True)
    base = ROW_SMALL - ROW_OUT
    flat[base : base + LATE_SMALL, :] = jnp.zeros((LATE_SMALL, LANES), F32)
    for i in range(sums.shape[1] // LANES):
        row = base + LATE_SMALL + i
        flat[row : row + 1, :] = sums[:, i * LANES : (i + 1) * LANES]
    flat[ROW_END - ROW_OUT :, :] = jnp.zeros((ROW_TOTAL - ROW_END, LANES), F32)
    first_out[...] = flat[:HEAD_ROWS, :]
    for target, out in enumerate((keep_out, send_out)):
        for p in range(PLANE):
            for z in range(1, Z):
                share = ids[target * PLANE + p] + z * 2 * PLANE
                rows = flat[pl.ds(share * SHARE - ROW_OUT, SHARE), :]
                out[p * (Z - 1) + z - 1] = rows.astype(out.dtype)


def result_kernel(middle, activated, w_down, small, result_out):
    result = middle[...] + dot(activated[...], w_down[...]) + small_vector(small, BIAS_DOWN, 2)
    result_out[...] = result.astype(BF16)


def attend_back_kernel(
    ids, project, weights, grad_attended, normed_turned, w_qkv, small, first_in,
    grad_project, keep_out, send_out, flat, wide,
):
    def some(g, carry):
        base = g * WIDE
        spans = [pl.ds(pl.multiple_of(base + s * SEQ, SEQ), SEQ) for s in range(GROUP)]
        grad_weights = [
            dot_nt(grad_attended[span, :], spread_heads(project[span, 2 * D :])) for span in spans
        ]
        scores_low, scores_turned, weights_turned = [], [], []
        for s, span in enumerate(spans):
            low, turned, mine_turned = [], [], []
            for h in range(HEADS):
                columns = slice(h * SEQ, (h + 1) * SEQ)
                mine_low = weights[span, columns]
                mine = mine_low.astype(F32)
                product = mine * grad_weights[s][:, columns]
                grad_scores = (product - mine * jnp.sum(product, axis=-1, keepdims=True)) * SCALE
                low.append(grad_scores.astype(BF16))
                turned.append(low[-1].T)
                mine_turned.append(mine_low.T)
            scores_low.append(jnp.concatenate(low, axis=1))
            scores_turned.append(jnp.concatenate(turned, axis=1))
            weights_turned.append(jnp.concatenate(mine_turned, axis=1))
        for s, span in enumerate(spans):
            key = spread_heads(project[span, D : 2 * D])
            grad_project[span, :D] = dot(scores_low[s], key).astype(BF16)
            query = spread_heads(project[span, :D])
            grad_project[span, D : 2 * D] = dot(scores_turned[s], query).astype(BF16)
            grad_value = dot(weights_turned[s], spread_heads(grad_attended[span, :]))
            grad_project[span, 2 * D :] = grad_value.astype(BF16)
        return carry

    lax.fori_loop(0, project.shape[0] // WIDE, some, 0)
    products = dot(normed_turned[...], grad_project[...])
    sums = jnp.sum(fold_rows(grad_project[...].astype(F32)), axis=0, keepdims=True)
    gain = jnp.broadcast_to(small_vector(small, GAIN_ONE, 2), (LANES, D)).T
    shift = jnp.broadcast_to(small_vector(small, SHIFT_ONE, 2), (LANES, D)).T
    grad_gain = jnp.zeros((D, LANES), F32)
    grad_shift = jnp.zeros((D, LANES), F32)
    per_row = 3 * D // LANES
    for j in range(per_row):
        columns = slice(j * LANES, (j + 1) * LANES)
        weight = w_qkv[:, columns].astype(F32)
        grad_gain += products[:, columns] * weight
        grad_shift += sums[:, columns] * weight
        flat[pl.ds(j, D, stride=per_row), :] = products[:, columns] * gain + sums[:, columns] * shift
    flat[ROW_OUT:, :] = first_in[...]
    grad_gain = jnp.sum(grad_gain.T, axis=0, keepdims=True)
    grad_shift = jnp.sum(grad_shift.T, axis=0, keepdims=True)
    late = jnp.concatenate([grad_gain, grad_shift, sums[:, :D], sums[:, 2 * D :]], axis=1)
    side = jnp.concatenate(
        [late[:, i * LANES : (i + 1) * LANES] for i in range(LATE_SMALL)]
        + [jnp.zeros((SIDE_ROWS - LATE_SMALL, LANES), F32)],
        axis=0,
    )
    wide[SHARE:SIDE, :] = jnp.zeros((SIDE - SHARE, LANES), F32)
    for target, out in enumerate((keep_out, send_out)):
        for p in range(PLANE):
            share = ids[target * PLANE + p]
            wide[:SHARE, :] = flat[pl.ds(share * SHARE, SHARE), :]
            wide[SIDE:, :] = jnp.where(share == 2 * PLANE - 1, side, 0.0)
            out[p] = wide[...].astype(out.dtype)


def input_grad_kernel(tok, grad_project, grad_middle, w_qkv, small, input_grad_out):
    gain = small_vector(small, GAIN_ONE, 2)

    def some(g, carry):
        span = pl.ds(pl.multiple_of(g * WIDE, WIDE), WIDE)
        normed, rate = normalize(tok[span, :].astype(F32))
        grad_normed = dot_nt(grad_project[span, :], w_qkv[...])
        input_grad_out[span, :] = grad_middle[span, :] + normalize_back(
            grad_normed, gain, normed, rate
        )
        return carry

    lax.fori_loop(0, tok.shape[0] // WIDE, some, 0)


def stack_kernel(*refs):
    for d, ref in enumerate(refs[:-1]):
        refs[-1][d] = ref[...]


def add_core_kernel(first, first_in, rest, rest_in, keep_out, *refs):
    sends, column = refs[:-1], refs[-1]
    end = SMALL_IN_SHARE + LATE_SMALL
    for p, out in enumerate((keep_out, *sends)):
        item = first[p] + first_in[p].astype(F32)
        span = slice(p * (Z - 1), (p + 1) * (Z - 1))
        column[0] = item[:SHARE, :]
        column[1:] = rest[span] + rest_in[span].astype(F32)
        column[Z - 1, SMALL_IN_SHARE:end, :] += item[SIDE : SIDE + LATE_SMALL, :]
        out[...] = column[...].astype(out.dtype)


def add_plane_kernel(ids, kept, *refs):
    arrived = refs[: PLANE - 1]
    keep_out, *sends, column = refs[PLANE - 1 :]
    column[...] = kept[...] + sum(item[...].astype(F32) for item in arrived)
    keep_out[...] = column[ids[0]]
    for d, out in enumerate(sends):
        out[...] = column[lax.rem(ids[0] + d + 1, Z)].astype(BF16)


def add_column_kernel(kept, *refs):
    refs[-1][...] = kept[...] + sum(item[...].astype(F32) for item in refs[:-1])


def like(*shape, kind=F32):
    return jax.ShapeDtypeStruct(shape, kind)


SMEM_SPEC = pl.BlockSpec(memory_space=pltpu.SMEM)
VMEM_SPEC = pl.BlockSpec(memory_space=pltpu.VMEM)

def cost(us):
    return pl.CostEstimate(flops=int(us * 1e9), bytes_accessed=1 << 20, transcendentals=0)


def call(kernel, name, ids, inputs, outs, scratch=(), us=1):
    with_ids = ids is not None
    results = pl.pallas_call(
        kernel,
        in_specs=[SMEM_SPEC] * with_ids + [VMEM_SPEC] * len(inputs),
        out_specs=[VMEM_SPEC] * len(outs),
        out_shape=list(outs),
        scratch_shapes=list(scratch),
        compiler_params=pltpu.CompilerParams(vmem_limit_bytes=VMEM_BYTES),
        cost_estimate=cost(us),
        name=name,
    )(*([ids] if with_ids else []), *inputs)
    return results if len(outs) > 1 else results[0]


def prepare(tokens, cotangent, params):
    rows = tokens.shape[0]
    turned = like(D, rows, kind=BF16)
    return call(
        prepare_kernel, "prepare", None, [tokens, cotangent, params],
        [like(rows, D), turned, turned, like(*params.shape, kind=BF16)], us=2,
    )


def attend(ids, segments, normed, bufs):
    rows = normed.shape[0]
    total = sum(buf.shape[0] * buf.shape[1] for buf in bufs)
    shapes = [
        (rows, 3 * D), (rows, HEADS * SEQ), (rows, D), (D, 3 * D), (D, D), (D, FF), (FF, D),
    ]
    return call(
        functools.partial(attend_kernel, len(bufs)), "attend", ids, [segments, normed, *bufs],
        [like(*shape, kind=BF16) for shape in shapes] + [like(SMALL_ROWS, LANES)],
        [pltpu.VMEM((total, LANES), F32)], us=6,
    )


def feed(ids, tokens, attended, cotangent, cot_turned, w_out, w_up, w_down, small, send_kind):
    rows = tokens.shape[0]
    return call(
        feed_kernel, "feed", ids,
        [tokens, attended, cotangent, cot_turned, w_out, w_up, w_down, small],
        [
            like(rows, D),
            like(rows, FF, kind=BF16),
            like(rows, D),
            like(rows, D, kind=BF16),
            like(PLANE * (Z - 1), SHARE, LANES),
            like(PLANE * (Z - 1), SHARE, LANES, kind=send_kind),
            like(HEAD_ROWS, LANES),
        ],
        [
            pltpu.VMEM((rows, D), BF16),
            pltpu.VMEM((rows, FF), BF16),
            pltpu.VMEM((rows, D), BF16),
            pltpu.VMEM((8, (SMALL_ROWS - LATE_SMALL) * LANES), F32),
            pltpu.VMEM((ROW_TOTAL - ROW_OUT, LANES), F32),
        ],
        us=8,
    )


def result(middle, activated, w_down, small):
    return call(
        result_kernel, "result", None, [middle, activated, w_down, small],
        [like(*middle.shape, kind=BF16)], us=2,
    )


def attend_back(ids, project, weights, grad_attended, normed_turned, w_qkv, small, first, send_kind):
    shape = (PLANE, SIDE + SIDE_ROWS, LANES)
    return call(
        attend_back_kernel, "attend_back", ids,
        [project, weights, grad_attended, normed_turned, w_qkv, small, first],
        [like(*project.shape, kind=BF16), like(*shape), like(*shape, kind=send_kind)],
        [pltpu.VMEM((FIRST_ROWS, LANES), F32), pltpu.VMEM(shape[1:], F32)], us=5,
    )


def input_gradient(tokens, grad_project, grad_middle, w_qkv, small):
    return call(
        input_grad_kernel, "input_grad", None, [tokens, grad_project, grad_middle, w_qkv, small],
        [like(*tokens.shape)], us=2,
    )


def block(prepared, tokens, segment_ids, cotangent, share_ids, shares, grad_ids, send_kind, core_exchange):
    normed, normed_turned, cot_turned = prepared
    segments = segment_ids.reshape(-1, SEQ)
    project, weights, attended, w_qkv, w_out, w_up, w_down, small = attend(
        share_ids, segments, normed, shares
    )
    middle, activated, grad_middle, grad_attended, rest, rest_send, first_grad = feed(
        grad_ids, tokens, attended, cotangent, cot_turned, w_out, w_up, w_down, small, send_kind
    )
    rest_in = core_exchange(rest_send)
    grad_project, first, first_send = attend_back(
        grad_ids, project, weights, grad_attended, normed_turned, w_qkv, small, first_grad, send_kind
    )
    first_in = core_exchange(first_send)
    outputs = result(middle, activated, w_down, small)
    input_grad = input_gradient(tokens, grad_project, grad_middle, w_qkv, small)
    return outputs, input_grad, first, first_in, rest, rest_in


def local_any(n, tokens, params, segment_ids, cotangent):
    *prepared, _ = prepare(tokens, cotangent, params)
    gathered = lax.all_gather(params, "fsdp", axis=0)
    ids = jnp.arange(n, dtype=jnp.int32)
    order = jnp.array([p * 2 + c for c in range(2) for p in range(PLANE)], jnp.int32)
    outputs, input_grad, first, first_send, rest, rest_send = block(
        prepared, tokens, segment_ids, cotangent, ids, [gathered], order, F32, lambda values: values
    )
    first = jnp.stack([first, first_send], axis=1)
    rest = jnp.stack([rest, rest_send]).reshape(2, PLANE, Z - 1, SHARE, LANES).transpose(2, 1, 0, 3, 4)
    flat = jnp.concatenate(
        [
            first[:, :, :SHARE].reshape(-1, LANES),
            rest.reshape(-1, LANES),
            jnp.zeros((n * params.shape[0] - ROW_TOTAL, LANES), F32),
        ],
        axis=0,
    )
    flat = flat.at[ROW_SMALL : ROW_SMALL + LATE_SMALL].add(
        first[PLANE - 1, 1, SIDE : SIDE + LATE_SMALL]
    )
    param_grad = lax.psum_scatter(flat, "fsdp", scatter_dimension=0, tiled=True)
    return outputs, input_grad, param_grad


def index_of(z, plane, core):
    return (z * PLANE + plane) * 2 + core


def move(values, step_z, step_plane, step_core):
    pairs = [
        (index_of(z, p, c), index_of((z + step_z) % Z, p ^ step_plane, c ^ step_core))
        for z in range(Z)
        for p in range(PLANE)
        for c in range(2)
    ]
    return lax.ppermute(values, "fsdp", pairs)


def local_slice(tokens, params, segment_ids, cotangent):
    me = lax.axis_index("fsdp").astype(jnp.int32)
    z, plane, core = me // (2 * PLANE), (me // 2) % PLANE, me % 2
    planes = [(dc, dp) for dc in range(2) for dp in range(PLANE)]
    share_ids = jnp.stack(
        [index_of((z - dz) % Z, plane ^ dp, core ^ dc) for dc, dp in planes for dz in range(Z)]
    )
    grad_ids = jnp.stack([(plane ^ dp) * 2 + (core ^ dc) for dc, dp in planes])

    *prepared, own = prepare(tokens, cotangent, params)
    column = call(
        stack_kernel, "stack", None, [own] + [move(params, d, 0, 0) for d in range(1, Z)],
        [like(Z, SHARE, LANES, kind=BF16)],
    )
    same = [column] + [move(column, 0, d, 0) for d in range(1, PLANE)]
    shares = same + [move(item, 0, 0, 1) for item in same]
    outputs, input_grad, first, first_in, rest, rest_in = block(
        prepared, tokens, segment_ids, cotangent, share_ids, shares, grad_ids, BF16,
        lambda values: move(values, 0, 0, 1),
    )

    part = (Z, SHARE, LANES)
    kept, *sends = call(
        add_core_kernel, "add_core", None, [first, first_in, rest, rest_in],
        [like(*part)] + [like(*part, kind=BF16)] * (PLANE - 1), [pltpu.VMEM(part, F32)],
    )
    arrived = [move(item, 0, d + 1, 0) for d, item in enumerate(sends)]
    kept, *sends = call(
        add_plane_kernel, "add_plane", z.reshape(1), [kept] + arrived,
        [like(SHARE, LANES)] + [like(SHARE, LANES, kind=BF16)] * (Z - 1), [pltpu.VMEM(part, F32)],
    )
    arrived = [move(item, d + 1, 0, 0) for d, item in enumerate(sends)]
    param_grad = call(
        add_column_kernel, "add_column", None, [kept] + arrived, [like(SHARE, LANES)]
    )
    return outputs, input_grad, param_grad


def solution(mesh):
    n = mesh.shape["fsdp"]
    local = local_slice if n == 2 * PLANE * Z else functools.partial(local_any, n)
    in_specs = (P("fsdp", None), P("fsdp", None), P("fsdp"), P("fsdp", None))
    out_specs = (P("fsdp", None), P("fsdp", None), P("fsdp", None))
    return jax.shard_map(local, mesh=mesh, in_specs=in_specs, out_specs=out_specs, check_vma=False)
```

time: 69.3 us -> 63.9 us (0.922)
  Pallas kernels: 26.9 us -> 20.8 us
  local copies, waits for them, and re-layouts: 1.02 us -> 3.82 us
  waiting for transfers between devices: 21.2 us -> 19.2 us
    pallas_call x9 -> x10, Pallas kernels: 26.9 us -> 20.8 us  [call(): pl.pallas_call(kernel, in_specs=[SMEM_SPEC] * with_ids + [VMEM_SPEC] * le...]
    unnamed x8 -> x16, local copies, waits for them, and re-layouts: 0.82 us -> 3.62 us
    ppermute x18, waiting for transfers between devices: 21.2 us -> 19.2 us  [move(): return lax.ppermute(values, 'fsdp', pairs)]
  transfers between devices with their start and end apart: 18 -> 18, of which waited for: 14 -> 10; matrix products, arithmetic and copies ran while one was open for 0% -> 0% of each run, Pallas kernels for 15% -> 12%
where the time goes in v6:
time: 63.9 us; the launch traced here: 63.6 us
  Pallas kernels  20.8 us (33%)
  waiting for transfers between devices  19.2 us (30%)
  starting transfers between devices  19.1 us (30%)
  local copies, waits for them, and re-layouts  3.82 us (6%)
  between operations  0.79 us (1%)
    pallas_call x10, Pallas kernels, call(): pl.pallas_call(kernel, in_specs=[SMEM_SPEC] * with_ids + [VMEM_SPEC] * le...  20.8 us
    ppermute x18, waiting for transfers between devices, move(): return lax.ppermute(values, 'fsdp', pairs)  19.2 us
    ppermute x18, starting transfers between devices, move(): return lax.ppermute(values, 'fsdp', pairs)  19.1 us
    unnamed x16, local copies, waits for them, and re-layouts  3.62 us
  transfers between devices with their start and end apart: 18, of which 10 were waited for; matrix products, arithmetic and copies ran while one was open for 0% of the time, Pallas kernels for 12%

profile of v6, /device:TPU:0, one launch (start us, length us, event | category | flops | bytes accessed | tf_op | source)
XLA Modules:
  0.0 63.6 jit_solution(8853605343360379119)
XLA Ops:
  0.6 3.1 %collective-permute-start = (bf16[193,128]{1,0:T(8,128)(2,1)}, bf16[193,128]{1,0:T(8,128)(2,1)S(1)}, u32[]{:S(2)}, u32[]{:S(2)}) collective-permute-start(bf16[193,128]{1,0:T(8,128)(2,1)} %params.1), channel_id=1, source_target_pairs={{0,8},{1,9},{2,10},{3,11},{4,12},{5,13},{6,14},{7,15},{8,16},{9,17... | collective-permute-start | bytes 148232 | tf_op jit(solution)/shard_map/ppermute | solution.py:533
  3.7 2.6 %collective-permute-start.1 = (bf16[193,128]{1,0:T(8,128)(2,1)}, bf16[193,128]{1,0:T(8,128)(2,1)S(1)}, u32[]{:S(2)}, u32[]{:S(2)}) collective-permute-start(bf16[193,128]{1,0:T(8,128)(2,1)} %params.1), channel_id=1, source_target_pairs={{0,16},{1,17},{2,18},{3,19},{4,20},{5,21},{6,22},{7,23},{8,24},{9,... | collective-permute-start | bytes 148232 | tf_op jit(solution)/shard_map/ppermute | solution.py:533
  6.3 1.3 %collective-permute-start.2 = (bf16[193,128]{1,0:T(8,128)(2,1)}, bf16[193,128]{1,0:T(8,128)(2,1)S(1)}, u32[]{:S(2)}, u32[]{:S(2)}) collective-permute-start(bf16[193,128]{1,0:T(8,128)(2,1)} %params.1), channel_id=1, source_target_pairs={{0,24},{1,25},{2,26},{3,27},{4,28},{5,29},{6,30},{7,31},{8,0},{9,1... | collective-permute-start | bytes 148232 | tf_op jit(solution)/shard_map/ppermute | solution.py:533
  7.6 1.0 %copy-done = bf16[1024,256]{1,0:T(8,128)(2,1)S(1)} copy-done((bf16[1024,256]{1,0:T(8,128)(2,1)S(1)}, bf16[1024,256]{1,0:T(8,128)(2,1)}, u32[]{:S(2)}) %copy-start) | copy-done | bytes 524312
  8.7 1.0 %copy-done.2 = bf16[1024,256]{1,0:T(8,128)(2,1)S(1)} copy-done((bf16[1024,256]{1,0:T(8,128)(2,1)S(1)}, bf16[1024,256]{1,0:T(8,128)(2,1)}, u32[]{:S(2)}) %copy-start.2) | copy-done | bytes 524312
  9.7 0.8 %copy-done.4 = bf16[193,128]{1,0:T(8,128)(2,1)S(1)} copy-done((bf16[193,128]{1,0:T(8,128)(2,1)S(1)}, bf16[193,128]{1,0:T(8,128)(2,1)}, u32[]{:S(2)}) %copy-start.4) | copy-done | bytes 49432
  10.5 0.7 %prepare.1 = (f32[1024,256]{1,0:T(8,128)S(1)}, bf16[256,1024]{1,0:T(8,128)(2,1)S(1)}, bf16[256,1024]{1,0:T(8,128)(2,1)S(1)}, bf16[193,128]{1,0:T(8,128)(2,1)S(1)}) custom-call(bf16[1024,256]{1,0:T(8,128)(2,1)S(1)} %copy-done.2, bf16[1024,256]{1,0:T(8,128)(2,1)S(1)} %copy-done, bf16[193,128]{1,0:T(8,128)(2,1)S(1)} %copy-done.4), custom_call_target="tpu_custom_call" | custom-call | flops 2000000000 | bytes 1048576 | tf_op jit(solution)/shard_map/prepare/pallas_call | solution.py:394
  11.2 0.0 copy-start.6
  11.2 0.0 collective-permute-done.refs_1_
  11.2 0.0 collective-permute-done.2.refs_3_
  11.2 0.0 copy-start.5
  11.3 0.7 %copy-done.6 = bf16[256,1024]{1,0:T(8,128)(2,1)} copy-done((bf16[256,1024]{1,0:T(8,128)(2,1)}, bf16[256,1024]{1,0:T(8,128)(2,1)S(1)}, u32[]{:S(2)}) %copy-start.6) | copy-done | bytes 524312
  12.0 1.5 %collective-permute-start.3 = (bf16[4,193,128]{2,1,0:T(8,128)(2,1)S(1)}, bf16[4,193,128]{2,1,0:T(8,128)(2,1)S(1)}, u32[]{:S(2)}, u32[]{:S(2)}) collective-permute-start(bf16[4,193,128]{2,1,0:T(8,128)(2,1)S(1)} %stack.169.refs_0_), channel_id=1, source_target_pairs={{0,2},{1,3},{2,0},{3,1},{4,6},{5,7},{6,4},{7,5},{8,10},{9,11},{10,... | collective-permute-start | bytes 592904 | tf_op jit(solution)/shard_map/ppermute | solution.py:533
  13.5 1.5 %collective-permute-start.4 = (bf16[4,193,128]{2,1,0:T(8,128)(2,1)S(1)}, bf16[4,193,128]{2,1,0:T(8,128)(2,1)S(1)}, u32[]{:S(2)}, u32[]{:S(2)}) collective-permute-start(bf16[4,193,128]{2,1,0:T(8,128)(2,1)S(1)} %stack.169.refs_0_), channel_id=1, source_target_pairs={{0,4},{1,5},{2,6},{3,7},{4,0},{5,1},{6,2},{7,3},{8,12},{9,13},{10,... | collective-permute-start | bytes 592904 | tf_op jit(solution)/shard_map/ppermute | solution.py:533
  15.0 0.5 collective-permute-start.5
  15.5 4.5 %collective-permute-done.3.refs_1_ = bf16[4,193,128]{2,1,0:T(8,128)(2,1)S(1)} collective-permute-done((bf16[4,193,128]{2,1,0:T(8,128)(2,1)S(1)}, bf16[4,193,128]{2,1,0:T(8,128)(2,1)S(1)}, u32[]{:S(2)}, u32[]{:S(2)}) %collective-permute-start.3) | collective-permute-done | bytes 197664 | tf_op jit(solution)/shard_map/ppermute | solution.py:533
  20.0 0.0 collective-permute-start.7
  20.0 3.6 %collective-permute-done.4.refs_2_ = bf16[4,193,128]{2,1,0:T(8,128)(2,1)S(1)} collective-permute-done((bf16[4,193,128]{2,1,0:T(8,128)(2,1)S(1)}, bf16[4,193,128]{2,1,0:T(8,128)(2,1)S(1)}, u32[]{:S(2)}, u32[]{:S(2)}) %collective-permute-start.4) | collective-permute-done | bytes 197664 | tf_op jit(solution)/shard_map/ppermute | solution.py:533
  23.6 0.0 collective-permute-start.8
  23.6 0.5 collective-permute-start.9
  24.1 0.1 stack.135.ids
  24.2 0.1 stack.168.ids
  24.3 0.0 collective-permute-done.6.refs_4_
  24.3 0.0 collective-permute-done.7.refs_5_
  24.3 0.7 %collective-permute-done.8.refs_6_ = bf16[4,193,128]{2,1,0:T(8,128)(2,1)S(1)} collective-permute-done((bf16[4,193,128]{2,1,0:T(8,128)(2,1)S(1)}, bf16[4,193,128]{2,1,0:T(8,128)(2,1)S(1)}, u32[]{:S(2)}, u32[]{:S(2)}) %collective-permute-start.8) | collective-permute-done | bytes 197664 | tf_op jit(solution)/shard_map/ppermute | solution.py:533
  25.0 0.3 collective-permute-done.9.refs_7_
  25.3 3.7 %attend.1 = (bf16[1024,768]{1,0:T(8,128)(2,1)S(1)}, bf16[1024,512]{1,0:T(8,128)(2,1)S(1)}, bf16[1024,256]{1,0:T(8,128)(2,1)S(1)}, bf16[256,768]{1,0:T(8,128)(2,1...) custom-call(s32[32]{0:T(128)S(1)} %stack.168.ids, ...), custom_call_target="tpu_custom_call" | custom-call | flops 6000000000 | bytes 1048576 | tf_op jit(solution)/shard_map/attend/pallas_call | solution.py:394
  29.1 8.1 %feed.1 = (f32[1024,256]{1,0:T(8,128)S(1)}, bf16[1024,1024]{1,0:T(8,128)(2,1)S(1)}, f32[1024,256]{1,0:T(8,128)S(1)}, bf16[1024,256]{1,0:T(8,128)(2,1)S(1)}, f32[...) custom-call(s32[8]{0:T(128)S(1)} %stack.135.ids, ...), custom_call_target="tpu_custom_call" | custom-call | flops 8000000000 | bytes 1048576 | tf_op jit(solution)/shard_map/feed/pallas_call | solution.py:394
  37.2 0.3 collective-permute-start.11
  37.5 3.7 %attend_back.1 = (bf16[1024,768]{1,0:T(8,128)(2,1)S(1)}, f32[4,224,128]{2,1,0:T(8,128)S(1)}, bf16[4,224,128]{2,1,0:T(8,128)(2,1)S(1)}) custom-call(s32[8]{0:T(128)S(1)} %stack.135.ids, bf16[1024,768]{1,0:T(8,128)(2,1)S(1)} %get-tuple-element.43.project, bf16[1024,512]{1,0:T(8,128)(2,1)S(1)} %get-tuple-element.44.weights, ...), custom_call_target="tpu_custom_call" | custom-call | flops 5000000000 | bytes 1048576 | tf_op jit(solution)/shard_map/attend_back/pallas_call | solution.py:394
  41.1 0.4 collective-permute-start.10
  41.5 1.2 %collective-permute-done.10.first_in = bf16[4,224,128]{2,1,0:T(8,128)(2,1)S(1)} collective-permute-done((bf16[4,224,128]{2,1,0:T(8,128)(2,1)S(1)}, bf16[4,224,128]{2,1,0:T(8,128)(2,1)S(1)}, u32[]{:S(2)}, u32[]{:S(2)}) %collective-permute-start.10) | collective-permute-done | bytes 229408 | tf_op jit(solution)/shard_map/ppermute | solution.py:533
  42.7 0.2 add_core.1
  42.9 0.9 %collective-permute-start.12 = (bf16[4,193,128]{2,1,0:T(8,128)(2,1)S(1)}, bf16[4,193,128]{2,1,0:T(8,128)(2,1)S(1)}, u32[]{:S(2)}, u32[]{:S(2)}) collective-permute-start(bf16[4,193,128]{2,1,0:T(8,128)(2,1)S(1)} %get-tuple-element.56), channel_id=1, source_target_pairs={{0,2},{1,3},{2,0},{3,1},{4,6},{5,7},{6,4},{7,5},{8,10},{9,11},{10,... | collective-permute-start | bytes 592904 | tf_op jit(solution)/shard_map/ppermute | solution.py:533
  43.9 1.2 %collective-permute-start.13 = (bf16[4,193,128]{2,1,0:T(8,128)(2,1)S(1)}, bf16[4,193,128]{2,1,0:T(8,128)(2,1)S(1)}, u32[]{:S(2)}, u32[]{:S(2)}) collective-permute-start(bf16[4,193,128]{2,1,0:T(8,128)(2,1)S(1)} %get-tuple-element.57), channel_id=1, source_target_pairs={{0,4},{1,5},{2,6},{3,7},{4,0},{5,1},{6,2},{7,3},{8,12},{9,13},{10,... | collective-permute-start | bytes 592904 | tf_op jit(solution)/shard_map/ppermute | solution.py:533
  45.0 1.4 %collective-permute-start.14 = (bf16[4,193,128]{2,1,0:T(8,128)(2,1)S(1)}, bf16[4,193,128]{2,1,0:T(8,128)(2,1)S(1)}, u32[]{:S(2)}, u32[]{:S(2)}) collective-permute-start(bf16[4,193,128]{2,1,0:T(8,128)(2,1)S(1)} %get-tuple-element.58), channel_id=1, source_target_pairs={{0,6},{1,7},{2,4},{3,5},{4,2},{5,3},{6,0},{7,1},{8,14},{9,15},{10,... | collective-permute-start | bytes 592904 | tf_op jit(solution)/shard_map/ppermute | solution.py:533
  46.5 1.5 %result.1 = bf16[1024,256]{1,0:T(8,128)(2,1)} custom-call(f32[1024,256]{1,0:T(8,128)S(1)} %get-tuple-element.41.middle, bf16[1024,1024]{1,0:T(8,128)(2,1)S(1)} %get-tuple-element.42.activated, bf16[1024,256]{1,0:T(8,128)(2,1)S(1)} %get-tuple-element.39.w_down, f32[24,128]{1,0:T(8,128)S(1)} %get-tuple-element.40.small), custom_call_target="tpu_custom_call" | custom-call | flops 2000000000 | bytes 1048576 | tf_op jit(solution)/shard_map/result/pallas_call | solution.py:394
  48.0 2.9 %collective-permute-done.12.refs_0_ = bf16[4,193,128]{2,1,0:T(8,128)(2,1)S(1)} collective-permute-done((bf16[4,193,128]{2,1,0:T(8,128)(2,1)S(1)}, bf16[4,193,128]{2,1,0:T(8,128)(2,1)S(1)}, u32[]{:S(2)}, u32[]{:S(2)}) %collective-permute-start.12) | collective-permute-done | bytes 197664 | tf_op jit(solution)/shard_map/ppermute | solution.py:533
  50.9 3.1 %collective-permute-done.13.refs_1_ = bf16[4,193,128]{2,1,0:T(8,128)(2,1)S(1)} collective-permute-done((bf16[4,193,128]{2,1,0:T(8,128)(2,1)S(1)}, bf16[4,193,128]{2,1,0:T(8,128)(2,1)S(1)}, u32[]{:S(2)}, u32[]{:S(2)}) %collective-permute-start.13) | collective-permute-done | bytes 197664 | tf_op jit(solution)/shard_map/ppermute | solution.py:533
  54.0 1.6 %collective-permute-done.14.refs_2_ = bf16[4,193,128]{2,1,0:T(8,128)(2,1)S(1)} collective-permute-done((bf16[4,193,128]{2,1,0:T(8,128)(2,1)S(1)}, bf16[4,193,128]{2,1,0:T(8,128)(2,1)S(1)}, u32[]{:S(2)}, u32[]{:S(2)}) %collective-permute-start.14) | collective-permute-done | bytes 197664 | tf_op jit(solution)/shard_map/ppermute | solution.py:533
  55.6 0.2 add_plane.1
  55.8 0.7 %collective-permute-start.15 = (bf16[193,128]{1,0:T(8,128)(2,1)S(1)}, bf16[193,128]{1,0:T(8,128)(2,1)S(1)}, u32[]{:S(2)}, u32[]{:S(2)}) collective-permute-start(bf16[193,128]{1,0:T(8,128)(2,1)S(1)} %get-tuple-element.60), channel_id=1, source_target_pairs={{0,8},{1,9},{2,10},{3,11},{4,12},{5,13},{6,14},{7,15},{8,16},{9,17... | collective-permute-start | bytes 148232 | tf_op jit(solution)/shard_map/ppermute | solution.py:533
  56.5 1.2 %collective-permute-start.16 = (bf16[193,128]{1,0:T(8,128)(2,1)S(1)}, bf16[193,128]{1,0:T(8,128)(2,1)S(1)}, u32[]{:S(2)}, u32[]{:S(2)}) collective-permute-start(bf16[193,128]{1,0:T(8,128)(2,1)S(1)} %get-tuple-element.61), channel_id=1, source_target_pairs={{0,16},{1,17},{2,18},{3,19},{4,20},{5,21},{6,22},{7,23},{8,24},{9,... | collective-permute-start | bytes 148232 | tf_op jit(solution)/shard_map/ppermute | solution.py:533
  57.7 2.0 %collective-permute-start.17 = (bf16[193,128]{1,0:T(8,128)(2,1)S(1)}, bf16[193,128]{1,0:T(8,128)(2,1)S(1)}, u32[]{:S(2)}, u32[]{:S(2)}) collective-permute-start(bf16[193,128]{1,0:T(8,128)(2,1)S(1)} %get-tuple-element.62), channel_id=1, source_target_pairs={{0,24},{1,25},{2,26},{3,27},{4,28},{5,29},{6,30},{7,31},{8,0},{9,1... | collective-permute-start | bytes 148232 | tf_op jit(solution)/shard_map/ppermute | solution.py:533
  59.7 2.1 %input_grad.1 = f32[1024,256]{1,0:T(8,128)} custom-call(bf16[1024,256]{1,0:T(8,128)(2,1)S(1)} %copy-done.3, bf16[1024,768]{1,0:T(8,128)(2,1)S(1)} %get-tuple-element.49.grad_project, f32[1024,256]{1,0:T(8,128)S(1)} %get-tuple-element.50.grad_middle, bf16[256,768]{1,0:T(8,128)(2,1)S(1)} %get-tuple-element.47.w_qkv, f32[24,128]{1,0:T(8,128)S(1)} %get-tuple-element.40.small), custom_call_target="tpu_custom_call" | custom-call | flops 2000000000 | bytes 1048576 | tf_op jit(solution)/shard_map/input_grad/pallas_call | solution.py:394
  61.7 0.2 collective-permute-done.15.refs_0_
  61.9 1.0 %collective-permute-done.16.refs_1_ = bf16[193,128]{1,0:T(8,128)(2,1)S(1)} collective-permute-done((bf16[193,128]{1,0:T(8,128)(2,1)S(1)}, bf16[193,128]{1,0:T(8,128)(2,1)S(1)}, u32[]{:S(2)}, u32[]{:S(2)}) %collective-permute-start.16) | collective-permute-done | bytes 49440 | tf_op jit(solution)/shard_map/ppermute | solution.py:533
  63.0 0.7 %add_column.1 = f32[193,128]{1,0:T(8,128)} custom-call(f32[193,128]{1,0:T(8,128)S(1)} %get-tuple-element.59.kept, bf16[193,128]{1,0:T(8,128)(2,1)S(1)} %collective-permute-done.15.refs_0_, bf16[193,128]{1,0:T(8,128)(2,1)S(1)} %collective-permute-done.16.refs_1_, bf16[193,128]{1,0:T(8,128)(2,1)S(1)} %collective-permute-done.17.refs_2_), custom_call_target="tpu_custom_call" | custom-call | flops 1000000000 | bytes 1048576 | tf_op jit(solution)/shard_map/add_column/pallas_call | solution.py:394
  (16 shorter events, 0.0 us)
Async XLA Ops:
  0.6 10.6 %collective-permute-start = (bf16[193,128]{1,0:T(8,128)(2,1)}, bf16[193,128]{1,0:T(8,128)(2,1)S(1)}, u32[]{:S(2)}, u32[]{:S(2)}) collective-permute-start(bf16[193,128]{1,0:T(8,128)(2,1)} %params.1), channel_id=1, source_target_pairs={{0,8},{1,9},{2,10},{3,11},{4,12},{5,13},{6,14},{7,15},{8,16},{9,17... | collective-permute-start | bytes 148232 | tf_op jit(solution)/shard_map/ppermute | solution.py:533
  3.7 7.5 %collective-permute-start.1 = (bf16[193,128]{1,0:T(8,128)(2,1)}, bf16[193,128]{1,0:T(8,128)(2,1)S(1)}, u32[]{:S(2)}, u32[]{:S(2)}) collective-permute-start(bf16[193,128]{1,0:T(8,128)(2,1)} %params.1), channel_id=1, source_target_pairs={{0,16},{1,17},{2,18},{3,19},{4,20},{5,21},{6,22},{7,23},{8,24},{9,... | collective-permute-start | bytes 148232 | tf_op jit(solution)/shard_map/ppermute | solution.py:533
  6.3 4.9 %collective-permute-start.2 = (bf16[193,128]{1,0:T(8,128)(2,1)}, bf16[193,128]{1,0:T(8,128)(2,1)S(1)}, u32[]{:S(2)}, u32[]{:S(2)}) collective-permute-start(bf16[193,128]{1,0:T(8,128)(2,1)} %params.1), channel_id=1, source_target_pairs={{0,24},{1,25},{2,26},{3,27},{4,28},{5,29},{6,30},{7,31},{8,0},{9,1... | collective-permute-start | bytes 148232 | tf_op jit(solution)/shard_map/ppermute | solution.py:533
  7.6 1.0 %copy-start = (bf16[1024,256]{1,0:T(8,128)(2,1)S(1)}, bf16[1024,256]{1,0:T(8,128)(2,1)}, u32[]{:S(2)}) copy-start(bf16[1024,256]{1,0:T(8,128)(2,1)} %cot.3) | copy-start | bytes 1572868
  8.7 1.0 %copy-start.2 = (bf16[1024,256]{1,0:T(8,128)(2,1)S(1)}, bf16[1024,256]{1,0:T(8,128)(2,1)}, u32[]{:S(2)}) copy-start(bf16[1024,256]{1,0:T(8,128)(2,1)} %tok.5) | copy-start | bytes 1572868
  9.7 0.8 %copy-start.4 = (bf16[193,128]{1,0:T(8,128)(2,1)S(1)}, bf16[193,128]{1,0:T(8,128)(2,1)}, u32[]{:S(2)}) copy-start(bf16[193,128]{1,0:T(8,128)(2,1)} %params.1) | copy-start | bytes 148228
  11.2 0.8 %copy-start.6 = (bf16[256,1024]{1,0:T(8,128)(2,1)}, bf16[256,1024]{1,0:T(8,128)(2,1)S(1)}, u32[]{:S(2)}) copy-start(bf16[256,1024]{1,0:T(8,128)(2,1)S(1)} %get-tuple-element.36.cot_turned) | copy-start | bytes 1572868
  11.2 14.1 %copy-start.5 = (s32[1024]{0:T(1024)S(1)}, s32[1024]{0:T(1024)}, u32[]{:S(2)}) copy-start(s32[1024]{0:T(1024)} %param.6) | copy-start | bytes 12292
  12.0 8.0 %collective-permute-start.3 = (bf16[4,193,128]{2,1,0:T(8,128)(2,1)S(1)}, bf16[4,193,128]{2,1,0:T(8,128)(2,1)S(1)}, u32[]{:S(2)}, u32[]{:S(2)}) collective-permute-start(bf16[4,193,128]{2,1,0:T(8,128)(2,1)S(1)} %stack.169.refs_0_), channel_id=1, source_target_pairs={{0,2},{1,3},{2,0},{3,1},{4,6},{5,7},{6,4},{7,5},{8,10},{9,11},{10,... | collective-permute-start | bytes 592904 | tf_op jit(solution)/shard_map/ppermute | solution.py:533
  13.5 10.1 %collective-permute-start.4 = (bf16[4,193,128]{2,1,0:T(8,128)(2,1)S(1)}, bf16[4,193,128]{2,1,0:T(8,128)(2,1)S(1)}, u32[]{:S(2)}, u32[]{:S(2)}) collective-permute-start(bf16[4,193,128]{2,1,0:T(8,128)(2,1)S(1)} %stack.169.refs_0_), channel_id=1, source_target_pairs={{0,4},{1,5},{2,6},{3,7},{4,0},{5,1},{6,2},{7,3},{8,12},{9,13},{10,... | collective-permute-start | bytes 592904 | tf_op jit(solution)/shard_map/ppermute | solution.py:533
  15.0 8.6 %collective-permute-start.5 = (bf16[4,193,128]{2,1,0:T(8,128)(2,1)S(1)}, bf16[4,193,128]{2,1,0:T(8,128)(2,1)S(1)}, u32[]{:S(2)}, u32[]{:S(2)}) collective-permute-start(bf16[4,193,128]{2,1,0:T(8,128)(2,1)S(1)} %stack.169.refs_0_), channel_id=1, source_target_pairs={{0,6},{1,7},{2,4},{3,5},{4,2},{5,3},{6,0},{7,1},{8,14},{9,15},{10,... | collective-permute-start | bytes 592904 | tf_op jit(solution)/shard_map/ppermute | solution.py:533
  15.5 8.8 %collective-permute-start.6 = (bf16[4,193,128]{2,1,0:T(8,128)(2,1)S(1)}, bf16[4,193,128]{2,1,0:T(8,128)(2,1)S(1)}, u32[]{:S(2)}, u32[]{:S(2)}) collective-permute-start(bf16[4,193,128]{2,1,0:T(8,128)(2,1)S(1)} %stack.169.refs_0_), channel_id=1, source_target_pairs={{0,1},{1,0},{2,3},{3,2},{4,5},{5,4},{6,7},{7,6},{8,9},{9,8},{10,11... | collective-permute-start | bytes 592904 | tf_op jit(solution)/shard_map/ppermute | solution.py:533
  20.0 4.3 %collective-permute-start.7 = (bf16[4,193,128]{2,1,0:T(8,128)(2,1)S(1)}, bf16[4,193,128]{2,1,0:T(8,128)(2,1)S(1)}, u32[]{:S(2)}, u32[]{:S(2)}) collective-permute-start(bf16[4,193,128]{2,1,0:T(8,128)(2,1)S(1)} %collective-permute-done.3.refs_1_), channel_id=1, source_target_pairs={{0,1},{1,0},{2,3},{3,2},{4,5},{5,4},{6,7},{7,6},{8,9},{9,8},{10,11... | collective-permute-start | bytes 592904 | tf_op jit(solution)/shard_map/ppermute | solution.py:533
  23.6 1.5 %collective-permute-start.8 = (bf16[4,193,128]{2,1,0:T(8,128)(2,1)S(1)}, bf16[4,193,128]{2,1,0:T(8,128)(2,1)S(1)}, u32[]{:S(2)}, u32[]{:S(2)}) collective-permute-start(bf16[4,193,128]{2,1,0:T(8,128)(2,1)S(1)} %collective-permute-done.4.refs_2_), channel_id=1, source_target_pairs={{0,1},{1,0},{2,3},{3,2},{4,5},{5,4},{6,7},{7,6},{8,9},{9,8},{10,11... | collective-permute-start | bytes 592904 | tf_op jit(solution)/shard_map/ppermute | solution.py:533
  23.6 1.7 %collective-permute-start.9 = (bf16[4,193,128]{2,1,0:T(8,128)(2,1)S(1)}, bf16[4,193,128]{2,1,0:T(8,128)(2,1)S(1)}, u32[]{:S(2)}, u32[]{:S(2)}) collective-permute-start(bf16[4,193,128]{2,1,0:T(8,128)(2,1)S(1)} %collective-permute-done.5.refs_3_), channel_id=1, source_target_pairs={{0,1},{1,0},{2,3},{3,2},{4,5},{5,4},{6,7},{7,6},{8,9},{9,8},{10,11... | collective-permute-start | bytes 592904 | tf_op jit(solution)/shard_map/ppermute | solution.py:533
  25.3 3.7 %copy-start.1 = (bf16[1024,256]{1,0:T(8,128)(2,1)S(1)}, bf16[1024,256]{1,0:T(8,128)(2,1)}, u32[]{:S(2)}) copy-start(bf16[1024,256]{1,0:T(8,128)(2,1)} %cot.3) | copy-start | bytes 1572868
  25.3 3.7 %copy-start.3 = (bf16[1024,256]{1,0:T(8,128)(2,1)S(1)}, bf16[1024,256]{1,0:T(8,128)(2,1)}, u32[]{:S(2)}) copy-start(bf16[1024,256]{1,0:T(8,128)(2,1)} %tok.5) | copy-start | bytes 1572868
  25.3 3.7 %copy-start.7 = (bf16[256,1024]{1,0:T(8,128)(2,1)S(1)}, bf16[256,1024]{1,0:T(8,128)(2,1)}, u32[]{:S(2)}) copy-start(bf16[256,1024]{1,0:T(8,128)(2,1)} %copy-done.6) | copy-start | bytes 1572868
  37.2 5.5 %collective-permute-start.11 = (bf16[12,193,128]{2,1,0:T(8,128)(2,1)S(1)}, bf16[12,193,128]{2,1,0:T(8,128)(2,1)S(1)}, u32[]{:S(2)}, u32[]{:S(2)}) collective-permute-start(bf16[12,193,128]{2,1,0:T(8,128)(2,1)S(1)} %get-tuple-element.54), channel_id=1, source_target_pairs={{0,1},{1,0},{2,3},{3,2},{4,5},{5,4},{6,7},{7,6},{8,9},{9,8},{10,11... | collective-permute-start | bytes 1778696 | tf_op jit(solution)/shard_map/ppermute | solution.py:533
  41.1 1.6 %collective-permute-start.10 = (bf16[4,224,128]{2,1,0:T(8,128)(2,1)S(1)}, bf16[4,224,128]{2,1,0:T(8,128)(2,1)S(1)}, u32[]{:S(2)}, u32[]{:S(2)}) collective-permute-start(bf16[4,224,128]{2,1,0:T(8,128)(2,1)S(1)} %get-tuple-element.52), channel_id=1, source_target_pairs={{0,1},{1,0},{2,3},{3,2},{4,5},{5,4},{6,7},{7,6},{8,9},{9,8},{10,11... | collective-permute-start | bytes 688136 | tf_op jit(solution)/shard_map/ppermute | solution.py:533
  42.9 8.0 %collective-permute-start.12 = (bf16[4,193,128]{2,1,0:T(8,128)(2,1)S(1)}, bf16[4,193,128]{2,1,0:T(8,128)(2,1)S(1)}, u32[]{:S(2)}, u32[]{:S(2)}) collective-permute-start(bf16[4,193,128]{2,1,0:T(8,128)(2,1)S(1)} %get-tuple-element.56), channel_id=1, source_target_pairs={{0,2},{1,3},{2,0},{3,1},{4,6},{5,7},{6,4},{7,5},{8,10},{9,11},{10,... | collective-permute-start | bytes 592904 | tf_op jit(solution)/shard_map/ppermute | solution.py:533
  43.9 10.1 %collective-permute-start.13 = (bf16[4,193,128]{2,1,0:T(8,128)(2,1)S(1)}, bf16[4,193,128]{2,1,0:T(8,128)(2,1)S(1)}, u32[]{:S(2)}, u32[]{:S(2)}) collective-permute-start(bf16[4,193,128]{2,1,0:T(8,128)(2,1)S(1)} %get-tuple-element.57), channel_id=1, source_target_pairs={{0,4},{1,5},{2,6},{3,7},{4,0},{5,1},{6,2},{7,3},{8,12},{9,13},{10,... | collective-permute-start | bytes 592904 | tf_op jit(solution)/shard_map/ppermute | solution.py:533
  45.0 10.6 %collective-permute-start.14 = (bf16[4,193,128]{2,1,0:T(8,128)(2,1)S(1)}, bf16[4,193,128]{2,1,0:T(8,128)(2,1)S(1)}, u32[]{:S(2)}, u32[]{:S(2)}) collective-permute-start(bf16[4,193,128]{2,1,0:T(8,128)(2,1)S(1)} %get-tuple-element.58), channel_id=1, source_target_pairs={{0,6},{1,7},{2,4},{3,5},{4,2},{5,3},{6,0},{7,1},{8,14},{9,15},{10,... | collective-permute-start | bytes 592904 | tf_op jit(solution)/shard_map/ppermute | solution.py:533
  55.8 6.1 %collective-permute-start.15 = (bf16[193,128]{1,0:T(8,128)(2,1)S(1)}, bf16[193,128]{1,0:T(8,128)(2,1)S(1)}, u32[]{:S(2)}, u32[]{:S(2)}) collective-permute-start(bf16[193,128]{1,0:T(8,128)(2,1)S(1)} %get-tuple-element.60), channel_id=1, source_target_pairs={{0,8},{1,9},{2,10},{3,11},{4,12},{5,13},{6,14},{7,15},{8,16},{9,17... | collective-permute-start | bytes 148232 | tf_op jit(solution)/shard_map/ppermute | solution.py:533
  56.5 6.4 %collective-permute-start.16 = (bf16[193,128]{1,0:T(8,128)(2,1)S(1)}, bf16[193,128]{1,0:T(8,128)(2,1)S(1)}, u32[]{:S(2)}, u32[]{:S(2)}) collective-permute-start(bf16[193,128]{1,0:T(8,128)(2,1)S(1)} %get-tuple-element.61), channel_id=1, source_target_pairs={{0,16},{1,17},{2,18},{3,19},{4,20},{5,21},{6,22},{7,23},{8,24},{9,... | collective-permute-start | bytes 148232 | tf_op jit(solution)/shard_map/ppermute | solution.py:533
  57.7 5.3 %collective-permute-start.17 = (bf16[193,128]{1,0:T(8,128)(2,1)S(1)}, bf16[193,128]{1,0:T(8,128)(2,1)S(1)}, u32[]{:S(2)}, u32[]{:S(2)}) collective-permute-start(bf16[193,128]{1,0:T(8,128)(2,1)S(1)} %get-tuple-element.62), channel_id=1, source_target_pairs={{0,24},{1,25},{2,26},{3,27},{4,28},{5,29},{6,30},{7,31},{8,0},{9,1... | collective-permute-start | bytes 148232 | tf_op jit(solution)/shard_map/ppermute | solution.py:533

commit v7 on v6

--- a/solution.py
+++ b/solution.py
@@ -30,7 +30,7 @@
 ROW_TOTAL = 6176
 GAIN_ONE, SHIFT_ONE, BIAS_QUERY, BIAS_VALUE, BIAS_OUT = 0, 2, 4, 6, 8
 GAIN_TWO, SHIFT_TWO, BIAS_UP, BIAS_DOWN = 10, 12, 14, 22
-SMALL_ROWS = 24
+SMALL_ROWS = 32
 LATE_SMALL = 8
 
 SHARE = 193
@@ -109,38 +109,38 @@
         flat[pl.ds(start + j, rows, stride=per_row), :] = matrix[:, j * LANES : (j + 1) * LANES]
 
 
-def prepare_kernel(tok, cot, params, normed_out, normed_turned, cot_turned, own):
+def prepare_kernel(tok, params, normed_out, normed_turned, own):
     normed, _ = normalize(tok[...].astype(F32))
     normed_out[...] = normed
     normed_turned[...] = normed.astype(BF16).T
-    cot_turned[...] = cot[...].T
     own[...] = params[...]
 
 
-def unpack(ids, bufs, flat):
-    slot = 0
-    for buf in bufs:
-        count, rows, _ = buf.shape
-
-        def place(i, carry, buf=buf, slot=slot, rows=rows):
-            flat[pl.ds(ids[slot + i] * rows, rows), :] = buf[i].astype(F32)
-            return carry
-
-        lax.fori_loop(0, count, place, 0)
-        slot += count
-
-
-def attend_kernel(n_bufs, ids, seg, normed, *refs):
-    bufs = refs[:n_bufs]
-    (
-        project_out, weights_out, attended_out, w_qkv, w_out, w_up, w_down, small, flat,
-    ) = refs[n_bufs:]
-    unpack(ids, bufs, flat)
+def sort_kernel(ids, *refs):
+    received, (first, rest, stage, wide) = refs[:Z], refs[Z:]
+    for d in range(Z):
+        stage[lax.rem(ids[0] + Z - d, Z)] = received[d][...]
+    rest[...] = stage[1:]
+    wide[:SHARE, :] = stage[0].astype(F32)
+    wide[SHARE:SIDE, :] = jnp.zeros((SIDE - SHARE, LANES), F32)
+    last = stage[Z - 1].astype(F32)
+    wide[SIDE:, :] = last[SMALL_IN_SHARE:, :]
+    first[...] = wide[...].astype(BF16)
+
+
+def attend_kernel(ids, seg, normed, *refs):
+    bufs = refs[: 2 * PLANE]
+    project_out, weights_out, attended_out, w_qkv, small, first_out, flat = refs[2 * PLANE :]
+    for slot, buf in enumerate(bufs):
+        wide = buf[...].astype(F32)
+        flat[pl.ds(ids[slot] * SHARE, SHARE), :] = wide[:SHARE, :]
+
+        @pl.when(ids[slot] == 2 * PLANE - 1)
+        def _():
+            small[...] = wide[SIDE:, :]
+
     matrix_from_flat(flat, ROW_QKV, D, 3 * D, w_qkv)
-    matrix_from_flat(flat, ROW_OUT, D, D, w_out)
-    matrix_from_flat(flat, ROW_UP, D, FF, w_up)
-    matrix_from_flat(flat, ROW_DOWN, FF, D, w_down)
-    small[...] = flat[ROW_SMALL:ROW_END, :]
+    first_out[...] = flat[ROW_OUT:FIRST_ROWS, :]
 
     gain = small_vector(small, GAIN_ONE, 2)
     shift = small_vector(small, SHIFT_ONE, 2)
@@ -190,63 +190,93 @@
 
 
 def feed_kernel(
-    ids, tok, attended, cot, cot_turned, w_out, w_up, w_down, small,
-    middle_out, activated_out, grad_middle_out, grad_attended_out, keep_out, send_out, first_out,
-    normed_low_all, grad_hidden, grad_middle_low_all, acc_small, flat,
+    ids, tok, attended, cot, small, first_in, *refs,
 ):
-    acc_small[...] = jnp.zeros_like(acc_small)
+    bufs = refs[: 2 * PLANE]
+    (
+        middle_out, activated_out, grad_middle_out, grad_attended_out, w_down, keep_out, send_out, first_out,
+        w_out, w_up, grad_hidden, flat,
+    ) = refs[2 * PLANE :]
+    flat[:HEAD_ROWS, :] = first_in[...]
+    for slot, buf in enumerate(bufs):
+        for z in range(1, Z):
+            share = ids[slot] + z * 2 * PLANE
+            flat[pl.ds(share * SHARE - ROW_OUT, SHARE), :] = buf[z - 1].astype(F32)
+    matrix_from_flat(flat, 0, D, D, w_out)
+    matrix_from_flat(flat, ROW_UP - ROW_OUT, D, FF, w_up)
+    matrix_from_flat(flat, ROW_DOWN - ROW_OUT, FF, D, w_down)
+
     gain = small_vector(small, GAIN_TWO, 2)
-    shift = small_vector(small, SHIFT_TWO, 2)
-    bias_out = small_vector(small, BIAS_OUT, 2)
+    middle = (
+        tok[...].astype(F32) + dot(attended[...], w_out[...]) + small_vector(small, BIAS_OUT, 2)
+    )
+    middle_out[...] = middle
+    normed, rate = normalize(middle)
+    normed_low = (normed * gain + small_vector(small, SHIFT_TWO, 2)).astype(BF16)
+    normed_turned = normed_low.T
+    cotangent = cot[...]
+    cot_turned = cotangent.T
     slope = 0.7978845608028654
     cubic = slope * 0.044715
-
-    def some(g, carry):
-        base = pl.multiple_of(g * WIDE, WIDE)
-        span = pl.ds(base, WIDE)
-        middle = tok[span, :].astype(F32) + dot(attended[span, :], w_out[...]) + bias_out
-        middle_out[span, :] = middle
-        normed, rate = normalize(middle)
-        normed_low = (normed * gain + shift).astype(BF16)
-        normed_low_all[span, :] = normed_low
-        cotangent = cot[span, :]
-        for c in range(0, FF, CHUNK):
-            columns = slice(c, c + CHUNK)
-            bias = small_vector(small, BIAS_UP + c // LANES, CHUNK // LANES)
-            hidden_all = dot(normed_low, w_up[:, columns])
-            grad_all = dot_nt(cotangent, w_down[columns, :])
-            total = jnp.zeros((8, CHUNK), F32)
-            for r in range(0, WIDE, STRIP):
-                rows = slice(r, r + STRIP)
-                strip = pl.ds(pl.multiple_of(base + r, STRIP), STRIP)
-                hidden = hidden_all[rows] + bias
-                square = hidden * hidden
-                half = 0.5 + 0.5 * jnp.tanh(hidden * (slope + cubic * square))
-                activated = hidden * half
-                derivative = half + activated * (1.0 - half) * (2 * slope + (6 * cubic) * square)
-                low = (grad_all[rows] * derivative).astype(BF16)
-                activated_out[strip, columns] = activated.astype(BF16)
-                grad_hidden[strip, columns] = low
-                total += fold_rows(low.astype(F32))
-            acc_small[:, 3 * D + c : 3 * D + c + CHUNK] += total
-        grad_result = cotangent.astype(F32)
-        grad_normed = dot_nt(grad_hidden[span, :], w_up[...])
-        grad_middle = grad_result + normalize_back(grad_normed, gain, normed, rate)
-        grad_middle_out[span, :] = grad_middle
-        grad_middle_low = grad_middle.astype(BF16)
-        grad_middle_low_all[span, :] = grad_middle_low
-        grad_attended_out[span, :] = dot_nt(grad_middle_low, w_out[...]).astype(BF16)
-        acc_small[:, 0:D] += fold_rows(grad_middle_low.astype(F32))
-        acc_small[:, D : 2 * D] += fold_rows(grad_normed * normed)
-        acc_small[:, 2 * D : 3 * D] += fold_rows(grad_normed)
-        acc_small[:, 3 * D + FF :] += fold_rows(grad_result)
-        return carry
-
-    lax.fori_loop(0, tok.shape[0] // WIDE, some, 0)
-    turned_to_flat(dot(cot_turned[...], activated_out[...]), FF, D, flat, ROW_DOWN - ROW_OUT)
-    matrix_to_flat(dot_tn(normed_low_all[...], grad_hidden[...]), D, FF, flat, ROW_UP - ROW_OUT)
-    matrix_to_flat(dot_tn(attended[...], grad_middle_low_all[...]), D, D, flat, 0)
-    sums = jnp.sum(acc_small[...], axis=0, keepdims=True)
+    row_up, row_down = ROW_UP - ROW_OUT, ROW_DOWN - ROW_OUT
+
+    def products(c):
+        columns = slice(c, c + CHUNK)
+        return dot(normed_low, w_up[:, columns]), dot_nt(cotangent, w_down[columns, :])
+
+    def bend(c, hidden_all, grad_all):
+        columns = slice(c, c + CHUNK)
+        bias = small_vector(small, BIAS_UP + c // LANES, CHUNK // LANES)
+        total = jnp.zeros((8, CHUNK), F32)
+        for r in range(0, tok.shape[0], STRIP):
+            rows = slice(r, r + STRIP)
+            hidden = hidden_all[rows] + bias
+            square = hidden * hidden
+            half = 0.5 + 0.5 * jnp.tanh(hidden * (slope + cubic * square))
+            activated = hidden * half
+            derivative = half + activated * (1.0 - half) * (2 * slope + (6 * cubic) * square)
+            low = (grad_all[rows] * derivative).astype(BF16)
+            activated_out[rows, columns] = activated.astype(BF16)
+            grad_hidden[rows, columns] = low
+            total += fold_rows(low.astype(F32))
+        return total
+
+    def weight_gradients(c):
+        columns = slice(c, c + CHUNK)
+        turned_to_flat(dot(cot_turned, activated_out[:, columns]), CHUNK, D, flat, row_down + c * D // LANES)
+        grads = dot(normed_turned, grad_hidden[:, columns])
+        for j in range(CHUNK // LANES):
+            flat[pl.ds(row_up + c // LANES + j, D, stride=FF // LANES), :] = grads[
+                :, j * LANES : (j + 1) * LANES
+            ]
+
+    ahead, totals = products(0), []
+    for c in range(0, FF, CHUNK):
+        now = ahead
+        if c + CHUNK < FF:
+            ahead = products(c + CHUNK)
+        if c > 0:
+            weight_gradients(c - CHUNK)
+        totals.append(bend(c, *now))
+    grad_normed = dot_nt(grad_hidden[...], w_up[...])
+    weight_gradients(FF - CHUNK)
+    grad_result = cotangent.astype(F32)
+    grad_middle = grad_result + normalize_back(grad_normed, gain, normed, rate)
+    grad_middle_out[...] = grad_middle
+    grad_middle_low = grad_middle.astype(BF16)
+    grad_attended_out[...] = dot_nt(grad_middle_low, w_out[...]).astype(BF16)
+    matrix_to_flat(dot_tn(attended[...], grad_middle_low), D, D, flat, 0)
+    sums = jnp.concatenate(
+        [
+            fold_rows(grad_middle_low.astype(F32)),
+            fold_rows(grad_normed * normed),
+            fold_rows(grad_normed),
+            *totals,
+            fold_rows(grad_result),
+        ],
+        axis=1,
+    )
+    sums = jnp.sum(sums, axis=0, keepdims=True)
     base = ROW_SMALL - ROW_OUT
     flat[base : base + LATE_SMALL, :] = jnp.zeros((LATE_SMALL, LANES), F32)
     for i in range(sums.shape[1] // LANES):
@@ -348,27 +378,21 @@
     lax.fori_loop(0, tok.shape[0] // WIDE, some, 0)
 
 
-def stack_kernel(*refs):
-    for d, ref in enumerate(refs[:-1]):
-        refs[-1][d] = ref[...]
-
-
-def add_core_kernel(first, first_in, rest, rest_in, keep_out, *refs):
-    sends, column = refs[:-1], refs[-1]
+def add_core_kernel(kept, received, keep_out, *sends):
+    part = kept.shape[0] // PLANE
+    for p, out in enumerate((keep_out, *sends)):
+        span = slice(p * part, (p + 1) * part)
+        out[...] = (kept[span] + received[span].astype(F32)).astype(out.dtype)
+
+
+def add_plane_kernel(ids, first_kept, rest_kept, *refs):
+    firsts, rests = refs[: PLANE - 1], refs[PLANE - 1 : 2 * (PLANE - 1)]
+    keep_out, *sends, column = refs[2 * (PLANE - 1) :]
+    first = first_kept[0] + sum(item[0].astype(F32) for item in firsts)
+    column[0] = first[:SHARE, :]
+    column[1:] = rest_kept[...] + sum(item[...].astype(F32) for item in rests)
     end = SMALL_IN_SHARE + LATE_SMALL
-    for p, out in enumerate((keep_out, *sends)):
-        item = first[p] + first_in[p].astype(F32)
-        span = slice(p * (Z - 1), (p + 1) * (Z - 1))
-        column[0] = item[:SHARE, :]
-        column[1:] = rest[span] + rest_in[span].astype(F32)
-        column[Z - 1, SMALL_IN_SHARE:end, :] += item[SIDE : SIDE + LATE_SMALL, :]
-        out[...] = column[...].astype(out.dtype)
-
-
-def add_plane_kernel(ids, kept, *refs):
-    arrived = refs[: PLANE - 1]
-    keep_out, *sends, column = refs[PLANE - 1 :]
-    column[...] = kept[...] + sum(item[...].astype(F32) for item in arrived)
+    column[Z - 1, SMALL_IN_SHARE:end, :] += first[SIDE : SIDE + LATE_SMALL, :]
     keep_out[...] = column[ids[0]]
     for d, out in enumerate(sends):
         out[...] = column[lax.rem(ids[0] + d + 1, Z)].astype(BF16)
@@ -386,7 +410,7 @@
 VMEM_SPEC = pl.BlockSpec(memory_space=pltpu.VMEM)
 
 def cost(us):
-    return pl.CostEstimate(flops=int(us * 1e9), bytes_accessed=1 << 20, transcendentals=0)
+    return pl.CostEstimate(flops=int(us * 5e7), bytes_accessed=1 << 20, transcendentals=0)
 
 
 def call(kernel, name, ids, inputs, outs, scratch=(), us=1):
@@ -404,47 +428,43 @@
     return results if len(outs) > 1 else results[0]
 
 
-def prepare(tokens, cotangent, params):
+def prepare(tokens, params):
     rows = tokens.shape[0]
-    turned = like(D, rows, kind=BF16)
     return call(
-        prepare_kernel, "prepare", None, [tokens, cotangent, params],
-        [like(rows, D), turned, turned, like(*params.shape, kind=BF16)], us=2,
+        prepare_kernel, "prepare", None, [tokens, params],
+        [like(rows, D), like(D, rows, kind=BF16), like(*params.shape, kind=BF16)], us=2,
     )
 
 
 def attend(ids, segments, normed, bufs):
     rows = normed.shape[0]
-    total = sum(buf.shape[0] * buf.shape[1] for buf in bufs)
-    shapes = [
-        (rows, 3 * D), (rows, HEADS * SEQ), (rows, D), (D, 3 * D), (D, D), (D, FF), (FF, D),
-    ]
+    shapes = [(rows, 3 * D), (rows, HEADS * SEQ), (rows, D), (D, 3 * D)]
     return call(
-        functools.partial(attend_kernel, len(bufs)), "attend", ids, [segments, normed, *bufs],
-        [like(*shape, kind=BF16) for shape in shapes] + [like(SMALL_ROWS, LANES)],
-        [pltpu.VMEM((total, LANES), F32)], us=6,
-    )
-
-
-def feed(ids, tokens, attended, cotangent, cot_turned, w_out, w_up, w_down, small, send_kind):
+        attend_kernel, "attend", ids, [segments, normed, *bufs],
+        [like(*shape, kind=BF16) for shape in shapes]
+        + [like(SMALL_ROWS, LANES), like(HEAD_ROWS, LANES)],
+        [pltpu.VMEM((FIRST_ROWS, LANES), F32)], us=6,
+    )
+
+
+def feed(ids, tokens, attended, cotangent, small, first, bufs, send_kind):
     rows = tokens.shape[0]
     return call(
-        feed_kernel, "feed", ids,
-        [tokens, attended, cotangent, cot_turned, w_out, w_up, w_down, small],
+        feed_kernel, "feed", ids, [tokens, attended, cotangent, small, first, *bufs],
         [
             like(rows, D),
             like(rows, FF, kind=BF16),
             like(rows, D),
             like(rows, D, kind=BF16),
+            like(FF, D, kind=BF16),
             like(PLANE * (Z - 1), SHARE, LANES),
             like(PLANE * (Z - 1), SHARE, LANES, kind=send_kind),
             like(HEAD_ROWS, LANES),
         ],
         [
-            pltpu.VMEM((rows, D), BF16),
+            pltpu.VMEM((D, D), BF16),
+            pltpu.VMEM((D, FF), BF16),
             pltpu.VMEM((rows, FF), BF16),
-            pltpu.VMEM((rows, D), BF16),
-            pltpu.VMEM((8, (SMALL_ROWS - LATE_SMALL) * LANES), F32),
             pltpu.VMEM((ROW_TOTAL - ROW_OUT, LANES), F32),
         ],
         us=8,
@@ -475,40 +495,36 @@
     )
 
 
-def block(prepared, tokens, segment_ids, cotangent, share_ids, shares, grad_ids, send_kind, core_exchange):
-    normed, normed_turned, cot_turned = prepared
-    segments = segment_ids.reshape(-1, SEQ)
-    project, weights, attended, w_qkv, w_out, w_up, w_down, small = attend(
-        share_ids, segments, normed, shares
-    )
-    middle, activated, grad_middle, grad_attended, rest, rest_send, first_grad = feed(
-        grad_ids, tokens, attended, cotangent, cot_turned, w_out, w_up, w_down, small, send_kind
-    )
-    rest_in = core_exchange(rest_send)
+def local_any(n, tokens, params, segment_ids, cotangent):
+    total = n * params.shape[0]
+    normed, normed_turned, _ = prepare(tokens, params)
+    gathered = lax.all_gather(params, "fsdp", axis=0).reshape(total, LANES)
+    shares = gathered[:ROW_TOTAL].reshape(Z, 2 * PLANE, SHARE, LANES)
+    order = [p * 2 + c for c in range(2) for p in range(PLANE)]
+    side = jnp.concatenate(
+        [jnp.zeros((SIDE - SHARE, LANES), BF16), gathered[ROW_SMALL:ROW_TOTAL]], axis=0
+    )
+    firsts = [jnp.concatenate([shares[0, k], side], axis=0) for k in order]
+    rests = [shares[1:, k] for k in order]
+    ids = jnp.array(order, jnp.int32)
+    project, weights, attended, w_qkv, small, first = attend(
+        ids, segment_ids.reshape(-1, SEQ), normed, firsts
+    )
+    middle, activated, grad_middle, grad_attended, w_down, rest, rest_send, first_grad = feed(
+        ids, tokens, attended, cotangent, small, first, rests, F32
+    )
+    outputs = result(middle, activated, w_down, small)
     grad_project, first, first_send = attend_back(
-        grad_ids, project, weights, grad_attended, normed_turned, w_qkv, small, first_grad, send_kind
-    )
-    first_in = core_exchange(first_send)
-    outputs = result(middle, activated, w_down, small)
+        ids, project, weights, grad_attended, normed_turned, w_qkv, small, first_grad, F32
+    )
     input_grad = input_gradient(tokens, grad_project, grad_middle, w_qkv, small)
-    return outputs, input_grad, first, first_in, rest, rest_in
-
-
-def local_any(n, tokens, params, segment_ids, cotangent):
-    *prepared, _ = prepare(tokens, cotangent, params)
-    gathered = lax.all_gather(params, "fsdp", axis=0)
-    ids = jnp.arange(n, dtype=jnp.int32)
-    order = jnp.array([p * 2 + c for c in range(2) for p in range(PLANE)], jnp.int32)
-    outputs, input_grad, first, first_send, rest, rest_send = block(
-        prepared, tokens, segment_ids, cotangent, ids, [gathered], order, F32, lambda values: values
-    )
     first = jnp.stack([first, first_send], axis=1)
     rest = jnp.stack([rest, rest_send]).reshape(2, PLANE, Z - 1, SHARE, LANES).transpose(2, 1, 0, 3, 4)
     flat = jnp.concatenate(
         [
             first[:, :, :SHARE].reshape(-1, LANES),
             rest.reshape(-1, LANES),
-            jnp.zeros((n * params.shape[0] - ROW_TOTAL, LANES), F32),
+            jnp.zeros((total - ROW_TOTAL, LANES), F32),
         ],
         axis=0,
     )
@@ -533,36 +549,61 @@
     return lax.ppermute(values, "fsdp", pairs)
 
 
+STEPS = (3, 1, 2)
+
+
+def add_core(keep, send):
+    part = (keep.shape[0] // PLANE,) + keep.shape[1:]
+    return call(
+        add_core_kernel, "add_core", None, [keep, send],
+        [like(*part)] + [like(*part, kind=BF16)] * (PLANE - 1),
+    )
+
+
 def local_slice(tokens, params, segment_ids, cotangent):
     me = lax.axis_index("fsdp").astype(jnp.int32)
     z, plane, core = me // (2 * PLANE), (me // 2) % PLANE, me % 2
-    planes = [(dc, dp) for dc in range(2) for dp in range(PLANE)]
-    share_ids = jnp.stack(
-        [index_of((z - dz) % Z, plane ^ dp, core ^ dc) for dc, dp in planes for dz in range(Z)]
-    )
-    grad_ids = jnp.stack([(plane ^ dp) * 2 + (core ^ dc) for dc, dp in planes])
-
-    *prepared, own = prepare(tokens, cotangent, params)
-    column = call(
-        stack_kernel, "stack", None, [own] + [move(params, d, 0, 0) for d in range(1, Z)],
-        [like(Z, SHARE, LANES, kind=BF16)],
-    )
-    same = [column] + [move(column, 0, d, 0) for d in range(1, PLANE)]
-    shares = same + [move(item, 0, 0, 1) for item in same]
-    outputs, input_grad, first, first_in, rest, rest_in = block(
-        prepared, tokens, segment_ids, cotangent, share_ids, shares, grad_ids, BF16,
-        lambda values: move(values, 0, 0, 1),
-    )
-
-    part = (Z, SHARE, LANES)
+    where = z.reshape(1)
+    ids = jnp.stack(
+        [(plane ^ dp) * 2 + (core ^ dc) for dc in range(2) for dp in (0, *STEPS)]
+    )
+
+    normed, normed_turned, own = prepare(tokens, params)
+    first, rest = call(
+        sort_kernel, "sort_shares", where, [own] + [move(params, d, 0, 0) for d in range(1, Z)],
+        [like(SIDE + SMALL_ROWS, LANES, kind=BF16), like(Z - 1, SHARE, LANES, kind=BF16)],
+        [pltpu.VMEM((Z, SHARE, LANES), BF16), pltpu.VMEM((SIDE + SMALL_ROWS, LANES), F32)],
+    )
+    firsts = [first] + [move(first, 0, d, 0) for d in STEPS]
+    rests = [move(rest, 0, d, 0) for d in STEPS]
+    firsts = firsts + [move(item, 0, 0, 1) for item in firsts]
+    project, weights, attended, w_qkv, small, first = attend(
+        ids, segment_ids.reshape(-1, SEQ), normed, firsts
+    )
+    *rests, attended = lax.optimization_barrier((*rests, attended))
+    rests = [rest] + rests
+    rests = rests + [move(item, 0, 0, 1) for item in rests]
+    middle, activated, grad_middle, grad_attended, w_down, keep, send, first_grad = feed(
+        ids, tokens, attended, cotangent, small, first, rests, BF16
+    )
+
+    received = move(send, 0, 0, 1)
+    outputs = result(middle, activated, w_down, small)
+    received, outputs = lax.optimization_barrier((received, outputs))
+    rest_kept, *sends = add_core(keep, received)
+    *sends, grad_attended = lax.optimization_barrier((*sends, grad_attended))
+    rest_sums = [move(item, 0, d, 0) for item, d in zip(sends, STEPS)]
+    grad_project, keep, send = attend_back(
+        ids, project, weights, grad_attended, normed_turned, w_qkv, small, first_grad, BF16
+    )
+    rest_sums[0], keep = lax.optimization_barrier((rest_sums[0], keep))
+    first_kept, *sends = add_core(keep, move(send, 0, 0, 1))
+    first_sums = [move(item, 0, d, 0) for item, d in zip(sends, STEPS)]
+    input_grad = input_gradient(tokens, grad_project, grad_middle, w_qkv, small)
     kept, *sends = call(
-        add_core_kernel, "add_core", None, [first, first_in, rest, rest_in],
-        [like(*part)] + [like(*part, kind=BF16)] * (PLANE - 1), [pltpu.VMEM(part, F32)],
-    )
-    arrived = [move(item, 0, d + 1, 0) for d, item in enumerate(sends)]
-    kept, *sends = call(
-        add_plane_kernel, "add_plane", z.reshape(1), [kept] + arrived,
-        [like(SHARE, LANES)] + [like(SHARE, LANES, kind=BF16)] * (Z - 1), [pltpu.VMEM(part, F32)],
+        add_plane_kernel, "add_plane", where, [first_kept, rest_kept] + first_sums + rest_sums,
+        [like(SHARE, LANES)] + [like(SHARE, LANES, kind=BF16)] * (Z - 1),
+        [pltpu.VMEM((Z, SHARE, LANES), F32)],
     )
     arrived = [move(item, d + 1, 0, 0) for d, item in enumerate(sends)]
     param_grad = call(

time: 63.9 us -> 64.7 us (1.013)
  starting transfers between devices: 19.1 us -> 26.4 us
  waiting for transfers between devices: 19.2 us -> 14 us
  Pallas kernels: 20.8 us -> 19.1 us
    ppermute x18 -> x28, starting transfers between devices: 19.1 us -> 26.4 us  [move(): return lax.ppermute(values, 'fsdp', pairs)]
    ppermute x18 -> x28, waiting for transfers between devices: 19.2 us -> 14 us  [move(): return lax.ppermute(values, 'fsdp', pairs)]
    pallas_call x10 -> x11, Pallas kernels: 20.8 us -> 19.1 us  [call(): pl.pallas_call(kernel, in_specs=[SMEM_SPEC] * with_ids + [VMEM_SPEC] * le...]
    unnamed x16 -> x14, local copies, waits for them, and re-layouts: 3.62 us -> 3.99 us
  transfers between devices with their start and end apart: 18 -> 28, of which waited for: 10 -> 14; matrix products, arithmetic and copies ran while one was open for 0% -> 0% of each run, Pallas kernels for 12% -> 12%
where the time goes in v7:
time: 64.7 us; the launch traced here: 64.3 us
  starting transfers between devices  26.4 us (41%)
  Pallas kernels  19.1 us (30%)
  waiting for transfers between devices  14 us (22%)
  local copies, waits for them, and re-layouts  4.07 us (6%)
  between operations  0.75 us (1%)
    ppermute x28, starting transfers between devices, move(): return lax.ppermute(values, 'fsdp', pairs)  26.4 us
    pallas_call x11, Pallas kernels, call(): pl.pallas_call(kernel, in_specs=[SMEM_SPEC] * with_ids + [VMEM_SPEC] * le...  19.1 us
    ppermute x28, waiting for transfers between devices, move(): return lax.ppermute(values, 'fsdp', pairs)  14 us
    unnamed x14, local copies, waits for them, and re-layouts  3.99 us
  transfers between devices with their start and end apart: 28, of which 14 were waited for; matrix products, arithmetic and copies ran while one was open for 0% of the time, Pallas kernels for 12%

profile of v7, /device:TPU:0, one launch (start us, length us, event | category | flops | bytes accessed | tf_op | source)
XLA Modules:
  0.0 64.3 jit_solution(7300948290896552123)
XLA Ops:
  0.6 3.1 %collective-permute-start = (bf16[193,128]{1,0:T(8,128)(2,1)}, bf16[193,128]{1,0:T(8,128)(2,1)S(1)}, u32[]{:S(2)}, u32[]{:S(2)}) collective-permute-start(bf16[193,128]{1,0:T(8,128)(2,1)} %params.1), channel_id=1, source_target_pairs={{0,8},{1,9},{2,10},{3,11},{4,12},{5,13},{6,14},{7,15},{8,16},{9,17... | collective-permute-start | bytes 148232 | tf_op jit(solution)/shard_map/ppermute | solution.py:549
  3.7 2.1 %collective-permute-start.2 = (bf16[193,128]{1,0:T(8,128)(2,1)}, bf16[193,128]{1,0:T(8,128)(2,1)S(1)}, u32[]{:S(2)}, u32[]{:S(2)}) collective-permute-start(bf16[193,128]{1,0:T(8,128)(2,1)} %params.1), channel_id=1, source_target_pairs={{0,24},{1,25},{2,26},{3,27},{4,28},{5,29},{6,30},{7,31},{8,0},{9,1... | collective-permute-start | bytes 148232 | tf_op jit(solution)/shard_map/ppermute | solution.py:549
  5.8 0.9 %collective-permute-start.1 = (bf16[193,128]{1,0:T(8,128)(2,1)}, bf16[193,128]{1,0:T(8,128)(2,1)S(1)}, u32[]{:S(2)}, u32[]{:S(2)}) collective-permute-start(bf16[193,128]{1,0:T(8,128)(2,1)} %params.1), channel_id=1, source_target_pairs={{0,16},{1,17},{2,18},{3,19},{4,20},{5,21},{6,22},{7,23},{8,24},{9,... | collective-permute-start | bytes 148232 | tf_op jit(solution)/shard_map/ppermute | solution.py:549
  6.7 1.0 %copy-done = bf16[1024,256]{1,0:T(8,128)(2,1)S(1)} copy-done((bf16[1024,256]{1,0:T(8,128)(2,1)S(1)}, bf16[1024,256]{1,0:T(8,128)(2,1)}, u32[]{:S(2)}) %copy-start) | copy-done | bytes 524312
  7.8 0.8 %copy-done.5 = bf16[193,128]{1,0:T(8,128)(2,1)S(1)} copy-done((bf16[193,128]{1,0:T(8,128)(2,1)S(1)}, bf16[193,128]{1,0:T(8,128)(2,1)}, u32[]{:S(2)}) %copy-start.5) | copy-done | bytes 49432
  8.6 0.5 prepare.1
  9.1 2.1 %collective-permute-done.1.refs_2_ = bf16[193,128]{1,0:T(8,128)(2,1)S(1)} collective-permute-done((bf16[193,128]{1,0:T(8,128)(2,1)}, bf16[193,128]{1,0:T(8,128)(2,1)S(1)}, u32[]{:S(2)}, u32[]{:S(2)}) %collective-permute-start.1) | collective-permute-done | bytes 49440 | tf_op jit(solution)/shard_map/ppermute | solution.py:549
  11.3 1.6 %collective-permute-start.8 = (bf16[240,128]{1,0:T(8,128)(2,1)S(1)}, bf16[240,128]{1,0:T(8,128)(2,1)S(1)}, u32[]{:S(2)}, u32[]{:S(2)}) collective-permute-start(bf16[240,128]{1,0:T(8,128)(2,1)S(1)} %get-tuple-element.52.refs_0_), channel_id=1, source_target_pairs={{0,4},{1,5},{2,6},{3,7},{4,0},{5,1},{6,2},{7,3},{8,12},{9,13},{10,... | collective-permute-start | bytes 184328 | tf_op jit(solution)/shard_map/ppermute | solution.py:549
  12.9 1.5 %collective-permute-start.7 = (bf16[240,128]{1,0:T(8,128)(2,1)S(1)}, bf16[240,128]{1,0:T(8,128)(2,1)S(1)}, u32[]{:S(2)}, u32[]{:S(2)}) collective-permute-start(bf16[240,128]{1,0:T(8,128)(2,1)S(1)} %get-tuple-element.52.refs_0_), channel_id=1, source_target_pairs={{0,2},{1,3},{2,0},{3,1},{4,6},{5,7},{6,4},{7,5},{8,10},{9,11},{10,... | collective-permute-start | bytes 184328 | tf_op jit(solution)/shard_map/ppermute | solution.py:549
  14.4 0.5 collective-permute-start.6
  14.8 0.7 %collective-permute-done.8.refs_3_ = bf16[240,128]{1,0:T(8,128)(2,1)S(1)} collective-permute-done((bf16[240,128]{1,0:T(8,128)(2,1)S(1)}, bf16[240,128]{1,0:T(8,128)(2,1)S(1)}, u32[]{:S(2)}, u32[]{:S(2)}) %collective-permute-start.8) | collective-permute-done | bytes 61472 | tf_op jit(solution)/shard_map/ppermute | solution.py:549
  15.6 1.5 %collective-permute-start.5 = (bf16[3,193,128]{2,1,0:T(8,128)(2,1)S(1)}, bf16[3,193,128]{2,1,0:T(8,128)(2,1)S(1)}, u32[]{:S(2)}, u32[]{:S(2)}) collective-permute-start(bf16[3,193,128]{2,1,0:T(8,128)(2,1)S(1)} %get-tuple-element.50.refs_0_), channel_id=1, source_target_pairs={{0,4},{1,5},{2,6},{3,7},{4,0},{5,1},{6,2},{7,3},{8,12},{9,13},{10,... | collective-permute-start | bytes 444680 | tf_op jit(solution)/shard_map/ppermute | solution.py:549
  17.1 1.5 %collective-permute-start.4 = (bf16[3,193,128]{2,1,0:T(8,128)(2,1)S(1)}, bf16[3,193,128]{2,1,0:T(8,128)(2,1)S(1)}, u32[]{:S(2)}, u32[]{:S(2)}) collective-permute-start(bf16[3,193,128]{2,1,0:T(8,128)(2,1)S(1)} %get-tuple-element.50.refs_0_), channel_id=1, source_target_pairs={{0,2},{1,3},{2,0},{3,1},{4,6},{5,7},{6,4},{7,5},{8,10},{9,11},{10,... | collective-permute-start | bytes 444680 | tf_op jit(solution)/shard_map/ppermute | solution.py:549
  18.6 0.5 collective-permute-start.3
  19.1 0.5 collective-permute-done.6.refs_1_
  19.6 0.6 copy-done.3
  20.2 0.5 collective-permute-start.10
  21.1 0.6 collective-permute-done.10.refs_5_
  21.7 0.8 %copy-done.4 = bf16[240,128]{1,0:T(8,128)(2,1)S(1)} copy-done((bf16[240,128]{1,0:T(8,128)(2,1)S(1)}, bf16[240,128]{1,0:T(8,128)(2,1)}, u32[]{:S(2)}) %copy-start.4) | copy-done | bytes 61464
  22.5 0.7 %copy-done.6 = s32[1024]{0:T(1024)S(1)} copy-done((s32[1024]{0:T(1024)S(1)}, s32[1024]{0:T(1024)}, u32[]{:S(2)}) %copy-start.6) | copy-done | bytes 4120
  23.2 3.4 %attend.1 = (bf16[1024,768]{1,0:T(8,128)(2,1)S(1)}, bf16[1024,512]{1,0:T(8,128)(2,1)S(1)}, bf16[1024,256]{1,0:T(8,128)(2,1)S(1)}, bf16[256,768]{1,0:T(8,128)(2,1...) custom-call(s32[8]{0:T(128)S(1)} %stack.35.ids, s32[8,128]{1,0:T(8,128)S(1)} %bitcast.10, ...), custom_call_target="tpu_custom_call" | custom-call | flops 300000000 | bytes 1048576 | tf_op jit(solution)/shard_map/attend/pallas_call | solution.py:418
  26.6 0.4 collective-permute-start.14
  27.2 0.3 collective-permute-start.16
  27.6 0.5 collective-permute-done.14.refs_5_
  28.1 0.3 collective-permute-done.15.refs_6_
  28.4 0.2 collective-permute-done.16.refs_7_
  28.7 6.8 %feed.1 = (f32[1024,256]{1,0:T(8,128)S(1)}, bf16[1024,1024]{1,0:T(8,128)(2,1)S(1)}, f32[1024,256]{1,0:T(8,128)S(1)}, bf16[1024,256]{1,0:T(8,128)(2,1)S(1)}, bf16...) custom-call(s32[8]{0:T(128)S(1)} %stack.35.ids, ...), custom_call_target="tpu_custom_call" | custom-call | flops 400000000 | bytes 1048576 | tf_op jit(solution)/shard_map/feed/pallas_call | solution.py:418
  35.5 0.4 collective-permute-start.17
  35.9 1.5 %result.1 = bf16[1024,256]{1,0:T(8,128)(2,1)} custom-call(f32[1024,256]{1,0:T(8,128)S(1)} %get-tuple-element.61.middle, bf16[1024,1024]{1,0:T(8,128)(2,1)S(1)} %get-tuple-element.62.activated, bf16[1024,256]{1,0:T(8,128)(2,1)S(1)} %get-tuple-element.63.w_down, f32[32,128]{1,0:T(8,128)S(1)} %get-tuple-element.55.small), custom_call_target="tpu_custom_call" | custom-call | flops 100000000 | bytes 1048576 | tf_op jit(solution)/shard_map/result/pallas_call | solution.py:418
  37.4 0.2 collective-permute-done.17.received
  37.7 3.8 %attend_back.1 = (bf16[1024,768]{1,0:T(8,128)(2,1)S(1)}, f32[4,224,128]{2,1,0:T(8,128)S(1)}, bf16[4,224,128]{2,1,0:T(8,128)(2,1)S(1)}) custom-call(s32[8]{0:T(128)S(1)} %stack.35.ids, bf16[1024,768]{1,0:T(8,128)(2,1)S(1)} %get-tuple-element.65.project, bf16[1024,512]{1,0:T(8,128)(2,1)S(1)} %get-tuple-element.66.weights, ...), custom_call_target="tpu_custom_call" | custom-call | flops 250000000 | bytes 1048576 | tf_op jit(solution)/shard_map/attend_back/pallas_call | solution.py:418
  41.5 0.4 collective-permute-start.19
  41.8 2.1 %collective-permute-start.18 = (bf16[3,193,128]{2,1,0:T(8,128)(2,1)S(1)}, bf16[3,193,128]{2,1,0:T(8,128)(2,1)S(1)}, u32[]{:S(2)}, u32[]{:S(2)}) collective-permute-start(bf16[3,193,128]{2,1,0:T(8,128)(2,1)S(1)} %get-tuple-element.79), channel_id=1, source_target_pairs={{0,6},{1,7},{2,4},{3,5},{4,2},{5,3},{6,0},{7,1},{8,14},{9,15},{10,... | collective-permute-start | bytes 444680 | tf_op jit(solution)/shard_map/ppermute | solution.py:549
  43.9 0.5 collective-permute-start.23
  44.4 0.9 %collective-permute-start.24 = (bf16[3,193,128]{2,1,0:T(8,128)(2,1)S(1)}, bf16[3,193,128]{2,1,0:T(8,128)(2,1)S(1)}, u32[]{:S(2)}, u32[]{:S(2)}) collective-permute-start(bf16[3,193,128]{2,1,0:T(8,128)(2,1)S(1)} %get-tuple-element.90), channel_id=1, source_target_pairs={{0,4},{1,5},{2,6},{3,7},{4,0},{5,1},{6,2},{7,3},{8,12},{9,13},{10,... | collective-permute-start | bytes 444680 | tf_op jit(solution)/shard_map/ppermute | solution.py:549
  45.3 4.2 %collective-permute-done.18.refs_3_ = bf16[3,193,128]{2,1,0:T(8,128)(2,1)S(1)} collective-permute-done((bf16[3,193,128]{2,1,0:T(8,128)(2,1)S(1)}, bf16[3,193,128]{2,1,0:T(8,128)(2,1)S(1)}, u32[]{:S(2)}, u32[]{:S(2)}) %collective-permute-start.18) | collective-permute-done | bytes 148256 | tf_op jit(solution)/shard_map/ppermute | solution.py:549
  49.6 2.2 %collective-permute-start.20 = (bf16[1,224,128]{2,1,0:T(8,128)(2,1)S(1)}, bf16[1,224,128]{2,1,0:T(8,128)(2,1)S(1)}, u32[]{:S(2)}, u32[]{:S(2)}) collective-permute-start(bf16[1,224,128]{2,1,0:T(8,128)(2,1)S(1)} %get-tuple-element.85), channel_id=1, source_target_pairs={{0,6},{1,7},{2,4},{3,5},{4,2},{5,3},{6,0},{7,1},{8,14},{9,15},{10,... | collective-permute-start | bytes 172040 | tf_op jit(solution)/shard_map/ppermute | solution.py:549
  51.8 0.5 collective-permute-start.21
  52.3 0.9 %collective-permute-start.22 = (bf16[1,224,128]{2,1,0:T(8,128)(2,1)S(1)}, bf16[1,224,128]{2,1,0:T(8,128)(2,1)S(1)}, u32[]{:S(2)}, u32[]{:S(2)}) collective-permute-start(bf16[1,224,128]{2,1,0:T(8,128)(2,1)S(1)} %get-tuple-element.87), channel_id=1, source_target_pairs={{0,4},{1,5},{2,6},{3,7},{4,0},{5,1},{6,2},{7,3},{8,12},{9,13},{10,... | collective-permute-start | bytes 172040 | tf_op jit(solution)/shard_map/ppermute | solution.py:549
  53.2 1.6 %collective-permute-done.20.refs_0_ = bf16[1,224,128]{2,1,0:T(8,128)(2,1)S(1)} collective-permute-done((bf16[1,224,128]{2,1,0:T(8,128)(2,1)S(1)}, bf16[1,224,128]{2,1,0:T(8,128)(2,1)S(1)}, u32[]{:S(2)}, u32[]{:S(2)}) %collective-permute-start.20) | collective-permute-done | bytes 57376 | tf_op jit(solution)/shard_map/ppermute | solution.py:549
  54.8 1.2 %collective-permute-done.21.refs_1_ = bf16[1,224,128]{2,1,0:T(8,128)(2,1)S(1)} collective-permute-done((bf16[1,224,128]{2,1,0:T(8,128)(2,1)S(1)}, bf16[1,224,128]{2,1,0:T(8,128)(2,1)S(1)}, u32[]{:S(2)}, u32[]{:S(2)}) %collective-permute-start.21) | collective-permute-done | bytes 57376 | tf_op jit(solution)/shard_map/ppermute | solution.py:549
  56.0 0.5 collective-permute-done.22.refs_2_
  56.5 0.2 add_plane.1
  56.7 2.8 %collective-permute-start.26 = (bf16[193,128]{1,0:T(8,128)(2,1)S(1)}, bf16[193,128]{1,0:T(8,128)(2,1)S(1)}, u32[]{:S(2)}, u32[]{:S(2)}) collective-permute-start(bf16[193,128]{1,0:T(8,128)(2,1)S(1)} %get-tuple-element.93), channel_id=1, source_target_pairs={{0,16},{1,17},{2,18},{3,19},{4,20},{5,21},{6,22},{7,23},{8,24},{9,... | collective-permute-start | bytes 148232 | tf_op jit(solution)/shard_map/ppermute | solution.py:549
  59.6 1.0 %collective-permute-start.27 = (bf16[193,128]{1,0:T(8,128)(2,1)S(1)}, bf16[193,128]{1,0:T(8,128)(2,1)S(1)}, u32[]{:S(2)}, u32[]{:S(2)}) collective-permute-start(bf16[193,128]{1,0:T(8,128)(2,1)S(1)} %get-tuple-element.94), channel_id=1, source_target_pairs={{0,24},{1,25},{2,26},{3,27},{4,28},{5,29},{6,30},{7,31},{8,0},{9,1... | collective-permute-start | bytes 148232 | tf_op jit(solution)/shard_map/ppermute | solution.py:549
  60.5 2.1 %input_grad.1 = f32[1024,256]{1,0:T(8,128)} custom-call(bf16[1024,256]{1,0:T(8,128)(2,1)S(1)} %copy-done.1, bf16[1024,768]{1,0:T(8,128)(2,1)S(1)} %get-tuple-element.77.grad_project, f32[1024,256]{1,0:T(8,128)S(1)} %get-tuple-element.78.grad_middle, bf16[256,768]{1,0:T(8,128)(2,1)S(1)} %get-tuple-element.75.w_qkv, f32[32,128]{1,0:T(8,128)S(1)} %get-tuple-element.55.small), custom_call_target="tpu_custom_call" | custom-call | flops 100000000 | bytes 1048576 | tf_op jit(solution)/shard_map/input_grad/pallas_call | solution.py:418
  62.6 1.0 %collective-permute-done.27.refs_2_ = bf16[193,128]{1,0:T(8,128)(2,1)S(1)} collective-permute-done((bf16[193,128]{1,0:T(8,128)(2,1)S(1)}, bf16[193,128]{1,0:T(8,128)(2,1)S(1)}, u32[]{:S(2)}, u32[]{:S(2)}) %collective-permute-start.27) | collective-permute-done | bytes 49440 | tf_op jit(solution)/shard_map/ppermute | solution.py:549
  63.7 0.7 %add_column.1 = f32[193,128]{1,0:T(8,128)} custom-call(f32[193,128]{1,0:T(8,128)S(1)} %get-tuple-element.91.kept, bf16[193,128]{1,0:T(8,128)(2,1)S(1)} %collective-permute-done.25.refs_0_, bf16[193,128]{1,0:T(8,128)(2,1)S(1)} %collective-permute-done.26.refs_1_, bf16[193,128]{1,0:T(8,128)(2,1)S(1)} %collective-permute-done.27.refs_2_), custom_call_target="tpu_custom_call" | custom-call | flops 50000000 | bytes 1048576 | tf_op jit(solution)/shard_map/add_column/pallas_call | solution.py:418
  (34 shorter events, 0.9 us)
Async XLA Ops:
  0.6 8.5 %collective-permute-start = (bf16[193,128]{1,0:T(8,128)(2,1)}, bf16[193,128]{1,0:T(8,128)(2,1)S(1)}, u32[]{:S(2)}, u32[]{:S(2)}) collective-permute-start(bf16[193,128]{1,0:T(8,128)(2,1)} %params.1), channel_id=1, source_target_pairs={{0,8},{1,9},{2,10},{3,11},{4,12},{5,13},{6,14},{7,15},{8,16},{9,17... | collective-permute-start | bytes 148232 | tf_op jit(solution)/shard_map/ppermute | solution.py:549
  3.7 5.4 %collective-permute-start.2 = (bf16[193,128]{1,0:T(8,128)(2,1)}, bf16[193,128]{1,0:T(8,128)(2,1)S(1)}, u32[]{:S(2)}, u32[]{:S(2)}) collective-permute-start(bf16[193,128]{1,0:T(8,128)(2,1)} %params.1), channel_id=1, source_target_pairs={{0,24},{1,25},{2,26},{3,27},{4,28},{5,29},{6,30},{7,31},{8,0},{9,1... | collective-permute-start | bytes 148232 | tf_op jit(solution)/shard_map/ppermute | solution.py:549
  5.8 5.4 %collective-permute-start.1 = (bf16[193,128]{1,0:T(8,128)(2,1)}, bf16[193,128]{1,0:T(8,128)(2,1)S(1)}, u32[]{:S(2)}, u32[]{:S(2)}) collective-permute-start(bf16[193,128]{1,0:T(8,128)(2,1)} %params.1), channel_id=1, source_target_pairs={{0,16},{1,17},{2,18},{3,19},{4,20},{5,21},{6,22},{7,23},{8,24},{9,... | collective-permute-start | bytes 148232 | tf_op jit(solution)/shard_map/ppermute | solution.py:549
  6.7 1.0 %copy-start = (bf16[1024,256]{1,0:T(8,128)(2,1)S(1)}, bf16[1024,256]{1,0:T(8,128)(2,1)}, u32[]{:S(2)}) copy-start(bf16[1024,256]{1,0:T(8,128)(2,1)} %tok.5) | copy-start | bytes 1572868
  7.8 0.8 %copy-start.5 = (bf16[193,128]{1,0:T(8,128)(2,1)S(1)}, bf16[193,128]{1,0:T(8,128)(2,1)}, u32[]{:S(2)}) copy-start(bf16[193,128]{1,0:T(8,128)(2,1)} %params.1) | copy-start | bytes 148228
  8.6 20.1 %copy-start.1 = (bf16[1024,256]{1,0:T(8,128)(2,1)S(1)}, bf16[1024,256]{1,0:T(8,128)(2,1)}, u32[]{:S(2)}) copy-start(bf16[1024,256]{1,0:T(8,128)(2,1)} %tok.5) | copy-start | bytes 1572868
  8.6 20.1 %copy-start.2 = (bf16[1024,256]{1,0:T(8,128)(2,1)S(1)}, bf16[1024,256]{1,0:T(8,128)(2,1)}, u32[]{:S(2)}) copy-start(bf16[1024,256]{1,0:T(8,128)(2,1)} %cot.1) | copy-start | bytes 1572868
  11.3 4.3 %collective-permute-start.8 = (bf16[240,128]{1,0:T(8,128)(2,1)S(1)}, bf16[240,128]{1,0:T(8,128)(2,1)S(1)}, u32[]{:S(2)}, u32[]{:S(2)}) collective-permute-start(bf16[240,128]{1,0:T(8,128)(2,1)S(1)} %get-tuple-element.52.refs_0_), channel_id=1, source_target_pairs={{0,4},{1,5},{2,6},{3,7},{4,0},{5,1},{6,2},{7,3},{8,12},{9,13},{10,... | collective-permute-start | bytes 184328 | tf_op jit(solution)/shard_map/ppermute | solution.py:549
  12.9 4.2 %collective-permute-start.9 = (bf16[240,128]{1,0:T(8,128)(2,1)S(1)}, bf16[240,128]{1,0:T(8,128)(2,1)S(1)}, u32[]{:S(2)}, u32[]{:S(2)}) collective-permute-start(bf16[240,128]{1,0:T(8,128)(2,1)S(1)} %get-tuple-element.52.refs_0_), channel_id=1, source_target_pairs={{0,1},{1,0},{2,3},{3,2},{4,5},{5,4},{6,7},{7,6},{8,9},{9,8},{10,11... | collective-permute-start | bytes 184328 | tf_op jit(solution)/shard_map/ppermute | solution.py:549
  12.9 5.7 %collective-permute-start.7 = (bf16[240,128]{1,0:T(8,128)(2,1)S(1)}, bf16[240,128]{1,0:T(8,128)(2,1)S(1)}, u32[]{:S(2)}, u32[]{:S(2)}) collective-permute-start(bf16[240,128]{1,0:T(8,128)(2,1)S(1)} %get-tuple-element.52.refs_0_), channel_id=1, source_target_pairs={{0,2},{1,3},{2,0},{3,1},{4,6},{5,7},{6,4},{7,5},{8,10},{9,11},{10,... | collective-permute-start | bytes 184328 | tf_op jit(solution)/shard_map/ppermute | solution.py:549
  14.4 5.2 %collective-permute-start.6 = (bf16[240,128]{1,0:T(8,128)(2,1)S(1)}, bf16[240,128]{1,0:T(8,128)(2,1)S(1)}, u32[]{:S(2)}, u32[]{:S(2)}) collective-permute-start(bf16[240,128]{1,0:T(8,128)(2,1)S(1)} %get-tuple-element.52.refs_0_), channel_id=1, source_target_pairs={{0,6},{1,7},{2,4},{3,5},{4,2},{5,3},{6,0},{7,1},{8,14},{9,15},{10,... | collective-permute-start | bytes 184328 | tf_op jit(solution)/shard_map/ppermute | solution.py:549
  15.6 4.0 %collective-permute-start.12 = (bf16[240,128]{1,0:T(8,128)(2,1)S(1)}, bf16[240,128]{1,0:T(8,128)(2,1)S(1)}, u32[]{:S(2)}, u32[]{:S(2)}) collective-permute-start(bf16[240,128]{1,0:T(8,128)(2,1)S(1)} %collective-permute-done.8.refs_3_), channel_id=1, source_target_pairs={{0,1},{1,0},{2,3},{3,2},{4,5},{5,4},{6,7},{7,6},{8,9},{9,8},{10,11... | collective-permute-start | bytes 184328 | tf_op jit(solution)/shard_map/ppermute | solution.py:549
  15.6 11.0 %collective-permute-start.5 = (bf16[3,193,128]{2,1,0:T(8,128)(2,1)S(1)}, bf16[3,193,128]{2,1,0:T(8,128)(2,1)S(1)}, u32[]{:S(2)}, u32[]{:S(2)}) collective-permute-start(bf16[3,193,128]{2,1,0:T(8,128)(2,1)S(1)} %get-tuple-element.50.refs_0_), channel_id=1, source_target_pairs={{0,4},{1,5},{2,6},{3,7},{4,0},{5,1},{6,2},{7,3},{8,12},{9,13},{10,... | collective-permute-start | bytes 444680 | tf_op jit(solution)/shard_map/ppermute | solution.py:549
  17.1 9.5 %collective-permute-start.4 = (bf16[3,193,128]{2,1,0:T(8,128)(2,1)S(1)}, bf16[3,193,128]{2,1,0:T(8,128)(2,1)S(1)}, u32[]{:S(2)}, u32[]{:S(2)}) collective-permute-start(bf16[3,193,128]{2,1,0:T(8,128)(2,1)S(1)} %get-tuple-element.50.refs_0_), channel_id=1, source_target_pairs={{0,2},{1,3},{2,0},{3,1},{4,6},{5,7},{6,4},{7,5},{8,10},{9,11},{10,... | collective-permute-start | bytes 444680 | tf_op jit(solution)/shard_map/ppermute | solution.py:549
  18.6 8.0 %collective-permute-start.3 = (bf16[3,193,128]{2,1,0:T(8,128)(2,1)S(1)}, bf16[3,193,128]{2,1,0:T(8,128)(2,1)S(1)}, u32[]{:S(2)}, u32[]{:S(2)}) collective-permute-start(bf16[3,193,128]{2,1,0:T(8,128)(2,1)S(1)} %get-tuple-element.50.refs_0_), channel_id=1, source_target_pairs={{0,6},{1,7},{2,4},{3,5},{4,2},{5,3},{6,0},{7,1},{8,14},{9,15},{10,... | collective-permute-start | bytes 444680 | tf_op jit(solution)/shard_map/ppermute | solution.py:549
  19.5 1.4 %collective-permute-start.11 = (bf16[240,128]{1,0:T(8,128)(2,1)S(1)}, bf16[240,128]{1,0:T(8,128)(2,1)}, u32[]{:S(2)}, u32[]{:S(2)}) collective-permute-start(bf16[240,128]{1,0:T(8,128)(2,1)S(1)} %collective-permute-done.7.refs_2_), channel_id=1, source_target_pairs={{0,1},{1,0},{2,3},{3,2},{4,5},{5,4},{6,7},{7,6},{8,9},{9,8},{10,11... | collective-permute-start | bytes 184328 | tf_op jit(solution)/shard_map/ppermute | solution.py:549
  19.6 0.6 copy-start.3
  20.2 1.5 %collective-permute-start.10 = (bf16[240,128]{1,0:T(8,128)(2,1)S(1)}, bf16[240,128]{1,0:T(8,128)(2,1)}, u32[]{:S(2)}, u32[]{:S(2)}) collective-permute-start(bf16[240,128]{1,0:T(8,128)(2,1)S(1)} %collective-permute-done.6.refs_1_), channel_id=1, source_target_pairs={{0,1},{1,0},{2,3},{3,2},{4,5},{5,4},{6,7},{7,6},{8,9},{9,8},{10,11... | collective-permute-start | bytes 184328 | tf_op jit(solution)/shard_map/ppermute | solution.py:549
  20.9 6.6 %collective-permute-start.13 = (bf16[3,193,128]{2,1,0:T(8,128)(2,1)S(1)}, bf16[3,193,128]{2,1,0:T(8,128)(2,1)S(1)}, u32[]{:S(2)}, u32[]{:S(2)}) collective-permute-start(bf16[3,193,128]{2,1,0:T(8,128)(2,1)S(1)} %get-tuple-element.50.refs_0_), channel_id=1, source_target_pairs={{0,1},{1,0},{2,3},{3,2},{4,5},{5,4},{6,7},{7,6},{8,9},{9,8},{10,11... | collective-permute-start | bytes 444680 | tf_op jit(solution)/shard_map/ppermute | solution.py:549
  21.7 0.8 %copy-start.4 = (bf16[240,128]{1,0:T(8,128)(2,1)S(1)}, bf16[240,128]{1,0:T(8,128)(2,1)}, u32[]{:S(2)}) copy-start(bf16[240,128]{1,0:T(8,128)(2,1)} %copy-done.3) | copy-start | bytes 184324
  22.5 0.7 %copy-start.6 = (s32[1024]{0:T(1024)S(1)}, s32[1024]{0:T(1024)}, u32[]{:S(2)}) copy-start(s32[1024]{0:T(1024)} %param.6) | copy-start | bytes 12292
  26.6 1.4 %collective-permute-start.14 = (bf16[3,193,128]{2,1,0:T(8,128)(2,1)S(1)}, bf16[3,193,128]{2,1,0:T(8,128)(2,1)S(1)}, u32[]{:S(2)}, u32[]{:S(2)}) collective-permute-start(bf16[3,193,128]{2,1,0:T(8,128)(2,1)S(1)} %collective-permute-done.3.refs_1_), channel_id=1, source_target_pairs={{0,1},{1,0},{2,3},{3,2},{4,5},{5,4},{6,7},{7,6},{8,9},{9,8},{10,11... | collective-permute-start | bytes 444680 | tf_op jit(solution)/shard_map/ppermute | solution.py:549
  27.0 1.4 %collective-permute-start.15 = (bf16[3,193,128]{2,1,0:T(8,128)(2,1)S(1)}, bf16[3,193,128]{2,1,0:T(8,128)(2,1)S(1)}, u32[]{:S(2)}, u32[]{:S(2)}) collective-permute-start(bf16[3,193,128]{2,1,0:T(8,128)(2,1)S(1)} %collective-permute-done.4.refs_2_), channel_id=1, source_target_pairs={{0,1},{1,0},{2,3},{3,2},{4,5},{5,4},{6,7},{7,6},{8,9},{9,8},{10,11... | collective-permute-start | bytes 444680 | tf_op jit(solution)/shard_map/ppermute | solution.py:549
  27.2 1.4 %collective-permute-start.16 = (bf16[3,193,128]{2,1,0:T(8,128)(2,1)S(1)}, bf16[3,193,128]{2,1,0:T(8,128)(2,1)S(1)}, u32[]{:S(2)}, u32[]{:S(2)}) collective-permute-start(bf16[3,193,128]{2,1,0:T(8,128)(2,1)S(1)} %collective-permute-done.5.refs_3_), channel_id=1, source_target_pairs={{0,1},{1,0},{2,3},{3,2},{4,5},{5,4},{6,7},{7,6},{8,9},{9,8},{10,11... | collective-permute-start | bytes 444680 | tf_op jit(solution)/shard_map/ppermute | solution.py:549
  35.5 2.1 %collective-permute-start.17 = (bf16[12,193,128]{2,1,0:T(8,128)(2,1)S(1)}, bf16[12,193,128]{2,1,0:T(8,128)(2,1)S(1)}, u32[]{:S(2)}, u32[]{:S(2)}) collective-permute-start(bf16[12,193,128]{2,1,0:T(8,128)(2,1)S(1)} %get-tuple-element.60), channel_id=1, source_target_pairs={{0,1},{1,0},{2,3},{3,2},{4,5},{5,4},{6,7},{7,6},{8,9},{9,8},{10,11... | collective-permute-start | bytes 1778696 | tf_op jit(solution)/shard_map/ppermute | solution.py:549
  41.5 8.1 %collective-permute-start.19 = (bf16[4,224,128]{2,1,0:T(8,128)(2,1)S(1)}, bf16[4,224,128]{2,1,0:T(8,128)(2,1)S(1)}, u32[]{:S(2)}, u32[]{:S(2)}) collective-permute-start(bf16[4,224,128]{2,1,0:T(8,128)(2,1)S(1)} %get-tuple-element.82), channel_id=1, source_target_pairs={{0,1},{1,0},{2,3},{3,2},{4,5},{5,4},{6,7},{7,6},{8,9},{9,8},{10,11... | collective-permute-start | bytes 688136 | tf_op jit(solution)/shard_map/ppermute | solution.py:549
  41.8 7.7 %collective-permute-start.18 = (bf16[3,193,128]{2,1,0:T(8,128)(2,1)S(1)}, bf16[3,193,128]{2,1,0:T(8,128)(2,1)S(1)}, u32[]{:S(2)}, u32[]{:S(2)}) collective-permute-start(bf16[3,193,128]{2,1,0:T(8,128)(2,1)S(1)} %get-tuple-element.79), channel_id=1, source_target_pairs={{0,6},{1,7},{2,4},{3,5},{4,2},{5,3},{6,0},{7,1},{8,14},{9,15},{10,... | collective-permute-start | bytes 444680 | tf_op jit(solution)/shard_map/ppermute | solution.py:549
  43.9 9.3 %collective-permute-start.23 = (bf16[3,193,128]{2,1,0:T(8,128)(2,1)S(1)}, bf16[3,193,128]{2,1,0:T(8,128)(2,1)S(1)}, u32[]{:S(2)}, u32[]{:S(2)}) collective-permute-start(bf16[3,193,128]{2,1,0:T(8,128)(2,1)S(1)} %get-tuple-element.89), channel_id=1, source_target_pairs={{0,2},{1,3},{2,0},{3,1},{4,6},{5,7},{6,4},{7,5},{8,10},{9,11},{10,... | collective-permute-start | bytes 444680 | tf_op jit(solution)/shard_map/ppermute | solution.py:549
  44.4 8.7 %collective-permute-start.24 = (bf16[3,193,128]{2,1,0:T(8,128)(2,1)S(1)}, bf16[3,193,128]{2,1,0:T(8,128)(2,1)S(1)}, u32[]{:S(2)}, u32[]{:S(2)}) collective-permute-start(bf16[3,193,128]{2,1,0:T(8,128)(2,1)S(1)} %get-tuple-element.90), channel_id=1, source_target_pairs={{0,4},{1,5},{2,6},{3,7},{4,0},{5,1},{6,2},{7,3},{8,12},{9,13},{10,... | collective-permute-start | bytes 444680 | tf_op jit(solution)/shard_map/ppermute | solution.py:549
  49.6 5.1 %collective-permute-start.20 = (bf16[1,224,128]{2,1,0:T(8,128)(2,1)S(1)}, bf16[1,224,128]{2,1,0:T(8,128)(2,1)S(1)}, u32[]{:S(2)}, u32[]{:S(2)}) collective-permute-start(bf16[1,224,128]{2,1,0:T(8,128)(2,1)S(1)} %get-tuple-element.85), channel_id=1, source_target_pairs={{0,6},{1,7},{2,4},{3,5},{4,2},{5,3},{6,0},{7,1},{8,14},{9,15},{10,... | collective-permute-start | bytes 172040 | tf_op jit(solution)/shard_map/ppermute | solution.py:549
  51.8 4.2 %collective-permute-start.21 = (bf16[1,224,128]{2,1,0:T(8,128)(2,1)S(1)}, bf16[1,224,128]{2,1,0:T(8,128)(2,1)S(1)}, u32[]{:S(2)}, u32[]{:S(2)}) collective-permute-start(bf16[1,224,128]{2,1,0:T(8,128)(2,1)S(1)} %get-tuple-element.86), channel_id=1, source_target_pairs={{0,2},{1,3},{2,0},{3,1},{4,6},{5,7},{6,4},{7,5},{8,10},{9,11},{10,... | collective-permute-start | bytes 172040 | tf_op jit(solution)/shard_map/ppermute | solution.py:549
  52.3 4.2 %collective-permute-start.22 = (bf16[1,224,128]{2,1,0:T(8,128)(2,1)S(1)}, bf16[1,224,128]{2,1,0:T(8,128)(2,1)S(1)}, u32[]{:S(2)}, u32[]{:S(2)}) collective-permute-start(bf16[1,224,128]{2,1,0:T(8,128)(2,1)S(1)} %get-tuple-element.87), channel_id=1, source_target_pairs={{0,4},{1,5},{2,6},{3,7},{4,0},{5,1},{6,2},{7,3},{8,12},{9,13},{10,... | collective-permute-start | bytes 172040 | tf_op jit(solution)/shard_map/ppermute | solution.py:549
  56.7 6.0 %collective-permute-start.25 = (bf16[193,128]{1,0:T(8,128)(2,1)S(1)}, bf16[193,128]{1,0:T(8,128)(2,1)S(1)}, u32[]{:S(2)}, u32[]{:S(2)}) collective-permute-start(bf16[193,128]{1,0:T(8,128)(2,1)S(1)} %get-tuple-element.92), channel_id=1, source_target_pairs={{0,8},{1,9},{2,10},{3,11},{4,12},{5,13},{6,14},{7,15},{8,16},{9,17... | collective-permute-start | bytes 148232 | tf_op jit(solution)/shard_map/ppermute | solution.py:549
  56.7 5.9 %collective-permute-start.26 = (bf16[193,128]{1,0:T(8,128)(2,1)S(1)}, bf16[193,128]{1,0:T(8,128)(2,1)S(1)}, u32[]{:S(2)}, u32[]{:S(2)}) collective-permute-start(bf16[193,128]{1,0:T(8,128)(2,1)S(1)} %get-tuple-element.93), channel_id=1, source_target_pairs={{0,16},{1,17},{2,18},{3,19},{4,20},{5,21},{6,22},{7,23},{8,24},{9,... | collective-permute-start | bytes 148232 | tf_op jit(solution)/shard_map/ppermute | solution.py:549
  59.6 4.1 %collective-permute-start.27 = (bf16[193,128]{1,0:T(8,128)(2,1)S(1)}, bf16[193,128]{1,0:T(8,128)(2,1)S(1)}, u32[]{:S(2)}, u32[]{:S(2)}) collective-permute-start(bf16[193,128]{1,0:T(8,128)(2,1)S(1)} %get-tuple-element.94), channel_id=1, source_target_pairs={{0,24},{1,25},{2,26},{3,27},{4,28},{5,29},{6,30},{7,31},{8,0},{9,1... | collective-permute-start | bytes 148232 | tf_op jit(solution)/shard_map/ppermute | solution.py:549

commit v8 on v7

--- a/solution.py
+++ b/solution.py
@@ -109,11 +109,17 @@
         flat[pl.ds(start + j, rows, stride=per_row), :] = matrix[:, j * LANES : (j + 1) * LANES]
 
 
-def prepare_kernel(tok, params, normed_out, normed_turned, own):
+def prepare_kernel(tok, params, seg, normed_out, normed_turned, own, allowed):
     normed, _ = normalize(tok[...].astype(F32))
     normed_out[...] = normed
     normed_turned[...] = normed.astype(BF16).T
     own[...] = params[...]
+    causal = lax.broadcasted_iota(jnp.int32, (SEQ, SEQ), 1) <= lax.broadcasted_iota(
+        jnp.int32, (SEQ, SEQ), 0
+    )
+    for s in range(seg.shape[0]):
+        across = jnp.broadcast_to(seg[s : s + 1, :].astype(F32), (SEQ, SEQ))
+        allowed[s * SEQ : (s + 1) * SEQ, :] = (causal & (across == across.T)).astype(F32)
 
 
 def sort_kernel(ids, *refs):
@@ -128,9 +134,9 @@
     first[...] = wide[...].astype(BF16)
 
 
-def attend_kernel(ids, seg, normed, *refs):
-    bufs = refs[: 2 * PLANE]
-    project_out, weights_out, attended_out, w_qkv, small, first_out, flat = refs[2 * PLANE :]
+def attend_kernel(ids, allowed, normed, *refs):
+    bufs = [ref.at[p] for ref in refs[:2] for p in range(PLANE)]
+    project_out, weights_out, attended_out, w_qkv, small, first_out, flat = refs[2:]
     for slot, buf in enumerate(bufs):
         wide = buf[...].astype(F32)
         flat[pl.ds(ids[slot] * SHARE, SHARE), :] = wide[:SHARE, :]
@@ -152,20 +158,14 @@
         ],
         axis=1,
     )
-    causal = lax.broadcasted_iota(jnp.int32, (SEQ, SEQ), 1) <= lax.broadcasted_iota(
-        jnp.int32, (SEQ, SEQ), 0
-    )
-
     def some(g, carry):
         span = pl.ds(pl.multiple_of(g * WIDE, WIDE), WIDE)
         normed_low = (normed[span, :] * gain + shift).astype(BF16)
         project = (dot(normed_low, w_qkv[...]) + bias).astype(BF16)
         project_out[span, :] = project
-        scores, values, allowed = [], [], []
+        scores, values = [], []
         for s in range(GROUP):
             rows = slice(s * SEQ, (s + 1) * SEQ)
-            across = jnp.broadcast_to(seg[pl.ds(g * GROUP + s, 1), :].astype(F32), (SEQ, SEQ))
-            allowed.append(causal & (across == across.T))
             scores.append(
                 dot_nt(project[rows, :D] * SCALE, spread_heads(project[rows, D : 2 * D]))
             )
@@ -173,8 +173,9 @@
         weights = []
         for s in range(GROUP):
             low = []
+            open_pairs = allowed[pl.ds(pl.multiple_of(g * WIDE + s * SEQ, SEQ), SEQ), :] > 0.5
             for h in range(HEADS):
-                mine = jnp.where(allowed[s], scores[s][:, h * SEQ : (h + 1) * SEQ], -1e30)
+                mine = jnp.where(open_pairs, scores[s][:, h * SEQ : (h + 1) * SEQ], -1e30)
                 grown = jnp.exp(mine - jnp.max(mine, axis=-1, keepdims=True))
                 low.append(
                     (grown * (1.0 / jnp.sum(grown, axis=-1, keepdims=True))).astype(BF16)
@@ -192,11 +193,14 @@
 def feed_kernel(
     ids, tok, attended, cot, small, first_in, *refs,
 ):
-    bufs = refs[: 2 * PLANE]
+    bufs = []
+    for own, others in (refs[0:2], refs[2:4]):
+        bufs.append(own)
+        bufs += [others.at[pl.ds(p * (Z - 1), Z - 1)] for p in range(PLANE - 1)]
     (
         middle_out, activated_out, grad_middle_out, grad_attended_out, w_down, keep_out, send_out, first_out,
         w_out, w_up, grad_hidden, flat,
-    ) = refs[2 * PLANE :]
+    ) = refs[4:]
     flat[:HEAD_ROWS, :] = first_in[...]
     for slot, buf in enumerate(bufs):
         for z in range(1, Z):
@@ -297,10 +301,7 @@
     result_out[...] = result.astype(BF16)
 
 
-def attend_back_kernel(
-    ids, project, weights, grad_attended, normed_turned, w_qkv, small, first_in,
-    grad_project, keep_out, send_out, flat, wide,
-):
+def attend_back_kernel(project, weights, grad_attended, grad_project):
     def some(g, carry):
         base = g * WIDE
         spans = [pl.ds(pl.multiple_of(base + s * SEQ, SEQ), SEQ) for s in range(GROUP)]
@@ -332,6 +333,11 @@
         return carry
 
     lax.fori_loop(0, project.shape[0] // WIDE, some, 0)
+
+
+def project_back_kernel(
+    ids, grad_project, normed_turned, w_qkv, small, first_in, keep_out, send_out, flat, wide
+):
     products = dot(normed_turned[...], grad_project[...])
     sums = jnp.sum(fold_rows(grad_project[...].astype(F32)), axis=0, keepdims=True)
     gain = jnp.broadcast_to(small_vector(small, GAIN_ONE, 2), (LANES, D)).T
@@ -378,6 +384,13 @@
     lax.fori_loop(0, tok.shape[0] // WIDE, some, 0)
 
 
+def stack_kernel(*refs):
+    row = 0
+    for ref in refs[:-1]:
+        refs[-1][row : row + ref.shape[0]] = ref[...]
+        row += ref.shape[0]
+
+
 def add_core_kernel(kept, received, keep_out, *sends):
     part = kept.shape[0] // PLANE
     for p, out in enumerate((keep_out, *sends)):
@@ -410,7 +423,7 @@
 VMEM_SPEC = pl.BlockSpec(memory_space=pltpu.VMEM)
 
 def cost(us):
-    return pl.CostEstimate(flops=int(us * 5e7), bytes_accessed=1 << 20, transcendentals=0)
+    return pl.CostEstimate(flops=int(us * 1e9), bytes_accessed=1 << 20, transcendentals=0)
 
 
 def call(kernel, name, ids, inputs, outs, scratch=(), us=1):
@@ -428,19 +441,30 @@
     return results if len(outs) > 1 else results[0]
 
 
-def prepare(tokens, params):
+def prepare(tokens, params, segment_ids):
     rows = tokens.shape[0]
     return call(
-        prepare_kernel, "prepare", None, [tokens, params],
-        [like(rows, D), like(D, rows, kind=BF16), like(*params.shape, kind=BF16)], us=2,
-    )
-
-
-def attend(ids, segments, normed, bufs):
+        prepare_kernel, "prepare", None, [tokens, params, segment_ids.reshape(-1, SEQ)],
+        [
+            like(rows, D),
+            like(D, rows, kind=BF16),
+            like(*params.shape, kind=BF16),
+            like(rows, SEQ),
+        ],
+        us=2,
+    )
+
+
+def stack(items):
+    shape = (sum(item.shape[0] for item in items),) + items[0].shape[1:]
+    return call(stack_kernel, "stack", None, items, [like(*shape, kind=items[0].dtype)])
+
+
+def attend(ids, allowed, normed, bufs):
     rows = normed.shape[0]
     shapes = [(rows, 3 * D), (rows, HEADS * SEQ), (rows, D), (D, 3 * D)]
     return call(
-        attend_kernel, "attend", ids, [segments, normed, *bufs],
+        attend_kernel, "attend", ids, [allowed, normed, *bufs],
         [like(*shape, kind=BF16) for shape in shapes]
         + [like(SMALL_ROWS, LANES), like(HEAD_ROWS, LANES)],
         [pltpu.VMEM((FIRST_ROWS, LANES), F32)], us=6,
@@ -478,13 +502,19 @@
     )
 
 
-def attend_back(ids, project, weights, grad_attended, normed_turned, w_qkv, small, first, send_kind):
+def attend_back(project, weights, grad_attended):
+    return call(
+        attend_back_kernel, "attend_back", None, [project, weights, grad_attended],
+        [like(*project.shape, kind=BF16)], us=3,
+    )
+
+
+def project_back(ids, grad_project, normed_turned, w_qkv, small, first, send_kind):
     shape = (PLANE, SIDE + SIDE_ROWS, LANES)
     return call(
-        attend_back_kernel, "attend_back", ids,
-        [project, weights, grad_attended, normed_turned, w_qkv, small, first],
-        [like(*project.shape, kind=BF16), like(*shape), like(*shape, kind=send_kind)],
-        [pltpu.VMEM((FIRST_ROWS, LANES), F32), pltpu.VMEM(shape[1:], F32)], us=5,
+        project_back_kernel, "project_back", ids, [grad_project, normed_turned, w_qkv, small, first],
+        [like(*shape), like(*shape, kind=send_kind)],
+        [pltpu.VMEM((FIRST_ROWS, LANES), F32), pltpu.VMEM(shape[1:], F32)], us=1,
     )
 
 
@@ -497,26 +527,28 @@
 
 def local_any(n, tokens, params, segment_ids, cotangent):
     total = n * params.shape[0]
-    normed, normed_turned, _ = prepare(tokens, params)
+    normed, normed_turned, _, allowed = prepare(tokens, params, segment_ids)
     gathered = lax.all_gather(params, "fsdp", axis=0).reshape(total, LANES)
     shares = gathered[:ROW_TOTAL].reshape(Z, 2 * PLANE, SHARE, LANES)
     order = [p * 2 + c for c in range(2) for p in range(PLANE)]
     side = jnp.concatenate(
         [jnp.zeros((SIDE - SHARE, LANES), BF16), gathered[ROW_SMALL:ROW_TOTAL]], axis=0
     )
-    firsts = [jnp.concatenate([shares[0, k], side], axis=0) for k in order]
-    rests = [shares[1:, k] for k in order]
+    firsts = [
+        jnp.stack([jnp.concatenate([shares[0, k], side], axis=0) for k in group])
+        for group in (order[:PLANE], order[PLANE:])
+    ]
+    rests = []
+    for group in (order[:PLANE], order[PLANE:]):
+        rests += [shares[1:, group[0]], jnp.concatenate([shares[1:, k] for k in group[1:]])]
     ids = jnp.array(order, jnp.int32)
-    project, weights, attended, w_qkv, small, first = attend(
-        ids, segment_ids.reshape(-1, SEQ), normed, firsts
-    )
+    project, weights, attended, w_qkv, small, first = attend(ids, allowed, normed, firsts)
     middle, activated, grad_middle, grad_attended, w_down, rest, rest_send, first_grad = feed(
         ids, tokens, attended, cotangent, small, first, rests, F32
     )
     outputs = result(middle, activated, w_down, small)
-    grad_project, first, first_send = attend_back(
-        ids, project, weights, grad_attended, normed_turned, w_qkv, small, first_grad, F32
-    )
+    grad_project = attend_back(project, weights, grad_attended)
+    first, first_send = project_back(ids, grad_project, normed_turned, w_qkv, small, first_grad, F32)
     input_grad = input_gradient(tokens, grad_project, grad_middle, w_qkv, small)
     first = jnp.stack([first, first_send], axis=1)
     rest = jnp.stack([rest, rest_send]).reshape(2, PLANE, Z - 1, SHARE, LANES).transpose(2, 1, 0, 3, 4)
@@ -568,21 +600,21 @@
         [(plane ^ dp) * 2 + (core ^ dc) for dc in range(2) for dp in (0, *STEPS)]
     )
 
-    normed, normed_turned, own = prepare(tokens, params)
+    normed, normed_turned, own, allowed = prepare(tokens, params, segment_ids)
     first, rest = call(
         sort_kernel, "sort_shares", where, [own] + [move(params, d, 0, 0) for d in range(1, Z)],
         [like(SIDE + SMALL_ROWS, LANES, kind=BF16), like(Z - 1, SHARE, LANES, kind=BF16)],
         [pltpu.VMEM((Z, SHARE, LANES), BF16), pltpu.VMEM((SIDE + SMALL_ROWS, LANES), F32)],
     )
-    firsts = [first] + [move(first, 0, d, 0) for d in STEPS]
+    firsts = [move(first, 0, d, 0) for d in STEPS]
     rests = [move(rest, 0, d, 0) for d in STEPS]
-    firsts = firsts + [move(item, 0, 0, 1) for item in firsts]
+    firsts = stack([item[None] for item in (first, *firsts)])
     project, weights, attended, w_qkv, small, first = attend(
-        ids, segment_ids.reshape(-1, SEQ), normed, firsts
+        ids, allowed, normed, [firsts, move(firsts, 0, 0, 1)]
     )
     *rests, attended = lax.optimization_barrier((*rests, attended))
-    rests = [rest] + rests
-    rests = rests + [move(item, 0, 0, 1) for item in rests]
+    rests = stack(rests)
+    rests = [rest, rests, move(rest, 0, 0, 1), move(rests, 0, 0, 1)]
     middle, activated, grad_middle, grad_attended, w_down, keep, send, first_grad = feed(
         ids, tokens, attended, cotangent, small, first, rests, BF16
     )
@@ -593,10 +625,9 @@
     rest_kept, *sends = add_core(keep, received)
     *sends, grad_attended = lax.optimization_barrier((*sends, grad_attended))
     rest_sums = [move(item, 0, d, 0) for item, d in zip(sends, STEPS)]
-    grad_project, keep, send = attend_back(
-        ids, project, weights, grad_attended, normed_turned, w_qkv, small, first_grad, BF16
-    )
-    rest_sums[0], keep = lax.optimization_barrier((rest_sums[0], keep))
+    grad_project = attend_back(project, weights, grad_attended)
+    rest_sums[0], grad_project = lax.optimization_barrier((rest_sums[0], grad_project))
+    keep, send = project_back(ids, grad_project, normed_turned, w_qkv, small, first_grad, BF16)
     first_kept, *sends = add_core(keep, move(send, 0, 0, 1))
     first_sums = [move(item, 0, d, 0) for item, d in zip(sends, STEPS)]
     input_grad = input_gradient(tokens, grad_project, grad_middle, w_qkv, small)

time: 64.7 us -> 67.5 us (1.043)
  waiting for transfers between devices: 14 us -> 21.5 us
  starting transfers between devices: 26.4 us -> 23.5 us
  local copies, waits for them, and re-layouts: 4.07 us -> 2.62 us
    ppermute x28 -> x23, waiting for transfers between devices: 14 us -> 21.5 us  [move(): return lax.ppermute(values, 'fsdp', pairs)]
    ppermute x28 -> x23, starting transfers between devices: 26.4 us -> 23.5 us  [move(): return lax.ppermute(values, 'fsdp', pairs)]
    unnamed x14 -> x10, local copies, waits for them, and re-layouts: 3.99 us -> 2.54 us
    pallas_call x11 -> x14, Pallas kernels: 19.1 us -> 18.7 us  [call(): pl.pallas_call(kernel, in_specs=[SMEM_SPEC] * with_ids + [VMEM_SPEC] * le...]
  transfers between devices with their start and end apart: 28 -> 23, of which waited for: 14 -> 17; matrix products, arithmetic and copies ran while one was open for 0% -> 0% of each run, Pallas kernels for 12% -> 14%
where the time goes in v8:
time: 67.5 us; the launch traced here: 67.2 us
  starting transfers between devices  23.5 us (35%)
  waiting for transfers between devices  21.5 us (32%)
  Pallas kernels  18.7 us (28%)
  local copies, waits for them, and re-layouts  2.62 us (4%)
  between operations  0.82 us (1%)
    ppermute x23, starting transfers between devices, move(): return lax.ppermute(values, 'fsdp', pairs)  23.5 us
    ppermute x23, waiting for transfers between devices, move(): return lax.ppermute(values, 'fsdp', pairs)  21.5 us
    pallas_call x14, Pallas kernels, call(): pl.pallas_call(kernel, in_specs=[SMEM_SPEC] * with_ids + [VMEM_SPEC] * le...  18.7 us
    unnamed x10, local copies, waits for them, and re-layouts  2.54 us
  transfers between devices with their start and end apart: 23, of which 17 were waited for; matrix products, arithmetic and copies ran while one was open for 0% of the time, Pallas kernels for 14%

profile of v8, /device:TPU:0, one launch (start us, length us, event | category | flops | bytes accessed | tf_op | source)
XLA Modules:
  0.0 67.2 jit_solution(14721602693280450243)
XLA Ops:
  0.6 3.1 %collective-permute-start = (bf16[193,128]{1,0:T(8,128)(2,1)}, bf16[193,128]{1,0:T(8,128)(2,1)S(1)}, u32[]{:S(2)}, u32[]{:S(2)}) collective-permute-start(bf16[193,128]{1,0:T(8,128)(2,1)} %params.1), channel_id=1, source_target_pairs={{0,8},{1,9},{2,10},{3,11},{4,12},{5,13},{6,14},{7,15},{8,16},{9,17... | collective-permute-start | bytes 148232 | tf_op jit(solution)/shard_map/ppermute | solution.py:581
  3.7 2.1 %collective-permute-start.2 = (bf16[193,128]{1,0:T(8,128)(2,1)}, bf16[193,128]{1,0:T(8,128)(2,1)S(1)}, u32[]{:S(2)}, u32[]{:S(2)}) collective-permute-start(bf16[193,128]{1,0:T(8,128)(2,1)} %params.1), channel_id=1, source_target_pairs={{0,24},{1,25},{2,26},{3,27},{4,28},{5,29},{6,30},{7,31},{8,0},{9,1... | collective-permute-start | bytes 148232 | tf_op jit(solution)/shard_map/ppermute | solution.py:581
  5.8 0.9 %collective-permute-start.1 = (bf16[193,128]{1,0:T(8,128)(2,1)}, bf16[193,128]{1,0:T(8,128)(2,1)S(1)}, u32[]{:S(2)}, u32[]{:S(2)}) collective-permute-start(bf16[193,128]{1,0:T(8,128)(2,1)} %params.1), channel_id=1, source_target_pairs={{0,16},{1,17},{2,18},{3,19},{4,20},{5,21},{6,22},{7,23},{8,24},{9,... | collective-permute-start | bytes 148232 | tf_op jit(solution)/shard_map/ppermute | solution.py:581
  6.7 1.0 %copy-done.1 = bf16[1024,256]{1,0:T(8,128)(2,1)S(1)} copy-done((bf16[1024,256]{1,0:T(8,128)(2,1)S(1)}, bf16[1024,256]{1,0:T(8,128)(2,1)}, u32[]{:S(2)}) %copy-start.1) | copy-done | bytes 524312
  7.8 0.8 %copy-done.3 = bf16[193,128]{1,0:T(8,128)(2,1)S(1)} copy-done((bf16[193,128]{1,0:T(8,128)(2,1)S(1)}, bf16[193,128]{1,0:T(8,128)(2,1)}, u32[]{:S(2)}) %copy-start.3) | copy-done | bytes 49432
  8.6 0.7 %copy-done.4 = s32[1024]{0:T(1024)S(1)} copy-done((s32[1024]{0:T(1024)S(1)}, s32[1024]{0:T(1024)}, u32[]{:S(2)}) %copy-start.4) | copy-done | bytes 4120
  9.3 0.7 prepare.1
  10.0 1.2 %collective-permute-done.1.refs_2_ = bf16[193,128]{1,0:T(8,128)(2,1)S(1)} collective-permute-done((bf16[193,128]{1,0:T(8,128)(2,1)}, bf16[193,128]{1,0:T(8,128)(2,1)S(1)}, u32[]{:S(2)}, u32[]{:S(2)}) %collective-permute-start.1) | collective-permute-done | bytes 49440 | tf_op jit(solution)/shard_map/ppermute | solution.py:581
  11.3 1.6 %collective-permute-start.8 = (bf16[240,128]{1,0:T(8,128)(2,1)S(1)}, bf16[240,128]{1,0:T(8,128)(2,1)S(1)}, u32[]{:S(2)}, u32[]{:S(2)}) collective-permute-start(bf16[240,128]{1,0:T(8,128)(2,1)S(1)} %get-tuple-element.53), channel_id=1, source_target_pairs={{0,4},{1,5},{2,6},{3,7},{4,0},{5,1},{6,2},{7,3},{8,12},{9,13},{10,... | collective-permute-start | bytes 184328 | tf_op jit(solution)/shard_map/ppermute | solution.py:581
  12.9 1.5 %collective-permute-start.7 = (bf16[240,128]{1,0:T(8,128)(2,1)S(1)}, bf16[240,128]{1,0:T(8,128)(2,1)S(1)}, u32[]{:S(2)}, u32[]{:S(2)}) collective-permute-start(bf16[240,128]{1,0:T(8,128)(2,1)S(1)} %get-tuple-element.53), channel_id=1, source_target_pairs={{0,2},{1,3},{2,0},{3,1},{4,6},{5,7},{6,4},{7,5},{8,10},{9,11},{10,... | collective-permute-start | bytes 184328 | tf_op jit(solution)/shard_map/ppermute | solution.py:581
  14.4 0.5 collective-permute-start.6
  14.8 0.7 %collective-permute-done.8 = bf16[240,128]{1,0:T(8,128)(2,1)S(1)} collective-permute-done((bf16[240,128]{1,0:T(8,128)(2,1)S(1)}, bf16[240,128]{1,0:T(8,128)(2,1)S(1)}, u32[]{:S(2)}, u32[]{:S(2)}) %collective-permute-start.8) | collective-permute-done | bytes 61472 | tf_op jit(solution)/shard_map/ppermute | solution.py:581
  15.6 1.5 %collective-permute-done.7 = bf16[240,128]{1,0:T(8,128)(2,1)S(1)} collective-permute-done((bf16[240,128]{1,0:T(8,128)(2,1)S(1)}, bf16[240,128]{1,0:T(8,128)(2,1)S(1)}, u32[]{:S(2)}, u32[]{:S(2)}) %collective-permute-start.7) | collective-permute-done | bytes 61472 | tf_op jit(solution)/shard_map/ppermute | solution.py:581
  17.1 2.4 %collective-permute-done.6 = bf16[240,128]{1,0:T(8,128)(2,1)S(1)} collective-permute-done((bf16[240,128]{1,0:T(8,128)(2,1)S(1)}, bf16[240,128]{1,0:T(8,128)(2,1)S(1)}, u32[]{:S(2)}, u32[]{:S(2)}) %collective-permute-start.6) | collective-permute-done | bytes 61472 | tf_op jit(solution)/shard_map/ppermute | solution.py:581
  19.7 0.5 collective-permute-start.5
  20.2 0.7 %collective-permute-start.4 = (bf16[3,193,128]{2,1,0:T(8,128)(2,1)S(1)}, bf16[3,193,128]{2,1,0:T(8,128)(2,1)S(1)}, u32[]{:S(2)}, u32[]{:S(2)}) collective-permute-start(bf16[3,193,128]{2,1,0:T(8,128)(2,1)S(1)} %get-tuple-element.50.refs_0_), channel_id=1, source_target_pairs={{0,2},{1,3},{2,0},{3,1},{4,6},{5,7},{6,4},{7,5},{8,10},{9,11},{10,... | collective-permute-start | bytes 444680 | tf_op jit(solution)/shard_map/ppermute | solution.py:581
  20.9 2.3 %collective-permute-start.3 = (bf16[3,193,128]{2,1,0:T(8,128)(2,1)S(1)}, bf16[3,193,128]{2,1,0:T(8,128)(2,1)S(1)}, u32[]{:S(2)}, u32[]{:S(2)}) collective-permute-start(bf16[3,193,128]{2,1,0:T(8,128)(2,1)S(1)} %get-tuple-element.50.refs_0_), channel_id=1, source_target_pairs={{0,6},{1,7},{2,4},{3,5},{4,2},{5,3},{6,0},{7,1},{8,14},{9,15},{10,... | collective-permute-start | bytes 444680 | tf_op jit(solution)/shard_map/ppermute | solution.py:581
  23.2 3.0 %attend.1 = (bf16[1024,768]{1,0:T(8,128)(2,1)S(1)}, bf16[1024,512]{1,0:T(8,128)(2,1)S(1)}, bf16[1024,256]{1,0:T(8,128)(2,1)S(1)}, bf16[256,768]{1,0:T(8,128)(2,1...) custom-call(s32[8]{0:T(128)S(1)} %stack.37.ids, f32[1024,128]{1,0:T(8,128)S(1)} %get-tuple-element.51.allowed, ...), custom_call_target="tpu_custom_call" | custom-call | flops 6000000000 | bytes 1048576 | tf_op jit(solution)/shard_map/attend/pallas_call | solution.py:431
  26.3 0.8 %collective-permute-done.4.refs_1_ = bf16[3,193,128]{2,1,0:T(8,128)(2,1)S(1)} collective-permute-done((bf16[3,193,128]{2,1,0:T(8,128)(2,1)S(1)}, bf16[3,193,128]{2,1,0:T(8,128)(2,1)S(1)}, u32[]{:S(2)}, u32[]{:S(2)}) %collective-permute-start.4) | collective-permute-done | bytes 148256 | tf_op jit(solution)/shard_map/ppermute | solution.py:581
  27.0 3.5 %collective-permute-done.3.refs_0_ = bf16[3,193,128]{2,1,0:T(8,128)(2,1)S(1)} collective-permute-done((bf16[3,193,128]{2,1,0:T(8,128)(2,1)S(1)}, bf16[3,193,128]{2,1,0:T(8,128)(2,1)S(1)}, u32[]{:S(2)}, u32[]{:S(2)}) %collective-permute-start.3) | collective-permute-done | bytes 148256 | tf_op jit(solution)/shard_map/ppermute | solution.py:581
  30.7 0.5 collective-permute-start.10
  31.2 1.5 %collective-permute-done.10.refs_2_ = bf16[3,193,128]{2,1,0:T(8,128)(2,1)S(1)} collective-permute-done((bf16[3,193,128]{2,1,0:T(8,128)(2,1)S(1)}, bf16[3,193,128]{2,1,0:T(8,128)(2,1)S(1)}, u32[]{:S(2)}, u32[]{:S(2)}) %collective-permute-start.10) | collective-permute-done | bytes 148256 | tf_op jit(solution)/shard_map/ppermute | solution.py:581
  32.7 6.8 %feed.1 = (f32[1024,256]{1,0:T(8,128)S(1)}, bf16[1024,1024]{1,0:T(8,128)(2,1)S(1)}, f32[1024,256]{1,0:T(8,128)S(1)}, bf16[1024,256]{1,0:T(8,128)(2,1)S(1)}, bf16...) custom-call(s32[8]{0:T(128)S(1)} %stack.37.ids, ...), custom_call_target="tpu_custom_call" | custom-call | flops 8000000000 | bytes 1048576 | tf_op jit(solution)/shard_map/feed/pallas_call | solution.py:431
  39.5 0.2 collective-permute-start.12
  39.7 1.5 %result.1 = bf16[1024,256]{1,0:T(8,128)(2,1)} custom-call(f32[1024,256]{1,0:T(8,128)S(1)} %get-tuple-element.62.middle, bf16[1024,1024]{1,0:T(8,128)(2,1)S(1)} %get-tuple-element.63.activated, bf16[1024,256]{1,0:T(8,128)(2,1)S(1)} %get-tuple-element.64.w_down, f32[32,128]{1,0:T(8,128)S(1)} %get-tuple-element.56.small), custom_call_target="tpu_custom_call" | custom-call | flops 2000000000 | bytes 1048576 | tf_op jit(solution)/shard_map/result/pallas_call | solution.py:431
  41.2 0.4 collective-permute-done.12.received
  41.8 0.7 %collective-permute-start.13 = (bf16[3,193,128]{2,1,0:T(8,128)(2,1)S(1)}, bf16[3,193,128]{2,1,0:T(8,128)(2,1)S(1)}, u32[]{:S(2)}, u32[]{:S(2)}) collective-permute-start(bf16[3,193,128]{2,1,0:T(8,128)(2,1)S(1)} %get-tuple-element.72), channel_id=1, source_target_pairs={{0,6},{1,7},{2,4},{3,5},{4,2},{5,3},{6,0},{7,1},{8,14},{9,15},{10,... | collective-permute-start | bytes 444680 | tf_op jit(solution)/shard_map/ppermute | solution.py:581
  42.5 2.2 %attend_back.1.grad_project = bf16[1024,768]{1,0:T(8,128)(2,1)S(1)} custom-call(bf16[1024,768]{1,0:T(8,128)(2,1)S(1)} %get-tuple-element.73.project, bf16[1024,512]{1,0:T(8,128)(2,1)S(1)} %get-tuple-element.74.weights, bf16[1024,256]{1,0:T(8,128)(2,1)S(1)} %get-tuple-element.75.grad_attended), custom_call_target="tpu_custom_call" | custom-call | flops 3000000000 | bytes 1048576 | tf_op jit(solution)/shard_map/attend_back/pallas_call | solution.py:431
  44.7 4.0 %collective-permute-done.13.refs_3_ = bf16[3,193,128]{2,1,0:T(8,128)(2,1)S(1)} collective-permute-done((bf16[3,193,128]{2,1,0:T(8,128)(2,1)S(1)}, bf16[3,193,128]{2,1,0:T(8,128)(2,1)S(1)}, u32[]{:S(2)}, u32[]{:S(2)}) %collective-permute-start.13) | collective-permute-done | bytes 148256 | tf_op jit(solution)/shard_map/ppermute | solution.py:581
  48.7 1.3 %project_back.1 = (f32[4,224,128]{2,1,0:T(8,128)S(1)}, bf16[4,224,128]{2,1,0:T(8,128)(2,1)S(1)}) custom-call(s32[8]{0:T(128)S(1)} %stack.37.ids, bf16[1024,768]{1,0:T(8,128)(2,1)S(1)} %attend_back.1.grad_project, bf16[256,1024]{1,0:T(8,128)(2,1)S(1)} %get-tuple-element.79.normed_turned, bf16[256,768]{1,0:T(8,128)(2,1)S(1)} %get-tuple-element.78.w_qkv, ...), custom_call_target="tpu_custom_call" | custom-call | flops 1000000000 | bytes 1048576 | tf_op jit(solution)/shard_map/project_back/pallas_call | solution.py:431
  50.1 0.6 collective-permute-start.18
  50.8 0.7 %collective-permute-start.19 = (bf16[3,193,128]{2,1,0:T(8,128)(2,1)S(1)}, bf16[3,193,128]{2,1,0:T(8,128)(2,1)S(1)}, u32[]{:S(2)}, u32[]{:S(2)}) collective-permute-start(bf16[3,193,128]{2,1,0:T(8,128)(2,1)S(1)} %get-tuple-element.90), channel_id=1, source_target_pairs={{0,4},{1,5},{2,6},{3,7},{4,0},{5,1},{6,2},{7,3},{8,12},{9,13},{10,... | collective-permute-start | bytes 444680 | tf_op jit(solution)/shard_map/ppermute | solution.py:581
  51.4 0.2 collective-permute-done.14.received
  51.7 2.1 %collective-permute-start.15 = (bf16[1,224,128]{2,1,0:T(8,128)(2,1)S(1)}, bf16[1,224,128]{2,1,0:T(8,128)(2,1)S(1)}, u32[]{:S(2)}, u32[]{:S(2)}) collective-permute-start(bf16[1,224,128]{2,1,0:T(8,128)(2,1)S(1)} %get-tuple-element.85), channel_id=1, source_target_pairs={{0,6},{1,7},{2,4},{3,5},{4,2},{5,3},{6,0},{7,1},{8,14},{9,15},{10,... | collective-permute-start | bytes 172040 | tf_op jit(solution)/shard_map/ppermute | solution.py:581
  53.8 0.5 collective-permute-start.16
  54.4 0.9 %collective-permute-start.17 = (bf16[1,224,128]{2,1,0:T(8,128)(2,1)S(1)}, bf16[1,224,128]{2,1,0:T(8,128)(2,1)S(1)}, u32[]{:S(2)}, u32[]{:S(2)}) collective-permute-start(bf16[1,224,128]{2,1,0:T(8,128)(2,1)S(1)} %get-tuple-element.87), channel_id=1, source_target_pairs={{0,4},{1,5},{2,6},{3,7},{4,0},{5,1},{6,2},{7,3},{8,12},{9,13},{10,... | collective-permute-start | bytes 172040 | tf_op jit(solution)/shard_map/ppermute | solution.py:581
  55.2 1.8 %collective-permute-done.18.refs_4_ = bf16[3,193,128]{2,1,0:T(8,128)(2,1)S(1)} collective-permute-done((bf16[3,193,128]{2,1,0:T(8,128)(2,1)S(1)}, bf16[3,193,128]{2,1,0:T(8,128)(2,1)S(1)}, u32[]{:S(2)}, u32[]{:S(2)}) %collective-permute-start.18) | collective-permute-done | bytes 148256 | tf_op jit(solution)/shard_map/ppermute | solution.py:581
  57.0 1.6 %collective-permute-done.19.refs_5_ = bf16[3,193,128]{2,1,0:T(8,128)(2,1)S(1)} collective-permute-done((bf16[3,193,128]{2,1,0:T(8,128)(2,1)S(1)}, bf16[3,193,128]{2,1,0:T(8,128)(2,1)S(1)}, u32[]{:S(2)}, u32[]{:S(2)}) %collective-permute-start.19) | collective-permute-done | bytes 148256 | tf_op jit(solution)/shard_map/ppermute | solution.py:581
  58.6 0.4 collective-permute-done.16.refs_1_
  59.0 0.3 collective-permute-done.17.refs_2_
  59.4 0.4 collective-permute-start.20
  59.8 2.5 %collective-permute-start.21 = (bf16[193,128]{1,0:T(8,128)(2,1)S(1)}, bf16[193,128]{1,0:T(8,128)(2,1)S(1)}, u32[]{:S(2)}, u32[]{:S(2)}) collective-permute-start(bf16[193,128]{1,0:T(8,128)(2,1)S(1)} %get-tuple-element.93), channel_id=1, source_target_pairs={{0,16},{1,17},{2,18},{3,19},{4,20},{5,21},{6,22},{7,23},{8,24},{9,... | collective-permute-start | bytes 148232 | tf_op jit(solution)/shard_map/ppermute | solution.py:581
  62.3 1.0 %collective-permute-start.22 = (bf16[193,128]{1,0:T(8,128)(2,1)S(1)}, bf16[193,128]{1,0:T(8,128)(2,1)S(1)}, u32[]{:S(2)}, u32[]{:S(2)}) collective-permute-start(bf16[193,128]{1,0:T(8,128)(2,1)S(1)} %get-tuple-element.94), channel_id=1, source_target_pairs={{0,24},{1,25},{2,26},{3,27},{4,28},{5,29},{6,30},{7,31},{8,0},{9,1... | collective-permute-start | bytes 148232 | tf_op jit(solution)/shard_map/ppermute | solution.py:581
  63.3 2.0 %input_grad.1 = f32[1024,256]{1,0:T(8,128)} custom-call(bf16[1024,256]{1,0:T(8,128)(2,1)S(1)} %copy-done.2, bf16[1024,768]{1,0:T(8,128)(2,1)S(1)} %attend_back.1.grad_project, f32[1024,256]{1,0:T(8,128)S(1)} %get-tuple-element.77.grad_middle, bf16[256,768]{1,0:T(8,128)(2,1)S(1)} %get-tuple-element.78.w_qkv, f32[32,128]{1,0:T(8,128)S(1)} %get-tuple-element.56.small), custom_call_target="tpu_custom_call" | custom-call | flops 2000000000 | bytes 1048576 | tf_op jit(solution)/shard_map/input_grad/pallas_call | solution.py:431
  65.3 0.3 collective-permute-done.20.refs_0_
  65.6 0.8 %collective-permute-done.21.refs_1_ = bf16[193,128]{1,0:T(8,128)(2,1)S(1)} collective-permute-done((bf16[193,128]{1,0:T(8,128)(2,1)S(1)}, bf16[193,128]{1,0:T(8,128)(2,1)S(1)}, u32[]{:S(2)}, u32[]{:S(2)}) %collective-permute-start.21) | collective-permute-done | bytes 49440 | tf_op jit(solution)/shard_map/ppermute | solution.py:581
  66.4 0.2 collective-permute-done.22.refs_2_
  66.6 0.7 add_column.1
  (23 shorter events, 0.8 us)
Async XLA Ops:
  0.6 9.3 %collective-permute-start = (bf16[193,128]{1,0:T(8,128)(2,1)}, bf16[193,128]{1,0:T(8,128)(2,1)S(1)}, u32[]{:S(2)}, u32[]{:S(2)}) collective-permute-start(bf16[193,128]{1,0:T(8,128)(2,1)} %params.1), channel_id=1, source_target_pairs={{0,8},{1,9},{2,10},{3,11},{4,12},{5,13},{6,14},{7,15},{8,16},{9,17... | collective-permute-start | bytes 148232 | tf_op jit(solution)/shard_map/ppermute | solution.py:581
  3.7 6.3 %collective-permute-start.2 = (bf16[193,128]{1,0:T(8,128)(2,1)}, bf16[193,128]{1,0:T(8,128)(2,1)S(1)}, u32[]{:S(2)}, u32[]{:S(2)}) collective-permute-start(bf16[193,128]{1,0:T(8,128)(2,1)} %params.1), channel_id=1, source_target_pairs={{0,24},{1,25},{2,26},{3,27},{4,28},{5,29},{6,30},{7,31},{8,0},{9,1... | collective-permute-start | bytes 148232 | tf_op jit(solution)/shard_map/ppermute | solution.py:581
  5.8 5.4 %collective-permute-start.1 = (bf16[193,128]{1,0:T(8,128)(2,1)}, bf16[193,128]{1,0:T(8,128)(2,1)S(1)}, u32[]{:S(2)}, u32[]{:S(2)}) collective-permute-start(bf16[193,128]{1,0:T(8,128)(2,1)} %params.1), channel_id=1, source_target_pairs={{0,16},{1,17},{2,18},{3,19},{4,20},{5,21},{6,22},{7,23},{8,24},{9,... | collective-permute-start | bytes 148232 | tf_op jit(solution)/shard_map/ppermute | solution.py:581
  6.7 1.0 %copy-start.1 = (bf16[1024,256]{1,0:T(8,128)(2,1)S(1)}, bf16[1024,256]{1,0:T(8,128)(2,1)}, u32[]{:S(2)}) copy-start(bf16[1024,256]{1,0:T(8,128)(2,1)} %tok.5) | copy-start | bytes 1572868
  7.8 0.8 %copy-start.3 = (bf16[193,128]{1,0:T(8,128)(2,1)S(1)}, bf16[193,128]{1,0:T(8,128)(2,1)}, u32[]{:S(2)}) copy-start(bf16[193,128]{1,0:T(8,128)(2,1)} %params.1) | copy-start | bytes 148228
  8.6 0.7 %copy-start.4 = (s32[1024]{0:T(1024)S(1)}, s32[1024]{0:T(1024)}, u32[]{:S(2)}) copy-start(s32[1024]{0:T(1024)} %param.6) | copy-start | bytes 12292
  11.3 4.3 %collective-permute-start.8 = (bf16[240,128]{1,0:T(8,128)(2,1)S(1)}, bf16[240,128]{1,0:T(8,128)(2,1)S(1)}, u32[]{:S(2)}, u32[]{:S(2)}) collective-permute-start(bf16[240,128]{1,0:T(8,128)(2,1)S(1)} %get-tuple-element.53), channel_id=1, source_target_pairs={{0,4},{1,5},{2,6},{3,7},{4,0},{5,1},{6,2},{7,3},{8,12},{9,13},{10,... | collective-permute-start | bytes 184328 | tf_op jit(solution)/shard_map/ppermute | solution.py:581
  12.9 4.2 %collective-permute-start.7 = (bf16[240,128]{1,0:T(8,128)(2,1)S(1)}, bf16[240,128]{1,0:T(8,128)(2,1)S(1)}, u32[]{:S(2)}, u32[]{:S(2)}) collective-permute-start(bf16[240,128]{1,0:T(8,128)(2,1)S(1)} %get-tuple-element.53), channel_id=1, source_target_pairs={{0,2},{1,3},{2,0},{3,1},{4,6},{5,7},{6,4},{7,5},{8,10},{9,11},{10,... | collective-permute-start | bytes 184328 | tf_op jit(solution)/shard_map/ppermute | solution.py:581
  14.4 5.1 %collective-permute-start.6 = (bf16[240,128]{1,0:T(8,128)(2,1)S(1)}, bf16[240,128]{1,0:T(8,128)(2,1)S(1)}, u32[]{:S(2)}, u32[]{:S(2)}) collective-permute-start(bf16[240,128]{1,0:T(8,128)(2,1)S(1)} %get-tuple-element.53), channel_id=1, source_target_pairs={{0,6},{1,7},{2,4},{3,5},{4,2},{5,3},{6,0},{7,1},{8,14},{9,15},{10,... | collective-permute-start | bytes 184328 | tf_op jit(solution)/shard_map/ppermute | solution.py:581
  19.5 3.7 %collective-permute-start.9 = (bf16[4,240,128]{2,1,0:T(8,128)(2,1)S(1)}, bf16[4,240,128]{2,1,0:T(8,128)(2,1)S(1)}, u32[]{:S(2)}, u32[]{:S(2)}) collective-permute-start(bf16[4,240,128]{2,1,0:T(8,128)(2,1)S(1)} %stack.38.refs_0_), channel_id=1, source_target_pairs={{0,1},{1,0},{2,3},{3,2},{4,5},{5,4},{6,7},{7,6},{8,9},{9,8},{10,11... | collective-permute-start | bytes 737288 | tf_op jit(solution)/shard_map/ppermute | solution.py:581
  19.7 6.5 %collective-permute-start.5 = (bf16[3,193,128]{2,1,0:T(8,128)(2,1)S(1)}, bf16[3,193,128]{2,1,0:T(8,128)(2,1)S(1)}, u32[]{:S(2)}, u32[]{:S(2)}) collective-permute-start(bf16[3,193,128]{2,1,0:T(8,128)(2,1)S(1)} %get-tuple-element.50.refs_0_), channel_id=1, source_target_pairs={{0,4},{1,5},{2,6},{3,7},{4,0},{5,1},{6,2},{7,3},{8,12},{9,13},{10,... | collective-permute-start | bytes 444680 | tf_op jit(solution)/shard_map/ppermute | solution.py:581
  20.2 6.8 %collective-permute-start.4 = (bf16[3,193,128]{2,1,0:T(8,128)(2,1)S(1)}, bf16[3,193,128]{2,1,0:T(8,128)(2,1)S(1)}, u32[]{:S(2)}, u32[]{:S(2)}) collective-permute-start(bf16[3,193,128]{2,1,0:T(8,128)(2,1)S(1)} %get-tuple-element.50.refs_0_), channel_id=1, source_target_pairs={{0,2},{1,3},{2,0},{3,1},{4,6},{5,7},{6,4},{7,5},{8,10},{9,11},{10,... | collective-permute-start | bytes 444680 | tf_op jit(solution)/shard_map/ppermute | solution.py:581
  20.9 9.6 %collective-permute-start.3 = (bf16[3,193,128]{2,1,0:T(8,128)(2,1)S(1)}, bf16[3,193,128]{2,1,0:T(8,128)(2,1)S(1)}, u32[]{:S(2)}, u32[]{:S(2)}) collective-permute-start(bf16[3,193,128]{2,1,0:T(8,128)(2,1)S(1)} %get-tuple-element.50.refs_0_), channel_id=1, source_target_pairs={{0,6},{1,7},{2,4},{3,5},{4,2},{5,3},{6,0},{7,1},{8,14},{9,15},{10,... | collective-permute-start | bytes 444680 | tf_op jit(solution)/shard_map/ppermute | solution.py:581
  30.5 2.2 %copy-start = (bf16[1024,256]{1,0:T(8,128)(2,1)S(1)}, bf16[1024,256]{1,0:T(8,128)(2,1)}, u32[]{:S(2)}) copy-start(bf16[1024,256]{1,0:T(8,128)(2,1)} %cot.1) | copy-start | bytes 1572868
  30.5 2.2 %copy-start.2 = (bf16[1024,256]{1,0:T(8,128)(2,1)S(1)}, bf16[1024,256]{1,0:T(8,128)(2,1)}, u32[]{:S(2)}) copy-start(bf16[1024,256]{1,0:T(8,128)(2,1)} %tok.5) | copy-start | bytes 1572868
  30.6 2.1 %collective-permute-start.11 = (bf16[9,193,128]{2,1,0:T(8,128)(2,1)S(1)}, bf16[9,193,128]{2,1,0:T(8,128)(2,1)S(1)}, u32[]{:S(2)}, u32[]{:S(2)}) collective-permute-start(bf16[9,193,128]{2,1,0:T(8,128)(2,1)S(1)} %stack.39.refs_1_), channel_id=1, source_target_pairs={{0,1},{1,0},{2,3},{3,2},{4,5},{5,4},{6,7},{7,6},{8,9},{9,8},{10,11... | collective-permute-start | bytes 1334024 | tf_op jit(solution)/shard_map/ppermute | solution.py:581
  30.7 2.0 %collective-permute-start.10 = (bf16[3,193,128]{2,1,0:T(8,128)(2,1)S(1)}, bf16[3,193,128]{2,1,0:T(8,128)(2,1)S(1)}, u32[]{:S(2)}, u32[]{:S(2)}) collective-permute-start(bf16[3,193,128]{2,1,0:T(8,128)(2,1)S(1)} %get-tuple-element.50.refs_0_), channel_id=1, source_target_pairs={{0,1},{1,0},{2,3},{3,2},{4,5},{5,4},{6,7},{7,6},{8,9},{9,8},{10,11... | collective-permute-start | bytes 444680 | tf_op jit(solution)/shard_map/ppermute | solution.py:581
  39.5 2.1 %collective-permute-start.12 = (bf16[12,193,128]{2,1,0:T(8,128)(2,1)S(1)}, bf16[12,193,128]{2,1,0:T(8,128)(2,1)S(1)}, u32[]{:S(2)}, u32[]{:S(2)}) collective-permute-start(bf16[12,193,128]{2,1,0:T(8,128)(2,1)S(1)} %get-tuple-element.61), channel_id=1, source_target_pairs={{0,1},{1,0},{2,3},{3,2},{4,5},{5,4},{6,7},{7,6},{8,9},{9,8},{10,11... | collective-permute-start | bytes 1778696 | tf_op jit(solution)/shard_map/ppermute | solution.py:581
  41.8 7.0 %collective-permute-start.13 = (bf16[3,193,128]{2,1,0:T(8,128)(2,1)S(1)}, bf16[3,193,128]{2,1,0:T(8,128)(2,1)S(1)}, u32[]{:S(2)}, u32[]{:S(2)}) collective-permute-start(bf16[3,193,128]{2,1,0:T(8,128)(2,1)S(1)} %get-tuple-element.72), channel_id=1, source_target_pairs={{0,6},{1,7},{2,4},{3,5},{4,2},{5,3},{6,0},{7,1},{8,14},{9,15},{10,... | collective-permute-start | bytes 444680 | tf_op jit(solution)/shard_map/ppermute | solution.py:581
  50.1 1.6 %collective-permute-start.14 = (bf16[4,224,128]{2,1,0:T(8,128)(2,1)S(1)}, bf16[4,224,128]{2,1,0:T(8,128)(2,1)S(1)}, u32[]{:S(2)}, u32[]{:S(2)}) collective-permute-start(bf16[4,224,128]{2,1,0:T(8,128)(2,1)S(1)} %get-tuple-element.82), channel_id=1, source_target_pairs={{0,1},{1,0},{2,3},{3,2},{4,5},{5,4},{6,7},{7,6},{8,9},{9,8},{10,11... | collective-permute-start | bytes 688136 | tf_op jit(solution)/shard_map/ppermute | solution.py:581
  50.1 6.8 %collective-permute-start.18 = (bf16[3,193,128]{2,1,0:T(8,128)(2,1)S(1)}, bf16[3,193,128]{2,1,0:T(8,128)(2,1)S(1)}, u32[]{:S(2)}, u32[]{:S(2)}) collective-permute-start(bf16[3,193,128]{2,1,0:T(8,128)(2,1)S(1)} %get-tuple-element.89), channel_id=1, source_target_pairs={{0,2},{1,3},{2,0},{3,1},{4,6},{5,7},{6,4},{7,5},{8,10},{9,11},{10,... | collective-permute-start | bytes 444680 | tf_op jit(solution)/shard_map/ppermute | solution.py:581
  50.8 7.8 %collective-permute-start.19 = (bf16[3,193,128]{2,1,0:T(8,128)(2,1)S(1)}, bf16[3,193,128]{2,1,0:T(8,128)(2,1)S(1)}, u32[]{:S(2)}, u32[]{:S(2)}) collective-permute-start(bf16[3,193,128]{2,1,0:T(8,128)(2,1)S(1)} %get-tuple-element.90), channel_id=1, source_target_pairs={{0,4},{1,5},{2,6},{3,7},{4,0},{5,1},{6,2},{7,3},{8,12},{9,13},{10,... | collective-permute-start | bytes 444680 | tf_op jit(solution)/shard_map/ppermute | solution.py:581
  51.7 6.9 %collective-permute-start.15 = (bf16[1,224,128]{2,1,0:T(8,128)(2,1)S(1)}, bf16[1,224,128]{2,1,0:T(8,128)(2,1)S(1)}, u32[]{:S(2)}, u32[]{:S(2)}) collective-permute-start(bf16[1,224,128]{2,1,0:T(8,128)(2,1)S(1)} %get-tuple-element.85), channel_id=1, source_target_pairs={{0,6},{1,7},{2,4},{3,5},{4,2},{5,3},{6,0},{7,1},{8,14},{9,15},{10,... | collective-permute-start | bytes 172040 | tf_op jit(solution)/shard_map/ppermute | solution.py:581
  53.8 5.2 %collective-permute-start.16 = (bf16[1,224,128]{2,1,0:T(8,128)(2,1)S(1)}, bf16[1,224,128]{2,1,0:T(8,128)(2,1)S(1)}, u32[]{:S(2)}, u32[]{:S(2)}) collective-permute-start(bf16[1,224,128]{2,1,0:T(8,128)(2,1)S(1)} %get-tuple-element.86), channel_id=1, source_target_pairs={{0,2},{1,3},{2,0},{3,1},{4,6},{5,7},{6,4},{7,5},{8,10},{9,11},{10,... | collective-permute-start | bytes 172040 | tf_op jit(solution)/shard_map/ppermute | solution.py:581
  54.4 4.9 %collective-permute-start.17 = (bf16[1,224,128]{2,1,0:T(8,128)(2,1)S(1)}, bf16[1,224,128]{2,1,0:T(8,128)(2,1)S(1)}, u32[]{:S(2)}, u32[]{:S(2)}) collective-permute-start(bf16[1,224,128]{2,1,0:T(8,128)(2,1)S(1)} %get-tuple-element.87), channel_id=1, source_target_pairs={{0,4},{1,5},{2,6},{3,7},{4,0},{5,1},{6,2},{7,3},{8,12},{9,13},{10,... | collective-permute-start | bytes 172040 | tf_op jit(solution)/shard_map/ppermute | solution.py:581
  59.4 6.2 %collective-permute-start.20 = (bf16[193,128]{1,0:T(8,128)(2,1)S(1)}, bf16[193,128]{1,0:T(8,128)(2,1)S(1)}, u32[]{:S(2)}, u32[]{:S(2)}) collective-permute-start(bf16[193,128]{1,0:T(8,128)(2,1)S(1)} %get-tuple-element.92), channel_id=1, source_target_pairs={{0,8},{1,9},{2,10},{3,11},{4,12},{5,13},{6,14},{7,15},{8,16},{9,17... | collective-permute-start | bytes 148232 | tf_op jit(solution)/shard_map/ppermute | solution.py:581
  59.8 6.6 %collective-permute-start.21 = (bf16[193,128]{1,0:T(8,128)(2,1)S(1)}, bf16[193,128]{1,0:T(8,128)(2,1)S(1)}, u32[]{:S(2)}, u32[]{:S(2)}) collective-permute-start(bf16[193,128]{1,0:T(8,128)(2,1)S(1)} %get-tuple-element.93), channel_id=1, source_target_pairs={{0,16},{1,17},{2,18},{3,19},{4,20},{5,21},{6,22},{7,23},{8,24},{9,... | collective-permute-start | bytes 148232 | tf_op jit(solution)/shard_map/ppermute | solution.py:581
  62.3 4.2 %collective-permute-start.22 = (bf16[193,128]{1,0:T(8,128)(2,1)S(1)}, bf16[193,128]{1,0:T(8,128)(2,1)S(1)}, u32[]{:S(2)}, u32[]{:S(2)}) collective-permute-start(bf16[193,128]{1,0:T(8,128)(2,1)S(1)} %get-tuple-element.94), channel_id=1, source_target_pairs={{0,24},{1,25},{2,26},{3,27},{4,28},{5,29},{6,30},{7,31},{8,0},{9,1... | collective-permute-start | bytes 148232 | tf_op jit(solution)/shard_map/ppermute | solution.py:581

commit v9 on v8

--- a/solution.py
+++ b/solution.py
@@ -135,8 +135,8 @@
 
 
 def attend_kernel(ids, allowed, normed, *refs):
-    bufs = [ref.at[p] for ref in refs[:2] for p in range(PLANE)]
-    project_out, weights_out, attended_out, w_qkv, small, first_out, flat = refs[2:]
+    bufs = refs[: 2 * PLANE]
+    project_out, weights_out, attended_out, w_qkv, small, first_out, flat = refs[2 * PLANE :]
     for slot, buf in enumerate(bufs):
         wide = buf[...].astype(F32)
         flat[pl.ds(ids[slot] * SHARE, SHARE), :] = wide[:SHARE, :]
@@ -301,7 +301,10 @@
     result_out[...] = result.astype(BF16)
 
 
-def attend_back_kernel(project, weights, grad_attended, grad_project):
+def attend_back_kernel(
+    ids, project, weights, grad_attended, normed_turned, w_qkv, small, first_in,
+    grad_project, keep_out, send_out, flat, wide,
+):
     def some(g, carry):
         base = g * WIDE
         spans = [pl.ds(pl.multiple_of(base + s * SEQ, SEQ), SEQ) for s in range(GROUP)]
@@ -333,11 +336,6 @@
         return carry
 
     lax.fori_loop(0, project.shape[0] // WIDE, some, 0)
-
-
-def project_back_kernel(
-    ids, grad_project, normed_turned, w_qkv, small, first_in, keep_out, send_out, flat, wide
-):
     products = dot(normed_turned[...], grad_project[...])
     sums = jnp.sum(fold_rows(grad_project[...].astype(F32)), axis=0, keepdims=True)
     gain = jnp.broadcast_to(small_vector(small, GAIN_ONE, 2), (LANES, D)).T
@@ -391,21 +389,22 @@
         row += ref.shape[0]
 
 
-def add_core_kernel(kept, received, keep_out, *sends):
-    part = kept.shape[0] // PLANE
+def add_core_kernel(first, first_in, rest, rest_in, keep_out, *refs):
+    sends, column = refs[:-1], refs[-1]
+    end = SMALL_IN_SHARE + LATE_SMALL
     for p, out in enumerate((keep_out, *sends)):
-        span = slice(p * part, (p + 1) * part)
-        out[...] = (kept[span] + received[span].astype(F32)).astype(out.dtype)
-
-
-def add_plane_kernel(ids, first_kept, rest_kept, *refs):
-    firsts, rests = refs[: PLANE - 1], refs[PLANE - 1 : 2 * (PLANE - 1)]
-    keep_out, *sends, column = refs[2 * (PLANE - 1) :]
-    first = first_kept[0] + sum(item[0].astype(F32) for item in firsts)
-    column[0] = first[:SHARE, :]
-    column[1:] = rest_kept[...] + sum(item[...].astype(F32) for item in rests)
-    end = SMALL_IN_SHARE + LATE_SMALL
-    column[Z - 1, SMALL_IN_SHARE:end, :] += first[SIDE : SIDE + LATE_SMALL, :]
+        item = first[p] + first_in[p].astype(F32)
+        span = slice(p * (Z - 1), (p + 1) * (Z - 1))
+        column[0] = item[:SHARE, :]
+        column[1:] = rest[span] + rest_in[span].astype(F32)
+        column[Z - 1, SMALL_IN_SHARE:end, :] += item[SIDE : SIDE + LATE_SMALL, :]
+        out[...] = column[...].astype(out.dtype)
+
+
+def add_plane_kernel(ids, kept, *refs):
+    arrived = refs[: PLANE - 1]
+    keep_out, *sends, column = refs[PLANE - 1 :]
+    column[...] = kept[...] + sum(item[...].astype(F32) for item in arrived)
     keep_out[...] = column[ids[0]]
     for d, out in enumerate(sends):
         out[...] = column[lax.rem(ids[0] + d + 1, Z)].astype(BF16)
@@ -467,7 +466,7 @@
         attend_kernel, "attend", ids, [allowed, normed, *bufs],
         [like(*shape, kind=BF16) for shape in shapes]
         + [like(SMALL_ROWS, LANES), like(HEAD_ROWS, LANES)],
-        [pltpu.VMEM((FIRST_ROWS, LANES), F32)], us=6,
+        [pltpu.VMEM((FIRST_ROWS, LANES), F32)], us=0.2,
     )
 
 
@@ -502,19 +501,13 @@
     )
 
 
-def attend_back(project, weights, grad_attended):
-    return call(
-        attend_back_kernel, "attend_back", None, [project, weights, grad_attended],
-        [like(*project.shape, kind=BF16)], us=3,
-    )
-
-
-def project_back(ids, grad_project, normed_turned, w_qkv, small, first, send_kind):
+def attend_back(ids, project, weights, grad_attended, normed_turned, w_qkv, small, first, send_kind):
     shape = (PLANE, SIDE + SIDE_ROWS, LANES)
     return call(
-        project_back_kernel, "project_back", ids, [grad_project, normed_turned, w_qkv, small, first],
-        [like(*shape), like(*shape, kind=send_kind)],
-        [pltpu.VMEM((FIRST_ROWS, LANES), F32), pltpu.VMEM(shape[1:], F32)], us=1,
+        attend_back_kernel, "attend_back", ids,
+        [project, weights, grad_attended, normed_turned, w_qkv, small, first],
+        [like(*project.shape, kind=BF16), like(*shape), like(*shape, kind=send_kind)],
+        [pltpu.VMEM((FIRST_ROWS, LANES), F32), pltpu.VMEM(shape[1:], F32)], us=4,
     )
 
 
@@ -534,10 +527,7 @@
     side = jnp.concatenate(
         [jnp.zeros((SIDE - SHARE, LANES), BF16), gathered[ROW_SMALL:ROW_TOTAL]], axis=0
     )
-    firsts = [
-        jnp.stack([jnp.concatenate([shares[0, k], side], axis=0) for k in group])
-        for group in (order[:PLANE], order[PLANE:])
-    ]
+    firsts = [jnp.concatenate([shares[0, k], side], axis=0) for k in order]
     rests = []
     for group in (order[:PLANE], order[PLANE:]):
         rests += [shares[1:, group[0]], jnp.concatenate([shares[1:, k] for k in group[1:]])]
@@ -547,8 +537,9 @@
         ids, tokens, attended, cotangent, small, first, rests, F32
     )
     outputs = result(middle, activated, w_down, small)
-    grad_project = attend_back(project, weights, grad_attended)
-    first, first_send = project_back(ids, grad_project, normed_turned, w_qkv, small, first_grad, F32)
+    grad_project, first, first_send = attend_back(
+        ids, project, weights, grad_attended, normed_turned, w_qkv, small, first_grad, F32
+    )
     input_grad = input_gradient(tokens, grad_project, grad_middle, w_qkv, small)
     first = jnp.stack([first, first_send], axis=1)
     rest = jnp.stack([rest, rest_send]).reshape(2, PLANE, Z - 1, SHARE, LANES).transpose(2, 1, 0, 3, 4)
@@ -584,14 +575,6 @@
 STEPS = (3, 1, 2)
 
 
-def add_core(keep, send):
-    part = (keep.shape[0] // PLANE,) + keep.shape[1:]
-    return call(
-        add_core_kernel, "add_core", None, [keep, send],
-        [like(*part)] + [like(*part, kind=BF16)] * (PLANE - 1),
-    )
-
-
 def local_slice(tokens, params, segment_ids, cotangent):
     me = lax.axis_index("fsdp").astype(jnp.int32)
     z, plane, core = me // (2 * PLANE), (me // 2) % PLANE, me % 2
@@ -606,35 +589,33 @@
         [like(SIDE + SMALL_ROWS, LANES, kind=BF16), like(Z - 1, SHARE, LANES, kind=BF16)],
         [pltpu.VMEM((Z, SHARE, LANES), BF16), pltpu.VMEM((SIDE + SMALL_ROWS, LANES), F32)],
     )
-    firsts = [move(first, 0, d, 0) for d in STEPS]
+    firsts = [first] + [move(first, 0, d, 0) for d in STEPS]
     rests = [move(rest, 0, d, 0) for d in STEPS]
-    firsts = stack([item[None] for item in (first, *firsts)])
-    project, weights, attended, w_qkv, small, first = attend(
-        ids, allowed, normed, [firsts, move(firsts, 0, 0, 1)]
-    )
+    firsts = firsts + [move(item, 0, 0, 1) for item in firsts]
+    project, weights, attended, w_qkv, small, first = attend(ids, allowed, normed, firsts)
     *rests, attended = lax.optimization_barrier((*rests, attended))
     rests = stack(rests)
     rests = [rest, rests, move(rest, 0, 0, 1), move(rests, 0, 0, 1)]
-    middle, activated, grad_middle, grad_attended, w_down, keep, send, first_grad = feed(
+    middle, activated, grad_middle, grad_attended, w_down, rest, send, first_grad = feed(
         ids, tokens, attended, cotangent, small, first, rests, BF16
     )
 
-    received = move(send, 0, 0, 1)
+    rest_in = move(send, 0, 0, 1)
+    grad_project, first, send = attend_back(
+        ids, project, weights, grad_attended, normed_turned, w_qkv, small, first_grad, BF16
+    )
+    first_in = move(send, 0, 0, 1)
+    part = (Z, SHARE, LANES)
+    kept, *sends = call(
+        add_core_kernel, "add_core", None, [first, first_in, rest, rest_in],
+        [like(*part)] + [like(*part, kind=BF16)] * (PLANE - 1), [pltpu.VMEM(part, F32)],
+    )
+    arrived = [move(item, 0, d, 0) for item, d in zip(sends, STEPS)]
     outputs = result(middle, activated, w_down, small)
-    received, outputs = lax.optimization_barrier((received, outputs))
-    rest_kept, *sends = add_core(keep, received)
-    *sends, grad_attended = lax.optimization_barrier((*sends, grad_attended))
-    rest_sums = [move(item, 0, d, 0) for item, d in zip(sends, STEPS)]
-    grad_project = attend_back(project, weights, grad_attended)
-    rest_sums[0], grad_project = lax.optimization_barrier((rest_sums[0], grad_project))
-    keep, send = project_back(ids, grad_project, normed_turned, w_qkv, small, first_grad, BF16)
-    first_kept, *sends = add_core(keep, move(send, 0, 0, 1))
-    first_sums = [move(item, 0, d, 0) for item, d in zip(sends, STEPS)]
     input_grad = input_gradient(tokens, grad_project, grad_middle, w_qkv, small)
     kept, *sends = call(
-        add_plane_kernel, "add_plane", where, [first_kept, rest_kept] + first_sums + rest_sums,
-        [like(SHARE, LANES)] + [like(SHARE, LANES, kind=BF16)] * (Z - 1),
-        [pltpu.VMEM((Z, SHARE, LANES), F32)],
+        add_plane_kernel, "add_plane", where, [kept] + arrived,
+        [like(SHARE, LANES)] + [like(SHARE, LANES, kind=BF16)] * (Z - 1), [pltpu.VMEM(part, F32)],
     )
     arrived = [move(item, d + 1, 0, 0) for d, item in enumerate(sends)]
     param_grad = call(

time: 67.5 us -> 62.2 us (0.921)
  waiting for transfers between devices: 21.5 us -> 15.5 us
    ppermute x23, waiting for transfers between devices: 21.5 us -> 15.5 us  [move(): return lax.ppermute(values, 'fsdp', pairs)]
    pallas_call x14 -> x11, Pallas kernels: 18.7 us -> 19 us  [call(): pl.pallas_call(kernel, in_specs=[SMEM_SPEC] * with_ids + [VMEM_SPEC] * le...]
  transfers between devices with their start and end apart: 23 -> 23, of which waited for: 17 -> 12; matrix products, arithmetic and copies ran while one was open for 0% -> 0% of each run, Pallas kernels for 14% -> 18%
where the time goes in v9:
time: 62.2 us; the launch traced here: 62 us
  starting transfers between devices  24.1 us (39%)
  Pallas kernels  19 us (31%)
  waiting for transfers between devices  15.5 us (25%)
  local copies, waits for them, and re-layouts  2.63 us (4%)
  between operations  0.79 us (1%)
    ppermute x23, starting transfers between devices, move(): return lax.ppermute(values, 'fsdp', pairs)  24.1 us
    pallas_call x11, Pallas kernels, call(): pl.pallas_call(kernel, in_specs=[SMEM_SPEC] * with_ids + [VMEM_SPEC] * le...  19 us
    ppermute x23, waiting for transfers between devices, move(): return lax.ppermute(values, 'fsdp', pairs)  15.5 us
    unnamed x10, local copies, waits for them, and re-layouts  2.54 us
  transfers between devices with their start and end apart: 23, of which 12 were waited for; matrix products, arithmetic and copies ran while one was open for 0% of the time, Pallas kernels for 18%

profile of v9, /device:TPU:0, one launch (start us, length us, event | category | flops | bytes accessed | tf_op | source)
XLA Modules:
  0.0 62.0 jit_solution(15485805453651897309)
XLA Ops:
  0.6 3.1 %collective-permute-start = (bf16[193,128]{1,0:T(8,128)(2,1)}, bf16[193,128]{1,0:T(8,128)(2,1)S(1)}, u32[]{:S(2)}, u32[]{:S(2)}) collective-permute-start(bf16[193,128]{1,0:T(8,128)(2,1)} %params.1), channel_id=1, source_target_pairs={{0,8},{1,9},{2,10},{3,11},{4,12},{5,13},{6,14},{7,15},{8,16},{9,17... | collective-permute-start | bytes 148232 | tf_op jit(solution)/shard_map/ppermute | solution.py:572
  3.7 2.6 %collective-permute-start.1 = (bf16[193,128]{1,0:T(8,128)(2,1)}, bf16[193,128]{1,0:T(8,128)(2,1)S(1)}, u32[]{:S(2)}, u32[]{:S(2)}) collective-permute-start(bf16[193,128]{1,0:T(8,128)(2,1)} %params.1), channel_id=1, source_target_pairs={{0,16},{1,17},{2,18},{3,19},{4,20},{5,21},{6,22},{7,23},{8,24},{9,... | collective-permute-start | bytes 148232 | tf_op jit(solution)/shard_map/ppermute | solution.py:572
  6.3 1.3 %collective-permute-start.2 = (bf16[193,128]{1,0:T(8,128)(2,1)}, bf16[193,128]{1,0:T(8,128)(2,1)S(1)}, u32[]{:S(2)}, u32[]{:S(2)}) collective-permute-start(bf16[193,128]{1,0:T(8,128)(2,1)} %params.1), channel_id=1, source_target_pairs={{0,24},{1,25},{2,26},{3,27},{4,28},{5,29},{6,30},{7,31},{8,0},{9,1... | collective-permute-start | bytes 148232 | tf_op jit(solution)/shard_map/ppermute | solution.py:572
  7.6 1.0 %copy-done.1 = bf16[1024,256]{1,0:T(8,128)(2,1)S(1)} copy-done((bf16[1024,256]{1,0:T(8,128)(2,1)S(1)}, bf16[1024,256]{1,0:T(8,128)(2,1)}, u32[]{:S(2)}) %copy-start.1) | copy-done | bytes 524312
  8.7 0.8 %copy-done.3 = bf16[193,128]{1,0:T(8,128)(2,1)S(1)} copy-done((bf16[193,128]{1,0:T(8,128)(2,1)S(1)}, bf16[193,128]{1,0:T(8,128)(2,1)}, u32[]{:S(2)}) %copy-start.3) | copy-done | bytes 49432
  9.5 0.7 %copy-done.4 = s32[1024]{0:T(1024)S(1)} copy-done((s32[1024]{0:T(1024)S(1)}, s32[1024]{0:T(1024)}, u32[]{:S(2)}) %copy-start.4) | copy-done | bytes 4120
  10.2 0.7 %prepare.1 = (f32[1024,256]{1,0:T(8,128)S(1)}, bf16[256,1024]{1,0:T(8,128)(2,1)S(1)}, bf16[193,128]{1,0:T(8,128)(2,1)S(1)}, f32[1024,128]{1,0:T(8,128)S(1)}) custom-call(bf16[1024,256]{1,0:T(8,128)(2,1)S(1)} %copy-done.1, bf16[193,128]{1,0:T(8,128)(2,1)S(1)} %copy-done.3, s32[8,128]{1,0:T(8,128)S(1)} %bitcast.10), custom_call_target="tpu_custom_call" | custom-call | flops 2000000000 | bytes 1048576 | tf_op jit(solution)/shard_map/prepare/pallas_call | solution.py:430
  10.9 0.1 sort_shares.1
  11.0 2.5 %collective-permute-start.6 = (bf16[240,128]{1,0:T(8,128)(2,1)S(1)}, bf16[240,128]{1,0:T(8,128)(2,1)S(1)}, u32[]{:S(2)}, u32[]{:S(2)}) collective-permute-start(bf16[240,128]{1,0:T(8,128)(2,1)S(1)} %get-tuple-element.42.refs_0_), channel_id=1, source_target_pairs={{0,6},{1,7},{2,4},{3,5},{4,2},{5,3},{6,0},{7,1},{8,14},{9,15},{10,... | collective-permute-start | bytes 184328 | tf_op jit(solution)/shard_map/ppermute | solution.py:572
  13.5 0.5 collective-permute-start.7
  14.0 0.5 collective-permute-start.8
  14.5 2.4 %collective-permute-start.3 = (bf16[3,193,128]{2,1,0:T(8,128)(2,1)S(1)}, bf16[3,193,128]{2,1,0:T(8,128)(2,1)S(1)}, u32[]{:S(2)}, u32[]{:S(2)}) collective-permute-start(bf16[3,193,128]{2,1,0:T(8,128)(2,1)S(1)} %get-tuple-element.39.refs_0_), channel_id=1, source_target_pairs={{0,6},{1,7},{2,4},{3,5},{4,2},{5,3},{6,0},{7,1},{8,14},{9,15},{10,... | collective-permute-start | bytes 444680 | tf_op jit(solution)/shard_map/ppermute | solution.py:572
  17.0 0.5 collective-permute-start.4
  17.5 0.5 collective-permute-start.5
  18.0 0.3 collective-permute-done.7.refs_2_
  18.3 1.4 %collective-permute-done.8.refs_3_ = bf16[240,128]{1,0:T(8,128)(2,1)S(1)} collective-permute-done((bf16[240,128]{1,0:T(8,128)(2,1)S(1)}, bf16[240,128]{1,0:T(8,128)(2,1)S(1)}, u32[]{:S(2)}, u32[]{:S(2)}) %collective-permute-start.8) | collective-permute-done | bytes 61472 | tf_op jit(solution)/shard_map/ppermute | solution.py:572
  19.8 0.5 collective-permute-start.11
  20.3 0.7 %collective-permute-done.10.refs_5_ = bf16[240,128]{1,0:T(8,128)(2,1)S(1)} collective-permute-done((bf16[240,128]{1,0:T(8,128)(2,1)S(1)}, bf16[240,128]{1,0:T(8,128)(2,1)S(1)}, u32[]{:S(2)}, u32[]{:S(2)}) %collective-permute-start.10) | collective-permute-done | bytes 61472 | tf_op jit(solution)/shard_map/ppermute | solution.py:572
  21.0 0.2 collective-permute-start.12
  21.2 0.1 stack.36.ids
  21.3 1.0 %collective-permute-done.12.refs_7_ = bf16[240,128]{1,0:T(8,128)(2,1)S(1)} collective-permute-done((bf16[240,128]{1,0:T(8,128)(2,1)S(1)}, bf16[240,128]{1,0:T(8,128)(2,1)S(1)}, u32[]{:S(2)}, u32[]{:S(2)}) %collective-permute-start.12) | collective-permute-done | bytes 61472 | tf_op jit(solution)/shard_map/ppermute | solution.py:572
  22.3 3.0 %attend.1 = (bf16[1024,768]{1,0:T(8,128)(2,1)S(1)}, bf16[1024,512]{1,0:T(8,128)(2,1)S(1)}, bf16[1024,256]{1,0:T(8,128)(2,1)S(1)}, bf16[256,768]{1,0:T(8,128)(2,1...) custom-call(s32[8]{0:T(128)S(1)} %stack.36.ids, f32[1024,128]{1,0:T(8,128)S(1)} %get-tuple-element.40.allowed, ...), custom_call_target="tpu_custom_call" | custom-call | flops 200000000 | bytes 1048576 | tf_op jit(solution)/shard_map/attend/pallas_call | solution.py:430
  25.3 0.0 copy-start
  25.4 0.2 collective-permute-start.14
  25.6 0.4 collective-permute-start.13
  26.0 1.5 %collective-permute-done.13.refs_2_ = bf16[3,193,128]{2,1,0:T(8,128)(2,1)S(1)} collective-permute-done((bf16[3,193,128]{2,1,0:T(8,128)(2,1)S(1)}, bf16[3,193,128]{2,1,0:T(8,128)(2,1)S(1)}, u32[]{:S(2)}, u32[]{:S(2)}) %collective-permute-start.13) | collective-permute-done | bytes 148256 | tf_op jit(solution)/shard_map/ppermute | solution.py:572
  27.5 6.9 %feed.1 = (f32[1024,256]{1,0:T(8,128)S(1)}, bf16[1024,1024]{1,0:T(8,128)(2,1)S(1)}, f32[1024,256]{1,0:T(8,128)S(1)}, bf16[1024,256]{1,0:T(8,128)(2,1)S(1)}, bf16...) custom-call(s32[8]{0:T(128)S(1)} %stack.36.ids, ...), custom_call_target="tpu_custom_call" | custom-call | flops 8000000000 | bytes 1048576 | tf_op jit(solution)/shard_map/feed/pallas_call | solution.py:430
  34.4 0.2 collective-permute-start.16
  34.6 3.7 %attend_back.1 = (bf16[1024,768]{1,0:T(8,128)(2,1)S(1)}, f32[4,224,128]{2,1,0:T(8,128)S(1)}, bf16[4,224,128]{2,1,0:T(8,128)(2,1)S(1)}) custom-call(s32[8]{0:T(128)S(1)} %stack.36.ids, bf16[1024,768]{1,0:T(8,128)(2,1)S(1)} %get-tuple-element.53.project, bf16[1024,512]{1,0:T(8,128)(2,1)S(1)} %get-tuple-element.54.weights, ...), custom_call_target="tpu_custom_call" | custom-call | flops 4000000000 | bytes 1048576 | tf_op jit(solution)/shard_map/attend_back/pallas_call | solution.py:430
  38.3 0.4 collective-permute-start.15
  38.8 1.1 %collective-permute-done.15.first_in = bf16[4,224,128]{2,1,0:T(8,128)(2,1)S(1)} collective-permute-done((bf16[4,224,128]{2,1,0:T(8,128)(2,1)S(1)}, bf16[4,224,128]{2,1,0:T(8,128)(2,1)S(1)}, u32[]{:S(2)}, u32[]{:S(2)}) %collective-permute-start.15) | collective-permute-done | bytes 229408 | tf_op jit(solution)/shard_map/ppermute | solution.py:572
  39.9 0.2 add_core.1
  40.1 2.2 %collective-permute-start.17 = (bf16[4,193,128]{2,1,0:T(8,128)(2,1)S(1)}, bf16[4,193,128]{2,1,0:T(8,128)(2,1)S(1)}, u32[]{:S(2)}, u32[]{:S(2)}) collective-permute-start(bf16[4,193,128]{2,1,0:T(8,128)(2,1)S(1)} %get-tuple-element.66), channel_id=1, source_target_pairs={{0,6},{1,7},{2,4},{3,5},{4,2},{5,3},{6,0},{7,1},{8,14},{9,15},{10,... | collective-permute-start | bytes 592904 | tf_op jit(solution)/shard_map/ppermute | solution.py:572
  42.3 0.3 collective-permute-start.18
  42.6 1.3 %collective-permute-start.19 = (bf16[4,193,128]{2,1,0:T(8,128)(2,1)S(1)}, bf16[4,193,128]{2,1,0:T(8,128)(2,1)S(1)}, u32[]{:S(2)}, u32[]{:S(2)}) collective-permute-start(bf16[4,193,128]{2,1,0:T(8,128)(2,1)S(1)} %get-tuple-element.68), channel_id=1, source_target_pairs={{0,4},{1,5},{2,6},{3,7},{4,0},{5,1},{6,2},{7,3},{8,12},{9,13},{10,... | collective-permute-start | bytes 592904 | tf_op jit(solution)/shard_map/ppermute | solution.py:572
  43.9 2.1 %input_grad.1 = f32[1024,256]{1,0:T(8,128)} custom-call(bf16[1024,256]{1,0:T(8,128)(2,1)S(1)} %copy-done.2, bf16[1024,768]{1,0:T(8,128)(2,1)S(1)} %get-tuple-element.59.grad_project, f32[1024,256]{1,0:T(8,128)S(1)} %get-tuple-element.60.grad_middle, bf16[256,768]{1,0:T(8,128)(2,1)S(1)} %get-tuple-element.57.w_qkv, f32[32,128]{1,0:T(8,128)S(1)} %get-tuple-element.45.small), custom_call_target="tpu_custom_call" | custom-call | flops 2000000000 | bytes 1048576 | tf_op jit(solution)/shard_map/input_grad/pallas_call | solution.py:430
  45.9 3.1 %collective-permute-done.17.refs_0_ = bf16[4,193,128]{2,1,0:T(8,128)(2,1)S(1)} collective-permute-done((bf16[4,193,128]{2,1,0:T(8,128)(2,1)S(1)}, bf16[4,193,128]{2,1,0:T(8,128)(2,1)S(1)}, u32[]{:S(2)}, u32[]{:S(2)}) %collective-permute-start.17) | collective-permute-done | bytes 197664 | tf_op jit(solution)/shard_map/ppermute | solution.py:572
  49.0 3.4 %collective-permute-done.18.refs_1_ = bf16[4,193,128]{2,1,0:T(8,128)(2,1)S(1)} collective-permute-done((bf16[4,193,128]{2,1,0:T(8,128)(2,1)S(1)}, bf16[4,193,128]{2,1,0:T(8,128)(2,1)S(1)}, u32[]{:S(2)}, u32[]{:S(2)}) %collective-permute-start.18) | collective-permute-done | bytes 197664 | tf_op jit(solution)/shard_map/ppermute | solution.py:572
  52.4 0.4 collective-permute-done.19.refs_2_
  52.8 0.2 add_plane.1
  53.0 2.0 %collective-permute-start.20 = (bf16[193,128]{1,0:T(8,128)(2,1)S(1)}, bf16[193,128]{1,0:T(8,128)(2,1)S(1)}, u32[]{:S(2)}, u32[]{:S(2)}) collective-permute-start(bf16[193,128]{1,0:T(8,128)(2,1)S(1)} %get-tuple-element.70), channel_id=1, source_target_pairs={{0,8},{1,9},{2,10},{3,11},{4,12},{5,13},{6,14},{7,15},{8,16},{9,17... | collective-permute-start | bytes 148232 | tf_op jit(solution)/shard_map/ppermute | solution.py:572
  55.0 1.5 %collective-permute-start.21 = (bf16[193,128]{1,0:T(8,128)(2,1)S(1)}, bf16[193,128]{1,0:T(8,128)(2,1)S(1)}, u32[]{:S(2)}, u32[]{:S(2)}) collective-permute-start(bf16[193,128]{1,0:T(8,128)(2,1)S(1)} %get-tuple-element.71), channel_id=1, source_target_pairs={{0,16},{1,17},{2,18},{3,19},{4,20},{5,21},{6,22},{7,23},{8,24},{9,... | collective-permute-start | bytes 148232 | tf_op jit(solution)/shard_map/ppermute | solution.py:572
  56.4 1.0 %collective-permute-start.22 = (bf16[193,128]{1,0:T(8,128)(2,1)S(1)}, bf16[193,128]{1,0:T(8,128)(2,1)S(1)}, u32[]{:S(2)}, u32[]{:S(2)}) collective-permute-start(bf16[193,128]{1,0:T(8,128)(2,1)S(1)} %get-tuple-element.72), channel_id=1, source_target_pairs={{0,24},{1,25},{2,26},{3,27},{4,28},{5,29},{6,30},{7,31},{8,0},{9,1... | collective-permute-start | bytes 148232 | tf_op jit(solution)/shard_map/ppermute | solution.py:572
  57.4 1.5 %result.1 = bf16[1024,256]{1,0:T(8,128)(2,1)} custom-call(f32[1024,256]{1,0:T(8,128)S(1)} %get-tuple-element.50.middle, bf16[1024,1024]{1,0:T(8,128)(2,1)S(1)} %get-tuple-element.51.activated, bf16[1024,256]{1,0:T(8,128)(2,1)S(1)} %get-tuple-element.52.w_down, f32[32,128]{1,0:T(8,128)S(1)} %get-tuple-element.45.small), custom_call_target="tpu_custom_call" | custom-call | flops 2000000000 | bytes 1048576 | tf_op jit(solution)/shard_map/result/pallas_call | solution.py:430
  58.9 0.3 collective-permute-done.20.refs_0_
  59.3 1.6 %collective-permute-done.21.refs_1_ = bf16[193,128]{1,0:T(8,128)(2,1)S(1)} collective-permute-done((bf16[193,128]{1,0:T(8,128)(2,1)S(1)}, bf16[193,128]{1,0:T(8,128)(2,1)S(1)}, u32[]{:S(2)}, u32[]{:S(2)}) %collective-permute-start.21) | collective-permute-done | bytes 49440 | tf_op jit(solution)/shard_map/ppermute | solution.py:572
  60.9 0.5 collective-permute-done.22.refs_2_
  61.3 0.7 %add_column.1 = f32[193,128]{1,0:T(8,128)} custom-call(f32[193,128]{1,0:T(8,128)S(1)} %get-tuple-element.69.kept, bf16[193,128]{1,0:T(8,128)(2,1)S(1)} %collective-permute-done.20.refs_0_, bf16[193,128]{1,0:T(8,128)(2,1)S(1)} %collective-permute-done.21.refs_1_, bf16[193,128]{1,0:T(8,128)(2,1)S(1)} %collective-permute-done.22.refs_2_), custom_call_target="tpu_custom_call" | custom-call | flops 1000000000 | bytes 1048576 | tf_op jit(solution)/shard_map/add_column/pallas_call | solution.py:430
  (20 shorter events, 0.1 us)
Async XLA Ops:
  0.6 10.2 %collective-permute-start = (bf16[193,128]{1,0:T(8,128)(2,1)}, bf16[193,128]{1,0:T(8,128)(2,1)S(1)}, u32[]{:S(2)}, u32[]{:S(2)}) collective-permute-start(bf16[193,128]{1,0:T(8,128)(2,1)} %params.1), channel_id=1, source_target_pairs={{0,8},{1,9},{2,10},{3,11},{4,12},{5,13},{6,14},{7,15},{8,16},{9,17... | collective-permute-start | bytes 148232 | tf_op jit(solution)/shard_map/ppermute | solution.py:572
  3.7 7.2 %collective-permute-start.1 = (bf16[193,128]{1,0:T(8,128)(2,1)}, bf16[193,128]{1,0:T(8,128)(2,1)S(1)}, u32[]{:S(2)}, u32[]{:S(2)}) collective-permute-start(bf16[193,128]{1,0:T(8,128)(2,1)} %params.1), channel_id=1, source_target_pairs={{0,16},{1,17},{2,18},{3,19},{4,20},{5,21},{6,22},{7,23},{8,24},{9,... | collective-permute-start | bytes 148232 | tf_op jit(solution)/shard_map/ppermute | solution.py:572
  6.3 4.6 %collective-permute-start.2 = (bf16[193,128]{1,0:T(8,128)(2,1)}, bf16[193,128]{1,0:T(8,128)(2,1)S(1)}, u32[]{:S(2)}, u32[]{:S(2)}) collective-permute-start(bf16[193,128]{1,0:T(8,128)(2,1)} %params.1), channel_id=1, source_target_pairs={{0,24},{1,25},{2,26},{3,27},{4,28},{5,29},{6,30},{7,31},{8,0},{9,1... | collective-permute-start | bytes 148232 | tf_op jit(solution)/shard_map/ppermute | solution.py:572
  7.6 1.0 %copy-start.1 = (bf16[1024,256]{1,0:T(8,128)(2,1)S(1)}, bf16[1024,256]{1,0:T(8,128)(2,1)}, u32[]{:S(2)}) copy-start(bf16[1024,256]{1,0:T(8,128)(2,1)} %tok.5) | copy-start | bytes 1572868
  8.7 0.8 %copy-start.3 = (bf16[193,128]{1,0:T(8,128)(2,1)S(1)}, bf16[193,128]{1,0:T(8,128)(2,1)}, u32[]{:S(2)}) copy-start(bf16[193,128]{1,0:T(8,128)(2,1)} %params.1) | copy-start | bytes 148228
  9.5 0.7 %copy-start.4 = (s32[1024]{0:T(1024)S(1)}, s32[1024]{0:T(1024)}, u32[]{:S(2)}) copy-start(s32[1024]{0:T(1024)} %param.6) | copy-start | bytes 12292
  11.0 6.5 %collective-permute-start.6 = (bf16[240,128]{1,0:T(8,128)(2,1)S(1)}, bf16[240,128]{1,0:T(8,128)(2,1)S(1)}, u32[]{:S(2)}, u32[]{:S(2)}) collective-permute-start(bf16[240,128]{1,0:T(8,128)(2,1)S(1)} %get-tuple-element.42.refs_0_), channel_id=1, source_target_pairs={{0,6},{1,7},{2,4},{3,5},{4,2},{5,3},{6,0},{7,1},{8,14},{9,15},{10,... | collective-permute-start | bytes 184328 | tf_op jit(solution)/shard_map/ppermute | solution.py:572
  13.5 4.8 %collective-permute-start.7 = (bf16[240,128]{1,0:T(8,128)(2,1)S(1)}, bf16[240,128]{1,0:T(8,128)(2,1)S(1)}, u32[]{:S(2)}, u32[]{:S(2)}) collective-permute-start(bf16[240,128]{1,0:T(8,128)(2,1)S(1)} %get-tuple-element.42.refs_0_), channel_id=1, source_target_pairs={{0,2},{1,3},{2,0},{3,1},{4,6},{5,7},{6,4},{7,5},{8,10},{9,11},{10,... | collective-permute-start | bytes 184328 | tf_op jit(solution)/shard_map/ppermute | solution.py:572
  14.0 5.8 %collective-permute-start.8 = (bf16[240,128]{1,0:T(8,128)(2,1)S(1)}, bf16[240,128]{1,0:T(8,128)(2,1)S(1)}, u32[]{:S(2)}, u32[]{:S(2)}) collective-permute-start(bf16[240,128]{1,0:T(8,128)(2,1)S(1)} %get-tuple-element.42.refs_0_), channel_id=1, source_target_pairs={{0,4},{1,5},{2,6},{3,7},{4,0},{5,1},{6,2},{7,3},{8,12},{9,13},{10,... | collective-permute-start | bytes 184328 | tf_op jit(solution)/shard_map/ppermute | solution.py:572
  14.5 10.8 %collective-permute-start.3 = (bf16[3,193,128]{2,1,0:T(8,128)(2,1)S(1)}, bf16[3,193,128]{2,1,0:T(8,128)(2,1)S(1)}, u32[]{:S(2)}, u32[]{:S(2)}) collective-permute-start(bf16[3,193,128]{2,1,0:T(8,128)(2,1)S(1)} %get-tuple-element.39.refs_0_), channel_id=1, source_target_pairs={{0,6},{1,7},{2,4},{3,5},{4,2},{5,3},{6,0},{7,1},{8,14},{9,15},{10,... | collective-permute-start | bytes 444680 | tf_op jit(solution)/shard_map/ppermute | solution.py:572
  17.0 8.4 %collective-permute-start.4 = (bf16[3,193,128]{2,1,0:T(8,128)(2,1)S(1)}, bf16[3,193,128]{2,1,0:T(8,128)(2,1)S(1)}, u32[]{:S(2)}, u32[]{:S(2)}) collective-permute-start(bf16[3,193,128]{2,1,0:T(8,128)(2,1)S(1)} %get-tuple-element.39.refs_0_), channel_id=1, source_target_pairs={{0,2},{1,3},{2,0},{3,1},{4,6},{5,7},{6,4},{7,5},{8,10},{9,11},{10,... | collective-permute-start | bytes 444680 | tf_op jit(solution)/shard_map/ppermute | solution.py:572
  17.5 7.8 %collective-permute-start.5 = (bf16[3,193,128]{2,1,0:T(8,128)(2,1)S(1)}, bf16[3,193,128]{2,1,0:T(8,128)(2,1)S(1)}, u32[]{:S(2)}, u32[]{:S(2)}) collective-permute-start(bf16[3,193,128]{2,1,0:T(8,128)(2,1)S(1)} %get-tuple-element.39.refs_0_), channel_id=1, source_target_pairs={{0,4},{1,5},{2,6},{3,7},{4,0},{5,1},{6,2},{7,3},{8,12},{9,13},{10,... | collective-permute-start | bytes 444680 | tf_op jit(solution)/shard_map/ppermute | solution.py:572
  18.3 1.4 %collective-permute-start.9 = (bf16[240,128]{1,0:T(8,128)(2,1)S(1)}, bf16[240,128]{1,0:T(8,128)(2,1)S(1)}, u32[]{:S(2)}, u32[]{:S(2)}) collective-permute-start(bf16[240,128]{1,0:T(8,128)(2,1)S(1)} %get-tuple-element.42.refs_0_), channel_id=1, source_target_pairs={{0,1},{1,0},{2,3},{3,2},{4,5},{5,4},{6,7},{7,6},{8,9},{9,8},{10,11... | collective-permute-start | bytes 184328 | tf_op jit(solution)/shard_map/ppermute | solution.py:572
  19.8 1.2 %collective-permute-start.10 = (bf16[240,128]{1,0:T(8,128)(2,1)S(1)}, bf16[240,128]{1,0:T(8,128)(2,1)S(1)}, u32[]{:S(2)}, u32[]{:S(2)}) collective-permute-start(bf16[240,128]{1,0:T(8,128)(2,1)S(1)} %collective-permute-done.6.refs_1_), channel_id=1, source_target_pairs={{0,1},{1,0},{2,3},{3,2},{4,5},{5,4},{6,7},{7,6},{8,9},{9,8},{10,11... | collective-permute-start | bytes 184328 | tf_op jit(solution)/shard_map/ppermute | solution.py:572
  19.8 1.5 %collective-permute-start.11 = (bf16[240,128]{1,0:T(8,128)(2,1)S(1)}, bf16[240,128]{1,0:T(8,128)(2,1)S(1)}, u32[]{:S(2)}, u32[]{:S(2)}) collective-permute-start(bf16[240,128]{1,0:T(8,128)(2,1)S(1)} %collective-permute-done.7.refs_2_), channel_id=1, source_target_pairs={{0,1},{1,0},{2,3},{3,2},{4,5},{5,4},{6,7},{7,6},{8,9},{9,8},{10,11... | collective-permute-start | bytes 184328 | tf_op jit(solution)/shard_map/ppermute | solution.py:572
  21.0 1.2 %collective-permute-start.12 = (bf16[240,128]{1,0:T(8,128)(2,1)S(1)}, bf16[240,128]{1,0:T(8,128)(2,1)S(1)}, u32[]{:S(2)}, u32[]{:S(2)}) collective-permute-start(bf16[240,128]{1,0:T(8,128)(2,1)S(1)} %collective-permute-done.8.refs_3_), channel_id=1, source_target_pairs={{0,1},{1,0},{2,3},{3,2},{4,5},{5,4},{6,7},{7,6},{8,9},{9,8},{10,11... | collective-permute-start | bytes 184328 | tf_op jit(solution)/shard_map/ppermute | solution.py:572
  25.3 2.2 %copy-start = (bf16[1024,256]{1,0:T(8,128)(2,1)S(1)}, bf16[1024,256]{1,0:T(8,128)(2,1)}, u32[]{:S(2)}) copy-start(bf16[1024,256]{1,0:T(8,128)(2,1)} %cot.1) | copy-start | bytes 1572868
  25.3 2.2 %copy-start.2 = (bf16[1024,256]{1,0:T(8,128)(2,1)S(1)}, bf16[1024,256]{1,0:T(8,128)(2,1)}, u32[]{:S(2)}) copy-start(bf16[1024,256]{1,0:T(8,128)(2,1)} %tok.5) | copy-start | bytes 1572868
  25.4 2.1 %collective-permute-start.14 = (bf16[9,193,128]{2,1,0:T(8,128)(2,1)S(1)}, bf16[9,193,128]{2,1,0:T(8,128)(2,1)S(1)}, u32[]{:S(2)}, u32[]{:S(2)}) collective-permute-start(bf16[9,193,128]{2,1,0:T(8,128)(2,1)S(1)} %stack.37.refs_1_), channel_id=1, source_target_pairs={{0,1},{1,0},{2,3},{3,2},{4,5},{5,4},{6,7},{7,6},{8,9},{9,8},{10,11... | collective-permute-start | bytes 1334024 | tf_op jit(solution)/shard_map/ppermute | solution.py:572
  25.6 1.9 %collective-permute-start.13 = (bf16[3,193,128]{2,1,0:T(8,128)(2,1)S(1)}, bf16[3,193,128]{2,1,0:T(8,128)(2,1)S(1)}, u32[]{:S(2)}, u32[]{:S(2)}) collective-permute-start(bf16[3,193,128]{2,1,0:T(8,128)(2,1)S(1)} %get-tuple-element.39.refs_0_), channel_id=1, source_target_pairs={{0,1},{1,0},{2,3},{3,2},{4,5},{5,4},{6,7},{7,6},{8,9},{9,8},{10,11... | collective-permute-start | bytes 444680 | tf_op jit(solution)/shard_map/ppermute | solution.py:572
  34.4 5.5 %collective-permute-start.16 = (bf16[12,193,128]{2,1,0:T(8,128)(2,1)S(1)}, bf16[12,193,128]{2,1,0:T(8,128)(2,1)S(1)}, u32[]{:S(2)}, u32[]{:S(2)}) collective-permute-start(bf16[12,193,128]{2,1,0:T(8,128)(2,1)S(1)} %get-tuple-element.64), channel_id=1, source_target_pairs={{0,1},{1,0},{2,3},{3,2},{4,5},{5,4},{6,7},{7,6},{8,9},{9,8},{10,11... | collective-permute-start | bytes 1778696 | tf_op jit(solution)/shard_map/ppermute | solution.py:572
  38.3 1.6 %collective-permute-start.15 = (bf16[4,224,128]{2,1,0:T(8,128)(2,1)S(1)}, bf16[4,224,128]{2,1,0:T(8,128)(2,1)S(1)}, u32[]{:S(2)}, u32[]{:S(2)}) collective-permute-start(bf16[4,224,128]{2,1,0:T(8,128)(2,1)S(1)} %get-tuple-element.62), channel_id=1, source_target_pairs={{0,1},{1,0},{2,3},{3,2},{4,5},{5,4},{6,7},{7,6},{8,9},{9,8},{10,11... | collective-permute-start | bytes 688136 | tf_op jit(solution)/shard_map/ppermute | solution.py:572
  40.1 8.9 %collective-permute-start.17 = (bf16[4,193,128]{2,1,0:T(8,128)(2,1)S(1)}, bf16[4,193,128]{2,1,0:T(8,128)(2,1)S(1)}, u32[]{:S(2)}, u32[]{:S(2)}) collective-permute-start(bf16[4,193,128]{2,1,0:T(8,128)(2,1)S(1)} %get-tuple-element.66), channel_id=1, source_target_pairs={{0,6},{1,7},{2,4},{3,5},{4,2},{5,3},{6,0},{7,1},{8,14},{9,15},{10,... | collective-permute-start | bytes 592904 | tf_op jit(solution)/shard_map/ppermute | solution.py:572
  42.3 10.1 %collective-permute-start.18 = (bf16[4,193,128]{2,1,0:T(8,128)(2,1)S(1)}, bf16[4,193,128]{2,1,0:T(8,128)(2,1)S(1)}, u32[]{:S(2)}, u32[]{:S(2)}) collective-permute-start(bf16[4,193,128]{2,1,0:T(8,128)(2,1)S(1)} %get-tuple-element.67), channel_id=1, source_target_pairs={{0,2},{1,3},{2,0},{3,1},{4,6},{5,7},{6,4},{7,5},{8,10},{9,11},{10,... | collective-permute-start | bytes 592904 | tf_op jit(solution)/shard_map/ppermute | solution.py:572
  42.6 10.2 %collective-permute-start.19 = (bf16[4,193,128]{2,1,0:T(8,128)(2,1)S(1)}, bf16[4,193,128]{2,1,0:T(8,128)(2,1)S(1)}, u32[]{:S(2)}, u32[]{:S(2)}) collective-permute-start(bf16[4,193,128]{2,1,0:T(8,128)(2,1)S(1)} %get-tuple-element.68), channel_id=1, source_target_pairs={{0,4},{1,5},{2,6},{3,7},{4,0},{5,1},{6,2},{7,3},{8,12},{9,13},{10,... | collective-permute-start | bytes 592904 | tf_op jit(solution)/shard_map/ppermute | solution.py:572
  53.0 6.3 %collective-permute-start.20 = (bf16[193,128]{1,0:T(8,128)(2,1)S(1)}, bf16[193,128]{1,0:T(8,128)(2,1)S(1)}, u32[]{:S(2)}, u32[]{:S(2)}) collective-permute-start(bf16[193,128]{1,0:T(8,128)(2,1)S(1)} %get-tuple-element.70), channel_id=1, source_target_pairs={{0,8},{1,9},{2,10},{3,11},{4,12},{5,13},{6,14},{7,15},{8,16},{9,17... | collective-permute-start | bytes 148232 | tf_op jit(solution)/shard_map/ppermute | solution.py:572
  55.0 5.9 %collective-permute-start.21 = (bf16[193,128]{1,0:T(8,128)(2,1)S(1)}, bf16[193,128]{1,0:T(8,128)(2,1)S(1)}, u32[]{:S(2)}, u32[]{:S(2)}) collective-permute-start(bf16[193,128]{1,0:T(8,128)(2,1)S(1)} %get-tuple-element.71), channel_id=1, source_target_pairs={{0,16},{1,17},{2,18},{3,19},{4,20},{5,21},{6,22},{7,23},{8,24},{9,... | collective-permute-start | bytes 148232 | tf_op jit(solution)/shard_map/ppermute | solution.py:572
  56.4 4.9 %collective-permute-start.22 = (bf16[193,128]{1,0:T(8,128)(2,1)S(1)}, bf16[193,128]{1,0:T(8,128)(2,1)S(1)}, u32[]{:S(2)}, u32[]{:S(2)}) collective-permute-start(bf16[193,128]{1,0:T(8,128)(2,1)S(1)} %get-tuple-element.72), channel_id=1, source_target_pairs={{0,24},{1,25},{2,26},{3,27},{4,28},{5,29},{6,30},{7,31},{8,0},{9,1... | collective-permute-start | bytes 148232 | tf_op jit(solution)/shard_map/ppermute | solution.py:572

commit v10 on v9

--- a/solution.py
+++ b/solution.py
@@ -158,8 +158,8 @@
         ],
         axis=1,
     )
-    def some(g, carry):
-        span = pl.ds(pl.multiple_of(g * WIDE, WIDE), WIDE)
+    for g in range(normed.shape[0] // WIDE):
+        span = slice(g * WIDE, (g + 1) * WIDE)
         normed_low = (normed[span, :] * gain + shift).astype(BF16)
         project = (dot(normed_low, w_qkv[...]) + bias).astype(BF16)
         project_out[span, :] = project
@@ -173,7 +173,7 @@
         weights = []
         for s in range(GROUP):
             low = []
-            open_pairs = allowed[pl.ds(pl.multiple_of(g * WIDE + s * SEQ, SEQ), SEQ), :] > 0.5
+            open_pairs = allowed[g * WIDE + s * SEQ : g * WIDE + (s + 1) * SEQ, :] > 0.5
             for h in range(HEADS):
                 mine = jnp.where(open_pairs, scores[s][:, h * SEQ : (h + 1) * SEQ], -1e30)
                 grown = jnp.exp(mine - jnp.max(mine, axis=-1, keepdims=True))
@@ -185,9 +185,6 @@
         attended_out[span, :] = jnp.concatenate(
             [dot(weights[s], values[s]).astype(BF16) for s in range(GROUP)], axis=0
         )
-        return carry
-
-    lax.fori_loop(0, normed.shape[0] // WIDE, some, 0)
 
 
 def feed_kernel(
@@ -211,28 +208,30 @@
     matrix_from_flat(flat, ROW_DOWN - ROW_OUT, FF, D, w_down)
 
     gain = small_vector(small, GAIN_TWO, 2)
-    middle = (
-        tok[...].astype(F32) + dot(attended[...], w_out[...]) + small_vector(small, BIAS_OUT, 2)
-    )
-    middle_out[...] = middle
-    normed, rate = normalize(middle)
-    normed_low = (normed * gain + small_vector(small, SHIFT_TWO, 2)).astype(BF16)
-    normed_turned = normed_low.T
-    cotangent = cot[...]
-    cot_turned = cotangent.T
+    shift = small_vector(small, SHIFT_TWO, 2)
+    bias_out = small_vector(small, BIAS_OUT, 2)
     slope = 0.7978845608028654
     cubic = slope * 0.044715
     row_up, row_down = ROW_UP - ROW_OUT, ROW_DOWN - ROW_OUT
-
-    def products(c):
+    spans = [slice(r, r + WIDE) for r in range(0, tok.shape[0], WIDE)]
+    cot_turned = cot[...].T
+
+    def head(span):
+        middle = tok[span, :].astype(F32) + dot(attended[span, :], w_out[...]) + bias_out
+        middle_out[span, :] = middle
+        normed, rate = normalize(middle)
+        normed_low = (normed * gain + shift).astype(BF16)
+        return normed, rate, normed_low, normed_low.T
+
+    def products(span, normed_low, c):
         columns = slice(c, c + CHUNK)
-        return dot(normed_low, w_up[:, columns]), dot_nt(cotangent, w_down[columns, :])
-
-    def bend(c, hidden_all, grad_all):
+        return dot(normed_low, w_up[:, columns]), dot_nt(cot[span, :], w_down[columns, :])
+
+    def bend(span, c, hidden_all, grad_all):
         columns = slice(c, c + CHUNK)
         bias = small_vector(small, BIAS_UP + c // LANES, CHUNK // LANES)
         total = jnp.zeros((8, CHUNK), F32)
-        for r in range(0, tok.shape[0], STRIP):
+        for r in range(0, WIDE, STRIP):
             rows = slice(r, r + STRIP)
             hidden = hidden_all[rows] + bias
             square = hidden * hidden
@@ -240,12 +239,12 @@
             activated = hidden * half
             derivative = half + activated * (1.0 - half) * (2 * slope + (6 * cubic) * square)
             low = (grad_all[rows] * derivative).astype(BF16)
-            activated_out[rows, columns] = activated.astype(BF16)
-            grad_hidden[rows, columns] = low
+            activated_out[span.start + r : span.start + r + STRIP, columns] = activated.astype(BF16)
+            grad_hidden[span.start + r : span.start + r + STRIP, columns] = low
             total += fold_rows(low.astype(F32))
         return total
 
-    def weight_gradients(c):
+    def weight_gradients(normed_turned, c):
         columns = slice(c, c + CHUNK)
         turned_to_flat(dot(cot_turned, activated_out[:, columns]), CHUNK, D, flat, row_down + c * D // LANES)
         grads = dot(normed_turned, grad_hidden[:, columns])
@@ -254,32 +253,42 @@
                 :, j * LANES : (j + 1) * LANES
             ]
 
-    ahead, totals = products(0), []
-    for c in range(0, FF, CHUNK):
-        now = ahead
-        if c + CHUNK < FF:
-            ahead = products(c + CHUNK)
-        if c > 0:
-            weight_gradients(c - CHUNK)
-        totals.append(bend(c, *now))
-    grad_normed = dot_nt(grad_hidden[...], w_up[...])
-    weight_gradients(FF - CHUNK)
-    grad_result = cotangent.astype(F32)
-    grad_middle = grad_result + normalize_back(grad_normed, gain, normed, rate)
-    grad_middle_out[...] = grad_middle
-    grad_middle_low = grad_middle.astype(BF16)
-    grad_attended_out[...] = dot_nt(grad_middle_low, w_out[...]).astype(BF16)
-    matrix_to_flat(dot_tn(attended[...], grad_middle_low), D, D, flat, 0)
-    sums = jnp.concatenate(
-        [
-            fold_rows(grad_middle_low.astype(F32)),
-            fold_rows(grad_normed * normed),
-            fold_rows(grad_normed),
-            *totals,
-            fold_rows(grad_result),
-        ],
-        axis=1,
-    )
+    def tail(span, normed, rate):
+        grad_normed = dot_nt(grad_hidden[span, :], w_up[...])
+        grad_result = cot[span, :].astype(F32)
+        grad_middle = grad_result + normalize_back(grad_normed, gain, normed, rate)
+        grad_middle_out[span, :] = grad_middle
+        low = grad_middle.astype(BF16)
+        grad_attended_out[span, :] = dot_nt(low, w_out[...]).astype(BF16)
+        sums = [low.astype(F32), grad_normed * normed, grad_normed, grad_result]
+        return dot_tn(attended[span, :], low), [fold_rows(item) for item in sums]
+
+    chunks = range(0, FF, CHUNK)
+    heads = [head(spans[0])]
+    totals = [0.0] * len(chunks)
+    grad_out, sums = 0.0, [0.0] * 4
+    for n, span in enumerate(spans):
+        normed, rate, normed_low, _ = heads[n]
+        ahead = products(span, normed_low, 0)
+        if n + 1 < len(spans):
+            heads.append(head(spans[n + 1]))
+        if n > 0:
+            added, more = tail(spans[n - 1], *heads[n - 1][:2])
+            grad_out, sums = grad_out + added, [a + b for a, b in zip(sums, more)]
+        if n + 1 == len(spans):
+            normed_turned = jnp.concatenate([item[3] for item in heads], axis=1)
+        for i, c in enumerate(chunks):
+            now = ahead
+            if c + CHUNK < FF:
+                ahead = products(span, normed_low, c + CHUNK)
+            if n + 1 == len(spans) and c > 0:
+                weight_gradients(normed_turned, c - CHUNK)
+            totals[i] += bend(span, c, *now)
+    added, more = tail(spans[-1], *heads[-1][:2])
+    grad_out, sums = grad_out + added, [a + b for a, b in zip(sums, more)]
+    weight_gradients(normed_turned, FF - CHUNK)
+    matrix_to_flat(grad_out, D, D, flat, 0)
+    sums = jnp.concatenate([*sums[:3], *totals, sums[3]], axis=1)
     sums = jnp.sum(sums, axis=0, keepdims=True)
     base = ROW_SMALL - ROW_OUT
     flat[base : base + LATE_SMALL, :] = jnp.zeros((LATE_SMALL, LANES), F32)
@@ -305,9 +314,9 @@
     ids, project, weights, grad_attended, normed_turned, w_qkv, small, first_in,
     grad_project, keep_out, send_out, flat, wide,
 ):
-    def some(g, carry):
-        base = g * WIDE
-        spans = [pl.ds(pl.multiple_of(base + s * SEQ, SEQ), SEQ) for s in range(GROUP)]
+    products, sums = 0.0, 0.0
+    for g in range(project.shape[0] // WIDE):
+        spans = [slice(r, r + SEQ) for r in range(g * WIDE, (g + 1) * WIDE, SEQ)]
         grad_weights = [
             dot_nt(grad_attended[span, :], spread_heads(project[span, 2 * D :])) for span in spans
         ]
@@ -333,11 +342,10 @@
             grad_project[span, D : 2 * D] = dot(scores_turned[s], query).astype(BF16)
             grad_value = dot(weights_turned[s], spread_heads(grad_attended[span, :]))
             grad_project[span, 2 * D :] = grad_value.astype(BF16)
-        return carry
-
-    lax.fori_loop(0, project.shape[0] // WIDE, some, 0)
-    products = dot(normed_turned[...], grad_project[...])
-    sums = jnp.sum(fold_rows(grad_project[...].astype(F32)), axis=0, keepdims=True)
+        span = slice(g * WIDE, (g + 1) * WIDE)
+        products += dot(normed_turned[:, span], grad_project[span, :])
+        sums += fold_rows(grad_project[span, :].astype(F32))
+    sums = jnp.sum(sums, axis=0, keepdims=True)
     gain = jnp.broadcast_to(small_vector(small, GAIN_ONE, 2), (LANES, D)).T
     shift = jnp.broadcast_to(small_vector(small, SHIFT_ONE, 2), (LANES, D)).T
     grad_gain = jnp.zeros((D, LANES), F32)

time: 62.2 us -> 62.5 us (level)
  transfers between devices with their start and end apart: 23 -> 23, of which waited for: 12 -> 12; matrix products, arithmetic and copies ran while one was open for 0% -> 0% of each run, Pallas kernels for 18% -> 17%
where the time goes in v10:
time: 62.5 us; the launch traced here: 62.3 us
  starting transfers between devices  24.1 us (39%)
  Pallas kernels  19.3 us (31%)
  waiting for transfers between devices  15.5 us (25%)
  local copies, waits for them, and re-layouts  2.63 us (4%)
  between operations  0.79 us (1%)
    ppermute x23, starting transfers between devices, move(): return lax.ppermute(values, 'fsdp', pairs)  24.1 us
    pallas_call x11, Pallas kernels, call(): pl.pallas_call(kernel, in_specs=[SMEM_SPEC] * with_ids + [VMEM_SPEC] * le...  19.3 us
    ppermute x23, waiting for transfers between devices, move(): return lax.ppermute(values, 'fsdp', pairs)  15.5 us
    unnamed x10, local copies, waits for them, and re-layouts  2.54 us
  transfers between devices with their start and end apart: 23, of which 12 were waited for; matrix products, arithmetic and copies ran while one was open for 0% of the time, Pallas kernels for 17%

profile of v10, /device:TPU:0, one launch (start us, length us, event | category | flops | bytes accessed | tf_op | source)
XLA Modules:
  0.0 62.3 jit_solution(12076077563307930562)
XLA Ops:
  0.6 3.1 %collective-permute-start = (bf16[193,128]{1,0:T(8,128)(2,1)}, bf16[193,128]{1,0:T(8,128)(2,1)S(1)}, u32[]{:S(2)}, u32[]{:S(2)}) collective-permute-start(bf16[193,128]{1,0:T(8,128)(2,1)} %params.1), channel_id=1, source_target_pairs={{0,8},{1,9},{2,10},{3,11},{4,12},{5,13},{6,14},{7,15},{8,16},{9,17... | collective-permute-start | bytes 148232 | tf_op jit(solution)/shard_map/ppermute | solution.py:580
  3.7 2.6 %collective-permute-start.1 = (bf16[193,128]{1,0:T(8,128)(2,1)}, bf16[193,128]{1,0:T(8,128)(2,1)S(1)}, u32[]{:S(2)}, u32[]{:S(2)}) collective-permute-start(bf16[193,128]{1,0:T(8,128)(2,1)} %params.1), channel_id=1, source_target_pairs={{0,16},{1,17},{2,18},{3,19},{4,20},{5,21},{6,22},{7,23},{8,24},{9,... | collective-permute-start | bytes 148232 | tf_op jit(solution)/shard_map/ppermute | solution.py:580
  6.3 1.3 %collective-permute-start.2 = (bf16[193,128]{1,0:T(8,128)(2,1)}, bf16[193,128]{1,0:T(8,128)(2,1)S(1)}, u32[]{:S(2)}, u32[]{:S(2)}) collective-permute-start(bf16[193,128]{1,0:T(8,128)(2,1)} %params.1), channel_id=1, source_target_pairs={{0,24},{1,25},{2,26},{3,27},{4,28},{5,29},{6,30},{7,31},{8,0},{9,1... | collective-permute-start | bytes 148232 | tf_op jit(solution)/shard_map/ppermute | solution.py:580
  7.6 1.0 %copy-done.1 = bf16[1024,256]{1,0:T(8,128)(2,1)S(1)} copy-done((bf16[1024,256]{1,0:T(8,128)(2,1)S(1)}, bf16[1024,256]{1,0:T(8,128)(2,1)}, u32[]{:S(2)}) %copy-start.1) | copy-done | bytes 524312
  8.7 0.8 %copy-done.3 = bf16[193,128]{1,0:T(8,128)(2,1)S(1)} copy-done((bf16[193,128]{1,0:T(8,128)(2,1)S(1)}, bf16[193,128]{1,0:T(8,128)(2,1)}, u32[]{:S(2)}) %copy-start.3) | copy-done | bytes 49432
  9.5 0.7 %copy-done.4 = s32[1024]{0:T(1024)S(1)} copy-done((s32[1024]{0:T(1024)S(1)}, s32[1024]{0:T(1024)}, u32[]{:S(2)}) %copy-start.4) | copy-done | bytes 4120
  10.2 0.7 %prepare.1 = (f32[1024,256]{1,0:T(8,128)S(1)}, bf16[256,1024]{1,0:T(8,128)(2,1)S(1)}, bf16[193,128]{1,0:T(8,128)(2,1)S(1)}, f32[1024,128]{1,0:T(8,128)S(1)}) custom-call(bf16[1024,256]{1,0:T(8,128)(2,1)S(1)} %copy-done.1, bf16[193,128]{1,0:T(8,128)(2,1)S(1)} %copy-done.3, s32[8,128]{1,0:T(8,128)S(1)} %bitcast.10), custom_call_target="tpu_custom_call" | custom-call | flops 2000000000 | bytes 1048576 | tf_op jit(solution)/shard_map/prepare/pallas_call | solution.py:438
  10.9 0.1 sort_shares.1
  11.0 2.5 %collective-permute-start.6 = (bf16[240,128]{1,0:T(8,128)(2,1)S(1)}, bf16[240,128]{1,0:T(8,128)(2,1)S(1)}, u32[]{:S(2)}, u32[]{:S(2)}) collective-permute-start(bf16[240,128]{1,0:T(8,128)(2,1)S(1)} %get-tuple-element.42.refs_0_), channel_id=1, source_target_pairs={{0,6},{1,7},{2,4},{3,5},{4,2},{5,3},{6,0},{7,1},{8,14},{9,15},{10,... | collective-permute-start | bytes 184328 | tf_op jit(solution)/shard_map/ppermute | solution.py:580
  13.5 0.5 collective-permute-start.7
  14.0 0.5 collective-permute-start.8
  14.5 2.4 %collective-permute-start.3 = (bf16[3,193,128]{2,1,0:T(8,128)(2,1)S(1)}, bf16[3,193,128]{2,1,0:T(8,128)(2,1)S(1)}, u32[]{:S(2)}, u32[]{:S(2)}) collective-permute-start(bf16[3,193,128]{2,1,0:T(8,128)(2,1)S(1)} %get-tuple-element.39.refs_0_), channel_id=1, source_target_pairs={{0,6},{1,7},{2,4},{3,5},{4,2},{5,3},{6,0},{7,1},{8,14},{9,15},{10,... | collective-permute-start | bytes 444680 | tf_op jit(solution)/shard_map/ppermute | solution.py:580
  17.0 0.5 collective-permute-start.4
  17.5 0.5 collective-permute-start.5
  18.0 0.3 collective-permute-done.7.refs_2_
  18.3 1.4 %collective-permute-done.8.refs_3_ = bf16[240,128]{1,0:T(8,128)(2,1)S(1)} collective-permute-done((bf16[240,128]{1,0:T(8,128)(2,1)S(1)}, bf16[240,128]{1,0:T(8,128)(2,1)S(1)}, u32[]{:S(2)}, u32[]{:S(2)}) %collective-permute-start.8) | collective-permute-done | bytes 61472 | tf_op jit(solution)/shard_map/ppermute | solution.py:580
  19.8 0.5 collective-permute-start.11
  20.3 0.7 %collective-permute-done.10.refs_5_ = bf16[240,128]{1,0:T(8,128)(2,1)S(1)} collective-permute-done((bf16[240,128]{1,0:T(8,128)(2,1)S(1)}, bf16[240,128]{1,0:T(8,128)(2,1)S(1)}, u32[]{:S(2)}, u32[]{:S(2)}) %collective-permute-start.10) | collective-permute-done | bytes 61472 | tf_op jit(solution)/shard_map/ppermute | solution.py:580
  21.0 0.2 collective-permute-start.12
  21.2 0.1 stack.36.ids
  21.3 1.0 %collective-permute-done.12.refs_7_ = bf16[240,128]{1,0:T(8,128)(2,1)S(1)} collective-permute-done((bf16[240,128]{1,0:T(8,128)(2,1)S(1)}, bf16[240,128]{1,0:T(8,128)(2,1)S(1)}, u32[]{:S(2)}, u32[]{:S(2)}) %collective-permute-start.12) | collective-permute-done | bytes 61472 | tf_op jit(solution)/shard_map/ppermute | solution.py:580
  22.3 2.9 %attend.1 = (bf16[1024,768]{1,0:T(8,128)(2,1)S(1)}, bf16[1024,512]{1,0:T(8,128)(2,1)S(1)}, bf16[1024,256]{1,0:T(8,128)(2,1)S(1)}, bf16[256,768]{1,0:T(8,128)(2,1...) custom-call(s32[8]{0:T(128)S(1)} %stack.36.ids, f32[1024,128]{1,0:T(8,128)S(1)} %get-tuple-element.40.allowed, ...), custom_call_target="tpu_custom_call" | custom-call | flops 200000000 | bytes 1048576 | tf_op jit(solution)/shard_map/attend/pallas_call | solution.py:438
  25.2 0.0 copy-start
  25.3 0.2 collective-permute-start.14
  25.5 0.4 collective-permute-start.13
  25.8 1.5 %collective-permute-done.13.refs_2_ = bf16[3,193,128]{2,1,0:T(8,128)(2,1)S(1)} collective-permute-done((bf16[3,193,128]{2,1,0:T(8,128)(2,1)S(1)}, bf16[3,193,128]{2,1,0:T(8,128)(2,1)S(1)}, u32[]{:S(2)}, u32[]{:S(2)}) %collective-permute-start.13) | collective-permute-done | bytes 148256 | tf_op jit(solution)/shard_map/ppermute | solution.py:580
  27.4 7.5 %feed.1 = (f32[1024,256]{1,0:T(8,128)S(1)}, bf16[1024,1024]{1,0:T(8,128)(2,1)S(1)}, f32[1024,256]{1,0:T(8,128)S(1)}, bf16[1024,256]{1,0:T(8,128)(2,1)S(1)}, bf16...) custom-call(s32[8]{0:T(128)S(1)} %stack.36.ids, ...), custom_call_target="tpu_custom_call" | custom-call | flops 8000000000 | bytes 1048576 | tf_op jit(solution)/shard_map/feed/pallas_call | solution.py:438
  34.9 0.2 collective-permute-start.16
  35.2 3.5 %attend_back.1 = (bf16[1024,768]{1,0:T(8,128)(2,1)S(1)}, f32[4,224,128]{2,1,0:T(8,128)S(1)}, bf16[4,224,128]{2,1,0:T(8,128)(2,1)S(1)}) custom-call(s32[8]{0:T(128)S(1)} %stack.36.ids, bf16[1024,768]{1,0:T(8,128)(2,1)S(1)} %get-tuple-element.53.project, bf16[1024,512]{1,0:T(8,128)(2,1)S(1)} %get-tuple-element.54.weights, ...), custom_call_target="tpu_custom_call" | custom-call | flops 4000000000 | bytes 1048576 | tf_op jit(solution)/shard_map/attend_back/pallas_call | solution.py:438
  38.6 0.4 collective-permute-start.15
  39.1 1.1 %collective-permute-done.15.first_in = bf16[4,224,128]{2,1,0:T(8,128)(2,1)S(1)} collective-permute-done((bf16[4,224,128]{2,1,0:T(8,128)(2,1)S(1)}, bf16[4,224,128]{2,1,0:T(8,128)(2,1)S(1)}, u32[]{:S(2)}, u32[]{:S(2)}) %collective-permute-start.15) | collective-permute-done | bytes 229408 | tf_op jit(solution)/shard_map/ppermute | solution.py:580
  40.2 0.2 add_core.1
  40.4 2.2 %collective-permute-start.17 = (bf16[4,193,128]{2,1,0:T(8,128)(2,1)S(1)}, bf16[4,193,128]{2,1,0:T(8,128)(2,1)S(1)}, u32[]{:S(2)}, u32[]{:S(2)}) collective-permute-start(bf16[4,193,128]{2,1,0:T(8,128)(2,1)S(1)} %get-tuple-element.66), channel_id=1, source_target_pairs={{0,6},{1,7},{2,4},{3,5},{4,2},{5,3},{6,0},{7,1},{8,14},{9,15},{10,... | collective-permute-start | bytes 592904 | tf_op jit(solution)/shard_map/ppermute | solution.py:580
  42.6 0.3 collective-permute-start.18
  42.9 1.3 %collective-permute-start.19 = (bf16[4,193,128]{2,1,0:T(8,128)(2,1)S(1)}, bf16[4,193,128]{2,1,0:T(8,128)(2,1)S(1)}, u32[]{:S(2)}, u32[]{:S(2)}) collective-permute-start(bf16[4,193,128]{2,1,0:T(8,128)(2,1)S(1)} %get-tuple-element.68), channel_id=1, source_target_pairs={{0,4},{1,5},{2,6},{3,7},{4,0},{5,1},{6,2},{7,3},{8,12},{9,13},{10,... | collective-permute-start | bytes 592904 | tf_op jit(solution)/shard_map/ppermute | solution.py:580
  44.1 2.1 %input_grad.1 = f32[1024,256]{1,0:T(8,128)} custom-call(bf16[1024,256]{1,0:T(8,128)(2,1)S(1)} %copy-done.2, bf16[1024,768]{1,0:T(8,128)(2,1)S(1)} %get-tuple-element.59.grad_project, f32[1024,256]{1,0:T(8,128)S(1)} %get-tuple-element.60.grad_middle, bf16[256,768]{1,0:T(8,128)(2,1)S(1)} %get-tuple-element.57.w_qkv, f32[32,128]{1,0:T(8,128)S(1)} %get-tuple-element.45.small), custom_call_target="tpu_custom_call" | custom-call | flops 2000000000 | bytes 1048576 | tf_op jit(solution)/shard_map/input_grad/pallas_call | solution.py:438
  46.2 3.1 %collective-permute-done.17.refs_0_ = bf16[4,193,128]{2,1,0:T(8,128)(2,1)S(1)} collective-permute-done((bf16[4,193,128]{2,1,0:T(8,128)(2,1)S(1)}, bf16[4,193,128]{2,1,0:T(8,128)(2,1)S(1)}, u32[]{:S(2)}, u32[]{:S(2)}) %collective-permute-start.17) | collective-permute-done | bytes 197664 | tf_op jit(solution)/shard_map/ppermute | solution.py:580
  49.3 3.4 %collective-permute-done.18.refs_1_ = bf16[4,193,128]{2,1,0:T(8,128)(2,1)S(1)} collective-permute-done((bf16[4,193,128]{2,1,0:T(8,128)(2,1)S(1)}, bf16[4,193,128]{2,1,0:T(8,128)(2,1)S(1)}, u32[]{:S(2)}, u32[]{:S(2)}) %collective-permute-start.18) | collective-permute-done | bytes 197664 | tf_op jit(solution)/shard_map/ppermute | solution.py:580
  52.7 0.4 collective-permute-done.19.refs_2_
  53.1 0.2 add_plane.1
  53.3 1.9 %collective-permute-start.20 = (bf16[193,128]{1,0:T(8,128)(2,1)S(1)}, bf16[193,128]{1,0:T(8,128)(2,1)S(1)}, u32[]{:S(2)}, u32[]{:S(2)}) collective-permute-start(bf16[193,128]{1,0:T(8,128)(2,1)S(1)} %get-tuple-element.70), channel_id=1, source_target_pairs={{0,8},{1,9},{2,10},{3,11},{4,12},{5,13},{6,14},{7,15},{8,16},{9,17... | collective-permute-start | bytes 148232 | tf_op jit(solution)/shard_map/ppermute | solution.py:580
  55.2 1.5 %collective-permute-start.21 = (bf16[193,128]{1,0:T(8,128)(2,1)S(1)}, bf16[193,128]{1,0:T(8,128)(2,1)S(1)}, u32[]{:S(2)}, u32[]{:S(2)}) collective-permute-start(bf16[193,128]{1,0:T(8,128)(2,1)S(1)} %get-tuple-element.71), channel_id=1, source_target_pairs={{0,16},{1,17},{2,18},{3,19},{4,20},{5,21},{6,22},{7,23},{8,24},{9,... | collective-permute-start | bytes 148232 | tf_op jit(solution)/shard_map/ppermute | solution.py:580
  56.7 1.0 %collective-permute-start.22 = (bf16[193,128]{1,0:T(8,128)(2,1)S(1)}, bf16[193,128]{1,0:T(8,128)(2,1)S(1)}, u32[]{:S(2)}, u32[]{:S(2)}) collective-permute-start(bf16[193,128]{1,0:T(8,128)(2,1)S(1)} %get-tuple-element.72), channel_id=1, source_target_pairs={{0,24},{1,25},{2,26},{3,27},{4,28},{5,29},{6,30},{7,31},{8,0},{9,1... | collective-permute-start | bytes 148232 | tf_op jit(solution)/shard_map/ppermute | solution.py:580
  57.7 1.5 %result.1 = bf16[1024,256]{1,0:T(8,128)(2,1)} custom-call(f32[1024,256]{1,0:T(8,128)S(1)} %get-tuple-element.50.middle, bf16[1024,1024]{1,0:T(8,128)(2,1)S(1)} %get-tuple-element.51.activated, bf16[1024,256]{1,0:T(8,128)(2,1)S(1)} %get-tuple-element.52.w_down, f32[32,128]{1,0:T(8,128)S(1)} %get-tuple-element.45.small), custom_call_target="tpu_custom_call" | custom-call | flops 2000000000 | bytes 1048576 | tf_op jit(solution)/shard_map/result/pallas_call | solution.py:438
  59.2 0.3 collective-permute-done.20.refs_0_
  59.5 1.6 %collective-permute-done.21.refs_1_ = bf16[193,128]{1,0:T(8,128)(2,1)S(1)} collective-permute-done((bf16[193,128]{1,0:T(8,128)(2,1)S(1)}, bf16[193,128]{1,0:T(8,128)(2,1)S(1)}, u32[]{:S(2)}, u32[]{:S(2)}) %collective-permute-start.21) | collective-permute-done | bytes 49440 | tf_op jit(solution)/shard_map/ppermute | solution.py:580
  61.1 0.5 collective-permute-done.22.refs_2_
  61.6 0.7 %add_column.1 = f32[193,128]{1,0:T(8,128)} custom-call(f32[193,128]{1,0:T(8,128)S(1)} %get-tuple-element.69.kept, bf16[193,128]{1,0:T(8,128)(2,1)S(1)} %collective-permute-done.20.refs_0_, bf16[193,128]{1,0:T(8,128)(2,1)S(1)} %collective-permute-done.21.refs_1_, bf16[193,128]{1,0:T(8,128)(2,1)S(1)} %collective-permute-done.22.refs_2_), custom_call_target="tpu_custom_call" | custom-call | flops 1000000000 | bytes 1048576 | tf_op jit(solution)/shard_map/add_column/pallas_call | solution.py:438
  (20 shorter events, 0.1 us)
Async XLA Ops:
  0.6 10.2 %collective-permute-start = (bf16[193,128]{1,0:T(8,128)(2,1)}, bf16[193,128]{1,0:T(8,128)(2,1)S(1)}, u32[]{:S(2)}, u32[]{:S(2)}) collective-permute-start(bf16[193,128]{1,0:T(8,128)(2,1)} %params.1), channel_id=1, source_target_pairs={{0,8},{1,9},{2,10},{3,11},{4,12},{5,13},{6,14},{7,15},{8,16},{9,17... | collective-permute-start | bytes 148232 | tf_op jit(solution)/shard_map/ppermute | solution.py:580
  3.7 7.2 %collective-permute-start.1 = (bf16[193,128]{1,0:T(8,128)(2,1)}, bf16[193,128]{1,0:T(8,128)(2,1)S(1)}, u32[]{:S(2)}, u32[]{:S(2)}) collective-permute-start(bf16[193,128]{1,0:T(8,128)(2,1)} %params.1), channel_id=1, source_target_pairs={{0,16},{1,17},{2,18},{3,19},{4,20},{5,21},{6,22},{7,23},{8,24},{9,... | collective-permute-start | bytes 148232 | tf_op jit(solution)/shard_map/ppermute | solution.py:580
  6.3 4.6 %collective-permute-start.2 = (bf16[193,128]{1,0:T(8,128)(2,1)}, bf16[193,128]{1,0:T(8,128)(2,1)S(1)}, u32[]{:S(2)}, u32[]{:S(2)}) collective-permute-start(bf16[193,128]{1,0:T(8,128)(2,1)} %params.1), channel_id=1, source_target_pairs={{0,24},{1,25},{2,26},{3,27},{4,28},{5,29},{6,30},{7,31},{8,0},{9,1... | collective-permute-start | bytes 148232 | tf_op jit(solution)/shard_map/ppermute | solution.py:580
  7.6 1.0 %copy-start.1 = (bf16[1024,256]{1,0:T(8,128)(2,1)S(1)}, bf16[1024,256]{1,0:T(8,128)(2,1)}, u32[]{:S(2)}) copy-start(bf16[1024,256]{1,0:T(8,128)(2,1)} %tok.5) | copy-start | bytes 1572868
  8.7 0.8 %copy-start.3 = (bf16[193,128]{1,0:T(8,128)(2,1)S(1)}, bf16[193,128]{1,0:T(8,128)(2,1)}, u32[]{:S(2)}) copy-start(bf16[193,128]{1,0:T(8,128)(2,1)} %params.1) | copy-start | bytes 148228
  9.5 0.7 %copy-start.4 = (s32[1024]{0:T(1024)S(1)}, s32[1024]{0:T(1024)}, u32[]{:S(2)}) copy-start(s32[1024]{0:T(1024)} %param.6) | copy-start | bytes 12292
  11.0 6.5 %collective-permute-start.6 = (bf16[240,128]{1,0:T(8,128)(2,1)S(1)}, bf16[240,128]{1,0:T(8,128)(2,1)S(1)}, u32[]{:S(2)}, u32[]{:S(2)}) collective-permute-start(bf16[240,128]{1,0:T(8,128)(2,1)S(1)} %get-tuple-element.42.refs_0_), channel_id=1, source_target_pairs={{0,6},{1,7},{2,4},{3,5},{4,2},{5,3},{6,0},{7,1},{8,14},{9,15},{10,... | collective-permute-start | bytes 184328 | tf_op jit(solution)/shard_map/ppermute | solution.py:580
  13.5 4.8 %collective-permute-start.7 = (bf16[240,128]{1,0:T(8,128)(2,1)S(1)}, bf16[240,128]{1,0:T(8,128)(2,1)S(1)}, u32[]{:S(2)}, u32[]{:S(2)}) collective-permute-start(bf16[240,128]{1,0:T(8,128)(2,1)S(1)} %get-tuple-element.42.refs_0_), channel_id=1, source_target_pairs={{0,2},{1,3},{2,0},{3,1},{4,6},{5,7},{6,4},{7,5},{8,10},{9,11},{10,... | collective-permute-start | bytes 184328 | tf_op jit(solution)/shard_map/ppermute | solution.py:580
  14.0 5.8 %collective-permute-start.8 = (bf16[240,128]{1,0:T(8,128)(2,1)S(1)}, bf16[240,128]{1,0:T(8,128)(2,1)S(1)}, u32[]{:S(2)}, u32[]{:S(2)}) collective-permute-start(bf16[240,128]{1,0:T(8,128)(2,1)S(1)} %get-tuple-element.42.refs_0_), channel_id=1, source_target_pairs={{0,4},{1,5},{2,6},{3,7},{4,0},{5,1},{6,2},{7,3},{8,12},{9,13},{10,... | collective-permute-start | bytes 184328 | tf_op jit(solution)/shard_map/ppermute | solution.py:580
  14.5 10.6 %collective-permute-start.3 = (bf16[3,193,128]{2,1,0:T(8,128)(2,1)S(1)}, bf16[3,193,128]{2,1,0:T(8,128)(2,1)S(1)}, u32[]{:S(2)}, u32[]{:S(2)}) collective-permute-start(bf16[3,193,128]{2,1,0:T(8,128)(2,1)S(1)} %get-tuple-element.39.refs_0_), channel_id=1, source_target_pairs={{0,6},{1,7},{2,4},{3,5},{4,2},{5,3},{6,0},{7,1},{8,14},{9,15},{10,... | collective-permute-start | bytes 444680 | tf_op jit(solution)/shard_map/ppermute | solution.py:580
  17.0 8.2 %collective-permute-start.4 = (bf16[3,193,128]{2,1,0:T(8,128)(2,1)S(1)}, bf16[3,193,128]{2,1,0:T(8,128)(2,1)S(1)}, u32[]{:S(2)}, u32[]{:S(2)}) collective-permute-start(bf16[3,193,128]{2,1,0:T(8,128)(2,1)S(1)} %get-tuple-element.39.refs_0_), channel_id=1, source_target_pairs={{0,2},{1,3},{2,0},{3,1},{4,6},{5,7},{6,4},{7,5},{8,10},{9,11},{10,... | collective-permute-start | bytes 444680 | tf_op jit(solution)/shard_map/ppermute | solution.py:580
  17.5 7.7 %collective-permute-start.5 = (bf16[3,193,128]{2,1,0:T(8,128)(2,1)S(1)}, bf16[3,193,128]{2,1,0:T(8,128)(2,1)S(1)}, u32[]{:S(2)}, u32[]{:S(2)}) collective-permute-start(bf16[3,193,128]{2,1,0:T(8,128)(2,1)S(1)} %get-tuple-element.39.refs_0_), channel_id=1, source_target_pairs={{0,4},{1,5},{2,6},{3,7},{4,0},{5,1},{6,2},{7,3},{8,12},{9,13},{10,... | collective-permute-start | bytes 444680 | tf_op jit(solution)/shard_map/ppermute | solution.py:580
  18.3 1.4 %collective-permute-start.9 = (bf16[240,128]{1,0:T(8,128)(2,1)S(1)}, bf16[240,128]{1,0:T(8,128)(2,1)S(1)}, u32[]{:S(2)}, u32[]{:S(2)}) collective-permute-start(bf16[240,128]{1,0:T(8,128)(2,1)S(1)} %get-tuple-element.42.refs_0_), channel_id=1, source_target_pairs={{0,1},{1,0},{2,3},{3,2},{4,5},{5,4},{6,7},{7,6},{8,9},{9,8},{10,11... | collective-permute-start | bytes 184328 | tf_op jit(solution)/shard_map/ppermute | solution.py:580
  19.8 1.2 %collective-permute-start.10 = (bf16[240,128]{1,0:T(8,128)(2,1)S(1)}, bf16[240,128]{1,0:T(8,128)(2,1)S(1)}, u32[]{:S(2)}, u32[]{:S(2)}) collective-permute-start(bf16[240,128]{1,0:T(8,128)(2,1)S(1)} %collective-permute-done.6.refs_1_), channel_id=1, source_target_pairs={{0,1},{1,0},{2,3},{3,2},{4,5},{5,4},{6,7},{7,6},{8,9},{9,8},{10,11... | collective-permute-start | bytes 184328 | tf_op jit(solution)/shard_map/ppermute | solution.py:580
  19.8 1.5 %collective-permute-start.11 = (bf16[240,128]{1,0:T(8,128)(2,1)S(1)}, bf16[240,128]{1,0:T(8,128)(2,1)S(1)}, u32[]{:S(2)}, u32[]{:S(2)}) collective-permute-start(bf16[240,128]{1,0:T(8,128)(2,1)S(1)} %collective-permute-done.7.refs_2_), channel_id=1, source_target_pairs={{0,1},{1,0},{2,3},{3,2},{4,5},{5,4},{6,7},{7,6},{8,9},{9,8},{10,11... | collective-permute-start | bytes 184328 | tf_op jit(solution)/shard_map/ppermute | solution.py:580
  21.0 1.2 %collective-permute-start.12 = (bf16[240,128]{1,0:T(8,128)(2,1)S(1)}, bf16[240,128]{1,0:T(8,128)(2,1)S(1)}, u32[]{:S(2)}, u32[]{:S(2)}) collective-permute-start(bf16[240,128]{1,0:T(8,128)(2,1)S(1)} %collective-permute-done.8.refs_3_), channel_id=1, source_target_pairs={{0,1},{1,0},{2,3},{3,2},{4,5},{5,4},{6,7},{7,6},{8,9},{9,8},{10,11... | collective-permute-start | bytes 184328 | tf_op jit(solution)/shard_map/ppermute | solution.py:580
  25.2 2.2 %copy-start = (bf16[1024,256]{1,0:T(8,128)(2,1)S(1)}, bf16[1024,256]{1,0:T(8,128)(2,1)}, u32[]{:S(2)}) copy-start(bf16[1024,256]{1,0:T(8,128)(2,1)} %cot.1) | copy-start | bytes 1572868
  25.2 2.2 %copy-start.2 = (bf16[1024,256]{1,0:T(8,128)(2,1)S(1)}, bf16[1024,256]{1,0:T(8,128)(2,1)}, u32[]{:S(2)}) copy-start(bf16[1024,256]{1,0:T(8,128)(2,1)} %tok.5) | copy-start | bytes 1572868
  25.3 2.1 %collective-permute-start.14 = (bf16[9,193,128]{2,1,0:T(8,128)(2,1)S(1)}, bf16[9,193,128]{2,1,0:T(8,128)(2,1)S(1)}, u32[]{:S(2)}, u32[]{:S(2)}) collective-permute-start(bf16[9,193,128]{2,1,0:T(8,128)(2,1)S(1)} %stack.37.refs_1_), channel_id=1, source_target_pairs={{0,1},{1,0},{2,3},{3,2},{4,5},{5,4},{6,7},{7,6},{8,9},{9,8},{10,11... | collective-permute-start | bytes 1334024 | tf_op jit(solution)/shard_map/ppermute | solution.py:580
  25.5 1.9 %collective-permute-start.13 = (bf16[3,193,128]{2,1,0:T(8,128)(2,1)S(1)}, bf16[3,193,128]{2,1,0:T(8,128)(2,1)S(1)}, u32[]{:S(2)}, u32[]{:S(2)}) collective-permute-start(bf16[3,193,128]{2,1,0:T(8,128)(2,1)S(1)} %get-tuple-element.39.refs_0_), channel_id=1, source_target_pairs={{0,1},{1,0},{2,3},{3,2},{4,5},{5,4},{6,7},{7,6},{8,9},{9,8},{10,11... | collective-permute-start | bytes 444680 | tf_op jit(solution)/shard_map/ppermute | solution.py:580
  34.9 5.3 %collective-permute-start.16 = (bf16[12,193,128]{2,1,0:T(8,128)(2,1)S(1)}, bf16[12,193,128]{2,1,0:T(8,128)(2,1)S(1)}, u32[]{:S(2)}, u32[]{:S(2)}) collective-permute-start(bf16[12,193,128]{2,1,0:T(8,128)(2,1)S(1)} %get-tuple-element.64), channel_id=1, source_target_pairs={{0,1},{1,0},{2,3},{3,2},{4,5},{5,4},{6,7},{7,6},{8,9},{9,8},{10,11... | collective-permute-start | bytes 1778696 | tf_op jit(solution)/shard_map/ppermute | solution.py:580
  38.6 1.6 %collective-permute-start.15 = (bf16[4,224,128]{2,1,0:T(8,128)(2,1)S(1)}, bf16[4,224,128]{2,1,0:T(8,128)(2,1)S(1)}, u32[]{:S(2)}, u32[]{:S(2)}) collective-permute-start(bf16[4,224,128]{2,1,0:T(8,128)(2,1)S(1)} %get-tuple-element.62), channel_id=1, source_target_pairs={{0,1},{1,0},{2,3},{3,2},{4,5},{5,4},{6,7},{7,6},{8,9},{9,8},{10,11... | collective-permute-start | bytes 688136 | tf_op jit(solution)/shard_map/ppermute | solution.py:580
  40.4 8.9 %collective-permute-start.17 = (bf16[4,193,128]{2,1,0:T(8,128)(2,1)S(1)}, bf16[4,193,128]{2,1,0:T(8,128)(2,1)S(1)}, u32[]{:S(2)}, u32[]{:S(2)}) collective-permute-start(bf16[4,193,128]{2,1,0:T(8,128)(2,1)S(1)} %get-tuple-element.66), channel_id=1, source_target_pairs={{0,6},{1,7},{2,4},{3,5},{4,2},{5,3},{6,0},{7,1},{8,14},{9,15},{10,... | collective-permute-start | bytes 592904 | tf_op jit(solution)/shard_map/ppermute | solution.py:580
  42.6 10.1 %collective-permute-start.18 = (bf16[4,193,128]{2,1,0:T(8,128)(2,1)S(1)}, bf16[4,193,128]{2,1,0:T(8,128)(2,1)S(1)}, u32[]{:S(2)}, u32[]{:S(2)}) collective-permute-start(bf16[4,193,128]{2,1,0:T(8,128)(2,1)S(1)} %get-tuple-element.67), channel_id=1, source_target_pairs={{0,2},{1,3},{2,0},{3,1},{4,6},{5,7},{6,4},{7,5},{8,10},{9,11},{10,... | collective-permute-start | bytes 592904 | tf_op jit(solution)/shard_map/ppermute | solution.py:580
  42.9 10.2 %collective-permute-start.19 = (bf16[4,193,128]{2,1,0:T(8,128)(2,1)S(1)}, bf16[4,193,128]{2,1,0:T(8,128)(2,1)S(1)}, u32[]{:S(2)}, u32[]{:S(2)}) collective-permute-start(bf16[4,193,128]{2,1,0:T(8,128)(2,1)S(1)} %get-tuple-element.68), channel_id=1, source_target_pairs={{0,4},{1,5},{2,6},{3,7},{4,0},{5,1},{6,2},{7,3},{8,12},{9,13},{10,... | collective-permute-start | bytes 592904 | tf_op jit(solution)/shard_map/ppermute | solution.py:580
  53.3 6.2 %collective-permute-start.20 = (bf16[193,128]{1,0:T(8,128)(2,1)S(1)}, bf16[193,128]{1,0:T(8,128)(2,1)S(1)}, u32[]{:S(2)}, u32[]{:S(2)}) collective-permute-start(bf16[193,128]{1,0:T(8,128)(2,1)S(1)} %get-tuple-element.70), channel_id=1, source_target_pairs={{0,8},{1,9},{2,10},{3,11},{4,12},{5,13},{6,14},{7,15},{8,16},{9,17... | collective-permute-start | bytes 148232 | tf_op jit(solution)/shard_map/ppermute | solution.py:580
  55.2 5.9 %collective-permute-start.21 = (bf16[193,128]{1,0:T(8,128)(2,1)S(1)}, bf16[193,128]{1,0:T(8,128)(2,1)S(1)}, u32[]{:S(2)}, u32[]{:S(2)}) collective-permute-start(bf16[193,128]{1,0:T(8,128)(2,1)S(1)} %get-tuple-element.71), channel_id=1, source_target_pairs={{0,16},{1,17},{2,18},{3,19},{4,20},{5,21},{6,22},{7,23},{8,24},{9,... | collective-permute-start | bytes 148232 | tf_op jit(solution)/shard_map/ppermute | solution.py:580
  56.7 4.9 %collective-permute-start.22 = (bf16[193,128]{1,0:T(8,128)(2,1)S(1)}, bf16[193,128]{1,0:T(8,128)(2,1)S(1)}, u32[]{:S(2)}, u32[]{:S(2)}) collective-permute-start(bf16[193,128]{1,0:T(8,128)(2,1)S(1)} %get-tuple-element.72), channel_id=1, source_target_pairs={{0,24},{1,25},{2,26},{3,27},{4,28},{5,29},{6,30},{7,31},{8,0},{9,1... | collective-permute-start | bytes 148232 | tf_op jit(solution)/shard_map/ppermute | solution.py:580

commit v11 on v9

--- a/solution.py
+++ b/solution.py
@@ -38,6 +38,7 @@
 FIRST_ROWS = 2 * PLANE * SHARE
 HEAD_ROWS = FIRST_ROWS - ROW_OUT
 SIDE, SIDE_ROWS = 208, 16
+PARTS = (slice(0, 96), slice(96, SHARE))
 SMALL_IN_SHARE = ROW_SMALL - (2 * PLANE * Z - 1) * SHARE
 
 F32 = jnp.float32
@@ -158,8 +159,8 @@
         ],
         axis=1,
     )
-    def some(g, carry):
-        span = pl.ds(pl.multiple_of(g * WIDE, WIDE), WIDE)
+    for g in range(normed.shape[0] // WIDE):
+        span = slice(g * WIDE, (g + 1) * WIDE)
         normed_low = (normed[span, :] * gain + shift).astype(BF16)
         project = (dot(normed_low, w_qkv[...]) + bias).astype(BF16)
         project_out[span, :] = project
@@ -173,7 +174,7 @@
         weights = []
         for s in range(GROUP):
             low = []
-            open_pairs = allowed[pl.ds(pl.multiple_of(g * WIDE + s * SEQ, SEQ), SEQ), :] > 0.5
+            open_pairs = allowed[g * WIDE + s * SEQ : g * WIDE + (s + 1) * SEQ, :] > 0.5
             for h in range(HEADS):
                 mine = jnp.where(open_pairs, scores[s][:, h * SEQ : (h + 1) * SEQ], -1e30)
                 grown = jnp.exp(mine - jnp.max(mine, axis=-1, keepdims=True))
@@ -185,9 +186,6 @@
         attended_out[span, :] = jnp.concatenate(
             [dot(weights[s], values[s]).astype(BF16) for s in range(GROUP)], axis=0
         )
-        return carry
-
-    lax.fori_loop(0, normed.shape[0] // WIDE, some, 0)
 
 
 def feed_kernel(
@@ -305,9 +303,9 @@
     ids, project, weights, grad_attended, normed_turned, w_qkv, small, first_in,
     grad_project, keep_out, send_out, flat, wide,
 ):
-    def some(g, carry):
-        base = g * WIDE
-        spans = [pl.ds(pl.multiple_of(base + s * SEQ, SEQ), SEQ) for s in range(GROUP)]
+    products, sums = 0.0, 0.0
+    for g in range(project.shape[0] // WIDE):
+        spans = [slice(r, r + SEQ) for r in range(g * WIDE, (g + 1) * WIDE, SEQ)]
         grad_weights = [
             dot_nt(grad_attended[span, :], spread_heads(project[span, 2 * D :])) for span in spans
         ]
@@ -333,11 +331,10 @@
             grad_project[span, D : 2 * D] = dot(scores_turned[s], query).astype(BF16)
             grad_value = dot(weights_turned[s], spread_heads(grad_attended[span, :]))
             grad_project[span, 2 * D :] = grad_value.astype(BF16)
-        return carry
-
-    lax.fori_loop(0, project.shape[0] // WIDE, some, 0)
-    products = dot(normed_turned[...], grad_project[...])
-    sums = jnp.sum(fold_rows(grad_project[...].astype(F32)), axis=0, keepdims=True)
+        span = slice(g * WIDE, (g + 1) * WIDE)
+        products += dot(normed_turned[:, span], grad_project[span, :])
+        sums += fold_rows(grad_project[span, :].astype(F32))
+    sums = jnp.sum(sums, axis=0, keepdims=True)
     gain = jnp.broadcast_to(small_vector(small, GAIN_ONE, 2), (LANES, D)).T
     shift = jnp.broadcast_to(small_vector(small, SHIFT_ONE, 2), (LANES, D)).T
     grad_gain = jnp.zeros((D, LANES), F32)
@@ -389,16 +386,18 @@
         row += ref.shape[0]
 
 
-def add_core_kernel(first, first_in, rest, rest_in, keep_out, *refs):
-    sends, column = refs[:-1], refs[-1]
+def add_core_kernel(first, first_in, rest, rest_in, *refs):
+    outs, column = refs[:-1], refs[-1]
     end = SMALL_IN_SHARE + LATE_SMALL
-    for p, out in enumerate((keep_out, *sends)):
+    for p in range(PLANE):
         item = first[p] + first_in[p].astype(F32)
         span = slice(p * (Z - 1), (p + 1) * (Z - 1))
         column[0] = item[:SHARE, :]
         column[1:] = rest[span] + rest_in[span].astype(F32)
         column[Z - 1, SMALL_IN_SHARE:end, :] += item[SIDE : SIDE + LATE_SMALL, :]
-        out[...] = column[...].astype(out.dtype)
+        for part, rows in enumerate(PARTS):
+            out = outs[p * len(PARTS) + part]
+            out[...] = column[:, rows, :].astype(out.dtype)
 
 
 def add_plane_kernel(ids, kept, *refs):
@@ -410,8 +409,10 @@
         out[...] = column[lax.rem(ids[0] + d + 1, Z)].astype(BF16)
 
 
-def add_column_kernel(kept, *refs):
-    refs[-1][...] = kept[...] + sum(item[...].astype(F32) for item in refs[:-1])
+def add_column_kernel(*refs):
+    for part, rows in enumerate(PARTS):
+        kept, *arrived = refs[part * Z : (part + 1) * Z]
+        refs[-1][rows, :] = kept[...] + sum(item[...].astype(F32) for item in arrived)
 
 
 def like(*shape, kind=F32):
@@ -605,22 +606,26 @@
         ids, project, weights, grad_attended, normed_turned, w_qkv, small, first_grad, BF16
     )
     first_in = move(send, 0, 0, 1)
-    part = (Z, SHARE, LANES)
-    kept, *sends = call(
+    parts = [(Z, rows.stop - rows.start, LANES) for rows in PARTS]
+    sums = call(
         add_core_kernel, "add_core", None, [first, first_in, rest, rest_in],
-        [like(*part)] + [like(*part, kind=BF16)] * (PLANE - 1), [pltpu.VMEM(part, F32)],
-    )
-    arrived = [move(item, 0, d, 0) for item, d in zip(sends, STEPS)]
+        [like(*part, kind=BF16 if p else F32) for p in range(PLANE) for part in parts],
+        [pltpu.VMEM((Z, SHARE, LANES), F32)],
+    )
+    sums = [sums[n::2] for n in range(2)]
+    grad_project, *sums[0] = lax.optimization_barrier((grad_project, *sums[0]))
     outputs = result(middle, activated, w_down, small)
     input_grad = input_gradient(tokens, grad_project, grad_middle, w_qkv, small)
-    kept, *sends = call(
-        add_plane_kernel, "add_plane", where, [kept] + arrived,
-        [like(SHARE, LANES)] + [like(SHARE, LANES, kind=BF16)] * (Z - 1), [pltpu.VMEM(part, F32)],
-    )
-    arrived = [move(item, d + 1, 0, 0) for d, item in enumerate(sends)]
-    param_grad = call(
-        add_column_kernel, "add_column", None, [kept] + arrived, [like(SHARE, LANES)]
-    )
+    input_grad, *sums[1] = lax.optimization_barrier((input_grad, *sums[1]))
+    arrived = [[move(item, 0, d, 0) for item, d in zip(part[1:], STEPS)] for part in sums]
+    columns = []
+    for n, part in enumerate(parts):
+        kept, *sends = call(
+            add_plane_kernel, "add_plane", where, [sums[n][0]] + arrived[n],
+            [like(*part[1:])] + [like(*part[1:], kind=BF16)] * (Z - 1), [pltpu.VMEM(part, F32)],
+        )
+        columns += [kept] + [move(item, d + 1, 0, 0) for d, item in enumerate(sends)]
+    param_grad = call(add_column_kernel, "add_column", None, columns, [like(SHARE, LANES)])
     return outputs, input_grad, param_grad
 
 

time: 62.2 us -> 62.1 us (level)
  starting transfers between devices: 24.1 us -> 32.7 us
  waiting for transfers between devices: 15.5 us -> 7.07 us
    ppermute x23 -> x29, starting transfers between devices: 24.1 us -> 32.7 us  [move(): return lax.ppermute(values, 'fsdp', pairs)]
    ppermute x23 -> x29, waiting for transfers between devices: 15.5 us -> 7.07 us  [move(): return lax.ppermute(values, 'fsdp', pairs)]
    pallas_call x11 -> x12, Pallas kernels: 19 us -> 18.7 us  [call(): pl.pallas_call(kernel, in_specs=[SMEM_SPEC] * with_ids + [VMEM_SPEC] * le...]
  transfers between devices with their start and end apart: 23 -> 29, of which waited for: 12 -> 8; matrix products, arithmetic and copies ran while one was open for 0% -> 0% of each run, Pallas kernels for 18% -> 17%
where the time goes in v11:
time: 62.1 us; the launch traced here: 61.9 us
  starting transfers between devices  32.7 us (53%)
  Pallas kernels  18.7 us (30%)
  waiting for transfers between devices  7.07 us (11%)
  local copies, waits for them, and re-layouts  2.63 us (4%)
  between operations  0.8 us (1%)
    ppermute x29, starting transfers between devices, move(): return lax.ppermute(values, 'fsdp', pairs)  32.7 us
    pallas_call x12, Pallas kernels, call(): pl.pallas_call(kernel, in_specs=[SMEM_SPEC] * with_ids + [VMEM_SPEC] * le...  18.7 us
    ppermute x29, waiting for transfers between devices, move(): return lax.ppermute(values, 'fsdp', pairs)  7.07 us
    unnamed x10, local copies, waits for them, and re-layouts  2.54 us
  transfers between devices with their start and end apart: 29, of which 8 were waited for; matrix products, arithmetic and copies ran while one was open for 0% of the time, Pallas kernels for 17%

profile of v11, /device:TPU:0, one launch (start us, length us, event | category | flops | bytes accessed | tf_op | source)
XLA Modules:
  0.0 61.9 jit_solution(3664746321592821097)
XLA Ops:
  0.6 3.1 %collective-permute-start = (bf16[193,128]{1,0:T(8,128)(2,1)}, bf16[193,128]{1,0:T(8,128)(2,1)S(1)}, u32[]{:S(2)}, u32[]{:S(2)}) collective-permute-start(bf16[193,128]{1,0:T(8,128)(2,1)} %params.1), channel_id=1, source_target_pairs={{0,8},{1,9},{2,10},{3,11},{4,12},{5,13},{6,14},{7,15},{8,16},{9,17... | collective-permute-start | bytes 148232 | tf_op jit(solution)/shard_map/ppermute | solution.py:573
  3.7 2.6 %collective-permute-start.1 = (bf16[193,128]{1,0:T(8,128)(2,1)}, bf16[193,128]{1,0:T(8,128)(2,1)S(1)}, u32[]{:S(2)}, u32[]{:S(2)}) collective-permute-start(bf16[193,128]{1,0:T(8,128)(2,1)} %params.1), channel_id=1, source_target_pairs={{0,16},{1,17},{2,18},{3,19},{4,20},{5,21},{6,22},{7,23},{8,24},{9,... | collective-permute-start | bytes 148232 | tf_op jit(solution)/shard_map/ppermute | solution.py:573
  6.3 1.3 %collective-permute-start.2 = (bf16[193,128]{1,0:T(8,128)(2,1)}, bf16[193,128]{1,0:T(8,128)(2,1)S(1)}, u32[]{:S(2)}, u32[]{:S(2)}) collective-permute-start(bf16[193,128]{1,0:T(8,128)(2,1)} %params.1), channel_id=1, source_target_pairs={{0,24},{1,25},{2,26},{3,27},{4,28},{5,29},{6,30},{7,31},{8,0},{9,1... | collective-permute-start | bytes 148232 | tf_op jit(solution)/shard_map/ppermute | solution.py:573
  7.6 1.0 %copy-done.1 = bf16[1024,256]{1,0:T(8,128)(2,1)S(1)} copy-done((bf16[1024,256]{1,0:T(8,128)(2,1)S(1)}, bf16[1024,256]{1,0:T(8,128)(2,1)}, u32[]{:S(2)}) %copy-start.1) | copy-done | bytes 524312
  8.7 0.8 %copy-done.3 = bf16[193,128]{1,0:T(8,128)(2,1)S(1)} copy-done((bf16[193,128]{1,0:T(8,128)(2,1)S(1)}, bf16[193,128]{1,0:T(8,128)(2,1)}, u32[]{:S(2)}) %copy-start.3) | copy-done | bytes 49432
  9.5 0.7 %copy-done.4 = s32[1024]{0:T(1024)S(1)} copy-done((s32[1024]{0:T(1024)S(1)}, s32[1024]{0:T(1024)}, u32[]{:S(2)}) %copy-start.4) | copy-done | bytes 4120
  10.2 0.7 %prepare.1 = (f32[1024,256]{1,0:T(8,128)S(1)}, bf16[256,1024]{1,0:T(8,128)(2,1)S(1)}, bf16[193,128]{1,0:T(8,128)(2,1)S(1)}, f32[1024,128]{1,0:T(8,128)S(1)}) custom-call(bf16[1024,256]{1,0:T(8,128)(2,1)S(1)} %copy-done.1, bf16[193,128]{1,0:T(8,128)(2,1)S(1)} %copy-done.3, s32[8,128]{1,0:T(8,128)S(1)} %bitcast.10), custom_call_target="tpu_custom_call" | custom-call | flops 2000000000 | bytes 1048576 | tf_op jit(solution)/shard_map/prepare/pallas_call | solution.py:431
  11.0 2.5 %collective-permute-start.6 = (bf16[240,128]{1,0:T(8,128)(2,1)S(1)}, bf16[240,128]{1,0:T(8,128)(2,1)S(1)}, u32[]{:S(2)}, u32[]{:S(2)}) collective-permute-start(bf16[240,128]{1,0:T(8,128)(2,1)S(1)} %get-tuple-element.60.refs_0_), channel_id=1, source_target_pairs={{0,6},{1,7},{2,4},{3,5},{4,2},{5,3},{6,0},{7,1},{8,14},{9,15},{10,... | collective-permute-start | bytes 184328 | tf_op jit(solution)/shard_map/ppermute | solution.py:573
  13.5 0.5 collective-permute-start.7
  14.0 0.5 collective-permute-start.8
  14.5 2.4 %collective-permute-start.3 = (bf16[3,193,128]{2,1,0:T(8,128)(2,1)S(1)}, bf16[3,193,128]{2,1,0:T(8,128)(2,1)S(1)}, u32[]{:S(2)}, u32[]{:S(2)}) collective-permute-start(bf16[3,193,128]{2,1,0:T(8,128)(2,1)S(1)} %get-tuple-element.57.refs_0_), channel_id=1, source_target_pairs={{0,6},{1,7},{2,4},{3,5},{4,2},{5,3},{6,0},{7,1},{8,14},{9,15},{10,... | collective-permute-start | bytes 444680 | tf_op jit(solution)/shard_map/ppermute | solution.py:573
  17.0 0.5 collective-permute-start.4
  17.5 0.5 collective-permute-start.5
  18.0 0.3 collective-permute-done.7.refs_2_
  18.3 1.4 %collective-permute-done.8.refs_3_ = bf16[240,128]{1,0:T(8,128)(2,1)S(1)} collective-permute-done((bf16[240,128]{1,0:T(8,128)(2,1)S(1)}, bf16[240,128]{1,0:T(8,128)(2,1)S(1)}, u32[]{:S(2)}, u32[]{:S(2)}) %collective-permute-start.8) | collective-permute-done | bytes 61472 | tf_op jit(solution)/shard_map/ppermute | solution.py:573
  19.8 0.5 collective-permute-start.11
  20.3 0.7 %collective-permute-done.10.refs_5_ = bf16[240,128]{1,0:T(8,128)(2,1)S(1)} collective-permute-done((bf16[240,128]{1,0:T(8,128)(2,1)S(1)}, bf16[240,128]{1,0:T(8,128)(2,1)S(1)}, u32[]{:S(2)}, u32[]{:S(2)}) %collective-permute-start.10) | collective-permute-done | bytes 61472 | tf_op jit(solution)/shard_map/ppermute | solution.py:573
  21.0 0.2 collective-permute-start.12
  21.2 0.1 stack.36.ids
  21.3 1.0 %collective-permute-done.12.refs_7_ = bf16[240,128]{1,0:T(8,128)(2,1)S(1)} collective-permute-done((bf16[240,128]{1,0:T(8,128)(2,1)S(1)}, bf16[240,128]{1,0:T(8,128)(2,1)S(1)}, u32[]{:S(2)}, u32[]{:S(2)}) %collective-permute-start.12) | collective-permute-done | bytes 61472 | tf_op jit(solution)/shard_map/ppermute | solution.py:573
  22.3 2.9 %attend.1 = (bf16[1024,768]{1,0:T(8,128)(2,1)S(1)}, bf16[1024,512]{1,0:T(8,128)(2,1)S(1)}, bf16[1024,256]{1,0:T(8,128)(2,1)S(1)}, bf16[256,768]{1,0:T(8,128)(2,1...) custom-call(s32[8]{0:T(128)S(1)} %stack.36.ids, f32[1024,128]{1,0:T(8,128)S(1)} %get-tuple-element.58.allowed, ...), custom_call_target="tpu_custom_call" | custom-call | flops 200000000 | bytes 1048576 | tf_op jit(solution)/shard_map/attend/pallas_call | solution.py:431
  25.3 0.2 collective-permute-start.14
  25.5 0.4 collective-permute-start.13
  25.8 1.5 %collective-permute-done.13.refs_2_ = bf16[3,193,128]{2,1,0:T(8,128)(2,1)S(1)} collective-permute-done((bf16[3,193,128]{2,1,0:T(8,128)(2,1)S(1)}, bf16[3,193,128]{2,1,0:T(8,128)(2,1)S(1)}, u32[]{:S(2)}, u32[]{:S(2)}) %collective-permute-start.13) | collective-permute-done | bytes 148256 | tf_op jit(solution)/shard_map/ppermute | solution.py:573
  27.4 6.9 %feed.1 = (f32[1024,256]{1,0:T(8,128)S(1)}, bf16[1024,1024]{1,0:T(8,128)(2,1)S(1)}, f32[1024,256]{1,0:T(8,128)S(1)}, bf16[1024,256]{1,0:T(8,128)(2,1)S(1)}, bf16...) custom-call(s32[8]{0:T(128)S(1)} %stack.36.ids, ...), custom_call_target="tpu_custom_call" | custom-call | flops 8000000000 | bytes 1048576 | tf_op jit(solution)/shard_map/feed/pallas_call | solution.py:431
  34.3 0.2 collective-permute-start.16
  34.5 3.5 %attend_back.1 = (bf16[1024,768]{1,0:T(8,128)(2,1)S(1)}, f32[4,224,128]{2,1,0:T(8,128)S(1)}, bf16[4,224,128]{2,1,0:T(8,128)(2,1)S(1)}) custom-call(s32[8]{0:T(128)S(1)} %stack.36.ids, bf16[1024,768]{1,0:T(8,128)(2,1)S(1)} %get-tuple-element.71.project, bf16[1024,512]{1,0:T(8,128)(2,1)S(1)} %get-tuple-element.72.weights, ...), custom_call_target="tpu_custom_call" | custom-call | flops 4000000000 | bytes 1048576 | tf_op jit(solution)/shard_map/attend_back/pallas_call | solution.py:431
  38.0 0.4 collective-permute-start.15
  38.4 1.1 %collective-permute-done.15.first_in = bf16[4,224,128]{2,1,0:T(8,128)(2,1)S(1)} collective-permute-done((bf16[4,224,128]{2,1,0:T(8,128)(2,1)S(1)}, bf16[4,224,128]{2,1,0:T(8,128)(2,1)S(1)}, u32[]{:S(2)}, u32[]{:S(2)}) %collective-permute-start.15) | collective-permute-done | bytes 229408 | tf_op jit(solution)/shard_map/ppermute | solution.py:573
  39.6 0.2 add_core.1
  39.8 2.2 %collective-permute-start.17 = (bf16[4,96,128]{2,1,0:T(8,128)(2,1)S(1)}, bf16[4,96,128]{2,1,0:T(8,128)(2,1)S(1)}, u32[]{:S(2)}, u32[]{:S(2)}) collective-permute-start(bf16[4,96,128]{2,1,0:T(8,128)(2,1)S(1)} %get-tuple-element.94), channel_id=1, source_target_pairs={{0,6},{1,7},{2,4},{3,5},{4,2},{5,3},{6,0},{7,1},{8,14},{9,15},{10,... | collective-permute-start | bytes 294920 | tf_op jit(solution)/shard_map/ppermute | solution.py:573
  42.0 0.3 collective-permute-start.18
  42.3 1.3 %collective-permute-start.19 = (bf16[4,96,128]{2,1,0:T(8,128)(2,1)S(1)}, bf16[4,96,128]{2,1,0:T(8,128)(2,1)S(1)}, u32[]{:S(2)}, u32[]{:S(2)}) collective-permute-start(bf16[4,96,128]{2,1,0:T(8,128)(2,1)S(1)} %get-tuple-element.96), channel_id=1, source_target_pairs={{0,4},{1,5},{2,6},{3,7},{4,0},{5,1},{6,2},{7,3},{8,12},{9,13},{10,... | collective-permute-start | bytes 294920 | tf_op jit(solution)/shard_map/ppermute | solution.py:573
  43.5 2.1 %input_grad.1 = f32[1024,256]{1,0:T(8,128)} custom-call(bf16[1024,256]{1,0:T(8,128)(2,1)S(1)} %copy-done.2, bf16[1024,768]{1,0:T(8,128)(2,1)S(1)} %get-tuple-element.86.grad_project, f32[1024,256]{1,0:T(8,128)S(1)} %get-tuple-element.87.grad_middle, bf16[256,768]{1,0:T(8,128)(2,1)S(1)} %get-tuple-element.75.w_qkv, f32[32,128]{1,0:T(8,128)S(1)} %get-tuple-element.63.small), custom_call_target="tpu_custom_call" | custom-call | flops 2000000000 | bytes 1048576 | tf_op jit(solution)/shard_map/input_grad/pallas_call | solution.py:431
  45.6 1.9 %collective-permute-start.23 = (bf16[4,97,128]{2,1,0:T(8,128)(2,1)S(1)}, bf16[4,97,128]{2,1,0:T(8,128)(2,1)S(1)}, u32[]{:S(2)}, u32[]{:S(2)}) collective-permute-start(bf16[4,97,128]{2,1,0:T(8,128)(2,1)S(1)} %get-tuple-element.102), channel_id=1, source_target_pairs={{0,6},{1,7},{2,4},{3,5},{4,2},{5,3},{6,0},{7,1},{8,14},{9,15},{10,... | collective-permute-start | bytes 297992 | tf_op jit(solution)/shard_map/ppermute | solution.py:573
  47.5 0.3 collective-permute-start.24
  47.8 1.3 %collective-permute-start.25 = (bf16[4,97,128]{2,1,0:T(8,128)(2,1)S(1)}, bf16[4,97,128]{2,1,0:T(8,128)(2,1)S(1)}, u32[]{:S(2)}, u32[]{:S(2)}) collective-permute-start(bf16[4,97,128]{2,1,0:T(8,128)(2,1)S(1)} %get-tuple-element.104), channel_id=1, source_target_pairs={{0,4},{1,5},{2,6},{3,7},{4,0},{5,1},{6,2},{7,3},{8,12},{9,13},{10,... | collective-permute-start | bytes 297992 | tf_op jit(solution)/shard_map/ppermute | solution.py:573
  49.1 1.8 %collective-permute-start.20 = (bf16[96,128]{1,0:T(8,128)(2,1)S(1)}, bf16[96,128]{1,0:T(8,128)(2,1)S(1)}, u32[]{:S(2)}, u32[]{:S(2)}) collective-permute-start(bf16[96,128]{1,0:T(8,128)(2,1)S(1)} %get-tuple-element.98), channel_id=1, source_target_pairs={{0,8},{1,9},{2,10},{3,11},{4,12},{5,13},{6,14},{7,15},{8,16},{9,17... | collective-permute-start | bytes 73736 | tf_op jit(solution)/shard_map/ppermute | solution.py:573
  50.9 1.5 %collective-permute-start.21 = (bf16[96,128]{1,0:T(8,128)(2,1)S(1)}, bf16[96,128]{1,0:T(8,128)(2,1)S(1)}, u32[]{:S(2)}, u32[]{:S(2)}) collective-permute-start(bf16[96,128]{1,0:T(8,128)(2,1)S(1)} %get-tuple-element.99), channel_id=1, source_target_pairs={{0,16},{1,17},{2,18},{3,19},{4,20},{5,21},{6,22},{7,23},{8,24},{9,... | collective-permute-start | bytes 73736 | tf_op jit(solution)/shard_map/ppermute | solution.py:573
  52.4 2.4 %collective-permute-start.22 = (bf16[96,128]{1,0:T(8,128)(2,1)S(1)}, bf16[96,128]{1,0:T(8,128)(2,1)S(1)}, u32[]{:S(2)}, u32[]{:S(2)}) collective-permute-start(bf16[96,128]{1,0:T(8,128)(2,1)S(1)} %get-tuple-element.100), channel_id=1, source_target_pairs={{0,24},{1,25},{2,26},{3,27},{4,28},{5,29},{6,30},{7,31},{8,0},{9,1... | collective-permute-start | bytes 73736 | tf_op jit(solution)/shard_map/ppermute | solution.py:573
  54.8 0.1 add_plane.3
  54.9 0.1 collective-permute-start.26
  55.0 1.6 %collective-permute-start.27 = (bf16[97,128]{1,0:T(8,128)(2,1)S(1)}, bf16[97,128]{1,0:T(8,128)(2,1)S(1)}, u32[]{:S(2)}, u32[]{:S(2)}) collective-permute-start(bf16[97,128]{1,0:T(8,128)(2,1)S(1)} %get-tuple-element.107), channel_id=1, source_target_pairs={{0,16},{1,17},{2,18},{3,19},{4,20},{5,21},{6,22},{7,23},{8,24},{9,... | collective-permute-start | bytes 74504 | tf_op jit(solution)/shard_map/ppermute | solution.py:573
  56.6 2.2 %collective-permute-start.28 = (bf16[97,128]{1,0:T(8,128)(2,1)S(1)}, bf16[97,128]{1,0:T(8,128)(2,1)S(1)}, u32[]{:S(2)}, u32[]{:S(2)}) collective-permute-start(bf16[97,128]{1,0:T(8,128)(2,1)S(1)} %get-tuple-element.108), channel_id=1, source_target_pairs={{0,24},{1,25},{2,26},{3,27},{4,28},{5,29},{6,30},{7,31},{8,0},{9,1... | collective-permute-start | bytes 74504 | tf_op jit(solution)/shard_map/ppermute | solution.py:573
  58.8 1.5 %result.1 = bf16[1024,256]{1,0:T(8,128)(2,1)} custom-call(f32[1024,256]{1,0:T(8,128)S(1)} %get-tuple-element.68.middle, bf16[1024,1024]{1,0:T(8,128)(2,1)S(1)} %get-tuple-element.69.activated, bf16[1024,256]{1,0:T(8,128)(2,1)S(1)} %get-tuple-element.70.w_down, f32[32,128]{1,0:T(8,128)S(1)} %get-tuple-element.63.small), custom_call_target="tpu_custom_call" | custom-call | flops 2000000000 | bytes 1048576 | tf_op jit(solution)/shard_map/result/pallas_call | solution.py:431
  60.3 0.3 collective-permute-done.26.refs_5_
  60.6 0.6 collective-permute-done.28.refs_7_
  61.2 0.7 %add_column.1 = f32[193,128]{1,0:T(8,128)} custom-call(f32[96,128]{1,0:T(8,128)S(1)} %get-tuple-element.97.refs_0_, bf16[96,128]{1,0:T(8,128)(2,1)S(1)} %collective-permute-done.20.refs_1_, bf16[96,128]{1,0:T(8,128)(2,1)S(1)} %collective-permute-done.21.refs_2_, bf16[96,128]{1,0:T(8,128)(2,1)S(1)} %collective-permute-done.22.refs_3_, ...), custom_call_target="tpu_custom_call" | custom-call | flops 1000000000 | bytes 1048576 | tf_op jit(solution)/shard_map/add_column/pallas_call | solution.py:431
  (33 shorter events, 0.2 us)
Async XLA Ops:
  0.6 10.2 %collective-permute-start = (bf16[193,128]{1,0:T(8,128)(2,1)}, bf16[193,128]{1,0:T(8,128)(2,1)S(1)}, u32[]{:S(2)}, u32[]{:S(2)}) collective-permute-start(bf16[193,128]{1,0:T(8,128)(2,1)} %params.1), channel_id=1, source_target_pairs={{0,8},{1,9},{2,10},{3,11},{4,12},{5,13},{6,14},{7,15},{8,16},{9,17... | collective-permute-start | bytes 148232 | tf_op jit(solution)/shard_map/ppermute | solution.py:573
  3.7 7.2 %collective-permute-start.1 = (bf16[193,128]{1,0:T(8,128)(2,1)}, bf16[193,128]{1,0:T(8,128)(2,1)S(1)}, u32[]{:S(2)}, u32[]{:S(2)}) collective-permute-start(bf16[193,128]{1,0:T(8,128)(2,1)} %params.1), channel_id=1, source_target_pairs={{0,16},{1,17},{2,18},{3,19},{4,20},{5,21},{6,22},{7,23},{8,24},{9,... | collective-permute-start | bytes 148232 | tf_op jit(solution)/shard_map/ppermute | solution.py:573
  6.3 4.6 %collective-permute-start.2 = (bf16[193,128]{1,0:T(8,128)(2,1)}, bf16[193,128]{1,0:T(8,128)(2,1)S(1)}, u32[]{:S(2)}, u32[]{:S(2)}) collective-permute-start(bf16[193,128]{1,0:T(8,128)(2,1)} %params.1), channel_id=1, source_target_pairs={{0,24},{1,25},{2,26},{3,27},{4,28},{5,29},{6,30},{7,31},{8,0},{9,1... | collective-permute-start | bytes 148232 | tf_op jit(solution)/shard_map/ppermute | solution.py:573
  7.6 1.0 %copy-start.1 = (bf16[1024,256]{1,0:T(8,128)(2,1)S(1)}, bf16[1024,256]{1,0:T(8,128)(2,1)}, u32[]{:S(2)}) copy-start(bf16[1024,256]{1,0:T(8,128)(2,1)} %tok.5) | copy-start | bytes 1572868
  8.7 0.8 %copy-start.3 = (bf16[193,128]{1,0:T(8,128)(2,1)S(1)}, bf16[193,128]{1,0:T(8,128)(2,1)}, u32[]{:S(2)}) copy-start(bf16[193,128]{1,0:T(8,128)(2,1)} %params.1) | copy-start | bytes 148228
  9.5 0.7 %copy-start.4 = (s32[1024]{0:T(1024)S(1)}, s32[1024]{0:T(1024)}, u32[]{:S(2)}) copy-start(s32[1024]{0:T(1024)} %param.6) | copy-start | bytes 12292
  11.0 6.5 %collective-permute-start.6 = (bf16[240,128]{1,0:T(8,128)(2,1)S(1)}, bf16[240,128]{1,0:T(8,128)(2,1)S(1)}, u32[]{:S(2)}, u32[]{:S(2)}) collective-permute-start(bf16[240,128]{1,0:T(8,128)(2,1)S(1)} %get-tuple-element.60.refs_0_), channel_id=1, source_target_pairs={{0,6},{1,7},{2,4},{3,5},{4,2},{5,3},{6,0},{7,1},{8,14},{9,15},{10,... | collective-permute-start | bytes 184328 | tf_op jit(solution)/shard_map/ppermute | solution.py:573
  13.5 4.8 %collective-permute-start.7 = (bf16[240,128]{1,0:T(8,128)(2,1)S(1)}, bf16[240,128]{1,0:T(8,128)(2,1)S(1)}, u32[]{:S(2)}, u32[]{:S(2)}) collective-permute-start(bf16[240,128]{1,0:T(8,128)(2,1)S(1)} %get-tuple-element.60.refs_0_), channel_id=1, source_target_pairs={{0,2},{1,3},{2,0},{3,1},{4,6},{5,7},{6,4},{7,5},{8,10},{9,11},{10,... | collective-permute-start | bytes 184328 | tf_op jit(solution)/shard_map/ppermute | solution.py:573
  14.0 5.8 %collective-permute-start.8 = (bf16[240,128]{1,0:T(8,128)(2,1)S(1)}, bf16[240,128]{1,0:T(8,128)(2,1)S(1)}, u32[]{:S(2)}, u32[]{:S(2)}) collective-permute-start(bf16[240,128]{1,0:T(8,128)(2,1)S(1)} %get-tuple-element.60.refs_0_), channel_id=1, source_target_pairs={{0,4},{1,5},{2,6},{3,7},{4,0},{5,1},{6,2},{7,3},{8,12},{9,13},{10,... | collective-permute-start | bytes 184328 | tf_op jit(solution)/shard_map/ppermute | solution.py:573
  14.5 10.6 %collective-permute-start.3 = (bf16[3,193,128]{2,1,0:T(8,128)(2,1)S(1)}, bf16[3,193,128]{2,1,0:T(8,128)(2,1)S(1)}, u32[]{:S(2)}, u32[]{:S(2)}) collective-permute-start(bf16[3,193,128]{2,1,0:T(8,128)(2,1)S(1)} %get-tuple-element.57.refs_0_), channel_id=1, source_target_pairs={{0,6},{1,7},{2,4},{3,5},{4,2},{5,3},{6,0},{7,1},{8,14},{9,15},{10,... | collective-permute-start | bytes 444680 | tf_op jit(solution)/shard_map/ppermute | solution.py:573
  17.0 8.2 %collective-permute-start.4 = (bf16[3,193,128]{2,1,0:T(8,128)(2,1)S(1)}, bf16[3,193,128]{2,1,0:T(8,128)(2,1)S(1)}, u32[]{:S(2)}, u32[]{:S(2)}) collective-permute-start(bf16[3,193,128]{2,1,0:T(8,128)(2,1)S(1)} %get-tuple-element.57.refs_0_), channel_id=1, source_target_pairs={{0,2},{1,3},{2,0},{3,1},{4,6},{5,7},{6,4},{7,5},{8,10},{9,11},{10,... | collective-permute-start | bytes 444680 | tf_op jit(solution)/shard_map/ppermute | solution.py:573
  17.5 7.7 %collective-permute-start.5 = (bf16[3,193,128]{2,1,0:T(8,128)(2,1)S(1)}, bf16[3,193,128]{2,1,0:T(8,128)(2,1)S(1)}, u32[]{:S(2)}, u32[]{:S(2)}) collective-permute-start(bf16[3,193,128]{2,1,0:T(8,128)(2,1)S(1)} %get-tuple-element.57.refs_0_), channel_id=1, source_target_pairs={{0,4},{1,5},{2,6},{3,7},{4,0},{5,1},{6,2},{7,3},{8,12},{9,13},{10,... | collective-permute-start | bytes 444680 | tf_op jit(solution)/shard_map/ppermute | solution.py:573
  18.3 1.4 %collective-permute-start.9 = (bf16[240,128]{1,0:T(8,128)(2,1)S(1)}, bf16[240,128]{1,0:T(8,128)(2,1)S(1)}, u32[]{:S(2)}, u32[]{:S(2)}) collective-permute-start(bf16[240,128]{1,0:T(8,128)(2,1)S(1)} %get-tuple-element.60.refs_0_), channel_id=1, source_target_pairs={{0,1},{1,0},{2,3},{3,2},{4,5},{5,4},{6,7},{7,6},{8,9},{9,8},{10,11... | collective-permute-start | bytes 184328 | tf_op jit(solution)/shard_map/ppermute | solution.py:573
  19.8 1.2 %collective-permute-start.10 = (bf16[240,128]{1,0:T(8,128)(2,1)S(1)}, bf16[240,128]{1,0:T(8,128)(2,1)S(1)}, u32[]{:S(2)}, u32[]{:S(2)}) collective-permute-start(bf16[240,128]{1,0:T(8,128)(2,1)S(1)} %collective-permute-done.6.refs_1_), channel_id=1, source_target_pairs={{0,1},{1,0},{2,3},{3,2},{4,5},{5,4},{6,7},{7,6},{8,9},{9,8},{10,11... | collective-permute-start | bytes 184328 | tf_op jit(solution)/shard_map/ppermute | solution.py:573
  19.8 1.5 %collective-permute-start.11 = (bf16[240,128]{1,0:T(8,128)(2,1)S(1)}, bf16[240,128]{1,0:T(8,128)(2,1)S(1)}, u32[]{:S(2)}, u32[]{:S(2)}) collective-permute-start(bf16[240,128]{1,0:T(8,128)(2,1)S(1)} %collective-permute-done.7.refs_2_), channel_id=1, source_target_pairs={{0,1},{1,0},{2,3},{3,2},{4,5},{5,4},{6,7},{7,6},{8,9},{9,8},{10,11... | collective-permute-start | bytes 184328 | tf_op jit(solution)/shard_map/ppermute | solution.py:573
  21.0 1.2 %collective-permute-start.12 = (bf16[240,128]{1,0:T(8,128)(2,1)S(1)}, bf16[240,128]{1,0:T(8,128)(2,1)S(1)}, u32[]{:S(2)}, u32[]{:S(2)}) collective-permute-start(bf16[240,128]{1,0:T(8,128)(2,1)S(1)} %collective-permute-done.8.refs_3_), channel_id=1, source_target_pairs={{0,1},{1,0},{2,3},{3,2},{4,5},{5,4},{6,7},{7,6},{8,9},{9,8},{10,11... | collective-permute-start | bytes 184328 | tf_op jit(solution)/shard_map/ppermute | solution.py:573
  25.2 2.2 %copy-start = (bf16[1024,256]{1,0:T(8,128)(2,1)S(1)}, bf16[1024,256]{1,0:T(8,128)(2,1)}, u32[]{:S(2)}) copy-start(bf16[1024,256]{1,0:T(8,128)(2,1)} %cot.1) | copy-start | bytes 1572868
  25.2 2.2 %copy-start.2 = (bf16[1024,256]{1,0:T(8,128)(2,1)S(1)}, bf16[1024,256]{1,0:T(8,128)(2,1)}, u32[]{:S(2)}) copy-start(bf16[1024,256]{1,0:T(8,128)(2,1)} %tok.5) | copy-start | bytes 1572868
  25.3 2.1 %collective-permute-start.14 = (bf16[9,193,128]{2,1,0:T(8,128)(2,1)S(1)}, bf16[9,193,128]{2,1,0:T(8,128)(2,1)S(1)}, u32[]{:S(2)}, u32[]{:S(2)}) collective-permute-start(bf16[9,193,128]{2,1,0:T(8,128)(2,1)S(1)} %stack.37.refs_1_), channel_id=1, source_target_pairs={{0,1},{1,0},{2,3},{3,2},{4,5},{5,4},{6,7},{7,6},{8,9},{9,8},{10,11... | collective-permute-start | bytes 1334024 | tf_op jit(solution)/shard_map/ppermute | solution.py:573
  25.5 1.9 %collective-permute-start.13 = (bf16[3,193,128]{2,1,0:T(8,128)(2,1)S(1)}, bf16[3,193,128]{2,1,0:T(8,128)(2,1)S(1)}, u32[]{:S(2)}, u32[]{:S(2)}) collective-permute-start(bf16[3,193,128]{2,1,0:T(8,128)(2,1)S(1)} %get-tuple-element.57.refs_0_), channel_id=1, source_target_pairs={{0,1},{1,0},{2,3},{3,2},{4,5},{5,4},{6,7},{7,6},{8,9},{9,8},{10,11... | collective-permute-start | bytes 444680 | tf_op jit(solution)/shard_map/ppermute | solution.py:573
  34.3 5.3 %collective-permute-start.16 = (bf16[12,193,128]{2,1,0:T(8,128)(2,1)S(1)}, bf16[12,193,128]{2,1,0:T(8,128)(2,1)S(1)}, u32[]{:S(2)}, u32[]{:S(2)}) collective-permute-start(bf16[12,193,128]{2,1,0:T(8,128)(2,1)S(1)} %get-tuple-element.81), channel_id=1, source_target_pairs={{0,1},{1,0},{2,3},{3,2},{4,5},{5,4},{6,7},{7,6},{8,9},{9,8},{10,11... | collective-permute-start | bytes 1778696 | tf_op jit(solution)/shard_map/ppermute | solution.py:573
  38.0 1.6 %collective-permute-start.15 = (bf16[4,224,128]{2,1,0:T(8,128)(2,1)S(1)}, bf16[4,224,128]{2,1,0:T(8,128)(2,1)S(1)}, u32[]{:S(2)}, u32[]{:S(2)}) collective-permute-start(bf16[4,224,128]{2,1,0:T(8,128)(2,1)S(1)} %get-tuple-element.79), channel_id=1, source_target_pairs={{0,1},{1,0},{2,3},{3,2},{4,5},{5,4},{6,7},{7,6},{8,9},{9,8},{10,11... | collective-permute-start | bytes 688136 | tf_op jit(solution)/shard_map/ppermute | solution.py:573
  39.8 8.0 %collective-permute-start.17 = (bf16[4,96,128]{2,1,0:T(8,128)(2,1)S(1)}, bf16[4,96,128]{2,1,0:T(8,128)(2,1)S(1)}, u32[]{:S(2)}, u32[]{:S(2)}) collective-permute-start(bf16[4,96,128]{2,1,0:T(8,128)(2,1)S(1)} %get-tuple-element.94), channel_id=1, source_target_pairs={{0,6},{1,7},{2,4},{3,5},{4,2},{5,3},{6,0},{7,1},{8,14},{9,15},{10,... | collective-permute-start | bytes 294920 | tf_op jit(solution)/shard_map/ppermute | solution.py:573
  42.0 7.1 %collective-permute-start.18 = (bf16[4,96,128]{2,1,0:T(8,128)(2,1)S(1)}, bf16[4,96,128]{2,1,0:T(8,128)(2,1)S(1)}, u32[]{:S(2)}, u32[]{:S(2)}) collective-permute-start(bf16[4,96,128]{2,1,0:T(8,128)(2,1)S(1)} %get-tuple-element.95), channel_id=1, source_target_pairs={{0,2},{1,3},{2,0},{3,1},{4,6},{5,7},{6,4},{7,5},{8,10},{9,11},{10,... | collective-permute-start | bytes 294920 | tf_op jit(solution)/shard_map/ppermute | solution.py:573
  42.3 6.8 %collective-permute-start.19 = (bf16[4,96,128]{2,1,0:T(8,128)(2,1)S(1)}, bf16[4,96,128]{2,1,0:T(8,128)(2,1)S(1)}, u32[]{:S(2)}, u32[]{:S(2)}) collective-permute-start(bf16[4,96,128]{2,1,0:T(8,128)(2,1)S(1)} %get-tuple-element.96), channel_id=1, source_target_pairs={{0,4},{1,5},{2,6},{3,7},{4,0},{5,1},{6,2},{7,3},{8,12},{9,13},{10,... | collective-permute-start | bytes 294920 | tf_op jit(solution)/shard_map/ppermute | solution.py:573
  45.6 6.8 %collective-permute-start.23 = (bf16[4,97,128]{2,1,0:T(8,128)(2,1)S(1)}, bf16[4,97,128]{2,1,0:T(8,128)(2,1)S(1)}, u32[]{:S(2)}, u32[]{:S(2)}) collective-permute-start(bf16[4,97,128]{2,1,0:T(8,128)(2,1)S(1)} %get-tuple-element.102), channel_id=1, source_target_pairs={{0,6},{1,7},{2,4},{3,5},{4,2},{5,3},{6,0},{7,1},{8,14},{9,15},{10,... | collective-permute-start | bytes 297992 | tf_op jit(solution)/shard_map/ppermute | solution.py:573
  47.5 7.3 %collective-permute-start.24 = (bf16[4,97,128]{2,1,0:T(8,128)(2,1)S(1)}, bf16[4,97,128]{2,1,0:T(8,128)(2,1)S(1)}, u32[]{:S(2)}, u32[]{:S(2)}) collective-permute-start(bf16[4,97,128]{2,1,0:T(8,128)(2,1)S(1)} %get-tuple-element.103), channel_id=1, source_target_pairs={{0,2},{1,3},{2,0},{3,1},{4,6},{5,7},{6,4},{7,5},{8,10},{9,11},{10,... | collective-permute-start | bytes 297992 | tf_op jit(solution)/shard_map/ppermute | solution.py:573
  47.8 7.0 %collective-permute-start.25 = (bf16[4,97,128]{2,1,0:T(8,128)(2,1)S(1)}, bf16[4,97,128]{2,1,0:T(8,128)(2,1)S(1)}, u32[]{:S(2)}, u32[]{:S(2)}) collective-permute-start(bf16[4,97,128]{2,1,0:T(8,128)(2,1)S(1)} %get-tuple-element.104), channel_id=1, source_target_pairs={{0,4},{1,5},{2,6},{3,7},{4,0},{5,1},{6,2},{7,3},{8,12},{9,13},{10,... | collective-permute-start | bytes 297992 | tf_op jit(solution)/shard_map/ppermute | solution.py:573
  49.1 7.4 %collective-permute-start.20 = (bf16[96,128]{1,0:T(8,128)(2,1)S(1)}, bf16[96,128]{1,0:T(8,128)(2,1)S(1)}, u32[]{:S(2)}, u32[]{:S(2)}) collective-permute-start(bf16[96,128]{1,0:T(8,128)(2,1)S(1)} %get-tuple-element.98), channel_id=1, source_target_pairs={{0,8},{1,9},{2,10},{3,11},{4,12},{5,13},{6,14},{7,15},{8,16},{9,17... | collective-permute-start | bytes 73736 | tf_op jit(solution)/shard_map/ppermute | solution.py:573
  50.9 9.4 %collective-permute-start.21 = (bf16[96,128]{1,0:T(8,128)(2,1)S(1)}, bf16[96,128]{1,0:T(8,128)(2,1)S(1)}, u32[]{:S(2)}, u32[]{:S(2)}) collective-permute-start(bf16[96,128]{1,0:T(8,128)(2,1)S(1)} %get-tuple-element.99), channel_id=1, source_target_pairs={{0,16},{1,17},{2,18},{3,19},{4,20},{5,21},{6,22},{7,23},{8,24},{9,... | collective-permute-start | bytes 73736 | tf_op jit(solution)/shard_map/ppermute | solution.py:573
  52.4 7.9 %collective-permute-start.22 = (bf16[96,128]{1,0:T(8,128)(2,1)S(1)}, bf16[96,128]{1,0:T(8,128)(2,1)S(1)}, u32[]{:S(2)}, u32[]{:S(2)}) collective-permute-start(bf16[96,128]{1,0:T(8,128)(2,1)S(1)} %get-tuple-element.100), channel_id=1, source_target_pairs={{0,24},{1,25},{2,26},{3,27},{4,28},{5,29},{6,30},{7,31},{8,0},{9,1... | collective-permute-start | bytes 73736 | tf_op jit(solution)/shard_map/ppermute | solution.py:573
  54.9 5.7 %collective-permute-start.26 = (bf16[97,128]{1,0:T(8,128)(2,1)S(1)}, bf16[97,128]{1,0:T(8,128)(2,1)S(1)}, u32[]{:S(2)}, u32[]{:S(2)}) collective-permute-start(bf16[97,128]{1,0:T(8,128)(2,1)S(1)} %get-tuple-element.106), channel_id=1, source_target_pairs={{0,8},{1,9},{2,10},{3,11},{4,12},{5,13},{6,14},{7,15},{8,16},{9,17... | collective-permute-start | bytes 74504 | tf_op jit(solution)/shard_map/ppermute | solution.py:573
  55.0 5.6 %collective-permute-start.27 = (bf16[97,128]{1,0:T(8,128)(2,1)S(1)}, bf16[97,128]{1,0:T(8,128)(2,1)S(1)}, u32[]{:S(2)}, u32[]{:S(2)}) collective-permute-start(bf16[97,128]{1,0:T(8,128)(2,1)S(1)} %get-tuple-element.107), channel_id=1, source_target_pairs={{0,16},{1,17},{2,18},{3,19},{4,20},{5,21},{6,22},{7,23},{8,24},{9,... | collective-permute-start | bytes 74504 | tf_op jit(solution)/shard_map/ppermute | solution.py:573
  56.6 4.6 %collective-permute-start.28 = (bf16[97,128]{1,0:T(8,128)(2,1)S(1)}, bf16[97,128]{1,0:T(8,128)(2,1)S(1)}, u32[]{:S(2)}, u32[]{:S(2)}) collective-permute-start(bf16[97,128]{1,0:T(8,128)(2,1)S(1)} %get-tuple-element.108), channel_id=1, source_target_pairs={{0,24},{1,25},{2,26},{3,27},{4,28},{5,29},{6,30},{7,31},{8,0},{9,1... | collective-permute-start | bytes 74504 | tf_op jit(solution)/shard_map/ppermute | solution.py:573

commit v12 on v11

--- a/solution.py
+++ b/solution.py
@@ -38,6 +38,8 @@
 FIRST_ROWS = 2 * PLANE * SHARE
 HEAD_ROWS = FIRST_ROWS - ROW_OUT
 SIDE, SIDE_ROWS = 208, 16
+SLOTS, NO_SHARE = 10, 2 * PLANE
+STEPS = (3, 1, 2)
 PARTS = (slice(0, 96), slice(96, SHARE))
 SMALL_IN_SHARE = ROW_SMALL - (2 * PLANE * Z - 1) * SHARE
 
@@ -132,12 +134,12 @@
     wide[SHARE:SIDE, :] = jnp.zeros((SIDE - SHARE, LANES), F32)
     last = stage[Z - 1].astype(F32)
     wide[SIDE:, :] = last[SMALL_IN_SHARE:, :]
-    first[...] = wide[...].astype(BF16)
+    first[0] = wide[...].astype(BF16)
 
 
 def attend_kernel(ids, allowed, normed, *refs):
-    bufs = refs[: 2 * PLANE]
-    project_out, weights_out, attended_out, w_qkv, small, first_out, flat = refs[2 * PLANE :]
+    bufs = [ref.at[i] for ref in refs[:3] for i in range(ref.shape[0])]
+    project_out, weights_out, attended_out, w_qkv, small, first_out, flat = refs[3:]
     for slot, buf in enumerate(bufs):
         wide = buf[...].astype(F32)
         flat[pl.ds(ids[slot] * SHARE, SHARE), :] = wide[:SHARE, :]
@@ -191,19 +193,17 @@
 def feed_kernel(
     ids, tok, attended, cot, small, first_in, *refs,
 ):
-    bufs = []
-    for own, others in (refs[0:2], refs[2:4]):
-        bufs.append(own)
-        bufs += [others.at[pl.ds(p * (Z - 1), Z - 1)] for p in range(PLANE - 1)]
+    bufs = [ref.at[pl.ds(i, Z - 1)] for ref in refs[:3] for i in range(0, ref.shape[0], Z - 1)]
     (
         middle_out, activated_out, grad_middle_out, grad_attended_out, w_down, keep_out, send_out, first_out,
         w_out, w_up, grad_hidden, flat,
-    ) = refs[4:]
+    ) = refs[3:]
     flat[:HEAD_ROWS, :] = first_in[...]
     for slot, buf in enumerate(bufs):
         for z in range(1, Z):
-            share = ids[slot] + z * 2 * PLANE
-            flat[pl.ds(share * SHARE - ROW_OUT, SHARE), :] = buf[z - 1].astype(F32)
+            row = (ids[slot] + z * 2 * PLANE) * SHARE - ROW_OUT
+            row = jnp.where(ids[slot] == NO_SHARE, ROW_TOTAL - ROW_OUT, row)
+            flat[pl.ds(row, SHARE), :] = buf[z - 1].astype(F32)
     matrix_from_flat(flat, 0, D, D, w_out)
     matrix_from_flat(flat, ROW_UP - ROW_OUT, D, FF, w_up)
     matrix_from_flat(flat, ROW_DOWN - ROW_OUT, FF, D, w_down)
@@ -284,12 +284,12 @@
     for i in range(sums.shape[1] // LANES):
         row = base + LATE_SMALL + i
         flat[row : row + 1, :] = sums[:, i * LANES : (i + 1) * LANES]
-    flat[ROW_END - ROW_OUT :, :] = jnp.zeros((ROW_TOTAL - ROW_END, LANES), F32)
+    flat[ROW_END - ROW_OUT : ROW_TOTAL - ROW_OUT, :] = jnp.zeros((ROW_TOTAL - ROW_END, LANES), F32)
     first_out[...] = flat[:HEAD_ROWS, :]
     for target, out in enumerate((keep_out, send_out)):
         for p in range(PLANE):
             for z in range(1, Z):
-                share = ids[target * PLANE + p] + z * 2 * PLANE
+                share = ids[SLOTS + target * PLANE + p] + z * 2 * PLANE
                 rows = flat[pl.ds(share * SHARE - ROW_OUT, SHARE), :]
                 out[p * (Z - 1) + z - 1] = rows.astype(out.dtype)
 
@@ -455,6 +455,19 @@
     )
 
 
+def slot_ids(plane, core, choose):
+    mine, others = choose(core == 0, 1, 2), choose(core == 0, 2, 1)
+    pairs = [
+        (plane, core, True), (plane ^ mine, core, True), (plane ^ 3, core, core == 1),
+        (plane ^ others, core ^ 1, True), (plane ^ 3, core ^ 1, core == 0),
+    ]
+    return [
+        choose(there, p * 2 + c, NO_SHARE)
+        for p, first, there in pairs
+        for c in (first, first ^ 1)
+    ]
+
+
 def stack(items):
     shape = (sum(item.shape[0] for item in items),) + items[0].shape[1:]
     return call(stack_kernel, "stack", None, items, [like(*shape, kind=items[0].dtype)])
@@ -467,7 +480,7 @@
         attend_kernel, "attend", ids, [allowed, normed, *bufs],
         [like(*shape, kind=BF16) for shape in shapes]
         + [like(SMALL_ROWS, LANES), like(HEAD_ROWS, LANES)],
-        [pltpu.VMEM((FIRST_ROWS, LANES), F32)], us=0.2,
+        [pltpu.VMEM((FIRST_ROWS + SHARE, LANES), F32)], us=0.2,
     )
 
 
@@ -489,7 +502,7 @@
             pltpu.VMEM((D, D), BF16),
             pltpu.VMEM((D, FF), BF16),
             pltpu.VMEM((rows, FF), BF16),
-            pltpu.VMEM((ROW_TOTAL - ROW_OUT, LANES), F32),
+            pltpu.VMEM((ROW_TOTAL - ROW_OUT + SHARE, LANES), F32),
         ],
         us=8,
     )
@@ -524,26 +537,33 @@
     normed, normed_turned, _, allowed = prepare(tokens, params, segment_ids)
     gathered = lax.all_gather(params, "fsdp", axis=0).reshape(total, LANES)
     shares = gathered[:ROW_TOTAL].reshape(Z, 2 * PLANE, SHARE, LANES)
-    order = [p * 2 + c for c in range(2) for p in range(PLANE)]
+    order = [p * 2 + c for c in range(2) for p in (0, *STEPS)]
     side = jnp.concatenate(
         [jnp.zeros((SIDE - SHARE, LANES), BF16), gathered[ROW_SMALL:ROW_TOTAL]], axis=0
     )
-    firsts = [jnp.concatenate([shares[0, k], side], axis=0) for k in order]
-    rests = []
-    for group in (order[:PLANE], order[PLANE:]):
-        rests += [shares[1:, group[0]], jnp.concatenate([shares[1:, k] for k in group[1:]])]
-    ids = jnp.array(order, jnp.int32)
-    project, weights, attended, w_qkv, small, first = attend(ids, allowed, normed, firsts)
+    places = slot_ids(0, 0, lambda there, yes, no: yes if there else no)
+    firsts = [
+        jnp.concatenate([shares[0, k % NO_SHARE], side], axis=0)[None] for k in places
+    ]
+    rests = [shares[1:, k % NO_SHARE] for k in places]
+    firsts, rests = (
+        [jnp.concatenate(items[i:j]) for i, j in ((0, 2), (2, 6), (6, SLOTS))]
+        for items in (firsts, rests)
+    )
+    in_ids, ids = jnp.array(places, jnp.int32), jnp.array(order, jnp.int32)
+    project, weights, attended, w_qkv, small, first = attend(in_ids, allowed, normed, firsts)
     middle, activated, grad_middle, grad_attended, w_down, rest, rest_send, first_grad = feed(
-        ids, tokens, attended, cotangent, small, first, rests, F32
+        jnp.concatenate([in_ids, ids]), tokens, attended, cotangent, small, first, rests, F32
     )
     outputs = result(middle, activated, w_down, small)
     grad_project, first, first_send = attend_back(
         ids, project, weights, grad_attended, normed_turned, w_qkv, small, first_grad, F32
     )
     input_grad = input_gradient(tokens, grad_project, grad_middle, w_qkv, small)
-    first = jnp.stack([first, first_send], axis=1)
-    rest = jnp.stack([rest, rest_send]).reshape(2, PLANE, Z - 1, SHARE, LANES).transpose(2, 1, 0, 3, 4)
+    back = [order.index(k) for k in range(2 * PLANE)]
+    first = jnp.concatenate([first, first_send])[jnp.array(back)].reshape(PLANE, 2, -1, LANES)
+    rest = jnp.concatenate([rest, rest_send]).reshape(2 * PLANE, Z - 1, SHARE, LANES)
+    rest = rest[jnp.array(back)].transpose(1, 0, 2, 3)
     flat = jnp.concatenate(
         [
             first[:, :, :SHARE].reshape(-1, LANES),
@@ -573,13 +593,35 @@
     return lax.ppermute(values, "fsdp", pairs)
 
 
-STEPS = (3, 1, 2)
+def to_neighbour(values):
+    return lax.ppermute(
+        values, "fsdp",
+        [
+            (index_of(z, p, c), index_of(z, p ^ (1 + c), c))
+            for z in range(Z)
+            for p in range(PLANE)
+            for c in range(2)
+        ],
+    )
+
+
+def to_diagonal(values):
+    return lax.ppermute(
+        values, "fsdp",
+        [(index_of(z, p, 1), index_of(z, p ^ 3, 1)) for z in range(Z) for p in range(PLANE)],
+    )
+
+
+def spread(own):
+    pair = stack([own, move(own, 0, 0, 1)])
+    return pair, [to_neighbour(pair), to_diagonal(pair)]
 
 
 def local_slice(tokens, params, segment_ids, cotangent):
     me = lax.axis_index("fsdp").astype(jnp.int32)
     z, plane, core = me // (2 * PLANE), (me // 2) % PLANE, me % 2
     where = z.reshape(1)
+    in_ids = jnp.stack(slot_ids(plane, core, jnp.where)).astype(jnp.int32)
     ids = jnp.stack(
         [(plane ^ dp) * 2 + (core ^ dc) for dc in range(2) for dp in (0, *STEPS)]
     )
@@ -587,18 +629,20 @@
     normed, normed_turned, own, allowed = prepare(tokens, params, segment_ids)
     first, rest = call(
         sort_kernel, "sort_shares", where, [own] + [move(params, d, 0, 0) for d in range(1, Z)],
-        [like(SIDE + SMALL_ROWS, LANES, kind=BF16), like(Z - 1, SHARE, LANES, kind=BF16)],
+        [like(1, SIDE + SMALL_ROWS, LANES, kind=BF16), like(Z - 1, SHARE, LANES, kind=BF16)],
         [pltpu.VMEM((Z, SHARE, LANES), BF16), pltpu.VMEM((SIDE + SMALL_ROWS, LANES), F32)],
     )
-    firsts = [first] + [move(first, 0, d, 0) for d in STEPS]
-    rests = [move(rest, 0, d, 0) for d in STEPS]
-    firsts = firsts + [move(item, 0, 0, 1) for item in firsts]
-    project, weights, attended, w_qkv, small, first = attend(ids, allowed, normed, firsts)
-    *rests, attended = lax.optimization_barrier((*rests, attended))
-    rests = stack(rests)
-    rests = [rest, rests, move(rest, 0, 0, 1), move(rests, 0, 0, 1)]
+    pair, received = spread(first)
+    rest_pair, rest_received = spread(rest)
+    received = stack(received)
+    project, weights, attended, w_qkv, small, first = attend(
+        in_ids, allowed, normed, [pair, received, move(received, 0, 0, 1)]
+    )
+    *rest_received, attended = lax.optimization_barrier((*rest_received, attended))
+    rest_received = stack(rest_received)
+    rests = [rest_pair, rest_received, move(rest_received, 0, 0, 1)]
     middle, activated, grad_middle, grad_attended, w_down, rest, send, first_grad = feed(
-        ids, tokens, attended, cotangent, small, first, rests, BF16
+        jnp.concatenate([in_ids, ids]), tokens, attended, cotangent, small, first, rests, BF16
     )
 
     rest_in = move(send, 0, 0, 1)
@@ -606,6 +650,8 @@
         ids, project, weights, grad_attended, normed_turned, w_qkv, small, first_grad, BF16
     )
     first_in = move(send, 0, 0, 1)
+    input_grad = input_gradient(tokens, grad_project, grad_middle, w_qkv, small)
+    first_in, input_grad = lax.optimization_barrier((first_in, input_grad))
     parts = [(Z, rows.stop - rows.start, LANES) for rows in PARTS]
     sums = call(
         add_core_kernel, "add_core", None, [first, first_in, rest, rest_in],
@@ -613,10 +659,7 @@
         [pltpu.VMEM((Z, SHARE, LANES), F32)],
     )
     sums = [sums[n::2] for n in range(2)]
-    grad_project, *sums[0] = lax.optimization_barrier((grad_project, *sums[0]))
     outputs = result(middle, activated, w_down, small)
-    input_grad = input_gradient(tokens, grad_project, grad_middle, w_qkv, small)
-    input_grad, *sums[1] = lax.optimization_barrier((input_grad, *sums[1]))
     arrived = [[move(item, 0, d, 0) for item, d in zip(part[1:], STEPS)] for part in sums]
     columns = []
     for n, part in enumerate(parts):

time: 62.1 us -> 69.3 us (1.12)
  local copies, waits for them, and re-layouts: 2.63 us -> 7.61 us
  Pallas kernels: 18.7 us -> 20.2 us
  waiting for transfers between devices: 7.07 us -> 7.87 us
    unnamed x10 -> x34, local copies, waits for them, and re-layouts: 2.54 us -> 7.34 us
    ppermute x29 -> x21, starting transfers between devices: 32.7 us -> 28.1 us  [move(): return lax.ppermute(values, 'fsdp', pairs)]
    ppermute x0 -> x4, starting transfers between devices: none -> 4.22 us  [the longest x2 2.16 us: to_neighbour(): lax.ppermute(values, 'fsdp', [(index_of(z, p, c), index_of(z, p ^ 1 + c,...]
    pallas_call x12 -> x15, Pallas kernels: 18.7 us -> 20.2 us  [call(): pl.pallas_call(kernel, in_specs=[SMEM_SPEC] * with_ids + [VMEM_SPEC] * le...]
    ppermute x29 -> x21, waiting for transfers between devices: 7.07 us -> 7.19 us  [move(): return lax.ppermute(values, 'fsdp', pairs)]
  transfers between devices with their start and end apart: 29 -> 25, of which waited for: 8 -> 7; matrix products, arithmetic and copies ran while one was open for 0% -> 0% of each run, Pallas kernels for 17% -> 16%
where the time goes in v12:
time: 69.3 us; the launch traced here: 68.8 us
  starting transfers between devices  32.3 us (47%)
  Pallas kernels  20.2 us (29%)
  waiting for transfers between devices  7.87 us (11%)
  local copies, waits for them, and re-layouts  7.61 us (11%)
  between operations  0.85 us (1%)
    ppermute x21, starting transfers between devices, move(): return lax.ppermute(values, 'fsdp', pairs)  28.1 us
    pallas_call x15, Pallas kernels, call(): pl.pallas_call(kernel, in_specs=[SMEM_SPEC] * with_ids + [VMEM_SPEC] * le...  20.2 us
    unnamed x34, local copies, waits for them, and re-layouts  7.34 us
    ppermute x21, waiting for transfers between devices, move(): return lax.ppermute(values, 'fsdp', pairs)  7.19 us
    ppermute x2, starting transfers between devices, to_neighbour(): lax.ppermute(values, 'fsdp', [(index_of(z, p, c), index_of(z, p ^ 1 + c,...  2.16 us
    ppermute x2, starting transfers between devices, to_diagonal(): lax.ppermute(values, 'fsdp', [(index_of(z, p, 1), index_of(z, p ^ 3, 1))...  2.07 us
  transfers between devices with their start and end apart: 25, of which 7 were waited for; matrix products, arithmetic and copies ran while one was open for 0% of the time, Pallas kernels for 16%

profile of v12, /device:TPU:0, one launch (start us, length us, event | category | flops | bytes accessed | tf_op | source)
XLA Modules:
  0.0 68.8 jit_solution(13834352068741130685)
XLA Ops:
  0.6 3.1 %collective-permute-start = (bf16[193,128]{1,0:T(8,128)(2,1)}, bf16[193,128]{1,0:T(8,128)(2,1)S(1)}, u32[]{:S(2)}, u32[]{:S(2)}) collective-permute-start(bf16[193,128]{1,0:T(8,128)(2,1)} %params.1), channel_id=1, source_target_pairs={{0,8},{1,9},{2,10},{3,11},{4,12},{5,13},{6,14},{7,15},{8,16},{9,17... | collective-permute-start | bytes 148232 | tf_op jit(solution)/shard_map/ppermute | solution.py:593
  3.7 2.6 %collective-permute-start.1 = (bf16[193,128]{1,0:T(8,128)(2,1)}, bf16[193,128]{1,0:T(8,128)(2,1)S(1)}, u32[]{:S(2)}, u32[]{:S(2)}) collective-permute-start(bf16[193,128]{1,0:T(8,128)(2,1)} %params.1), channel_id=1, source_target_pairs={{0,16},{1,17},{2,18},{3,19},{4,20},{5,21},{6,22},{7,23},{8,24},{9,... | collective-permute-start | bytes 148232 | tf_op jit(solution)/shard_map/ppermute | solution.py:593
  6.3 1.3 %collective-permute-start.2 = (bf16[193,128]{1,0:T(8,128)(2,1)}, bf16[193,128]{1,0:T(8,128)(2,1)S(1)}, u32[]{:S(2)}, u32[]{:S(2)}) collective-permute-start(bf16[193,128]{1,0:T(8,128)(2,1)} %params.1), channel_id=1, source_target_pairs={{0,24},{1,25},{2,26},{3,27},{4,28},{5,29},{6,30},{7,31},{8,0},{9,1... | collective-permute-start | bytes 148232 | tf_op jit(solution)/shard_map/ppermute | solution.py:593
  7.6 1.0 %copy-done.3 = bf16[1024,256]{1,0:T(8,128)(2,1)S(1)} copy-done((bf16[1024,256]{1,0:T(8,128)(2,1)S(1)}, bf16[1024,256]{1,0:T(8,128)(2,1)}, u32[]{:S(2)}) %copy-start.3) | copy-done | bytes 524312
  8.7 0.8 %copy-done.10 = bf16[193,128]{1,0:T(8,128)(2,1)S(1)} copy-done((bf16[193,128]{1,0:T(8,128)(2,1)S(1)}, bf16[193,128]{1,0:T(8,128)(2,1)}, u32[]{:S(2)}) %copy-start.10) | copy-done | bytes 49432
  9.5 0.7 copy-done.14
  10.2 0.7 prepare.1
  10.9 0.8 %copy-done.15 = bf16[256,1024]{1,0:T(8,128)(2,1)} copy-done((bf16[256,1024]{1,0:T(8,128)(2,1)}, bf16[256,1024]{1,0:T(8,128)(2,1)S(1)}, u32[]{:S(2)}) %copy-start.15) | copy-done | bytes 524312
  11.8 0.5 collective-permute-start.3
  12.3 0.7 %collective-permute-done.6.refs_1_ = bf16[1,240,128]{2,1,0:T(8,128)(2,1)S(1)} collective-permute-done((bf16[1,240,128]{2,1,0:T(8,128)(2,1)S(1)}, bf16[1,240,128]{2,1,0:T(8,128)(2,1)S(1)}, u32[]{:S(2)}, u32[]{:S(2)}) %collective-permute-start.6) | collective-permute-done | bytes 61472 | tf_op jit(solution)/shard_map/ppermute | solution.py:593
  13.0 1.6 %collective-permute-start.7 = (bf16[2,240,128]{2,1,0:T(8,128)(2,1)S(1)}, bf16[2,240,128]{2,1,0:T(8,128)(2,1)S(1)}, u32[]{:S(2)}, u32[]{:S(2)}) collective-permute-start(bf16[2,240,128]{2,1,0:T(8,128)(2,1)S(1)} %stack.79.refs_0_), channel_id=1, source_target_pairs={{0,2},{1,5},{2,0},{3,7},{4,6},{5,1},{6,4},{7,3},{8,10},{9,13},{10,... | collective-permute-start | bytes 368648 | tf_op jit(solution)/shard_map/ppermute | solution.py:597
  14.6 0.7 collective-permute-start.8
  15.3 0.6 collective-permute-start.4
  15.9 1.4 %collective-permute-start.5 = (bf16[6,193,128]{2,1,0:T(8,128)(2,1)S(1)}, bf16[6,193,128]{2,1,0:T(8,128)(2,1)}, u32[]{:S(2)}, u32[]{:S(2)}) collective-permute-start(bf16[6,193,128]{2,1,0:T(8,128)(2,1)S(1)} %stack.78.refs_0_), channel_id=1, source_target_pairs={{1,7},{3,5},{5,3},{7,1},{9,15},{11,13},{13,11},{15,9},{17,23},{19,... | collective-permute-start | bytes 889352 | tf_op jit(solution)/shard_map/ppermute | solution.py:609
  17.3 0.7 collective-permute-done.7.refs_0_
  18.0 4.4 %collective-permute-start.9 = (bf16[4,240,128]{2,1,0:T(8,128)(2,1)S(1)}, bf16[4,240,128]{2,1,0:T(8,128)(2,1)S(1)}, u32[]{:S(2)}, u32[]{:S(2)}) collective-permute-start(bf16[4,240,128]{2,1,0:T(8,128)(2,1)S(1)} %stack.80.refs_1_), channel_id=1, source_target_pairs={{0,1},{1,0},{2,3},{3,2},{4,5},{5,4},{6,7},{7,6},{8,9},{9,8},{10,11... | collective-permute-start | bytes 737288 | tf_op jit(solution)/shard_map/ppermute | solution.py:593
  22.5 1.1 %collective-permute-done.9.refs_2_ = bf16[4,240,128]{2,1,0:T(8,128)(2,1)S(1)} collective-permute-done((bf16[4,240,128]{2,1,0:T(8,128)(2,1)S(1)}, bf16[4,240,128]{2,1,0:T(8,128)(2,1)S(1)}, u32[]{:S(2)}, u32[]{:S(2)}) %collective-permute-start.9) | collective-permute-done | bytes 245792 | tf_op jit(solution)/shard_map/ppermute | solution.py:593
  23.5 2.9 %attend.1 = (bf16[1024,768]{1,0:T(8,128)(2,1)S(1)}, bf16[1024,512]{1,0:T(8,128)(2,1)S(1)}, bf16[1024,256]{1,0:T(8,128)(2,1)S(1)}, bf16[256,768]{1,0:T(8,128)(2,1...) custom-call(s32[10]{0:T(128)S(1)} %stack.76.ids, f32[1024,128]{1,0:T(8,128)S(1)} %get-tuple-element.49.allowed, ...), custom_call_target="tpu_custom_call" | custom-call | flops 200000000 | bytes 1048576 | tf_op jit(solution)/shard_map/attend/pallas_call | solution.py:431
  26.5 1.2 %copy-done = bf16[1024,768]{1,0:T(8,128)(2,1)} copy-done((bf16[1024,768]{1,0:T(8,128)(2,1)}, bf16[1024,768]{1,0:T(8,128)(2,1)S(1)}, u32[]{:S(2)}) %copy-start) | copy-done | bytes 1572888
  27.7 1.4 %stack.81.refs_1_ = bf16[12,193,128]{2,1,0:T(8,128)(2,1)S(1)} custom-call(bf16[6,193,128]{2,1,0:T(8,128)(2,1)} %collective-permute-done.4.refs_0_, bf16[6,193,128]{2,1,0:T(8,128)(2,1)} %collective-permute-done.5.refs_1_), custom_call_target="tpu_custom_call" | custom-call | flops 1000000000 | bytes 1048576 | tf_op jit(solution)/shard_map/stack/pallas_call | solution.py:431
  29.2 0.4 collective-permute-start.10
  29.8 1.5 %collective-permute-done.10.refs_2_ = bf16[12,193,128]{2,1,0:T(8,128)(2,1)S(1)} collective-permute-done((bf16[12,193,128]{2,1,0:T(8,128)(2,1)S(1)}, bf16[12,193,128]{2,1,0:T(8,128)(2,1)S(1)}, u32[]{:S(2)}, u32[]{:S(2)}) %collective-permute-start.10) | collective-permute-done | bytes 592928 | tf_op jit(solution)/shard_map/ppermute | solution.py:593
  31.3 1.0 %copy-done.4 = bf16[1024,256]{1,0:T(8,128)(2,1)S(1)} copy-done((bf16[1024,256]{1,0:T(8,128)(2,1)S(1)}, bf16[1024,256]{1,0:T(8,128)(2,1)}, u32[]{:S(2)}) %copy-start.4) | copy-done | bytes 524312
  32.3 1.0 %copy-done.7 = bf16[1024,256]{1,0:T(8,128)(2,1)S(1)} copy-done((bf16[1024,256]{1,0:T(8,128)(2,1)S(1)}, bf16[1024,256]{1,0:T(8,128)(2,1)}, u32[]{:S(2)}) %copy-start.7) | copy-done | bytes 524312
  33.4 0.7 %copy-done.12 = f32[32,128]{1,0:T(8,128)S(1)} copy-done((f32[32,128]{1,0:T(8,128)S(1)}, f32[32,128]{1,0:T(8,128)}, u32[]{:S(2)}) %copy-start.12) | copy-done | bytes 16408
  34.1 6.8 %feed.1 = (f32[1024,256]{1,0:T(8,128)S(1)}, bf16[1024,1024]{1,0:T(8,128)(2,1)S(1)}, f32[1024,256]{1,0:T(8,128)S(1)}, bf16[1024,256]{1,0:T(8,128)(2,1)S(1)}, bf16...) custom-call(s32[18]{0:T(128)S(1)} %concatenate.4.ids, ...), custom_call_target="tpu_custom_call" | custom-call | flops 8000000000 | bytes 1048576 | tf_op jit(solution)/shard_map/feed/pallas_call | solution.py:431
  40.9 0.4 collective-permute-start.12
  41.4 3.5 %attend_back.1 = (bf16[1024,768]{1,0:T(8,128)(2,1)S(1)}, f32[4,224,128]{2,1,0:T(8,128)S(1)}, bf16[4,224,128]{2,1,0:T(8,128)(2,1)S(1)}) custom-call(s32[8]{0:T(128)S(1)} %stack.77.ids, bf16[1024,768]{1,0:T(8,128)(2,1)S(1)} %copy-done.1, bf16[1024,512]{1,0:T(8,128)(2,1)S(1)} %get-tuple-element.62.weights, ...), custom_call_target="tpu_custom_call" | custom-call | flops 4000000000 | bytes 1048576 | tf_op jit(solution)/shard_map/attend_back/pallas_call | solution.py:431
  44.9 0.2 collective-permute-start.11
  45.1 2.2 %input_grad.1 = f32[1024,256]{1,0:T(8,128)} custom-call(bf16[1024,256]{1,0:T(8,128)(2,1)S(1)} %copy-done.5, bf16[1024,768]{1,0:T(8,128)(2,1)S(1)} %get-tuple-element.68.grad_project, f32[1024,256]{1,0:T(8,128)S(1)} %get-tuple-element.69.grad_middle, bf16[256,768]{1,0:T(8,128)(2,1)S(1)} %copy-done.9, f32[32,128]{1,0:T(8,128)S(1)} %copy-done.13), custom_call_target="tpu_custom_call" | custom-call | flops 2000000000 | bytes 1048576 | tf_op jit(solution)/shard_map/input_grad/pallas_call | solution.py:431
  47.3 0.2 add_core.1
  47.5 1.6 %collective-permute-start.13 = (bf16[4,96,128]{2,1,0:T(8,128)(2,1)S(1)}, bf16[4,96,128]{2,1,0:T(8,128)(2,1)S(1)}, u32[]{:S(2)}, u32[]{:S(2)}) collective-permute-start(bf16[4,96,128]{2,1,0:T(8,128)(2,1)S(1)} %get-tuple-element.76), channel_id=1, source_target_pairs={{0,6},{1,7},{2,4},{3,5},{4,2},{5,3},{6,0},{7,1},{8,14},{9,15},{10,... | collective-permute-start | bytes 294920 | tf_op jit(solution)/shard_map/ppermute | solution.py:593
  49.1 0.5 collective-permute-start.14
  49.6 1.5 %collective-permute-start.15 = (bf16[4,96,128]{2,1,0:T(8,128)(2,1)S(1)}, bf16[4,96,128]{2,1,0:T(8,128)(2,1)S(1)}, u32[]{:S(2)}, u32[]{:S(2)}) collective-permute-start(bf16[4,96,128]{2,1,0:T(8,128)(2,1)S(1)} %get-tuple-element.78), channel_id=1, source_target_pairs={{0,4},{1,5},{2,6},{3,7},{4,0},{5,1},{6,2},{7,3},{8,12},{9,13},{10,... | collective-permute-start | bytes 294920 | tf_op jit(solution)/shard_map/ppermute | solution.py:593
  51.1 1.5 %collective-permute-start.19 = (bf16[4,97,128]{2,1,0:T(8,128)(2,1)S(1)}, bf16[4,97,128]{2,1,0:T(8,128)(2,1)S(1)}, u32[]{:S(2)}, u32[]{:S(2)}) collective-permute-start(bf16[4,97,128]{2,1,0:T(8,128)(2,1)S(1)} %get-tuple-element.84), channel_id=1, source_target_pairs={{0,6},{1,7},{2,4},{3,5},{4,2},{5,3},{6,0},{7,1},{8,14},{9,15},{10,... | collective-permute-start | bytes 297992 | tf_op jit(solution)/shard_map/ppermute | solution.py:593
  52.6 0.5 collective-permute-start.20
  53.1 1.0 %collective-permute-done.13.refs_0_ = bf16[4,96,128]{2,1,0:T(8,128)(2,1)S(1)} collective-permute-done((bf16[4,96,128]{2,1,0:T(8,128)(2,1)S(1)}, bf16[4,96,128]{2,1,0:T(8,128)(2,1)S(1)}, u32[]{:S(2)}, u32[]{:S(2)}) %collective-permute-start.13) | collective-permute-done | bytes 98336 | tf_op jit(solution)/shard_map/ppermute | solution.py:593
  54.1 0.6 collective-permute-start.21
  54.6 0.6 collective-permute-done.14.refs_1_
  55.3 2.2 %collective-permute-done.15.refs_2_ = bf16[4,96,128]{2,1,0:T(8,128)(2,1)S(1)} collective-permute-done((bf16[4,96,128]{2,1,0:T(8,128)(2,1)S(1)}, bf16[4,96,128]{2,1,0:T(8,128)(2,1)S(1)}, u32[]{:S(2)}, u32[]{:S(2)}) %collective-permute-start.15) | collective-permute-done | bytes 98336 | tf_op jit(solution)/shard_map/ppermute | solution.py:593
  57.6 0.7 %collective-permute-start.16 = (bf16[96,128]{1,0:T(8,128)(2,1)S(1)}, bf16[96,128]{1,0:T(8,128)(2,1)S(1)}, u32[]{:S(2)}, u32[]{:S(2)}) collective-permute-start(bf16[96,128]{1,0:T(8,128)(2,1)S(1)} %get-tuple-element.80), channel_id=1, source_target_pairs={{0,8},{1,9},{2,10},{3,11},{4,12},{5,13},{6,14},{7,15},{8,16},{9,17... | collective-permute-start | bytes 73736 | tf_op jit(solution)/shard_map/ppermute | solution.py:593
  58.3 2.0 %collective-permute-start.17 = (bf16[96,128]{1,0:T(8,128)(2,1)S(1)}, bf16[96,128]{1,0:T(8,128)(2,1)S(1)}, u32[]{:S(2)}, u32[]{:S(2)}) collective-permute-start(bf16[96,128]{1,0:T(8,128)(2,1)S(1)} %get-tuple-element.81), channel_id=1, source_target_pairs={{0,16},{1,17},{2,18},{3,19},{4,20},{5,21},{6,22},{7,23},{8,24},{9,... | collective-permute-start | bytes 73736 | tf_op jit(solution)/shard_map/ppermute | solution.py:593
  60.3 1.2 %collective-permute-start.18 = (bf16[96,128]{1,0:T(8,128)(2,1)S(1)}, bf16[96,128]{1,0:T(8,128)(2,1)S(1)}, u32[]{:S(2)}, u32[]{:S(2)}) collective-permute-start(bf16[96,128]{1,0:T(8,128)(2,1)S(1)} %get-tuple-element.82), channel_id=1, source_target_pairs={{0,24},{1,25},{2,26},{3,27},{4,28},{5,29},{6,30},{7,31},{8,0},{9,1... | collective-permute-start | bytes 73736 | tf_op jit(solution)/shard_map/ppermute | solution.py:593
  61.6 0.9 %collective-permute-start.22 = (bf16[97,128]{1,0:T(8,128)(2,1)S(1)}, bf16[97,128]{1,0:T(8,128)(2,1)S(1)}, u32[]{:S(2)}, u32[]{:S(2)}) collective-permute-start(bf16[97,128]{1,0:T(8,128)(2,1)S(1)} %get-tuple-element.88), channel_id=1, source_target_pairs={{0,8},{1,9},{2,10},{3,11},{4,12},{5,13},{6,14},{7,15},{8,16},{9,17... | collective-permute-start | bytes 74504 | tf_op jit(solution)/shard_map/ppermute | solution.py:593
  62.5 1.3 %collective-permute-start.23 = (bf16[97,128]{1,0:T(8,128)(2,1)S(1)}, bf16[97,128]{1,0:T(8,128)(2,1)S(1)}, u32[]{:S(2)}, u32[]{:S(2)}) collective-permute-start(bf16[97,128]{1,0:T(8,128)(2,1)S(1)} %get-tuple-element.89), channel_id=1, source_target_pairs={{0,16},{1,17},{2,18},{3,19},{4,20},{5,21},{6,22},{7,23},{8,24},{9,... | collective-permute-start | bytes 74504 | tf_op jit(solution)/shard_map/ppermute | solution.py:593
  63.7 2.8 %collective-permute-start.24 = (bf16[97,128]{1,0:T(8,128)(2,1)S(1)}, bf16[97,128]{1,0:T(8,128)(2,1)S(1)}, u32[]{:S(2)}, u32[]{:S(2)}) collective-permute-start(bf16[97,128]{1,0:T(8,128)(2,1)S(1)} %get-tuple-element.90), channel_id=1, source_target_pairs={{0,24},{1,25},{2,26},{3,27},{4,28},{5,29},{6,30},{7,31},{8,0},{9,1... | collective-permute-start | bytes 74504 | tf_op jit(solution)/shard_map/ppermute | solution.py:593
  66.6 1.5 %result.1 = bf16[1024,256]{1,0:T(8,128)(2,1)} custom-call(f32[1024,256]{1,0:T(8,128)S(1)} %get-tuple-element.58.middle, bf16[1024,1024]{1,0:T(8,128)(2,1)S(1)} %get-tuple-element.59.activated, bf16[1024,256]{1,0:T(8,128)(2,1)S(1)} %get-tuple-element.60.w_down, f32[32,128]{1,0:T(8,128)S(1)} %copy-done.13), custom_call_target="tpu_custom_call" | custom-call | flops 2000000000 | bytes 1048576 | tf_op jit(solution)/shard_map/result/pallas_call | solution.py:431
  68.1 0.7 add_column.1
  (54 shorter events, 0.7 us)
Async XLA Ops:
  0.6 11.0 %collective-permute-start = (bf16[193,128]{1,0:T(8,128)(2,1)}, bf16[193,128]{1,0:T(8,128)(2,1)S(1)}, u32[]{:S(2)}, u32[]{:S(2)}) collective-permute-start(bf16[193,128]{1,0:T(8,128)(2,1)} %params.1), channel_id=1, source_target_pairs={{0,8},{1,9},{2,10},{3,11},{4,12},{5,13},{6,14},{7,15},{8,16},{9,17... | collective-permute-start | bytes 148232 | tf_op jit(solution)/shard_map/ppermute | solution.py:593
  3.7 8.0 %collective-permute-start.1 = (bf16[193,128]{1,0:T(8,128)(2,1)}, bf16[193,128]{1,0:T(8,128)(2,1)S(1)}, u32[]{:S(2)}, u32[]{:S(2)}) collective-permute-start(bf16[193,128]{1,0:T(8,128)(2,1)} %params.1), channel_id=1, source_target_pairs={{0,16},{1,17},{2,18},{3,19},{4,20},{5,21},{6,22},{7,23},{8,24},{9,... | collective-permute-start | bytes 148232 | tf_op jit(solution)/shard_map/ppermute | solution.py:593
  6.3 5.4 %collective-permute-start.2 = (bf16[193,128]{1,0:T(8,128)(2,1)}, bf16[193,128]{1,0:T(8,128)(2,1)S(1)}, u32[]{:S(2)}, u32[]{:S(2)}) collective-permute-start(bf16[193,128]{1,0:T(8,128)(2,1)} %params.1), channel_id=1, source_target_pairs={{0,24},{1,25},{2,26},{3,27},{4,28},{5,29},{6,30},{7,31},{8,0},{9,1... | collective-permute-start | bytes 148232 | tf_op jit(solution)/shard_map/ppermute | solution.py:593
  7.6 1.0 %copy-start.3 = (bf16[1024,256]{1,0:T(8,128)(2,1)S(1)}, bf16[1024,256]{1,0:T(8,128)(2,1)}, u32[]{:S(2)}) copy-start(bf16[1024,256]{1,0:T(8,128)(2,1)} %tok.5) | copy-start | bytes 1572868
  8.7 0.8 %copy-start.10 = (bf16[193,128]{1,0:T(8,128)(2,1)S(1)}, bf16[193,128]{1,0:T(8,128)(2,1)}, u32[]{:S(2)}) copy-start(bf16[193,128]{1,0:T(8,128)(2,1)} %params.1) | copy-start | bytes 148228
  9.5 0.7 copy-start.14
  10.9 0.8 %copy-start.15 = (bf16[256,1024]{1,0:T(8,128)(2,1)}, bf16[256,1024]{1,0:T(8,128)(2,1)S(1)}, u32[]{:S(2)}) copy-start(bf16[256,1024]{1,0:T(8,128)(2,1)S(1)} %get-tuple-element.64.normed_turned) | copy-start | bytes 1572868
  11.7 1.3 %collective-permute-start.6 = (bf16[1,240,128]{2,1,0:T(8,128)(2,1)S(1)}, bf16[1,240,128]{2,1,0:T(8,128)(2,1)S(1)}, u32[]{:S(2)}, u32[]{:S(2)}) collective-permute-start(bf16[1,240,128]{2,1,0:T(8,128)(2,1)S(1)} %get-tuple-element.51.refs_0_), channel_id=1, source_target_pairs={{0,1},{1,0},{2,3},{3,2},{4,5},{5,4},{6,7},{7,6},{8,9},{9,8},{10,11... | collective-permute-start | bytes 184328 | tf_op jit(solution)/shard_map/ppermute | solution.py:593
  11.8 3.5 %collective-permute-start.3 = (bf16[3,193,128]{2,1,0:T(8,128)(2,1)S(1)}, bf16[3,193,128]{2,1,0:T(8,128)(2,1)S(1)}, u32[]{:S(2)}, u32[]{:S(2)}) collective-permute-start(bf16[3,193,128]{2,1,0:T(8,128)(2,1)S(1)} %get-tuple-element.48.refs_0_), channel_id=1, source_target_pairs={{0,1},{1,0},{2,3},{3,2},{4,5},{5,4},{6,7},{7,6},{8,9},{9,8},{10,11... | collective-permute-start | bytes 444680 | tf_op jit(solution)/shard_map/ppermute | solution.py:593
  13.0 4.9 %collective-permute-start.7 = (bf16[2,240,128]{2,1,0:T(8,128)(2,1)S(1)}, bf16[2,240,128]{2,1,0:T(8,128)(2,1)S(1)}, u32[]{:S(2)}, u32[]{:S(2)}) collective-permute-start(bf16[2,240,128]{2,1,0:T(8,128)(2,1)S(1)} %stack.79.refs_0_), channel_id=1, source_target_pairs={{0,2},{1,5},{2,0},{3,7},{4,6},{5,1},{6,4},{7,3},{8,10},{9,13},{10,... | collective-permute-start | bytes 368648 | tf_op jit(solution)/shard_map/ppermute | solution.py:597
  14.6 3.4 %collective-permute-start.8 = (bf16[2,240,128]{2,1,0:T(8,128)(2,1)S(1)}, bf16[2,240,128]{2,1,0:T(8,128)(2,1)S(1)}, u32[]{:S(2)}, u32[]{:S(2)}) collective-permute-start(bf16[2,240,128]{2,1,0:T(8,128)(2,1)S(1)} %stack.79.refs_0_), channel_id=1, source_target_pairs={{1,7},{3,5},{5,3},{7,1},{9,15},{11,13},{13,11},{15,9},{17,23},{19,... | collective-permute-start | bytes 368648 | tf_op jit(solution)/shard_map/ppermute | solution.py:609
  15.3 12.4 %collective-permute-start.4 = (bf16[6,193,128]{2,1,0:T(8,128)(2,1)S(1)}, bf16[6,193,128]{2,1,0:T(8,128)(2,1)}, u32[]{:S(2)}, u32[]{:S(2)}) collective-permute-start(bf16[6,193,128]{2,1,0:T(8,128)(2,1)S(1)} %stack.78.refs_0_), channel_id=1, source_target_pairs={{0,2},{1,5},{2,0},{3,7},{4,6},{5,1},{6,4},{7,3},{8,10},{9,13},{10,... | collective-permute-start | bytes 889352 | tf_op jit(solution)/shard_map/ppermute | solution.py:597
  15.9 11.8 %collective-permute-start.5 = (bf16[6,193,128]{2,1,0:T(8,128)(2,1)S(1)}, bf16[6,193,128]{2,1,0:T(8,128)(2,1)}, u32[]{:S(2)}, u32[]{:S(2)}) collective-permute-start(bf16[6,193,128]{2,1,0:T(8,128)(2,1)S(1)} %stack.78.refs_0_), channel_id=1, source_target_pairs={{1,7},{3,5},{5,3},{7,1},{9,15},{11,13},{13,11},{15,9},{17,23},{19,... | collective-permute-start | bytes 889352 | tf_op jit(solution)/shard_map/ppermute | solution.py:609
  18.0 5.5 %collective-permute-start.9 = (bf16[4,240,128]{2,1,0:T(8,128)(2,1)S(1)}, bf16[4,240,128]{2,1,0:T(8,128)(2,1)S(1)}, u32[]{:S(2)}, u32[]{:S(2)}) collective-permute-start(bf16[4,240,128]{2,1,0:T(8,128)(2,1)S(1)} %stack.80.refs_1_), channel_id=1, source_target_pairs={{0,1},{1,0},{2,3},{3,2},{4,5},{5,4},{6,7},{7,6},{8,9},{9,8},{10,11... | collective-permute-start | bytes 737288 | tf_op jit(solution)/shard_map/ppermute | solution.py:593
  26.5 1.2 %copy-start = (bf16[1024,768]{1,0:T(8,128)(2,1)}, bf16[1024,768]{1,0:T(8,128)(2,1)S(1)}, u32[]{:S(2)}) copy-start(bf16[1024,768]{1,0:T(8,128)(2,1)S(1)} %get-tuple-element.61.project) | copy-start | bytes 4718596
  27.7 1.5 %copy-start.6 = (bf16[1024,256]{1,0:T(8,128)(2,1)}, bf16[1024,256]{1,0:T(8,128)(2,1)S(1)}, u32[]{:S(2)}) copy-start(bf16[1024,256]{1,0:T(8,128)(2,1)S(1)} %get-tuple-element.53.attended) | copy-start | bytes 1572868
  27.7 1.5 %copy-start.8 = (bf16[256,768]{1,0:T(8,128)(2,1)}, bf16[256,768]{1,0:T(8,128)(2,1)S(1)}, u32[]{:S(2)}) copy-start(bf16[256,768]{1,0:T(8,128)(2,1)S(1)} %get-tuple-element.65.w_qkv) | copy-start | bytes 1179652
  27.7 1.5 %copy-start.11 = (f32[32,128]{1,0:T(8,128)}, f32[32,128]{1,0:T(8,128)S(1)}, u32[]{:S(2)}) copy-start(f32[32,128]{1,0:T(8,128)S(1)} %get-tuple-element.54.small) | copy-start | bytes 49156
  27.7 3.6 %copy-start.2 = (bf16[1024,256]{1,0:T(8,128)(2,1)S(1)}, bf16[1024,256]{1,0:T(8,128)(2,1)}, u32[]{:S(2)}) copy-start(bf16[1024,256]{1,0:T(8,128)(2,1)} %cot.1) | copy-start | bytes 1572868
  29.2 2.1 %collective-permute-start.10 = (bf16[12,193,128]{2,1,0:T(8,128)(2,1)S(1)}, bf16[12,193,128]{2,1,0:T(8,128)(2,1)S(1)}, u32[]{:S(2)}, u32[]{:S(2)}) collective-permute-start(bf16[12,193,128]{2,1,0:T(8,128)(2,1)S(1)} %stack.81.refs_1_), channel_id=1, source_target_pairs={{0,1},{1,0},{2,3},{3,2},{4,5},{5,4},{6,7},{7,6},{8,9},{9,8},{10,11... | collective-permute-start | bytes 1778696 | tf_op jit(solution)/shard_map/ppermute | solution.py:593
  31.3 1.0 %copy-start.4 = (bf16[1024,256]{1,0:T(8,128)(2,1)S(1)}, bf16[1024,256]{1,0:T(8,128)(2,1)}, u32[]{:S(2)}) copy-start(bf16[1024,256]{1,0:T(8,128)(2,1)} %tok.5) | copy-start | bytes 1572868
  32.3 1.0 %copy-start.7 = (bf16[1024,256]{1,0:T(8,128)(2,1)S(1)}, bf16[1024,256]{1,0:T(8,128)(2,1)}, u32[]{:S(2)}) copy-start(bf16[1024,256]{1,0:T(8,128)(2,1)} %copy-done.6) | copy-start | bytes 1572868
  33.4 0.7 %copy-start.12 = (f32[32,128]{1,0:T(8,128)S(1)}, f32[32,128]{1,0:T(8,128)}, u32[]{:S(2)}) copy-start(f32[32,128]{1,0:T(8,128)} %copy-done.11) | copy-start | bytes 49156
  34.1 7.3 %copy-start.1 = (bf16[1024,768]{1,0:T(8,128)(2,1)S(1)}, bf16[1024,768]{1,0:T(8,128)(2,1)}, u32[]{:S(2)}) copy-start(bf16[1024,768]{1,0:T(8,128)(2,1)} %copy-done) | copy-start | bytes 4718596
  34.1 7.3 %copy-start.9 = (bf16[256,768]{1,0:T(8,128)(2,1)S(1)}, bf16[256,768]{1,0:T(8,128)(2,1)}, u32[]{:S(2)}) copy-start(bf16[256,768]{1,0:T(8,128)(2,1)} %copy-done.8) | copy-start | bytes 1179652
  34.1 7.3 %copy-start.16 = (bf16[256,1024]{1,0:T(8,128)(2,1)S(1)}, bf16[256,1024]{1,0:T(8,128)(2,1)}, u32[]{:S(2)}) copy-start(bf16[256,1024]{1,0:T(8,128)(2,1)} %copy-done.15) | copy-start | bytes 1572868
  40.9 6.3 %collective-permute-start.12 = (bf16[12,193,128]{2,1,0:T(8,128)(2,1)S(1)}, bf16[12,193,128]{2,1,0:T(8,128)(2,1)S(1)}, u32[]{:S(2)}, u32[]{:S(2)}) collective-permute-start(bf16[12,193,128]{2,1,0:T(8,128)(2,1)S(1)} %get-tuple-element.74), channel_id=1, source_target_pairs={{0,1},{1,0},{2,3},{3,2},{4,5},{5,4},{6,7},{7,6},{8,9},{9,8},{10,11... | collective-permute-start | bytes 1778696 | tf_op jit(solution)/shard_map/ppermute | solution.py:593
  41.4 3.7 %copy-start.5 = (bf16[1024,256]{1,0:T(8,128)(2,1)S(1)}, bf16[1024,256]{1,0:T(8,128)(2,1)}, u32[]{:S(2)}) copy-start(bf16[1024,256]{1,0:T(8,128)(2,1)} %tok.5) | copy-start | bytes 1572868
  41.4 3.7 %copy-start.13 = (f32[32,128]{1,0:T(8,128)S(1)}, f32[32,128]{1,0:T(8,128)}, u32[]{:S(2)}) copy-start(f32[32,128]{1,0:T(8,128)} %copy-done.11) | copy-start | bytes 49156
  44.9 2.4 %collective-permute-start.11 = (bf16[4,224,128]{2,1,0:T(8,128)(2,1)S(1)}, bf16[4,224,128]{2,1,0:T(8,128)(2,1)S(1)}, u32[]{:S(2)}, u32[]{:S(2)}) collective-permute-start(bf16[4,224,128]{2,1,0:T(8,128)(2,1)S(1)} %get-tuple-element.67), channel_id=1, source_target_pairs={{0,1},{1,0},{2,3},{3,2},{4,5},{5,4},{6,7},{7,6},{8,9},{9,8},{10,11... | collective-permute-start | bytes 688136 | tf_op jit(solution)/shard_map/ppermute | solution.py:593
  47.5 6.6 %collective-permute-start.13 = (bf16[4,96,128]{2,1,0:T(8,128)(2,1)S(1)}, bf16[4,96,128]{2,1,0:T(8,128)(2,1)S(1)}, u32[]{:S(2)}, u32[]{:S(2)}) collective-permute-start(bf16[4,96,128]{2,1,0:T(8,128)(2,1)S(1)} %get-tuple-element.76), channel_id=1, source_target_pairs={{0,6},{1,7},{2,4},{3,5},{4,2},{5,3},{6,0},{7,1},{8,14},{9,15},{10,... | collective-permute-start | bytes 294920 | tf_op jit(solution)/shard_map/ppermute | solution.py:593
  49.1 6.2 %collective-permute-start.14 = (bf16[4,96,128]{2,1,0:T(8,128)(2,1)S(1)}, bf16[4,96,128]{2,1,0:T(8,128)(2,1)S(1)}, u32[]{:S(2)}, u32[]{:S(2)}) collective-permute-start(bf16[4,96,128]{2,1,0:T(8,128)(2,1)S(1)} %get-tuple-element.77), channel_id=1, source_target_pairs={{0,2},{1,3},{2,0},{3,1},{4,6},{5,7},{6,4},{7,5},{8,10},{9,11},{10,... | collective-permute-start | bytes 294920 | tf_op jit(solution)/shard_map/ppermute | solution.py:593
  49.6 7.9 %collective-permute-start.15 = (bf16[4,96,128]{2,1,0:T(8,128)(2,1)S(1)}, bf16[4,96,128]{2,1,0:T(8,128)(2,1)S(1)}, u32[]{:S(2)}, u32[]{:S(2)}) collective-permute-start(bf16[4,96,128]{2,1,0:T(8,128)(2,1)S(1)} %get-tuple-element.78), channel_id=1, source_target_pairs={{0,4},{1,5},{2,6},{3,7},{4,0},{5,1},{6,2},{7,3},{8,12},{9,13},{10,... | collective-permute-start | bytes 294920 | tf_op jit(solution)/shard_map/ppermute | solution.py:593
  51.1 9.2 %collective-permute-start.19 = (bf16[4,97,128]{2,1,0:T(8,128)(2,1)S(1)}, bf16[4,97,128]{2,1,0:T(8,128)(2,1)S(1)}, u32[]{:S(2)}, u32[]{:S(2)}) collective-permute-start(bf16[4,97,128]{2,1,0:T(8,128)(2,1)S(1)} %get-tuple-element.84), channel_id=1, source_target_pairs={{0,6},{1,7},{2,4},{3,5},{4,2},{5,3},{6,0},{7,1},{8,14},{9,15},{10,... | collective-permute-start | bytes 297992 | tf_op jit(solution)/shard_map/ppermute | solution.py:593
  52.6 8.9 %collective-permute-start.20 = (bf16[4,97,128]{2,1,0:T(8,128)(2,1)S(1)}, bf16[4,97,128]{2,1,0:T(8,128)(2,1)S(1)}, u32[]{:S(2)}, u32[]{:S(2)}) collective-permute-start(bf16[4,97,128]{2,1,0:T(8,128)(2,1)S(1)} %get-tuple-element.85), channel_id=1, source_target_pairs={{0,2},{1,3},{2,0},{3,1},{4,6},{5,7},{6,4},{7,5},{8,10},{9,11},{10,... | collective-permute-start | bytes 297992 | tf_op jit(solution)/shard_map/ppermute | solution.py:593
  54.1 7.4 %collective-permute-start.21 = (bf16[4,97,128]{2,1,0:T(8,128)(2,1)S(1)}, bf16[4,97,128]{2,1,0:T(8,128)(2,1)S(1)}, u32[]{:S(2)}, u32[]{:S(2)}) collective-permute-start(bf16[4,97,128]{2,1,0:T(8,128)(2,1)S(1)} %get-tuple-element.86), channel_id=1, source_target_pairs={{0,4},{1,5},{2,6},{3,7},{4,0},{5,1},{6,2},{7,3},{8,12},{9,13},{10,... | collective-permute-start | bytes 297992 | tf_op jit(solution)/shard_map/ppermute | solution.py:593
  57.6 6.1 %collective-permute-start.16 = (bf16[96,128]{1,0:T(8,128)(2,1)S(1)}, bf16[96,128]{1,0:T(8,128)(2,1)S(1)}, u32[]{:S(2)}, u32[]{:S(2)}) collective-permute-start(bf16[96,128]{1,0:T(8,128)(2,1)S(1)} %get-tuple-element.80), channel_id=1, source_target_pairs={{0,8},{1,9},{2,10},{3,11},{4,12},{5,13},{6,14},{7,15},{8,16},{9,17... | collective-permute-start | bytes 73736 | tf_op jit(solution)/shard_map/ppermute | solution.py:593
  58.3 9.8 %collective-permute-start.17 = (bf16[96,128]{1,0:T(8,128)(2,1)S(1)}, bf16[96,128]{1,0:T(8,128)(2,1)S(1)}, u32[]{:S(2)}, u32[]{:S(2)}) collective-permute-start(bf16[96,128]{1,0:T(8,128)(2,1)S(1)} %get-tuple-element.81), channel_id=1, source_target_pairs={{0,16},{1,17},{2,18},{3,19},{4,20},{5,21},{6,22},{7,23},{8,24},{9,... | collective-permute-start | bytes 73736 | tf_op jit(solution)/shard_map/ppermute | solution.py:593
  60.3 7.8 %collective-permute-start.18 = (bf16[96,128]{1,0:T(8,128)(2,1)S(1)}, bf16[96,128]{1,0:T(8,128)(2,1)S(1)}, u32[]{:S(2)}, u32[]{:S(2)}) collective-permute-start(bf16[96,128]{1,0:T(8,128)(2,1)S(1)} %get-tuple-element.82), channel_id=1, source_target_pairs={{0,24},{1,25},{2,26},{3,27},{4,28},{5,29},{6,30},{7,31},{8,0},{9,1... | collective-permute-start | bytes 73736 | tf_op jit(solution)/shard_map/ppermute | solution.py:593
  61.6 6.5 %collective-permute-start.22 = (bf16[97,128]{1,0:T(8,128)(2,1)S(1)}, bf16[97,128]{1,0:T(8,128)(2,1)S(1)}, u32[]{:S(2)}, u32[]{:S(2)}) collective-permute-start(bf16[97,128]{1,0:T(8,128)(2,1)S(1)} %get-tuple-element.88), channel_id=1, source_target_pairs={{0,8},{1,9},{2,10},{3,11},{4,12},{5,13},{6,14},{7,15},{8,16},{9,17... | collective-permute-start | bytes 74504 | tf_op jit(solution)/shard_map/ppermute | solution.py:593
  62.5 5.6 %collective-permute-start.23 = (bf16[97,128]{1,0:T(8,128)(2,1)S(1)}, bf16[97,128]{1,0:T(8,128)(2,1)S(1)}, u32[]{:S(2)}, u32[]{:S(2)}) collective-permute-start(bf16[97,128]{1,0:T(8,128)(2,1)S(1)} %get-tuple-element.89), channel_id=1, source_target_pairs={{0,16},{1,17},{2,18},{3,19},{4,20},{5,21},{6,22},{7,23},{8,24},{9,... | collective-permute-start | bytes 74504 | tf_op jit(solution)/shard_map/ppermute | solution.py:593
  63.7 4.4 %collective-permute-start.24 = (bf16[97,128]{1,0:T(8,128)(2,1)S(1)}, bf16[97,128]{1,0:T(8,128)(2,1)S(1)}, u32[]{:S(2)}, u32[]{:S(2)}) collective-permute-start(bf16[97,128]{1,0:T(8,128)(2,1)S(1)} %get-tuple-element.90), channel_id=1, source_target_pairs={{0,24},{1,25},{2,26},{3,27},{4,28},{5,29},{6,30},{7,31},{8,0},{9,1... | collective-permute-start | bytes 74504 | tf_op jit(solution)/shard_map/ppermute | solution.py:593

commit v13 on v9

--- a/solution.py
+++ b/solution.py
@@ -97,12 +97,6 @@
         ].astype(BF16)
 
 
-def turned_to_flat(turned, rows, columns, flat, start):
-    per_row = columns // LANES
-    for j in range(per_row):
-        flat[pl.ds(start + j, rows, stride=per_row), :] = turned[j * LANES : (j + 1) * LANES, :].T
-
-
 def matrix_to_flat(matrix, rows, columns, flat, start):
     per_row = columns // LANES
     for j in range(per_row):
@@ -114,8 +108,8 @@
     normed_out[...] = normed
     normed_turned[...] = normed.astype(BF16).T
     own[...] = params[...]
-    causal = lax.broadcasted_iota(jnp.int32, (SEQ, SEQ), 1) <= lax.broadcasted_iota(
-        jnp.int32, (SEQ, SEQ), 0
+    causal = lax.broadcasted_iota(jnp.int32, (SEQ, SEQ), 0) <= lax.broadcasted_iota(
+        jnp.int32, (SEQ, SEQ), 1
     )
     for s in range(seg.shape[0]):
         across = jnp.broadcast_to(seg[s : s + 1, :].astype(F32), (SEQ, SEQ))
@@ -158,36 +152,32 @@
         ],
         axis=1,
     )
-    def some(g, carry):
-        span = pl.ds(pl.multiple_of(g * WIDE, WIDE), WIDE)
-        normed_low = (normed[span, :] * gain + shift).astype(BF16)
-        project = (dot(normed_low, w_qkv[...]) + bias).astype(BF16)
-        project_out[span, :] = project
-        scores, values = [], []
-        for s in range(GROUP):
-            rows = slice(s * SEQ, (s + 1) * SEQ)
-            scores.append(
-                dot_nt(project[rows, :D] * SCALE, spread_heads(project[rows, D : 2 * D]))
+    project_out[...] = (
+        dot((normed[...] * gain + shift).astype(BF16), w_qkv[...]) + bias
+    ).astype(BF16)
+    for g in range(normed.shape[0] // WIDE):
+        starts = range(g * WIDE, (g + 1) * WIDE, SEQ)
+        scores = [
+            dot_nt(
+                spread_heads(project_out[r : r + SEQ, D : 2 * D]),
+                project_out[r : r + SEQ, :D] * SCALE,
             )
-            values.append(spread_heads(project[rows, 2 * D :]))
+            for r in starts
+        ]
         weights = []
-        for s in range(GROUP):
-            low = []
-            open_pairs = allowed[pl.ds(pl.multiple_of(g * WIDE + s * SEQ, SEQ), SEQ), :] > 0.5
+        for r, score in zip(starts, scores):
+            open_pairs = allowed[r : r + SEQ, :] > 0.5
+            turned = []
             for h in range(HEADS):
-                mine = jnp.where(open_pairs, scores[s][:, h * SEQ : (h + 1) * SEQ], -1e30)
-                grown = jnp.exp(mine - jnp.max(mine, axis=-1, keepdims=True))
-                low.append(
-                    (grown * (1.0 / jnp.sum(grown, axis=-1, keepdims=True))).astype(BF16)
-                )
-            weights.append(jnp.concatenate(low, axis=1))
-        weights_out[span, :] = jnp.concatenate(weights, axis=0)
-        attended_out[span, :] = jnp.concatenate(
-            [dot(weights[s], values[s]).astype(BF16) for s in range(GROUP)], axis=0
-        )
-        return carry
-
-    lax.fori_loop(0, normed.shape[0] // WIDE, some, 0)
+                mine = jnp.where(open_pairs, score[h * SEQ : (h + 1) * SEQ, :], -1e30)
+                grown = jnp.exp(mine - jnp.max(mine, axis=0, keepdims=True))
+                low = (grown * (1.0 / jnp.sum(grown, axis=0, keepdims=True))).astype(BF16)
+                weights_out[r : r + SEQ, h * SEQ : (h + 1) * SEQ] = low
+                turned.append(low.T)
+            weights.append(jnp.concatenate(turned, axis=1))
+        for r, weight in zip(starts, weights):
+            value = spread_heads(project_out[r : r + SEQ, 2 * D :])
+            attended_out[r : r + SEQ, :] = dot(weight, value).astype(BF16)
 
 
 def feed_kernel(
@@ -219,7 +209,6 @@
     normed_low = (normed * gain + small_vector(small, SHIFT_TWO, 2)).astype(BF16)
     normed_turned = normed_low.T
     cotangent = cot[...]
-    cot_turned = cotangent.T
     slope = 0.7978845608028654
     cubic = slope * 0.044715
     row_up, row_down = ROW_UP - ROW_OUT, ROW_DOWN - ROW_OUT
@@ -247,7 +236,10 @@
 
     def weight_gradients(c):
         columns = slice(c, c + CHUNK)
-        turned_to_flat(dot(cot_turned, activated_out[:, columns]), CHUNK, D, flat, row_down + c * D // LANES)
+        if (c // CHUNK) % 2:
+            start, rows = c - CHUNK, 2 * CHUNK
+            turned = activated_out[:, start : start + rows].T
+            matrix_to_flat(dot(turned, cotangent), rows, D, flat, row_down + start * D // LANES)
         grads = dot(normed_turned, grad_hidden[:, columns])
         for j in range(CHUNK // LANES):
             flat[pl.ds(row_up + c // LANES + j, D, stride=FF // LANES), :] = grads[
@@ -305,39 +297,34 @@
     ids, project, weights, grad_attended, normed_turned, w_qkv, small, first_in,
     grad_project, keep_out, send_out, flat, wide,
 ):
-    def some(g, carry):
-        base = g * WIDE
-        spans = [pl.ds(pl.multiple_of(base + s * SEQ, SEQ), SEQ) for s in range(GROUP)]
+    products, sums = 0.0, 0.0
+    for g in range(project.shape[0] // WIDE):
+        spans = [slice(r, r + SEQ) for r in range(g * WIDE, (g + 1) * WIDE, SEQ)]
         grad_weights = [
-            dot_nt(grad_attended[span, :], spread_heads(project[span, 2 * D :])) for span in spans
+            dot_nt(spread_heads(project[span, 2 * D :]), grad_attended[span, :]) for span in spans
         ]
-        scores_low, scores_turned, weights_turned = [], [], []
-        for s, span in enumerate(spans):
-            low, turned, mine_turned = [], [], []
+        scores_low, scores_turned = [], []
+        for span, grads in zip(spans, grad_weights):
+            low, turned = [], []
             for h in range(HEADS):
-                columns = slice(h * SEQ, (h + 1) * SEQ)
-                mine_low = weights[span, columns]
-                mine = mine_low.astype(F32)
-                product = mine * grad_weights[s][:, columns]
-                grad_scores = (product - mine * jnp.sum(product, axis=-1, keepdims=True)) * SCALE
-                low.append(grad_scores.astype(BF16))
-                turned.append(low[-1].T)
-                mine_turned.append(mine_low.T)
+                mine = weights[span, h * SEQ : (h + 1) * SEQ].astype(F32)
+                product = mine * grads[h * SEQ : (h + 1) * SEQ, :]
+                grad_scores = (product - mine * jnp.sum(product, axis=0, keepdims=True)) * SCALE
+                turned.append(grad_scores.astype(BF16))
+                low.append(turned[-1].T)
             scores_low.append(jnp.concatenate(low, axis=1))
             scores_turned.append(jnp.concatenate(turned, axis=1))
-            weights_turned.append(jnp.concatenate(mine_turned, axis=1))
         for s, span in enumerate(spans):
             key = spread_heads(project[span, D : 2 * D])
             grad_project[span, :D] = dot(scores_low[s], key).astype(BF16)
             query = spread_heads(project[span, :D])
             grad_project[span, D : 2 * D] = dot(scores_turned[s], query).astype(BF16)
-            grad_value = dot(weights_turned[s], spread_heads(grad_attended[span, :]))
+            grad_value = dot(weights[span, :], spread_heads(grad_attended[span, :]))
             grad_project[span, 2 * D :] = grad_value.astype(BF16)
-        return carry
-
-    lax.fori_loop(0, project.shape[0] // WIDE, some, 0)
-    products = dot(normed_turned[...], grad_project[...])
-    sums = jnp.sum(fold_rows(grad_project[...].astype(F32)), axis=0, keepdims=True)
+        span = slice(g * WIDE, (g + 1) * WIDE)
+        products += dot(normed_turned[:, span], grad_project[span, :])
+        sums += fold_rows(grad_project[span, :].astype(F32))
+    sums = jnp.sum(sums, axis=0, keepdims=True)
     gain = jnp.broadcast_to(small_vector(small, GAIN_ONE, 2), (LANES, D)).T
     shift = jnp.broadcast_to(small_vector(small, SHIFT_ONE, 2), (LANES, D)).T
     grad_gain = jnp.zeros((D, LANES), F32)

time: 62.2 us -> 60.8 us (0.977)
  Pallas kernels: 19 us -> 17.6 us
    pallas_call x11, Pallas kernels: 19 us -> 17.6 us  [call(): pl.pallas_call(kernel, in_specs=[SMEM_SPEC] * with_ids + [VMEM_SPEC] * le...]
  transfers between devices with their start and end apart: 23 -> 23, of which waited for: 12 -> 12; matrix products, arithmetic and copies ran while one was open for 0% -> 0% of each run, Pallas kernels for 18% -> 17%
where the time goes in v13:
time: 60.8 us; the launch traced here: 60.5 us
  starting transfers between devices  24.1 us (40%)
  Pallas kernels  17.6 us (29%)
  waiting for transfers between devices  15.5 us (25%)
  local copies, waits for them, and re-layouts  2.63 us (4%)
  between operations  0.79 us (1%)
    ppermute x23, starting transfers between devices, move(): return lax.ppermute(values, 'fsdp', pairs)  24.1 us
    pallas_call x11, Pallas kernels, call(): pl.pallas_call(kernel, in_specs=[SMEM_SPEC] * with_ids + [VMEM_SPEC] * le...  17.6 us
    ppermute x23, waiting for transfers between devices, move(): return lax.ppermute(values, 'fsdp', pairs)  15.5 us
    unnamed x10, local copies, waits for them, and re-layouts  2.54 us
  transfers between devices with their start and end apart: 23, of which 12 were waited for; matrix products, arithmetic and copies ran while one was open for 0% of the time, Pallas kernels for 17%

profile of v13, /device:TPU:0, one launch (start us, length us, event | category | flops | bytes accessed | tf_op | source)
XLA Modules:
  0.0 60.5 jit_solution(1008943865292532192)
XLA Ops:
  0.6 3.1 %collective-permute-start = (bf16[193,128]{1,0:T(8,128)(2,1)}, bf16[193,128]{1,0:T(8,128)(2,1)S(1)}, u32[]{:S(2)}, u32[]{:S(2)}) collective-permute-start(bf16[193,128]{1,0:T(8,128)(2,1)} %params.1), channel_id=1, source_target_pairs={{0,8},{1,9},{2,10},{3,11},{4,12},{5,13},{6,14},{7,15},{8,16},{9,17... | collective-permute-start | bytes 148232 | tf_op jit(solution)/shard_map/ppermute | solution.py:559
  3.7 2.6 %collective-permute-start.1 = (bf16[193,128]{1,0:T(8,128)(2,1)}, bf16[193,128]{1,0:T(8,128)(2,1)S(1)}, u32[]{:S(2)}, u32[]{:S(2)}) collective-permute-start(bf16[193,128]{1,0:T(8,128)(2,1)} %params.1), channel_id=1, source_target_pairs={{0,16},{1,17},{2,18},{3,19},{4,20},{5,21},{6,22},{7,23},{8,24},{9,... | collective-permute-start | bytes 148232 | tf_op jit(solution)/shard_map/ppermute | solution.py:559
  6.3 1.3 %collective-permute-start.2 = (bf16[193,128]{1,0:T(8,128)(2,1)}, bf16[193,128]{1,0:T(8,128)(2,1)S(1)}, u32[]{:S(2)}, u32[]{:S(2)}) collective-permute-start(bf16[193,128]{1,0:T(8,128)(2,1)} %params.1), channel_id=1, source_target_pairs={{0,24},{1,25},{2,26},{3,27},{4,28},{5,29},{6,30},{7,31},{8,0},{9,1... | collective-permute-start | bytes 148232 | tf_op jit(solution)/shard_map/ppermute | solution.py:559
  7.6 1.0 %copy-done.1 = bf16[1024,256]{1,0:T(8,128)(2,1)S(1)} copy-done((bf16[1024,256]{1,0:T(8,128)(2,1)S(1)}, bf16[1024,256]{1,0:T(8,128)(2,1)}, u32[]{:S(2)}) %copy-start.1) | copy-done | bytes 524312
  8.7 0.8 %copy-done.3 = bf16[193,128]{1,0:T(8,128)(2,1)S(1)} copy-done((bf16[193,128]{1,0:T(8,128)(2,1)S(1)}, bf16[193,128]{1,0:T(8,128)(2,1)}, u32[]{:S(2)}) %copy-start.3) | copy-done | bytes 49432
  9.5 0.7 %copy-done.4 = s32[1024]{0:T(1024)S(1)} copy-done((s32[1024]{0:T(1024)S(1)}, s32[1024]{0:T(1024)}, u32[]{:S(2)}) %copy-start.4) | copy-done | bytes 4120
  10.2 0.7 %prepare.1 = (f32[1024,256]{1,0:T(8,128)S(1)}, bf16[256,1024]{1,0:T(8,128)(2,1)S(1)}, bf16[193,128]{1,0:T(8,128)(2,1)S(1)}, f32[1024,128]{1,0:T(8,128)S(1)}) custom-call(bf16[1024,256]{1,0:T(8,128)(2,1)S(1)} %copy-done.1, bf16[193,128]{1,0:T(8,128)(2,1)S(1)} %copy-done.3, s32[8,128]{1,0:T(8,128)S(1)} %bitcast.10), custom_call_target="tpu_custom_call" | custom-call | flops 2000000000 | bytes 1048576 | tf_op jit(solution)/shard_map/prepare/pallas_call | solution.py:417
  10.9 0.1 sort_shares.1
  11.0 2.5 %collective-permute-start.6 = (bf16[240,128]{1,0:T(8,128)(2,1)S(1)}, bf16[240,128]{1,0:T(8,128)(2,1)S(1)}, u32[]{:S(2)}, u32[]{:S(2)}) collective-permute-start(bf16[240,128]{1,0:T(8,128)(2,1)S(1)} %get-tuple-element.42.refs_0_), channel_id=1, source_target_pairs={{0,6},{1,7},{2,4},{3,5},{4,2},{5,3},{6,0},{7,1},{8,14},{9,15},{10,... | collective-permute-start | bytes 184328 | tf_op jit(solution)/shard_map/ppermute | solution.py:559
  13.5 0.5 collective-permute-start.7
  14.0 0.5 collective-permute-start.8
  14.5 2.4 %collective-permute-start.3 = (bf16[3,193,128]{2,1,0:T(8,128)(2,1)S(1)}, bf16[3,193,128]{2,1,0:T(8,128)(2,1)S(1)}, u32[]{:S(2)}, u32[]{:S(2)}) collective-permute-start(bf16[3,193,128]{2,1,0:T(8,128)(2,1)S(1)} %get-tuple-element.39.refs_0_), channel_id=1, source_target_pairs={{0,6},{1,7},{2,4},{3,5},{4,2},{5,3},{6,0},{7,1},{8,14},{9,15},{10,... | collective-permute-start | bytes 444680 | tf_op jit(solution)/shard_map/ppermute | solution.py:559
  17.0 0.5 collective-permute-start.4
  17.5 0.5 collective-permute-start.5
  18.0 0.3 collective-permute-done.7.refs_2_
  18.3 1.4 %collective-permute-done.8.refs_3_ = bf16[240,128]{1,0:T(8,128)(2,1)S(1)} collective-permute-done((bf16[240,128]{1,0:T(8,128)(2,1)S(1)}, bf16[240,128]{1,0:T(8,128)(2,1)S(1)}, u32[]{:S(2)}, u32[]{:S(2)}) %collective-permute-start.8) | collective-permute-done | bytes 61472 | tf_op jit(solution)/shard_map/ppermute | solution.py:559
  19.8 0.5 collective-permute-start.11
  20.3 0.7 %collective-permute-done.10.refs_5_ = bf16[240,128]{1,0:T(8,128)(2,1)S(1)} collective-permute-done((bf16[240,128]{1,0:T(8,128)(2,1)S(1)}, bf16[240,128]{1,0:T(8,128)(2,1)S(1)}, u32[]{:S(2)}, u32[]{:S(2)}) %collective-permute-start.10) | collective-permute-done | bytes 61472 | tf_op jit(solution)/shard_map/ppermute | solution.py:559
  21.0 0.2 collective-permute-start.12
  21.2 0.1 stack.36.ids
  21.3 1.0 %collective-permute-done.12.refs_7_ = bf16[240,128]{1,0:T(8,128)(2,1)S(1)} collective-permute-done((bf16[240,128]{1,0:T(8,128)(2,1)S(1)}, bf16[240,128]{1,0:T(8,128)(2,1)S(1)}, u32[]{:S(2)}, u32[]{:S(2)}) %collective-permute-start.12) | collective-permute-done | bytes 61472 | tf_op jit(solution)/shard_map/ppermute | solution.py:559
  22.3 2.6 %attend.1 = (bf16[1024,768]{1,0:T(8,128)(2,1)S(1)}, bf16[1024,512]{1,0:T(8,128)(2,1)S(1)}, bf16[1024,256]{1,0:T(8,128)(2,1)S(1)}, bf16[256,768]{1,0:T(8,128)(2,1...) custom-call(s32[8]{0:T(128)S(1)} %stack.36.ids, f32[1024,128]{1,0:T(8,128)S(1)} %get-tuple-element.40.allowed, ...), custom_call_target="tpu_custom_call" | custom-call | flops 200000000 | bytes 1048576 | tf_op jit(solution)/shard_map/attend/pallas_call | solution.py:417
  24.9 0.0 copy-start
  25.0 0.2 collective-permute-start.14
  25.2 0.4 collective-permute-start.13
  25.6 1.5 %collective-permute-done.13.refs_2_ = bf16[3,193,128]{2,1,0:T(8,128)(2,1)S(1)} collective-permute-done((bf16[3,193,128]{2,1,0:T(8,128)(2,1)S(1)}, bf16[3,193,128]{2,1,0:T(8,128)(2,1)S(1)}, u32[]{:S(2)}, u32[]{:S(2)}) %collective-permute-start.13) | collective-permute-done | bytes 148256 | tf_op jit(solution)/shard_map/ppermute | solution.py:559
  27.1 6.3 %feed.1 = (f32[1024,256]{1,0:T(8,128)S(1)}, bf16[1024,1024]{1,0:T(8,128)(2,1)S(1)}, f32[1024,256]{1,0:T(8,128)S(1)}, bf16[1024,256]{1,0:T(8,128)(2,1)S(1)}, bf16...) custom-call(s32[8]{0:T(128)S(1)} %stack.36.ids, ...), custom_call_target="tpu_custom_call" | custom-call | flops 8000000000 | bytes 1048576 | tf_op jit(solution)/shard_map/feed/pallas_call | solution.py:417
  33.4 0.2 collective-permute-start.16
  33.7 3.2 %attend_back.1 = (bf16[1024,768]{1,0:T(8,128)(2,1)S(1)}, f32[4,224,128]{2,1,0:T(8,128)S(1)}, bf16[4,224,128]{2,1,0:T(8,128)(2,1)S(1)}) custom-call(s32[8]{0:T(128)S(1)} %stack.36.ids, bf16[1024,768]{1,0:T(8,128)(2,1)S(1)} %get-tuple-element.53.project, bf16[1024,512]{1,0:T(8,128)(2,1)S(1)} %get-tuple-element.54.weights, ...), custom_call_target="tpu_custom_call" | custom-call | flops 4000000000 | bytes 1048576 | tf_op jit(solution)/shard_map/attend_back/pallas_call | solution.py:417
  36.9 0.4 collective-permute-start.15
  37.3 1.1 %collective-permute-done.15.first_in = bf16[4,224,128]{2,1,0:T(8,128)(2,1)S(1)} collective-permute-done((bf16[4,224,128]{2,1,0:T(8,128)(2,1)S(1)}, bf16[4,224,128]{2,1,0:T(8,128)(2,1)S(1)}, u32[]{:S(2)}, u32[]{:S(2)}) %collective-permute-start.15) | collective-permute-done | bytes 229408 | tf_op jit(solution)/shard_map/ppermute | solution.py:559
  38.5 0.2 add_core.1
  38.7 2.2 %collective-permute-start.17 = (bf16[4,193,128]{2,1,0:T(8,128)(2,1)S(1)}, bf16[4,193,128]{2,1,0:T(8,128)(2,1)S(1)}, u32[]{:S(2)}, u32[]{:S(2)}) collective-permute-start(bf16[4,193,128]{2,1,0:T(8,128)(2,1)S(1)} %get-tuple-element.66), channel_id=1, source_target_pairs={{0,6},{1,7},{2,4},{3,5},{4,2},{5,3},{6,0},{7,1},{8,14},{9,15},{10,... | collective-permute-start | bytes 592904 | tf_op jit(solution)/shard_map/ppermute | solution.py:559
  40.9 0.3 collective-permute-start.18
  41.2 1.3 %collective-permute-start.19 = (bf16[4,193,128]{2,1,0:T(8,128)(2,1)S(1)}, bf16[4,193,128]{2,1,0:T(8,128)(2,1)S(1)}, u32[]{:S(2)}, u32[]{:S(2)}) collective-permute-start(bf16[4,193,128]{2,1,0:T(8,128)(2,1)S(1)} %get-tuple-element.68), channel_id=1, source_target_pairs={{0,4},{1,5},{2,6},{3,7},{4,0},{5,1},{6,2},{7,3},{8,12},{9,13},{10,... | collective-permute-start | bytes 592904 | tf_op jit(solution)/shard_map/ppermute | solution.py:559
  42.4 2.1 %input_grad.1 = f32[1024,256]{1,0:T(8,128)} custom-call(bf16[1024,256]{1,0:T(8,128)(2,1)S(1)} %copy-done.2, bf16[1024,768]{1,0:T(8,128)(2,1)S(1)} %get-tuple-element.59.grad_project, f32[1024,256]{1,0:T(8,128)S(1)} %get-tuple-element.60.grad_middle, bf16[256,768]{1,0:T(8,128)(2,1)S(1)} %get-tuple-element.57.w_qkv, f32[32,128]{1,0:T(8,128)S(1)} %get-tuple-element.45.small), custom_call_target="tpu_custom_call" | custom-call | flops 2000000000 | bytes 1048576 | tf_op jit(solution)/shard_map/input_grad/pallas_call | solution.py:417
  44.5 3.1 %collective-permute-done.17.refs_0_ = bf16[4,193,128]{2,1,0:T(8,128)(2,1)S(1)} collective-permute-done((bf16[4,193,128]{2,1,0:T(8,128)(2,1)S(1)}, bf16[4,193,128]{2,1,0:T(8,128)(2,1)S(1)}, u32[]{:S(2)}, u32[]{:S(2)}) %collective-permute-start.17) | collective-permute-done | bytes 197664 | tf_op jit(solution)/shard_map/ppermute | solution.py:559
  47.6 3.4 %collective-permute-done.18.refs_1_ = bf16[4,193,128]{2,1,0:T(8,128)(2,1)S(1)} collective-permute-done((bf16[4,193,128]{2,1,0:T(8,128)(2,1)S(1)}, bf16[4,193,128]{2,1,0:T(8,128)(2,1)S(1)}, u32[]{:S(2)}, u32[]{:S(2)}) %collective-permute-start.18) | collective-permute-done | bytes 197664 | tf_op jit(solution)/shard_map/ppermute | solution.py:559
  51.0 0.4 collective-permute-done.19.refs_2_
  51.4 0.2 add_plane.1
  51.6 2.0 %collective-permute-start.20 = (bf16[193,128]{1,0:T(8,128)(2,1)S(1)}, bf16[193,128]{1,0:T(8,128)(2,1)S(1)}, u32[]{:S(2)}, u32[]{:S(2)}) collective-permute-start(bf16[193,128]{1,0:T(8,128)(2,1)S(1)} %get-tuple-element.70), channel_id=1, source_target_pairs={{0,8},{1,9},{2,10},{3,11},{4,12},{5,13},{6,14},{7,15},{8,16},{9,17... | collective-permute-start | bytes 148232 | tf_op jit(solution)/shard_map/ppermute | solution.py:559
  53.5 1.5 %collective-permute-start.21 = (bf16[193,128]{1,0:T(8,128)(2,1)S(1)}, bf16[193,128]{1,0:T(8,128)(2,1)S(1)}, u32[]{:S(2)}, u32[]{:S(2)}) collective-permute-start(bf16[193,128]{1,0:T(8,128)(2,1)S(1)} %get-tuple-element.71), channel_id=1, source_target_pairs={{0,16},{1,17},{2,18},{3,19},{4,20},{5,21},{6,22},{7,23},{8,24},{9,... | collective-permute-start | bytes 148232 | tf_op jit(solution)/shard_map/ppermute | solution.py:559
  55.0 1.0 %collective-permute-start.22 = (bf16[193,128]{1,0:T(8,128)(2,1)S(1)}, bf16[193,128]{1,0:T(8,128)(2,1)S(1)}, u32[]{:S(2)}, u32[]{:S(2)}) collective-permute-start(bf16[193,128]{1,0:T(8,128)(2,1)S(1)} %get-tuple-element.72), channel_id=1, source_target_pairs={{0,24},{1,25},{2,26},{3,27},{4,28},{5,29},{6,30},{7,31},{8,0},{9,1... | collective-permute-start | bytes 148232 | tf_op jit(solution)/shard_map/ppermute | solution.py:559
  56.0 1.5 %result.1 = bf16[1024,256]{1,0:T(8,128)(2,1)} custom-call(f32[1024,256]{1,0:T(8,128)S(1)} %get-tuple-element.50.middle, bf16[1024,1024]{1,0:T(8,128)(2,1)S(1)} %get-tuple-element.51.activated, bf16[1024,256]{1,0:T(8,128)(2,1)S(1)} %get-tuple-element.52.w_down, f32[32,128]{1,0:T(8,128)S(1)} %get-tuple-element.45.small), custom_call_target="tpu_custom_call" | custom-call | flops 2000000000 | bytes 1048576 | tf_op jit(solution)/shard_map/result/pallas_call | solution.py:417
  57.5 0.3 collective-permute-done.20.refs_0_
  57.8 1.6 %collective-permute-done.21.refs_1_ = bf16[193,128]{1,0:T(8,128)(2,1)S(1)} collective-permute-done((bf16[193,128]{1,0:T(8,128)(2,1)S(1)}, bf16[193,128]{1,0:T(8,128)(2,1)S(1)}, u32[]{:S(2)}, u32[]{:S(2)}) %collective-permute-start.21) | collective-permute-done | bytes 49440 | tf_op jit(solution)/shard_map/ppermute | solution.py:559
  59.4 0.5 collective-permute-done.22.refs_2_
  59.9 0.7 %add_column.1 = f32[193,128]{1,0:T(8,128)} custom-call(f32[193,128]{1,0:T(8,128)S(1)} %get-tuple-element.69.kept, bf16[193,128]{1,0:T(8,128)(2,1)S(1)} %collective-permute-done.20.refs_0_, bf16[193,128]{1,0:T(8,128)(2,1)S(1)} %collective-permute-done.21.refs_1_, bf16[193,128]{1,0:T(8,128)(2,1)S(1)} %collective-permute-done.22.refs_2_), custom_call_target="tpu_custom_call" | custom-call | flops 1000000000 | bytes 1048576 | tf_op jit(solution)/shard_map/add_column/pallas_call | solution.py:417
  (20 shorter events, 0.1 us)
Async XLA Ops:
  0.6 10.2 %collective-permute-start = (bf16[193,128]{1,0:T(8,128)(2,1)}, bf16[193,128]{1,0:T(8,128)(2,1)S(1)}, u32[]{:S(2)}, u32[]{:S(2)}) collective-permute-start(bf16[193,128]{1,0:T(8,128)(2,1)} %params.1), channel_id=1, source_target_pairs={{0,8},{1,9},{2,10},{3,11},{4,12},{5,13},{6,14},{7,15},{8,16},{9,17... | collective-permute-start | bytes 148232 | tf_op jit(solution)/shard_map/ppermute | solution.py:559
  3.7 7.2 %collective-permute-start.1 = (bf16[193,128]{1,0:T(8,128)(2,1)}, bf16[193,128]{1,0:T(8,128)(2,1)S(1)}, u32[]{:S(2)}, u32[]{:S(2)}) collective-permute-start(bf16[193,128]{1,0:T(8,128)(2,1)} %params.1), channel_id=1, source_target_pairs={{0,16},{1,17},{2,18},{3,19},{4,20},{5,21},{6,22},{7,23},{8,24},{9,... | collective-permute-start | bytes 148232 | tf_op jit(solution)/shard_map/ppermute | solution.py:559
  6.3 4.6 %collective-permute-start.2 = (bf16[193,128]{1,0:T(8,128)(2,1)}, bf16[193,128]{1,0:T(8,128)(2,1)S(1)}, u32[]{:S(2)}, u32[]{:S(2)}) collective-permute-start(bf16[193,128]{1,0:T(8,128)(2,1)} %params.1), channel_id=1, source_target_pairs={{0,24},{1,25},{2,26},{3,27},{4,28},{5,29},{6,30},{7,31},{8,0},{9,1... | collective-permute-start | bytes 148232 | tf_op jit(solution)/shard_map/ppermute | solution.py:559
  7.6 1.0 %copy-start.1 = (bf16[1024,256]{1,0:T(8,128)(2,1)S(1)}, bf16[1024,256]{1,0:T(8,128)(2,1)}, u32[]{:S(2)}) copy-start(bf16[1024,256]{1,0:T(8,128)(2,1)} %tok.5) | copy-start | bytes 1572868
  8.7 0.8 %copy-start.3 = (bf16[193,128]{1,0:T(8,128)(2,1)S(1)}, bf16[193,128]{1,0:T(8,128)(2,1)}, u32[]{:S(2)}) copy-start(bf16[193,128]{1,0:T(8,128)(2,1)} %params.1) | copy-start | bytes 148228
  9.5 0.7 %copy-start.4 = (s32[1024]{0:T(1024)S(1)}, s32[1024]{0:T(1024)}, u32[]{:S(2)}) copy-start(s32[1024]{0:T(1024)} %param.6) | copy-start | bytes 12292
  11.0 6.5 %collective-permute-start.6 = (bf16[240,128]{1,0:T(8,128)(2,1)S(1)}, bf16[240,128]{1,0:T(8,128)(2,1)S(1)}, u32[]{:S(2)}, u32[]{:S(2)}) collective-permute-start(bf16[240,128]{1,0:T(8,128)(2,1)S(1)} %get-tuple-element.42.refs_0_), channel_id=1, source_target_pairs={{0,6},{1,7},{2,4},{3,5},{4,2},{5,3},{6,0},{7,1},{8,14},{9,15},{10,... | collective-permute-start | bytes 184328 | tf_op jit(solution)/shard_map/ppermute | solution.py:559
  13.5 4.8 %collective-permute-start.7 = (bf16[240,128]{1,0:T(8,128)(2,1)S(1)}, bf16[240,128]{1,0:T(8,128)(2,1)S(1)}, u32[]{:S(2)}, u32[]{:S(2)}) collective-permute-start(bf16[240,128]{1,0:T(8,128)(2,1)S(1)} %get-tuple-element.42.refs_0_), channel_id=1, source_target_pairs={{0,2},{1,3},{2,0},{3,1},{4,6},{5,7},{6,4},{7,5},{8,10},{9,11},{10,... | collective-permute-start | bytes 184328 | tf_op jit(solution)/shard_map/ppermute | solution.py:559
  14.0 5.8 %collective-permute-start.8 = (bf16[240,128]{1,0:T(8,128)(2,1)S(1)}, bf16[240,128]{1,0:T(8,128)(2,1)S(1)}, u32[]{:S(2)}, u32[]{:S(2)}) collective-permute-start(bf16[240,128]{1,0:T(8,128)(2,1)S(1)} %get-tuple-element.42.refs_0_), channel_id=1, source_target_pairs={{0,4},{1,5},{2,6},{3,7},{4,0},{5,1},{6,2},{7,3},{8,12},{9,13},{10,... | collective-permute-start | bytes 184328 | tf_op jit(solution)/shard_map/ppermute | solution.py:559
  14.5 10.4 %collective-permute-start.3 = (bf16[3,193,128]{2,1,0:T(8,128)(2,1)S(1)}, bf16[3,193,128]{2,1,0:T(8,128)(2,1)S(1)}, u32[]{:S(2)}, u32[]{:S(2)}) collective-permute-start(bf16[3,193,128]{2,1,0:T(8,128)(2,1)S(1)} %get-tuple-element.39.refs_0_), channel_id=1, source_target_pairs={{0,6},{1,7},{2,4},{3,5},{4,2},{5,3},{6,0},{7,1},{8,14},{9,15},{10,... | collective-permute-start | bytes 444680 | tf_op jit(solution)/shard_map/ppermute | solution.py:559
  17.0 8.0 %collective-permute-start.4 = (bf16[3,193,128]{2,1,0:T(8,128)(2,1)S(1)}, bf16[3,193,128]{2,1,0:T(8,128)(2,1)S(1)}, u32[]{:S(2)}, u32[]{:S(2)}) collective-permute-start(bf16[3,193,128]{2,1,0:T(8,128)(2,1)S(1)} %get-tuple-element.39.refs_0_), channel_id=1, source_target_pairs={{0,2},{1,3},{2,0},{3,1},{4,6},{5,7},{6,4},{7,5},{8,10},{9,11},{10,... | collective-permute-start | bytes 444680 | tf_op jit(solution)/shard_map/ppermute | solution.py:559
  17.5 7.4 %collective-permute-start.5 = (bf16[3,193,128]{2,1,0:T(8,128)(2,1)S(1)}, bf16[3,193,128]{2,1,0:T(8,128)(2,1)S(1)}, u32[]{:S(2)}, u32[]{:S(2)}) collective-permute-start(bf16[3,193,128]{2,1,0:T(8,128)(2,1)S(1)} %get-tuple-element.39.refs_0_), channel_id=1, source_target_pairs={{0,4},{1,5},{2,6},{3,7},{4,0},{5,1},{6,2},{7,3},{8,12},{9,13},{10,... | collective-permute-start | bytes 444680 | tf_op jit(solution)/shard_map/ppermute | solution.py:559
  18.3 1.4 %collective-permute-start.9 = (bf16[240,128]{1,0:T(8,128)(2,1)S(1)}, bf16[240,128]{1,0:T(8,128)(2,1)S(1)}, u32[]{:S(2)}, u32[]{:S(2)}) collective-permute-start(bf16[240,128]{1,0:T(8,128)(2,1)S(1)} %get-tuple-element.42.refs_0_), channel_id=1, source_target_pairs={{0,1},{1,0},{2,3},{3,2},{4,5},{5,4},{6,7},{7,6},{8,9},{9,8},{10,11... | collective-permute-start | bytes 184328 | tf_op jit(solution)/shard_map/ppermute | solution.py:559
  19.8 1.2 %collective-permute-start.10 = (bf16[240,128]{1,0:T(8,128)(2,1)S(1)}, bf16[240,128]{1,0:T(8,128)(2,1)S(1)}, u32[]{:S(2)}, u32[]{:S(2)}) collective-permute-start(bf16[240,128]{1,0:T(8,128)(2,1)S(1)} %collective-permute-done.6.refs_1_), channel_id=1, source_target_pairs={{0,1},{1,0},{2,3},{3,2},{4,5},{5,4},{6,7},{7,6},{8,9},{9,8},{10,11... | collective-permute-start | bytes 184328 | tf_op jit(solution)/shard_map/ppermute | solution.py:559
  19.8 1.5 %collective-permute-start.11 = (bf16[240,128]{1,0:T(8,128)(2,1)S(1)}, bf16[240,128]{1,0:T(8,128)(2,1)S(1)}, u32[]{:S(2)}, u32[]{:S(2)}) collective-permute-start(bf16[240,128]{1,0:T(8,128)(2,1)S(1)} %collective-permute-done.7.refs_2_), channel_id=1, source_target_pairs={{0,1},{1,0},{2,3},{3,2},{4,5},{5,4},{6,7},{7,6},{8,9},{9,8},{10,11... | collective-permute-start | bytes 184328 | tf_op jit(solution)/shard_map/ppermute | solution.py:559
  21.0 1.2 %collective-permute-start.12 = (bf16[240,128]{1,0:T(8,128)(2,1)S(1)}, bf16[240,128]{1,0:T(8,128)(2,1)S(1)}, u32[]{:S(2)}, u32[]{:S(2)}) collective-permute-start(bf16[240,128]{1,0:T(8,128)(2,1)S(1)} %collective-permute-done.8.refs_3_), channel_id=1, source_target_pairs={{0,1},{1,0},{2,3},{3,2},{4,5},{5,4},{6,7},{7,6},{8,9},{9,8},{10,11... | collective-permute-start | bytes 184328 | tf_op jit(solution)/shard_map/ppermute | solution.py:559
  24.9 2.2 %copy-start = (bf16[1024,256]{1,0:T(8,128)(2,1)S(1)}, bf16[1024,256]{1,0:T(8,128)(2,1)}, u32[]{:S(2)}) copy-start(bf16[1024,256]{1,0:T(8,128)(2,1)} %cot.1) | copy-start | bytes 1572868
  24.9 2.2 %copy-start.2 = (bf16[1024,256]{1,0:T(8,128)(2,1)S(1)}, bf16[1024,256]{1,0:T(8,128)(2,1)}, u32[]{:S(2)}) copy-start(bf16[1024,256]{1,0:T(8,128)(2,1)} %tok.5) | copy-start | bytes 1572868
  25.0 2.1 %collective-permute-start.14 = (bf16[9,193,128]{2,1,0:T(8,128)(2,1)S(1)}, bf16[9,193,128]{2,1,0:T(8,128)(2,1)S(1)}, u32[]{:S(2)}, u32[]{:S(2)}) collective-permute-start(bf16[9,193,128]{2,1,0:T(8,128)(2,1)S(1)} %stack.37.refs_1_), channel_id=1, source_target_pairs={{0,1},{1,0},{2,3},{3,2},{4,5},{5,4},{6,7},{7,6},{8,9},{9,8},{10,11... | collective-permute-start | bytes 1334024 | tf_op jit(solution)/shard_map/ppermute | solution.py:559
  25.2 1.9 %collective-permute-start.13 = (bf16[3,193,128]{2,1,0:T(8,128)(2,1)S(1)}, bf16[3,193,128]{2,1,0:T(8,128)(2,1)S(1)}, u32[]{:S(2)}, u32[]{:S(2)}) collective-permute-start(bf16[3,193,128]{2,1,0:T(8,128)(2,1)S(1)} %get-tuple-element.39.refs_0_), channel_id=1, source_target_pairs={{0,1},{1,0},{2,3},{3,2},{4,5},{5,4},{6,7},{7,6},{8,9},{9,8},{10,11... | collective-permute-start | bytes 444680 | tf_op jit(solution)/shard_map/ppermute | solution.py:559
  33.4 5.0 %collective-permute-start.16 = (bf16[12,193,128]{2,1,0:T(8,128)(2,1)S(1)}, bf16[12,193,128]{2,1,0:T(8,128)(2,1)S(1)}, u32[]{:S(2)}, u32[]{:S(2)}) collective-permute-start(bf16[12,193,128]{2,1,0:T(8,128)(2,1)S(1)} %get-tuple-element.64), channel_id=1, source_target_pairs={{0,1},{1,0},{2,3},{3,2},{4,5},{5,4},{6,7},{7,6},{8,9},{9,8},{10,11... | collective-permute-start | bytes 1778696 | tf_op jit(solution)/shard_map/ppermute | solution.py:559
  36.9 1.6 %collective-permute-start.15 = (bf16[4,224,128]{2,1,0:T(8,128)(2,1)S(1)}, bf16[4,224,128]{2,1,0:T(8,128)(2,1)S(1)}, u32[]{:S(2)}, u32[]{:S(2)}) collective-permute-start(bf16[4,224,128]{2,1,0:T(8,128)(2,1)S(1)} %get-tuple-element.62), channel_id=1, source_target_pairs={{0,1},{1,0},{2,3},{3,2},{4,5},{5,4},{6,7},{7,6},{8,9},{9,8},{10,11... | collective-permute-start | bytes 688136 | tf_op jit(solution)/shard_map/ppermute | solution.py:559
  38.7 8.9 %collective-permute-start.17 = (bf16[4,193,128]{2,1,0:T(8,128)(2,1)S(1)}, bf16[4,193,128]{2,1,0:T(8,128)(2,1)S(1)}, u32[]{:S(2)}, u32[]{:S(2)}) collective-permute-start(bf16[4,193,128]{2,1,0:T(8,128)(2,1)S(1)} %get-tuple-element.66), channel_id=1, source_target_pairs={{0,6},{1,7},{2,4},{3,5},{4,2},{5,3},{6,0},{7,1},{8,14},{9,15},{10,... | collective-permute-start | bytes 592904 | tf_op jit(solution)/shard_map/ppermute | solution.py:559
  40.9 10.1 %collective-permute-start.18 = (bf16[4,193,128]{2,1,0:T(8,128)(2,1)S(1)}, bf16[4,193,128]{2,1,0:T(8,128)(2,1)S(1)}, u32[]{:S(2)}, u32[]{:S(2)}) collective-permute-start(bf16[4,193,128]{2,1,0:T(8,128)(2,1)S(1)} %get-tuple-element.67), channel_id=1, source_target_pairs={{0,2},{1,3},{2,0},{3,1},{4,6},{5,7},{6,4},{7,5},{8,10},{9,11},{10,... | collective-permute-start | bytes 592904 | tf_op jit(solution)/shard_map/ppermute | solution.py:559
  41.2 10.2 %collective-permute-start.19 = (bf16[4,193,128]{2,1,0:T(8,128)(2,1)S(1)}, bf16[4,193,128]{2,1,0:T(8,128)(2,1)S(1)}, u32[]{:S(2)}, u32[]{:S(2)}) collective-permute-start(bf16[4,193,128]{2,1,0:T(8,128)(2,1)S(1)} %get-tuple-element.68), channel_id=1, source_target_pairs={{0,4},{1,5},{2,6},{3,7},{4,0},{5,1},{6,2},{7,3},{8,12},{9,13},{10,... | collective-permute-start | bytes 592904 | tf_op jit(solution)/shard_map/ppermute | solution.py:559
  51.6 6.2 %collective-permute-start.20 = (bf16[193,128]{1,0:T(8,128)(2,1)S(1)}, bf16[193,128]{1,0:T(8,128)(2,1)S(1)}, u32[]{:S(2)}, u32[]{:S(2)}) collective-permute-start(bf16[193,128]{1,0:T(8,128)(2,1)S(1)} %get-tuple-element.70), channel_id=1, source_target_pairs={{0,8},{1,9},{2,10},{3,11},{4,12},{5,13},{6,14},{7,15},{8,16},{9,17... | collective-permute-start | bytes 148232 | tf_op jit(solution)/shard_map/ppermute | solution.py:559
  53.5 5.9 %collective-permute-start.21 = (bf16[193,128]{1,0:T(8,128)(2,1)S(1)}, bf16[193,128]{1,0:T(8,128)(2,1)S(1)}, u32[]{:S(2)}, u32[]{:S(2)}) collective-permute-start(bf16[193,128]{1,0:T(8,128)(2,1)S(1)} %get-tuple-element.71), channel_id=1, source_target_pairs={{0,16},{1,17},{2,18},{3,19},{4,20},{5,21},{6,22},{7,23},{8,24},{9,... | collective-permute-start | bytes 148232 | tf_op jit(solution)/shard_map/ppermute | solution.py:559
  55.0 4.9 %collective-permute-start.22 = (bf16[193,128]{1,0:T(8,128)(2,1)S(1)}, bf16[193,128]{1,0:T(8,128)(2,1)S(1)}, u32[]{:S(2)}, u32[]{:S(2)}) collective-permute-start(bf16[193,128]{1,0:T(8,128)(2,1)S(1)} %get-tuple-element.72), channel_id=1, source_target_pairs={{0,24},{1,25},{2,26},{3,27},{4,28},{5,29},{6,30},{7,31},{8,0},{9,1... | collective-permute-start | bytes 148232 | tf_op jit(solution)/shard_map/ppermute | solution.py:559

commit v14 on v13

--- a/solution.py
+++ b/solution.py
@@ -103,11 +103,14 @@
         flat[pl.ds(start + j, rows, stride=per_row), :] = matrix[:, j * LANES : (j + 1) * LANES]
 
 
-def prepare_kernel(tok, params, seg, normed_out, normed_turned, own, allowed):
+def copy_kernel(params, own):
+    own[...] = params[...]
+
+
+def prepare_kernel(tok, seg, normed_out, normed_turned, allowed):
     normed, _ = normalize(tok[...].astype(F32))
     normed_out[...] = normed
     normed_turned[...] = normed.astype(BF16).T
-    own[...] = params[...]
     causal = lax.broadcasted_iota(jnp.int32, (SEQ, SEQ), 0) <= lax.broadcasted_iota(
         jnp.int32, (SEQ, SEQ), 1
     )
@@ -427,14 +430,13 @@
     return results if len(outs) > 1 else results[0]
 
 
-def prepare(tokens, params, segment_ids):
+def prepare(tokens, segment_ids):
     rows = tokens.shape[0]
     return call(
-        prepare_kernel, "prepare", None, [tokens, params, segment_ids.reshape(-1, SEQ)],
+        prepare_kernel, "prepare", None, [tokens, segment_ids.reshape(-1, SEQ)],
         [
             like(rows, D),
             like(D, rows, kind=BF16),
-            like(*params.shape, kind=BF16),
             like(rows, SEQ),
         ],
         us=2,
@@ -507,7 +509,7 @@
 
 def local_any(n, tokens, params, segment_ids, cotangent):
     total = n * params.shape[0]
-    normed, normed_turned, _, allowed = prepare(tokens, params, segment_ids)
+    normed, normed_turned, allowed = prepare(tokens, segment_ids)
     gathered = lax.all_gather(params, "fsdp", axis=0).reshape(total, LANES)
     shares = gathered[:ROW_TOTAL].reshape(Z, 2 * PLANE, SHARE, LANES)
     order = [p * 2 + c for c in range(2) for p in range(PLANE)]
@@ -570,12 +572,14 @@
         [(plane ^ dp) * 2 + (core ^ dc) for dc in range(2) for dp in (0, *STEPS)]
     )
 
-    normed, normed_turned, own, allowed = prepare(tokens, params, segment_ids)
+    own = call(copy_kernel, "own", None, [params], [like(*params.shape, kind=BF16)])
     first, rest = call(
         sort_kernel, "sort_shares", where, [own] + [move(params, d, 0, 0) for d in range(1, Z)],
         [like(SIDE + SMALL_ROWS, LANES, kind=BF16), like(Z - 1, SHARE, LANES, kind=BF16)],
         [pltpu.VMEM((Z, SHARE, LANES), BF16), pltpu.VMEM((SIDE + SMALL_ROWS, LANES), F32)],
     )
+    first, late_tokens, late_segments = lax.optimization_barrier((first, tokens, segment_ids))
+    normed, normed_turned, allowed = prepare(late_tokens, late_segments)
     firsts = [first] + [move(first, 0, d, 0) for d in STEPS]
     rests = [move(rest, 0, d, 0) for d in STEPS]
     firsts = firsts + [move(item, 0, 0, 1) for item in firsts]

time: 60.8 us -> 62.3 us (1.025)
  waiting for transfers between devices: 15.5 us -> 19.6 us
  local copies, waits for them, and re-layouts: 2.63 us -> 0.93 us
  starting transfers between devices: 24.1 us -> 23.3 us
    ppermute x23, waiting for transfers between devices: 15.5 us -> 19.6 us  [move(): return lax.ppermute(values, 'fsdp', pairs)]
    unnamed x10 -> x8, local copies, waits for them, and re-layouts: 2.54 us -> 0.85 us
    ppermute x23, starting transfers between devices: 24.1 us -> 23.3 us  [move(): return lax.ppermute(values, 'fsdp', pairs)]
    pallas_call x11 -> x12, Pallas kernels: 17.6 us -> 17.6 us  [call(): pl.pallas_call(kernel, in_specs=[SMEM_SPEC] * with_ids + [VMEM_SPEC] * le...]
  transfers between devices with their start and end apart: 23 -> 23, of which waited for: 12 -> 13; matrix products, arithmetic and copies ran while one was open for 0% -> 0% of each run, Pallas kernels for 17% -> 16%
where the time goes in v14:
time: 62.3 us; the launch traced here: 62.1 us
  starting transfers between devices  23.3 us (37%)
  waiting for transfers between devices  19.6 us (31%)
  Pallas kernels  17.6 us (28%)
  local copies, waits for them, and re-layouts  0.93 us (1%)
  between operations  0.71 us (1%)
    ppermute x23, starting transfers between devices, move(): return lax.ppermute(values, 'fsdp', pairs)  23.3 us
    ppermute x23, waiting for transfers between devices, move(): return lax.ppermute(values, 'fsdp', pairs)  19.6 us
    pallas_call x12, Pallas kernels, call(): pl.pallas_call(kernel, in_specs=[SMEM_SPEC] * with_ids + [VMEM_SPEC] * le...  17.6 us
  transfers between devices with their start and end apart: 23, of which 13 were waited for; matrix products, arithmetic and copies ran while one was open for 0% of the time, Pallas kernels for 16%

profile of v14, /device:TPU:0, one launch (start us, length us, event | category | flops | bytes accessed | tf_op | source)
XLA Modules:
  0.0 62.1 jit_solution(3846839833559601149)
XLA Ops:
  0.6 3.1 %collective-permute-start = (bf16[193,128]{1,0:T(8,128)(2,1)}, bf16[193,128]{1,0:T(8,128)(2,1)S(1)}, u32[]{:S(2)}, u32[]{:S(2)}) collective-permute-start(bf16[193,128]{1,0:T(8,128)(2,1)} %params.1), channel_id=1, source_target_pairs={{0,8},{1,9},{2,10},{3,11},{4,12},{5,13},{6,14},{7,15},{8,16},{9,17... | collective-permute-start | bytes 148232 | tf_op jit(solution)/shard_map/ppermute | solution.py:561
  3.7 2.6 %collective-permute-start.1 = (bf16[193,128]{1,0:T(8,128)(2,1)}, bf16[193,128]{1,0:T(8,128)(2,1)S(1)}, u32[]{:S(2)}, u32[]{:S(2)}) collective-permute-start(bf16[193,128]{1,0:T(8,128)(2,1)} %params.1), channel_id=1, source_target_pairs={{0,16},{1,17},{2,18},{3,19},{4,20},{5,21},{6,22},{7,23},{8,24},{9,... | collective-permute-start | bytes 148232 | tf_op jit(solution)/shard_map/ppermute | solution.py:561
  6.3 1.3 %collective-permute-start.2 = (bf16[193,128]{1,0:T(8,128)(2,1)}, bf16[193,128]{1,0:T(8,128)(2,1)S(1)}, u32[]{:S(2)}, u32[]{:S(2)}) collective-permute-start(bf16[193,128]{1,0:T(8,128)(2,1)} %params.1), channel_id=1, source_target_pairs={{0,24},{1,25},{2,26},{3,27},{4,28},{5,29},{6,30},{7,31},{8,0},{9,1... | collective-permute-start | bytes 148232 | tf_op jit(solution)/shard_map/ppermute | solution.py:561
  7.6 0.8 %copy-done.2 = bf16[193,128]{1,0:T(8,128)(2,1)S(1)} copy-done((bf16[193,128]{1,0:T(8,128)(2,1)S(1)}, bf16[193,128]{1,0:T(8,128)(2,1)}, u32[]{:S(2)}) %copy-start.2) | copy-done | bytes 49432
  8.5 1.7 %collective-permute-done.1.refs_2_ = bf16[193,128]{1,0:T(8,128)(2,1)S(1)} collective-permute-done((bf16[193,128]{1,0:T(8,128)(2,1)}, bf16[193,128]{1,0:T(8,128)(2,1)S(1)}, u32[]{:S(2)}, u32[]{:S(2)}) %collective-permute-start.1) | collective-permute-done | bytes 49440 | tf_op jit(solution)/shard_map/ppermute | solution.py:561
  10.2 0.5 collective-permute-done.2.refs_3_
  10.7 2.6 %collective-permute-start.6 = (bf16[240,128]{1,0:T(8,128)(2,1)S(1)}, bf16[240,128]{1,0:T(8,128)(2,1)S(1)}, u32[]{:S(2)}, u32[]{:S(2)}) collective-permute-start(bf16[240,128]{1,0:T(8,128)(2,1)S(1)} %get-tuple-element.46.refs_0_), channel_id=1, source_target_pairs={{0,6},{1,7},{2,4},{3,5},{4,2},{5,3},{6,0},{7,1},{8,14},{9,15},{10,... | collective-permute-start | bytes 184328 | tf_op jit(solution)/shard_map/ppermute | solution.py:561
  13.4 0.5 collective-permute-start.7
  13.9 0.4 collective-permute-start.8
  14.3 0.0 collective-permute-start.9
  14.3 1.6 %collective-permute-done.6.refs_1_ = bf16[240,128]{1,0:T(8,128)(2,1)S(1)} collective-permute-done((bf16[240,128]{1,0:T(8,128)(2,1)S(1)}, bf16[240,128]{1,0:T(8,128)(2,1)S(1)}, u32[]{:S(2)}, u32[]{:S(2)}) %collective-permute-start.6) | collective-permute-done | bytes 61472 | tf_op jit(solution)/shard_map/ppermute | solution.py:561
  15.9 0.0 collective-permute-start.10
  15.9 0.1 stack.36.ids
  16.0 2.6 %collective-permute-start.3 = (bf16[3,193,128]{2,1,0:T(8,128)(2,1)S(1)}, bf16[3,193,128]{2,1,0:T(8,128)(2,1)S(1)}, u32[]{:S(2)}, u32[]{:S(2)}) collective-permute-start(bf16[3,193,128]{2,1,0:T(8,128)(2,1)S(1)} %get-tuple-element.40.refs_0_), channel_id=1, source_target_pairs={{0,6},{1,7},{2,4},{3,5},{4,2},{5,3},{6,0},{7,1},{8,14},{9,15},{10,... | collective-permute-start | bytes 444680 | tf_op jit(solution)/shard_map/ppermute | solution.py:561
  18.6 0.5 collective-permute-start.4
  19.1 0.4 collective-permute-start.5
  19.5 0.5 collective-permute-start.12
  20.0 0.7 %prepare.1 = (f32[1024,256]{1,0:T(8,128)S(1)}, bf16[256,1024]{1,0:T(8,128)(2,1)S(1)}, f32[1024,128]{1,0:T(8,128)S(1)}) custom-call(bf16[1024,256]{1,0:T(8,128)(2,1)S(1)} %copy-done.1, s32[8,128]{1,0:T(8,128)S(1)} %bitcast.10), custom_call_target="tpu_custom_call" | custom-call | flops 2000000000 | bytes 1048576 | tf_op jit(solution)/shard_map/prepare/pallas_call | solution.py:420
  20.7 0.0 collective-permute-done.11.refs_6_
  20.8 0.2 collective-permute-done.12.refs_7_
  20.9 2.6 %attend.1 = (bf16[1024,768]{1,0:T(8,128)(2,1)S(1)}, bf16[1024,512]{1,0:T(8,128)(2,1)S(1)}, bf16[1024,256]{1,0:T(8,128)(2,1)S(1)}, bf16[256,768]{1,0:T(8,128)(2,1...) custom-call(s32[8]{0:T(128)S(1)} %stack.36.ids, f32[1024,128]{1,0:T(8,128)S(1)} %get-tuple-element.44.allowed, ...), custom_call_target="tpu_custom_call" | custom-call | flops 200000000 | bytes 1048576 | tf_op jit(solution)/shard_map/attend/pallas_call | solution.py:420
  23.6 0.1 collective-permute-done.3.refs_0_
  23.7 3.1 %collective-permute-done.4.refs_1_ = bf16[3,193,128]{2,1,0:T(8,128)(2,1)S(1)} collective-permute-done((bf16[3,193,128]{2,1,0:T(8,128)(2,1)S(1)}, bf16[3,193,128]{2,1,0:T(8,128)(2,1)S(1)}, u32[]{:S(2)}, u32[]{:S(2)}) %collective-permute-start.4) | collective-permute-done | bytes 148256 | tf_op jit(solution)/shard_map/ppermute | solution.py:561
  26.9 0.1 collective-permute-start.14
  27.0 0.5 collective-permute-start.13
  27.5 1.5 %collective-permute-done.13.refs_2_ = bf16[3,193,128]{2,1,0:T(8,128)(2,1)S(1)} collective-permute-done((bf16[3,193,128]{2,1,0:T(8,128)(2,1)S(1)}, bf16[3,193,128]{2,1,0:T(8,128)(2,1)S(1)}, u32[]{:S(2)}, u32[]{:S(2)}) %collective-permute-start.13) | collective-permute-done | bytes 148256 | tf_op jit(solution)/shard_map/ppermute | solution.py:561
  29.0 6.3 %feed.1 = (f32[1024,256]{1,0:T(8,128)S(1)}, bf16[1024,1024]{1,0:T(8,128)(2,1)S(1)}, f32[1024,256]{1,0:T(8,128)S(1)}, bf16[1024,256]{1,0:T(8,128)(2,1)S(1)}, bf16...) custom-call(s32[8]{0:T(128)S(1)} %stack.36.ids, ...), custom_call_target="tpu_custom_call" | custom-call | flops 8000000000 | bytes 1048576 | tf_op jit(solution)/shard_map/feed/pallas_call | solution.py:420
  35.3 0.2 collective-permute-start.16
  35.5 3.3 %attend_back.1 = (bf16[1024,768]{1,0:T(8,128)(2,1)S(1)}, f32[4,224,128]{2,1,0:T(8,128)S(1)}, bf16[4,224,128]{2,1,0:T(8,128)(2,1)S(1)}) custom-call(s32[8]{0:T(128)S(1)} %stack.36.ids, bf16[1024,768]{1,0:T(8,128)(2,1)S(1)} %get-tuple-element.57.project, bf16[1024,512]{1,0:T(8,128)(2,1)S(1)} %get-tuple-element.58.weights, ...), custom_call_target="tpu_custom_call" | custom-call | flops 4000000000 | bytes 1048576 | tf_op jit(solution)/shard_map/attend_back/pallas_call | solution.py:420
  38.8 0.4 collective-permute-start.15
  39.2 1.1 %collective-permute-done.15.first_in = bf16[4,224,128]{2,1,0:T(8,128)(2,1)S(1)} collective-permute-done((bf16[4,224,128]{2,1,0:T(8,128)(2,1)S(1)}, bf16[4,224,128]{2,1,0:T(8,128)(2,1)S(1)}, u32[]{:S(2)}, u32[]{:S(2)}) %collective-permute-start.15) | collective-permute-done | bytes 229408 | tf_op jit(solution)/shard_map/ppermute | solution.py:561
  40.3 0.2 add_core.1
  40.5 2.4 %collective-permute-start.17 = (bf16[4,193,128]{2,1,0:T(8,128)(2,1)S(1)}, bf16[4,193,128]{2,1,0:T(8,128)(2,1)S(1)}, u32[]{:S(2)}, u32[]{:S(2)}) collective-permute-start(bf16[4,193,128]{2,1,0:T(8,128)(2,1)S(1)} %get-tuple-element.70), channel_id=1, source_target_pairs={{0,6},{1,7},{2,4},{3,5},{4,2},{5,3},{6,0},{7,1},{8,14},{9,15},{10,... | collective-permute-start | bytes 592904 | tf_op jit(solution)/shard_map/ppermute | solution.py:561
  43.0 0.5 collective-permute-start.18
  43.5 0.6 collective-permute-start.19
  44.1 2.0 %input_grad.1 = f32[1024,256]{1,0:T(8,128)} custom-call(bf16[1024,256]{1,0:T(8,128)(2,1)S(1)} %copy-done.1, bf16[1024,768]{1,0:T(8,128)(2,1)S(1)} %get-tuple-element.63.grad_project, f32[1024,256]{1,0:T(8,128)S(1)} %get-tuple-element.64.grad_middle, bf16[256,768]{1,0:T(8,128)(2,1)S(1)} %get-tuple-element.61.w_qkv, f32[32,128]{1,0:T(8,128)S(1)} %get-tuple-element.49.small), custom_call_target="tpu_custom_call" | custom-call | flops 2000000000 | bytes 1048576 | tf_op jit(solution)/shard_map/input_grad/pallas_call | solution.py:420
  46.1 3.3 %collective-permute-done.17.refs_0_ = bf16[4,193,128]{2,1,0:T(8,128)(2,1)S(1)} collective-permute-done((bf16[4,193,128]{2,1,0:T(8,128)(2,1)S(1)}, bf16[4,193,128]{2,1,0:T(8,128)(2,1)S(1)}, u32[]{:S(2)}, u32[]{:S(2)}) %collective-permute-start.17) | collective-permute-done | bytes 197664 | tf_op jit(solution)/shard_map/ppermute | solution.py:561
  49.5 3.8 %collective-permute-done.18.refs_1_ = bf16[4,193,128]{2,1,0:T(8,128)(2,1)S(1)} collective-permute-done((bf16[4,193,128]{2,1,0:T(8,128)(2,1)S(1)}, bf16[4,193,128]{2,1,0:T(8,128)(2,1)S(1)}, u32[]{:S(2)}, u32[]{:S(2)}) %collective-permute-start.18) | collective-permute-done | bytes 197664 | tf_op jit(solution)/shard_map/ppermute | solution.py:561
  53.2 0.0 collective-permute-done.19.refs_2_
  53.3 0.2 add_plane.1
  53.4 1.0 %collective-permute-start.20 = (bf16[193,128]{1,0:T(8,128)(2,1)S(1)}, bf16[193,128]{1,0:T(8,128)(2,1)S(1)}, u32[]{:S(2)}, u32[]{:S(2)}) collective-permute-start(bf16[193,128]{1,0:T(8,128)(2,1)S(1)} %get-tuple-element.74), channel_id=1, source_target_pairs={{0,8},{1,9},{2,10},{3,11},{4,12},{5,13},{6,14},{7,15},{8,16},{9,17... | collective-permute-start | bytes 148232 | tf_op jit(solution)/shard_map/ppermute | solution.py:561
  54.4 2.6 %collective-permute-start.21 = (bf16[193,128]{1,0:T(8,128)(2,1)S(1)}, bf16[193,128]{1,0:T(8,128)(2,1)S(1)}, u32[]{:S(2)}, u32[]{:S(2)}) collective-permute-start(bf16[193,128]{1,0:T(8,128)(2,1)S(1)} %get-tuple-element.75), channel_id=1, source_target_pairs={{0,16},{1,17},{2,18},{3,19},{4,20},{5,21},{6,22},{7,23},{8,24},{9,... | collective-permute-start | bytes 148232 | tf_op jit(solution)/shard_map/ppermute | solution.py:561
  57.0 0.4 collective-permute-start.22
  57.3 1.5 %result.1 = bf16[1024,256]{1,0:T(8,128)(2,1)} custom-call(f32[1024,256]{1,0:T(8,128)S(1)} %get-tuple-element.54.middle, bf16[1024,1024]{1,0:T(8,128)(2,1)S(1)} %get-tuple-element.55.activated, bf16[1024,256]{1,0:T(8,128)(2,1)S(1)} %get-tuple-element.56.w_down, f32[32,128]{1,0:T(8,128)S(1)} %get-tuple-element.49.small), custom_call_target="tpu_custom_call" | custom-call | flops 2000000000 | bytes 1048576 | tf_op jit(solution)/shard_map/result/pallas_call | solution.py:420
  58.9 1.2 %collective-permute-done.20.refs_0_ = bf16[193,128]{1,0:T(8,128)(2,1)S(1)} collective-permute-done((bf16[193,128]{1,0:T(8,128)(2,1)S(1)}, bf16[193,128]{1,0:T(8,128)(2,1)S(1)}, u32[]{:S(2)}, u32[]{:S(2)}) %collective-permute-start.20) | collective-permute-done | bytes 49440 | tf_op jit(solution)/shard_map/ppermute | solution.py:561
  60.1 1.2 %collective-permute-done.21.refs_1_ = bf16[193,128]{1,0:T(8,128)(2,1)S(1)} collective-permute-done((bf16[193,128]{1,0:T(8,128)(2,1)S(1)}, bf16[193,128]{1,0:T(8,128)(2,1)S(1)}, u32[]{:S(2)}, u32[]{:S(2)}) %collective-permute-start.21) | collective-permute-done | bytes 49440 | tf_op jit(solution)/shard_map/ppermute | solution.py:561
  61.3 0.1 collective-permute-done.22.refs_2_
  61.4 0.7 %add_column.1 = f32[193,128]{1,0:T(8,128)} custom-call(f32[193,128]{1,0:T(8,128)S(1)} %get-tuple-element.73.kept, bf16[193,128]{1,0:T(8,128)(2,1)S(1)} %collective-permute-done.20.refs_0_, bf16[193,128]{1,0:T(8,128)(2,1)S(1)} %collective-permute-done.21.refs_1_, bf16[193,128]{1,0:T(8,128)(2,1)S(1)} %collective-permute-done.22.refs_2_), custom_call_target="tpu_custom_call" | custom-call | flops 1000000000 | bytes 1048576 | tf_op jit(solution)/shard_map/add_column/pallas_call | solution.py:420
  (19 shorter events, 0.1 us)
Async XLA Ops:
  0.6 7.9 %collective-permute-start = (bf16[193,128]{1,0:T(8,128)(2,1)}, bf16[193,128]{1,0:T(8,128)(2,1)S(1)}, u32[]{:S(2)}, u32[]{:S(2)}) collective-permute-start(bf16[193,128]{1,0:T(8,128)(2,1)} %params.1), channel_id=1, source_target_pairs={{0,8},{1,9},{2,10},{3,11},{4,12},{5,13},{6,14},{7,15},{8,16},{9,17... | collective-permute-start | bytes 148232 | tf_op jit(solution)/shard_map/ppermute | solution.py:561
  3.7 6.5 %collective-permute-start.1 = (bf16[193,128]{1,0:T(8,128)(2,1)}, bf16[193,128]{1,0:T(8,128)(2,1)S(1)}, u32[]{:S(2)}, u32[]{:S(2)}) collective-permute-start(bf16[193,128]{1,0:T(8,128)(2,1)} %params.1), channel_id=1, source_target_pairs={{0,16},{1,17},{2,18},{3,19},{4,20},{5,21},{6,22},{7,23},{8,24},{9,... | collective-permute-start | bytes 148232 | tf_op jit(solution)/shard_map/ppermute | solution.py:561
  6.3 4.4 %collective-permute-start.2 = (bf16[193,128]{1,0:T(8,128)(2,1)}, bf16[193,128]{1,0:T(8,128)(2,1)S(1)}, u32[]{:S(2)}, u32[]{:S(2)}) collective-permute-start(bf16[193,128]{1,0:T(8,128)(2,1)} %params.1), channel_id=1, source_target_pairs={{0,24},{1,25},{2,26},{3,27},{4,28},{5,29},{6,30},{7,31},{8,0},{9,1... | collective-permute-start | bytes 148232 | tf_op jit(solution)/shard_map/ppermute | solution.py:561
  7.6 0.8 %copy-start.2 = (bf16[193,128]{1,0:T(8,128)(2,1)S(1)}, bf16[193,128]{1,0:T(8,128)(2,1)}, u32[]{:S(2)}) copy-start(bf16[193,128]{1,0:T(8,128)(2,1)} %params.1) | copy-start | bytes 148228
  10.7 9.3 %copy-start.1 = (bf16[1024,256]{1,0:T(8,128)(2,1)S(1)}, bf16[1024,256]{1,0:T(8,128)(2,1)}, u32[]{:S(2)}) copy-start(bf16[1024,256]{1,0:T(8,128)(2,1)} %tok.4) | copy-start | bytes 1572868
  10.7 9.3 %copy-start.3 = (s32[1024]{0:T(1024)S(1)}, s32[1024]{0:T(1024)}, u32[]{:S(2)}) copy-start(s32[1024]{0:T(1024)} %param.6) | copy-start | bytes 12292
  10.7 5.2 %collective-permute-start.6 = (bf16[240,128]{1,0:T(8,128)(2,1)S(1)}, bf16[240,128]{1,0:T(8,128)(2,1)S(1)}, u32[]{:S(2)}, u32[]{:S(2)}) collective-permute-start(bf16[240,128]{1,0:T(8,128)(2,1)S(1)} %get-tuple-element.46.refs_0_), channel_id=1, source_target_pairs={{0,6},{1,7},{2,4},{3,5},{4,2},{5,3},{6,0},{7,1},{8,14},{9,15},{10,... | collective-permute-start | bytes 184328 | tf_op jit(solution)/shard_map/ppermute | solution.py:561
  13.4 5.2 %collective-permute-start.7 = (bf16[240,128]{1,0:T(8,128)(2,1)S(1)}, bf16[240,128]{1,0:T(8,128)(2,1)S(1)}, u32[]{:S(2)}, u32[]{:S(2)}) collective-permute-start(bf16[240,128]{1,0:T(8,128)(2,1)S(1)} %get-tuple-element.46.refs_0_), channel_id=1, source_target_pairs={{0,2},{1,3},{2,0},{3,1},{4,6},{5,7},{6,4},{7,5},{8,10},{9,11},{10,... | collective-permute-start | bytes 184328 | tf_op jit(solution)/shard_map/ppermute | solution.py:561
  13.9 5.2 %collective-permute-start.8 = (bf16[240,128]{1,0:T(8,128)(2,1)S(1)}, bf16[240,128]{1,0:T(8,128)(2,1)S(1)}, u32[]{:S(2)}, u32[]{:S(2)}) collective-permute-start(bf16[240,128]{1,0:T(8,128)(2,1)S(1)} %get-tuple-element.46.refs_0_), channel_id=1, source_target_pairs={{0,4},{1,5},{2,6},{3,7},{4,0},{5,1},{6,2},{7,3},{8,12},{9,13},{10,... | collective-permute-start | bytes 184328 | tf_op jit(solution)/shard_map/ppermute | solution.py:561
  14.3 5.2 %collective-permute-start.9 = (bf16[240,128]{1,0:T(8,128)(2,1)S(1)}, bf16[240,128]{1,0:T(8,128)(2,1)S(1)}, u32[]{:S(2)}, u32[]{:S(2)}) collective-permute-start(bf16[240,128]{1,0:T(8,128)(2,1)S(1)} %get-tuple-element.46.refs_0_), channel_id=1, source_target_pairs={{0,1},{1,0},{2,3},{3,2},{4,5},{5,4},{6,7},{7,6},{8,9},{9,8},{10,11... | collective-permute-start | bytes 184328 | tf_op jit(solution)/shard_map/ppermute | solution.py:561
  15.9 3.6 %collective-permute-start.10 = (bf16[240,128]{1,0:T(8,128)(2,1)S(1)}, bf16[240,128]{1,0:T(8,128)(2,1)S(1)}, u32[]{:S(2)}, u32[]{:S(2)}) collective-permute-start(bf16[240,128]{1,0:T(8,128)(2,1)S(1)} %collective-permute-done.6.refs_1_), channel_id=1, source_target_pairs={{0,1},{1,0},{2,3},{3,2},{4,5},{5,4},{6,7},{7,6},{8,9},{9,8},{10,11... | collective-permute-start | bytes 184328 | tf_op jit(solution)/shard_map/ppermute | solution.py:561
  16.0 7.7 %collective-permute-start.3 = (bf16[3,193,128]{2,1,0:T(8,128)(2,1)S(1)}, bf16[3,193,128]{2,1,0:T(8,128)(2,1)S(1)}, u32[]{:S(2)}, u32[]{:S(2)}) collective-permute-start(bf16[3,193,128]{2,1,0:T(8,128)(2,1)S(1)} %get-tuple-element.40.refs_0_), channel_id=1, source_target_pairs={{0,6},{1,7},{2,4},{3,5},{4,2},{5,3},{6,0},{7,1},{8,14},{9,15},{10,... | collective-permute-start | bytes 444680 | tf_op jit(solution)/shard_map/ppermute | solution.py:561
  18.6 8.2 %collective-permute-start.4 = (bf16[3,193,128]{2,1,0:T(8,128)(2,1)S(1)}, bf16[3,193,128]{2,1,0:T(8,128)(2,1)S(1)}, u32[]{:S(2)}, u32[]{:S(2)}) collective-permute-start(bf16[3,193,128]{2,1,0:T(8,128)(2,1)S(1)} %get-tuple-element.40.refs_0_), channel_id=1, source_target_pairs={{0,2},{1,3},{2,0},{3,1},{4,6},{5,7},{6,4},{7,5},{8,10},{9,11},{10,... | collective-permute-start | bytes 444680 | tf_op jit(solution)/shard_map/ppermute | solution.py:561
  19.1 7.7 %collective-permute-start.5 = (bf16[3,193,128]{2,1,0:T(8,128)(2,1)S(1)}, bf16[3,193,128]{2,1,0:T(8,128)(2,1)S(1)}, u32[]{:S(2)}, u32[]{:S(2)}) collective-permute-start(bf16[3,193,128]{2,1,0:T(8,128)(2,1)S(1)} %get-tuple-element.40.refs_0_), channel_id=1, source_target_pairs={{0,4},{1,5},{2,6},{3,7},{4,0},{5,1},{6,2},{7,3},{8,12},{9,13},{10,... | collective-permute-start | bytes 444680 | tf_op jit(solution)/shard_map/ppermute | solution.py:561
  19.5 1.2 %collective-permute-start.11 = (bf16[240,128]{1,0:T(8,128)(2,1)S(1)}, bf16[240,128]{1,0:T(8,128)(2,1)S(1)}, u32[]{:S(2)}, u32[]{:S(2)}) collective-permute-start(bf16[240,128]{1,0:T(8,128)(2,1)S(1)} %collective-permute-done.7.refs_2_), channel_id=1, source_target_pairs={{0,1},{1,0},{2,3},{3,2},{4,5},{5,4},{6,7},{7,6},{8,9},{9,8},{10,11... | collective-permute-start | bytes 184328 | tf_op jit(solution)/shard_map/ppermute | solution.py:561
  19.5 1.4 %collective-permute-start.12 = (bf16[240,128]{1,0:T(8,128)(2,1)S(1)}, bf16[240,128]{1,0:T(8,128)(2,1)S(1)}, u32[]{:S(2)}, u32[]{:S(2)}) collective-permute-start(bf16[240,128]{1,0:T(8,128)(2,1)S(1)} %collective-permute-done.8.refs_3_), channel_id=1, source_target_pairs={{0,1},{1,0},{2,3},{3,2},{4,5},{5,4},{6,7},{7,6},{8,9},{9,8},{10,11... | collective-permute-start | bytes 184328 | tf_op jit(solution)/shard_map/ppermute | solution.py:561
  26.8 2.2 %copy-start = (bf16[1024,256]{1,0:T(8,128)(2,1)S(1)}, bf16[1024,256]{1,0:T(8,128)(2,1)}, u32[]{:S(2)}) copy-start(bf16[1024,256]{1,0:T(8,128)(2,1)} %cot.1) | copy-start | bytes 1572868
  26.9 2.1 %collective-permute-start.14 = (bf16[9,193,128]{2,1,0:T(8,128)(2,1)S(1)}, bf16[9,193,128]{2,1,0:T(8,128)(2,1)S(1)}, u32[]{:S(2)}, u32[]{:S(2)}) collective-permute-start(bf16[9,193,128]{2,1,0:T(8,128)(2,1)S(1)} %stack.37.refs_1_), channel_id=1, source_target_pairs={{0,1},{1,0},{2,3},{3,2},{4,5},{5,4},{6,7},{7,6},{8,9},{9,8},{10,11... | collective-permute-start | bytes 1334024 | tf_op jit(solution)/shard_map/ppermute | solution.py:561
  27.0 2.0 %collective-permute-start.13 = (bf16[3,193,128]{2,1,0:T(8,128)(2,1)S(1)}, bf16[3,193,128]{2,1,0:T(8,128)(2,1)S(1)}, u32[]{:S(2)}, u32[]{:S(2)}) collective-permute-start(bf16[3,193,128]{2,1,0:T(8,128)(2,1)S(1)} %get-tuple-element.40.refs_0_), channel_id=1, source_target_pairs={{0,1},{1,0},{2,3},{3,2},{4,5},{5,4},{6,7},{7,6},{8,9},{9,8},{10,11... | collective-permute-start | bytes 444680 | tf_op jit(solution)/shard_map/ppermute | solution.py:561
  35.3 5.0 %collective-permute-start.16 = (bf16[12,193,128]{2,1,0:T(8,128)(2,1)S(1)}, bf16[12,193,128]{2,1,0:T(8,128)(2,1)S(1)}, u32[]{:S(2)}, u32[]{:S(2)}) collective-permute-start(bf16[12,193,128]{2,1,0:T(8,128)(2,1)S(1)} %get-tuple-element.68), channel_id=1, source_target_pairs={{0,1},{1,0},{2,3},{3,2},{4,5},{5,4},{6,7},{7,6},{8,9},{9,8},{10,11... | collective-permute-start | bytes 1778696 | tf_op jit(solution)/shard_map/ppermute | solution.py:561
  38.8 1.6 %collective-permute-start.15 = (bf16[4,224,128]{2,1,0:T(8,128)(2,1)S(1)}, bf16[4,224,128]{2,1,0:T(8,128)(2,1)S(1)}, u32[]{:S(2)}, u32[]{:S(2)}) collective-permute-start(bf16[4,224,128]{2,1,0:T(8,128)(2,1)S(1)} %get-tuple-element.66), channel_id=1, source_target_pairs={{0,1},{1,0},{2,3},{3,2},{4,5},{5,4},{6,7},{7,6},{8,9},{9,8},{10,11... | collective-permute-start | bytes 688136 | tf_op jit(solution)/shard_map/ppermute | solution.py:561
  40.5 8.9 %collective-permute-start.17 = (bf16[4,193,128]{2,1,0:T(8,128)(2,1)S(1)}, bf16[4,193,128]{2,1,0:T(8,128)(2,1)S(1)}, u32[]{:S(2)}, u32[]{:S(2)}) collective-permute-start(bf16[4,193,128]{2,1,0:T(8,128)(2,1)S(1)} %get-tuple-element.70), channel_id=1, source_target_pairs={{0,6},{1,7},{2,4},{3,5},{4,2},{5,3},{6,0},{7,1},{8,14},{9,15},{10,... | collective-permute-start | bytes 592904 | tf_op jit(solution)/shard_map/ppermute | solution.py:561
  43.0 10.3 %collective-permute-start.18 = (bf16[4,193,128]{2,1,0:T(8,128)(2,1)S(1)}, bf16[4,193,128]{2,1,0:T(8,128)(2,1)S(1)}, u32[]{:S(2)}, u32[]{:S(2)}) collective-permute-start(bf16[4,193,128]{2,1,0:T(8,128)(2,1)S(1)} %get-tuple-element.71), channel_id=1, source_target_pairs={{0,2},{1,3},{2,0},{3,1},{4,6},{5,7},{6,4},{7,5},{8,10},{9,11},{10,... | collective-permute-start | bytes 592904 | tf_op jit(solution)/shard_map/ppermute | solution.py:561
  43.5 9.8 %collective-permute-start.19 = (bf16[4,193,128]{2,1,0:T(8,128)(2,1)S(1)}, bf16[4,193,128]{2,1,0:T(8,128)(2,1)S(1)}, u32[]{:S(2)}, u32[]{:S(2)}) collective-permute-start(bf16[4,193,128]{2,1,0:T(8,128)(2,1)S(1)} %get-tuple-element.72), channel_id=1, source_target_pairs={{0,4},{1,5},{2,6},{3,7},{4,0},{5,1},{6,2},{7,3},{8,12},{9,13},{10,... | collective-permute-start | bytes 592904 | tf_op jit(solution)/shard_map/ppermute | solution.py:561
  53.4 6.6 %collective-permute-start.20 = (bf16[193,128]{1,0:T(8,128)(2,1)S(1)}, bf16[193,128]{1,0:T(8,128)(2,1)S(1)}, u32[]{:S(2)}, u32[]{:S(2)}) collective-permute-start(bf16[193,128]{1,0:T(8,128)(2,1)S(1)} %get-tuple-element.74), channel_id=1, source_target_pairs={{0,8},{1,9},{2,10},{3,11},{4,12},{5,13},{6,14},{7,15},{8,16},{9,17... | collective-permute-start | bytes 148232 | tf_op jit(solution)/shard_map/ppermute | solution.py:561
  54.4 6.9 %collective-permute-start.21 = (bf16[193,128]{1,0:T(8,128)(2,1)S(1)}, bf16[193,128]{1,0:T(8,128)(2,1)S(1)}, u32[]{:S(2)}, u32[]{:S(2)}) collective-permute-start(bf16[193,128]{1,0:T(8,128)(2,1)S(1)} %get-tuple-element.75), channel_id=1, source_target_pairs={{0,16},{1,17},{2,18},{3,19},{4,20},{5,21},{6,22},{7,23},{8,24},{9,... | collective-permute-start | bytes 148232 | tf_op jit(solution)/shard_map/ppermute | solution.py:561
  57.0 4.4 %collective-permute-start.22 = (bf16[193,128]{1,0:T(8,128)(2,1)S(1)}, bf16[193,128]{1,0:T(8,128)(2,1)S(1)}, u32[]{:S(2)}, u32[]{:S(2)}) collective-permute-start(bf16[193,128]{1,0:T(8,128)(2,1)S(1)} %get-tuple-element.76), channel_id=1, source_target_pairs={{0,24},{1,25},{2,26},{3,27},{4,28},{5,29},{6,30},{7,31},{8,0},{9,1... | collective-permute-start | bytes 148232 | tf_op jit(solution)/shard_map/ppermute | solution.py:561

commit v15 on v13

--- a/solution.py
+++ b/solution.py
@@ -38,6 +38,7 @@
 FIRST_ROWS = 2 * PLANE * SHARE
 HEAD_ROWS = FIRST_ROWS - ROW_OUT
 SIDE, SIDE_ROWS = 208, 16
+FIRST_GROUPS = ((0, 2), (2, 4))
 SMALL_IN_SHARE = ROW_SMALL - (2 * PLANE * Z - 1) * SHARE
 
 F32 = jnp.float32
@@ -125,12 +126,12 @@
     wide[SHARE:SIDE, :] = jnp.zeros((SIDE - SHARE, LANES), F32)
     last = stage[Z - 1].astype(F32)
     wide[SIDE:, :] = last[SMALL_IN_SHARE:, :]
-    first[...] = wide[...].astype(BF16)
+    first[0] = wide[...].astype(BF16)
 
 
 def attend_kernel(ids, allowed, normed, *refs):
-    bufs = refs[: 2 * PLANE]
-    project_out, weights_out, attended_out, w_qkv, small, first_out, flat = refs[2 * PLANE :]
+    bufs = [ref.at[i] for ref in refs[:4] for i in range(ref.shape[0])]
+    project_out, weights_out, attended_out, w_qkv, small, first_out, flat = refs[4:]
     for slot, buf in enumerate(bufs):
         wide = buf[...].astype(F32)
         flat[pl.ds(ids[slot] * SHARE, SHARE), :] = wide[:SHARE, :]
@@ -443,7 +444,7 @@
 
 def stack(items):
     shape = (sum(item.shape[0] for item in items),) + items[0].shape[1:]
-    return call(stack_kernel, "stack", None, items, [like(*shape, kind=items[0].dtype)])
+    return call(stack_kernel, "stack", None, items, [like(*shape, kind=items[0].dtype)], us=0.01)
 
 
 def attend(ids, allowed, normed, bufs):
@@ -453,7 +454,7 @@
         attend_kernel, "attend", ids, [allowed, normed, *bufs],
         [like(*shape, kind=BF16) for shape in shapes]
         + [like(SMALL_ROWS, LANES), like(HEAD_ROWS, LANES)],
-        [pltpu.VMEM((FIRST_ROWS, LANES), F32)], us=0.2,
+        [pltpu.VMEM((FIRST_ROWS, LANES), F32)], us=0.01,
     )
 
 
@@ -514,7 +515,10 @@
     side = jnp.concatenate(
         [jnp.zeros((SIDE - SHARE, LANES), BF16), gathered[ROW_SMALL:ROW_TOTAL]], axis=0
     )
-    firsts = [jnp.concatenate([shares[0, k], side], axis=0) for k in order]
+    firsts = [jnp.concatenate([shares[0, k], side], axis=0)[None] for k in order]
+    firsts = [
+        jnp.concatenate(firsts[c + i : c + j]) for c in (0, PLANE) for i, j in FIRST_GROUPS
+    ]
     rests = []
     for group in (order[:PLANE], order[PLANE:]):
         rests += [shares[1:, group[0]], jnp.concatenate([shares[1:, k] for k in group[1:]])]
@@ -573,11 +577,12 @@
     normed, normed_turned, own, allowed = prepare(tokens, params, segment_ids)
     first, rest = call(
         sort_kernel, "sort_shares", where, [own] + [move(params, d, 0, 0) for d in range(1, Z)],
-        [like(SIDE + SMALL_ROWS, LANES, kind=BF16), like(Z - 1, SHARE, LANES, kind=BF16)],
+        [like(1, SIDE + SMALL_ROWS, LANES, kind=BF16), like(Z - 1, SHARE, LANES, kind=BF16)],
         [pltpu.VMEM((Z, SHARE, LANES), BF16), pltpu.VMEM((SIDE + SMALL_ROWS, LANES), F32)],
     )
     firsts = [first] + [move(first, 0, d, 0) for d in STEPS]
     rests = [move(rest, 0, d, 0) for d in STEPS]
+    firsts = [stack(firsts[i:j]) if j > i + 1 else firsts[i] for i, j in FIRST_GROUPS]
     firsts = firsts + [move(item, 0, 0, 1) for item in firsts]
     project, weights, attended, w_qkv, small, first = attend(ids, allowed, normed, firsts)
     *rests, attended = lax.optimization_barrier((*rests, attended))

time: 60.8 us -> 59.7 us (0.982)
  starting transfers between devices: 24.1 us -> 23 us
  local copies, waits for them, and re-layouts: 2.63 us -> 3.42 us
    ppermute x23 -> x21, starting transfers between devices: 24.1 us -> 23 us  [move(): return lax.ppermute(values, 'fsdp', pairs)]
    unnamed x10 -> x14, local copies, waits for them, and re-layouts: 2.54 us -> 3.33 us
    ppermute x23 -> x21, waiting for transfers between devices: 15.5 us -> 15 us  [move(): return lax.ppermute(values, 'fsdp', pairs)]
    pallas_call x11 -> x13, Pallas kernels: 17.6 us -> 17.3 us  [call(): pl.pallas_call(kernel, in_specs=[SMEM_SPEC] * with_ids + [VMEM_SPEC] * le...]
  transfers between devices with their start and end apart: 23 -> 21, of which waited for: 12 -> 10; matrix products, arithmetic and copies ran while one was open for 0% -> 0% of each run, Pallas kernels for 17% -> 17%
where the time goes in v15:
time: 59.7 us; the launch traced here: 59.4 us
  starting transfers between devices  23 us (39%)
  Pallas kernels  17.3 us (29%)
  waiting for transfers between devices  15 us (25%)
  local copies, waits for them, and re-layouts  3.42 us (6%)
  between operations  0.81 us (1%)
    ppermute x21, starting transfers between devices, move(): return lax.ppermute(values, 'fsdp', pairs)  23 us
    pallas_call x13, Pallas kernels, call(): pl.pallas_call(kernel, in_specs=[SMEM_SPEC] * with_ids + [VMEM_SPEC] * le...  17.3 us
    ppermute x21, waiting for transfers between devices, move(): return lax.ppermute(values, 'fsdp', pairs)  15 us
    unnamed x14, local copies, waits for them, and re-layouts  3.33 us
  transfers between devices with their start and end apart: 21, of which 10 were waited for; matrix products, arithmetic and copies ran while one was open for 0% of the time, Pallas kernels for 17%

profile of v15, /device:TPU:0, one launch (start us, length us, event | category | flops | bytes accessed | tf_op | source)
XLA Modules:
  0.0 59.4 jit_solution(8396842543774205328)
XLA Ops:
  0.6 3.1 %collective-permute-start = (bf16[193,128]{1,0:T(8,128)(2,1)}, bf16[193,128]{1,0:T(8,128)(2,1)S(1)}, u32[]{:S(2)}, u32[]{:S(2)}) collective-permute-start(bf16[193,128]{1,0:T(8,128)(2,1)} %params.1), channel_id=1, source_target_pairs={{0,8},{1,9},{2,10},{3,11},{4,12},{5,13},{6,14},{7,15},{8,16},{9,17... | collective-permute-start | bytes 148232 | tf_op jit(solution)/shard_map/ppermute | solution.py:563
  3.7 2.6 %collective-permute-start.1 = (bf16[193,128]{1,0:T(8,128)(2,1)}, bf16[193,128]{1,0:T(8,128)(2,1)S(1)}, u32[]{:S(2)}, u32[]{:S(2)}) collective-permute-start(bf16[193,128]{1,0:T(8,128)(2,1)} %params.1), channel_id=1, source_target_pairs={{0,16},{1,17},{2,18},{3,19},{4,20},{5,21},{6,22},{7,23},{8,24},{9,... | collective-permute-start | bytes 148232 | tf_op jit(solution)/shard_map/ppermute | solution.py:563
  6.3 1.3 %collective-permute-start.2 = (bf16[193,128]{1,0:T(8,128)(2,1)}, bf16[193,128]{1,0:T(8,128)(2,1)S(1)}, u32[]{:S(2)}, u32[]{:S(2)}) collective-permute-start(bf16[193,128]{1,0:T(8,128)(2,1)} %params.1), channel_id=1, source_target_pairs={{0,24},{1,25},{2,26},{3,27},{4,28},{5,29},{6,30},{7,31},{8,0},{9,1... | collective-permute-start | bytes 148232 | tf_op jit(solution)/shard_map/ppermute | solution.py:563
  7.6 1.0 %copy-done.1 = bf16[1024,256]{1,0:T(8,128)(2,1)S(1)} copy-done((bf16[1024,256]{1,0:T(8,128)(2,1)S(1)}, bf16[1024,256]{1,0:T(8,128)(2,1)}, u32[]{:S(2)}) %copy-start.1) | copy-done | bytes 524312
  8.7 0.8 %copy-done.3 = bf16[193,128]{1,0:T(8,128)(2,1)S(1)} copy-done((bf16[193,128]{1,0:T(8,128)(2,1)S(1)}, bf16[193,128]{1,0:T(8,128)(2,1)}, u32[]{:S(2)}) %copy-start.3) | copy-done | bytes 49432
  9.5 0.7 %copy-done.4 = s32[1024]{0:T(1024)S(1)} copy-done((s32[1024]{0:T(1024)S(1)}, s32[1024]{0:T(1024)}, u32[]{:S(2)}) %copy-start.4) | copy-done | bytes 4120
  10.2 0.7 %prepare.1 = (f32[1024,256]{1,0:T(8,128)S(1)}, bf16[256,1024]{1,0:T(8,128)(2,1)S(1)}, bf16[193,128]{1,0:T(8,128)(2,1)S(1)}, f32[1024,128]{1,0:T(8,128)S(1)}) custom-call(bf16[1024,256]{1,0:T(8,128)(2,1)S(1)} %copy-done.1, bf16[193,128]{1,0:T(8,128)(2,1)S(1)} %copy-done.3, s32[8,128]{1,0:T(8,128)S(1)} %bitcast.10), custom_call_target="tpu_custom_call" | custom-call | flops 2000000000 | bytes 1048576 | tf_op jit(solution)/shard_map/prepare/pallas_call | solution.py:418
  10.9 0.0 copy-start.5
  10.9 0.8 %copy-done.5 = bf16[256,1024]{1,0:T(8,128)(2,1)} copy-done((bf16[256,1024]{1,0:T(8,128)(2,1)}, bf16[256,1024]{1,0:T(8,128)(2,1)S(1)}, u32[]{:S(2)}) %copy-start.5) | copy-done | bytes 524312
  11.7 0.1 sort_shares.1
  11.7 2.5 %collective-permute-start.6 = (bf16[1,240,128]{2,1,0:T(8,128)(2,1)S(1)}, bf16[1,240,128]{2,1,0:T(8,128)(2,1)S(1)}, u32[]{:S(2)}, u32[]{:S(2)}) collective-permute-start(bf16[1,240,128]{2,1,0:T(8,128)(2,1)S(1)} %get-tuple-element.42.refs_0_), channel_id=1, source_target_pairs={{0,6},{1,7},{2,4},{3,5},{4,2},{5,3},{6,0},{7,1},{8,14},{9,15},{10,... | collective-permute-start | bytes 184328 | tf_op jit(solution)/shard_map/ppermute | solution.py:563
  14.2 0.5 collective-permute-start.7
  14.8 0.5 collective-permute-start.8
  15.3 2.4 %collective-permute-start.3 = (bf16[3,193,128]{2,1,0:T(8,128)(2,1)S(1)}, bf16[3,193,128]{2,1,0:T(8,128)(2,1)S(1)}, u32[]{:S(2)}, u32[]{:S(2)}) collective-permute-start(bf16[3,193,128]{2,1,0:T(8,128)(2,1)S(1)} %get-tuple-element.39.refs_0_), channel_id=1, source_target_pairs={{0,6},{1,7},{2,4},{3,5},{4,2},{5,3},{6,0},{7,1},{8,14},{9,15},{10,... | collective-permute-start | bytes 444680 | tf_op jit(solution)/shard_map/ppermute | solution.py:563
  17.7 0.5 collective-permute-start.4
  18.3 0.5 collective-permute-start.5
  18.8 0.3 collective-permute-done.7.refs_0_
  19.1 1.4 %collective-permute-done.8.refs_1_ = bf16[1,240,128]{2,1,0:T(8,128)(2,1)S(1)} collective-permute-done((bf16[1,240,128]{2,1,0:T(8,128)(2,1)S(1)}, bf16[1,240,128]{2,1,0:T(8,128)(2,1)S(1)}, u32[]{:S(2)}, u32[]{:S(2)}) %collective-permute-start.8) | collective-permute-done | bytes 61472 | tf_op jit(solution)/shard_map/ppermute | solution.py:563
  20.5 0.0 copy-start
  20.5 0.1 collective-permute-start.10
  20.7 0.1 stack.38.ids
  20.8 1.2 %collective-permute-done.10.refs_3_ = bf16[2,240,128]{2,1,0:T(8,128)(2,1)S(1)} collective-permute-done((bf16[2,240,128]{2,1,0:T(8,128)(2,1)S(1)}, bf16[2,240,128]{2,1,0:T(8,128)(2,1)S(1)}, u32[]{:S(2)}, u32[]{:S(2)}) %collective-permute-start.10) | collective-permute-done | bytes 122912 | tf_op jit(solution)/shard_map/ppermute | solution.py:563
  21.9 2.6 %attend.1 = (bf16[1024,768]{1,0:T(8,128)(2,1)S(1)}, bf16[1024,512]{1,0:T(8,128)(2,1)S(1)}, bf16[1024,256]{1,0:T(8,128)(2,1)S(1)}, bf16[256,768]{1,0:T(8,128)(2,1...) custom-call(s32[8]{0:T(128)S(1)} %stack.38.ids, f32[1024,128]{1,0:T(8,128)S(1)} %get-tuple-element.40.allowed, ...), custom_call_target="tpu_custom_call" | custom-call | flops 10000000 | bytes 1048576 | tf_op jit(solution)/shard_map/attend/pallas_call | solution.py:418
  24.6 0.2 collective-permute-start.12
  24.9 0.4 collective-permute-start.11
  25.2 1.5 %collective-permute-done.11.refs_2_ = bf16[3,193,128]{2,1,0:T(8,128)(2,1)S(1)} collective-permute-done((bf16[3,193,128]{2,1,0:T(8,128)(2,1)S(1)}, bf16[3,193,128]{2,1,0:T(8,128)(2,1)S(1)}, u32[]{:S(2)}, u32[]{:S(2)}) %collective-permute-start.11) | collective-permute-done | bytes 148256 | tf_op jit(solution)/shard_map/ppermute | solution.py:563
  26.8 0.0 copy-start.6
  26.8 6.2 %feed.1 = (f32[1024,256]{1,0:T(8,128)S(1)}, bf16[1024,1024]{1,0:T(8,128)(2,1)S(1)}, f32[1024,256]{1,0:T(8,128)S(1)}, bf16[1024,256]{1,0:T(8,128)(2,1)S(1)}, bf16...) custom-call(s32[8]{0:T(128)S(1)} %stack.38.ids, ...), custom_call_target="tpu_custom_call" | custom-call | flops 8000000000 | bytes 1048576 | tf_op jit(solution)/shard_map/feed/pallas_call | solution.py:418
  33.0 0.2 collective-permute-start.14
  33.2 3.1 %attend_back.1 = (bf16[1024,768]{1,0:T(8,128)(2,1)S(1)}, f32[4,224,128]{2,1,0:T(8,128)S(1)}, bf16[4,224,128]{2,1,0:T(8,128)(2,1)S(1)}) custom-call(s32[8]{0:T(128)S(1)} %stack.38.ids, bf16[1024,768]{1,0:T(8,128)(2,1)S(1)} %get-tuple-element.53.project, bf16[1024,512]{1,0:T(8,128)(2,1)S(1)} %get-tuple-element.54.weights, ...), custom_call_target="tpu_custom_call" | custom-call | flops 4000000000 | bytes 1048576 | tf_op jit(solution)/shard_map/attend_back/pallas_call | solution.py:418
  36.3 0.4 collective-permute-start.13
  36.7 1.1 %collective-permute-done.13.first_in = bf16[4,224,128]{2,1,0:T(8,128)(2,1)S(1)} collective-permute-done((bf16[4,224,128]{2,1,0:T(8,128)(2,1)S(1)}, bf16[4,224,128]{2,1,0:T(8,128)(2,1)S(1)}, u32[]{:S(2)}, u32[]{:S(2)}) %collective-permute-start.13) | collective-permute-done | bytes 229408 | tf_op jit(solution)/shard_map/ppermute | solution.py:563
  37.8 0.2 add_core.1
  38.1 2.2 %collective-permute-start.15 = (bf16[4,193,128]{2,1,0:T(8,128)(2,1)S(1)}, bf16[4,193,128]{2,1,0:T(8,128)(2,1)S(1)}, u32[]{:S(2)}, u32[]{:S(2)}) collective-permute-start(bf16[4,193,128]{2,1,0:T(8,128)(2,1)S(1)} %get-tuple-element.66), channel_id=1, source_target_pairs={{0,6},{1,7},{2,4},{3,5},{4,2},{5,3},{6,0},{7,1},{8,14},{9,15},{10,... | collective-permute-start | bytes 592904 | tf_op jit(solution)/shard_map/ppermute | solution.py:563
  40.3 0.4 collective-permute-start.16
  40.7 1.1 %collective-permute-start.17 = (bf16[4,193,128]{2,1,0:T(8,128)(2,1)S(1)}, bf16[4,193,128]{2,1,0:T(8,128)(2,1)S(1)}, u32[]{:S(2)}, u32[]{:S(2)}) collective-permute-start(bf16[4,193,128]{2,1,0:T(8,128)(2,1)S(1)} %get-tuple-element.68), channel_id=1, source_target_pairs={{0,4},{1,5},{2,6},{3,7},{4,0},{5,1},{6,2},{7,3},{8,12},{9,13},{10,... | collective-permute-start | bytes 592904 | tf_op jit(solution)/shard_map/ppermute | solution.py:563
  41.8 2.0 %input_grad.1 = f32[1024,256]{1,0:T(8,128)} custom-call(bf16[1024,256]{1,0:T(8,128)(2,1)S(1)} %copy-done.2, bf16[1024,768]{1,0:T(8,128)(2,1)S(1)} %get-tuple-element.59.grad_project, f32[1024,256]{1,0:T(8,128)S(1)} %get-tuple-element.60.grad_middle, bf16[256,768]{1,0:T(8,128)(2,1)S(1)} %get-tuple-element.57.w_qkv, f32[32,128]{1,0:T(8,128)S(1)} %get-tuple-element.45.small), custom_call_target="tpu_custom_call" | custom-call | flops 2000000000 | bytes 1048576 | tf_op jit(solution)/shard_map/input_grad/pallas_call | solution.py:418
  43.8 3.2 %collective-permute-done.15.refs_0_ = bf16[4,193,128]{2,1,0:T(8,128)(2,1)S(1)} collective-permute-done((bf16[4,193,128]{2,1,0:T(8,128)(2,1)S(1)}, bf16[4,193,128]{2,1,0:T(8,128)(2,1)S(1)}, u32[]{:S(2)}, u32[]{:S(2)}) %collective-permute-start.15) | collective-permute-done | bytes 197664 | tf_op jit(solution)/shard_map/ppermute | solution.py:563
  47.0 3.4 %collective-permute-done.16.refs_1_ = bf16[4,193,128]{2,1,0:T(8,128)(2,1)S(1)} collective-permute-done((bf16[4,193,128]{2,1,0:T(8,128)(2,1)S(1)}, bf16[4,193,128]{2,1,0:T(8,128)(2,1)S(1)}, u32[]{:S(2)}, u32[]{:S(2)}) %collective-permute-start.16) | collective-permute-done | bytes 197664 | tf_op jit(solution)/shard_map/ppermute | solution.py:563
  50.4 0.4 collective-permute-done.17.refs_2_
  50.8 0.2 add_plane.1
  50.9 0.8 %collective-permute-start.18 = (bf16[193,128]{1,0:T(8,128)(2,1)S(1)}, bf16[193,128]{1,0:T(8,128)(2,1)S(1)}, u32[]{:S(2)}, u32[]{:S(2)}) collective-permute-start(bf16[193,128]{1,0:T(8,128)(2,1)S(1)} %get-tuple-element.70), channel_id=1, source_target_pairs={{0,8},{1,9},{2,10},{3,11},{4,12},{5,13},{6,14},{7,15},{8,16},{9,17... | collective-permute-start | bytes 148232 | tf_op jit(solution)/shard_map/ppermute | solution.py:563
  51.7 1.9 %collective-permute-start.19 = (bf16[193,128]{1,0:T(8,128)(2,1)S(1)}, bf16[193,128]{1,0:T(8,128)(2,1)S(1)}, u32[]{:S(2)}, u32[]{:S(2)}) collective-permute-start(bf16[193,128]{1,0:T(8,128)(2,1)S(1)} %get-tuple-element.71), channel_id=1, source_target_pairs={{0,16},{1,17},{2,18},{3,19},{4,20},{5,21},{6,22},{7,23},{8,24},{9,... | collective-permute-start | bytes 148232 | tf_op jit(solution)/shard_map/ppermute | solution.py:563
  53.6 1.2 %collective-permute-start.20 = (bf16[193,128]{1,0:T(8,128)(2,1)S(1)}, bf16[193,128]{1,0:T(8,128)(2,1)S(1)}, u32[]{:S(2)}, u32[]{:S(2)}) collective-permute-start(bf16[193,128]{1,0:T(8,128)(2,1)S(1)} %get-tuple-element.72), channel_id=1, source_target_pairs={{0,24},{1,25},{2,26},{3,27},{4,28},{5,29},{6,30},{7,31},{8,0},{9,1... | collective-permute-start | bytes 148232 | tf_op jit(solution)/shard_map/ppermute | solution.py:563
  54.8 1.5 %result.1 = bf16[1024,256]{1,0:T(8,128)(2,1)} custom-call(f32[1024,256]{1,0:T(8,128)S(1)} %get-tuple-element.50.middle, bf16[1024,1024]{1,0:T(8,128)(2,1)S(1)} %get-tuple-element.51.activated, bf16[1024,256]{1,0:T(8,128)(2,1)S(1)} %get-tuple-element.52.w_down, f32[32,128]{1,0:T(8,128)S(1)} %get-tuple-element.45.small), custom_call_target="tpu_custom_call" | custom-call | flops 2000000000 | bytes 1048576 | tf_op jit(solution)/shard_map/result/pallas_call | solution.py:418
  56.3 1.1 %collective-permute-done.18.refs_0_ = bf16[193,128]{1,0:T(8,128)(2,1)S(1)} collective-permute-done((bf16[193,128]{1,0:T(8,128)(2,1)S(1)}, bf16[193,128]{1,0:T(8,128)(2,1)S(1)}, u32[]{:S(2)}, u32[]{:S(2)}) %collective-permute-start.18) | collective-permute-done | bytes 49440 | tf_op jit(solution)/shard_map/ppermute | solution.py:563
  57.5 1.3 %collective-permute-done.19.refs_1_ = bf16[193,128]{1,0:T(8,128)(2,1)S(1)} collective-permute-done((bf16[193,128]{1,0:T(8,128)(2,1)S(1)}, bf16[193,128]{1,0:T(8,128)(2,1)S(1)}, u32[]{:S(2)}, u32[]{:S(2)}) %collective-permute-start.19) | collective-permute-done | bytes 49440 | tf_op jit(solution)/shard_map/ppermute | solution.py:563
  58.8 0.7 %add_column.1 = f32[193,128]{1,0:T(8,128)} custom-call(f32[193,128]{1,0:T(8,128)S(1)} %get-tuple-element.69.kept, bf16[193,128]{1,0:T(8,128)(2,1)S(1)} %collective-permute-done.18.refs_0_, bf16[193,128]{1,0:T(8,128)(2,1)S(1)} %collective-permute-done.19.refs_1_, bf16[193,128]{1,0:T(8,128)(2,1)S(1)} %collective-permute-done.20.refs_2_), custom_call_target="tpu_custom_call" | custom-call | flops 1000000000 | bytes 1048576 | tf_op jit(solution)/shard_map/add_column/pallas_call | solution.py:418
  (22 shorter events, 0.1 us)
Async XLA Ops:
  0.6 11.0 %collective-permute-start = (bf16[193,128]{1,0:T(8,128)(2,1)}, bf16[193,128]{1,0:T(8,128)(2,1)S(1)}, u32[]{:S(2)}, u32[]{:S(2)}) collective-permute-start(bf16[193,128]{1,0:T(8,128)(2,1)} %params.1), channel_id=1, source_target_pairs={{0,8},{1,9},{2,10},{3,11},{4,12},{5,13},{6,14},{7,15},{8,16},{9,17... | collective-permute-start | bytes 148232 | tf_op jit(solution)/shard_map/ppermute | solution.py:563
  3.7 8.0 %collective-permute-start.1 = (bf16[193,128]{1,0:T(8,128)(2,1)}, bf16[193,128]{1,0:T(8,128)(2,1)S(1)}, u32[]{:S(2)}, u32[]{:S(2)}) collective-permute-start(bf16[193,128]{1,0:T(8,128)(2,1)} %params.1), channel_id=1, source_target_pairs={{0,16},{1,17},{2,18},{3,19},{4,20},{5,21},{6,22},{7,23},{8,24},{9,... | collective-permute-start | bytes 148232 | tf_op jit(solution)/shard_map/ppermute | solution.py:563
  6.3 5.4 %collective-permute-start.2 = (bf16[193,128]{1,0:T(8,128)(2,1)}, bf16[193,128]{1,0:T(8,128)(2,1)S(1)}, u32[]{:S(2)}, u32[]{:S(2)}) collective-permute-start(bf16[193,128]{1,0:T(8,128)(2,1)} %params.1), channel_id=1, source_target_pairs={{0,24},{1,25},{2,26},{3,27},{4,28},{5,29},{6,30},{7,31},{8,0},{9,1... | collective-permute-start | bytes 148232 | tf_op jit(solution)/shard_map/ppermute | solution.py:563
  7.6 1.0 %copy-start.1 = (bf16[1024,256]{1,0:T(8,128)(2,1)S(1)}, bf16[1024,256]{1,0:T(8,128)(2,1)}, u32[]{:S(2)}) copy-start(bf16[1024,256]{1,0:T(8,128)(2,1)} %tok.5) | copy-start | bytes 1572868
  8.7 0.8 %copy-start.3 = (bf16[193,128]{1,0:T(8,128)(2,1)S(1)}, bf16[193,128]{1,0:T(8,128)(2,1)}, u32[]{:S(2)}) copy-start(bf16[193,128]{1,0:T(8,128)(2,1)} %params.1) | copy-start | bytes 148228
  9.5 0.7 %copy-start.4 = (s32[1024]{0:T(1024)S(1)}, s32[1024]{0:T(1024)}, u32[]{:S(2)}) copy-start(s32[1024]{0:T(1024)} %param.6) | copy-start | bytes 12292
  10.9 0.8 %copy-start.5 = (bf16[256,1024]{1,0:T(8,128)(2,1)}, bf16[256,1024]{1,0:T(8,128)(2,1)S(1)}, u32[]{:S(2)}) copy-start(bf16[256,1024]{1,0:T(8,128)(2,1)S(1)} %get-tuple-element.56.normed_turned) | copy-start | bytes 1572868
  11.7 6.5 %collective-permute-start.6 = (bf16[1,240,128]{2,1,0:T(8,128)(2,1)S(1)}, bf16[1,240,128]{2,1,0:T(8,128)(2,1)S(1)}, u32[]{:S(2)}, u32[]{:S(2)}) collective-permute-start(bf16[1,240,128]{2,1,0:T(8,128)(2,1)S(1)} %get-tuple-element.42.refs_0_), channel_id=1, source_target_pairs={{0,6},{1,7},{2,4},{3,5},{4,2},{5,3},{6,0},{7,1},{8,14},{9,15},{10,... | collective-permute-start | bytes 184328 | tf_op jit(solution)/shard_map/ppermute | solution.py:563
  14.2 4.8 %collective-permute-start.7 = (bf16[1,240,128]{2,1,0:T(8,128)(2,1)S(1)}, bf16[1,240,128]{2,1,0:T(8,128)(2,1)S(1)}, u32[]{:S(2)}, u32[]{:S(2)}) collective-permute-start(bf16[1,240,128]{2,1,0:T(8,128)(2,1)S(1)} %get-tuple-element.42.refs_0_), channel_id=1, source_target_pairs={{0,2},{1,3},{2,0},{3,1},{4,6},{5,7},{6,4},{7,5},{8,10},{9,11},{10,... | collective-permute-start | bytes 184328 | tf_op jit(solution)/shard_map/ppermute | solution.py:563
  14.8 5.8 %collective-permute-start.8 = (bf16[1,240,128]{2,1,0:T(8,128)(2,1)S(1)}, bf16[1,240,128]{2,1,0:T(8,128)(2,1)S(1)}, u32[]{:S(2)}, u32[]{:S(2)}) collective-permute-start(bf16[1,240,128]{2,1,0:T(8,128)(2,1)S(1)} %get-tuple-element.42.refs_0_), channel_id=1, source_target_pairs={{0,4},{1,5},{2,6},{3,7},{4,0},{5,1},{6,2},{7,3},{8,12},{9,13},{10,... | collective-permute-start | bytes 184328 | tf_op jit(solution)/shard_map/ppermute | solution.py:563
  15.3 9.3 %collective-permute-start.3 = (bf16[3,193,128]{2,1,0:T(8,128)(2,1)S(1)}, bf16[3,193,128]{2,1,0:T(8,128)(2,1)S(1)}, u32[]{:S(2)}, u32[]{:S(2)}) collective-permute-start(bf16[3,193,128]{2,1,0:T(8,128)(2,1)S(1)} %get-tuple-element.39.refs_0_), channel_id=1, source_target_pairs={{0,6},{1,7},{2,4},{3,5},{4,2},{5,3},{6,0},{7,1},{8,14},{9,15},{10,... | collective-permute-start | bytes 444680 | tf_op jit(solution)/shard_map/ppermute | solution.py:563
  17.7 6.9 %collective-permute-start.4 = (bf16[3,193,128]{2,1,0:T(8,128)(2,1)S(1)}, bf16[3,193,128]{2,1,0:T(8,128)(2,1)S(1)}, u32[]{:S(2)}, u32[]{:S(2)}) collective-permute-start(bf16[3,193,128]{2,1,0:T(8,128)(2,1)S(1)} %get-tuple-element.39.refs_0_), channel_id=1, source_target_pairs={{0,2},{1,3},{2,0},{3,1},{4,6},{5,7},{6,4},{7,5},{8,10},{9,11},{10,... | collective-permute-start | bytes 444680 | tf_op jit(solution)/shard_map/ppermute | solution.py:563
  18.3 6.3 %collective-permute-start.5 = (bf16[3,193,128]{2,1,0:T(8,128)(2,1)S(1)}, bf16[3,193,128]{2,1,0:T(8,128)(2,1)S(1)}, u32[]{:S(2)}, u32[]{:S(2)}) collective-permute-start(bf16[3,193,128]{2,1,0:T(8,128)(2,1)S(1)} %get-tuple-element.39.refs_0_), channel_id=1, source_target_pairs={{0,4},{1,5},{2,6},{3,7},{4,0},{5,1},{6,2},{7,3},{8,12},{9,13},{10,... | collective-permute-start | bytes 444680 | tf_op jit(solution)/shard_map/ppermute | solution.py:563
  19.1 1.7 %collective-permute-start.9 = (bf16[2,240,128]{2,1,0:T(8,128)(2,1)S(1)}, bf16[2,240,128]{2,1,0:T(8,128)(2,1)S(1)}, u32[]{:S(2)}, u32[]{:S(2)}) collective-permute-start(bf16[2,240,128]{2,1,0:T(8,128)(2,1)S(1)} %stack.39.refs_0_), channel_id=1, source_target_pairs={{0,1},{1,0},{2,3},{3,2},{4,5},{5,4},{6,7},{7,6},{8,9},{9,8},{10,11... | collective-permute-start | bytes 368648 | tf_op jit(solution)/shard_map/ppermute | solution.py:563
  20.5 6.2 %copy-start = (bf16[1024,256]{1,0:T(8,128)(2,1)S(1)}, bf16[1024,256]{1,0:T(8,128)(2,1)}, u32[]{:S(2)}) copy-start(bf16[1024,256]{1,0:T(8,128)(2,1)} %cot.1) | copy-start | bytes 1572868
  20.5 1.4 %collective-permute-start.10 = (bf16[2,240,128]{2,1,0:T(8,128)(2,1)S(1)}, bf16[2,240,128]{2,1,0:T(8,128)(2,1)S(1)}, u32[]{:S(2)}, u32[]{:S(2)}) collective-permute-start(bf16[2,240,128]{2,1,0:T(8,128)(2,1)S(1)} %stack.40.refs_1_), channel_id=1, source_target_pairs={{0,1},{1,0},{2,3},{3,2},{4,5},{5,4},{6,7},{7,6},{8,9},{9,8},{10,11... | collective-permute-start | bytes 368648 | tf_op jit(solution)/shard_map/ppermute | solution.py:563
  20.8 6.0 %copy-start.2 = (bf16[1024,256]{1,0:T(8,128)(2,1)S(1)}, bf16[1024,256]{1,0:T(8,128)(2,1)}, u32[]{:S(2)}) copy-start(bf16[1024,256]{1,0:T(8,128)(2,1)} %tok.5) | copy-start | bytes 1572868
  24.6 2.1 %collective-permute-start.12 = (bf16[9,193,128]{2,1,0:T(8,128)(2,1)S(1)}, bf16[9,193,128]{2,1,0:T(8,128)(2,1)S(1)}, u32[]{:S(2)}, u32[]{:S(2)}) collective-permute-start(bf16[9,193,128]{2,1,0:T(8,128)(2,1)S(1)} %stack.41.refs_1_), channel_id=1, source_target_pairs={{0,1},{1,0},{2,3},{3,2},{4,5},{5,4},{6,7},{7,6},{8,9},{9,8},{10,11... | collective-permute-start | bytes 1334024 | tf_op jit(solution)/shard_map/ppermute | solution.py:563
  24.9 1.9 %collective-permute-start.11 = (bf16[3,193,128]{2,1,0:T(8,128)(2,1)S(1)}, bf16[3,193,128]{2,1,0:T(8,128)(2,1)S(1)}, u32[]{:S(2)}, u32[]{:S(2)}) collective-permute-start(bf16[3,193,128]{2,1,0:T(8,128)(2,1)S(1)} %get-tuple-element.39.refs_0_), channel_id=1, source_target_pairs={{0,1},{1,0},{2,3},{3,2},{4,5},{5,4},{6,7},{7,6},{8,9},{9,8},{10,11... | collective-permute-start | bytes 444680 | tf_op jit(solution)/shard_map/ppermute | solution.py:563
  26.8 6.4 %copy-start.6 = (bf16[256,1024]{1,0:T(8,128)(2,1)S(1)}, bf16[256,1024]{1,0:T(8,128)(2,1)}, u32[]{:S(2)}) copy-start(bf16[256,1024]{1,0:T(8,128)(2,1)} %copy-done.5) | copy-start | bytes 1572868
  33.0 4.9 %collective-permute-start.14 = (bf16[12,193,128]{2,1,0:T(8,128)(2,1)S(1)}, bf16[12,193,128]{2,1,0:T(8,128)(2,1)S(1)}, u32[]{:S(2)}, u32[]{:S(2)}) collective-permute-start(bf16[12,193,128]{2,1,0:T(8,128)(2,1)S(1)} %get-tuple-element.64), channel_id=1, source_target_pairs={{0,1},{1,0},{2,3},{3,2},{4,5},{5,4},{6,7},{7,6},{8,9},{9,8},{10,11... | collective-permute-start | bytes 1778696 | tf_op jit(solution)/shard_map/ppermute | solution.py:563
  36.3 1.6 %collective-permute-start.13 = (bf16[4,224,128]{2,1,0:T(8,128)(2,1)S(1)}, bf16[4,224,128]{2,1,0:T(8,128)(2,1)S(1)}, u32[]{:S(2)}, u32[]{:S(2)}) collective-permute-start(bf16[4,224,128]{2,1,0:T(8,128)(2,1)S(1)} %get-tuple-element.62), channel_id=1, source_target_pairs={{0,1},{1,0},{2,3},{3,2},{4,5},{5,4},{6,7},{7,6},{8,9},{9,8},{10,11... | collective-permute-start | bytes 688136 | tf_op jit(solution)/shard_map/ppermute | solution.py:563
  38.1 8.9 %collective-permute-start.15 = (bf16[4,193,128]{2,1,0:T(8,128)(2,1)S(1)}, bf16[4,193,128]{2,1,0:T(8,128)(2,1)S(1)}, u32[]{:S(2)}, u32[]{:S(2)}) collective-permute-start(bf16[4,193,128]{2,1,0:T(8,128)(2,1)S(1)} %get-tuple-element.66), channel_id=1, source_target_pairs={{0,6},{1,7},{2,4},{3,5},{4,2},{5,3},{6,0},{7,1},{8,14},{9,15},{10,... | collective-permute-start | bytes 592904 | tf_op jit(solution)/shard_map/ppermute | solution.py:563
  40.3 10.1 %collective-permute-start.16 = (bf16[4,193,128]{2,1,0:T(8,128)(2,1)S(1)}, bf16[4,193,128]{2,1,0:T(8,128)(2,1)S(1)}, u32[]{:S(2)}, u32[]{:S(2)}) collective-permute-start(bf16[4,193,128]{2,1,0:T(8,128)(2,1)S(1)} %get-tuple-element.67), channel_id=1, source_target_pairs={{0,2},{1,3},{2,0},{3,1},{4,6},{5,7},{6,4},{7,5},{8,10},{9,11},{10,... | collective-permute-start | bytes 592904 | tf_op jit(solution)/shard_map/ppermute | solution.py:563
  40.7 10.1 %collective-permute-start.17 = (bf16[4,193,128]{2,1,0:T(8,128)(2,1)S(1)}, bf16[4,193,128]{2,1,0:T(8,128)(2,1)S(1)}, u32[]{:S(2)}, u32[]{:S(2)}) collective-permute-start(bf16[4,193,128]{2,1,0:T(8,128)(2,1)S(1)} %get-tuple-element.68), channel_id=1, source_target_pairs={{0,4},{1,5},{2,6},{3,7},{4,0},{5,1},{6,2},{7,3},{8,12},{9,13},{10,... | collective-permute-start | bytes 592904 | tf_op jit(solution)/shard_map/ppermute | solution.py:563
  50.9 6.5 %collective-permute-start.18 = (bf16[193,128]{1,0:T(8,128)(2,1)S(1)}, bf16[193,128]{1,0:T(8,128)(2,1)S(1)}, u32[]{:S(2)}, u32[]{:S(2)}) collective-permute-start(bf16[193,128]{1,0:T(8,128)(2,1)S(1)} %get-tuple-element.70), channel_id=1, source_target_pairs={{0,8},{1,9},{2,10},{3,11},{4,12},{5,13},{6,14},{7,15},{8,16},{9,17... | collective-permute-start | bytes 148232 | tf_op jit(solution)/shard_map/ppermute | solution.py:563
  51.7 7.0 %collective-permute-start.19 = (bf16[193,128]{1,0:T(8,128)(2,1)S(1)}, bf16[193,128]{1,0:T(8,128)(2,1)S(1)}, u32[]{:S(2)}, u32[]{:S(2)}) collective-permute-start(bf16[193,128]{1,0:T(8,128)(2,1)S(1)} %get-tuple-element.71), channel_id=1, source_target_pairs={{0,16},{1,17},{2,18},{3,19},{4,20},{5,21},{6,22},{7,23},{8,24},{9,... | collective-permute-start | bytes 148232 | tf_op jit(solution)/shard_map/ppermute | solution.py:563
  53.6 5.1 %collective-permute-start.20 = (bf16[193,128]{1,0:T(8,128)(2,1)S(1)}, bf16[193,128]{1,0:T(8,128)(2,1)S(1)}, u32[]{:S(2)}, u32[]{:S(2)}) collective-permute-start(bf16[193,128]{1,0:T(8,128)(2,1)S(1)} %get-tuple-element.72), channel_id=1, source_target_pairs={{0,24},{1,25},{2,26},{3,27},{4,28},{5,29},{6,30},{7,31},{8,0},{9,1... | collective-permute-start | bytes 148232 | tf_op jit(solution)/shard_map/ppermute | solution.py:563

commit v16 on v15

--- a/solution.py
+++ b/solution.py
@@ -198,8 +198,6 @@
             share = ids[slot] + z * 2 * PLANE
             flat[pl.ds(share * SHARE - ROW_OUT, SHARE), :] = buf[z - 1].astype(F32)
     matrix_from_flat(flat, 0, D, D, w_out)
-    matrix_from_flat(flat, ROW_UP - ROW_OUT, D, FF, w_up)
-    matrix_from_flat(flat, ROW_DOWN - ROW_OUT, FF, D, w_down)
 
     gain = small_vector(small, GAIN_TWO, 2)
     middle = (
@@ -208,6 +206,8 @@
     middle_out[...] = middle
     normed, rate = normalize(middle)
     normed_low = (normed * gain + small_vector(small, SHIFT_TWO, 2)).astype(BF16)
+    matrix_from_flat(flat, ROW_UP - ROW_OUT, D, FF, w_up)
+    matrix_from_flat(flat, ROW_DOWN - ROW_OUT, FF, D, w_down)
     normed_turned = normed_low.T
     cotangent = cot[...]
     slope = 0.7978845608028654
@@ -379,13 +379,14 @@
 
 def add_core_kernel(first, first_in, rest, rest_in, keep_out, *refs):
     sends, column = refs[:-1], refs[-1]
-    end = SMALL_IN_SHARE + LATE_SMALL
+    start = (Z - 1) * SHARE + SMALL_IN_SHARE
     for p, out in enumerate((keep_out, *sends)):
         item = first[p] + first_in[p].astype(F32)
-        span = slice(p * (Z - 1), (p + 1) * (Z - 1))
-        column[0] = item[:SHARE, :]
-        column[1:] = rest[span] + rest_in[span].astype(F32)
-        column[Z - 1, SMALL_IN_SHARE:end, :] += item[SIDE : SIDE + LATE_SMALL, :]
+        column[:SHARE, :] = item[:SHARE, :]
+        for z in range(1, Z):
+            slot = p * (Z - 1) + z - 1
+            column[z * SHARE : (z + 1) * SHARE, :] = rest[slot] + rest_in[slot].astype(F32)
+        column[start : start + LATE_SMALL, :] += item[SIDE : SIDE + LATE_SMALL, :]
         out[...] = column[...].astype(out.dtype)
 
 
@@ -393,9 +394,9 @@
     arrived = refs[: PLANE - 1]
     keep_out, *sends, column = refs[PLANE - 1 :]
     column[...] = kept[...] + sum(item[...].astype(F32) for item in arrived)
-    keep_out[...] = column[ids[0]]
+    keep_out[...] = column[pl.ds(ids[0] * SHARE, SHARE), :]
     for d, out in enumerate(sends):
-        out[...] = column[lax.rem(ids[0] + d + 1, Z)].astype(BF16)
+        out[...] = column[pl.ds(lax.rem(ids[0] + d + 1, Z) * SHARE, SHARE), :].astype(BF16)
 
 
 def add_column_kernel(kept, *refs):
@@ -597,7 +598,7 @@
         ids, project, weights, grad_attended, normed_turned, w_qkv, small, first_grad, BF16
     )
     first_in = move(send, 0, 0, 1)
-    part = (Z, SHARE, LANES)
+    part = (Z * SHARE, LANES)
     kept, *sends = call(
         add_core_kernel, "add_core", None, [first, first_in, rest, rest_in],
         [like(*part)] + [like(*part, kind=BF16)] * (PLANE - 1), [pltpu.VMEM(part, F32)],

time: 59.7 us -> 59.4 us (level)
  no operation moved by 1% of the time
where the time goes in v16:
time: 59.4 us; the launch traced here: 59.2 us
  starting transfers between devices  23 us (39%)
  Pallas kernels  17.3 us (29%)
  waiting for transfers between devices  14.7 us (25%)
  local copies, waits for them, and re-layouts  3.42 us (6%)
  between operations  0.81 us (1%)
    ppermute x21, starting transfers between devices, move(): return lax.ppermute(values, 'fsdp', pairs)  23 us
    pallas_call x13, Pallas kernels, call(): pl.pallas_call(kernel, in_specs=[SMEM_SPEC] * with_ids + [VMEM_SPEC] * le...  17.3 us
    ppermute x21, waiting for transfers between devices, move(): return lax.ppermute(values, 'fsdp', pairs)  14.7 us
    unnamed x14, local copies, waits for them, and re-layouts  3.33 us
  transfers between devices with their start and end apart: 21, of which 10 were waited for; matrix products, arithmetic and copies ran while one was open for 0% of the time, Pallas kernels for 17%

profile of v16, /device:TPU:0, one launch (start us, length us, event | category | flops | bytes accessed | tf_op | source)
XLA Modules:
  0.0 59.2 jit_solution(14731618003306110342)
XLA Ops:
  0.6 3.1 %collective-permute-start = (bf16[193,128]{1,0:T(8,128)(2,1)}, bf16[193,128]{1,0:T(8,128)(2,1)S(1)}, u32[]{:S(2)}, u32[]{:S(2)}) collective-permute-start(bf16[193,128]{1,0:T(8,128)(2,1)} %params.1), channel_id=1, source_target_pairs={{0,8},{1,9},{2,10},{3,11},{4,12},{5,13},{6,14},{7,15},{8,16},{9,17... | collective-permute-start | bytes 148232 | tf_op jit(solution)/shard_map/ppermute | solution.py:564
  3.7 2.6 %collective-permute-start.1 = (bf16[193,128]{1,0:T(8,128)(2,1)}, bf16[193,128]{1,0:T(8,128)(2,1)S(1)}, u32[]{:S(2)}, u32[]{:S(2)}) collective-permute-start(bf16[193,128]{1,0:T(8,128)(2,1)} %params.1), channel_id=1, source_target_pairs={{0,16},{1,17},{2,18},{3,19},{4,20},{5,21},{6,22},{7,23},{8,24},{9,... | collective-permute-start | bytes 148232 | tf_op jit(solution)/shard_map/ppermute | solution.py:564
  6.3 1.3 %collective-permute-start.2 = (bf16[193,128]{1,0:T(8,128)(2,1)}, bf16[193,128]{1,0:T(8,128)(2,1)S(1)}, u32[]{:S(2)}, u32[]{:S(2)}) collective-permute-start(bf16[193,128]{1,0:T(8,128)(2,1)} %params.1), channel_id=1, source_target_pairs={{0,24},{1,25},{2,26},{3,27},{4,28},{5,29},{6,30},{7,31},{8,0},{9,1... | collective-permute-start | bytes 148232 | tf_op jit(solution)/shard_map/ppermute | solution.py:564
  7.6 1.0 %copy-done.1 = bf16[1024,256]{1,0:T(8,128)(2,1)S(1)} copy-done((bf16[1024,256]{1,0:T(8,128)(2,1)S(1)}, bf16[1024,256]{1,0:T(8,128)(2,1)}, u32[]{:S(2)}) %copy-start.1) | copy-done | bytes 524312
  8.7 0.8 %copy-done.3 = bf16[193,128]{1,0:T(8,128)(2,1)S(1)} copy-done((bf16[193,128]{1,0:T(8,128)(2,1)S(1)}, bf16[193,128]{1,0:T(8,128)(2,1)}, u32[]{:S(2)}) %copy-start.3) | copy-done | bytes 49432
  9.5 0.7 %copy-done.4 = s32[1024]{0:T(1024)S(1)} copy-done((s32[1024]{0:T(1024)S(1)}, s32[1024]{0:T(1024)}, u32[]{:S(2)}) %copy-start.4) | copy-done | bytes 4120
  10.2 0.7 %prepare.1 = (f32[1024,256]{1,0:T(8,128)S(1)}, bf16[256,1024]{1,0:T(8,128)(2,1)S(1)}, bf16[193,128]{1,0:T(8,128)(2,1)S(1)}, f32[1024,128]{1,0:T(8,128)S(1)}) custom-call(bf16[1024,256]{1,0:T(8,128)(2,1)S(1)} %copy-done.1, bf16[193,128]{1,0:T(8,128)(2,1)S(1)} %copy-done.3, s32[8,128]{1,0:T(8,128)S(1)} %bitcast.10), custom_call_target="tpu_custom_call" | custom-call | flops 2000000000 | bytes 1048576 | tf_op jit(solution)/shard_map/prepare/pallas_call | solution.py:419
  10.9 0.0 copy-start.5
  10.9 0.8 %copy-done.5 = bf16[256,1024]{1,0:T(8,128)(2,1)} copy-done((bf16[256,1024]{1,0:T(8,128)(2,1)}, bf16[256,1024]{1,0:T(8,128)(2,1)S(1)}, u32[]{:S(2)}) %copy-start.5) | copy-done | bytes 524312
  11.7 0.1 sort_shares.1
  11.7 2.5 %collective-permute-start.6 = (bf16[1,240,128]{2,1,0:T(8,128)(2,1)S(1)}, bf16[1,240,128]{2,1,0:T(8,128)(2,1)S(1)}, u32[]{:S(2)}, u32[]{:S(2)}) collective-permute-start(bf16[1,240,128]{2,1,0:T(8,128)(2,1)S(1)} %get-tuple-element.42.refs_0_), channel_id=1, source_target_pairs={{0,6},{1,7},{2,4},{3,5},{4,2},{5,3},{6,0},{7,1},{8,14},{9,15},{10,... | collective-permute-start | bytes 184328 | tf_op jit(solution)/shard_map/ppermute | solution.py:564
  14.2 0.5 collective-permute-start.7
  14.8 0.5 collective-permute-start.8
  15.3 2.4 %collective-permute-start.3 = (bf16[3,193,128]{2,1,0:T(8,128)(2,1)S(1)}, bf16[3,193,128]{2,1,0:T(8,128)(2,1)S(1)}, u32[]{:S(2)}, u32[]{:S(2)}) collective-permute-start(bf16[3,193,128]{2,1,0:T(8,128)(2,1)S(1)} %get-tuple-element.39.refs_0_), channel_id=1, source_target_pairs={{0,6},{1,7},{2,4},{3,5},{4,2},{5,3},{6,0},{7,1},{8,14},{9,15},{10,... | collective-permute-start | bytes 444680 | tf_op jit(solution)/shard_map/ppermute | solution.py:564
  17.7 0.5 collective-permute-start.4
  18.3 0.5 collective-permute-start.5
  18.8 0.3 collective-permute-done.7.refs_0_
  19.1 1.4 %collective-permute-done.8.refs_1_ = bf16[1,240,128]{2,1,0:T(8,128)(2,1)S(1)} collective-permute-done((bf16[1,240,128]{2,1,0:T(8,128)(2,1)S(1)}, bf16[1,240,128]{2,1,0:T(8,128)(2,1)S(1)}, u32[]{:S(2)}, u32[]{:S(2)}) %collective-permute-start.8) | collective-permute-done | bytes 61472 | tf_op jit(solution)/shard_map/ppermute | solution.py:564
  20.5 0.0 copy-start
  20.5 0.1 collective-permute-start.10
  20.7 0.1 stack.38.ids
  20.8 1.2 %collective-permute-done.10.refs_3_ = bf16[2,240,128]{2,1,0:T(8,128)(2,1)S(1)} collective-permute-done((bf16[2,240,128]{2,1,0:T(8,128)(2,1)S(1)}, bf16[2,240,128]{2,1,0:T(8,128)(2,1)S(1)}, u32[]{:S(2)}, u32[]{:S(2)}) %collective-permute-start.10) | collective-permute-done | bytes 122912 | tf_op jit(solution)/shard_map/ppermute | solution.py:564
  21.9 2.6 %attend.1 = (bf16[1024,768]{1,0:T(8,128)(2,1)S(1)}, bf16[1024,512]{1,0:T(8,128)(2,1)S(1)}, bf16[1024,256]{1,0:T(8,128)(2,1)S(1)}, bf16[256,768]{1,0:T(8,128)(2,1...) custom-call(s32[8]{0:T(128)S(1)} %stack.38.ids, f32[1024,128]{1,0:T(8,128)S(1)} %get-tuple-element.40.allowed, ...), custom_call_target="tpu_custom_call" | custom-call | flops 10000000 | bytes 1048576 | tf_op jit(solution)/shard_map/attend/pallas_call | solution.py:419
  24.6 0.2 collective-permute-start.12
  24.9 0.4 collective-permute-start.11
  25.2 1.5 %collective-permute-done.11.refs_2_ = bf16[3,193,128]{2,1,0:T(8,128)(2,1)S(1)} collective-permute-done((bf16[3,193,128]{2,1,0:T(8,128)(2,1)S(1)}, bf16[3,193,128]{2,1,0:T(8,128)(2,1)S(1)}, u32[]{:S(2)}, u32[]{:S(2)}) %collective-permute-start.11) | collective-permute-done | bytes 148256 | tf_op jit(solution)/shard_map/ppermute | solution.py:564
  26.8 0.0 copy-start.6
  26.8 6.2 %feed.1 = (f32[1024,256]{1,0:T(8,128)S(1)}, bf16[1024,1024]{1,0:T(8,128)(2,1)S(1)}, f32[1024,256]{1,0:T(8,128)S(1)}, bf16[1024,256]{1,0:T(8,128)(2,1)S(1)}, bf16...) custom-call(s32[8]{0:T(128)S(1)} %stack.38.ids, ...), custom_call_target="tpu_custom_call" | custom-call | flops 8000000000 | bytes 1048576 | tf_op jit(solution)/shard_map/feed/pallas_call | solution.py:419
  33.0 0.2 collective-permute-start.14
  33.2 3.1 %attend_back.1 = (bf16[1024,768]{1,0:T(8,128)(2,1)S(1)}, f32[4,224,128]{2,1,0:T(8,128)S(1)}, bf16[4,224,128]{2,1,0:T(8,128)(2,1)S(1)}) custom-call(s32[8]{0:T(128)S(1)} %stack.38.ids, bf16[1024,768]{1,0:T(8,128)(2,1)S(1)} %get-tuple-element.53.project, bf16[1024,512]{1,0:T(8,128)(2,1)S(1)} %get-tuple-element.54.weights, ...), custom_call_target="tpu_custom_call" | custom-call | flops 4000000000 | bytes 1048576 | tf_op jit(solution)/shard_map/attend_back/pallas_call | solution.py:419
  36.3 0.4 collective-permute-start.13
  36.7 1.1 %collective-permute-done.13.first_in = bf16[4,224,128]{2,1,0:T(8,128)(2,1)S(1)} collective-permute-done((bf16[4,224,128]{2,1,0:T(8,128)(2,1)S(1)}, bf16[4,224,128]{2,1,0:T(8,128)(2,1)S(1)}, u32[]{:S(2)}, u32[]{:S(2)}) %collective-permute-start.13) | collective-permute-done | bytes 229408 | tf_op jit(solution)/shard_map/ppermute | solution.py:564
  37.8 0.2 add_core.1
  38.1 2.2 %collective-permute-start.15 = (bf16[772,128]{1,0:T(8,128)(2,1)S(1)}, bf16[772,128]{1,0:T(8,128)(2,1)S(1)}, u32[]{:S(2)}, u32[]{:S(2)}) collective-permute-start(bf16[772,128]{1,0:T(8,128)(2,1)S(1)} %get-tuple-element.66), channel_id=1, source_target_pairs={{0,6},{1,7},{2,4},{3,5},{4,2},{5,3},{6,0},{7,1},{8,14},{9,15},{10,... | collective-permute-start | bytes 592904 | tf_op jit(solution)/shard_map/ppermute | solution.py:564
  40.3 0.4 collective-permute-start.16
  40.7 1.1 %collective-permute-start.17 = (bf16[772,128]{1,0:T(8,128)(2,1)S(1)}, bf16[772,128]{1,0:T(8,128)(2,1)S(1)}, u32[]{:S(2)}, u32[]{:S(2)}) collective-permute-start(bf16[772,128]{1,0:T(8,128)(2,1)S(1)} %get-tuple-element.68), channel_id=1, source_target_pairs={{0,4},{1,5},{2,6},{3,7},{4,0},{5,1},{6,2},{7,3},{8,12},{9,13},{10,... | collective-permute-start | bytes 592904 | tf_op jit(solution)/shard_map/ppermute | solution.py:564
  41.8 2.0 %input_grad.1 = f32[1024,256]{1,0:T(8,128)} custom-call(bf16[1024,256]{1,0:T(8,128)(2,1)S(1)} %copy-done.2, bf16[1024,768]{1,0:T(8,128)(2,1)S(1)} %get-tuple-element.59.grad_project, f32[1024,256]{1,0:T(8,128)S(1)} %get-tuple-element.60.grad_middle, bf16[256,768]{1,0:T(8,128)(2,1)S(1)} %get-tuple-element.57.w_qkv, f32[32,128]{1,0:T(8,128)S(1)} %get-tuple-element.45.small), custom_call_target="tpu_custom_call" | custom-call | flops 2000000000 | bytes 1048576 | tf_op jit(solution)/shard_map/input_grad/pallas_call | solution.py:419
  43.8 3.0 %collective-permute-done.15.refs_0_ = bf16[772,128]{1,0:T(8,128)(2,1)S(1)} collective-permute-done((bf16[772,128]{1,0:T(8,128)(2,1)S(1)}, bf16[772,128]{1,0:T(8,128)(2,1)S(1)}, u32[]{:S(2)}, u32[]{:S(2)}) %collective-permute-start.15) | collective-permute-done | bytes 197664 | tf_op jit(solution)/shard_map/ppermute | solution.py:564
  46.9 3.3 %collective-permute-done.16.refs_1_ = bf16[772,128]{1,0:T(8,128)(2,1)S(1)} collective-permute-done((bf16[772,128]{1,0:T(8,128)(2,1)S(1)}, bf16[772,128]{1,0:T(8,128)(2,1)S(1)}, u32[]{:S(2)}, u32[]{:S(2)}) %collective-permute-start.16) | collective-permute-done | bytes 197664 | tf_op jit(solution)/shard_map/ppermute | solution.py:564
  50.2 0.4 collective-permute-done.17.refs_2_
  50.5 0.2 add_plane.1
  50.7 0.8 %collective-permute-start.18 = (bf16[193,128]{1,0:T(8,128)(2,1)S(1)}, bf16[193,128]{1,0:T(8,128)(2,1)S(1)}, u32[]{:S(2)}, u32[]{:S(2)}) collective-permute-start(bf16[193,128]{1,0:T(8,128)(2,1)S(1)} %get-tuple-element.70), channel_id=1, source_target_pairs={{0,8},{1,9},{2,10},{3,11},{4,12},{5,13},{6,14},{7,15},{8,16},{9,17... | collective-permute-start | bytes 148232 | tf_op jit(solution)/shard_map/ppermute | solution.py:564
  51.5 1.9 %collective-permute-start.19 = (bf16[193,128]{1,0:T(8,128)(2,1)S(1)}, bf16[193,128]{1,0:T(8,128)(2,1)S(1)}, u32[]{:S(2)}, u32[]{:S(2)}) collective-permute-start(bf16[193,128]{1,0:T(8,128)(2,1)S(1)} %get-tuple-element.71), channel_id=1, source_target_pairs={{0,16},{1,17},{2,18},{3,19},{4,20},{5,21},{6,22},{7,23},{8,24},{9,... | collective-permute-start | bytes 148232 | tf_op jit(solution)/shard_map/ppermute | solution.py:564
  53.4 1.2 %collective-permute-start.20 = (bf16[193,128]{1,0:T(8,128)(2,1)S(1)}, bf16[193,128]{1,0:T(8,128)(2,1)S(1)}, u32[]{:S(2)}, u32[]{:S(2)}) collective-permute-start(bf16[193,128]{1,0:T(8,128)(2,1)S(1)} %get-tuple-element.72), channel_id=1, source_target_pairs={{0,24},{1,25},{2,26},{3,27},{4,28},{5,29},{6,30},{7,31},{8,0},{9,1... | collective-permute-start | bytes 148232 | tf_op jit(solution)/shard_map/ppermute | solution.py:564
  54.6 1.5 %result.1 = bf16[1024,256]{1,0:T(8,128)(2,1)} custom-call(f32[1024,256]{1,0:T(8,128)S(1)} %get-tuple-element.50.middle, bf16[1024,1024]{1,0:T(8,128)(2,1)S(1)} %get-tuple-element.51.activated, bf16[1024,256]{1,0:T(8,128)(2,1)S(1)} %get-tuple-element.52.w_down, f32[32,128]{1,0:T(8,128)S(1)} %get-tuple-element.45.small), custom_call_target="tpu_custom_call" | custom-call | flops 2000000000 | bytes 1048576 | tf_op jit(solution)/shard_map/result/pallas_call | solution.py:419
  56.1 1.1 %collective-permute-done.18.refs_0_ = bf16[193,128]{1,0:T(8,128)(2,1)S(1)} collective-permute-done((bf16[193,128]{1,0:T(8,128)(2,1)S(1)}, bf16[193,128]{1,0:T(8,128)(2,1)S(1)}, u32[]{:S(2)}, u32[]{:S(2)}) %collective-permute-start.18) | collective-permute-done | bytes 49440 | tf_op jit(solution)/shard_map/ppermute | solution.py:564
  57.2 1.3 %collective-permute-done.19.refs_1_ = bf16[193,128]{1,0:T(8,128)(2,1)S(1)} collective-permute-done((bf16[193,128]{1,0:T(8,128)(2,1)S(1)}, bf16[193,128]{1,0:T(8,128)(2,1)S(1)}, u32[]{:S(2)}, u32[]{:S(2)}) %collective-permute-start.19) | collective-permute-done | bytes 49440 | tf_op jit(solution)/shard_map/ppermute | solution.py:564
  58.5 0.7 %add_column.1 = f32[193,128]{1,0:T(8,128)} custom-call(f32[193,128]{1,0:T(8,128)S(1)} %get-tuple-element.69.kept, bf16[193,128]{1,0:T(8,128)(2,1)S(1)} %collective-permute-done.18.refs_0_, bf16[193,128]{1,0:T(8,128)(2,1)S(1)} %collective-permute-done.19.refs_1_, bf16[193,128]{1,0:T(8,128)(2,1)S(1)} %collective-permute-done.20.refs_2_), custom_call_target="tpu_custom_call" | custom-call | flops 1000000000 | bytes 1048576 | tf_op jit(solution)/shard_map/add_column/pallas_call | solution.py:419
  (22 shorter events, 0.1 us)
Async XLA Ops:
  0.6 11.0 %collective-permute-start = (bf16[193,128]{1,0:T(8,128)(2,1)}, bf16[193,128]{1,0:T(8,128)(2,1)S(1)}, u32[]{:S(2)}, u32[]{:S(2)}) collective-permute-start(bf16[193,128]{1,0:T(8,128)(2,1)} %params.1), channel_id=1, source_target_pairs={{0,8},{1,9},{2,10},{3,11},{4,12},{5,13},{6,14},{7,15},{8,16},{9,17... | collective-permute-start | bytes 148232 | tf_op jit(solution)/shard_map/ppermute | solution.py:564
  3.7 8.0 %collective-permute-start.1 = (bf16[193,128]{1,0:T(8,128)(2,1)}, bf16[193,128]{1,0:T(8,128)(2,1)S(1)}, u32[]{:S(2)}, u32[]{:S(2)}) collective-permute-start(bf16[193,128]{1,0:T(8,128)(2,1)} %params.1), channel_id=1, source_target_pairs={{0,16},{1,17},{2,18},{3,19},{4,20},{5,21},{6,22},{7,23},{8,24},{9,... | collective-permute-start | bytes 148232 | tf_op jit(solution)/shard_map/ppermute | solution.py:564
  6.3 5.4 %collective-permute-start.2 = (bf16[193,128]{1,0:T(8,128)(2,1)}, bf16[193,128]{1,0:T(8,128)(2,1)S(1)}, u32[]{:S(2)}, u32[]{:S(2)}) collective-permute-start(bf16[193,128]{1,0:T(8,128)(2,1)} %params.1), channel_id=1, source_target_pairs={{0,24},{1,25},{2,26},{3,27},{4,28},{5,29},{6,30},{7,31},{8,0},{9,1... | collective-permute-start | bytes 148232 | tf_op jit(solution)/shard_map/ppermute | solution.py:564
  7.6 1.0 %copy-start.1 = (bf16[1024,256]{1,0:T(8,128)(2,1)S(1)}, bf16[1024,256]{1,0:T(8,128)(2,1)}, u32[]{:S(2)}) copy-start(bf16[1024,256]{1,0:T(8,128)(2,1)} %tok.5) | copy-start | bytes 1572868
  8.7 0.8 %copy-start.3 = (bf16[193,128]{1,0:T(8,128)(2,1)S(1)}, bf16[193,128]{1,0:T(8,128)(2,1)}, u32[]{:S(2)}) copy-start(bf16[193,128]{1,0:T(8,128)(2,1)} %params.1) | copy-start | bytes 148228
  9.5 0.7 %copy-start.4 = (s32[1024]{0:T(1024)S(1)}, s32[1024]{0:T(1024)}, u32[]{:S(2)}) copy-start(s32[1024]{0:T(1024)} %param.6) | copy-start | bytes 12292
  10.9 0.8 %copy-start.5 = (bf16[256,1024]{1,0:T(8,128)(2,1)}, bf16[256,1024]{1,0:T(8,128)(2,1)S(1)}, u32[]{:S(2)}) copy-start(bf16[256,1024]{1,0:T(8,128)(2,1)S(1)} %get-tuple-element.56.normed_turned) | copy-start | bytes 1572868
  11.7 6.5 %collective-permute-start.6 = (bf16[1,240,128]{2,1,0:T(8,128)(2,1)S(1)}, bf16[1,240,128]{2,1,0:T(8,128)(2,1)S(1)}, u32[]{:S(2)}, u32[]{:S(2)}) collective-permute-start(bf16[1,240,128]{2,1,0:T(8,128)(2,1)S(1)} %get-tuple-element.42.refs_0_), channel_id=1, source_target_pairs={{0,6},{1,7},{2,4},{3,5},{4,2},{5,3},{6,0},{7,1},{8,14},{9,15},{10,... | collective-permute-start | bytes 184328 | tf_op jit(solution)/shard_map/ppermute | solution.py:564
  14.2 4.8 %collective-permute-start.7 = (bf16[1,240,128]{2,1,0:T(8,128)(2,1)S(1)}, bf16[1,240,128]{2,1,0:T(8,128)(2,1)S(1)}, u32[]{:S(2)}, u32[]{:S(2)}) collective-permute-start(bf16[1,240,128]{2,1,0:T(8,128)(2,1)S(1)} %get-tuple-element.42.refs_0_), channel_id=1, source_target_pairs={{0,2},{1,3},{2,0},{3,1},{4,6},{5,7},{6,4},{7,5},{8,10},{9,11},{10,... | collective-permute-start | bytes 184328 | tf_op jit(solution)/shard_map/ppermute | solution.py:564
  14.8 5.8 %collective-permute-start.8 = (bf16[1,240,128]{2,1,0:T(8,128)(2,1)S(1)}, bf16[1,240,128]{2,1,0:T(8,128)(2,1)S(1)}, u32[]{:S(2)}, u32[]{:S(2)}) collective-permute-start(bf16[1,240,128]{2,1,0:T(8,128)(2,1)S(1)} %get-tuple-element.42.refs_0_), channel_id=1, source_target_pairs={{0,4},{1,5},{2,6},{3,7},{4,0},{5,1},{6,2},{7,3},{8,12},{9,13},{10,... | collective-permute-start | bytes 184328 | tf_op jit(solution)/shard_map/ppermute | solution.py:564
  15.3 9.3 %collective-permute-start.3 = (bf16[3,193,128]{2,1,0:T(8,128)(2,1)S(1)}, bf16[3,193,128]{2,1,0:T(8,128)(2,1)S(1)}, u32[]{:S(2)}, u32[]{:S(2)}) collective-permute-start(bf16[3,193,128]{2,1,0:T(8,128)(2,1)S(1)} %get-tuple-element.39.refs_0_), channel_id=1, source_target_pairs={{0,6},{1,7},{2,4},{3,5},{4,2},{5,3},{6,0},{7,1},{8,14},{9,15},{10,... | collective-permute-start | bytes 444680 | tf_op jit(solution)/shard_map/ppermute | solution.py:564
  17.7 6.9 %collective-permute-start.4 = (bf16[3,193,128]{2,1,0:T(8,128)(2,1)S(1)}, bf16[3,193,128]{2,1,0:T(8,128)(2,1)S(1)}, u32[]{:S(2)}, u32[]{:S(2)}) collective-permute-start(bf16[3,193,128]{2,1,0:T(8,128)(2,1)S(1)} %get-tuple-element.39.refs_0_), channel_id=1, source_target_pairs={{0,2},{1,3},{2,0},{3,1},{4,6},{5,7},{6,4},{7,5},{8,10},{9,11},{10,... | collective-permute-start | bytes 444680 | tf_op jit(solution)/shard_map/ppermute | solution.py:564
  18.3 6.3 %collective-permute-start.5 = (bf16[3,193,128]{2,1,0:T(8,128)(2,1)S(1)}, bf16[3,193,128]{2,1,0:T(8,128)(2,1)S(1)}, u32[]{:S(2)}, u32[]{:S(2)}) collective-permute-start(bf16[3,193,128]{2,1,0:T(8,128)(2,1)S(1)} %get-tuple-element.39.refs_0_), channel_id=1, source_target_pairs={{0,4},{1,5},{2,6},{3,7},{4,0},{5,1},{6,2},{7,3},{8,12},{9,13},{10,... | collective-permute-start | bytes 444680 | tf_op jit(solution)/shard_map/ppermute | solution.py:564
  19.1 1.7 %collective-permute-start.9 = (bf16[2,240,128]{2,1,0:T(8,128)(2,1)S(1)}, bf16[2,240,128]{2,1,0:T(8,128)(2,1)S(1)}, u32[]{:S(2)}, u32[]{:S(2)}) collective-permute-start(bf16[2,240,128]{2,1,0:T(8,128)(2,1)S(1)} %stack.39.refs_0_), channel_id=1, source_target_pairs={{0,1},{1,0},{2,3},{3,2},{4,5},{5,4},{6,7},{7,6},{8,9},{9,8},{10,11... | collective-permute-start | bytes 368648 | tf_op jit(solution)/shard_map/ppermute | solution.py:564
  20.5 6.2 %copy-start = (bf16[1024,256]{1,0:T(8,128)(2,1)S(1)}, bf16[1024,256]{1,0:T(8,128)(2,1)}, u32[]{:S(2)}) copy-start(bf16[1024,256]{1,0:T(8,128)(2,1)} %cot.1) | copy-start | bytes 1572868
  20.5 1.4 %collective-permute-start.10 = (bf16[2,240,128]{2,1,0:T(8,128)(2,1)S(1)}, bf16[2,240,128]{2,1,0:T(8,128)(2,1)S(1)}, u32[]{:S(2)}, u32[]{:S(2)}) collective-permute-start(bf16[2,240,128]{2,1,0:T(8,128)(2,1)S(1)} %stack.40.refs_1_), channel_id=1, source_target_pairs={{0,1},{1,0},{2,3},{3,2},{4,5},{5,4},{6,7},{7,6},{8,9},{9,8},{10,11... | collective-permute-start | bytes 368648 | tf_op jit(solution)/shard_map/ppermute | solution.py:564
  20.8 6.0 %copy-start.2 = (bf16[1024,256]{1,0:T(8,128)(2,1)S(1)}, bf16[1024,256]{1,0:T(8,128)(2,1)}, u32[]{:S(2)}) copy-start(bf16[1024,256]{1,0:T(8,128)(2,1)} %tok.5) | copy-start | bytes 1572868
  24.6 2.1 %collective-permute-start.12 = (bf16[9,193,128]{2,1,0:T(8,128)(2,1)S(1)}, bf16[9,193,128]{2,1,0:T(8,128)(2,1)S(1)}, u32[]{:S(2)}, u32[]{:S(2)}) collective-permute-start(bf16[9,193,128]{2,1,0:T(8,128)(2,1)S(1)} %stack.41.refs_1_), channel_id=1, source_target_pairs={{0,1},{1,0},{2,3},{3,2},{4,5},{5,4},{6,7},{7,6},{8,9},{9,8},{10,11... | collective-permute-start | bytes 1334024 | tf_op jit(solution)/shard_map/ppermute | solution.py:564
  24.9 1.9 %collective-permute-start.11 = (bf16[3,193,128]{2,1,0:T(8,128)(2,1)S(1)}, bf16[3,193,128]{2,1,0:T(8,128)(2,1)S(1)}, u32[]{:S(2)}, u32[]{:S(2)}) collective-permute-start(bf16[3,193,128]{2,1,0:T(8,128)(2,1)S(1)} %get-tuple-element.39.refs_0_), channel_id=1, source_target_pairs={{0,1},{1,0},{2,3},{3,2},{4,5},{5,4},{6,7},{7,6},{8,9},{9,8},{10,11... | collective-permute-start | bytes 444680 | tf_op jit(solution)/shard_map/ppermute | solution.py:564
  26.8 6.4 %copy-start.6 = (bf16[256,1024]{1,0:T(8,128)(2,1)S(1)}, bf16[256,1024]{1,0:T(8,128)(2,1)}, u32[]{:S(2)}) copy-start(bf16[256,1024]{1,0:T(8,128)(2,1)} %copy-done.5) | copy-start | bytes 1572868
  33.0 4.9 %collective-permute-start.14 = (bf16[12,193,128]{2,1,0:T(8,128)(2,1)S(1)}, bf16[12,193,128]{2,1,0:T(8,128)(2,1)S(1)}, u32[]{:S(2)}, u32[]{:S(2)}) collective-permute-start(bf16[12,193,128]{2,1,0:T(8,128)(2,1)S(1)} %get-tuple-element.64), channel_id=1, source_target_pairs={{0,1},{1,0},{2,3},{3,2},{4,5},{5,4},{6,7},{7,6},{8,9},{9,8},{10,11... | collective-permute-start | bytes 1778696 | tf_op jit(solution)/shard_map/ppermute | solution.py:564
  36.3 1.6 %collective-permute-start.13 = (bf16[4,224,128]{2,1,0:T(8,128)(2,1)S(1)}, bf16[4,224,128]{2,1,0:T(8,128)(2,1)S(1)}, u32[]{:S(2)}, u32[]{:S(2)}) collective-permute-start(bf16[4,224,128]{2,1,0:T(8,128)(2,1)S(1)} %get-tuple-element.62), channel_id=1, source_target_pairs={{0,1},{1,0},{2,3},{3,2},{4,5},{5,4},{6,7},{7,6},{8,9},{9,8},{10,11... | collective-permute-start | bytes 688136 | tf_op jit(solution)/shard_map/ppermute | solution.py:564
  38.1 8.8 %collective-permute-start.15 = (bf16[772,128]{1,0:T(8,128)(2,1)S(1)}, bf16[772,128]{1,0:T(8,128)(2,1)S(1)}, u32[]{:S(2)}, u32[]{:S(2)}) collective-permute-start(bf16[772,128]{1,0:T(8,128)(2,1)S(1)} %get-tuple-element.66), channel_id=1, source_target_pairs={{0,6},{1,7},{2,4},{3,5},{4,2},{5,3},{6,0},{7,1},{8,14},{9,15},{10,... | collective-permute-start | bytes 592904 | tf_op jit(solution)/shard_map/ppermute | solution.py:564
  40.3 9.8 %collective-permute-start.16 = (bf16[772,128]{1,0:T(8,128)(2,1)S(1)}, bf16[772,128]{1,0:T(8,128)(2,1)S(1)}, u32[]{:S(2)}, u32[]{:S(2)}) collective-permute-start(bf16[772,128]{1,0:T(8,128)(2,1)S(1)} %get-tuple-element.67), channel_id=1, source_target_pairs={{0,2},{1,3},{2,0},{3,1},{4,6},{5,7},{6,4},{7,5},{8,10},{9,11},{10,... | collective-permute-start | bytes 592904 | tf_op jit(solution)/shard_map/ppermute | solution.py:564
  40.7 9.8 %collective-permute-start.17 = (bf16[772,128]{1,0:T(8,128)(2,1)S(1)}, bf16[772,128]{1,0:T(8,128)(2,1)S(1)}, u32[]{:S(2)}, u32[]{:S(2)}) collective-permute-start(bf16[772,128]{1,0:T(8,128)(2,1)S(1)} %get-tuple-element.68), channel_id=1, source_target_pairs={{0,4},{1,5},{2,6},{3,7},{4,0},{5,1},{6,2},{7,3},{8,12},{9,13},{10,... | collective-permute-start | bytes 592904 | tf_op jit(solution)/shard_map/ppermute | solution.py:564
  50.7 6.5 %collective-permute-start.18 = (bf16[193,128]{1,0:T(8,128)(2,1)S(1)}, bf16[193,128]{1,0:T(8,128)(2,1)S(1)}, u32[]{:S(2)}, u32[]{:S(2)}) collective-permute-start(bf16[193,128]{1,0:T(8,128)(2,1)S(1)} %get-tuple-element.70), channel_id=1, source_target_pairs={{0,8},{1,9},{2,10},{3,11},{4,12},{5,13},{6,14},{7,15},{8,16},{9,17... | collective-permute-start | bytes 148232 | tf_op jit(solution)/shard_map/ppermute | solution.py:564
  51.5 7.0 %collective-permute-start.19 = (bf16[193,128]{1,0:T(8,128)(2,1)S(1)}, bf16[193,128]{1,0:T(8,128)(2,1)S(1)}, u32[]{:S(2)}, u32[]{:S(2)}) collective-permute-start(bf16[193,128]{1,0:T(8,128)(2,1)S(1)} %get-tuple-element.71), channel_id=1, source_target_pairs={{0,16},{1,17},{2,18},{3,19},{4,20},{5,21},{6,22},{7,23},{8,24},{9,... | collective-permute-start | bytes 148232 | tf_op jit(solution)/shard_map/ppermute | solution.py:564
  53.4 5.1 %collective-permute-start.20 = (bf16[193,128]{1,0:T(8,128)(2,1)S(1)}, bf16[193,128]{1,0:T(8,128)(2,1)S(1)}, u32[]{:S(2)}, u32[]{:S(2)}) collective-permute-start(bf16[193,128]{1,0:T(8,128)(2,1)S(1)} %get-tuple-element.72), channel_id=1, source_target_pairs={{0,24},{1,25},{2,26},{3,27},{4,28},{5,29},{6,30},{7,31},{8,0},{9,1... | collective-permute-start | bytes 148232 | tf_op jit(solution)/shard_map/ppermute | solution.py:564

commit v17 on v15

--- a/solution.py
+++ b/solution.py
@@ -39,6 +39,7 @@
 HEAD_ROWS = FIRST_ROWS - ROW_OUT
 SIDE, SIDE_ROWS = 208, 16
 FIRST_GROUPS = ((0, 2), (2, 4))
+DIAGONAL_ROWS = SIDE + SMALL_ROWS + (Z - 1) * SIDE
 SMALL_IN_SHARE = ROW_SMALL - (2 * PLANE * Z - 1) * SHARE
 
 F32 = jnp.float32
@@ -118,7 +119,7 @@
 
 
 def sort_kernel(ids, *refs):
-    received, (first, rest, stage, wide) = refs[:Z], refs[Z:]
+    received, (first, rest, both, stage, wide) = refs[:Z], refs[Z:]
     for d in range(Z):
         stage[lax.rem(ids[0] + Z - d, Z)] = received[d][...]
     rest[...] = stage[1:]
@@ -127,6 +128,11 @@
     last = stage[Z - 1].astype(F32)
     wide[SIDE:, :] = last[SMALL_IN_SHARE:, :]
     first[0] = wide[...].astype(BF16)
+    both[: SIDE + SMALL_ROWS, :] = wide[...].astype(BF16)
+    for z in range(1, Z):
+        wide[:SHARE, :] = stage[z].astype(F32)
+        row = SIDE + SMALL_ROWS + (z - 1) * SIDE
+        both[row : row + SIDE, :] = wide[:SIDE, :].astype(BF16)
 
 
 def attend_kernel(ids, allowed, normed, *refs):
@@ -370,6 +376,20 @@
     lax.fori_loop(0, tok.shape[0] // WIDE, some, 0)
 
 
+def stack_first_kernel(own, both, out):
+    out[0] = own[0]
+    out[1] = both[: SIDE + SMALL_ROWS, :]
+
+
+def stack_rest_kernel(both, *refs):
+    others, out = refs[:-1], refs[-1]
+    for z in range(Z - 1):
+        row = SIDE + SMALL_ROWS + z * SIDE
+        out[z] = both[row : row + SIDE, :].astype(F32)[:SHARE, :].astype(BF16)
+    for i, item in enumerate(others, 1):
+        out[i * (Z - 1) : (i + 1) * (Z - 1)] = item[...]
+
+
 def stack_kernel(*refs):
     row = 0
     for ref in refs[:-1]:
@@ -575,18 +595,28 @@
     )
 
     normed, normed_turned, own, allowed = prepare(tokens, params, segment_ids)
-    first, rest = call(
+    first, rest, both = call(
         sort_kernel, "sort_shares", where, [own] + [move(params, d, 0, 0) for d in range(1, Z)],
-        [like(1, SIDE + SMALL_ROWS, LANES, kind=BF16), like(Z - 1, SHARE, LANES, kind=BF16)],
+        [like(1, SIDE + SMALL_ROWS, LANES, kind=BF16), like(Z - 1, SHARE, LANES, kind=BF16), like(DIAGONAL_ROWS, LANES, kind=BF16)],
         [pltpu.VMEM((Z, SHARE, LANES), BF16), pltpu.VMEM((SIDE + SMALL_ROWS, LANES), F32)],
     )
-    firsts = [first] + [move(first, 0, d, 0) for d in STEPS]
-    rests = [move(rest, 0, d, 0) for d in STEPS]
-    firsts = [stack(firsts[i:j]) if j > i + 1 else firsts[i] for i, j in FIRST_GROUPS]
+    both = move(both, 0, STEPS[0], 0)
+    firsts = [move(first, 0, d, 0) for d in STEPS[1:]]
+    rests = [move(rest, 0, d, 0) for d in STEPS[1:]]
+    firsts = [
+        call(
+            stack_first_kernel, "stack_first", None, [first, both],
+            [like(2, SIDE + SMALL_ROWS, LANES, kind=BF16)], us=0.01,
+        ),
+        stack(firsts),
+    ]
     firsts = firsts + [move(item, 0, 0, 1) for item in firsts]
     project, weights, attended, w_qkv, small, first = attend(ids, allowed, normed, firsts)
     *rests, attended = lax.optimization_barrier((*rests, attended))
-    rests = stack(rests)
+    rests = call(
+        stack_rest_kernel, "stack_rest", None, [both, *rests],
+        [like((PLANE - 1) * (Z - 1), SHARE, LANES, kind=BF16)], us=0.01,
+    )
     rests = [rest, rests, move(rest, 0, 0, 1), move(rests, 0, 0, 1)]
     middle, activated, grad_middle, grad_attended, w_down, rest, send, first_grad = feed(
         ids, tokens, attended, cotangent, small, first, rests, BF16

time: 59.7 us -> 61.4 us (1.028)
  waiting for transfers between devices: 15 us -> 16.8 us
    ppermute x21 -> x20, waiting for transfers between devices: 15 us -> 16.8 us  [move(): return lax.ppermute(values, 'fsdp', pairs)]
    ppermute x21 -> x20, starting transfers between devices: 23 us -> 22.8 us  [move(): return lax.ppermute(values, 'fsdp', pairs)]
  transfers between devices with their start and end apart: 21 -> 20, of which waited for: 10 -> 10; matrix products, arithmetic and copies ran while one was open for 0% -> 0% of each run, Pallas kernels for 17% -> 16%
where the time goes in v17:
time: 61.4 us; the launch traced here: 61.2 us
  starting transfers between devices  22.8 us (37%)
  Pallas kernels  17.3 us (28%)
  waiting for transfers between devices  16.8 us (27%)
  local copies, waits for them, and re-layouts  3.42 us (6%)
  between operations  0.77 us (1%)
    ppermute x20, starting transfers between devices, move(): return lax.ppermute(values, 'fsdp', pairs)  22.8 us
    pallas_call x13, Pallas kernels, call(): pl.pallas_call(kernel, in_specs=[SMEM_SPEC] * with_ids + [VMEM_SPEC] * le...  17.3 us
    ppermute x20, waiting for transfers between devices, move(): return lax.ppermute(values, 'fsdp', pairs)  16.8 us
    unnamed x14, local copies, waits for them, and re-layouts  3.33 us
  transfers between devices with their start and end apart: 20, of which 10 were waited for; matrix products, arithmetic and copies ran while one was open for 0% of the time, Pallas kernels for 16%

profile of v17, /device:TPU:0, one launch (start us, length us, event | category | flops | bytes accessed | tf_op | source)
XLA Modules:
  0.0 61.2 jit_solution(11420601233787740497)
XLA Ops:
  0.6 3.1 %collective-permute-start = (bf16[193,128]{1,0:T(8,128)(2,1)}, bf16[193,128]{1,0:T(8,128)(2,1)S(1)}, u32[]{:S(2)}, u32[]{:S(2)}) collective-permute-start(bf16[193,128]{1,0:T(8,128)(2,1)} %params.1), channel_id=1, source_target_pairs={{0,8},{1,9},{2,10},{3,11},{4,12},{5,13},{6,14},{7,15},{8,16},{9,17... | collective-permute-start | bytes 148232 | tf_op jit(solution)/shard_map/ppermute | solution.py:583
  3.7 2.6 %collective-permute-start.1 = (bf16[193,128]{1,0:T(8,128)(2,1)}, bf16[193,128]{1,0:T(8,128)(2,1)S(1)}, u32[]{:S(2)}, u32[]{:S(2)}) collective-permute-start(bf16[193,128]{1,0:T(8,128)(2,1)} %params.1), channel_id=1, source_target_pairs={{0,16},{1,17},{2,18},{3,19},{4,20},{5,21},{6,22},{7,23},{8,24},{9,... | collective-permute-start | bytes 148232 | tf_op jit(solution)/shard_map/ppermute | solution.py:583
  6.3 1.3 %collective-permute-start.2 = (bf16[193,128]{1,0:T(8,128)(2,1)}, bf16[193,128]{1,0:T(8,128)(2,1)S(1)}, u32[]{:S(2)}, u32[]{:S(2)}) collective-permute-start(bf16[193,128]{1,0:T(8,128)(2,1)} %params.1), channel_id=1, source_target_pairs={{0,24},{1,25},{2,26},{3,27},{4,28},{5,29},{6,30},{7,31},{8,0},{9,1... | collective-permute-start | bytes 148232 | tf_op jit(solution)/shard_map/ppermute | solution.py:583
  7.6 1.0 %copy-done.1 = bf16[1024,256]{1,0:T(8,128)(2,1)S(1)} copy-done((bf16[1024,256]{1,0:T(8,128)(2,1)S(1)}, bf16[1024,256]{1,0:T(8,128)(2,1)}, u32[]{:S(2)}) %copy-start.1) | copy-done | bytes 524312
  8.7 0.8 %copy-done.3 = bf16[193,128]{1,0:T(8,128)(2,1)S(1)} copy-done((bf16[193,128]{1,0:T(8,128)(2,1)S(1)}, bf16[193,128]{1,0:T(8,128)(2,1)}, u32[]{:S(2)}) %copy-start.3) | copy-done | bytes 49432
  9.5 0.7 %copy-done.4 = s32[1024]{0:T(1024)S(1)} copy-done((s32[1024]{0:T(1024)S(1)}, s32[1024]{0:T(1024)}, u32[]{:S(2)}) %copy-start.4) | copy-done | bytes 4120
  10.2 0.7 %prepare.1 = (f32[1024,256]{1,0:T(8,128)S(1)}, bf16[256,1024]{1,0:T(8,128)(2,1)S(1)}, bf16[193,128]{1,0:T(8,128)(2,1)S(1)}, f32[1024,128]{1,0:T(8,128)S(1)}) custom-call(bf16[1024,256]{1,0:T(8,128)(2,1)S(1)} %copy-done.1, bf16[193,128]{1,0:T(8,128)(2,1)S(1)} %copy-done.3, s32[8,128]{1,0:T(8,128)S(1)} %bitcast.10), custom_call_target="tpu_custom_call" | custom-call | flops 2000000000 | bytes 1048576 | tf_op jit(solution)/shard_map/prepare/pallas_call | solution.py:438
  10.9 0.0 copy-start.5
  10.9 0.8 %copy-done.5 = bf16[256,1024]{1,0:T(8,128)(2,1)} copy-done((bf16[256,1024]{1,0:T(8,128)(2,1)}, bf16[256,1024]{1,0:T(8,128)(2,1)S(1)}, u32[]{:S(2)}) %copy-start.5) | copy-done | bytes 524312
  11.7 0.1 sort_shares.1
  11.7 2.5 %collective-permute-start.5 = (bf16[864,128]{1,0:T(8,128)(2,1)S(1)}, bf16[864,128]{1,0:T(8,128)(2,1)S(1)}, u32[]{:S(2)}, u32[]{:S(2)}) collective-permute-start(bf16[864,128]{1,0:T(8,128)(2,1)S(1)} %get-tuple-element.43), channel_id=1, source_target_pairs={{0,6},{1,7},{2,4},{3,5},{4,2},{5,3},{6,0},{7,1},{8,14},{9,15},{10,... | collective-permute-start | bytes 663560 | tf_op jit(solution)/shard_map/ppermute | solution.py:583
  14.2 0.5 collective-permute-start.6
  14.8 0.5 collective-permute-start.7
  15.3 1.5 %collective-permute-start.3 = (bf16[3,193,128]{2,1,0:T(8,128)(2,1)S(1)}, bf16[3,193,128]{2,1,0:T(8,128)(2,1)S(1)}, u32[]{:S(2)}, u32[]{:S(2)}) collective-permute-start(bf16[3,193,128]{2,1,0:T(8,128)(2,1)S(1)} %get-tuple-element.39.refs_0_), channel_id=1, source_target_pairs={{0,2},{1,3},{2,0},{3,1},{4,6},{5,7},{6,4},{7,5},{8,10},{9,11},{10,... | collective-permute-start | bytes 444680 | tf_op jit(solution)/shard_map/ppermute | solution.py:583
  16.8 1.5 %collective-permute-start.4 = (bf16[3,193,128]{2,1,0:T(8,128)(2,1)S(1)}, bf16[3,193,128]{2,1,0:T(8,128)(2,1)S(1)}, u32[]{:S(2)}, u32[]{:S(2)}) collective-permute-start(bf16[3,193,128]{2,1,0:T(8,128)(2,1)S(1)} %get-tuple-element.39.refs_0_), channel_id=1, source_target_pairs={{0,4},{1,5},{2,6},{3,7},{4,0},{5,1},{6,2},{7,3},{8,12},{9,13},{10,... | collective-permute-start | bytes 444680 | tf_op jit(solution)/shard_map/ppermute | solution.py:583
  18.3 3.8 %collective-permute-done.6.refs_0_ = bf16[1,240,128]{2,1,0:T(8,128)(2,1)S(1)} collective-permute-done((bf16[1,240,128]{2,1,0:T(8,128)(2,1)S(1)}, bf16[1,240,128]{2,1,0:T(8,128)(2,1)S(1)}, u32[]{:S(2)}, u32[]{:S(2)}) %collective-permute-start.6) | collective-permute-done | bytes 61472 | tf_op jit(solution)/shard_map/ppermute | solution.py:583
  22.1 0.1 collective-permute-start.9
  22.2 0.5 collective-permute-start.8
  22.8 0.1 stack.36.ids
  22.9 0.7 %collective-permute-done.9.refs_3_ = bf16[2,240,128]{2,1,0:T(8,128)(2,1)S(1)} collective-permute-done((bf16[2,240,128]{2,1,0:T(8,128)(2,1)S(1)}, bf16[2,240,128]{2,1,0:T(8,128)(2,1)S(1)}, u32[]{:S(2)}, u32[]{:S(2)}) %collective-permute-start.9) | collective-permute-done | bytes 122912 | tf_op jit(solution)/shard_map/ppermute | solution.py:583
  23.5 0.2 collective-permute-done.8.refs_2_
  23.7 2.6 %attend.1 = (bf16[1024,768]{1,0:T(8,128)(2,1)S(1)}, bf16[1024,512]{1,0:T(8,128)(2,1)S(1)}, bf16[1024,256]{1,0:T(8,128)(2,1)S(1)}, bf16[256,768]{1,0:T(8,128)(2,1...) custom-call(s32[8]{0:T(128)S(1)} %stack.36.ids, f32[1024,128]{1,0:T(8,128)S(1)} %get-tuple-element.40.allowed, ...), custom_call_target="tpu_custom_call" | custom-call | flops 10000000 | bytes 1048576 | tf_op jit(solution)/shard_map/attend/pallas_call | solution.py:438
  26.4 0.1 stack_rest.1.refs_1_
  26.5 0.4 collective-permute-start.11
  26.9 0.2 collective-permute-start.10
  27.0 1.5 %collective-permute-done.10.refs_2_ = bf16[3,193,128]{2,1,0:T(8,128)(2,1)S(1)} collective-permute-done((bf16[3,193,128]{2,1,0:T(8,128)(2,1)S(1)}, bf16[3,193,128]{2,1,0:T(8,128)(2,1)S(1)}, u32[]{:S(2)}, u32[]{:S(2)}) %collective-permute-start.10) | collective-permute-done | bytes 148256 | tf_op jit(solution)/shard_map/ppermute | solution.py:583
  28.6 0.0 copy-start.6
  28.6 6.2 %feed.1 = (f32[1024,256]{1,0:T(8,128)S(1)}, bf16[1024,1024]{1,0:T(8,128)(2,1)S(1)}, f32[1024,256]{1,0:T(8,128)S(1)}, bf16[1024,256]{1,0:T(8,128)(2,1)S(1)}, bf16...) custom-call(s32[8]{0:T(128)S(1)} %stack.36.ids, ...), custom_call_target="tpu_custom_call" | custom-call | flops 8000000000 | bytes 1048576 | tf_op jit(solution)/shard_map/feed/pallas_call | solution.py:438
  34.8 0.4 collective-permute-start.13
  35.2 3.1 %attend_back.1 = (bf16[1024,768]{1,0:T(8,128)(2,1)S(1)}, f32[4,224,128]{2,1,0:T(8,128)S(1)}, bf16[4,224,128]{2,1,0:T(8,128)(2,1)S(1)}) custom-call(s32[8]{0:T(128)S(1)} %stack.36.ids, bf16[1024,768]{1,0:T(8,128)(2,1)S(1)} %get-tuple-element.53.project, bf16[1024,512]{1,0:T(8,128)(2,1)S(1)} %get-tuple-element.54.weights, ...), custom_call_target="tpu_custom_call" | custom-call | flops 4000000000 | bytes 1048576 | tf_op jit(solution)/shard_map/attend_back/pallas_call | solution.py:438
  38.3 0.2 collective-permute-start.12
  38.5 1.3 %collective-permute-done.12.first_in = bf16[4,224,128]{2,1,0:T(8,128)(2,1)S(1)} collective-permute-done((bf16[4,224,128]{2,1,0:T(8,128)(2,1)S(1)}, bf16[4,224,128]{2,1,0:T(8,128)(2,1)S(1)}, u32[]{:S(2)}, u32[]{:S(2)}) %collective-permute-start.12) | collective-permute-done | bytes 229408 | tf_op jit(solution)/shard_map/ppermute | solution.py:583
  39.9 0.2 add_core.1
  40.1 1.5 %collective-permute-start.14 = (bf16[4,193,128]{2,1,0:T(8,128)(2,1)S(1)}, bf16[4,193,128]{2,1,0:T(8,128)(2,1)S(1)}, u32[]{:S(2)}, u32[]{:S(2)}) collective-permute-start(bf16[4,193,128]{2,1,0:T(8,128)(2,1)S(1)} %get-tuple-element.66), channel_id=1, source_target_pairs={{0,6},{1,7},{2,4},{3,5},{4,2},{5,3},{6,0},{7,1},{8,14},{9,15},{10,... | collective-permute-start | bytes 592904 | tf_op jit(solution)/shard_map/ppermute | solution.py:583
  41.5 0.5 collective-permute-start.15
  42.1 1.6 %collective-permute-start.16 = (bf16[4,193,128]{2,1,0:T(8,128)(2,1)S(1)}, bf16[4,193,128]{2,1,0:T(8,128)(2,1)S(1)}, u32[]{:S(2)}, u32[]{:S(2)}) collective-permute-start(bf16[4,193,128]{2,1,0:T(8,128)(2,1)S(1)} %get-tuple-element.68), channel_id=1, source_target_pairs={{0,4},{1,5},{2,6},{3,7},{4,0},{5,1},{6,2},{7,3},{8,12},{9,13},{10,... | collective-permute-start | bytes 592904 | tf_op jit(solution)/shard_map/ppermute | solution.py:583
  43.6 2.0 %input_grad.1 = f32[1024,256]{1,0:T(8,128)} custom-call(bf16[1024,256]{1,0:T(8,128)(2,1)S(1)} %copy-done.2, bf16[1024,768]{1,0:T(8,128)(2,1)S(1)} %get-tuple-element.59.grad_project, f32[1024,256]{1,0:T(8,128)S(1)} %get-tuple-element.60.grad_middle, bf16[256,768]{1,0:T(8,128)(2,1)S(1)} %get-tuple-element.57.w_qkv, f32[32,128]{1,0:T(8,128)S(1)} %get-tuple-element.46.small), custom_call_target="tpu_custom_call" | custom-call | flops 2000000000 | bytes 1048576 | tf_op jit(solution)/shard_map/input_grad/pallas_call | solution.py:438
  45.7 3.3 %collective-permute-done.14.refs_0_ = bf16[4,193,128]{2,1,0:T(8,128)(2,1)S(1)} collective-permute-done((bf16[4,193,128]{2,1,0:T(8,128)(2,1)S(1)}, bf16[4,193,128]{2,1,0:T(8,128)(2,1)S(1)}, u32[]{:S(2)}, u32[]{:S(2)}) %collective-permute-start.14) | collective-permute-done | bytes 197664 | tf_op jit(solution)/shard_map/ppermute | solution.py:583
  49.0 2.6 %collective-permute-done.15.refs_1_ = bf16[4,193,128]{2,1,0:T(8,128)(2,1)S(1)} collective-permute-done((bf16[4,193,128]{2,1,0:T(8,128)(2,1)S(1)}, bf16[4,193,128]{2,1,0:T(8,128)(2,1)S(1)}, u32[]{:S(2)}, u32[]{:S(2)}) %collective-permute-start.15) | collective-permute-done | bytes 197664 | tf_op jit(solution)/shard_map/ppermute | solution.py:583
  51.6 1.0 %collective-permute-done.16.refs_2_ = bf16[4,193,128]{2,1,0:T(8,128)(2,1)S(1)} collective-permute-done((bf16[4,193,128]{2,1,0:T(8,128)(2,1)S(1)}, bf16[4,193,128]{2,1,0:T(8,128)(2,1)S(1)}, u32[]{:S(2)}, u32[]{:S(2)}) %collective-permute-start.16) | collective-permute-done | bytes 197664 | tf_op jit(solution)/shard_map/ppermute | solution.py:583
  52.6 0.2 add_plane.1
  52.8 0.7 %collective-permute-start.17 = (bf16[193,128]{1,0:T(8,128)(2,1)S(1)}, bf16[193,128]{1,0:T(8,128)(2,1)S(1)}, u32[]{:S(2)}, u32[]{:S(2)}) collective-permute-start(bf16[193,128]{1,0:T(8,128)(2,1)S(1)} %get-tuple-element.70), channel_id=1, source_target_pairs={{0,8},{1,9},{2,10},{3,11},{4,12},{5,13},{6,14},{7,15},{8,16},{9,17... | collective-permute-start | bytes 148232 | tf_op jit(solution)/shard_map/ppermute | solution.py:583
  53.5 1.4 %collective-permute-start.18 = (bf16[193,128]{1,0:T(8,128)(2,1)S(1)}, bf16[193,128]{1,0:T(8,128)(2,1)S(1)}, u32[]{:S(2)}, u32[]{:S(2)}) collective-permute-start(bf16[193,128]{1,0:T(8,128)(2,1)S(1)} %get-tuple-element.71), channel_id=1, source_target_pairs={{0,16},{1,17},{2,18},{3,19},{4,20},{5,21},{6,22},{7,23},{8,24},{9,... | collective-permute-start | bytes 148232 | tf_op jit(solution)/shard_map/ppermute | solution.py:583
  54.9 1.7 %collective-permute-start.19 = (bf16[193,128]{1,0:T(8,128)(2,1)S(1)}, bf16[193,128]{1,0:T(8,128)(2,1)S(1)}, u32[]{:S(2)}, u32[]{:S(2)}) collective-permute-start(bf16[193,128]{1,0:T(8,128)(2,1)S(1)} %get-tuple-element.72), channel_id=1, source_target_pairs={{0,24},{1,25},{2,26},{3,27},{4,28},{5,29},{6,30},{7,31},{8,0},{9,1... | collective-permute-start | bytes 148232 | tf_op jit(solution)/shard_map/ppermute | solution.py:583
  56.6 1.5 %result.1 = bf16[1024,256]{1,0:T(8,128)(2,1)} custom-call(f32[1024,256]{1,0:T(8,128)S(1)} %get-tuple-element.50.middle, bf16[1024,1024]{1,0:T(8,128)(2,1)S(1)} %get-tuple-element.51.activated, bf16[1024,256]{1,0:T(8,128)(2,1)S(1)} %get-tuple-element.52.w_down, f32[32,128]{1,0:T(8,128)S(1)} %get-tuple-element.46.small), custom_call_target="tpu_custom_call" | custom-call | flops 2000000000 | bytes 1048576 | tf_op jit(solution)/shard_map/result/pallas_call | solution.py:438
  58.1 1.1 %collective-permute-done.17.refs_0_ = bf16[193,128]{1,0:T(8,128)(2,1)S(1)} collective-permute-done((bf16[193,128]{1,0:T(8,128)(2,1)S(1)}, bf16[193,128]{1,0:T(8,128)(2,1)S(1)}, u32[]{:S(2)}, u32[]{:S(2)}) %collective-permute-start.17) | collective-permute-done | bytes 49440 | tf_op jit(solution)/shard_map/ppermute | solution.py:583
  59.3 1.2 %collective-permute-done.18.refs_1_ = bf16[193,128]{1,0:T(8,128)(2,1)S(1)} collective-permute-done((bf16[193,128]{1,0:T(8,128)(2,1)S(1)}, bf16[193,128]{1,0:T(8,128)(2,1)S(1)}, u32[]{:S(2)}, u32[]{:S(2)}) %collective-permute-start.18) | collective-permute-done | bytes 49440 | tf_op jit(solution)/shard_map/ppermute | solution.py:583
  60.5 0.7 %add_column.1 = f32[193,128]{1,0:T(8,128)} custom-call(f32[193,128]{1,0:T(8,128)S(1)} %get-tuple-element.69.kept, bf16[193,128]{1,0:T(8,128)(2,1)S(1)} %collective-permute-done.17.refs_0_, bf16[193,128]{1,0:T(8,128)(2,1)S(1)} %collective-permute-done.18.refs_1_, bf16[193,128]{1,0:T(8,128)(2,1)S(1)} %collective-permute-done.19.refs_2_), custom_call_target="tpu_custom_call" | custom-call | flops 1000000000 | bytes 1048576 | tf_op jit(solution)/shard_map/add_column/pallas_call | solution.py:438
  (20 shorter events, 0.1 us)
Async XLA Ops:
  0.6 11.0 %collective-permute-start = (bf16[193,128]{1,0:T(8,128)(2,1)}, bf16[193,128]{1,0:T(8,128)(2,1)S(1)}, u32[]{:S(2)}, u32[]{:S(2)}) collective-permute-start(bf16[193,128]{1,0:T(8,128)(2,1)} %params.1), channel_id=1, source_target_pairs={{0,8},{1,9},{2,10},{3,11},{4,12},{5,13},{6,14},{7,15},{8,16},{9,17... | collective-permute-start | bytes 148232 | tf_op jit(solution)/shard_map/ppermute | solution.py:583
  3.7 8.0 %collective-permute-start.1 = (bf16[193,128]{1,0:T(8,128)(2,1)}, bf16[193,128]{1,0:T(8,128)(2,1)S(1)}, u32[]{:S(2)}, u32[]{:S(2)}) collective-permute-start(bf16[193,128]{1,0:T(8,128)(2,1)} %params.1), channel_id=1, source_target_pairs={{0,16},{1,17},{2,18},{3,19},{4,20},{5,21},{6,22},{7,23},{8,24},{9,... | collective-permute-start | bytes 148232 | tf_op jit(solution)/shard_map/ppermute | solution.py:583
  6.3 5.4 %collective-permute-start.2 = (bf16[193,128]{1,0:T(8,128)(2,1)}, bf16[193,128]{1,0:T(8,128)(2,1)S(1)}, u32[]{:S(2)}, u32[]{:S(2)}) collective-permute-start(bf16[193,128]{1,0:T(8,128)(2,1)} %params.1), channel_id=1, source_target_pairs={{0,24},{1,25},{2,26},{3,27},{4,28},{5,29},{6,30},{7,31},{8,0},{9,1... | collective-permute-start | bytes 148232 | tf_op jit(solution)/shard_map/ppermute | solution.py:583
  7.6 1.0 %copy-start.1 = (bf16[1024,256]{1,0:T(8,128)(2,1)S(1)}, bf16[1024,256]{1,0:T(8,128)(2,1)}, u32[]{:S(2)}) copy-start(bf16[1024,256]{1,0:T(8,128)(2,1)} %tok.5) | copy-start | bytes 1572868
  8.7 0.8 %copy-start.3 = (bf16[193,128]{1,0:T(8,128)(2,1)S(1)}, bf16[193,128]{1,0:T(8,128)(2,1)}, u32[]{:S(2)}) copy-start(bf16[193,128]{1,0:T(8,128)(2,1)} %params.1) | copy-start | bytes 148228
  9.5 0.7 %copy-start.4 = (s32[1024]{0:T(1024)S(1)}, s32[1024]{0:T(1024)}, u32[]{:S(2)}) copy-start(s32[1024]{0:T(1024)} %param.6) | copy-start | bytes 12292
  10.9 0.8 %copy-start.5 = (bf16[256,1024]{1,0:T(8,128)(2,1)}, bf16[256,1024]{1,0:T(8,128)(2,1)S(1)}, u32[]{:S(2)}) copy-start(bf16[256,1024]{1,0:T(8,128)(2,1)S(1)} %get-tuple-element.56.normed_turned) | copy-start | bytes 1572868
  11.7 10.5 %collective-permute-start.5 = (bf16[864,128]{1,0:T(8,128)(2,1)S(1)}, bf16[864,128]{1,0:T(8,128)(2,1)S(1)}, u32[]{:S(2)}, u32[]{:S(2)}) collective-permute-start(bf16[864,128]{1,0:T(8,128)(2,1)S(1)} %get-tuple-element.43), channel_id=1, source_target_pairs={{0,6},{1,7},{2,4},{3,5},{4,2},{5,3},{6,0},{7,1},{8,14},{9,15},{10,... | collective-permute-start | bytes 663560 | tf_op jit(solution)/shard_map/ppermute | solution.py:583
  14.2 7.8 %collective-permute-start.6 = (bf16[1,240,128]{2,1,0:T(8,128)(2,1)S(1)}, bf16[1,240,128]{2,1,0:T(8,128)(2,1)S(1)}, u32[]{:S(2)}, u32[]{:S(2)}) collective-permute-start(bf16[1,240,128]{2,1,0:T(8,128)(2,1)S(1)} %get-tuple-element.42.own), channel_id=1, source_target_pairs={{0,2},{1,3},{2,0},{3,1},{4,6},{5,7},{6,4},{7,5},{8,10},{9,11},{10,... | collective-permute-start | bytes 184328 | tf_op jit(solution)/shard_map/ppermute | solution.py:583
  14.8 7.3 %collective-permute-start.7 = (bf16[1,240,128]{2,1,0:T(8,128)(2,1)S(1)}, bf16[1,240,128]{2,1,0:T(8,128)(2,1)S(1)}, u32[]{:S(2)}, u32[]{:S(2)}) collective-permute-start(bf16[1,240,128]{2,1,0:T(8,128)(2,1)S(1)} %get-tuple-element.42.own), channel_id=1, source_target_pairs={{0,4},{1,5},{2,6},{3,7},{4,0},{5,1},{6,2},{7,3},{8,12},{9,13},{10,... | collective-permute-start | bytes 184328 | tf_op jit(solution)/shard_map/ppermute | solution.py:583
  15.3 11.1 %collective-permute-start.3 = (bf16[3,193,128]{2,1,0:T(8,128)(2,1)S(1)}, bf16[3,193,128]{2,1,0:T(8,128)(2,1)S(1)}, u32[]{:S(2)}, u32[]{:S(2)}) collective-permute-start(bf16[3,193,128]{2,1,0:T(8,128)(2,1)S(1)} %get-tuple-element.39.refs_0_), channel_id=1, source_target_pairs={{0,2},{1,3},{2,0},{3,1},{4,6},{5,7},{6,4},{7,5},{8,10},{9,11},{10,... | collective-permute-start | bytes 444680 | tf_op jit(solution)/shard_map/ppermute | solution.py:583
  16.8 9.6 %collective-permute-start.4 = (bf16[3,193,128]{2,1,0:T(8,128)(2,1)S(1)}, bf16[3,193,128]{2,1,0:T(8,128)(2,1)S(1)}, u32[]{:S(2)}, u32[]{:S(2)}) collective-permute-start(bf16[3,193,128]{2,1,0:T(8,128)(2,1)S(1)} %get-tuple-element.39.refs_0_), channel_id=1, source_target_pairs={{0,4},{1,5},{2,6},{3,7},{4,0},{5,1},{6,2},{7,3},{8,12},{9,13},{10,... | collective-permute-start | bytes 444680 | tf_op jit(solution)/shard_map/ppermute | solution.py:583
  22.1 1.4 %collective-permute-start.9 = (bf16[2,240,128]{2,1,0:T(8,128)(2,1)S(1)}, bf16[2,240,128]{2,1,0:T(8,128)(2,1)S(1)}, u32[]{:S(2)}, u32[]{:S(2)}) collective-permute-start(bf16[2,240,128]{2,1,0:T(8,128)(2,1)S(1)} %stack.37.refs_1_), channel_id=1, source_target_pairs={{0,1},{1,0},{2,3},{3,2},{4,5},{5,4},{6,7},{7,6},{8,9},{9,8},{10,11... | collective-permute-start | bytes 368648 | tf_op jit(solution)/shard_map/ppermute | solution.py:583
  22.2 1.5 %collective-permute-start.8 = (bf16[2,240,128]{2,1,0:T(8,128)(2,1)S(1)}, bf16[2,240,128]{2,1,0:T(8,128)(2,1)S(1)}, u32[]{:S(2)}, u32[]{:S(2)}) collective-permute-start(bf16[2,240,128]{2,1,0:T(8,128)(2,1)S(1)} %stack_first.1.refs_0_), channel_id=1, source_target_pairs={{0,1},{1,0},{2,3},{3,2},{4,5},{5,4},{6,7},{7,6},{8,9},{9,8},{10,11... | collective-permute-start | bytes 368648 | tf_op jit(solution)/shard_map/ppermute | solution.py:583
  22.8 5.8 %copy-start = (bf16[1024,256]{1,0:T(8,128)(2,1)S(1)}, bf16[1024,256]{1,0:T(8,128)(2,1)}, u32[]{:S(2)}) copy-start(bf16[1024,256]{1,0:T(8,128)(2,1)} %cot.1) | copy-start | bytes 1572868
  22.9 5.7 %copy-start.2 = (bf16[1024,256]{1,0:T(8,128)(2,1)S(1)}, bf16[1024,256]{1,0:T(8,128)(2,1)}, u32[]{:S(2)}) copy-start(bf16[1024,256]{1,0:T(8,128)(2,1)} %tok.5) | copy-start | bytes 1572868
  26.5 2.1 %collective-permute-start.11 = (bf16[9,193,128]{2,1,0:T(8,128)(2,1)S(1)}, bf16[9,193,128]{2,1,0:T(8,128)(2,1)S(1)}, u32[]{:S(2)}, u32[]{:S(2)}) collective-permute-start(bf16[9,193,128]{2,1,0:T(8,128)(2,1)S(1)} %stack_rest.1.refs_1_), channel_id=1, source_target_pairs={{0,1},{1,0},{2,3},{3,2},{4,5},{5,4},{6,7},{7,6},{8,9},{9,8},{10,11... | collective-permute-start | bytes 1334024 | tf_op jit(solution)/shard_map/ppermute | solution.py:583
  26.9 1.7 %collective-permute-start.10 = (bf16[3,193,128]{2,1,0:T(8,128)(2,1)S(1)}, bf16[3,193,128]{2,1,0:T(8,128)(2,1)S(1)}, u32[]{:S(2)}, u32[]{:S(2)}) collective-permute-start(bf16[3,193,128]{2,1,0:T(8,128)(2,1)S(1)} %get-tuple-element.39.refs_0_), channel_id=1, source_target_pairs={{0,1},{1,0},{2,3},{3,2},{4,5},{5,4},{6,7},{7,6},{8,9},{9,8},{10,11... | collective-permute-start | bytes 444680 | tf_op jit(solution)/shard_map/ppermute | solution.py:583
  28.6 6.6 %copy-start.6 = (bf16[256,1024]{1,0:T(8,128)(2,1)S(1)}, bf16[256,1024]{1,0:T(8,128)(2,1)}, u32[]{:S(2)}) copy-start(bf16[256,1024]{1,0:T(8,128)(2,1)} %copy-done.5) | copy-start | bytes 1572868
  34.8 5.1 %collective-permute-start.13 = (bf16[12,193,128]{2,1,0:T(8,128)(2,1)S(1)}, bf16[12,193,128]{2,1,0:T(8,128)(2,1)S(1)}, u32[]{:S(2)}, u32[]{:S(2)}) collective-permute-start(bf16[12,193,128]{2,1,0:T(8,128)(2,1)S(1)} %get-tuple-element.64), channel_id=1, source_target_pairs={{0,1},{1,0},{2,3},{3,2},{4,5},{5,4},{6,7},{7,6},{8,9},{9,8},{10,11... | collective-permute-start | bytes 1778696 | tf_op jit(solution)/shard_map/ppermute | solution.py:583
  38.3 1.6 %collective-permute-start.12 = (bf16[4,224,128]{2,1,0:T(8,128)(2,1)S(1)}, bf16[4,224,128]{2,1,0:T(8,128)(2,1)S(1)}, u32[]{:S(2)}, u32[]{:S(2)}) collective-permute-start(bf16[4,224,128]{2,1,0:T(8,128)(2,1)S(1)} %get-tuple-element.62), channel_id=1, source_target_pairs={{0,1},{1,0},{2,3},{3,2},{4,5},{5,4},{6,7},{7,6},{8,9},{9,8},{10,11... | collective-permute-start | bytes 688136 | tf_op jit(solution)/shard_map/ppermute | solution.py:583
  40.1 8.9 %collective-permute-start.14 = (bf16[4,193,128]{2,1,0:T(8,128)(2,1)S(1)}, bf16[4,193,128]{2,1,0:T(8,128)(2,1)S(1)}, u32[]{:S(2)}, u32[]{:S(2)}) collective-permute-start(bf16[4,193,128]{2,1,0:T(8,128)(2,1)S(1)} %get-tuple-element.66), channel_id=1, source_target_pairs={{0,6},{1,7},{2,4},{3,5},{4,2},{5,3},{6,0},{7,1},{8,14},{9,15},{10,... | collective-permute-start | bytes 592904 | tf_op jit(solution)/shard_map/ppermute | solution.py:583
  41.5 10.1 %collective-permute-start.15 = (bf16[4,193,128]{2,1,0:T(8,128)(2,1)S(1)}, bf16[4,193,128]{2,1,0:T(8,128)(2,1)S(1)}, u32[]{:S(2)}, u32[]{:S(2)}) collective-permute-start(bf16[4,193,128]{2,1,0:T(8,128)(2,1)S(1)} %get-tuple-element.67), channel_id=1, source_target_pairs={{0,2},{1,3},{2,0},{3,1},{4,6},{5,7},{6,4},{7,5},{8,10},{9,11},{10,... | collective-permute-start | bytes 592904 | tf_op jit(solution)/shard_map/ppermute | solution.py:583
  42.1 10.5 %collective-permute-start.16 = (bf16[4,193,128]{2,1,0:T(8,128)(2,1)S(1)}, bf16[4,193,128]{2,1,0:T(8,128)(2,1)S(1)}, u32[]{:S(2)}, u32[]{:S(2)}) collective-permute-start(bf16[4,193,128]{2,1,0:T(8,128)(2,1)S(1)} %get-tuple-element.68), channel_id=1, source_target_pairs={{0,4},{1,5},{2,6},{3,7},{4,0},{5,1},{6,2},{7,3},{8,12},{9,13},{10,... | collective-permute-start | bytes 592904 | tf_op jit(solution)/shard_map/ppermute | solution.py:583
  52.8 6.5 %collective-permute-start.17 = (bf16[193,128]{1,0:T(8,128)(2,1)S(1)}, bf16[193,128]{1,0:T(8,128)(2,1)S(1)}, u32[]{:S(2)}, u32[]{:S(2)}) collective-permute-start(bf16[193,128]{1,0:T(8,128)(2,1)S(1)} %get-tuple-element.70), channel_id=1, source_target_pairs={{0,8},{1,9},{2,10},{3,11},{4,12},{5,13},{6,14},{7,15},{8,16},{9,17... | collective-permute-start | bytes 148232 | tf_op jit(solution)/shard_map/ppermute | solution.py:583
  53.5 7.0 %collective-permute-start.18 = (bf16[193,128]{1,0:T(8,128)(2,1)S(1)}, bf16[193,128]{1,0:T(8,128)(2,1)S(1)}, u32[]{:S(2)}, u32[]{:S(2)}) collective-permute-start(bf16[193,128]{1,0:T(8,128)(2,1)S(1)} %get-tuple-element.71), channel_id=1, source_target_pairs={{0,16},{1,17},{2,18},{3,19},{4,20},{5,21},{6,22},{7,23},{8,24},{9,... | collective-permute-start | bytes 148232 | tf_op jit(solution)/shard_map/ppermute | solution.py:583
  54.9 5.6 %collective-permute-start.19 = (bf16[193,128]{1,0:T(8,128)(2,1)S(1)}, bf16[193,128]{1,0:T(8,128)(2,1)S(1)}, u32[]{:S(2)}, u32[]{:S(2)}) collective-permute-start(bf16[193,128]{1,0:T(8,128)(2,1)S(1)} %get-tuple-element.72), channel_id=1, source_target_pairs={{0,24},{1,25},{2,26},{3,27},{4,28},{5,29},{6,30},{7,31},{8,0},{9,1... | collective-permute-start | bytes 148232 | tf_op jit(solution)/shard_map/ppermute | solution.py:583

commit v18 on v15

--- a/solution.py
+++ b/solution.py
@@ -284,7 +284,7 @@
     for target, out in enumerate((keep_out, send_out)):
         for p in range(PLANE):
             for z in range(1, Z):
-                share = ids[target * PLANE + p] + z * 2 * PLANE
+                share = ids[(2 + target) * PLANE + p] + z * 2 * PLANE
                 rows = flat[pl.ds(share * SHARE - ROW_OUT, SHARE), :]
                 out[p * (Z - 1) + z - 1] = rows.astype(out.dtype)
 
@@ -525,7 +525,7 @@
     ids = jnp.array(order, jnp.int32)
     project, weights, attended, w_qkv, small, first = attend(ids, allowed, normed, firsts)
     middle, activated, grad_middle, grad_attended, w_down, rest, rest_send, first_grad = feed(
-        ids, tokens, attended, cotangent, small, first, rests, F32
+        jnp.concatenate([ids, ids]), tokens, attended, cotangent, small, first, rests, F32
     )
     outputs = result(middle, activated, w_down, small)
     grad_project, first, first_send = attend_back(
@@ -564,15 +564,18 @@
 
 
 STEPS = (3, 1, 2)
+REST_STEPS = (1, 3, 2)
 
 
 def local_slice(tokens, params, segment_ids, cotangent):
     me = lax.axis_index("fsdp").astype(jnp.int32)
     z, plane, core = me // (2 * PLANE), (me // 2) % PLANE, me % 2
     where = z.reshape(1)
-    ids = jnp.stack(
-        [(plane ^ dp) * 2 + (core ^ dc) for dc in range(2) for dp in (0, *STEPS)]
-    )
+    ids, rest_ids = (
+        jnp.stack([(plane ^ dp) * 2 + (core ^ dc) for dc in range(2) for dp in (0, *steps)])
+        for steps in (STEPS, REST_STEPS)
+    )
+    feed_ids = jnp.concatenate([rest_ids, ids])
 
     normed, normed_turned, own, allowed = prepare(tokens, params, segment_ids)
     first, rest = call(
@@ -581,7 +584,7 @@
         [pltpu.VMEM((Z, SHARE, LANES), BF16), pltpu.VMEM((SIDE + SMALL_ROWS, LANES), F32)],
     )
     firsts = [first] + [move(first, 0, d, 0) for d in STEPS]
-    rests = [move(rest, 0, d, 0) for d in STEPS]
+    rests = [move(rest, 0, d, 0) for d in REST_STEPS]
     firsts = [stack(firsts[i:j]) if j > i + 1 else firsts[i] for i, j in FIRST_GROUPS]
     firsts = firsts + [move(item, 0, 0, 1) for item in firsts]
     project, weights, attended, w_qkv, small, first = attend(ids, allowed, normed, firsts)
@@ -589,7 +592,7 @@
     rests = stack(rests)
     rests = [rest, rests, move(rest, 0, 0, 1), move(rests, 0, 0, 1)]
     middle, activated, grad_middle, grad_attended, w_down, rest, send, first_grad = feed(
-        ids, tokens, attended, cotangent, small, first, rests, BF16
+        feed_ids, tokens, attended, cotangent, small, first, rests, BF16
     )
 
     rest_in = move(send, 0, 0, 1)

time: 59.7 us -> 66.8 us (1.12)
  local copies, waits for them, and re-layouts: 3.42 us -> 9.62 us
  waiting for transfers between devices: 15 us -> 13 us
  Pallas kernels: 17.3 us -> 18.8 us
  starting transfers between devices: 23 us -> 24.2 us
    unnamed x14 -> x32, local copies, waits for them, and re-layouts: 3.33 us -> 9.44 us
    ppermute x21, waiting for transfers between devices: 15 us -> 13 us  [move(): return lax.ppermute(values, 'fsdp', pairs)]
    pallas_call x13, Pallas kernels: 17.3 us -> 18.8 us  [call(): pl.pallas_call(kernel, in_specs=[SMEM_SPEC] * with_ids + [VMEM_SPEC] * le...]
    ppermute x21, starting transfers between devices: 23 us -> 24.2 us  [move(): return lax.ppermute(values, 'fsdp', pairs)]
  transfers between devices with their start and end apart: 21 -> 21, of which waited for: 10 -> 12; matrix products, arithmetic and copies ran while one was open for 0% -> 0% of each run, Pallas kernels for 17% -> 15%
where the time goes in v18:
time: 66.8 us; the launch traced here: 66.4 us
  starting transfers between devices  24.2 us (36%)
  Pallas kernels  18.8 us (28%)
  waiting for transfers between devices  13 us (19%)
  local copies, waits for them, and re-layouts  9.62 us (14%)
  between operations  0.75 us (1%)
    ppermute x21, starting transfers between devices, move(): return lax.ppermute(values, 'fsdp', pairs)  24.2 us
    pallas_call x13, Pallas kernels, call(): pl.pallas_call(kernel, in_specs=[SMEM_SPEC] * with_ids + [VMEM_SPEC] * le...  18.8 us
    ppermute x21, waiting for transfers between devices, move(): return lax.ppermute(values, 'fsdp', pairs)  13 us
    unnamed x32, local copies, waits for them, and re-layouts  9.44 us
  transfers between devices with their start and end apart: 21, of which 12 were waited for; matrix products, arithmetic and copies ran while one was open for 0% of the time, Pallas kernels for 15%

profile of v18, /device:TPU:0, one launch (start us, length us, event | category | flops | bytes accessed | tf_op | source)
XLA Modules:
  0.0 66.4 jit_solution(14871365020857829958)
XLA Ops:
  0.6 3.1 %collective-permute-start = (bf16[193,128]{1,0:T(8,128)(2,1)}, bf16[193,128]{1,0:T(8,128)(2,1)S(1)}, u32[]{:S(2)}, u32[]{:S(2)}) collective-permute-start(bf16[193,128]{1,0:T(8,128)(2,1)} %params.1), channel_id=1, source_target_pairs={{0,8},{1,9},{2,10},{3,11},{4,12},{5,13},{6,14},{7,15},{8,16},{9,17... | collective-permute-start | bytes 148232 | tf_op jit(solution)/shard_map/ppermute | solution.py:563
  3.7 2.6 %collective-permute-start.1 = (bf16[193,128]{1,0:T(8,128)(2,1)}, bf16[193,128]{1,0:T(8,128)(2,1)S(1)}, u32[]{:S(2)}, u32[]{:S(2)}) collective-permute-start(bf16[193,128]{1,0:T(8,128)(2,1)} %params.1), channel_id=1, source_target_pairs={{0,16},{1,17},{2,18},{3,19},{4,20},{5,21},{6,22},{7,23},{8,24},{9,... | collective-permute-start | bytes 148232 | tf_op jit(solution)/shard_map/ppermute | solution.py:563
  6.3 1.3 %collective-permute-start.2 = (bf16[193,128]{1,0:T(8,128)(2,1)}, bf16[193,128]{1,0:T(8,128)(2,1)S(1)}, u32[]{:S(2)}, u32[]{:S(2)}) collective-permute-start(bf16[193,128]{1,0:T(8,128)(2,1)} %params.1), channel_id=1, source_target_pairs={{0,24},{1,25},{2,26},{3,27},{4,28},{5,29},{6,30},{7,31},{8,0},{9,1... | collective-permute-start | bytes 148232 | tf_op jit(solution)/shard_map/ppermute | solution.py:563
  7.6 1.0 %copy-done.5 = bf16[1024,256]{1,0:T(8,128)(2,1)S(1)} copy-done((bf16[1024,256]{1,0:T(8,128)(2,1)S(1)}, bf16[1024,256]{1,0:T(8,128)(2,1)}, u32[]{:S(2)}) %copy-start.5) | copy-done | bytes 524312
  8.7 0.8 %copy-done.12 = bf16[193,128]{1,0:T(8,128)(2,1)S(1)} copy-done((bf16[193,128]{1,0:T(8,128)(2,1)S(1)}, bf16[193,128]{1,0:T(8,128)(2,1)}, u32[]{:S(2)}) %copy-start.12) | copy-done | bytes 49432
  9.5 0.7 %copy-done.13 = s32[1024]{0:T(1024)S(1)} copy-done((s32[1024]{0:T(1024)S(1)}, s32[1024]{0:T(1024)}, u32[]{:S(2)}) %copy-start.13) | copy-done | bytes 4120
  10.2 0.7 %prepare.1 = (f32[1024,256]{1,0:T(8,128)S(1)}, bf16[256,1024]{1,0:T(8,128)(2,1)S(1)}, bf16[193,128]{1,0:T(8,128)(2,1)S(1)}, f32[1024,128]{1,0:T(8,128)S(1)}) custom-call(bf16[1024,256]{1,0:T(8,128)(2,1)S(1)} %copy-done.5, bf16[193,128]{1,0:T(8,128)(2,1)S(1)} %copy-done.12, s32[8,128]{1,0:T(8,128)S(1)} %bitcast.10), custom_call_target="tpu_custom_call" | custom-call | flops 2000000000 | bytes 1048576 | tf_op jit(solution)/shard_map/prepare/pallas_call | solution.py:418
  10.9 0.8 %copy-done.14 = bf16[256,1024]{1,0:T(8,128)(2,1)} copy-done((bf16[256,1024]{1,0:T(8,128)(2,1)}, bf16[256,1024]{1,0:T(8,128)(2,1)S(1)}, u32[]{:S(2)}) %copy-start.14) | copy-done | bytes 524312
  11.7 0.7 %sort_shares.1 = (bf16[1,240,128]{2,1,0:T(8,128)(2,1)S(1)}, bf16[3,193,128]{2,1,0:T(8,128)(2,1)}) custom-call(s32[1]{0:T(128)} %bitcast.8.ids, bf16[193,128]{1,0:T(8,128)(2,1)S(1)} %get-tuple-element.38.refs_0_, bf16[193,128]{1,0:T(8,128)(2,1)S(1)} %collective-permute-done.refs_1_, bf16[193,128]{1,0:T(8,128)(2,1)S(1)} %collective-permute-done.1.refs_2_, ...), custom_call_target="tpu_custom_call" | custom-call | flops 1000000000 | bytes 1048576 | tf_op jit(solution)/shard_map/sort_shares/pallas_call | solution.py:418
  12.4 2.4 %collective-permute-start.6 = (bf16[1,240,128]{2,1,0:T(8,128)(2,1)S(1)}, bf16[1,240,128]{2,1,0:T(8,128)(2,1)S(1)}, u32[]{:S(2)}, u32[]{:S(2)}) collective-permute-start(bf16[1,240,128]{2,1,0:T(8,128)(2,1)S(1)} %get-tuple-element.42.refs_0_), channel_id=1, source_target_pairs={{0,6},{1,7},{2,4},{3,5},{4,2},{5,3},{6,0},{7,1},{8,14},{9,15},{10,... | collective-permute-start | bytes 184328 | tf_op jit(solution)/shard_map/ppermute | solution.py:563
  14.8 0.5 collective-permute-start.7
  15.3 0.5 collective-permute-start.8
  15.8 1.5 %collective-permute-start.3 = (bf16[3,193,128]{2,1,0:T(8,128)(2,1)}, bf16[3,193,128]{2,1,0:T(8,128)(2,1)S(1)}, u32[]{:S(2)}, u32[]{:S(2)}) collective-permute-start(bf16[3,193,128]{2,1,0:T(8,128)(2,1)} %get-tuple-element.39.refs_0_), channel_id=1, source_target_pairs={{0,2},{1,3},{2,0},{3,1},{4,6},{5,7},{6,4},{7,5},{8,10},{9,11},{10,... | collective-permute-start | bytes 444680 | tf_op jit(solution)/shard_map/ppermute | solution.py:563
  17.3 1.5 %collective-permute-start.4 = (bf16[3,193,128]{2,1,0:T(8,128)(2,1)}, bf16[3,193,128]{2,1,0:T(8,128)(2,1)S(1)}, u32[]{:S(2)}, u32[]{:S(2)}) collective-permute-start(bf16[3,193,128]{2,1,0:T(8,128)(2,1)} %get-tuple-element.39.refs_0_), channel_id=1, source_target_pairs={{0,6},{1,7},{2,4},{3,5},{4,2},{5,3},{6,0},{7,1},{8,14},{9,15},{10,... | collective-permute-start | bytes 444680 | tf_op jit(solution)/shard_map/ppermute | solution.py:563
  18.8 0.8 %collective-permute-start.5 = (bf16[3,193,128]{2,1,0:T(8,128)(2,1)}, bf16[3,193,128]{2,1,0:T(8,128)(2,1)S(1)}, u32[]{:S(2)}, u32[]{:S(2)}) collective-permute-start(bf16[3,193,128]{2,1,0:T(8,128)(2,1)} %get-tuple-element.39.refs_0_), channel_id=1, source_target_pairs={{0,4},{1,5},{2,6},{3,7},{4,0},{5,1},{6,2},{7,3},{8,12},{9,13},{10,... | collective-permute-start | bytes 444680 | tf_op jit(solution)/shard_map/ppermute | solution.py:563
  19.9 0.4 collective-permute-start.10
  20.4 0.6 collective-permute-done.9.refs_2_
  21.1 0.2 collective-permute-done.10.refs_3_
  21.3 2.6 %attend.1 = (bf16[1024,768]{1,0:T(8,128)(2,1)S(1)}, bf16[1024,512]{1,0:T(8,128)(2,1)S(1)}, bf16[1024,256]{1,0:T(8,128)(2,1)S(1)}, bf16[256,768]{1,0:T(8,128)(2,1...) custom-call(s32[8]{0:T(128)S(1)} %stack.46.ids, f32[1024,128]{1,0:T(8,128)S(1)} %get-tuple-element.40.allowed, ...), custom_call_target="tpu_custom_call" | custom-call | flops 10000000 | bytes 1048576 | tf_op jit(solution)/shard_map/attend/pallas_call | solution.py:418
  24.0 1.2 %copy-done = bf16[1024,768]{1,0:T(8,128)(2,1)} copy-done((bf16[1024,768]{1,0:T(8,128)(2,1)}, bf16[1024,768]{1,0:T(8,128)(2,1)S(1)}, u32[]{:S(2)}) %copy-start) | copy-done | bytes 1572888
  25.1 1.0 %copy-done.2 = bf16[1024,512]{1,0:T(8,128)(2,1)} copy-done((bf16[1024,512]{1,0:T(8,128)(2,1)}, bf16[1024,512]{1,0:T(8,128)(2,1)S(1)}, u32[]{:S(2)}) %copy-start.2) | copy-done | bytes 1048600
  26.2 0.4 collective-permute-start.12
  26.6 0.3 copy-done.8
  26.9 0.4 collective-permute-start.11
  27.3 1.2 %collective-permute-done.11.refs_2_ = bf16[3,193,128]{2,1,0:T(8,128)(2,1)S(1)} collective-permute-done((bf16[3,193,128]{2,1,0:T(8,128)(2,1)}, bf16[3,193,128]{2,1,0:T(8,128)(2,1)S(1)}, u32[]{:S(2)}, u32[]{:S(2)}) %collective-permute-start.11) | collective-permute-done | bytes 148256 | tf_op jit(solution)/shard_map/ppermute | solution.py:563
  28.5 0.7 %copy-done.10 = bf16[3,193,128]{2,1,0:T(8,128)(2,1)} copy-done((bf16[3,193,128]{2,1,0:T(8,128)(2,1)}, bf16[3,193,128]{2,1,0:T(8,128)(2,1)S(1)}, u32[]{:S(2)}) %copy-start.10) | copy-done | bytes 148248
  29.2 1.0 %copy-done.6 = bf16[1024,256]{1,0:T(8,128)(2,1)S(1)} copy-done((bf16[1024,256]{1,0:T(8,128)(2,1)S(1)}, bf16[1024,256]{1,0:T(8,128)(2,1)}, u32[]{:S(2)}) %copy-start.6) | copy-done | bytes 524312
  30.2 1.0 %copy-done.9 = bf16[1024,256]{1,0:T(8,128)(2,1)S(1)} copy-done((bf16[1024,256]{1,0:T(8,128)(2,1)S(1)}, bf16[1024,256]{1,0:T(8,128)(2,1)}, u32[]{:S(2)}) %copy-start.9) | copy-done | bytes 524312
  31.3 0.9 %copy-done.11 = bf16[3,193,128]{2,1,0:T(8,128)(2,1)S(1)} copy-done((bf16[3,193,128]{2,1,0:T(8,128)(2,1)S(1)}, bf16[3,193,128]{2,1,0:T(8,128)(2,1)}, u32[]{:S(2)}) %copy-start.11) | copy-done | bytes 148248
  32.2 6.8 %feed.1 = (f32[1024,256]{1,0:T(8,128)S(1)}, bf16[1024,1024]{1,0:T(8,128)(2,1)S(1)}, f32[1024,256]{1,0:T(8,128)S(1)}, bf16[1024,256]{1,0:T(8,128)(2,1)S(1)}, bf16...) custom-call(s32[16]{0:T(128)S(1)} %concatenate.4.ids, ...), custom_call_target="tpu_custom_call" | custom-call | flops 8000000000 | bytes 1048576 | tf_op jit(solution)/shard_map/feed/pallas_call | solution.py:418
  39.0 0.4 collective-permute-start.14
  39.4 3.3 %attend_back.1 = (bf16[1024,768]{1,0:T(8,128)(2,1)S(1)}, f32[4,224,128]{2,1,0:T(8,128)S(1)}, bf16[4,224,128]{2,1,0:T(8,128)(2,1)S(1)}) custom-call(s32[8]{0:T(128)S(1)} %stack.46.ids, bf16[1024,768]{1,0:T(8,128)(2,1)S(1)} %copy-done.1, bf16[1024,512]{1,0:T(8,128)(2,1)S(1)} %copy-done.3, bf16[1024,256]{1,0:T(8,128)(2,1)S(1)} %get-tuple-element.55.grad_attended, ...), custom_call_target="tpu_custom_call" | custom-call | flops 4000000000 | bytes 1048576 | tf_op jit(solution)/shard_map/attend_back/pallas_call | solution.py:418
  42.8 0.2 collective-permute-start.13
  43.0 1.3 %collective-permute-done.13.first_in = bf16[4,224,128]{2,1,0:T(8,128)(2,1)S(1)} collective-permute-done((bf16[4,224,128]{2,1,0:T(8,128)(2,1)S(1)}, bf16[4,224,128]{2,1,0:T(8,128)(2,1)S(1)}, u32[]{:S(2)}, u32[]{:S(2)}) %collective-permute-start.13) | collective-permute-done | bytes 229408 | tf_op jit(solution)/shard_map/ppermute | solution.py:563
  44.3 0.2 add_core.1
  44.6 2.2 %collective-permute-start.15 = (bf16[4,193,128]{2,1,0:T(8,128)(2,1)S(1)}, bf16[4,193,128]{2,1,0:T(8,128)(2,1)S(1)}, u32[]{:S(2)}, u32[]{:S(2)}) collective-permute-start(bf16[4,193,128]{2,1,0:T(8,128)(2,1)S(1)} %get-tuple-element.66), channel_id=1, source_target_pairs={{0,6},{1,7},{2,4},{3,5},{4,2},{5,3},{6,0},{7,1},{8,14},{9,15},{10,... | collective-permute-start | bytes 592904 | tf_op jit(solution)/shard_map/ppermute | solution.py:563
  46.8 0.5 collective-permute-start.16
  47.3 1.0 %collective-permute-start.17 = (bf16[4,193,128]{2,1,0:T(8,128)(2,1)S(1)}, bf16[4,193,128]{2,1,0:T(8,128)(2,1)S(1)}, u32[]{:S(2)}, u32[]{:S(2)}) collective-permute-start(bf16[4,193,128]{2,1,0:T(8,128)(2,1)S(1)} %get-tuple-element.68), channel_id=1, source_target_pairs={{0,4},{1,5},{2,6},{3,7},{4,0},{5,1},{6,2},{7,3},{8,12},{9,13},{10,... | collective-permute-start | bytes 592904 | tf_op jit(solution)/shard_map/ppermute | solution.py:563
  48.3 2.1 %input_grad.1 = f32[1024,256]{1,0:T(8,128)} custom-call(bf16[1024,256]{1,0:T(8,128)(2,1)S(1)} %copy-done.7, bf16[1024,768]{1,0:T(8,128)(2,1)S(1)} %get-tuple-element.59.grad_project, f32[1024,256]{1,0:T(8,128)S(1)} %get-tuple-element.60.grad_middle, bf16[256,768]{1,0:T(8,128)(2,1)S(1)} %get-tuple-element.57.w_qkv, f32[32,128]{1,0:T(8,128)S(1)} %get-tuple-element.45.small), custom_call_target="tpu_custom_call" | custom-call | flops 2000000000 | bytes 1048576 | tf_op jit(solution)/shard_map/input_grad/pallas_call | solution.py:418
  50.3 3.1 %collective-permute-done.15.refs_0_ = bf16[4,193,128]{2,1,0:T(8,128)(2,1)S(1)} collective-permute-done((bf16[4,193,128]{2,1,0:T(8,128)(2,1)S(1)}, bf16[4,193,128]{2,1,0:T(8,128)(2,1)S(1)}, u32[]{:S(2)}, u32[]{:S(2)}) %collective-permute-start.15) | collective-permute-done | bytes 197664 | tf_op jit(solution)/shard_map/ppermute | solution.py:563
  53.5 3.3 %collective-permute-done.16.refs_1_ = bf16[4,193,128]{2,1,0:T(8,128)(2,1)S(1)} collective-permute-done((bf16[4,193,128]{2,1,0:T(8,128)(2,1)S(1)}, bf16[4,193,128]{2,1,0:T(8,128)(2,1)S(1)}, u32[]{:S(2)}, u32[]{:S(2)}) %collective-permute-start.16) | collective-permute-done | bytes 197664 | tf_op jit(solution)/shard_map/ppermute | solution.py:563
  57.2 0.7 %collective-permute-start.18 = (bf16[193,128]{1,0:T(8,128)(2,1)S(1)}, bf16[193,128]{1,0:T(8,128)(2,1)S(1)}, u32[]{:S(2)}, u32[]{:S(2)}) collective-permute-start(bf16[193,128]{1,0:T(8,128)(2,1)S(1)} %get-tuple-element.70), channel_id=1, source_target_pairs={{0,8},{1,9},{2,10},{3,11},{4,12},{5,13},{6,14},{7,15},{8,16},{9,17... | collective-permute-start | bytes 148232 | tf_op jit(solution)/shard_map/ppermute | solution.py:563
  58.0 3.6 %collective-permute-start.19 = (bf16[193,128]{1,0:T(8,128)(2,1)S(1)}, bf16[193,128]{1,0:T(8,128)(2,1)S(1)}, u32[]{:S(2)}, u32[]{:S(2)}) collective-permute-start(bf16[193,128]{1,0:T(8,128)(2,1)S(1)} %get-tuple-element.71), channel_id=1, source_target_pairs={{0,16},{1,17},{2,18},{3,19},{4,20},{5,21},{6,22},{7,23},{8,24},{9,... | collective-permute-start | bytes 148232 | tf_op jit(solution)/shard_map/ppermute | solution.py:563
  61.5 1.5 %result.1 = bf16[1024,256]{1,0:T(8,128)(2,1)} custom-call(f32[1024,256]{1,0:T(8,128)S(1)} %get-tuple-element.50.middle, bf16[1024,1024]{1,0:T(8,128)(2,1)S(1)} %get-tuple-element.51.activated, bf16[1024,256]{1,0:T(8,128)(2,1)S(1)} %get-tuple-element.52.w_down, f32[32,128]{1,0:T(8,128)S(1)} %get-tuple-element.45.small), custom_call_target="tpu_custom_call" | custom-call | flops 2000000000 | bytes 1048576 | tf_op jit(solution)/shard_map/result/pallas_call | solution.py:418
  63.1 0.7 %collective-permute-done.18.refs_0_ = bf16[193,128]{1,0:T(8,128)(2,1)S(1)} collective-permute-done((bf16[193,128]{1,0:T(8,128)(2,1)S(1)}, bf16[193,128]{1,0:T(8,128)(2,1)S(1)}, u32[]{:S(2)}, u32[]{:S(2)}) %collective-permute-start.18) | collective-permute-done | bytes 49440 | tf_op jit(solution)/shard_map/ppermute | solution.py:563
  63.7 1.5 %collective-permute-done.19.refs_1_ = bf16[193,128]{1,0:T(8,128)(2,1)S(1)} collective-permute-done((bf16[193,128]{1,0:T(8,128)(2,1)S(1)}, bf16[193,128]{1,0:T(8,128)(2,1)S(1)}, u32[]{:S(2)}, u32[]{:S(2)}) %collective-permute-start.19) | collective-permute-done | bytes 49440 | tf_op jit(solution)/shard_map/ppermute | solution.py:563
  65.2 0.5 collective-permute-done.20.refs_2_
  65.7 0.7 %add_column.1 = f32[193,128]{1,0:T(8,128)} custom-call(f32[193,128]{1,0:T(8,128)S(1)} %get-tuple-element.69.kept, bf16[193,128]{1,0:T(8,128)(2,1)S(1)} %collective-permute-done.18.refs_0_, bf16[193,128]{1,0:T(8,128)(2,1)S(1)} %collective-permute-done.19.refs_1_, bf16[193,128]{1,0:T(8,128)(2,1)S(1)} %collective-permute-done.20.refs_2_), custom_call_target="tpu_custom_call" | custom-call | flops 1000000000 | bytes 1048576 | tf_op jit(solution)/shard_map/add_column/pallas_call | solution.py:418
  (41 shorter events, 0.9 us)
Async XLA Ops:
  0.6 11.0 %collective-permute-start = (bf16[193,128]{1,0:T(8,128)(2,1)}, bf16[193,128]{1,0:T(8,128)(2,1)S(1)}, u32[]{:S(2)}, u32[]{:S(2)}) collective-permute-start(bf16[193,128]{1,0:T(8,128)(2,1)} %params.1), channel_id=1, source_target_pairs={{0,8},{1,9},{2,10},{3,11},{4,12},{5,13},{6,14},{7,15},{8,16},{9,17... | collective-permute-start | bytes 148232 | tf_op jit(solution)/shard_map/ppermute | solution.py:563
  3.7 8.0 %collective-permute-start.1 = (bf16[193,128]{1,0:T(8,128)(2,1)}, bf16[193,128]{1,0:T(8,128)(2,1)S(1)}, u32[]{:S(2)}, u32[]{:S(2)}) collective-permute-start(bf16[193,128]{1,0:T(8,128)(2,1)} %params.1), channel_id=1, source_target_pairs={{0,16},{1,17},{2,18},{3,19},{4,20},{5,21},{6,22},{7,23},{8,24},{9,... | collective-permute-start | bytes 148232 | tf_op jit(solution)/shard_map/ppermute | solution.py:563
  6.3 5.4 %collective-permute-start.2 = (bf16[193,128]{1,0:T(8,128)(2,1)}, bf16[193,128]{1,0:T(8,128)(2,1)S(1)}, u32[]{:S(2)}, u32[]{:S(2)}) collective-permute-start(bf16[193,128]{1,0:T(8,128)(2,1)} %params.1), channel_id=1, source_target_pairs={{0,24},{1,25},{2,26},{3,27},{4,28},{5,29},{6,30},{7,31},{8,0},{9,1... | collective-permute-start | bytes 148232 | tf_op jit(solution)/shard_map/ppermute | solution.py:563
  7.6 1.0 %copy-start.5 = (bf16[1024,256]{1,0:T(8,128)(2,1)S(1)}, bf16[1024,256]{1,0:T(8,128)(2,1)}, u32[]{:S(2)}) copy-start(bf16[1024,256]{1,0:T(8,128)(2,1)} %tok.5) | copy-start | bytes 1572868
  8.7 0.8 %copy-start.12 = (bf16[193,128]{1,0:T(8,128)(2,1)S(1)}, bf16[193,128]{1,0:T(8,128)(2,1)}, u32[]{:S(2)}) copy-start(bf16[193,128]{1,0:T(8,128)(2,1)} %params.1) | copy-start | bytes 148228
  9.5 0.7 %copy-start.13 = (s32[1024]{0:T(1024)S(1)}, s32[1024]{0:T(1024)}, u32[]{:S(2)}) copy-start(s32[1024]{0:T(1024)} %param.6) | copy-start | bytes 12292
  10.9 0.8 %copy-start.14 = (bf16[256,1024]{1,0:T(8,128)(2,1)}, bf16[256,1024]{1,0:T(8,128)(2,1)S(1)}, u32[]{:S(2)}) copy-start(bf16[256,1024]{1,0:T(8,128)(2,1)S(1)} %get-tuple-element.56.normed_turned) | copy-start | bytes 1572868
  12.4 6.5 %collective-permute-start.6 = (bf16[1,240,128]{2,1,0:T(8,128)(2,1)S(1)}, bf16[1,240,128]{2,1,0:T(8,128)(2,1)S(1)}, u32[]{:S(2)}, u32[]{:S(2)}) collective-permute-start(bf16[1,240,128]{2,1,0:T(8,128)(2,1)S(1)} %get-tuple-element.42.refs_0_), channel_id=1, source_target_pairs={{0,6},{1,7},{2,4},{3,5},{4,2},{5,3},{6,0},{7,1},{8,14},{9,15},{10,... | collective-permute-start | bytes 184328 | tf_op jit(solution)/shard_map/ppermute | solution.py:563
  14.8 4.9 %collective-permute-start.7 = (bf16[1,240,128]{2,1,0:T(8,128)(2,1)S(1)}, bf16[1,240,128]{2,1,0:T(8,128)(2,1)S(1)}, u32[]{:S(2)}, u32[]{:S(2)}) collective-permute-start(bf16[1,240,128]{2,1,0:T(8,128)(2,1)S(1)} %get-tuple-element.42.refs_0_), channel_id=1, source_target_pairs={{0,2},{1,3},{2,0},{3,1},{4,6},{5,7},{6,4},{7,5},{8,10},{9,11},{10,... | collective-permute-start | bytes 184328 | tf_op jit(solution)/shard_map/ppermute | solution.py:563
  15.3 4.6 %collective-permute-start.8 = (bf16[1,240,128]{2,1,0:T(8,128)(2,1)S(1)}, bf16[1,240,128]{2,1,0:T(8,128)(2,1)S(1)}, u32[]{:S(2)}, u32[]{:S(2)}) collective-permute-start(bf16[1,240,128]{2,1,0:T(8,128)(2,1)S(1)} %get-tuple-element.42.refs_0_), channel_id=1, source_target_pairs={{0,4},{1,5},{2,6},{3,7},{4,0},{5,1},{6,2},{7,3},{8,12},{9,13},{10,... | collective-permute-start | bytes 184328 | tf_op jit(solution)/shard_map/ppermute | solution.py:563
  15.8 10.3 %collective-permute-start.3 = (bf16[3,193,128]{2,1,0:T(8,128)(2,1)}, bf16[3,193,128]{2,1,0:T(8,128)(2,1)S(1)}, u32[]{:S(2)}, u32[]{:S(2)}) collective-permute-start(bf16[3,193,128]{2,1,0:T(8,128)(2,1)} %get-tuple-element.39.refs_0_), channel_id=1, source_target_pairs={{0,2},{1,3},{2,0},{3,1},{4,6},{5,7},{6,4},{7,5},{8,10},{9,11},{10,... | collective-permute-start | bytes 444680 | tf_op jit(solution)/shard_map/ppermute | solution.py:563
  17.3 8.8 %collective-permute-start.4 = (bf16[3,193,128]{2,1,0:T(8,128)(2,1)}, bf16[3,193,128]{2,1,0:T(8,128)(2,1)S(1)}, u32[]{:S(2)}, u32[]{:S(2)}) collective-permute-start(bf16[3,193,128]{2,1,0:T(8,128)(2,1)} %get-tuple-element.39.refs_0_), channel_id=1, source_target_pairs={{0,6},{1,7},{2,4},{3,5},{4,2},{5,3},{6,0},{7,1},{8,14},{9,15},{10,... | collective-permute-start | bytes 444680 | tf_op jit(solution)/shard_map/ppermute | solution.py:563
  18.8 7.3 %collective-permute-start.5 = (bf16[3,193,128]{2,1,0:T(8,128)(2,1)}, bf16[3,193,128]{2,1,0:T(8,128)(2,1)S(1)}, u32[]{:S(2)}, u32[]{:S(2)}) collective-permute-start(bf16[3,193,128]{2,1,0:T(8,128)(2,1)} %get-tuple-element.39.refs_0_), channel_id=1, source_target_pairs={{0,4},{1,5},{2,6},{3,7},{4,0},{5,1},{6,2},{7,3},{8,12},{9,13},{10,... | collective-permute-start | bytes 444680 | tf_op jit(solution)/shard_map/ppermute | solution.py:563
  19.7 1.3 %collective-permute-start.9 = (bf16[2,240,128]{2,1,0:T(8,128)(2,1)S(1)}, bf16[2,240,128]{2,1,0:T(8,128)(2,1)S(1)}, u32[]{:S(2)}, u32[]{:S(2)}) collective-permute-start(bf16[2,240,128]{2,1,0:T(8,128)(2,1)S(1)} %stack.47.refs_0_), channel_id=1, source_target_pairs={{0,1},{1,0},{2,3},{3,2},{4,5},{5,4},{6,7},{7,6},{8,9},{9,8},{10,11... | collective-permute-start | bytes 368648 | tf_op jit(solution)/shard_map/ppermute | solution.py:563
  19.9 9.3 %copy-start.4 = (bf16[1024,256]{1,0:T(8,128)(2,1)S(1)}, bf16[1024,256]{1,0:T(8,128)(2,1)}, u32[]{:S(2)}) copy-start(bf16[1024,256]{1,0:T(8,128)(2,1)} %cot.1) | copy-start | bytes 1572868
  19.9 1.4 %collective-permute-start.10 = (bf16[2,240,128]{2,1,0:T(8,128)(2,1)S(1)}, bf16[2,240,128]{2,1,0:T(8,128)(2,1)S(1)}, u32[]{:S(2)}, u32[]{:S(2)}) collective-permute-start(bf16[2,240,128]{2,1,0:T(8,128)(2,1)S(1)} %stack.48.refs_1_), channel_id=1, source_target_pairs={{0,1},{1,0},{2,3},{3,2},{4,5},{5,4},{6,7},{7,6},{8,9},{9,8},{10,11... | collective-permute-start | bytes 368648 | tf_op jit(solution)/shard_map/ppermute | solution.py:563
  24.0 1.2 %copy-start = (bf16[1024,768]{1,0:T(8,128)(2,1)}, bf16[1024,768]{1,0:T(8,128)(2,1)S(1)}, u32[]{:S(2)}) copy-start(bf16[1024,768]{1,0:T(8,128)(2,1)S(1)} %get-tuple-element.53.project) | copy-start | bytes 4718596
  25.1 1.0 %copy-start.2 = (bf16[1024,512]{1,0:T(8,128)(2,1)}, bf16[1024,512]{1,0:T(8,128)(2,1)S(1)}, u32[]{:S(2)}) copy-start(bf16[1024,512]{1,0:T(8,128)(2,1)S(1)} %get-tuple-element.54.weights) | copy-start | bytes 3145732
  26.1 0.8 %copy-start.8 = (bf16[1024,256]{1,0:T(8,128)(2,1)}, bf16[1024,256]{1,0:T(8,128)(2,1)S(1)}, u32[]{:S(2)}) copy-start(bf16[1024,256]{1,0:T(8,128)(2,1)S(1)} %get-tuple-element.44.attended) | copy-start | bytes 1572868
  26.2 3.0 %collective-permute-start.12 = (bf16[9,193,128]{2,1,0:T(8,128)(2,1)S(1)}, bf16[9,193,128]{2,1,0:T(8,128)(2,1)S(1)}, u32[]{:S(2)}, u32[]{:S(2)}) collective-permute-start(bf16[9,193,128]{2,1,0:T(8,128)(2,1)S(1)} %stack.49.refs_1_), channel_id=1, source_target_pairs={{0,1},{1,0},{2,3},{3,2},{4,5},{5,4},{6,7},{7,6},{8,9},{9,8},{10,11... | collective-permute-start | bytes 1334024 | tf_op jit(solution)/shard_map/ppermute | solution.py:563
  26.9 1.6 %collective-permute-start.11 = (bf16[3,193,128]{2,1,0:T(8,128)(2,1)}, bf16[3,193,128]{2,1,0:T(8,128)(2,1)S(1)}, u32[]{:S(2)}, u32[]{:S(2)}) collective-permute-start(bf16[3,193,128]{2,1,0:T(8,128)(2,1)} %get-tuple-element.39.refs_0_), channel_id=1, source_target_pairs={{0,1},{1,0},{2,3},{3,2},{4,5},{5,4},{6,7},{7,6},{8,9},{9,8},{10,11... | collective-permute-start | bytes 444680 | tf_op jit(solution)/shard_map/ppermute | solution.py:563
  28.5 0.7 %copy-start.10 = (bf16[3,193,128]{2,1,0:T(8,128)(2,1)}, bf16[3,193,128]{2,1,0:T(8,128)(2,1)S(1)}, u32[]{:S(2)}) copy-start(bf16[3,193,128]{2,1,0:T(8,128)(2,1)S(1)} %collective-permute-done.11.refs_2_) | copy-start | bytes 444676
  29.2 1.0 %copy-start.6 = (bf16[1024,256]{1,0:T(8,128)(2,1)S(1)}, bf16[1024,256]{1,0:T(8,128)(2,1)}, u32[]{:S(2)}) copy-start(bf16[1024,256]{1,0:T(8,128)(2,1)} %tok.5) | copy-start | bytes 1572868
  30.2 1.0 %copy-start.9 = (bf16[1024,256]{1,0:T(8,128)(2,1)S(1)}, bf16[1024,256]{1,0:T(8,128)(2,1)}, u32[]{:S(2)}) copy-start(bf16[1024,256]{1,0:T(8,128)(2,1)} %copy-done.8) | copy-start | bytes 1572868
  31.3 0.9 %copy-start.11 = (bf16[3,193,128]{2,1,0:T(8,128)(2,1)S(1)}, bf16[3,193,128]{2,1,0:T(8,128)(2,1)}, u32[]{:S(2)}) copy-start(bf16[3,193,128]{2,1,0:T(8,128)(2,1)} %copy-done.10) | copy-start | bytes 444676
  32.2 7.3 %copy-start.1 = (bf16[1024,768]{1,0:T(8,128)(2,1)S(1)}, bf16[1024,768]{1,0:T(8,128)(2,1)}, u32[]{:S(2)}) copy-start(bf16[1024,768]{1,0:T(8,128)(2,1)} %copy-done) | copy-start | bytes 4718596
  32.2 7.3 %copy-start.3 = (bf16[1024,512]{1,0:T(8,128)(2,1)S(1)}, bf16[1024,512]{1,0:T(8,128)(2,1)}, u32[]{:S(2)}) copy-start(bf16[1024,512]{1,0:T(8,128)(2,1)} %copy-done.2) | copy-start | bytes 3145732
  32.2 7.3 %copy-start.15 = (bf16[256,1024]{1,0:T(8,128)(2,1)S(1)}, bf16[256,1024]{1,0:T(8,128)(2,1)}, u32[]{:S(2)}) copy-start(bf16[256,1024]{1,0:T(8,128)(2,1)} %copy-done.14) | copy-start | bytes 1572868
  39.0 5.3 %collective-permute-start.14 = (bf16[12,193,128]{2,1,0:T(8,128)(2,1)S(1)}, bf16[12,193,128]{2,1,0:T(8,128)(2,1)S(1)}, u32[]{:S(2)}, u32[]{:S(2)}) collective-permute-start(bf16[12,193,128]{2,1,0:T(8,128)(2,1)S(1)} %get-tuple-element.64), channel_id=1, source_target_pairs={{0,1},{1,0},{2,3},{3,2},{4,5},{5,4},{6,7},{7,6},{8,9},{9,8},{10,11... | collective-permute-start | bytes 1778696 | tf_op jit(solution)/shard_map/ppermute | solution.py:563
  42.8 1.6 %collective-permute-start.13 = (bf16[4,224,128]{2,1,0:T(8,128)(2,1)S(1)}, bf16[4,224,128]{2,1,0:T(8,128)(2,1)S(1)}, u32[]{:S(2)}, u32[]{:S(2)}) collective-permute-start(bf16[4,224,128]{2,1,0:T(8,128)(2,1)S(1)} %get-tuple-element.62), channel_id=1, source_target_pairs={{0,1},{1,0},{2,3},{3,2},{4,5},{5,4},{6,7},{7,6},{8,9},{9,8},{10,11... | collective-permute-start | bytes 688136 | tf_op jit(solution)/shard_map/ppermute | solution.py:563
  44.3 4.0 %copy-start.7 = (bf16[1024,256]{1,0:T(8,128)(2,1)S(1)}, bf16[1024,256]{1,0:T(8,128)(2,1)}, u32[]{:S(2)}) copy-start(bf16[1024,256]{1,0:T(8,128)(2,1)} %tok.5) | copy-start | bytes 1572868
  44.6 8.9 %collective-permute-start.15 = (bf16[4,193,128]{2,1,0:T(8,128)(2,1)S(1)}, bf16[4,193,128]{2,1,0:T(8,128)(2,1)S(1)}, u32[]{:S(2)}, u32[]{:S(2)}) collective-permute-start(bf16[4,193,128]{2,1,0:T(8,128)(2,1)S(1)} %get-tuple-element.66), channel_id=1, source_target_pairs={{0,6},{1,7},{2,4},{3,5},{4,2},{5,3},{6,0},{7,1},{8,14},{9,15},{10,... | collective-permute-start | bytes 592904 | tf_op jit(solution)/shard_map/ppermute | solution.py:563
  46.8 10.1 %collective-permute-start.16 = (bf16[4,193,128]{2,1,0:T(8,128)(2,1)S(1)}, bf16[4,193,128]{2,1,0:T(8,128)(2,1)S(1)}, u32[]{:S(2)}, u32[]{:S(2)}) collective-permute-start(bf16[4,193,128]{2,1,0:T(8,128)(2,1)S(1)} %get-tuple-element.67), channel_id=1, source_target_pairs={{0,2},{1,3},{2,0},{3,1},{4,6},{5,7},{6,4},{7,5},{8,10},{9,11},{10,... | collective-permute-start | bytes 592904 | tf_op jit(solution)/shard_map/ppermute | solution.py:563
  47.3 9.8 %collective-permute-start.17 = (bf16[4,193,128]{2,1,0:T(8,128)(2,1)S(1)}, bf16[4,193,128]{2,1,0:T(8,128)(2,1)S(1)}, u32[]{:S(2)}, u32[]{:S(2)}) collective-permute-start(bf16[4,193,128]{2,1,0:T(8,128)(2,1)S(1)} %get-tuple-element.68), channel_id=1, source_target_pairs={{0,4},{1,5},{2,6},{3,7},{4,0},{5,1},{6,2},{7,3},{8,12},{9,13},{10,... | collective-permute-start | bytes 592904 | tf_op jit(solution)/shard_map/ppermute | solution.py:563
  57.2 6.5 %collective-permute-start.18 = (bf16[193,128]{1,0:T(8,128)(2,1)S(1)}, bf16[193,128]{1,0:T(8,128)(2,1)S(1)}, u32[]{:S(2)}, u32[]{:S(2)}) collective-permute-start(bf16[193,128]{1,0:T(8,128)(2,1)S(1)} %get-tuple-element.70), channel_id=1, source_target_pairs={{0,8},{1,9},{2,10},{3,11},{4,12},{5,13},{6,14},{7,15},{8,16},{9,17... | collective-permute-start | bytes 148232 | tf_op jit(solution)/shard_map/ppermute | solution.py:563
  58.0 7.3 %collective-permute-start.19 = (bf16[193,128]{1,0:T(8,128)(2,1)S(1)}, bf16[193,128]{1,0:T(8,128)(2,1)S(1)}, u32[]{:S(2)}, u32[]{:S(2)}) collective-permute-start(bf16[193,128]{1,0:T(8,128)(2,1)S(1)} %get-tuple-element.71), channel_id=1, source_target_pairs={{0,16},{1,17},{2,18},{3,19},{4,20},{5,21},{6,22},{7,23},{8,24},{9,... | collective-permute-start | bytes 148232 | tf_op jit(solution)/shard_map/ppermute | solution.py:563
  61.5 4.2 %collective-permute-start.20 = (bf16[193,128]{1,0:T(8,128)(2,1)S(1)}, bf16[193,128]{1,0:T(8,128)(2,1)S(1)}, u32[]{:S(2)}, u32[]{:S(2)}) collective-permute-start(bf16[193,128]{1,0:T(8,128)(2,1)S(1)} %get-tuple-element.72), channel_id=1, source_target_pairs={{0,24},{1,25},{2,26},{3,27},{4,28},{5,29},{6,30},{7,31},{8,0},{9,1... | collective-permute-start | bytes 148232 | tf_op jit(solution)/shard_map/ppermute | solution.py:563
